TPU v7x, 32 devices: a whole 2x2x4 slice. The times are simulated.
32 devices in a mesh: hel: 4 (over x, core), rad: 8 (over z, y).
Axes of the slice: x: 2, y: 2, z: 4, core: 2. Of those that a mesh axis runs over, the one named last changes fastest.
Arguments:
- packet: bfloat16 [1024, 2, 16, 4, 512], P('rad', None, 'hel'), may hold values from -6 to 6
- first_propagator: bfloat16 [2, 1024, 1024], replicated, may hold values from -0.125 to 0.125
- second_propagator: bfloat16 [2, 512, 512], replicated, may hold values from -0.1875 to 0.1875
- potential: float32 [1024, 4, 512], P('rad'), may hold values from -3.140625 to 3.140625
- coupling: float32 [16, 4], replicated, may hold values from 0.2 to 0.8
- radial_weight: float32 [1024, 512], P('rad'), may hold values from 0.25 to 1
Outputs:
- advanced: bfloat16 [1024, 2, 16, 4, 512], P('rad', None, 'hel')
All inputs are finite; a program needn't handle non-finite values.
Results may differ from a plain program's by a relative error of at most 0.007.
Values may be sent and summed in bfloat16 or wider, within the bound.
No kernel may reach another device: no remote copies, remote signals or barrier semaphores. Data moves between devices by JAX's collectives and lax.ppermute only.
A program may use at most 128 MiB of HBM per device.

v0:
```python
import functools

import jax
import jax.numpy as jnp
from jax import lax
from jax.experimental import pallas as pl
from jax.experimental.pallas import tpu as pltpu
from jax.sharding import PartitionSpec as P

LANES = 128
LIMIT = 48 * 1024 * 1024
SMEM = pl.BlockSpec(memory_space=pltpu.SMEM)


def params(limit=LIMIT):
    return pltpu.CompilerParams(vmem_limit_bytes=limit)


def cost(flops, moved):
    return pl.CostEstimate(flops=flops, bytes_accessed=moved, transcendentals=0)


def complex_rows(real, imag):
    return jnp.concatenate([real, -imag], 1), jnp.concatenate([imag, real], 1)


def right_kernel(ranks, states, me_ref, second_ref, *refs):
    kinds = len(refs) - 2 - ranks
    packets, outs, wide, slabs = refs[:kinds], refs[kinds:-2], refs[-2], refs[-1]
    me = me_ref[0]
    rows = packets[0].shape[0]
    group = packets[0].shape[2]
    tiles = group // states
    piece = slabs.shape[2] // 2
    cuts = tiles * LANES // piece
    for n, packet in enumerate(packets):
        wide[...] = packet[...].reshape(rows * 2 * group, LANES).astype(jnp.float32)

        def part(c, j):
            return jnp.concatenate(
                [
                    wide[pl.ds(c * group + t * states + j, rows, stride=2 * group), :]
                    for t in range(tiles)
                ],
                1,
            ).astype(jnp.bfloat16)

        pairs = [complex_rows(part(0, j), part(1, j)) for j in range(states)]
        left = jnp.concatenate([p[0] for p in pairs] + [p[1] for p in pairs], 0)
        product = jnp.dot(left, second_ref[...], preferred_element_type=jnp.float32)
        product = product.astype(jnp.bfloat16)
        for c in range(2):
            for j in range(states):
                first = (c * states + j) * rows
                for p in range(cuts):
                    slabs[j * cuts + p, :, c * piece : (c + 1) * piece] = product[
                        first : first + rows, p * piece : (p + 1) * piece
                    ]
        for s, out in enumerate(outs):
            out[n] = slabs[me ^ s]


def right_call(me, second, view, chosen, ranks, states, piece):
    rows, _, _, group, _ = view.shape
    width = second.shape[1]
    block = rows // 2
    kinds = len(chosen)
    return pl.pallas_call(
        functools.partial(right_kernel, ranks, states),
        grid=(rows // block,),
        in_specs=[SMEM, pl.BlockSpec(second.shape, lambda i: (0, 0))]
        + [
            pl.BlockSpec((block, 2, None, group, LANES), lambda i, k=k: (i, 0, k, 0, 0))
            for k in chosen
        ],
        out_specs=[pl.BlockSpec((kinds, block, 2 * piece), lambda i: (0, i, 0))] * ranks,
        out_shape=[jax.ShapeDtypeStruct((kinds, rows, 2 * piece), jnp.bfloat16)] * ranks,
        scratch_shapes=[
            pltpu.VMEM((block * 2 * group, LANES), jnp.float32),
            pltpu.VMEM((ranks, block, 2 * piece), jnp.bfloat16),
        ],
        compiler_params=params(),
        cost_estimate=cost(
            8 * kinds * states * rows * width * width, 8 * kinds * states * rows * width
        ),
        name="right",
    )(me, second, *([view] * kinds))


def left_kernel(ranks, me_ref, first_ref, *refs):
    ins, outs, lines, slabs = refs[:ranks], refs[ranks:-2], refs[-2], refs[-1]
    me = me_ref[0]
    rows, wide = ins[0].shape
    piece = wide // 2
    whole = ranks * rows
    for s, part in enumerate(ins):
        value = part[...]
        first = pl.multiple_of((me ^ s) * rows, rows)
        lines[pl.ds(first, rows), :] = value
        lines[pl.ds(first + whole, rows), :] = jnp.concatenate(
            [-value[:, piece:], value[:, :piece]], 1
        )
    product = jnp.dot(first_ref[...], lines[...], preferred_element_type=jnp.float32)
    slabs[...] = product.astype(jnp.bfloat16).reshape(ranks, rows, wide)
    for s, out in enumerate(outs):
        out[...] = slabs[me ^ s]


def left_call(me, first, slabs):
    ranks = len(slabs)
    kinds, rows, wide = slabs[0].shape
    whole = ranks * rows
    spec = pl.BlockSpec((None, rows, wide), lambda i: (i, 0, 0))
    return pl.pallas_call(
        functools.partial(left_kernel, ranks),
        grid=(kinds,),
        in_specs=[SMEM, pl.BlockSpec(first.shape, lambda i: (0, 0))] + [spec] * ranks,
        out_specs=[spec] * ranks,
        out_shape=[jax.ShapeDtypeStruct(slabs[0].shape, jnp.bfloat16)] * ranks,
        scratch_shapes=[
            pltpu.VMEM((2 * whole, wide), jnp.bfloat16),
            pltpu.VMEM((ranks, rows, wide), jnp.bfloat16),
        ],
        compiler_params=params(),
        cost_estimate=cost(
            4 * kinds * whole * whole * wide, 4 * whole * whole + 4 * kinds * whole * wide
        ),
        name="left",
    )(me, first, *slabs)


def phase_kernel(ranks, me_ref, second_ref, cosine_ref, sine_ref, *refs):
    ins, outs, slabs = refs[:ranks], refs[ranks:-1], refs[-1]
    me = me_ref[0]
    states, rows, width = cosine_ref.shape
    piece = slabs.shape[2] // 2
    cuts = width // piece
    for n, out in enumerate(outs):
        for s, part in enumerate(ins):
            slabs[me ^ s] = part[n]
        pairs = []
        for j in range(states):
            real, imag = (
                jnp.concatenate(
                    [
                        slabs[j * cuts + p, :, c * piece : (c + 1) * piece]
                        for p in range(cuts)
                    ],
                    1,
                ).astype(jnp.float32)
                for c in range(2)
            )
            cosine, sine = cosine_ref[j], sine_ref[j]
            pairs.append(
                complex_rows(
                    (real * cosine + imag * sine).astype(jnp.bfloat16),
                    (imag * cosine - real * sine).astype(jnp.bfloat16),
                )
            )
        left = jnp.concatenate([p[0] for p in pairs] + [p[1] for p in pairs], 0)
        product = jnp.dot(left, second_ref[...], preferred_element_type=jnp.float32)
        out[...] = product.astype(jnp.bfloat16).reshape(2, states, rows, width)


def phase_call(me, second, cosine, sine, slabs):
    ranks = len(slabs)
    kinds, rows, wide = slabs[0].shape
    states, _, width = cosine.shape
    block = rows // 2
    table = pl.BlockSpec((states, block, width), lambda i: (0, i, 0))
    return pl.pallas_call(
        functools.partial(phase_kernel, ranks),
        grid=(rows // block,),
        in_specs=[SMEM, pl.BlockSpec(second.shape, lambda i: (0, 0)), table, table]
        + [pl.BlockSpec((kinds, block, wide), lambda i: (0, i, 0))] * ranks,
        out_specs=[pl.BlockSpec((2, states, block, width), lambda i: (0, 0, i, 0))] * kinds,
        out_shape=[jax.ShapeDtypeStruct((2, states, rows, width), jnp.bfloat16)] * kinds,
        scratch_shapes=[pltpu.VMEM((ranks, block, wide), jnp.bfloat16)],
        compiler_params=params(),
        cost_estimate=cost(
            8 * kinds * states * rows * width * width, 8 * kinds * states * rows * width
        ),
        name="phase",
    )(me, second, cosine, sine, *slabs)


def mix_kernel(up_ref, down_ref, weight_ref, *refs):
    kinetic, out, wide = refs[:-2], refs[-2], refs[-1]
    _, states, rows, width = kinetic[0].shape
    tiles = width // LANES
    group = tiles * states
    weight = weight_ref[...]
    for k in range(len(kinetic) - 2):
        below, here, above = kinetic[k : k + 3]
        for j in range(states):
            up, down = up_ref[k, j], down_ref[k, j]
            mixed = [
                up * above[c, j].astype(jnp.float32) + down * below[c, j].astype(jnp.float32)
                for c in range(2)
            ]
            parts = (
                here[0, j].astype(jnp.float32) + weight * mixed[1],
                here[1, j].astype(jnp.float32) - weight * mixed[0],
            )
            for c in range(2):
                for t in range(tiles):
                    wide[pl.ds(c * group + t * states + j, rows, stride=2 * group), :] = parts[c][
                        :, t * LANES : (t + 1) * LANES
                    ]
        out[:, :, k] = wide[...].astype(jnp.bfloat16).reshape(rows, 2, group, LANES)


def mix_call(up, down, weight, kinetic):
    _, states, rows, width = kinetic[0].shape
    blocks = len(kinetic) - 2
    group = width // LANES * states
    block = rows // 4
    return pl.pallas_call(
        mix_kernel,
        grid=(rows // block,),
        in_specs=[SMEM, SMEM, pl.BlockSpec((block, width), lambda i: (i, 0))]
        + [pl.BlockSpec((2, states, block, width), lambda i: (0, 0, i, 0))] * len(kinetic),
        out_specs=pl.BlockSpec((block, 2, blocks, group, LANES), lambda i: (i, 0, 0, 0, 0)),
        out_shape=jax.ShapeDtypeStruct((rows, 2, blocks, group, LANES), jnp.bfloat16),
        scratch_shapes=[pltpu.VMEM((block * 2 * group, LANES), jnp.float32)],
        compiler_params=params(),
        cost_estimate=cost(
            20 * blocks * states * rows * width, 10 * blocks * states * rows * width
        ),
        name="mix",
    )(up, down, weight, *kinetic)


def exchanged(slabs, axis):
    count = lax.axis_size(axis)
    result = [slabs[0]] + [None] * (count - 1)
    for s in reversed(range(1, count)):
        result[s] = lax.ppermute(slabs[s], axis, [(i, i ^ s) for i in range(count)])
    return result


def neighbour(edge, axis, step):
    count = lax.axis_size(axis)
    pairs = [(i, i + step) for i in range(count) if 0 <= i + step < count]
    return lax.ppermute(edge, axis, pairs)


def per_device(packet, first_propagator, second_propagator, potential, coupling, radial_weight):
    rows, _, blocks, states, width = packet.shape
    ranks = lax.axis_size("rad")
    whole = first_propagator.shape[1]
    tiles = width // LANES
    piece = states * width // ranks
    me = lax.axis_index("rad").astype(jnp.int32).reshape(1)
    second = second_propagator.reshape(2 * width, width)
    first = first_propagator.reshape(2 * whole, whole).T
    view = packet.reshape(rows, 2, blocks, states, tiles, LANES).transpose(0, 1, 2, 4, 3, 5)
    view = view.reshape(rows, 2, blocks, tiles * states, LANES)
    edges = sorted({0, blocks - 1})
    inner = [k for k in range(blocks) if k not in edges]
    chunks = [c for c in (edges, inner) if c]

    halves = [right_call(me, second, view, c, ranks, states, piece) for c in chunks]
    lines = [exchanged(h, "rad") for h in halves]
    moved = [left_call(me, first, x) for x in lines]
    backs = [exchanged(m, "rad") for m in moved]

    angles = potential.transpose(1, 0, 2)
    cosine, sine = jnp.cos(angles), jnp.sin(angles)
    kinetic = [None] * blocks
    for chosen, back in zip(chunks, backs):
        for k, value in zip(chosen, phase_call(me, second, cosine, sine, back)):
            kinetic[k] = value
    below = neighbour(kinetic[-1], "hel", 1)
    above = neighbour(kinetic[0], "hel", -1)

    count = coupling.shape[0]
    helicities = jnp.arange(count, dtype=jnp.int32)
    couple_up = jnp.where(helicities[:, None] < count - 1, coupling, 0.0)
    couple_down = jnp.concatenate(
        [jnp.zeros((1, coupling.shape[1]), jnp.float32), coupling[:-1]], axis=0
    )
    start = lax.axis_index("hel") * blocks
    up = lax.dynamic_slice_in_dim(couple_up, start, blocks, 0)
    down = lax.dynamic_slice_in_dim(couple_down, start, blocks, 0)
    out = mix_call(up, down, radial_weight, [below] + kinetic + [above])
    out = out.reshape(rows, 2, blocks, tiles, states, LANES).transpose(0, 1, 2, 4, 3, 5)
    return out.reshape(rows, 2, blocks, states, width)


def solution(mesh):
    return jax.shard_map(
        per_device,
        mesh=mesh,
        in_specs=(
            P("rad", None, "hel", None, None),
            P(),
            P(),
            P("rad", None, None),
            P(),
            P("rad", None),
        ),
        out_specs=P("rad", None, "hel", None, None),
        check_vma=False,
    )
```

profile of v0, /device:TPU:9, one launch (start us, length us, event | category | flops | bytes accessed | tf_op | source)
XLA Modules:
  0.0 228.2 jit_solution(109997867849914576)
XLA Ops:
  0.0 1.2 copy-done
  1.2 6.4 %right.2 = (bf16[2,128,512]{2,1,0:T(8,128)(2,1)S(1)}, bf16[2,128,512]{2,1,0:T(8,128)(2,1)S(1)}, bf16[2,128,512]{2,1,0:T(8,128)(2,1)S(1)}, bf16[2,128,512]{2,1,0:...) custom-call(s32[1]{0:T(128)} %bitcast.me_ref, ...), custom_call_target="tpu_custom_call" | custom-call | flops 2147483648 | bytes 4194304 | tf_op jit(solution)/shard_map/right/pallas_call | solution.py:68
  7.7 1.2 collective-permute-start
  9.1 1.2 collective-permute-start.2
  10.3 2.3 %collective-permute-start.3 = (bf16[2,128,512]{2,1,0:T(8,128)(2,1)}, bf16[2,128,512]{2,1,0:T(8,128)(2,1)S(1)}, u32[]{:S(2)}, u32[]{:S(2)}) collective-permute-start(bf16[2,128,512]{2,1,0:T(8,128)(2,1)} %get-tuple-element.45), channel_id=1, source_target_pairs={{0,4},{1,5},{2,6},{3,7},{4,0},{5,1},{6,2},{7,3},{8,12},{9,13},{10,... | collective-permute-start | bytes 786440 | tf_op jit(solution)/shard_map/ppermute | solution.py:238
  12.6 1.0 collective-permute-start.4
  13.6 1.2 collective-permute-done.refs_1_
  14.8 1.3 collective-permute-start.5
  16.1 7.3 %collective-permute-done.1.refs_2_ = bf16[2,128,512]{2,1,0:T(8,128)(2,1)S(1)} collective-permute-done((bf16[2,128,512]{2,1,0:T(8,128)(2,1)S(1)}, bf16[2,128,512]{2,1,0:T(8,128)(2,1)S(1)}, u32[]{:S(2)}, u32[]{:S(2)}) %collective-permute-start.1) | collective-permute-done | bytes 262176 | tf_op jit(solution)/shard_map/ppermute | solution.py:238
  23.4 6.5 %copy.14 = bf16[2048,1024]{0,1:T(8,128)(2,1)} copy(bf16[2048,1024]{1,0:T(8,128)(2,1)} %bitcast.27) | data formatting | bytes 8388608 | tf_op jit(solution)/shard_map/reshape | solution.py:256
  30.0 5.8 %right.3 = (bf16[2,128,512]{2,1,0:T(8,128)(2,1)S(1)}, bf16[2,128,512]{2,1,0:T(8,128)(2,1)S(1)}, bf16[2,128,512]{2,1,0:T(8,128)(2,1)S(1)}, bf16[2,128,512]{2,1,0:...) custom-call(s32[1]{0:T(128)} %bitcast.me_ref, ...), custom_call_target="tpu_custom_call" | custom-call | flops 2147483648 | bytes 4194304 | tf_op jit(solution)/shard_map/right/pallas_call | solution.py:68
  35.8 2.0 collective-permute-start.15
  37.8 3.6 %collective-permute-start.16 = (bf16[2,128,512]{2,1,0:T(8,128)(2,1)S(1)}, bf16[2,128,512]{2,1,0:T(8,128)(2,1)S(1)}, u32[]{:S(2)}, u32[]{:S(2)}) collective-permute-start(bf16[2,128,512]{2,1,0:T(8,128)(2,1)S(1)} %get-tuple-element.61), channel_id=1, source_target_pairs={{0,2},{1,3},{2,0},{3,1},{4,6},{5,7},{6,4},{7,5},{8,10},{9,11},{10,... | collective-permute-start | bytes 786440 | tf_op jit(solution)/shard_map/ppermute | solution.py:238
  41.3 2.7 %collective-permute-done.4.refs_5_ = bf16[2,128,512]{2,1,0:T(8,128)(2,1)S(1)} collective-permute-done((bf16[2,128,512]{2,1,0:T(8,128)(2,1)}, bf16[2,128,512]{2,1,0:T(8,128)(2,1)S(1)}, u32[]{:S(2)}, u32[]{:S(2)}) %collective-permute-start.4) | collective-permute-done | bytes 262176 | tf_op jit(solution)/shard_map/ppermute | solution.py:238
  44.1 6.7 %collective-permute-done.5.refs_6_ = bf16[2,128,512]{2,1,0:T(8,128)(2,1)S(1)} collective-permute-done((bf16[2,128,512]{2,1,0:T(8,128)(2,1)S(1)}, bf16[2,128,512]{2,1,0:T(8,128)(2,1)S(1)}, u32[]{:S(2)}, u32[]{:S(2)}) %collective-permute-start.5) | collective-permute-done | bytes 262176 | tf_op jit(solution)/shard_map/ppermute | solution.py:238
  50.8 8.8 %collective-permute-done.6.refs_7_ = bf16[2,128,512]{2,1,0:T(8,128)(2,1)} collective-permute-done((bf16[2,128,512]{2,1,0:T(8,128)(2,1)S(1)}, bf16[2,128,512]{2,1,0:T(8,128)(2,1)}, u32[]{:S(2)}, u32[]{:S(2)}) %collective-permute-start.6) | collective-permute-done | bytes 262176 | tf_op jit(solution)/shard_map/ppermute | solution.py:238
  59.5 7.5 %left.2 = (bf16[2,128,512]{2,1,0:T(8,128)(2,1)S(1)}, bf16[2,128,512]{2,1,0:T(8,128)(2,1)S(1)}, bf16[2,128,512]{2,1,0:T(8,128)(2,1)S(1)}, bf16[2,128,512]{2,1,0:T...) custom-call(s32[1]{0:T(128)} %bitcast.me_ref, ...), custom_call_target="tpu_custom_call" | custom-call | flops 4294967296 | bytes 8388608 | tf_op jit(solution)/shard_map/left/pallas_call | solution.py:114
  67.0 3.0 %collective-permute-start.20 = (bf16[2,128,512]{2,1,0:T(8,128)(2,1)S(1)}, bf16[2,128,512]{2,1,0:T(8,128)(2,1)S(1)}, u32[]{:S(2)}, u32[]{:S(2)}) collective-permute-start(bf16[2,128,512]{2,1,0:T(8,128)(2,1)S(1)} %get-tuple-element.65), channel_id=1, source_target_pairs={{0,6},{1,7},{2,4},{3,5},{4,2},{5,3},{6,0},{7,1},{8,14},{9,15},{10,... | collective-permute-start | bytes 786440 | tf_op jit(solution)/shard_map/ppermute | solution.py:238
  70.0 4.2 %collective-permute-start.10 = (bf16[2,128,512]{2,1,0:T(8,128)(2,1)S(1)}, bf16[2,128,512]{2,1,0:T(8,128)(2,1)S(1)}, u32[]{:S(2)}, u32[]{:S(2)}) collective-permute-start(bf16[2,128,512]{2,1,0:T(8,128)(2,1)S(1)} %get-tuple-element.53), channel_id=1, source_target_pairs={{0,4},{1,5},{2,6},{3,7},{4,0},{5,1},{6,2},{7,3},{8,12},{9,13},{10,... | collective-permute-start | bytes 786440 | tf_op jit(solution)/shard_map/ppermute | solution.py:238
  74.5 4.6 %sine_bitcast_fusion = (f32[4,128,512]{2,1,0:T(8,128)}, f32[4,128,512]{2,1,0:T(8,128)}) fusion(f32[128,4,512]{2,1,0:T(4,128)S(1)} %copy-done.10), kind=kLoop, calls=%fused_computation | loop fusion | bytes 3145728 | tf_op jit(solution)/shard_map/sin | solution.py:269
  79.1 19.4 %collective-permute-done.19.refs_5_ = bf16[2,128,512]{2,1,0:T(8,128)(2,1)S(1)} collective-permute-done((bf16[2,128,512]{2,1,0:T(8,128)(2,1)S(1)}, bf16[2,128,512]{2,1,0:T(8,128)(2,1)S(1)}, u32[]{:S(2)}, u32[]{:S(2)}) %collective-permute-start.19) | collective-permute-done | bytes 262176 | tf_op jit(solution)/shard_map/ppermute | solution.py:238
  98.5 14.2 %collective-permute-done.20.refs_6_ = bf16[2,128,512]{2,1,0:T(8,128)(2,1)S(1)} collective-permute-done((bf16[2,128,512]{2,1,0:T(8,128)(2,1)S(1)}, bf16[2,128,512]{2,1,0:T(8,128)(2,1)S(1)}, u32[]{:S(2)}, u32[]{:S(2)}) %collective-permute-start.20) | collective-permute-done | bytes 262176 | tf_op jit(solution)/shard_map/ppermute | solution.py:238
  112.7 3.0 %collective-permute-start.13 = (bf16[2,128,512]{2,1,0:T(8,128)(2,1)S(1)}, bf16[2,128,512]{2,1,0:T(8,128)(2,1)S(1)}, u32[]{:S(2)}, u32[]{:S(2)}) collective-permute-start(bf16[2,128,512]{2,1,0:T(8,128)(2,1)S(1)} %get-tuple-element.56), channel_id=1, source_target_pairs={{0,7},{1,6},{2,5},{3,4},{4,3},{5,2},{6,1},{7,0},{8,15},{9,14},{10,... | collective-permute-start | bytes 786440 | tf_op jit(solution)/shard_map/ppermute | solution.py:238
  115.7 8.8 %collective-permute-done.21.refs_7_ = bf16[2,128,512]{2,1,0:T(8,128)(2,1)S(1)} collective-permute-done((bf16[2,128,512]{2,1,0:T(8,128)(2,1)S(1)}, bf16[2,128,512]{2,1,0:T(8,128)(2,1)S(1)}, u32[]{:S(2)}, u32[]{:S(2)}) %collective-permute-start.21) | collective-permute-done | bytes 262176 | tf_op jit(solution)/shard_map/ppermute | solution.py:238
  125.1 4.3 %collective-permute-done.10.refs_4_ = bf16[2,128,512]{2,1,0:T(8,128)(2,1)S(1)} collective-permute-done((bf16[2,128,512]{2,1,0:T(8,128)(2,1)S(1)}, bf16[2,128,512]{2,1,0:T(8,128)(2,1)S(1)}, u32[]{:S(2)}, u32[]{:S(2)}) %collective-permute-start.10) | collective-permute-done | bytes 262176 | tf_op jit(solution)/shard_map/ppermute | solution.py:238
  129.4 1.3 collective-permute-start.8
  130.7 4.3 %collective-permute-done.11.refs_5_ = bf16[2,128,512]{2,1,0:T(8,128)(2,1)S(1)} collective-permute-done((bf16[2,128,512]{2,1,0:T(8,128)(2,1)S(1)}, bf16[2,128,512]{2,1,0:T(8,128)(2,1)S(1)}, u32[]{:S(2)}, u32[]{:S(2)}) %collective-permute-start.11) | collective-permute-done | bytes 262176 | tf_op jit(solution)/shard_map/ppermute | solution.py:238
  135.1 2.2 collective-permute-start.9
  137.3 8.0 %left.3 = (bf16[2,128,512]{2,1,0:T(8,128)(2,1)S(1)}, bf16[2,128,512]{2,1,0:T(8,128)(2,1)S(1)}, bf16[2,128,512]{2,1,0:T(8,128)(2,1)}, bf16[2,128,512]{2,1,0:T(8,1...) custom-call(s32[1]{0:T(128)} %bitcast.me_ref, ...), custom_call_target="tpu_custom_call" | custom-call | flops 4294967296 | bytes 8388608 | tf_op jit(solution)/shard_map/left/pallas_call | solution.py:114
  145.3 0.9 collective-permute-start.22
  146.3 2.8 %collective-permute-done.13.refs_7_ = bf16[2,128,512]{2,1,0:T(8,128)(2,1)S(1)} collective-permute-done((bf16[2,128,512]{2,1,0:T(8,128)(2,1)S(1)}, bf16[2,128,512]{2,1,0:T(8,128)(2,1)S(1)}, u32[]{:S(2)}, u32[]{:S(2)}) %collective-permute-start.13) | collective-permute-done | bytes 262176 | tf_op jit(solution)/shard_map/ppermute | solution.py:238
  149.1 4.0 %phase.2 = (bf16[2,4,128,512]{3,2,1,0:T(8,128)(2,1)S(1)}, bf16[2,4,128,512]{3,2,1,0:T(8,128)(2,1)S(1)}) custom-call(s32[1]{0:T(128)} %bitcast.me_ref, bf16[1024,512]{1,0:T(8,128)(2,1)S(1)} %bitcast.21, f32[4,128,512]{2,1,0:T(8,128)} %get-tuple-element.78.cosine_ref, f32[4,128,512]{2,1,0:T(8,128)} %get-tuple-element.77.sine_ref, ...), custom_call_target="tpu_custom_call" | custom-call | flops 2147483648 | bytes 4194304 | tf_op jit(solution)/shard_map/phase/pallas_call | solution.py:171
  153.1 5.8 %collective-permute-start.14 = (bf16[2,4,128,512]{3,2,1,0:T(8,128)(2,1)S(1)}, bf16[2,4,128,512]{3,2,1,0:T(8,128)(2,1)}, u32[]{:S(2)}, u32[]{:S(2)}) collective-permute-start(bf16[2,4,128,512]{3,2,1,0:T(8,128)(2,1)S(1)} %get-tuple-element.57.refs_4_), channel_id=1, source_target_pairs={{0,8},{8,16},{16,24},{1,9},{9,17},{17,25},{2,10},{10,18},{18,26},{... | collective-permute-start | bytes 3145736 | tf_op jit(solution)/shard_map/ppermute | solution.py:245
  158.9 2.1 collective-permute-start.29
  161.1 2.0 collective-permute-start.24
  163.8 1.7 collective-permute-start.25
  165.5 7.7 %collective-permute-done.23.refs_2_ = bf16[2,128,512]{2,1,0:T(8,128)(2,1)} collective-permute-done((bf16[2,128,512]{2,1,0:T(8,128)(2,1)}, bf16[2,128,512]{2,1,0:T(8,128)(2,1)}, u32[]{:S(2)}, u32[]{:S(2)}) %collective-permute-start.23) | collective-permute-done | bytes 262176 | tf_op jit(solution)/shard_map/ppermute | solution.py:238
  173.2 4.3 %collective-permute-start.26 = (bf16[2,128,512]{2,1,0:T(8,128)(2,1)}, bf16[2,128,512]{2,1,0:T(8,128)(2,1)}, u32[]{:S(2)}, u32[]{:S(2)}) collective-permute-start(bf16[2,128,512]{2,1,0:T(8,128)(2,1)} %copy-done.5), channel_id=1, source_target_pairs={{0,5},{1,4},{2,7},{3,6},{4,1},{5,0},{6,3},{7,2},{8,13},{9,12},{10,... | collective-permute-start | bytes 786440 | tf_op jit(solution)/shard_map/ppermute | solution.py:238
  177.5 0.7 collective-permute-done.24.refs_3_
  178.2 3.8 %collective-permute-start.27 = (bf16[2,128,512]{2,1,0:T(8,128)(2,1)}, bf16[2,128,512]{2,1,0:T(8,128)(2,1)}, u32[]{:S(2)}, u32[]{:S(2)}) collective-permute-start(bf16[2,128,512]{2,1,0:T(8,128)(2,1)} %copy-done.4), channel_id=1, source_target_pairs={{0,6},{1,7},{2,4},{3,5},{4,2},{5,3},{6,0},{7,1},{8,14},{9,15},{10,... | collective-permute-start | bytes 786440 | tf_op jit(solution)/shard_map/ppermute | solution.py:238
  182.0 0.9 collective-permute-done.25.refs_4_
  183.2 18.4 %collective-permute-done.26.refs_5_ = bf16[2,128,512]{2,1,0:T(8,128)(2,1)} collective-permute-done((bf16[2,128,512]{2,1,0:T(8,128)(2,1)}, bf16[2,128,512]{2,1,0:T(8,128)(2,1)}, u32[]{:S(2)}, u32[]{:S(2)}) %collective-permute-start.26) | collective-permute-done | bytes 262176 | tf_op jit(solution)/shard_map/ppermute | solution.py:238
  201.6 8.5 %collective-permute-done.27.refs_6_ = bf16[2,128,512]{2,1,0:T(8,128)(2,1)} collective-permute-done((bf16[2,128,512]{2,1,0:T(8,128)(2,1)}, bf16[2,128,512]{2,1,0:T(8,128)(2,1)}, u32[]{:S(2)}, u32[]{:S(2)}) %collective-permute-start.27) | collective-permute-done | bytes 262176 | tf_op jit(solution)/shard_map/ppermute | solution.py:238
  210.2 2.5 %collective-permute-done.28.refs_7_ = bf16[2,128,512]{2,1,0:T(8,128)(2,1)} collective-permute-done((bf16[2,128,512]{2,1,0:T(8,128)(2,1)}, bf16[2,128,512]{2,1,0:T(8,128)(2,1)}, u32[]{:S(2)}, u32[]{:S(2)}) %collective-permute-start.28) | collective-permute-done | bytes 262176 | tf_op jit(solution)/shard_map/ppermute | solution.py:238
  212.7 0.9 copy-done.7
  213.7 0.9 copy-done.9
  214.6 4.2 %phase.3 = (bf16[2,4,128,512]{3,2,1,0:T(8,128)(2,1)S(1)}, bf16[2,4,128,512]{3,2,1,0:T(8,128)(2,1)S(1)}) custom-call(s32[1]{0:T(128)} %bitcast.me_ref, bf16[1024,512]{1,0:T(8,128)(2,1)S(1)} %bitcast.22, f32[4,128,512]{2,1,0:T(8,128)} %get-tuple-element.78.cosine_ref, f32[4,128,512]{2,1,0:T(8,128)} %get-tuple-element.77.sine_ref, ...), custom_call_target="tpu_custom_call" | custom-call | flops 2147483648 | bytes 4194304 | tf_op jit(solution)/shard_map/phase/pallas_call | solution.py:171
  218.8 9.3 %mix.1 = bf16[128,2,4,16,128]{4,3,2,1,0:T(8,128)(2,1)} custom-call(f32[4,4]{1,0:T(4,128)S(1)} %get-tuple-element.80.up_ref, f32[4,4]{1,0:T(4,128)S(1)} %get-tuple-element.79.down_ref, f32[128,512]{1,0:T(8,128)S(1)} %copy-done.2, bf16[2,4,128,512]{3,2,1,0:T(8,128)(2,1)} %collective-permute-done.14.refs_0_, ...), custom_call_target="tpu_custom_call" | custom-call | flops 20971520 | bytes 10485760 | tf_op jit(solution)/shard_map/mix/pallas_call | solution.py:218
  (51 shorter events, 2.3 us)
Async XLA Ops:
  0.0 1.2 copy-start
  7.7 7.2 %collective-permute-start = (bf16[2,128,512]{2,1,0:T(8,128)(2,1)S(1)}, bf16[2,128,512]{2,1,0:T(8,128)(2,1)S(1)}, u32[]{:S(2)}, u32[]{:S(2)}) collective-permute-start(bf16[2,128,512]{2,1,0:T(8,128)(2,1)S(1)} %get-tuple-element.42), channel_id=1, source_target_pairs={{0,1},{1,0},{2,3},{3,2},{4,5},{5,4},{6,7},{7,6},{8,9},{9,8},{10,11... | collective-permute-start | bytes 786440 | tf_op jit(solution)/shard_map/ppermute | solution.py:238
  8.9 14.5 %collective-permute-start.1 = (bf16[2,128,512]{2,1,0:T(8,128)(2,1)S(1)}, bf16[2,128,512]{2,1,0:T(8,128)(2,1)S(1)}, u32[]{:S(2)}, u32[]{:S(2)}) collective-permute-start(bf16[2,128,512]{2,1,0:T(8,128)(2,1)S(1)} %get-tuple-element.43), channel_id=1, source_target_pairs={{0,2},{1,3},{2,0},{3,1},{4,6},{5,7},{6,4},{7,5},{8,10},{9,11},{10,... | collective-permute-start | bytes 786440 | tf_op jit(solution)/shard_map/ppermute | solution.py:238
  9.1 26.7 %collective-permute-start.2 = (bf16[2,128,512]{2,1,0:T(8,128)(2,1)}, bf16[2,128,512]{2,1,0:T(8,128)(2,1)S(1)}, u32[]{:S(2)}, u32[]{:S(2)}) collective-permute-start(bf16[2,128,512]{2,1,0:T(8,128)(2,1)} %get-tuple-element.44), channel_id=1, source_target_pairs={{0,3},{1,2},{2,1},{3,0},{4,7},{5,6},{6,5},{7,4},{8,11},{9,10},{10,... | collective-permute-start | bytes 786440 | tf_op jit(solution)/shard_map/ppermute | solution.py:238
  10.3 27.5 %collective-permute-start.3 = (bf16[2,128,512]{2,1,0:T(8,128)(2,1)}, bf16[2,128,512]{2,1,0:T(8,128)(2,1)S(1)}, u32[]{:S(2)}, u32[]{:S(2)}) collective-permute-start(bf16[2,128,512]{2,1,0:T(8,128)(2,1)} %get-tuple-element.45), channel_id=1, source_target_pairs={{0,4},{1,5},{2,6},{3,7},{4,0},{5,1},{6,2},{7,3},{8,12},{9,13},{10,... | collective-permute-start | bytes 786440 | tf_op jit(solution)/shard_map/ppermute | solution.py:238
  12.6 31.5 %collective-permute-start.4 = (bf16[2,128,512]{2,1,0:T(8,128)(2,1)}, bf16[2,128,512]{2,1,0:T(8,128)(2,1)S(1)}, u32[]{:S(2)}, u32[]{:S(2)}) collective-permute-start(bf16[2,128,512]{2,1,0:T(8,128)(2,1)} %get-tuple-element.46), channel_id=1, source_target_pairs={{0,5},{1,4},{2,7},{3,6},{4,1},{5,0},{6,3},{7,2},{8,13},{9,12},{10,... | collective-permute-start | bytes 786440 | tf_op jit(solution)/shard_map/ppermute | solution.py:238
  14.8 35.9 %collective-permute-start.5 = (bf16[2,128,512]{2,1,0:T(8,128)(2,1)S(1)}, bf16[2,128,512]{2,1,0:T(8,128)(2,1)S(1)}, u32[]{:S(2)}, u32[]{:S(2)}) collective-permute-start(bf16[2,128,512]{2,1,0:T(8,128)(2,1)S(1)} %get-tuple-element.47), channel_id=1, source_target_pairs={{0,6},{1,7},{2,4},{3,5},{4,2},{5,3},{6,0},{7,1},{8,14},{9,15},{10,... | collective-permute-start | bytes 786440 | tf_op jit(solution)/shard_map/ppermute | solution.py:238
  23.4 36.1 %collective-permute-start.6 = (bf16[2,128,512]{2,1,0:T(8,128)(2,1)S(1)}, bf16[2,128,512]{2,1,0:T(8,128)(2,1)}, u32[]{:S(2)}, u32[]{:S(2)}) collective-permute-start(bf16[2,128,512]{2,1,0:T(8,128)(2,1)S(1)} %get-tuple-element.48), channel_id=1, source_target_pairs={{0,7},{1,6},{2,5},{3,4},{4,3},{5,2},{6,1},{7,0},{8,15},{9,14},{10,... | collective-permute-start | bytes 786440 | tf_op jit(solution)/shard_map/ppermute | solution.py:238
  23.4 6.5 %copy-start.1 = (bf16[2,512,512]{2,1,0:T(8,128)(2,1)S(1)}, bf16[2,512,512]{2,1,0:T(8,128)(2,1)}, u32[]{:S(2)}) copy-start(bf16[2,512,512]{2,1,0:T(8,128)(2,1)} %param.8) | copy-start | bytes 3145732
  35.8 31.2 %collective-permute-start.15 = (bf16[2,128,512]{2,1,0:T(8,128)(2,1)S(1)}, bf16[2,128,512]{2,1,0:T(8,128)(2,1)S(1)}, u32[]{:S(2)}, u32[]{:S(2)}) collective-permute-start(bf16[2,128,512]{2,1,0:T(8,128)(2,1)S(1)} %get-tuple-element.60), channel_id=1, source_target_pairs={{0,1},{1,0},{2,3},{3,2},{4,5},{5,4},{6,7},{7,6},{8,9},{9,8},{10,11... | collective-permute-start | bytes 786440 | tf_op jit(solution)/shard_map/ppermute | solution.py:238
  37.8 32.2 %collective-permute-start.16 = (bf16[2,128,512]{2,1,0:T(8,128)(2,1)S(1)}, bf16[2,128,512]{2,1,0:T(8,128)(2,1)S(1)}, u32[]{:S(2)}, u32[]{:S(2)}) collective-permute-start(bf16[2,128,512]{2,1,0:T(8,128)(2,1)S(1)} %get-tuple-element.61), channel_id=1, source_target_pairs={{0,2},{1,3},{2,0},{3,1},{4,6},{5,7},{6,4},{7,5},{8,10},{9,11},{10,... | collective-permute-start | bytes 786440 | tf_op jit(solution)/shard_map/ppermute | solution.py:238
  44.1 25.9 %collective-permute-start.17 = (bf16[2,128,512]{2,1,0:T(8,128)(2,1)S(1)}, bf16[2,128,512]{2,1,0:T(8,128)(2,1)S(1)}, u32[]{:S(2)}, u32[]{:S(2)}) collective-permute-start(bf16[2,128,512]{2,1,0:T(8,128)(2,1)S(1)} %get-tuple-element.62), channel_id=1, source_target_pairs={{0,3},{1,2},{2,1},{3,0},{4,7},{5,6},{6,5},{7,4},{8,11},{9,10},{10,... | collective-permute-start | bytes 786440 | tf_op jit(solution)/shard_map/ppermute | solution.py:238
  50.7 23.5 %collective-permute-start.18 = (bf16[2,128,512]{2,1,0:T(8,128)(2,1)S(1)}, bf16[2,128,512]{2,1,0:T(8,128)(2,1)S(1)}, u32[]{:S(2)}, u32[]{:S(2)}) collective-permute-start(bf16[2,128,512]{2,1,0:T(8,128)(2,1)S(1)} %get-tuple-element.63), channel_id=1, source_target_pairs={{0,4},{1,5},{2,6},{3,7},{4,0},{5,1},{6,2},{7,3},{8,12},{9,13},{10,... | collective-permute-start | bytes 786440 | tf_op jit(solution)/shard_map/ppermute | solution.py:238
  59.5 39.0 %collective-permute-start.19 = (bf16[2,128,512]{2,1,0:T(8,128)(2,1)S(1)}, bf16[2,128,512]{2,1,0:T(8,128)(2,1)S(1)}, u32[]{:S(2)}, u32[]{:S(2)}) collective-permute-start(bf16[2,128,512]{2,1,0:T(8,128)(2,1)S(1)} %get-tuple-element.64), channel_id=1, source_target_pairs={{0,5},{1,4},{2,7},{3,6},{4,1},{5,0},{6,3},{7,2},{8,13},{9,12},{10,... | collective-permute-start | bytes 786440 | tf_op jit(solution)/shard_map/ppermute | solution.py:238
  59.5 15.0 %copy-start.10 = (f32[128,4,512]{2,1,0:T(4,128)S(1)}, f32[128,4,512]{2,1,0:T(4,128)}, u32[]{:S(2)}) copy-start(f32[128,4,512]{2,1,0:T(4,128)} %param.9) | copy-start | bytes 3145732
  67.0 45.7 %collective-permute-start.20 = (bf16[2,128,512]{2,1,0:T(8,128)(2,1)S(1)}, bf16[2,128,512]{2,1,0:T(8,128)(2,1)S(1)}, u32[]{:S(2)}, u32[]{:S(2)}) collective-permute-start(bf16[2,128,512]{2,1,0:T(8,128)(2,1)S(1)} %get-tuple-element.65), channel_id=1, source_target_pairs={{0,6},{1,7},{2,4},{3,5},{4,2},{5,3},{6,0},{7,1},{8,14},{9,15},{10,... | collective-permute-start | bytes 786440 | tf_op jit(solution)/shard_map/ppermute | solution.py:238
  70.0 54.5 %collective-permute-start.21 = (bf16[2,128,512]{2,1,0:T(8,128)(2,1)S(1)}, bf16[2,128,512]{2,1,0:T(8,128)(2,1)S(1)}, u32[]{:S(2)}, u32[]{:S(2)}) collective-permute-start(bf16[2,128,512]{2,1,0:T(8,128)(2,1)S(1)} %get-tuple-element.66), channel_id=1, source_target_pairs={{0,7},{1,6},{2,5},{3,4},{4,3},{5,2},{6,1},{7,0},{8,15},{9,14},{10,... | collective-permute-start | bytes 786440 | tf_op jit(solution)/shard_map/ppermute | solution.py:238
  70.0 59.4 %collective-permute-start.10 = (bf16[2,128,512]{2,1,0:T(8,128)(2,1)S(1)}, bf16[2,128,512]{2,1,0:T(8,128)(2,1)S(1)}, u32[]{:S(2)}, u32[]{:S(2)}) collective-permute-start(bf16[2,128,512]{2,1,0:T(8,128)(2,1)S(1)} %get-tuple-element.53), channel_id=1, source_target_pairs={{0,4},{1,5},{2,6},{3,7},{4,0},{5,1},{6,2},{7,3},{8,12},{9,13},{10,... | collective-permute-start | bytes 786440 | tf_op jit(solution)/shard_map/ppermute | solution.py:238
  74.2 60.8 %collective-permute-start.11 = (bf16[2,128,512]{2,1,0:T(8,128)(2,1)S(1)}, bf16[2,128,512]{2,1,0:T(8,128)(2,1)S(1)}, u32[]{:S(2)}, u32[]{:S(2)}) collective-permute-start(bf16[2,128,512]{2,1,0:T(8,128)(2,1)S(1)} %get-tuple-element.54), channel_id=1, source_target_pairs={{0,5},{1,4},{2,7},{3,6},{4,1},{5,0},{6,3},{7,2},{8,13},{9,12},{10,... | collective-permute-start | bytes 786440 | tf_op jit(solution)/shard_map/ppermute | solution.py:238
  98.5 46.8 %collective-permute-start.12 = (bf16[2,128,512]{2,1,0:T(8,128)(2,1)S(1)}, bf16[2,128,512]{2,1,0:T(8,128)(2,1)S(1)}, u32[]{:S(2)}, u32[]{:S(2)}) collective-permute-start(bf16[2,128,512]{2,1,0:T(8,128)(2,1)S(1)} %get-tuple-element.55), channel_id=1, source_target_pairs={{0,6},{1,7},{2,4},{3,5},{4,2},{5,3},{6,0},{7,1},{8,14},{9,15},{10,... | collective-permute-start | bytes 786440 | tf_op jit(solution)/shard_map/ppermute | solution.py:238
  112.7 36.4 %collective-permute-start.13 = (bf16[2,128,512]{2,1,0:T(8,128)(2,1)S(1)}, bf16[2,128,512]{2,1,0:T(8,128)(2,1)S(1)}, u32[]{:S(2)}, u32[]{:S(2)}) collective-permute-start(bf16[2,128,512]{2,1,0:T(8,128)(2,1)S(1)} %get-tuple-element.56), channel_id=1, source_target_pairs={{0,7},{1,6},{2,5},{3,4},{4,3},{5,2},{6,1},{7,0},{8,15},{9,14},{10,... | collective-permute-start | bytes 786440 | tf_op jit(solution)/shard_map/ppermute | solution.py:238
  124.5 24.6 %collective-permute-start.7 = (bf16[2,128,512]{2,1,0:T(8,128)(2,1)S(1)}, bf16[2,128,512]{2,1,0:T(8,128)(2,1)S(1)}, u32[]{:S(2)}, u32[]{:S(2)}) collective-permute-start(bf16[2,128,512]{2,1,0:T(8,128)(2,1)S(1)} %get-tuple-element.50), channel_id=1, source_target_pairs={{0,1},{1,0},{2,3},{3,2},{4,5},{5,4},{6,7},{7,6},{8,9},{9,8},{10,11... | collective-permute-start | bytes 786440 | tf_op jit(solution)/shard_map/ppermute | solution.py:238
  129.4 19.7 %collective-permute-start.8 = (bf16[2,128,512]{2,1,0:T(8,128)(2,1)S(1)}, bf16[2,128,512]{2,1,0:T(8,128)(2,1)S(1)}, u32[]{:S(2)}, u32[]{:S(2)}) collective-permute-start(bf16[2,128,512]{2,1,0:T(8,128)(2,1)S(1)} %get-tuple-element.51), channel_id=1, source_target_pairs={{0,2},{1,3},{2,0},{3,1},{4,6},{5,7},{6,4},{7,5},{8,10},{9,11},{10,... | collective-permute-start | bytes 786440 | tf_op jit(solution)/shard_map/ppermute | solution.py:238
  135.1 14.0 %collective-permute-start.9 = (bf16[2,128,512]{2,1,0:T(8,128)(2,1)S(1)}, bf16[2,128,512]{2,1,0:T(8,128)(2,1)S(1)}, u32[]{:S(2)}, u32[]{:S(2)}) collective-permute-start(bf16[2,128,512]{2,1,0:T(8,128)(2,1)S(1)} %get-tuple-element.52), channel_id=1, source_target_pairs={{0,3},{1,2},{2,1},{3,0},{4,7},{5,6},{6,5},{7,4},{8,11},{9,10},{10,... | collective-permute-start | bytes 786440 | tf_op jit(solution)/shard_map/ppermute | solution.py:238
  145.3 13.6 %copy-start.3 = (bf16[2,128,512]{2,1,0:T(8,128)(2,1)}, bf16[2,128,512]{2,1,0:T(8,128)(2,1)S(1)}, u32[]{:S(2)}) copy-start(bf16[2,128,512]{2,1,0:T(8,128)(2,1)S(1)} %get-tuple-element.74) | copy-start | bytes 786436
  145.3 13.6 %copy-start.4 = (bf16[2,128,512]{2,1,0:T(8,128)(2,1)}, bf16[2,128,512]{2,1,0:T(8,128)(2,1)S(1)}, u32[]{:S(2)}) copy-start(bf16[2,128,512]{2,1,0:T(8,128)(2,1)S(1)} %get-tuple-element.73) | copy-start | bytes 786436
  145.3 15.7 %copy-start.5 = (bf16[2,128,512]{2,1,0:T(8,128)(2,1)}, bf16[2,128,512]{2,1,0:T(8,128)(2,1)S(1)}, u32[]{:S(2)}) copy-start(bf16[2,128,512]{2,1,0:T(8,128)(2,1)S(1)} %get-tuple-element.72) | copy-start | bytes 786436
  145.3 17.8 %copy-start.8 = (bf16[2,128,512]{2,1,0:T(8,128)(2,1)}, bf16[2,128,512]{2,1,0:T(8,128)(2,1)S(1)}, u32[]{:S(2)}) copy-start(bf16[2,128,512]{2,1,0:T(8,128)(2,1)S(1)} %get-tuple-element.67.refs_0_) | copy-start | bytes 786436
  145.3 20.1 %copy-start.11 = (f32[16,4]{0,1:T(4,128)S(1)}, f32[16,4]{0,1:T(4,128)}, u32[]{:S(2)}) copy-start(f32[16,4]{0,1:T(4,128)} %param.10) | copy-start | bytes 772
  145.3 17.7 %collective-permute-start.22 = (bf16[2,128,512]{2,1,0:T(8,128)(2,1)S(1)}, bf16[2,128,512]{2,1,0:T(8,128)(2,1)S(1)}, u32[]{:S(2)}, u32[]{:S(2)}) collective-permute-start(bf16[2,128,512]{2,1,0:T(8,128)(2,1)S(1)} %get-tuple-element.68), channel_id=1, source_target_pairs={{0,1},{1,0},{2,3},{3,2},{4,5},{5,4},{6,7},{7,6},{8,9},{9,8},{10,11... | collective-permute-start | bytes 786440 | tf_op jit(solution)/shard_map/ppermute | solution.py:238
  153.0 65.8 %copy-start.2 = (f32[128,512]{1,0:T(8,128)S(1)}, f32[128,512]{1,0:T(8,128)}, u32[]{:S(2)}) copy-start(f32[128,512]{1,0:T(8,128)} %weight_ref.1) | copy-start | bytes 786436
  153.1 65.8 %collective-permute-start.14 = (bf16[2,4,128,512]{3,2,1,0:T(8,128)(2,1)S(1)}, bf16[2,4,128,512]{3,2,1,0:T(8,128)(2,1)}, u32[]{:S(2)}, u32[]{:S(2)}) collective-permute-start(bf16[2,4,128,512]{3,2,1,0:T(8,128)(2,1)S(1)} %get-tuple-element.57.refs_4_), channel_id=1, source_target_pairs={{0,8},{8,16},{16,24},{1,9},{9,17},{17,25},{2,10},{10,18},{18,26},{... | collective-permute-start | bytes 3145736 | tf_op jit(solution)/shard_map/ppermute | solution.py:245
  158.9 59.9 %collective-permute-start.29 = (bf16[2,4,128,512]{3,2,1,0:T(8,128)(2,1)S(1)}, bf16[2,4,128,512]{3,2,1,0:T(8,128)(2,1)}, u32[]{:S(2)}, u32[]{:S(2)}) collective-permute-start(bf16[2,4,128,512]{3,2,1,0:T(8,128)(2,1)S(1)} %get-tuple-element.58.refs_1_), channel_id=1, source_target_pairs={{8,0},{16,8},{24,16},{9,1},{17,9},{25,17},{10,2},{18,10},{26,18},{... | collective-permute-start | bytes 3145736 | tf_op jit(solution)/shard_map/ppermute | solution.py:245
  161.0 12.2 %collective-permute-start.23 = (bf16[2,128,512]{2,1,0:T(8,128)(2,1)}, bf16[2,128,512]{2,1,0:T(8,128)(2,1)}, u32[]{:S(2)}, u32[]{:S(2)}) collective-permute-start(bf16[2,128,512]{2,1,0:T(8,128)(2,1)} %get-tuple-element.69), channel_id=1, source_target_pairs={{0,2},{1,3},{2,0},{3,1},{4,6},{5,7},{6,4},{7,5},{8,10},{9,11},{10,... | collective-permute-start | bytes 786440 | tf_op jit(solution)/shard_map/ppermute | solution.py:238
  161.1 17.1 %collective-permute-start.24 = (bf16[2,128,512]{2,1,0:T(8,128)(2,1)}, bf16[2,128,512]{2,1,0:T(8,128)(2,1)}, u32[]{:S(2)}, u32[]{:S(2)}) collective-permute-start(bf16[2,128,512]{2,1,0:T(8,128)(2,1)} %get-tuple-element.70), channel_id=1, source_target_pairs={{0,3},{1,2},{2,1},{3,0},{4,7},{5,6},{6,5},{7,4},{8,11},{9,10},{10,... | collective-permute-start | bytes 786440 | tf_op jit(solution)/shard_map/ppermute | solution.py:238
  163.1 0.7 copy-start.6
  163.8 19.1 %collective-permute-start.25 = (bf16[2,128,512]{2,1,0:T(8,128)(2,1)}, bf16[2,128,512]{2,1,0:T(8,128)(2,1)}, u32[]{:S(2)}, u32[]{:S(2)}) collective-permute-start(bf16[2,128,512]{2,1,0:T(8,128)(2,1)} %get-tuple-element.71), channel_id=1, source_target_pairs={{0,4},{1,5},{2,6},{3,7},{4,0},{5,1},{6,2},{7,3},{8,12},{9,13},{10,... | collective-permute-start | bytes 786440 | tf_op jit(solution)/shard_map/ppermute | solution.py:238
  173.2 28.5 %collective-permute-start.26 = (bf16[2,128,512]{2,1,0:T(8,128)(2,1)}, bf16[2,128,512]{2,1,0:T(8,128)(2,1)}, u32[]{:S(2)}, u32[]{:S(2)}) collective-permute-start(bf16[2,128,512]{2,1,0:T(8,128)(2,1)} %copy-done.5), channel_id=1, source_target_pairs={{0,5},{1,4},{2,7},{3,6},{4,1},{5,0},{6,3},{7,2},{8,13},{9,12},{10,... | collective-permute-start | bytes 786440 | tf_op jit(solution)/shard_map/ppermute | solution.py:238
  178.2 32.0 %collective-permute-start.27 = (bf16[2,128,512]{2,1,0:T(8,128)(2,1)}, bf16[2,128,512]{2,1,0:T(8,128)(2,1)}, u32[]{:S(2)}, u32[]{:S(2)}) collective-permute-start(bf16[2,128,512]{2,1,0:T(8,128)(2,1)} %copy-done.4), channel_id=1, source_target_pairs={{0,6},{1,7},{2,4},{3,5},{4,2},{5,3},{6,0},{7,1},{8,14},{9,15},{10,... | collective-permute-start | bytes 786440 | tf_op jit(solution)/shard_map/ppermute | solution.py:238
  182.9 29.8 %collective-permute-start.28 = (bf16[2,128,512]{2,1,0:T(8,128)(2,1)}, bf16[2,128,512]{2,1,0:T(8,128)(2,1)}, u32[]{:S(2)}, u32[]{:S(2)}) collective-permute-start(bf16[2,128,512]{2,1,0:T(8,128)(2,1)} %copy-done.3), channel_id=1, source_target_pairs={{0,7},{1,6},{2,5},{3,4},{4,3},{5,2},{6,1},{7,0},{8,15},{9,14},{10,... | collective-permute-start | bytes 786440 | tf_op jit(solution)/shard_map/ppermute | solution.py:238
  212.7 1.0 copy-start.7
  213.7 0.9 copy-start.9
where the time goes:
time: 231 us; the launch traced here: 228 us
  waiting for transfers between devices  119 us (52%)
  starting transfers between devices  48.1 us (21%)
  Pallas kernels  45.1 us (20%)
  local copies, waits for them, and re-layouts  15.3 us (7%)
    ppermute x28, waiting for transfers between devices, exchanged(): result[s] = lax.ppermute(slabs[s], axis, [(i, i ^ s) for i in range(count)])  119 us
    ppermute x28, starting transfers between devices, exchanged(): result[s] = lax.ppermute(slabs[s], axis, [(i, i ^ s) for i in range(count)])  40.2 us
    pallas_call x2, Pallas kernels, left_call(): pl.pallas_call(functools.partial(left_kernel, ranks), grid=(kinds,), in_s...  15.5 us
    pallas_call x2, Pallas kernels, right_call(): pl.pallas_call(functools.partial(right_kernel, ranks, states), grid=(rows...  12.2 us
    pallas_call x1, Pallas kernels, mix_call(): pl.pallas_call(mix_kernel, grid=(rows // block,), in_specs=[SMEM, SMEM, p...  9.34 us
    pallas_call x2, Pallas kernels, phase_call(): pl.pallas_call(functools.partial(phase_kernel, ranks), grid=(rows // bloc...  8.13 us
    ppermute x2, starting transfers between devices, neighbour(): return lax.ppermute(edge, axis, pairs)  7.92 us
    reshape x1, local copies, waits for them, and re-layouts, per_device(): first = first_propagator.reshape(2 * whole, whole).T  6.51 us
  transfers between devices with their start and end apart: 30, of which 17 were waited for; matrix products, arithmetic and copies ran while one was open for 5% of the time, Pallas kernels for 13%

commit v1 on v0

--- a/solution.py
+++ b/solution.py
@@ -25,8 +25,10 @@
 
 
 def right_kernel(ranks, states, me_ref, second_ref, *refs):
-    kinds = len(refs) - 2 - ranks
-    packets, outs, wide, slabs = refs[:kinds], refs[kinds:-2], refs[-2], refs[-1]
+    half = ranks // 2
+    kinds = len(refs) - 3 - half
+    packets, near, far = refs[:kinds], refs[kinds], refs[kinds + 1 : -2]
+    wide, slabs = refs[-2:]
     me = me_ref[0]
     rows = packets[0].shape[0]
     group = packets[0].shape[2]
@@ -56,14 +58,16 @@
                     slabs[j * cuts + p, :, c * piece : (c + 1) * piece] = product[
                         first : first + rows, p * piece : (p + 1) * piece
                     ]
-        for s, out in enumerate(outs):
-            out[n] = slabs[me ^ s]
+        near[:, n] = slabs[pl.ds(me & half, half)]
+        for s, out in enumerate(far):
+            out[n] = slabs[me ^ (half + s)]
 
 
 def right_call(me, second, view, chosen, ranks, states, piece):
     rows, _, _, group, _ = view.shape
     width = second.shape[1]
     block = rows // 2
+    half = ranks // 2
     kinds = len(chosen)
     return pl.pallas_call(
         functools.partial(right_kernel, ranks, states),
@@ -73,8 +77,10 @@
             pl.BlockSpec((block, 2, None, group, LANES), lambda i, k=k: (i, 0, k, 0, 0))
             for k in chosen
         ],
-        out_specs=[pl.BlockSpec((kinds, block, 2 * piece), lambda i: (0, i, 0))] * ranks,
-        out_shape=[jax.ShapeDtypeStruct((kinds, rows, 2 * piece), jnp.bfloat16)] * ranks,
+        out_specs=[pl.BlockSpec((half, kinds, block, 2 * piece), lambda i: (0, 0, i, 0))]
+        + [pl.BlockSpec((kinds, block, 2 * piece), lambda i: (0, i, 0))] * half,
+        out_shape=[jax.ShapeDtypeStruct((half, kinds, rows, 2 * piece), jnp.bfloat16)]
+        + [jax.ShapeDtypeStruct((kinds, rows, 2 * piece), jnp.bfloat16)] * half,
         scratch_shapes=[
             pltpu.VMEM((block * 2 * group, LANES), jnp.float32),
             pltpu.VMEM((ranks, block, 2 * piece), jnp.bfloat16),
@@ -87,36 +93,47 @@
     )(me, second, *([view] * kinds))
 
 
+def sources(me, parts):
+    near, far = parts[0], parts[1:]
+    half = len(far)
+    for low in range(half):
+        yield (me & half) + low, near[low]
+    for s, part in enumerate(far):
+        yield me ^ (half + s), part[...]
+
+
 def left_kernel(ranks, me_ref, first_ref, *refs):
-    ins, outs, lines, slabs = refs[:ranks], refs[ranks:-2], refs[-2], refs[-1]
+    half = ranks // 2
+    ins, (near, *far), (lines, slabs) = refs[: half + 1], refs[half + 1 : -2], refs[-2:]
     me = me_ref[0]
-    rows, wide = ins[0].shape
+    _, rows, wide = near.shape
     piece = wide // 2
     whole = ranks * rows
-    for s, part in enumerate(ins):
-        value = part[...]
-        first = pl.multiple_of((me ^ s) * rows, rows)
+    for source, value in sources(me, ins):
+        first = pl.multiple_of(source * rows, rows)
         lines[pl.ds(first, rows), :] = value
         lines[pl.ds(first + whole, rows), :] = jnp.concatenate(
             [-value[:, piece:], value[:, :piece]], 1
         )
     product = jnp.dot(first_ref[...], lines[...], preferred_element_type=jnp.float32)
     slabs[...] = product.astype(jnp.bfloat16).reshape(ranks, rows, wide)
-    for s, out in enumerate(outs):
-        out[...] = slabs[me ^ s]
+    near[...] = slabs[pl.ds(me & half, half)]
+    for s, out in enumerate(far):
+        out[...] = slabs[me ^ (half + s)]
 
 
 def left_call(me, first, slabs):
-    ranks = len(slabs)
-    kinds, rows, wide = slabs[0].shape
+    half, kinds, rows, wide = slabs[0].shape
+    ranks = 2 * half
     whole = ranks * rows
-    spec = pl.BlockSpec((None, rows, wide), lambda i: (i, 0, 0))
+    specs = [pl.BlockSpec((half, None, rows, wide), lambda i: (0, i, 0, 0))]
+    specs += [pl.BlockSpec((None, rows, wide), lambda i: (i, 0, 0))] * half
     return pl.pallas_call(
         functools.partial(left_kernel, ranks),
         grid=(kinds,),
-        in_specs=[SMEM, pl.BlockSpec(first.shape, lambda i: (0, 0))] + [spec] * ranks,
-        out_specs=[spec] * ranks,
-        out_shape=[jax.ShapeDtypeStruct(slabs[0].shape, jnp.bfloat16)] * ranks,
+        in_specs=[SMEM, pl.BlockSpec(first.shape, lambda i: (0, 0))] + specs,
+        out_specs=specs,
+        out_shape=[jax.ShapeDtypeStruct(x.shape, jnp.bfloat16) for x in slabs],
         scratch_shapes=[
             pltpu.VMEM((2 * whole, wide), jnp.bfloat16),
             pltpu.VMEM((ranks, rows, wide), jnp.bfloat16),
@@ -130,14 +147,15 @@
 
 
 def phase_kernel(ranks, me_ref, second_ref, cosine_ref, sine_ref, *refs):
-    ins, outs, slabs = refs[:ranks], refs[ranks:-1], refs[-1]
+    half = ranks // 2
+    ins, outs, slabs = refs[: half + 1], refs[half + 1 : -1], refs[-1]
     me = me_ref[0]
     states, rows, width = cosine_ref.shape
     piece = slabs.shape[2] // 2
     cuts = width // piece
     for n, out in enumerate(outs):
-        for s, part in enumerate(ins):
-            slabs[me ^ s] = part[n]
+        for source, value in sources(me, [ins[0].at[:, n]] + [x.at[n] for x in ins[1:]]):
+            slabs[source] = value
         pairs = []
         for j in range(states):
             real, imag = (
@@ -163,8 +181,8 @@
 
 
 def phase_call(me, second, cosine, sine, slabs):
-    ranks = len(slabs)
-    kinds, rows, wide = slabs[0].shape
+    half, kinds, rows, wide = slabs[0].shape
+    ranks = 2 * half
     states, _, width = cosine.shape
     block = rows // 2
     table = pl.BlockSpec((states, block, width), lambda i: (0, i, 0))
@@ -172,7 +190,8 @@
         functools.partial(phase_kernel, ranks),
         grid=(rows // block,),
         in_specs=[SMEM, pl.BlockSpec(second.shape, lambda i: (0, 0)), table, table]
-        + [pl.BlockSpec((kinds, block, wide), lambda i: (0, i, 0))] * ranks,
+        + [pl.BlockSpec((half, kinds, block, wide), lambda i: (0, 0, i, 0))]
+        + [pl.BlockSpec((kinds, block, wide), lambda i: (0, i, 0))] * half,
         out_specs=[pl.BlockSpec((2, states, block, width), lambda i: (0, 0, i, 0))] * kinds,
         out_shape=[jax.ShapeDtypeStruct((2, states, rows, width), jnp.bfloat16)] * kinds,
         scratch_shapes=[pltpu.VMEM((ranks, block, wide), jnp.bfloat16)],
@@ -233,10 +252,14 @@
 
 def exchanged(slabs, axis):
     count = lax.axis_size(axis)
-    result = [slabs[0]] + [None] * (count - 1)
-    for s in reversed(range(1, count)):
-        result[s] = lax.ppermute(slabs[s], axis, [(i, i ^ s) for i in range(count)])
-    return result
+    half = count // 2
+    groups = [list(range(half)), list(range(half, count))]
+    far = [
+        lax.ppermute(slab, axis, [(i, i ^ (half + s)) for i in range(count)])
+        for s, slab in enumerate(slabs[1:])
+    ]
+    near = lax.all_to_all(slabs[0], axis, 0, 0, axis_index_groups=groups, tiled=True)
+    return [near] + far
 
 
 def neighbour(edge, axis, step):
@@ -258,7 +281,7 @@
     view = view.reshape(rows, 2, blocks, tiles * states, LANES)
     edges = sorted({0, blocks - 1})
     inner = [k for k in range(blocks) if k not in edges]
-    chunks = [c for c in (edges, inner) if c]
+    chunks = [[k] for k in edges + inner]
 
     halves = [right_call(me, second, view, c, ranks, states, piece) for c in chunks]
     lines = [exchanged(h, "rad") for h in halves]

time: 231 us -> 299 us (1.29)
  starting transfers between devices: 48.1 us -> 92 us
  local copies, waits for them, and re-layouts: 15.3 us -> 40.8 us
  waiting for transfers between devices: 119 us -> 103 us
  Pallas kernels: 45.1 us -> 57.9 us
    all_to_all x0 -> x8, starting transfers between devices: none -> 31.2 us  [exchanged(): lax.all_to_all(slabs[0], axis, 0, 0, axis_index_groups=groups, tiled=True)]
    unnamed x26 -> x100, local copies, waits for them, and re-layouts: 4.04 us -> 28.9 us
    ppermute x28 -> x32, waiting for transfers between devices: 119 us -> 95.7 us  [exchanged(): lax.ppermute(slab, axis, [(i, i ^ half + s) for i in range(count)])]
    ppermute x2, starting transfers between devices: 7.92 us -> 15.1 us  [neighbour(): return lax.ppermute(edge, axis, pairs)]
    all_to_all x0 -> x8, waiting for transfers between devices: none -> 6.87 us  [exchanged(): lax.all_to_all(slabs[0], axis, 0, 0, axis_index_groups=groups, tiled=True)]
    pallas_call x2 -> x4, Pallas kernels: 15.5 us -> 21.6 us  [left_call(): pl.pallas_call(functools.partial(left_kernel, ranks), grid=(kinds,), in_s...]
    ppermute x28 -> x32, starting transfers between devices: 40.2 us -> 45.7 us  [exchanged(): lax.ppermute(slab, axis, [(i, i ^ half + s) for i in range(count)])]
    pallas_call x2 -> x4, Pallas kernels: 12.2 us -> 16.5 us  [right_call(): pl.pallas_call(functools.partial(right_kernel, ranks, states), grid=(rows...]
  transfers between devices with their start and end apart: 30 -> 42, of which waited for: 17 -> 23; matrix products, arithmetic and copies ran while one was open for 5% -> 4% of each run, Pallas kernels for 13% -> 15%
where the time goes in v1:
time: 299 us; the launch traced here: 294 us
  waiting for transfers between devices  103 us (34%)
  starting transfers between devices  92 us (31%)
  Pallas kernels  57.9 us (19%)
  local copies, waits for them, and re-layouts  40.8 us (14%)
    ppermute x32, waiting for transfers between devices, exchanged(): lax.ppermute(slab, axis, [(i, i ^ half + s) for i in range(count)])  95.7 us
    ppermute x32, starting transfers between devices, exchanged(): lax.ppermute(slab, axis, [(i, i ^ half + s) for i in range(count)])  45.7 us
    all_to_all x8, starting transfers between devices, exchanged(): lax.all_to_all(slabs[0], axis, 0, 0, axis_index_groups=groups, tiled=True)  31.2 us
    unnamed x100, local copies, waits for them, and re-layouts  28.9 us
    pallas_call x4, Pallas kernels, left_call(): pl.pallas_call(functools.partial(left_kernel, ranks), grid=(kinds,), in_s...  21.6 us
    pallas_call x4, Pallas kernels, right_call(): pl.pallas_call(functools.partial(right_kernel, ranks, states), grid=(rows...  16.5 us
    ppermute x2, starting transfers between devices, neighbour(): return lax.ppermute(edge, axis, pairs)  15.1 us
    pallas_call x4, Pallas kernels, phase_call(): pl.pallas_call(functools.partial(phase_kernel, ranks), grid=(rows // bloc...  10.3 us
  transfers between devices with their start and end apart: 42, of which 23 were waited for; matrix products, arithmetic and copies ran while one was open for 4% of the time, Pallas kernels for 15%

profile of v1, /device:TPU:9, one launch (start us, length us, event | category | flops | bytes accessed | tf_op | source)
XLA Modules:
  0.0 294.3 jit_solution(9681759169231528058)
XLA Ops:
  1.2 4.2 %right.7 = (bf16[4,1,128,512]{3,2,1,0:T(8,128)(2,1)}, bf16[1,128,512]{2,1,0:T(8,128)(2,1)S(1)}, bf16[1,128,512]{2,1,0:T(8,128)(2,1)S(1)}, bf16[1,128,512]{2,1,0:T(8,128)(2,1)S(1)}, bf16[1,128,512]{2,1,0:T(8,128)(2,1)S(1)}) custom-call(s32[1]{0:T(128)} %bitcast.me_ref, bf16[1024,512]{1,0:T(8,128)(2,1)S(1)} %bitcast.19, bf16[128,2,4,16,128]{4,3,2,1,0:T(8,128)(2,1)} %bitcast.27), custom_call_target="tpu_custom_call" | custom-call | flops 1073741824 | bytes 2097152 | tf_op jit(solution)/shard_map/right/pallas_call | solution.py:72
  8.0 3.7 %all-to-all-start.6 = ((bf16[4,1,128,512]{3,2,1,0:T(8,128)(2,1)}), bf16[4,1,128,512]{3,2,1,0:T(8,128)(2,1)S(1)}, u32[]{:S(2)}, u32[]{:S(2)}) async-start(bf16[4,1,128,512]{3,2,1,0:T(8,128)(2,1)} %get-tuple-element.75), calls=%async_computation.6 | async-start | bytes 1048576 | tf_op jit(solution)/shard_map/all_to_all | solution.py:261
  11.7 4.1 %right.6 = (bf16[4,1,128,512]{3,2,1,0:T(8,128)(2,1)}, bf16[1,128,512]{2,1,0:T(8,128)(2,1)S(1)}, bf16[1,128,512]{2,1,0:T(8,128)(2,1)S(1)}, bf16[1,128,512]{2,1,0:T(8,128)(2,1)S(1)}, bf16[1,128,512]{2,1,0:T(8,128)(2,1)S(1)}) custom-call(s32[1]{0:T(128)} %bitcast.me_ref, bf16[1024,512]{1,0:T(8,128)(2,1)S(1)} %bitcast.20, bf16[128,2,4,16,128]{4,3,2,1,0:T(8,128)(2,1)} %bitcast.28), custom_call_target="tpu_custom_call" | custom-call | flops 1073741824 | bytes 2097152 | tf_op jit(solution)/shard_map/right/pallas_call | solution.py:72
  15.8 4.1 %all-to-all-done.6.refs_0_ = bf16[4,1,128,512]{3,2,1,0:T(8,128)(2,1)S(1)} async-done(((bf16[4,1,128,512]{3,2,1,0:T(8,128)(2,1)}), bf16[4,1,128,512]{3,2,1,0:T(8,128)(2,1)S(1)}, u32[]{:S(2)}, u32[]{:S(2)}) %all-to-all-start.6) | async-done | bytes 524320 | tf_op jit(solution)/shard_map/all_to_all | solution.py:261
  19.9 3.5 %all-to-all-start.4 = ((bf16[4,1,128,512]{3,2,1,0:T(8,128)(2,1)}), bf16[4,1,128,512]{3,2,1,0:T(8,128)(2,1)S(1)}, u32[]{:S(2)}, u32[]{:S(2)}) async-start(bf16[4,1,128,512]{3,2,1,0:T(8,128)(2,1)} %get-tuple-element.65), calls=%async_computation.4 | async-start | bytes 1048576 | tf_op jit(solution)/shard_map/all_to_all | solution.py:261
  23.3 4.1 %right.5 = (bf16[4,1,128,512]{3,2,1,0:T(8,128)(2,1)}, bf16[1,128,512]{2,1,0:T(8,128)(2,1)S(1)}, bf16[1,128,512]{2,1,0:T(8,128)(2,1)S(1)}, bf16[1,128,512]{2,1,0:T(8,128)(2,1)S(1)}, bf16[1,128,512]{2,1,0:T(8,128)(2,1)S(1)}) custom-call(s32[1]{0:T(128)} %bitcast.me_ref, bf16[1024,512]{1,0:T(8,128)(2,1)S(1)} %bitcast.21, bf16[128,2,4,16,128]{4,3,2,1,0:T(8,128)(2,1)} %bitcast.29), custom_call_target="tpu_custom_call" | custom-call | flops 1073741824 | bytes 2097152 | tf_op jit(solution)/shard_map/right/pallas_call | solution.py:72
  30.2 3.9 %all-to-all-start.2 = ((bf16[4,1,128,512]{3,2,1,0:T(8,128)(2,1)}), bf16[4,1,128,512]{3,2,1,0:T(8,128)(2,1)S(1)}, u32[]{:S(2)}, u32[]{:S(2)}) async-start(bf16[4,1,128,512]{3,2,1,0:T(8,128)(2,1)} %get-tuple-element.55), calls=%async_computation.2 | async-start | bytes 1048576 | tf_op jit(solution)/shard_map/all_to_all | solution.py:261
  34.1 4.1 %right.4 = (bf16[4,1,128,512]{3,2,1,0:T(8,128)(2,1)}, bf16[1,128,512]{2,1,0:T(8,128)(2,1)S(1)}, bf16[1,128,512]{2,1,0:T(8,128)(2,1)S(1)}, bf16[1,128,512]{2,1,0:T(8,128)(2,1)S(1)}, bf16[1,128,512]{2,1,0:T(8,128)(2,1)S(1)}) custom-call(s32[1]{0:T(128)} %bitcast.me_ref, bf16[1024,512]{1,0:T(8,128)(2,1)S(1)} %bitcast.22, bf16[128,2,4,16,128]{4,3,2,1,0:T(8,128)(2,1)} %bitcast.30), custom_call_target="tpu_custom_call" | custom-call | flops 1073741824 | bytes 2097152 | tf_op jit(solution)/shard_map/right/pallas_call | solution.py:72
  38.8 2.7 all-to-all-done.2.refs_0_
  41.5 3.5 %all-to-all-start = ((bf16[4,1,128,512]{3,2,1,0:T(8,128)(2,1)}), bf16[4,1,128,512]{3,2,1,0:T(8,128)(2,1)S(1)}, u32[]{:S(2)}, u32[]{:S(2)}) async-start(bf16[4,1,128,512]{3,2,1,0:T(8,128)(2,1)} %get-tuple-element.45), calls=%async_computation | async-start | bytes 1048576 | tf_op jit(solution)/shard_map/all_to_all | solution.py:261
  45.0 2.4 collective-permute-start.9
  49.9 6.4 %copy.14 = bf16[2048,1024]{0,1:T(8,128)(2,1)} copy(bf16[2048,1024]{1,0:T(8,128)(2,1)} %bitcast.31) | data formatting | bytes 8388608 | tf_op jit(solution)/shard_map/reshape | solution.py:279
  56.3 7.5 %collective-permute-done.10.refs_2_ = bf16[1,128,512]{2,1,0:T(8,128)(2,1)} collective-permute-done((bf16[1,128,512]{2,1,0:T(8,128)(2,1)}, bf16[1,128,512]{2,1,0:T(8,128)(2,1)}, u32[]{:S(2)}, u32[]{:S(2)}) %collective-permute-start.10) | collective-permute-done | bytes 131104 | tf_op jit(solution)/shard_map/ppermute | solution.py:258
  63.8 2.8 collective-permute-done.11.refs_3_
  66.6 2.8 collective-permute-done.12.refs_4_
  69.4 5.7 %left.5 = (bf16[4,1,128,512]{3,2,1,0:T(8,128)(2,1)}, bf16[1,128,512]{2,1,0:T(8,128)(2,1)}, bf16[1,128,512]{2,1,0:T(8,128)(2,1)}, bf16[1,128,512]{2,1,0:T(8,128)(2,1)S(1)}, bf16[1,128,512]{2,1,0:T(8,128)(2,1)S(1)}) custom-call(s32[1]{0:T(128)} %bitcast.me_ref, bf16[1024,2048]{1,0:T(8,128)(2,1)} %bitcast.32, ...), custom_call_target="tpu_custom_call" | custom-call | flops 2147483648 | bytes 6291456 | tf_op jit(solution)/shard_map/left/pallas_call | solution.py:131
  76.5 3.5 %all-to-all-start.3 = ((bf16[4,1,128,512]{3,2,1,0:T(8,128)(2,1)}), bf16[4,1,128,512]{3,2,1,0:T(8,128)(2,1)S(1)}, u32[]{:S(2)}, u32[]{:S(2)}) async-start(bf16[4,1,128,512]{3,2,1,0:T(8,128)(2,1)} %get-tuple-element.60), calls=%async_computation.3 | async-start | bytes 1048576 | tf_op jit(solution)/shard_map/all_to_all | solution.py:261
  80.0 2.7 collective-permute-start
  85.5 3.8 %collective-permute-done.refs_1_ = bf16[1,128,512]{2,1,0:T(8,128)(2,1)S(1)} collective-permute-done((bf16[1,128,512]{2,1,0:T(8,128)(2,1)}, bf16[1,128,512]{2,1,0:T(8,128)(2,1)S(1)}, u32[]{:S(2)}, u32[]{:S(2)}) %collective-permute-start) | collective-permute-done | bytes 131104 | tf_op jit(solution)/shard_map/ppermute | solution.py:258
  89.3 9.1 %collective-permute-done.1.refs_2_ = bf16[1,128,512]{2,1,0:T(8,128)(2,1)S(1)} collective-permute-done((bf16[1,128,512]{2,1,0:T(8,128)(2,1)S(1)}, bf16[1,128,512]{2,1,0:T(8,128)(2,1)S(1)}, u32[]{:S(2)}, u32[]{:S(2)}) %collective-permute-start.1) | collective-permute-done | bytes 131104 | tf_op jit(solution)/shard_map/ppermute | solution.py:258
  98.5 4.4 %collective-permute-done.2.refs_3_ = bf16[1,128,512]{2,1,0:T(8,128)(2,1)S(1)} collective-permute-done((bf16[1,128,512]{2,1,0:T(8,128)(2,1)S(1)}, bf16[1,128,512]{2,1,0:T(8,128)(2,1)S(1)}, u32[]{:S(2)}, u32[]{:S(2)}) %collective-permute-start.2) | collective-permute-done | bytes 131104 | tf_op jit(solution)/shard_map/ppermute | solution.py:258
  104.5 5.5 %left.4 = (bf16[4,1,128,512]{3,2,1,0:T(8,128)(2,1)}, bf16[1,128,512]{2,1,0:T(8,128)(2,1)S(1)}, bf16[1,128,512]{2,1,0:T(8,128)(2,1)S(1)}, bf16[1,128,512]{2,1,0:T(8,128)(2,1)S(1)}, bf16[1,128,512]{2,1,0:T(8,128)(2,1)S(1)}) custom-call(s32[1]{0:T(128)} %bitcast.me_ref, bf16[1024,2048]{1,0:T(8,128)(2,1)} %bitcast.33, ...), custom_call_target="tpu_custom_call" | custom-call | flops 2147483648 | bytes 6291456 | tf_op jit(solution)/shard_map/left/pallas_call | solution.py:131
  112.6 4.8 %all-to-all-start.1 = ((bf16[4,1,128,512]{3,2,1,0:T(8,128)(2,1)}), bf16[4,1,128,512]{3,2,1,0:T(8,128)(2,1)S(1)}, u32[]{:S(2)}, u32[]{:S(2)}) async-start(bf16[4,1,128,512]{3,2,1,0:T(8,128)(2,1)} %get-tuple-element.50), calls=%async_computation.1 | async-start | bytes 1048576 | tf_op jit(solution)/shard_map/all_to_all | solution.py:261
  122.2 4.0 %collective-permute-start.13 = (bf16[1,128,512]{2,1,0:T(8,128)(2,1)}, bf16[1,128,512]{2,1,0:T(8,128)(2,1)S(1)}, u32[]{:S(2)}, u32[]{:S(2)}) collective-permute-start(bf16[1,128,512]{2,1,0:T(8,128)(2,1)} %get-tuple-element.61), channel_id=1, source_target_pairs={{0,4},{1,5},{2,6},{3,7},{4,0},{5,1},{6,2},{7,3},{8,12},{9,13},{10,... | collective-permute-start | bytes 393224 | tf_op jit(solution)/shard_map/ppermute | solution.py:258
  127.0 2.8 collective-permute-done.18.refs_2_
  129.9 15.3 %collective-permute-done.19.refs_3_ = bf16[1,128,512]{2,1,0:T(8,128)(2,1)S(1)} collective-permute-done((bf16[1,128,512]{2,1,0:T(8,128)(2,1)S(1)}, bf16[1,128,512]{2,1,0:T(8,128)(2,1)S(1)}, u32[]{:S(2)}, u32[]{:S(2)}) %collective-permute-start.19) | collective-permute-done | bytes 131104 | tf_op jit(solution)/shard_map/ppermute | solution.py:258
  147.3 5.6 %left.6 = (bf16[4,1,128,512]{3,2,1,0:T(8,128)(2,1)}, bf16[1,128,512]{2,1,0:T(8,128)(2,1)S(1)}, bf16[1,128,512]{2,1,0:T(8,128)(2,1)}, bf16[1,128,512]{2,1,0:T(8,128)(2,1)}, bf16[1,128,512]{2,1,0:T(8,128)(2,1)S(1)}) custom-call(s32[1]{0:T(128)} %bitcast.me_ref, bf16[1024,2048]{1,0:T(8,128)(2,1)} %bitcast.34, ...), custom_call_target="tpu_custom_call" | custom-call | flops 2147483648 | bytes 6291456 | tf_op jit(solution)/shard_map/left/pallas_call | solution.py:131
  154.3 4.3 %all-to-all-start.5 = ((bf16[4,1,128,512]{3,2,1,0:T(8,128)(2,1)}), bf16[4,1,128,512]{3,2,1,0:T(8,128)(2,1)}, u32[]{:S(2)}, u32[]{:S(2)}) async-start(bf16[4,1,128,512]{3,2,1,0:T(8,128)(2,1)} %get-tuple-element.70), calls=%async_computation.5 | async-start | bytes 1048576 | tf_op jit(solution)/shard_map/all_to_all | solution.py:261
  158.6 3.8 %collective-permute-start.16 = (bf16[1,128,512]{2,1,0:T(8,128)(2,1)}, bf16[1,128,512]{2,1,0:T(8,128)(2,1)S(1)}, u32[]{:S(2)}, u32[]{:S(2)}) collective-permute-start(bf16[1,128,512]{2,1,0:T(8,128)(2,1)} %copy-done.30), channel_id=1, source_target_pairs={{0,7},{1,6},{2,5},{3,4},{4,3},{5,2},{6,1},{7,0},{8,15},{9,14},{10,... | collective-permute-start | bytes 393224 | tf_op jit(solution)/shard_map/ppermute | solution.py:258
  167.2 4.8 %sine_bitcast_fusion = (f32[4,128,512]{2,1,0:T(8,128)S(1)}, f32[4,128,512]{2,1,0:T(8,128)S(1)}) fusion(f32[128,4,512]{2,1,0:T(4,128)} %param.9), kind=kLoop, calls=%fused_computation | loop fusion | bytes 3145728 | tf_op jit(solution)/shard_map/sin | solution.py:292
  172.0 2.8 collective-permute-start.25
  174.8 9.2 %collective-permute-done.5.refs_2_ = bf16[1,128,512]{2,1,0:T(8,128)(2,1)S(1)} collective-permute-done((bf16[1,128,512]{2,1,0:T(8,128)(2,1)}, bf16[1,128,512]{2,1,0:T(8,128)(2,1)S(1)}, u32[]{:S(2)}, u32[]{:S(2)}) %collective-permute-start.5) | collective-permute-done | bytes 131104 | tf_op jit(solution)/shard_map/ppermute | solution.py:258
  183.9 3.7 %collective-permute-start.26 = (bf16[1,128,512]{2,1,0:T(8,128)(2,1)}, bf16[1,128,512]{2,1,0:T(8,128)(2,1)S(1)}, u32[]{:S(2)}, u32[]{:S(2)}) collective-permute-start(bf16[1,128,512]{2,1,0:T(8,128)(2,1)} %copy-done.28), channel_id=1, source_target_pairs={{0,5},{1,4},{2,7},{3,6},{4,1},{5,0},{6,3},{7,2},{8,13},{9,12},{10,... | collective-permute-start | bytes 393224 | tf_op jit(solution)/shard_map/ppermute | solution.py:258
  187.7 9.5 %collective-permute-done.6.refs_3_ = bf16[1,128,512]{2,1,0:T(8,128)(2,1)S(1)} collective-permute-done((bf16[1,128,512]{2,1,0:T(8,128)(2,1)}, bf16[1,128,512]{2,1,0:T(8,128)(2,1)S(1)}, u32[]{:S(2)}, u32[]{:S(2)}) %collective-permute-start.6) | collective-permute-done | bytes 131104 | tf_op jit(solution)/shard_map/ppermute | solution.py:258
  199.3 2.5 phase.4.refs_4_
  201.8 13.1 %collective-permute-start.8 = (bf16[2,4,128,512]{3,2,1,0:T(8,128)(2,1)}, bf16[2,4,128,512]{3,2,1,0:T(8,128)(2,1)}, u32[]{:S(2)}, u32[]{:S(2)}) collective-permute-start(bf16[2,4,128,512]{3,2,1,0:T(8,128)(2,1)} %phase.4.refs_4_), channel_id=1, source_target_pairs={{0,8},{8,16},{16,24},{1,9},{9,17},{17,25},{2,10},{10,18},{18,26},{... | collective-permute-start | bytes 3145736 | tf_op jit(solution)/shard_map/ppermute | solution.py:268
  214.9 2.5 phase.5.refs_1_
  219.5 4.7 %left.7 = (bf16[4,1,128,512]{3,2,1,0:T(8,128)(2,1)S(1)}, bf16[1,128,512]{2,1,0:T(8,128)(2,1)S(1)}, bf16[1,128,512]{2,1,0:T(8,128)(2,1)S(1)}, bf16[1,128,512]{2,1,0:T(8,128)(2,1)S(1)}, bf16[1,128,512]{2,1,0:T(8,128)(2,1)S(1)}) custom-call(s32[1]{0:T(128)} %bitcast.me_ref, bf16[1024,2048]{1,0:T(8,128)(2,1)} %bitcast.35, ...), custom_call_target="tpu_custom_call" | custom-call | flops 2147483648 | bytes 6291456 | tf_op jit(solution)/shard_map/left/pallas_call | solution.py:131
  227.7 4.1 %all-to-all-start.7 = ((bf16[4,1,128,512]{3,2,1,0:T(8,128)(2,1)}), bf16[4,1,128,512]{3,2,1,0:T(8,128)(2,1)}, u32[]{:S(2)}, u32[]{:S(2)}) async-start(bf16[4,1,128,512]{3,2,1,0:T(8,128)(2,1)} %copy-done.10), calls=%async_computation.7 | async-start | bytes 1048576 | tf_op jit(solution)/shard_map/all_to_all | solution.py:261
  233.7 2.6 collective-permute-start.23
  236.3 6.1 %collective-permute-done.21.refs_1_ = bf16[1,128,512]{2,1,0:T(8,128)(2,1)S(1)} collective-permute-done((bf16[1,128,512]{2,1,0:T(8,128)(2,1)S(1)}, bf16[1,128,512]{2,1,0:T(8,128)(2,1)S(1)}, u32[]{:S(2)}, u32[]{:S(2)}) %collective-permute-start.21) | collective-permute-done | bytes 131104 | tf_op jit(solution)/shard_map/ppermute | solution.py:258
  243.3 6.6 %collective-permute-done.22.refs_2_ = bf16[1,128,512]{2,1,0:T(8,128)(2,1)S(1)} collective-permute-done((bf16[1,128,512]{2,1,0:T(8,128)(2,1)}, bf16[1,128,512]{2,1,0:T(8,128)(2,1)S(1)}, u32[]{:S(2)}, u32[]{:S(2)}) %collective-permute-start.22) | collective-permute-done | bytes 131104 | tf_op jit(solution)/shard_map/ppermute | solution.py:258
  253.7 3.6 %collective-permute-done.23.refs_3_ = bf16[1,128,512]{2,1,0:T(8,128)(2,1)S(1)} collective-permute-done((bf16[1,128,512]{2,1,0:T(8,128)(2,1)}, bf16[1,128,512]{2,1,0:T(8,128)(2,1)S(1)}, u32[]{:S(2)}, u32[]{:S(2)}) %collective-permute-start.23) | collective-permute-done | bytes 131104 | tf_op jit(solution)/shard_map/ppermute | solution.py:258
  258.0 3.4 %collective-permute-done.24.refs_4_ = bf16[1,128,512]{2,1,0:T(8,128)(2,1)S(1)} collective-permute-done((bf16[1,128,512]{2,1,0:T(8,128)(2,1)}, bf16[1,128,512]{2,1,0:T(8,128)(2,1)S(1)}, u32[]{:S(2)}, u32[]{:S(2)}) %collective-permute-start.24) | collective-permute-done | bytes 131104 | tf_op jit(solution)/shard_map/ppermute | solution.py:258
  264.3 2.5 collective-permute-done.29.refs_1_
  272.4 2.6 phase.6.refs_2_
  282.1 2.6 phase.7.refs_3_
  284.8 9.5 %mix.1 = bf16[128,2,4,16,128]{4,3,2,1,0:T(8,128)(2,1)} custom-call(f32[4,4]{1,0:T(4,128)S(1)} %get-tuple-element.88.up_ref, f32[4,4]{1,0:T(4,128)S(1)} %get-tuple-element.87.down_ref, f32[128,512]{1,0:T(8,128)S(1)} %copy-done.11, bf16[2,4,128,512]{3,2,1,0:T(8,128)(2,1)} %collective-permute-done.8.refs_0_, bf16[2,4,128,512]{3,2,1,0:T(8,128)(2,1)} %phase.5.refs_1_, ...), custom_call_target="tpu_custom_call" | custom-call | flops 20971520 | bytes 10485760 | tf_op jit(solution)/shard_map/mix/pallas_call | solution.py:237
  (155 shorter events, 62.4 us)
Async XLA Ops:
  8.0 11.8 %all-to-all-start.6 = ((bf16[4,1,128,512]{3,2,1,0:T(8,128)(2,1)}), bf16[4,1,128,512]{3,2,1,0:T(8,128)(2,1)S(1)}, u32[]{:S(2)}, u32[]{:S(2)}) async-start(bf16[4,1,128,512]{3,2,1,0:T(8,128)(2,1)} %get-tuple-element.75), calls=%async_computation.6 | async-start | bytes 1048576 | tf_op jit(solution)/shard_map/all_to_all | solution.py:261
  19.9 18.3 %copy-start.8 = (bf16[4,1,128,512]{3,2,1,0:T(8,128)(2,1)}, bf16[4,1,128,512]{3,2,1,0:T(8,128)(2,1)S(1)}, u32[]{:S(2)}) copy-start(bf16[4,1,128,512]{3,2,1,0:T(8,128)(2,1)S(1)} %all-to-all-done.6.refs_0_) | copy-start | bytes 1572868
  19.9 10.3 %all-to-all-start.4 = ((bf16[4,1,128,512]{3,2,1,0:T(8,128)(2,1)}), bf16[4,1,128,512]{3,2,1,0:T(8,128)(2,1)S(1)}, u32[]{:S(2)}, u32[]{:S(2)}) async-start(bf16[4,1,128,512]{3,2,1,0:T(8,128)(2,1)} %get-tuple-element.65), calls=%async_computation.4 | async-start | bytes 1048576 | tf_op jit(solution)/shard_map/all_to_all | solution.py:261
  30.2 11.3 %all-to-all-start.2 = ((bf16[4,1,128,512]{3,2,1,0:T(8,128)(2,1)}), bf16[4,1,128,512]{3,2,1,0:T(8,128)(2,1)S(1)}, u32[]{:S(2)}, u32[]{:S(2)}) async-start(bf16[4,1,128,512]{3,2,1,0:T(8,128)(2,1)} %get-tuple-element.55), calls=%async_computation.2 | async-start | bytes 1048576 | tf_op jit(solution)/shard_map/all_to_all | solution.py:261
  41.5 35.0 %all-to-all-start = ((bf16[4,1,128,512]{3,2,1,0:T(8,128)(2,1)}), bf16[4,1,128,512]{3,2,1,0:T(8,128)(2,1)S(1)}, u32[]{:S(2)}, u32[]{:S(2)}) async-start(bf16[4,1,128,512]{3,2,1,0:T(8,128)(2,1)} %get-tuple-element.45), calls=%async_computation | async-start | bytes 1048576 | tf_op jit(solution)/shard_map/all_to_all | solution.py:261
  45.0 11.3 %collective-permute-start.9 = (bf16[1,128,512]{2,1,0:T(8,128)(2,1)}, bf16[1,128,512]{2,1,0:T(8,128)(2,1)}, u32[]{:S(2)}, u32[]{:S(2)}) collective-permute-start(bf16[1,128,512]{2,1,0:T(8,128)(2,1)} %copy-done.47), channel_id=1, source_target_pairs={{0,4},{1,5},{2,6},{3,7},{4,0},{5,1},{6,2},{7,3},{8,12},{9,13},{10,... | collective-permute-start | bytes 393224 | tf_op jit(solution)/shard_map/ppermute | solution.py:258
  47.4 16.4 %collective-permute-start.10 = (bf16[1,128,512]{2,1,0:T(8,128)(2,1)}, bf16[1,128,512]{2,1,0:T(8,128)(2,1)}, u32[]{:S(2)}, u32[]{:S(2)}) collective-permute-start(bf16[1,128,512]{2,1,0:T(8,128)(2,1)} %copy-done.46), channel_id=1, source_target_pairs={{0,5},{1,4},{2,7},{3,6},{4,1},{5,0},{6,3},{7,2},{8,13},{9,12},{10,... | collective-permute-start | bytes 393224 | tf_op jit(solution)/shard_map/ppermute | solution.py:258
  47.5 19.1 %collective-permute-start.11 = (bf16[1,128,512]{2,1,0:T(8,128)(2,1)}, bf16[1,128,512]{2,1,0:T(8,128)(2,1)}, u32[]{:S(2)}, u32[]{:S(2)}) collective-permute-start(bf16[1,128,512]{2,1,0:T(8,128)(2,1)} %copy-done.45), channel_id=1, source_target_pairs={{0,6},{1,7},{2,4},{3,5},{4,2},{5,3},{6,0},{7,1},{8,14},{9,15},{10,... | collective-permute-start | bytes 393224 | tf_op jit(solution)/shard_map/ppermute | solution.py:258
  49.0 20.4 %collective-permute-start.12 = (bf16[1,128,512]{2,1,0:T(8,128)(2,1)}, bf16[1,128,512]{2,1,0:T(8,128)(2,1)}, u32[]{:S(2)}, u32[]{:S(2)}) collective-permute-start(bf16[1,128,512]{2,1,0:T(8,128)(2,1)} %copy-done.44), channel_id=1, source_target_pairs={{0,7},{1,6},{2,5},{3,4},{4,3},{5,2},{6,1},{7,0},{8,15},{9,14},{10,... | collective-permute-start | bytes 393224 | tf_op jit(solution)/shard_map/ppermute | solution.py:258
  76.5 36.1 %all-to-all-start.3 = ((bf16[4,1,128,512]{3,2,1,0:T(8,128)(2,1)}), bf16[4,1,128,512]{3,2,1,0:T(8,128)(2,1)S(1)}, u32[]{:S(2)}, u32[]{:S(2)}) async-start(bf16[4,1,128,512]{3,2,1,0:T(8,128)(2,1)} %get-tuple-element.60), calls=%async_computation.3 | async-start | bytes 1048576 | tf_op jit(solution)/shard_map/all_to_all | solution.py:261
  80.0 9.4 %collective-permute-start = (bf16[1,128,512]{2,1,0:T(8,128)(2,1)}, bf16[1,128,512]{2,1,0:T(8,128)(2,1)S(1)}, u32[]{:S(2)}, u32[]{:S(2)}) collective-permute-start(bf16[1,128,512]{2,1,0:T(8,128)(2,1)} %copy-done.43), channel_id=1, source_target_pairs={{0,4},{1,5},{2,6},{3,7},{4,0},{5,1},{6,2},{7,3},{8,12},{9,13},{10,... | collective-permute-start | bytes 393224 | tf_op jit(solution)/shard_map/ppermute | solution.py:258
  82.7 15.8 %collective-permute-start.1 = (bf16[1,128,512]{2,1,0:T(8,128)(2,1)S(1)}, bf16[1,128,512]{2,1,0:T(8,128)(2,1)S(1)}, u32[]{:S(2)}, u32[]{:S(2)}) collective-permute-start(bf16[1,128,512]{2,1,0:T(8,128)(2,1)S(1)} %get-tuple-element.47), channel_id=1, source_target_pairs={{0,5},{1,4},{2,7},{3,6},{4,1},{5,0},{6,3},{7,2},{8,13},{9,12},{10,... | collective-permute-start | bytes 393224 | tf_op jit(solution)/shard_map/ppermute | solution.py:258
  83.6 19.3 %collective-permute-start.2 = (bf16[1,128,512]{2,1,0:T(8,128)(2,1)S(1)}, bf16[1,128,512]{2,1,0:T(8,128)(2,1)S(1)}, u32[]{:S(2)}, u32[]{:S(2)}) collective-permute-start(bf16[1,128,512]{2,1,0:T(8,128)(2,1)S(1)} %get-tuple-element.48), channel_id=1, source_target_pairs={{0,6},{1,7},{2,4},{3,5},{4,2},{5,3},{6,0},{7,1},{8,14},{9,15},{10,... | collective-permute-start | bytes 393224 | tf_op jit(solution)/shard_map/ppermute | solution.py:258
  85.5 18.9 %collective-permute-start.3 = (bf16[1,128,512]{2,1,0:T(8,128)(2,1)S(1)}, bf16[1,128,512]{2,1,0:T(8,128)(2,1)S(1)}, u32[]{:S(2)}, u32[]{:S(2)}) collective-permute-start(bf16[1,128,512]{2,1,0:T(8,128)(2,1)S(1)} %get-tuple-element.49), channel_id=1, source_target_pairs={{0,7},{1,6},{2,5},{3,4},{4,3},{5,2},{6,1},{7,0},{8,15},{9,14},{10,... | collective-permute-start | bytes 393224 | tf_op jit(solution)/shard_map/ppermute | solution.py:258
  112.6 40.3 %copy-start.4 = (bf16[4,1,128,512]{3,2,1,0:T(8,128)(2,1)}, bf16[4,1,128,512]{3,2,1,0:T(8,128)(2,1)S(1)}, u32[]{:S(2)}) copy-start(bf16[4,1,128,512]{3,2,1,0:T(8,128)(2,1)S(1)} %all-to-all-done.3.refs_0_) | copy-start | bytes 1572868
  112.6 41.6 %all-to-all-start.1 = ((bf16[4,1,128,512]{3,2,1,0:T(8,128)(2,1)}), bf16[4,1,128,512]{3,2,1,0:T(8,128)(2,1)S(1)}, u32[]{:S(2)}, u32[]{:S(2)}) async-start(bf16[4,1,128,512]{3,2,1,0:T(8,128)(2,1)} %get-tuple-element.50), calls=%async_computation.1 | async-start | bytes 1048576 | tf_op jit(solution)/shard_map/all_to_all | solution.py:261
  117.4 8.7 %collective-permute-start.17 = (bf16[1,128,512]{2,1,0:T(8,128)(2,1)S(1)}, bf16[1,128,512]{2,1,0:T(8,128)(2,1)S(1)}, u32[]{:S(2)}, u32[]{:S(2)}) collective-permute-start(bf16[1,128,512]{2,1,0:T(8,128)(2,1)S(1)} %get-tuple-element.66), channel_id=1, source_target_pairs={{0,4},{1,5},{2,6},{3,7},{4,0},{5,1},{6,2},{7,3},{8,12},{9,13},{10,... | collective-permute-start | bytes 393224 | tf_op jit(solution)/shard_map/ppermute | solution.py:258
  119.6 10.3 %collective-permute-start.18 = (bf16[1,128,512]{2,1,0:T(8,128)(2,1)S(1)}, bf16[1,128,512]{2,1,0:T(8,128)(2,1)S(1)}, u32[]{:S(2)}, u32[]{:S(2)}) collective-permute-start(bf16[1,128,512]{2,1,0:T(8,128)(2,1)S(1)} %get-tuple-element.67), channel_id=1, source_target_pairs={{0,5},{1,4},{2,7},{3,6},{4,1},{5,0},{6,3},{7,2},{8,13},{9,12},{10,... | collective-permute-start | bytes 393224 | tf_op jit(solution)/shard_map/ppermute | solution.py:258
  120.7 24.5 %collective-permute-start.19 = (bf16[1,128,512]{2,1,0:T(8,128)(2,1)S(1)}, bf16[1,128,512]{2,1,0:T(8,128)(2,1)S(1)}, u32[]{:S(2)}, u32[]{:S(2)}) collective-permute-start(bf16[1,128,512]{2,1,0:T(8,128)(2,1)S(1)} %get-tuple-element.68), channel_id=1, source_target_pairs={{0,6},{1,7},{2,4},{3,5},{4,2},{5,3},{6,0},{7,1},{8,14},{9,15},{10,... | collective-permute-start | bytes 393224 | tf_op jit(solution)/shard_map/ppermute | solution.py:258
  122.0 25.4 %collective-permute-start.20 = (bf16[1,128,512]{2,1,0:T(8,128)(2,1)S(1)}, bf16[1,128,512]{2,1,0:T(8,128)(2,1)S(1)}, u32[]{:S(2)}, u32[]{:S(2)}) collective-permute-start(bf16[1,128,512]{2,1,0:T(8,128)(2,1)S(1)} %get-tuple-element.69), channel_id=1, source_target_pairs={{0,7},{1,6},{2,5},{3,4},{4,3},{5,2},{6,1},{7,0},{8,15},{9,14},{10,... | collective-permute-start | bytes 393224 | tf_op jit(solution)/shard_map/ppermute | solution.py:258
  122.2 40.2 %collective-permute-start.13 = (bf16[1,128,512]{2,1,0:T(8,128)(2,1)}, bf16[1,128,512]{2,1,0:T(8,128)(2,1)S(1)}, u32[]{:S(2)}, u32[]{:S(2)}) collective-permute-start(bf16[1,128,512]{2,1,0:T(8,128)(2,1)} %get-tuple-element.61), channel_id=1, source_target_pairs={{0,4},{1,5},{2,6},{3,7},{4,0},{5,1},{6,2},{7,3},{8,12},{9,13},{10,... | collective-permute-start | bytes 393224 | tf_op jit(solution)/shard_map/ppermute | solution.py:258
  126.2 38.6 %collective-permute-start.14 = (bf16[1,128,512]{2,1,0:T(8,128)(2,1)}, bf16[1,128,512]{2,1,0:T(8,128)(2,1)S(1)}, u32[]{:S(2)}, u32[]{:S(2)}) collective-permute-start(bf16[1,128,512]{2,1,0:T(8,128)(2,1)} %get-tuple-element.62), channel_id=1, source_target_pairs={{0,5},{1,4},{2,7},{3,6},{4,1},{5,0},{6,3},{7,2},{8,13},{9,12},{10,... | collective-permute-start | bytes 393224 | tf_op jit(solution)/shard_map/ppermute | solution.py:258
  129.9 35.9 %collective-permute-start.15 = (bf16[1,128,512]{2,1,0:T(8,128)(2,1)}, bf16[1,128,512]{2,1,0:T(8,128)(2,1)S(1)}, u32[]{:S(2)}, u32[]{:S(2)}) collective-permute-start(bf16[1,128,512]{2,1,0:T(8,128)(2,1)} %copy-done.34), channel_id=1, source_target_pairs={{0,6},{1,7},{2,4},{3,5},{4,2},{5,3},{6,0},{7,1},{8,14},{9,15},{10,... | collective-permute-start | bytes 393224 | tf_op jit(solution)/shard_map/ppermute | solution.py:258
  154.3 73.4 %all-to-all-start.5 = ((bf16[4,1,128,512]{3,2,1,0:T(8,128)(2,1)}), bf16[4,1,128,512]{3,2,1,0:T(8,128)(2,1)}, u32[]{:S(2)}, u32[]{:S(2)}) async-start(bf16[4,1,128,512]{3,2,1,0:T(8,128)(2,1)} %get-tuple-element.70), calls=%async_computation.5 | async-start | bytes 1048576 | tf_op jit(solution)/shard_map/all_to_all | solution.py:261
  158.6 43.2 %collective-permute-start.16 = (bf16[1,128,512]{2,1,0:T(8,128)(2,1)}, bf16[1,128,512]{2,1,0:T(8,128)(2,1)S(1)}, u32[]{:S(2)}, u32[]{:S(2)}) collective-permute-start(bf16[1,128,512]{2,1,0:T(8,128)(2,1)} %copy-done.30), channel_id=1, source_target_pairs={{0,7},{1,6},{2,5},{3,4},{4,3},{5,2},{6,1},{7,0},{8,15},{9,14},{10,... | collective-permute-start | bytes 393224 | tf_op jit(solution)/shard_map/ppermute | solution.py:258
  162.4 9.6 %collective-permute-start.4 = (bf16[1,128,512]{2,1,0:T(8,128)(2,1)}, bf16[1,128,512]{2,1,0:T(8,128)(2,1)S(1)}, u32[]{:S(2)}, u32[]{:S(2)}) collective-permute-start(bf16[1,128,512]{2,1,0:T(8,128)(2,1)} %copy-done.38), channel_id=1, source_target_pairs={{0,4},{1,5},{2,6},{3,7},{4,0},{5,1},{6,2},{7,3},{8,12},{9,13},{10,... | collective-permute-start | bytes 393224 | tf_op jit(solution)/shard_map/ppermute | solution.py:258
  162.4 21.5 %collective-permute-start.5 = (bf16[1,128,512]{2,1,0:T(8,128)(2,1)}, bf16[1,128,512]{2,1,0:T(8,128)(2,1)S(1)}, u32[]{:S(2)}, u32[]{:S(2)}) collective-permute-start(bf16[1,128,512]{2,1,0:T(8,128)(2,1)} %copy-done.37), channel_id=1, source_target_pairs={{0,5},{1,4},{2,7},{3,6},{4,1},{5,0},{6,3},{7,2},{8,13},{9,12},{10,... | collective-permute-start | bytes 393224 | tf_op jit(solution)/shard_map/ppermute | solution.py:258
  164.8 32.4 %collective-permute-start.6 = (bf16[1,128,512]{2,1,0:T(8,128)(2,1)}, bf16[1,128,512]{2,1,0:T(8,128)(2,1)S(1)}, u32[]{:S(2)}, u32[]{:S(2)}) collective-permute-start(bf16[1,128,512]{2,1,0:T(8,128)(2,1)} %copy-done.36), channel_id=1, source_target_pairs={{0,6},{1,7},{2,4},{3,5},{4,2},{5,3},{6,0},{7,1},{8,14},{9,15},{10,... | collective-permute-start | bytes 393224 | tf_op jit(solution)/shard_map/ppermute | solution.py:258
  165.7 49.1 %copy-start.5 = (bf16[4,1,128,512]{3,2,1,0:T(8,128)(2,1)S(1)}, bf16[4,1,128,512]{3,2,1,0:T(8,128)(2,1)}, u32[]{:S(2)}) copy-start(bf16[4,1,128,512]{3,2,1,0:T(8,128)(2,1)} %copy-done.4) | copy-start | bytes 1572868
  165.7 32.5 %collective-permute-start.7 = (bf16[1,128,512]{2,1,0:T(8,128)(2,1)}, bf16[1,128,512]{2,1,0:T(8,128)(2,1)S(1)}, u32[]{:S(2)}, u32[]{:S(2)}) collective-permute-start(bf16[1,128,512]{2,1,0:T(8,128)(2,1)} %copy-done.35), channel_id=1, source_target_pairs={{0,7},{1,6},{2,5},{3,4},{4,3},{5,2},{6,1},{7,0},{8,15},{9,14},{10,... | collective-permute-start | bytes 393224 | tf_op jit(solution)/shard_map/ppermute | solution.py:258
  172.0 45.5 %collective-permute-start.25 = (bf16[1,128,512]{2,1,0:T(8,128)(2,1)}, bf16[1,128,512]{2,1,0:T(8,128)(2,1)S(1)}, u32[]{:S(2)}, u32[]{:S(2)}) collective-permute-start(bf16[1,128,512]{2,1,0:T(8,128)(2,1)} %copy-done.29), channel_id=1, source_target_pairs={{0,4},{1,5},{2,6},{3,7},{4,0},{5,1},{6,2},{7,3},{8,12},{9,13},{10,... | collective-permute-start | bytes 393224 | tf_op jit(solution)/shard_map/ppermute | solution.py:258
  183.9 35.6 %collective-permute-start.26 = (bf16[1,128,512]{2,1,0:T(8,128)(2,1)}, bf16[1,128,512]{2,1,0:T(8,128)(2,1)S(1)}, u32[]{:S(2)}, u32[]{:S(2)}) collective-permute-start(bf16[1,128,512]{2,1,0:T(8,128)(2,1)} %copy-done.28), channel_id=1, source_target_pairs={{0,5},{1,4},{2,7},{3,6},{4,1},{5,0},{6,3},{7,2},{8,13},{9,12},{10,... | collective-permute-start | bytes 393224 | tf_op jit(solution)/shard_map/ppermute | solution.py:258
  197.2 22.3 %collective-permute-start.27 = (bf16[1,128,512]{2,1,0:T(8,128)(2,1)}, bf16[1,128,512]{2,1,0:T(8,128)(2,1)S(1)}, u32[]{:S(2)}, u32[]{:S(2)}) collective-permute-start(bf16[1,128,512]{2,1,0:T(8,128)(2,1)} %copy-done.27), channel_id=1, source_target_pairs={{0,6},{1,7},{2,4},{3,5},{4,2},{5,3},{6,0},{7,1},{8,14},{9,15},{10,... | collective-permute-start | bytes 393224 | tf_op jit(solution)/shard_map/ppermute | solution.py:258
  198.2 21.3 %collective-permute-start.28 = (bf16[1,128,512]{2,1,0:T(8,128)(2,1)}, bf16[1,128,512]{2,1,0:T(8,128)(2,1)S(1)}, u32[]{:S(2)}, u32[]{:S(2)}) collective-permute-start(bf16[1,128,512]{2,1,0:T(8,128)(2,1)} %copy-done.26), channel_id=1, source_target_pairs={{0,7},{1,6},{2,5},{3,4},{4,3},{5,2},{6,1},{7,0},{8,15},{9,14},{10,... | collective-permute-start | bytes 393224 | tf_op jit(solution)/shard_map/ppermute | solution.py:258
  199.3 20.2 %copy-start.9 = (bf16[4,1,128,512]{3,2,1,0:T(8,128)(2,1)S(1)}, bf16[4,1,128,512]{3,2,1,0:T(8,128)(2,1)}, u32[]{:S(2)}) copy-start(bf16[4,1,128,512]{3,2,1,0:T(8,128)(2,1)} %copy-done.8) | copy-start | bytes 1572868
  201.8 83.0 %collective-permute-start.8 = (bf16[2,4,128,512]{3,2,1,0:T(8,128)(2,1)}, bf16[2,4,128,512]{3,2,1,0:T(8,128)(2,1)}, u32[]{:S(2)}, u32[]{:S(2)}) collective-permute-start(bf16[2,4,128,512]{3,2,1,0:T(8,128)(2,1)} %phase.4.refs_4_), channel_id=1, source_target_pairs={{0,8},{8,16},{16,24},{1,9},{9,17},{17,25},{2,10},{10,18},{18,26},{... | collective-permute-start | bytes 3145736 | tf_op jit(solution)/shard_map/ppermute | solution.py:268
  217.4 14.4 %copy-start.33 = (bf16[1,128,512]{2,1,0:T(8,128)(2,1)S(1)}, bf16[1,128,512]{2,1,0:T(8,128)(2,1)}, u32[]{:S(2)}) copy-start(bf16[1,128,512]{2,1,0:T(8,128)(2,1)} %copy-done.32) | copy-start | bytes 393220
  217.4 36.0 %copy-start.48 = (f32[16,4]{0,1:T(4,128)S(1)}, f32[16,4]{0,1:T(4,128)}, u32[]{:S(2)}) copy-start(f32[16,4]{0,1:T(4,128)} %param.10) | copy-start | bytes 772
  217.4 67.3 %collective-permute-start.33 = (bf16[2,4,128,512]{3,2,1,0:T(8,128)(2,1)}, bf16[2,4,128,512]{3,2,1,0:T(8,128)(2,1)}, u32[]{:S(2)}, u32[]{:S(2)}) collective-permute-start(bf16[2,4,128,512]{3,2,1,0:T(8,128)(2,1)} %phase.5.refs_1_), channel_id=1, source_target_pairs={{8,0},{16,8},{24,16},{9,1},{17,9},{25,17},{10,2},{18,10},{26,18},{... | collective-permute-start | bytes 3145736 | tf_op jit(solution)/shard_map/ppermute | solution.py:268
  227.7 51.7 %all-to-all-start.7 = ((bf16[4,1,128,512]{3,2,1,0:T(8,128)(2,1)}), bf16[4,1,128,512]{3,2,1,0:T(8,128)(2,1)}, u32[]{:S(2)}, u32[]{:S(2)}) async-start(bf16[4,1,128,512]{3,2,1,0:T(8,128)(2,1)} %copy-done.10), calls=%async_computation.7 | async-start | bytes 1048576 | tf_op jit(solution)/shard_map/all_to_all | solution.py:261
  231.8 10.5 %collective-permute-start.21 = (bf16[1,128,512]{2,1,0:T(8,128)(2,1)S(1)}, bf16[1,128,512]{2,1,0:T(8,128)(2,1)S(1)}, u32[]{:S(2)}, u32[]{:S(2)}) collective-permute-start(bf16[1,128,512]{2,1,0:T(8,128)(2,1)S(1)} %copy-done.33), channel_id=1, source_target_pairs={{0,4},{1,5},{2,6},{3,7},{4,0},{5,1},{6,2},{7,3},{8,12},{9,13},{10,... | collective-permute-start | bytes 393224 | tf_op jit(solution)/shard_map/ppermute | solution.py:258
  232.5 17.5 %collective-permute-start.22 = (bf16[1,128,512]{2,1,0:T(8,128)(2,1)}, bf16[1,128,512]{2,1,0:T(8,128)(2,1)S(1)}, u32[]{:S(2)}, u32[]{:S(2)}) collective-permute-start(bf16[1,128,512]{2,1,0:T(8,128)(2,1)} %get-tuple-element.72), channel_id=1, source_target_pairs={{0,5},{1,4},{2,7},{3,6},{4,1},{5,0},{6,3},{7,2},{8,13},{9,12},{10,... | collective-permute-start | bytes 393224 | tf_op jit(solution)/shard_map/ppermute | solution.py:258
  233.7 23.6 %collective-permute-start.23 = (bf16[1,128,512]{2,1,0:T(8,128)(2,1)}, bf16[1,128,512]{2,1,0:T(8,128)(2,1)S(1)}, u32[]{:S(2)}, u32[]{:S(2)}) collective-permute-start(bf16[1,128,512]{2,1,0:T(8,128)(2,1)} %get-tuple-element.73), channel_id=1, source_target_pairs={{0,6},{1,7},{2,4},{3,5},{4,2},{5,3},{6,0},{7,1},{8,14},{9,15},{10,... | collective-permute-start | bytes 393224 | tf_op jit(solution)/shard_map/ppermute | solution.py:258
  243.0 18.4 %collective-permute-start.24 = (bf16[1,128,512]{2,1,0:T(8,128)(2,1)}, bf16[1,128,512]{2,1,0:T(8,128)(2,1)S(1)}, u32[]{:S(2)}, u32[]{:S(2)}) collective-permute-start(bf16[1,128,512]{2,1,0:T(8,128)(2,1)} %copy-done.31), channel_id=1, source_target_pairs={{0,7},{1,6},{2,5},{3,4},{4,3},{5,2},{6,1},{7,0},{8,15},{9,14},{10,... | collective-permute-start | bytes 393224 | tf_op jit(solution)/shard_map/ppermute | solution.py:258
  250.6 16.2 %collective-permute-start.29 = (bf16[1,128,512]{2,1,0:T(8,128)(2,1)}, bf16[1,128,512]{2,1,0:T(8,128)(2,1)S(1)}, u32[]{:S(2)}, u32[]{:S(2)}) collective-permute-start(bf16[1,128,512]{2,1,0:T(8,128)(2,1)} %copy-done.42), channel_id=1, source_target_pairs={{0,4},{1,5},{2,6},{3,7},{4,0},{5,1},{6,2},{7,3},{8,12},{9,13},{10,... | collective-permute-start | bytes 393224 | tf_op jit(solution)/shard_map/ppermute | solution.py:258
  258.0 18.0 %collective-permute-start.30 = (bf16[1,128,512]{2,1,0:T(8,128)(2,1)}, bf16[1,128,512]{2,1,0:T(8,128)(2,1)S(1)}, u32[]{:S(2)}, u32[]{:S(2)}) collective-permute-start(bf16[1,128,512]{2,1,0:T(8,128)(2,1)} %copy-done.41), channel_id=1, source_target_pairs={{0,5},{1,4},{2,7},{3,6},{4,1},{5,0},{6,3},{7,2},{8,13},{9,12},{10,... | collective-permute-start | bytes 393224 | tf_op jit(solution)/shard_map/ppermute | solution.py:258
  262.1 15.0 %collective-permute-start.31 = (bf16[1,128,512]{2,1,0:T(8,128)(2,1)}, bf16[1,128,512]{2,1,0:T(8,128)(2,1)S(1)}, u32[]{:S(2)}, u32[]{:S(2)}) collective-permute-start(bf16[1,128,512]{2,1,0:T(8,128)(2,1)} %copy-done.40), channel_id=1, source_target_pairs={{0,6},{1,7},{2,4},{3,5},{4,2},{5,3},{6,0},{7,1},{8,14},{9,15},{10,... | collective-permute-start | bytes 393224 | tf_op jit(solution)/shard_map/ppermute | solution.py:258
  266.8 11.9 %collective-permute-start.32 = (bf16[1,128,512]{2,1,0:T(8,128)(2,1)}, bf16[1,128,512]{2,1,0:T(8,128)(2,1)S(1)}, u32[]{:S(2)}, u32[]{:S(2)}) collective-permute-start(bf16[1,128,512]{2,1,0:T(8,128)(2,1)} %copy-done.39), channel_id=1, source_target_pairs={{0,7},{1,6},{2,5},{3,4},{4,3},{5,2},{6,1},{7,0},{8,15},{9,14},{10,... | collective-permute-start | bytes 393224 | tf_op jit(solution)/shard_map/ppermute | solution.py:258
  (43 other events, 65.8 us)

commit v2 on v0

--- a/solution.py
+++ b/solution.py
@@ -10,6 +10,7 @@
 LANES = 128
 LIMIT = 48 * 1024 * 1024
 SMEM = pl.BlockSpec(memory_space=pltpu.SMEM)
+AFTER = pl.BlockSpec(memory_space=pl.ANY)
 
 
 def params(limit=LIMIT):
@@ -24,7 +25,8 @@
     return jnp.concatenate([real, -imag], 1), jnp.concatenate([imag, real], 1)
 
 
-def right_kernel(ranks, states, me_ref, second_ref, *refs):
+def right_kernel(after, ranks, states, me_ref, second_ref, *refs):
+    refs = refs[after:]
     kinds = len(refs) - 2 - ranks
     packets, outs, wide, slabs = refs[:kinds], refs[kinds:-2], refs[-2], refs[-1]
     me = me_ref[0]
@@ -60,15 +62,16 @@
             out[n] = slabs[me ^ s]
 
 
-def right_call(me, second, view, chosen, ranks, states, piece):
+def right_call(after, me, second, view, chosen, ranks, states, piece):
     rows, _, _, group, _ = view.shape
     width = second.shape[1]
     block = rows // 2
     kinds = len(chosen)
     return pl.pallas_call(
-        functools.partial(right_kernel, ranks, states),
+        functools.partial(right_kernel, len(after), ranks, states),
         grid=(rows // block,),
         in_specs=[SMEM, pl.BlockSpec(second.shape, lambda i: (0, 0))]
+        + [AFTER] * len(after)
         + [
             pl.BlockSpec((block, 2, None, group, LANES), lambda i, k=k: (i, 0, k, 0, 0))
             for k in chosen
@@ -84,10 +87,11 @@
             8 * kinds * states * rows * width * width, 8 * kinds * states * rows * width
         ),
         name="right",
-    )(me, second, *([view] * kinds))
-
-
-def left_kernel(ranks, me_ref, first_ref, *refs):
+    )(me, second, *after, *([view] * kinds))
+
+
+def left_kernel(after, ranks, me_ref, first_ref, *refs):
+    refs = refs[after:]
     ins, outs, lines, slabs = refs[:ranks], refs[ranks:-2], refs[-2], refs[-1]
     me = me_ref[0]
     rows, wide = ins[0].shape
@@ -106,15 +110,17 @@
         out[...] = slabs[me ^ s]
 
 
-def left_call(me, first, slabs):
+def left_call(after, me, first, slabs):
     ranks = len(slabs)
     kinds, rows, wide = slabs[0].shape
     whole = ranks * rows
     spec = pl.BlockSpec((None, rows, wide), lambda i: (i, 0, 0))
     return pl.pallas_call(
-        functools.partial(left_kernel, ranks),
+        functools.partial(left_kernel, len(after), ranks),
         grid=(kinds,),
-        in_specs=[SMEM, pl.BlockSpec(first.shape, lambda i: (0, 0))] + [spec] * ranks,
+        in_specs=[SMEM, pl.BlockSpec(first.shape, lambda i: (0, 0))]
+        + [AFTER] * len(after)
+        + [spec] * ranks,
         out_specs=[spec] * ranks,
         out_shape=[jax.ShapeDtypeStruct(slabs[0].shape, jnp.bfloat16)] * ranks,
         scratch_shapes=[
@@ -126,10 +132,11 @@
             4 * kinds * whole * whole * wide, 4 * whole * whole + 4 * kinds * whole * wide
         ),
         name="left",
-    )(me, first, *slabs)
-
-
-def phase_kernel(ranks, me_ref, second_ref, cosine_ref, sine_ref, *refs):
+    )(me, first, *after, *slabs)
+
+
+def phase_kernel(after, ranks, me_ref, second_ref, cosine_ref, sine_ref, *refs):
+    refs = refs[after:]
     ins, outs, slabs = refs[:ranks], refs[ranks:-1], refs[-1]
     me = me_ref[0]
     states, rows, width = cosine_ref.shape
@@ -162,16 +169,17 @@
         out[...] = product.astype(jnp.bfloat16).reshape(2, states, rows, width)
 
 
-def phase_call(me, second, cosine, sine, slabs):
+def phase_call(after, me, second, cosine, sine, slabs):
     ranks = len(slabs)
     kinds, rows, wide = slabs[0].shape
     states, _, width = cosine.shape
     block = rows // 2
     table = pl.BlockSpec((states, block, width), lambda i: (0, i, 0))
     return pl.pallas_call(
-        functools.partial(phase_kernel, ranks),
+        functools.partial(phase_kernel, len(after), ranks),
         grid=(rows // block,),
         in_specs=[SMEM, pl.BlockSpec(second.shape, lambda i: (0, 0)), table, table]
+        + [AFTER] * len(after)
         + [pl.BlockSpec((kinds, block, wide), lambda i: (0, i, 0))] * ranks,
         out_specs=[pl.BlockSpec((2, states, block, width), lambda i: (0, 0, i, 0))] * kinds,
         out_shape=[jax.ShapeDtypeStruct((2, states, rows, width), jnp.bfloat16)] * kinds,
@@ -181,7 +189,7 @@
             8 * kinds * states * rows * width * width, 8 * kinds * states * rows * width
         ),
         name="phase",
-    )(me, second, cosine, sine, *slabs)
+    )(me, second, cosine, sine, *after, *slabs)
 
 
 def mix_kernel(up_ref, down_ref, weight_ref, *refs):
@@ -257,22 +265,34 @@
     view = packet.reshape(rows, 2, blocks, states, tiles, LANES).transpose(0, 1, 2, 4, 3, 5)
     view = view.reshape(rows, 2, blocks, tiles * states, LANES)
     edges = sorted({0, blocks - 1})
-    inner = [k for k in range(blocks) if k not in edges]
-    chunks = [c for c in (edges, inner) if c]
-
-    halves = [right_call(me, second, view, c, ranks, states, piece) for c in chunks]
-    lines = [exchanged(h, "rad") for h in halves]
-    moved = [left_call(me, first, x) for x in lines]
-    backs = [exchanged(m, "rad") for m in moved]
+    chunks = [edges] + [[k] for k in range(blocks) if k not in edges]
+
+    last = me
+    lines = []
+    for chosen in chunks:
+        half = right_call([last], me, second, view, chosen, ranks, states, piece)
+        last = half[0]
+        lines.append(exchanged(half, "rad"))
+    backs = []
+    for line in lines:
+        moved = left_call([last], me, first, line)
+        last = moved[0]
+        backs.append(exchanged(moved, "rad"))
 
     angles = potential.transpose(1, 0, 2)
     cosine, sine = jnp.cos(angles), jnp.sin(angles)
     kinetic = [None] * blocks
-    for chosen, back in zip(chunks, backs):
-        for k, value in zip(chosen, phase_call(me, second, cosine, sine, back)):
+    for n, (chosen, back) in enumerate(zip(chunks, backs)):
+        after = [last, below, above] if n == 1 else [last]
+        if n == 0:
+            after += backs[1][4:]
+        values = phase_call(after, me, second, cosine, sine, back)
+        last = values[0]
+        for k, value in zip(chosen, values):
             kinetic[k] = value
-    below = neighbour(kinetic[-1], "hel", 1)
-    above = neighbour(kinetic[0], "hel", -1)
+        if n == 0:
+            below = neighbour(kinetic[-1], "hel", 1)
+            above = neighbour(kinetic[0], "hel", -1)
 
     count = coupling.shape[0]
     helicities = jnp.arange(count, dtype=jnp.int32)

time: 231 us -> 246 us (1.065)
  local copies, waits for them, and re-layouts: 15.3 us -> 21.3 us
  Pallas kernels: 45.1 us -> 50.6 us
  starting transfers between devices: 48.1 us -> 52.8 us
    ppermute x28 -> x42, starting transfers between devices: 40.2 us -> 45.9 us  [exchanged(): result[s] = lax.ppermute(slabs[s], axis, [(i, i ^ s) for i in range(count)])]
    unnamed x26 -> x76, local copies, waits for them, and re-layouts: 4.04 us -> 9.48 us
    pallas_call x6 -> x9, Pallas kernels: 35.8 us -> 41.1 us  [the longest x3 17.9 us: left_call(): pl.pallas_call(functools.partial(left_kernel, len(after), ranks), grid=(k...]
    ppermute x28 -> x42, waiting for transfers between devices: 119 us -> 120 us  [exchanged(): result[s] = lax.ppermute(slabs[s], axis, [(i, i ^ s) for i in range(count)])]
  transfers between devices with their start and end apart: 30 -> 44, of which waited for: 17 -> 24; matrix products, arithmetic and copies ran while one was open for 5% -> 5% of each run, Pallas kernels for 13% -> 11%
where the time goes in v2:
time: 246 us; the launch traced here: 245 us
  waiting for transfers between devices  120 us (49%)
  starting transfers between devices  52.8 us (21%)
  Pallas kernels  50.6 us (21%)
  local copies, waits for them, and re-layouts  21.3 us (9%)
    ppermute x42, waiting for transfers between devices, exchanged(): result[s] = lax.ppermute(slabs[s], axis, [(i, i ^ s) for i in range(count)])  120 us
    ppermute x42, starting transfers between devices, exchanged(): result[s] = lax.ppermute(slabs[s], axis, [(i, i ^ s) for i in range(count)])  45.9 us
    pallas_call x3, Pallas kernels, left_call(): pl.pallas_call(functools.partial(left_kernel, len(after), ranks), grid=(k...  17.9 us
    pallas_call x3, Pallas kernels, right_call(): pl.pallas_call(functools.partial(right_kernel, len(after), ranks, states)...  13.3 us
    pallas_call x3, Pallas kernels, phase_call(): pl.pallas_call(functools.partial(phase_kernel, len(after), ranks), grid=(...  9.88 us
    pallas_call x1, Pallas kernels, mix_call(): pl.pallas_call(mix_kernel, grid=(rows // block,), in_specs=[SMEM, SMEM, p...  9.51 us
    unnamed x76, local copies, waits for them, and re-layouts  9.48 us
    ppermute x2, starting transfers between devices, neighbour(): return lax.ppermute(edge, axis, pairs)  6.97 us
  transfers between devices with their start and end apart: 44, of which 24 were waited for; matrix products, arithmetic and copies ran while one was open for 5% of the time, Pallas kernels for 11%

profile of v2, /device:TPU:9, one launch (start us, length us, event | category | flops | bytes accessed | tf_op | source)
XLA Modules:
  0.0 245.5 jit_solution(10082389327971761207)
XLA Ops:
  1.2 6.4 %right.3 = (bf16[2,128,512]{2,1,0:T(8,128)(2,1)S(1)}, bf16[2,128,512]{2,1,0:T(8,128)(2,1)S(1)}, bf16[2,128,512]{2,1,0:T(8,128)(2,1)S(1)}, bf16[2,128,512]{2,1,0:...) custom-call(s32[1]{0:T(128)} %bitcast.me_ref.refs_0_, ...), custom_call_target="tpu_custom_call" | custom-call | flops 2147483648 | bytes 4194304 | tf_op jit(solution)/shard_map/right/pallas_call | solution.py:70
  7.6 1.2 collective-permute-start
  9.0 3.4 %right.4 = (bf16[1,128,512]{2,1,0:T(8,128)(2,1)S(1)}, bf16[1,128,512]{2,1,0:T(8,128)(2,1)S(1)}, bf16[1,128,512]{2,1,0:T(8,128)(2,1)S(1)}, bf16[1,128,512]{2,1,0:...) custom-call(s32[1]{0:T(128)} %bitcast.me_ref.refs_0_, ...), custom_call_target="tpu_custom_call" | custom-call | flops 1073741824 | bytes 2097152 | tf_op jit(solution)/shard_map/right/pallas_call | solution.py:70
  15.7 2.3 collective-permute-start.10
  18.0 2.2 collective-permute-start.2
  20.3 3.9 %collective-permute-done.10.refs_5_ = bf16[1,128,512]{2,1,0:T(8,128)(2,1)S(1)} collective-permute-done((bf16[1,128,512]{2,1,0:T(8,128)(2,1)S(1)}, bf16[1,128,512]{2,1,0:T(8,128)(2,1)S(1)}, u32[]{:S(2)}, u32[]{:S(2)}) %collective-permute-start.10) | collective-permute-done | bytes 131104 | tf_op jit(solution)/shard_map/ppermute | solution.py:246
  24.8 3.6 %collective-permute-start.3 = (bf16[2,128,512]{2,1,0:T(8,128)(2,1)S(1)}, bf16[2,128,512]{2,1,0:T(8,128)(2,1)S(1)}, u32[]{:S(2)}, u32[]{:S(2)}) collective-permute-start(bf16[2,128,512]{2,1,0:T(8,128)(2,1)S(1)} %get-tuple-element.61), channel_id=1, source_target_pairs={{0,4},{1,5},{2,6},{3,7},{4,0},{5,1},{6,2},{7,3},{8,12},{9,13},{10,... | collective-permute-start | bytes 786440 | tf_op jit(solution)/shard_map/ppermute | solution.py:246
  29.3 4.0 %collective-permute-start.4 = (bf16[2,128,512]{2,1,0:T(8,128)(2,1)S(1)}, bf16[2,128,512]{2,1,0:T(8,128)(2,1)}, u32[]{:S(2)}, u32[]{:S(2)}) collective-permute-start(bf16[2,128,512]{2,1,0:T(8,128)(2,1)S(1)} %get-tuple-element.62), channel_id=1, source_target_pairs={{0,5},{1,4},{2,7},{3,6},{4,1},{5,0},{6,3},{7,2},{8,13},{9,12},{10,... | collective-permute-start | bytes 786440 | tf_op jit(solution)/shard_map/ppermute | solution.py:246
  35.1 6.5 %copy.14 = bf16[2048,1024]{0,1:T(8,128)(2,1)} copy(bf16[2048,1024]{1,0:T(8,128)(2,1)} %bitcast.29) | data formatting | bytes 8388608 | tf_op jit(solution)/shard_map/reshape | solution.py:264
  41.7 3.5 %right.5 = (bf16[1,128,512]{2,1,0:T(8,128)(2,1)S(1)}, bf16[1,128,512]{2,1,0:T(8,128)(2,1)S(1)}, bf16[1,128,512]{2,1,0:T(8,128)(2,1)S(1)}, bf16[1,128,512]{2,1,0:...) custom-call(s32[1]{0:T(128)} %bitcast.me_ref.refs_0_, ...), custom_call_target="tpu_custom_call" | custom-call | flops 1073741824 | bytes 2097152 | tf_op jit(solution)/shard_map/right/pallas_call | solution.py:70
  45.2 1.5 collective-permute-start.12
  46.7 12.9 %collective-permute-done.3.refs_5_ = bf16[2,128,512]{2,1,0:T(8,128)(2,1)S(1)} collective-permute-done((bf16[2,128,512]{2,1,0:T(8,128)(2,1)S(1)}, bf16[2,128,512]{2,1,0:T(8,128)(2,1)S(1)}, u32[]{:S(2)}, u32[]{:S(2)}) %collective-permute-start.3) | collective-permute-done | bytes 262176 | tf_op jit(solution)/shard_map/ppermute | solution.py:246
  60.3 6.2 %collective-permute-done.4.refs_6_ = bf16[2,128,512]{2,1,0:T(8,128)(2,1)} collective-permute-done((bf16[2,128,512]{2,1,0:T(8,128)(2,1)S(1)}, bf16[2,128,512]{2,1,0:T(8,128)(2,1)}, u32[]{:S(2)}, u32[]{:S(2)}) %collective-permute-start.4) | collective-permute-done | bytes 262176 | tf_op jit(solution)/shard_map/ppermute | solution.py:246
  66.6 8.9 %collective-permute-done.5.refs_7_ = bf16[2,128,512]{2,1,0:T(8,128)(2,1)} collective-permute-done((bf16[2,128,512]{2,1,0:T(8,128)(2,1)S(1)}, bf16[2,128,512]{2,1,0:T(8,128)(2,1)}, u32[]{:S(2)}, u32[]{:S(2)}) %collective-permute-start.5) | collective-permute-done | bytes 262176 | tf_op jit(solution)/shard_map/ppermute | solution.py:246
  75.5 5.3 %collective-permute-done.6.refs_8_ = bf16[2,128,512]{2,1,0:T(8,128)(2,1)} collective-permute-done((bf16[2,128,512]{2,1,0:T(8,128)(2,1)S(1)}, bf16[2,128,512]{2,1,0:T(8,128)(2,1)}, u32[]{:S(2)}, u32[]{:S(2)}) %collective-permute-start.6) | collective-permute-done | bytes 262176 | tf_op jit(solution)/shard_map/ppermute | solution.py:246
  80.9 7.7 %left.3 = (bf16[2,128,512]{2,1,0:T(8,128)(2,1)S(1)}, bf16[2,128,512]{2,1,0:T(8,128)(2,1)S(1)}, bf16[2,128,512]{2,1,0:T(8,128)(2,1)S(1)}, bf16[2,128,512]{2,1,0:T...) custom-call(s32[1]{0:T(128)} %bitcast.me_ref.refs_0_, ...), custom_call_target="tpu_custom_call" | custom-call | flops 4294967296 | bytes 8388608 | tf_op jit(solution)/shard_map/left/pallas_call | solution.py:118
  88.6 1.5 collective-permute-start.14
  92.5 1.5 collective-permute-start.17
  94.9 5.4 %left.4 = (bf16[1,128,512]{2,1,0:T(8,128)(2,1)S(1)}, bf16[1,128,512]{2,1,0:T(8,128)(2,1)}, bf16[1,128,512]{2,1,0:T(8,128)(2,1)}, bf16[1,128,512]{2,1,0:T(8,128)(...) custom-call(s32[1]{0:T(128)} %bitcast.me_ref.refs_0_, ...), custom_call_target="tpu_custom_call" | custom-call | flops 2147483648 | bytes 6291456 | tf_op jit(solution)/shard_map/left/pallas_call | solution.py:118
  100.7 2.0 collective-permute-start.20
  102.7 3.3 %collective-permute-start.21 = (bf16[1,128,512]{2,1,0:T(8,128)(2,1)S(1)}, bf16[1,128,512]{2,1,0:T(8,128)(2,1)S(1)}, u32[]{:S(2)}, u32[]{:S(2)}) collective-permute-start(bf16[1,128,512]{2,1,0:T(8,128)(2,1)S(1)} %get-tuple-element.82), channel_id=1, source_target_pairs={{0,4},{1,5},{2,6},{3,7},{4,0},{5,1},{6,2},{7,3},{8,12},{9,13},{10,... | collective-permute-start | bytes 393224 | tf_op jit(solution)/shard_map/ppermute | solution.py:246
  106.6 8.6 %collective-permute-done.19.refs_7_ = bf16[1,128,512]{2,1,0:T(8,128)(2,1)S(1)} collective-permute-done((bf16[1,128,512]{2,1,0:T(8,128)(2,1)S(1)}, bf16[1,128,512]{2,1,0:T(8,128)(2,1)S(1)}, u32[]{:S(2)}, u32[]{:S(2)}) %collective-permute-start.19) | collective-permute-done | bytes 131104 | tf_op jit(solution)/shard_map/ppermute | solution.py:246
  115.2 4.2 %collective-permute-done.20.refs_8_ = bf16[1,128,512]{2,1,0:T(8,128)(2,1)S(1)} collective-permute-done((bf16[1,128,512]{2,1,0:T(8,128)(2,1)S(1)}, bf16[1,128,512]{2,1,0:T(8,128)(2,1)S(1)}, u32[]{:S(2)}, u32[]{:S(2)}) %collective-permute-start.20) | collective-permute-done | bytes 131104 | tf_op jit(solution)/shard_map/ppermute | solution.py:246
  119.9 3.8 %collective-permute-done.21.refs_1_.refs_7_ = bf16[1,128,512]{2,1,0:T(8,128)(2,1)S(1)} collective-permute-done((bf16[1,128,512]{2,1,0:T(8,128)(2,1)S(1)}, bf16[1,128,512]{2,1,0:T(8,128)(2,1)S(1)}, u32[]{:S(2)}, u32[]{:S(2)}) %collective-permute-start.21) | collective-permute-done | bytes 131104 | tf_op jit(solution)/shard_map/ppermute | solution.py:246
  124.7 5.9 %collective-permute-done.22.refs_2_.refs_8_ = bf16[1,128,512]{2,1,0:T(8,128)(2,1)S(1)} collective-permute-done((bf16[1,128,512]{2,1,0:T(8,128)(2,1)S(1)}, bf16[1,128,512]{2,1,0:T(8,128)(2,1)S(1)}, u32[]{:S(2)}, u32[]{:S(2)}) %collective-permute-start.22) | collective-permute-done | bytes 131104 | tf_op jit(solution)/shard_map/ppermute | solution.py:246
  131.1 3.5 %collective-permute-done.23.refs_3_.refs_9_ = bf16[1,128,512]{2,1,0:T(8,128)(2,1)S(1)} collective-permute-done((bf16[1,128,512]{2,1,0:T(8,128)(2,1)S(1)}, bf16[1,128,512]{2,1,0:T(8,128)(2,1)S(1)}, u32[]{:S(2)}, u32[]{:S(2)}) %collective-permute-start.23) | collective-permute-done | bytes 131104 | tf_op jit(solution)/shard_map/ppermute | solution.py:246
  134.6 4.0 %collective-permute-done.24.refs_4_.refs_10_ = bf16[1,128,512]{2,1,0:T(8,128)(2,1)S(1)} collective-permute-done((bf16[1,128,512]{2,1,0:T(8,128)(2,1)S(1)}, bf16[1,128,512]{2,1,0:T(8,128)(2,1)S(1)}, u32[]{:S(2)}, u32[]{:S(2)}) %collective-permute-start.24) | collective-permute-done | bytes 131104 | tf_op jit(solution)/shard_map/ppermute | solution.py:246
  139.8 3.6 %collective-permute-start.31 = (bf16[2,128,512]{2,1,0:T(8,128)(2,1)S(1)}, bf16[2,128,512]{2,1,0:T(8,128)(2,1)S(1)}, u32[]{:S(2)}, u32[]{:S(2)}) collective-permute-start(bf16[2,128,512]{2,1,0:T(8,128)(2,1)S(1)} %get-tuple-element.92), channel_id=1, source_target_pairs={{0,7},{1,6},{2,5},{3,4},{4,3},{5,2},{6,1},{7,0},{8,15},{9,14},{10,... | collective-permute-start | bytes 786440 | tf_op jit(solution)/shard_map/ppermute | solution.py:246
  143.4 4.6 %sine_bitcast_fusion = (f32[4,128,512]{2,1,0:T(8,128)}, f32[4,128,512]{2,1,0:T(8,128)}) fusion(f32[128,4,512]{2,1,0:T(4,128)S(1)} %copy-done.35), kind=kLoop, calls=%fused_computation | loop fusion | bytes 3145728 | tf_op jit(solution)/shard_map/sin | solution.py:283
  148.0 4.7 %left.5 = (bf16[1,128,512]{2,1,0:T(8,128)(2,1)S(1)}, bf16[1,128,512]{2,1,0:T(8,128)(2,1)S(1)}, bf16[1,128,512]{2,1,0:T(8,128)(2,1)S(1)}, bf16[1,128,512]{2,1,0:T...) custom-call(s32[1]{0:T(128)} %bitcast.me_ref.refs_0_, ...), custom_call_target="tpu_custom_call" | custom-call | flops 2147483648 | bytes 6291456 | tf_op jit(solution)/shard_map/left/pallas_call | solution.py:118
  153.4 4.0 %collective-permute-done.28.refs_9_ = bf16[2,128,512]{2,1,0:T(8,128)(2,1)S(1)} collective-permute-done((bf16[2,128,512]{2,1,0:T(8,128)(2,1)S(1)}, bf16[2,128,512]{2,1,0:T(8,128)(2,1)S(1)}, u32[]{:S(2)}, u32[]{:S(2)}) %collective-permute-start.28) | collective-permute-done | bytes 262176 | tf_op jit(solution)/shard_map/ppermute | solution.py:246
  157.4 14.0 %collective-permute-done.29.refs_10_ = bf16[2,128,512]{2,1,0:T(8,128)(2,1)S(1)} collective-permute-done((bf16[2,128,512]{2,1,0:T(8,128)(2,1)S(1)}, bf16[2,128,512]{2,1,0:T(8,128)(2,1)S(1)}, u32[]{:S(2)}, u32[]{:S(2)}) %collective-permute-start.29) | collective-permute-done | bytes 262176 | tf_op jit(solution)/shard_map/ppermute | solution.py:246
  171.4 7.0 %collective-permute-done.30.refs_11_ = bf16[2,128,512]{2,1,0:T(8,128)(2,1)S(1)} collective-permute-done((bf16[2,128,512]{2,1,0:T(8,128)(2,1)S(1)}, bf16[2,128,512]{2,1,0:T(8,128)(2,1)S(1)}, u32[]{:S(2)}, u32[]{:S(2)}) %collective-permute-start.30) | collective-permute-done | bytes 262176 | tf_op jit(solution)/shard_map/ppermute | solution.py:246
  178.5 6.0 %collective-permute-done.31.refs_12_ = bf16[2,128,512]{2,1,0:T(8,128)(2,1)S(1)} collective-permute-done((bf16[2,128,512]{2,1,0:T(8,128)(2,1)S(1)}, bf16[2,128,512]{2,1,0:T(8,128)(2,1)S(1)}, u32[]{:S(2)}, u32[]{:S(2)}) %collective-permute-start.31) | collective-permute-done | bytes 262176 | tf_op jit(solution)/shard_map/ppermute | solution.py:246
  184.4 4.8 %phase.3 = (bf16[2,4,128,512]{3,2,1,0:T(8,128)(2,1)}, bf16[2,4,128,512]{3,2,1,0:T(8,128)(2,1)}) custom-call(s32[1]{0:T(128)} %bitcast.me_ref.refs_0_, bf16[1024,512]{1,0:T(8,128)(2,1)S(1)} %bitcast.22, f32[4,128,512]{2,1,0:T(8,128)} %get-tuple-element.106.cosine_ref, f32[4,128,512]{2,1,0:T(8,128)} %get-tuple-element.105.sine_ref, ...), custom_call_target="tpu_custom_call" | custom-call | flops 2147483648 | bytes 4194304 | tf_op jit(solution)/shard_map/phase/pallas_call | solution.py:178
  189.3 5.0 %collective-permute-start.32 = (bf16[2,4,128,512]{3,2,1,0:T(8,128)(2,1)}, bf16[2,4,128,512]{3,2,1,0:T(8,128)(2,1)}, u32[]{:S(2)}, u32[]{:S(2)}) collective-permute-start(bf16[2,4,128,512]{3,2,1,0:T(8,128)(2,1)} %get-tuple-element.93.refs_4_), channel_id=1, source_target_pairs={{0,8},{8,16},{16,24},{1,9},{9,17},{17,25},{2,10},{10,18},{18,26},{... | collective-permute-start | bytes 3145736 | tf_op jit(solution)/shard_map/ppermute | solution.py:253
  194.3 1.9 collective-permute-start.33
  196.3 1.4 collective-permute-start.34
  197.7 1.3 collective-permute-start.36
  199.0 2.2 collective-permute-done.34.refs_4_
  206.1 2.2 collective-permute-done.37.refs_2_
  208.7 3.1 %collective-permute-start.41 = (bf16[1,128,512]{2,1,0:T(8,128)(2,1)}, bf16[1,128,512]{2,1,0:T(8,128)(2,1)S(1)}, u32[]{:S(2)}, u32[]{:S(2)}) collective-permute-start(bf16[1,128,512]{2,1,0:T(8,128)(2,1)} %copy-done.16), channel_id=1, source_target_pairs={{0,5},{1,4},{2,7},{3,6},{4,1},{5,0},{6,3},{7,2},{8,13},{9,12},{10,... | collective-permute-start | bytes 393224 | tf_op jit(solution)/shard_map/ppermute | solution.py:246
  215.6 2.5 %phase.4.refs_0_.refs_2_ = bf16[2,4,128,512]{3,2,1,0:T(8,128)(2,1)S(1)} custom-call(s32[1]{0:T(128)} %bitcast.me_ref.refs_0_, bf16[1024,512]{1,0:T(8,128)(2,1)S(1)} %bitcast.23, f32[4,128,512]{2,1,0:T(8,128)S(1)} %copy-done.3, f32[4,128,512]{2,1,0:T(8,128)S(1)} %copy-done.2, bf16[2,4,128,512]{3,2,1,0:T(8,128)(2,1)} %get-tuple-element.94.refs_0_.refs_1_, ...), custom_call_target="tpu_custom_call" | custom-call | flops 1073741824 | bytes 2097152 | tf_op jit(solution)/shard_map/phase/pallas_call | solution.py:178
  219.1 6.3 %collective-permute-done.41.refs_6_ = bf16[1,128,512]{2,1,0:T(8,128)(2,1)S(1)} collective-permute-done((bf16[1,128,512]{2,1,0:T(8,128)(2,1)}, bf16[1,128,512]{2,1,0:T(8,128)(2,1)S(1)}, u32[]{:S(2)}, u32[]{:S(2)}) %collective-permute-start.41) | collective-permute-done | bytes 131104 | tf_op jit(solution)/shard_map/ppermute | solution.py:246
  225.4 4.4 %collective-permute-done.42.refs_7_ = bf16[1,128,512]{2,1,0:T(8,128)(2,1)S(1)} collective-permute-done((bf16[1,128,512]{2,1,0:T(8,128)(2,1)}, bf16[1,128,512]{2,1,0:T(8,128)(2,1)S(1)}, u32[]{:S(2)}, u32[]{:S(2)}) %collective-permute-start.42) | collective-permute-done | bytes 131104 | tf_op jit(solution)/shard_map/ppermute | solution.py:246
  229.8 3.7 %collective-permute-done.43.refs_8_ = bf16[1,128,512]{2,1,0:T(8,128)(2,1)S(1)} collective-permute-done((bf16[1,128,512]{2,1,0:T(8,128)(2,1)}, bf16[1,128,512]{2,1,0:T(8,128)(2,1)S(1)}, u32[]{:S(2)}, u32[]{:S(2)}) %collective-permute-start.43) | collective-permute-done | bytes 131104 | tf_op jit(solution)/shard_map/ppermute | solution.py:246
  233.4 2.5 %phase.5.refs_3_ = bf16[2,4,128,512]{3,2,1,0:T(8,128)(2,1)S(1)} custom-call(s32[1]{0:T(128)} %bitcast.me_ref.refs_0_, bf16[1024,512]{1,0:T(8,128)(2,1)S(1)} %bitcast.24, f32[4,128,512]{2,1,0:T(8,128)S(1)} %copy-done.3, f32[4,128,512]{2,1,0:T(8,128)S(1)} %copy-done.2, bf16[2,4,128,512]{3,2,1,0:T(8,128)(2,1)} %copy-done.4, ...), custom_call_target="tpu_custom_call" | custom-call | flops 1073741824 | bytes 2097152 | tf_op jit(solution)/shard_map/phase/pallas_call | solution.py:178
  236.0 9.5 %mix.1 = bf16[128,2,4,16,128]{4,3,2,1,0:T(8,128)(2,1)} custom-call(f32[4,4]{1,0:T(4,128)S(1)} %get-tuple-element.108.up_ref, f32[4,4]{1,0:T(4,128)S(1)} %get-tuple-element.107.down_ref, f32[128,512]{1,0:T(8,128)S(1)} %copy-done.6, bf16[2,4,128,512]{3,2,1,0:T(8,128)(2,1)} %collective-permute-done.32.refs_1_.refs_0_, ...), custom_call_target="tpu_custom_call" | custom-call | flops 20971520 | bytes 10485760 | tf_op jit(solution)/shard_map/mix/pallas_call | solution.py:226
  (132 shorter events, 26.8 us)
Async XLA Ops:
  7.6 25.7 %collective-permute-start = (bf16[2,128,512]{2,1,0:T(8,128)(2,1)S(1)}, bf16[2,128,512]{2,1,0:T(8,128)(2,1)S(1)}, u32[]{:S(2)}, u32[]{:S(2)}) collective-permute-start(bf16[2,128,512]{2,1,0:T(8,128)(2,1)S(1)} %get-tuple-element.58), channel_id=1, source_target_pairs={{0,1},{1,0},{2,3},{3,2},{4,5},{5,4},{6,7},{7,6},{8,9},{9,8},{10,11... | collective-permute-start | bytes 786440 | tf_op jit(solution)/shard_map/ppermute | solution.py:246
  8.9 25.4 %collective-permute-start.1 = (bf16[2,128,512]{2,1,0:T(8,128)(2,1)S(1)}, bf16[2,128,512]{2,1,0:T(8,128)(2,1)S(1)}, u32[]{:S(2)}, u32[]{:S(2)}) collective-permute-start(bf16[2,128,512]{2,1,0:T(8,128)(2,1)S(1)} %get-tuple-element.59), channel_id=1, source_target_pairs={{0,2},{1,3},{2,0},{3,1},{4,6},{5,7},{6,4},{7,5},{8,10},{9,11},{10,... | collective-permute-start | bytes 786440 | tf_op jit(solution)/shard_map/ppermute | solution.py:246
  15.7 8.4 %collective-permute-start.10 = (bf16[1,128,512]{2,1,0:T(8,128)(2,1)S(1)}, bf16[1,128,512]{2,1,0:T(8,128)(2,1)S(1)}, u32[]{:S(2)}, u32[]{:S(2)}) collective-permute-start(bf16[1,128,512]{2,1,0:T(8,128)(2,1)S(1)} %get-tuple-element.69), channel_id=1, source_target_pairs={{0,4},{1,5},{2,6},{3,7},{4,0},{5,1},{6,2},{7,3},{8,12},{9,13},{10,... | collective-permute-start | bytes 393224 | tf_op jit(solution)/shard_map/ppermute | solution.py:246
  18.0 10.6 %collective-permute-start.11 = (bf16[1,128,512]{2,1,0:T(8,128)(2,1)S(1)}, bf16[1,128,512]{2,1,0:T(8,128)(2,1)S(1)}, u32[]{:S(2)}, u32[]{:S(2)}) collective-permute-start(bf16[1,128,512]{2,1,0:T(8,128)(2,1)S(1)} %get-tuple-element.70), channel_id=1, source_target_pairs={{0,5},{1,4},{2,7},{3,6},{4,1},{5,0},{6,3},{7,2},{8,13},{9,12},{10,... | collective-permute-start | bytes 393224 | tf_op jit(solution)/shard_map/ppermute | solution.py:246
  18.0 27.1 %collective-permute-start.2 = (bf16[2,128,512]{2,1,0:T(8,128)(2,1)}, bf16[2,128,512]{2,1,0:T(8,128)(2,1)S(1)}, u32[]{:S(2)}, u32[]{:S(2)}) collective-permute-start(bf16[2,128,512]{2,1,0:T(8,128)(2,1)} %get-tuple-element.60), channel_id=1, source_target_pairs={{0,3},{1,2},{2,1},{3,0},{4,7},{5,6},{6,5},{7,4},{8,11},{9,10},{10,... | collective-permute-start | bytes 786440 | tf_op jit(solution)/shard_map/ppermute | solution.py:246
  24.8 34.7 %collective-permute-start.3 = (bf16[2,128,512]{2,1,0:T(8,128)(2,1)S(1)}, bf16[2,128,512]{2,1,0:T(8,128)(2,1)S(1)}, u32[]{:S(2)}, u32[]{:S(2)}) collective-permute-start(bf16[2,128,512]{2,1,0:T(8,128)(2,1)S(1)} %get-tuple-element.61), channel_id=1, source_target_pairs={{0,4},{1,5},{2,6},{3,7},{4,0},{5,1},{6,2},{7,3},{8,12},{9,13},{10,... | collective-permute-start | bytes 786440 | tf_op jit(solution)/shard_map/ppermute | solution.py:246
  29.3 37.3 %collective-permute-start.4 = (bf16[2,128,512]{2,1,0:T(8,128)(2,1)S(1)}, bf16[2,128,512]{2,1,0:T(8,128)(2,1)}, u32[]{:S(2)}, u32[]{:S(2)}) collective-permute-start(bf16[2,128,512]{2,1,0:T(8,128)(2,1)S(1)} %get-tuple-element.62), channel_id=1, source_target_pairs={{0,5},{1,4},{2,7},{3,6},{4,1},{5,0},{6,3},{7,2},{8,13},{9,12},{10,... | collective-permute-start | bytes 786440 | tf_op jit(solution)/shard_map/ppermute | solution.py:246
  33.3 42.2 %collective-permute-start.5 = (bf16[2,128,512]{2,1,0:T(8,128)(2,1)S(1)}, bf16[2,128,512]{2,1,0:T(8,128)(2,1)}, u32[]{:S(2)}, u32[]{:S(2)}) collective-permute-start(bf16[2,128,512]{2,1,0:T(8,128)(2,1)S(1)} %get-tuple-element.63), channel_id=1, source_target_pairs={{0,6},{1,7},{2,4},{3,5},{4,2},{5,3},{6,0},{7,1},{8,14},{9,15},{10,... | collective-permute-start | bytes 786440 | tf_op jit(solution)/shard_map/ppermute | solution.py:246
  34.3 46.6 %collective-permute-start.6 = (bf16[2,128,512]{2,1,0:T(8,128)(2,1)S(1)}, bf16[2,128,512]{2,1,0:T(8,128)(2,1)}, u32[]{:S(2)}, u32[]{:S(2)}) collective-permute-start(bf16[2,128,512]{2,1,0:T(8,128)(2,1)S(1)} %get-tuple-element.64), channel_id=1, source_target_pairs={{0,7},{1,6},{2,5},{3,4},{4,3},{5,2},{6,1},{7,0},{8,15},{9,14},{10,... | collective-permute-start | bytes 786440 | tf_op jit(solution)/shard_map/ppermute | solution.py:246
  45.2 43.4 %collective-permute-start.12 = (bf16[1,128,512]{2,1,0:T(8,128)(2,1)S(1)}, bf16[1,128,512]{2,1,0:T(8,128)(2,1)S(1)}, u32[]{:S(2)}, u32[]{:S(2)}) collective-permute-start(bf16[1,128,512]{2,1,0:T(8,128)(2,1)S(1)} %copy-done.34), channel_id=1, source_target_pairs={{0,6},{1,7},{2,4},{3,5},{4,2},{5,3},{6,0},{7,1},{8,14},{9,15},{10,... | collective-permute-start | bytes 393224 | tf_op jit(solution)/shard_map/ppermute | solution.py:246
  59.6 30.6 %collective-permute-start.13 = (bf16[1,128,512]{2,1,0:T(8,128)(2,1)S(1)}, bf16[1,128,512]{2,1,0:T(8,128)(2,1)S(1)}, u32[]{:S(2)}, u32[]{:S(2)}) collective-permute-start(bf16[1,128,512]{2,1,0:T(8,128)(2,1)S(1)} %copy-done.31), channel_id=1, source_target_pairs={{0,7},{1,6},{2,5},{3,4},{4,3},{5,2},{6,1},{7,0},{8,15},{9,14},{10,... | collective-permute-start | bytes 393224 | tf_op jit(solution)/shard_map/ppermute | solution.py:246
  66.6 24.8 %collective-permute-start.7 = (bf16[1,128,512]{2,1,0:T(8,128)(2,1)S(1)}, bf16[1,128,512]{2,1,0:T(8,128)(2,1)S(1)}, u32[]{:S(2)}, u32[]{:S(2)}) collective-permute-start(bf16[1,128,512]{2,1,0:T(8,128)(2,1)S(1)} %copy-done.28), channel_id=1, source_target_pairs={{0,1},{1,0},{2,3},{3,2},{4,5},{5,4},{6,7},{7,6},{8,9},{9,8},{10,11... | collective-permute-start | bytes 393224 | tf_op jit(solution)/shard_map/ppermute | solution.py:246
  75.5 17.0 %collective-permute-start.8 = (bf16[1,128,512]{2,1,0:T(8,128)(2,1)S(1)}, bf16[1,128,512]{2,1,0:T(8,128)(2,1)S(1)}, u32[]{:S(2)}, u32[]{:S(2)}) collective-permute-start(bf16[1,128,512]{2,1,0:T(8,128)(2,1)S(1)} %copy-done.26), channel_id=1, source_target_pairs={{0,2},{1,3},{2,0},{3,1},{4,6},{5,7},{6,4},{7,5},{8,10},{9,11},{10,... | collective-permute-start | bytes 393224 | tf_op jit(solution)/shard_map/ppermute | solution.py:246
  80.8 13.2 %collective-permute-start.9 = (bf16[1,128,512]{2,1,0:T(8,128)(2,1)S(1)}, bf16[1,128,512]{2,1,0:T(8,128)(2,1)S(1)}, u32[]{:S(2)}, u32[]{:S(2)}) collective-permute-start(bf16[1,128,512]{2,1,0:T(8,128)(2,1)S(1)} %copy-done.24), channel_id=1, source_target_pairs={{0,3},{1,2},{2,1},{3,0},{4,7},{5,6},{6,5},{7,4},{8,11},{9,10},{10,... | collective-permute-start | bytes 393224 | tf_op jit(solution)/shard_map/ppermute | solution.py:246
  88.6 54.8 %copy-start.35 = (f32[128,4,512]{2,1,0:T(4,128)S(1)}, f32[128,4,512]{2,1,0:T(4,128)}, u32[]{:S(2)}) copy-start(f32[128,4,512]{2,1,0:T(4,128)} %param.9) | copy-start | bytes 3145732
  88.6 11.7 %collective-permute-start.14 = (bf16[1,128,512]{2,1,0:T(8,128)(2,1)S(1)}, bf16[1,128,512]{2,1,0:T(8,128)(2,1)S(1)}, u32[]{:S(2)}, u32[]{:S(2)}) collective-permute-start(bf16[1,128,512]{2,1,0:T(8,128)(2,1)S(1)} %get-tuple-element.74), channel_id=1, source_target_pairs={{0,1},{1,0},{2,3},{3,2},{4,5},{5,4},{6,7},{7,6},{8,9},{9,8},{10,11... | collective-permute-start | bytes 393224 | tf_op jit(solution)/shard_map/ppermute | solution.py:246
  90.1 10.6 %collective-permute-start.15 = (bf16[1,128,512]{2,1,0:T(8,128)(2,1)S(1)}, bf16[1,128,512]{2,1,0:T(8,128)(2,1)S(1)}, u32[]{:S(2)}, u32[]{:S(2)}) collective-permute-start(bf16[1,128,512]{2,1,0:T(8,128)(2,1)S(1)} %get-tuple-element.75), channel_id=1, source_target_pairs={{0,2},{1,3},{2,0},{3,1},{4,6},{5,7},{6,4},{7,5},{8,10},{9,11},{10,... | collective-permute-start | bytes 393224 | tf_op jit(solution)/shard_map/ppermute | solution.py:246
  91.3 11.4 %collective-permute-start.16 = (bf16[1,128,512]{2,1,0:T(8,128)(2,1)S(1)}, bf16[1,128,512]{2,1,0:T(8,128)(2,1)S(1)}, u32[]{:S(2)}, u32[]{:S(2)}) collective-permute-start(bf16[1,128,512]{2,1,0:T(8,128)(2,1)S(1)} %get-tuple-element.76), channel_id=1, source_target_pairs={{0,3},{1,2},{2,1},{3,0},{4,7},{5,6},{6,5},{7,4},{8,11},{9,10},{10,... | collective-permute-start | bytes 393224 | tf_op jit(solution)/shard_map/ppermute | solution.py:246
  92.5 13.5 %collective-permute-start.17 = (bf16[1,128,512]{2,1,0:T(8,128)(2,1)S(1)}, bf16[1,128,512]{2,1,0:T(8,128)(2,1)S(1)}, u32[]{:S(2)}, u32[]{:S(2)}) collective-permute-start(bf16[1,128,512]{2,1,0:T(8,128)(2,1)S(1)} %get-tuple-element.77), channel_id=1, source_target_pairs={{0,4},{1,5},{2,6},{3,7},{4,0},{5,1},{6,2},{7,3},{8,12},{9,13},{10,... | collective-permute-start | bytes 393224 | tf_op jit(solution)/shard_map/ppermute | solution.py:246
  94.0 12.2 %collective-permute-start.18 = (bf16[1,128,512]{2,1,0:T(8,128)(2,1)S(1)}, bf16[1,128,512]{2,1,0:T(8,128)(2,1)S(1)}, u32[]{:S(2)}, u32[]{:S(2)}) collective-permute-start(bf16[1,128,512]{2,1,0:T(8,128)(2,1)S(1)} %get-tuple-element.78), channel_id=1, source_target_pairs={{0,5},{1,4},{2,7},{3,6},{4,1},{5,0},{6,3},{7,2},{8,13},{9,12},{10,... | collective-permute-start | bytes 393224 | tf_op jit(solution)/shard_map/ppermute | solution.py:246
  100.3 88.9 %copy-start.13 = (bf16[1,128,512]{2,1,0:T(8,128)(2,1)}, bf16[1,128,512]{2,1,0:T(8,128)(2,1)S(1)}, u32[]{:S(2)}) copy-start(bf16[1,128,512]{2,1,0:T(8,128)(2,1)S(1)} %get-tuple-element.97) | copy-start | bytes 393220
  100.3 14.9 %collective-permute-start.19 = (bf16[1,128,512]{2,1,0:T(8,128)(2,1)S(1)}, bf16[1,128,512]{2,1,0:T(8,128)(2,1)S(1)}, u32[]{:S(2)}, u32[]{:S(2)}) collective-permute-start(bf16[1,128,512]{2,1,0:T(8,128)(2,1)S(1)} %get-tuple-element.79), channel_id=1, source_target_pairs={{0,6},{1,7},{2,4},{3,5},{4,2},{5,3},{6,0},{7,1},{8,14},{9,15},{10,... | collective-permute-start | bytes 393224 | tf_op jit(solution)/shard_map/ppermute | solution.py:246
  100.7 18.8 %collective-permute-start.20 = (bf16[1,128,512]{2,1,0:T(8,128)(2,1)S(1)}, bf16[1,128,512]{2,1,0:T(8,128)(2,1)S(1)}, u32[]{:S(2)}, u32[]{:S(2)}) collective-permute-start(bf16[1,128,512]{2,1,0:T(8,128)(2,1)S(1)} %get-tuple-element.80), channel_id=1, source_target_pairs={{0,7},{1,6},{2,5},{3,4},{4,3},{5,2},{6,1},{7,0},{8,15},{9,14},{10,... | collective-permute-start | bytes 393224 | tf_op jit(solution)/shard_map/ppermute | solution.py:246
  102.7 21.0 %collective-permute-start.21 = (bf16[1,128,512]{2,1,0:T(8,128)(2,1)S(1)}, bf16[1,128,512]{2,1,0:T(8,128)(2,1)S(1)}, u32[]{:S(2)}, u32[]{:S(2)}) collective-permute-start(bf16[1,128,512]{2,1,0:T(8,128)(2,1)S(1)} %get-tuple-element.82), channel_id=1, source_target_pairs={{0,4},{1,5},{2,6},{3,7},{4,0},{5,1},{6,2},{7,3},{8,12},{9,13},{10,... | collective-permute-start | bytes 393224 | tf_op jit(solution)/shard_map/ppermute | solution.py:246
  106.0 32.6 %collective-permute-start.25 = (bf16[2,128,512]{2,1,0:T(8,128)(2,1)S(1)}, bf16[2,128,512]{2,1,0:T(8,128)(2,1)S(1)}, u32[]{:S(2)}, u32[]{:S(2)}) collective-permute-start(bf16[2,128,512]{2,1,0:T(8,128)(2,1)S(1)} %get-tuple-element.86), channel_id=1, source_target_pairs={{0,1},{1,0},{2,3},{3,2},{4,5},{5,4},{6,7},{7,6},{8,9},{9,8},{10,11... | collective-permute-start | bytes 786440 | tf_op jit(solution)/shard_map/ppermute | solution.py:246
  106.2 33.5 %collective-permute-start.26 = (bf16[2,128,512]{2,1,0:T(8,128)(2,1)S(1)}, bf16[2,128,512]{2,1,0:T(8,128)(2,1)S(1)}, u32[]{:S(2)}, u32[]{:S(2)}) collective-permute-start(bf16[2,128,512]{2,1,0:T(8,128)(2,1)S(1)} %get-tuple-element.87), channel_id=1, source_target_pairs={{0,2},{1,3},{2,0},{3,1},{4,6},{5,7},{6,4},{7,5},{8,10},{9,11},{10,... | collective-permute-start | bytes 786440 | tf_op jit(solution)/shard_map/ppermute | solution.py:246
  115.2 15.3 %collective-permute-start.22 = (bf16[1,128,512]{2,1,0:T(8,128)(2,1)S(1)}, bf16[1,128,512]{2,1,0:T(8,128)(2,1)S(1)}, u32[]{:S(2)}, u32[]{:S(2)}) collective-permute-start(bf16[1,128,512]{2,1,0:T(8,128)(2,1)S(1)} %get-tuple-element.83), channel_id=1, source_target_pairs={{0,5},{1,4},{2,7},{3,6},{4,1},{5,0},{6,3},{7,2},{8,13},{9,12},{10,... | collective-permute-start | bytes 393224 | tf_op jit(solution)/shard_map/ppermute | solution.py:246
  119.5 15.1 %collective-permute-start.23 = (bf16[1,128,512]{2,1,0:T(8,128)(2,1)S(1)}, bf16[1,128,512]{2,1,0:T(8,128)(2,1)S(1)}, u32[]{:S(2)}, u32[]{:S(2)}) collective-permute-start(bf16[1,128,512]{2,1,0:T(8,128)(2,1)S(1)} %get-tuple-element.84), channel_id=1, source_target_pairs={{0,6},{1,7},{2,4},{3,5},{4,2},{5,3},{6,0},{7,1},{8,14},{9,15},{10,... | collective-permute-start | bytes 393224 | tf_op jit(solution)/shard_map/ppermute | solution.py:246
  123.7 14.9 %collective-permute-start.24 = (bf16[1,128,512]{2,1,0:T(8,128)(2,1)S(1)}, bf16[1,128,512]{2,1,0:T(8,128)(2,1)S(1)}, u32[]{:S(2)}, u32[]{:S(2)}) collective-permute-start(bf16[1,128,512]{2,1,0:T(8,128)(2,1)S(1)} %get-tuple-element.85), channel_id=1, source_target_pairs={{0,7},{1,6},{2,5},{3,4},{4,3},{5,2},{6,1},{7,0},{8,15},{9,14},{10,... | collective-permute-start | bytes 393224 | tf_op jit(solution)/shard_map/ppermute | solution.py:246
  130.6 22.8 %collective-permute-start.27 = (bf16[2,128,512]{2,1,0:T(8,128)(2,1)S(1)}, bf16[2,128,512]{2,1,0:T(8,128)(2,1)S(1)}, u32[]{:S(2)}, u32[]{:S(2)}) collective-permute-start(bf16[2,128,512]{2,1,0:T(8,128)(2,1)S(1)} %get-tuple-element.88), channel_id=1, source_target_pairs={{0,3},{1,2},{2,1},{3,0},{4,7},{5,6},{6,5},{7,4},{8,11},{9,10},{10,... | collective-permute-start | bytes 786440 | tf_op jit(solution)/shard_map/ppermute | solution.py:246
  134.6 22.8 %collective-permute-start.28 = (bf16[2,128,512]{2,1,0:T(8,128)(2,1)S(1)}, bf16[2,128,512]{2,1,0:T(8,128)(2,1)S(1)}, u32[]{:S(2)}, u32[]{:S(2)}) collective-permute-start(bf16[2,128,512]{2,1,0:T(8,128)(2,1)S(1)} %get-tuple-element.89), channel_id=1, source_target_pairs={{0,4},{1,5},{2,6},{3,7},{4,0},{5,1},{6,2},{7,3},{8,12},{9,13},{10,... | collective-permute-start | bytes 786440 | tf_op jit(solution)/shard_map/ppermute | solution.py:246
  138.6 32.8 %collective-permute-start.29 = (bf16[2,128,512]{2,1,0:T(8,128)(2,1)S(1)}, bf16[2,128,512]{2,1,0:T(8,128)(2,1)S(1)}, u32[]{:S(2)}, u32[]{:S(2)}) collective-permute-start(bf16[2,128,512]{2,1,0:T(8,128)(2,1)S(1)} %get-tuple-element.90), channel_id=1, source_target_pairs={{0,5},{1,4},{2,7},{3,6},{4,1},{5,0},{6,3},{7,2},{8,13},{9,12},{10,... | collective-permute-start | bytes 786440 | tf_op jit(solution)/shard_map/ppermute | solution.py:246
  138.6 39.8 %collective-permute-start.30 = (bf16[2,128,512]{2,1,0:T(8,128)(2,1)S(1)}, bf16[2,128,512]{2,1,0:T(8,128)(2,1)S(1)}, u32[]{:S(2)}, u32[]{:S(2)}) collective-permute-start(bf16[2,128,512]{2,1,0:T(8,128)(2,1)S(1)} %get-tuple-element.91), channel_id=1, source_target_pairs={{0,6},{1,7},{2,4},{3,5},{4,2},{5,3},{6,0},{7,1},{8,14},{9,15},{10,... | collective-permute-start | bytes 786440 | tf_op jit(solution)/shard_map/ppermute | solution.py:246
  139.8 44.7 %collective-permute-start.31 = (bf16[2,128,512]{2,1,0:T(8,128)(2,1)S(1)}, bf16[2,128,512]{2,1,0:T(8,128)(2,1)S(1)}, u32[]{:S(2)}, u32[]{:S(2)}) collective-permute-start(bf16[2,128,512]{2,1,0:T(8,128)(2,1)S(1)} %get-tuple-element.92), channel_id=1, source_target_pairs={{0,7},{1,6},{2,5},{3,4},{4,3},{5,2},{6,1},{7,0},{8,15},{9,14},{10,... | collective-permute-start | bytes 786440 | tf_op jit(solution)/shard_map/ppermute | solution.py:246
  153.4 60.4 %copy-start.2 = (f32[4,128,512]{2,1,0:T(8,128)S(1)}, f32[4,128,512]{2,1,0:T(8,128)}, u32[]{:S(2)}) copy-start(f32[4,128,512]{2,1,0:T(8,128)} %get-tuple-element.105.sine_ref) | copy-start | bytes 3145732
  153.4 60.3 %copy-start.3 = (f32[4,128,512]{2,1,0:T(8,128)S(1)}, f32[4,128,512]{2,1,0:T(8,128)}, u32[]{:S(2)}) copy-start(f32[4,128,512]{2,1,0:T(8,128)} %get-tuple-element.106.cosine_ref) | copy-start | bytes 3145732
  189.3 22.5 %collective-permute-start.32 = (bf16[2,4,128,512]{3,2,1,0:T(8,128)(2,1)}, bf16[2,4,128,512]{3,2,1,0:T(8,128)(2,1)}, u32[]{:S(2)}, u32[]{:S(2)}) collective-permute-start(bf16[2,4,128,512]{3,2,1,0:T(8,128)(2,1)} %get-tuple-element.93.refs_4_), channel_id=1, source_target_pairs={{0,8},{8,16},{16,24},{1,9},{9,17},{17,25},{2,10},{10,18},{18,26},{... | collective-permute-start | bytes 3145736 | tf_op jit(solution)/shard_map/ppermute | solution.py:253
  194.3 18.1 %collective-permute-start.33 = (bf16[2,4,128,512]{3,2,1,0:T(8,128)(2,1)}, bf16[2,4,128,512]{3,2,1,0:T(8,128)(2,1)}, u32[]{:S(2)}, u32[]{:S(2)}) collective-permute-start(bf16[2,4,128,512]{3,2,1,0:T(8,128)(2,1)} %get-tuple-element.94.refs_0_.refs_1_), channel_id=1, source_target_pairs={{8,0},{16,8},{24,16},{9,1},{17,9},{25,17},{10,2},{18,10},{26,18},{... | collective-permute-start | bytes 3145736 | tf_op jit(solution)/shard_map/ppermute | solution.py:253
  196.3 5.0 %collective-permute-start.34 = (bf16[1,128,512]{2,1,0:T(8,128)(2,1)}, bf16[1,128,512]{2,1,0:T(8,128)(2,1)}, u32[]{:S(2)}, u32[]{:S(2)}) collective-permute-start(bf16[1,128,512]{2,1,0:T(8,128)(2,1)} %get-tuple-element.95), channel_id=1, source_target_pairs={{0,1},{1,0},{2,3},{3,2},{4,5},{5,4},{6,7},{7,6},{8,9},{9,8},{10,11... | collective-permute-start | bytes 393224 | tf_op jit(solution)/shard_map/ppermute | solution.py:246
  197.7 5.8 %collective-permute-start.35 = (bf16[1,128,512]{2,1,0:T(8,128)(2,1)}, bf16[1,128,512]{2,1,0:T(8,128)(2,1)}, u32[]{:S(2)}, u32[]{:S(2)}) collective-permute-start(bf16[1,128,512]{2,1,0:T(8,128)(2,1)} %get-tuple-element.96), channel_id=1, source_target_pairs={{0,2},{1,3},{2,0},{3,1},{4,6},{5,7},{6,4},{7,5},{8,10},{9,11},{10,... | collective-permute-start | bytes 393224 | tf_op jit(solution)/shard_map/ppermute | solution.py:246
  197.7 7.6 %collective-permute-start.36 = (bf16[1,128,512]{2,1,0:T(8,128)(2,1)}, bf16[1,128,512]{2,1,0:T(8,128)(2,1)}, u32[]{:S(2)}, u32[]{:S(2)}) collective-permute-start(bf16[1,128,512]{2,1,0:T(8,128)(2,1)} %copy-done.13), channel_id=1, source_target_pairs={{0,3},{1,2},{2,1},{3,0},{4,7},{5,6},{6,5},{7,4},{8,11},{9,10},{10,... | collective-permute-start | bytes 393224 | tf_op jit(solution)/shard_map/ppermute | solution.py:246
  201.2 7.1 %collective-permute-start.37 = (bf16[1,128,512]{2,1,0:T(8,128)(2,1)}, bf16[1,128,512]{2,1,0:T(8,128)(2,1)}, u32[]{:S(2)}, u32[]{:S(2)}) collective-permute-start(bf16[1,128,512]{2,1,0:T(8,128)(2,1)} %copy-done.32), channel_id=1, source_target_pairs={{0,1},{1,0},{2,3},{3,2},{4,5},{5,4},{6,7},{7,6},{8,9},{9,8},{10,11... | collective-permute-start | bytes 393224 | tf_op jit(solution)/shard_map/ppermute | solution.py:246
  203.5 5.2 %collective-permute-start.38 = (bf16[1,128,512]{2,1,0:T(8,128)(2,1)}, bf16[1,128,512]{2,1,0:T(8,128)(2,1)}, u32[]{:S(2)}, u32[]{:S(2)}) collective-permute-start(bf16[1,128,512]{2,1,0:T(8,128)(2,1)} %copy-done.29), channel_id=1, source_target_pairs={{0,2},{1,3},{2,0},{3,1},{4,6},{5,7},{6,4},{7,5},{8,10},{9,11},{10,... | collective-permute-start | bytes 393224 | tf_op jit(solution)/shard_map/ppermute | solution.py:246
  205.3 13.8 %collective-permute-start.39 = (bf16[1,128,512]{2,1,0:T(8,128)(2,1)}, bf16[1,128,512]{2,1,0:T(8,128)(2,1)S(1)}, u32[]{:S(2)}, u32[]{:S(2)}) collective-permute-start(bf16[1,128,512]{2,1,0:T(8,128)(2,1)} %copy-done.18), channel_id=1, source_target_pairs={{0,3},{1,2},{2,1},{3,0},{4,7},{5,6},{6,5},{7,4},{8,11},{9,10},{10,... | collective-permute-start | bytes 393224 | tf_op jit(solution)/shard_map/ppermute | solution.py:246
  208.3 10.8 %collective-permute-start.40 = (bf16[1,128,512]{2,1,0:T(8,128)(2,1)}, bf16[1,128,512]{2,1,0:T(8,128)(2,1)S(1)}, u32[]{:S(2)}, u32[]{:S(2)}) collective-permute-start(bf16[1,128,512]{2,1,0:T(8,128)(2,1)} %copy-done.17), channel_id=1, source_target_pairs={{0,4},{1,5},{2,6},{3,7},{4,0},{5,1},{6,2},{7,3},{8,12},{9,13},{10,... | collective-permute-start | bytes 393224 | tf_op jit(solution)/shard_map/ppermute | solution.py:246
  208.7 16.7 %collective-permute-start.41 = (bf16[1,128,512]{2,1,0:T(8,128)(2,1)}, bf16[1,128,512]{2,1,0:T(8,128)(2,1)S(1)}, u32[]{:S(2)}, u32[]{:S(2)}) collective-permute-start(bf16[1,128,512]{2,1,0:T(8,128)(2,1)} %copy-done.16), channel_id=1, source_target_pairs={{0,5},{1,4},{2,7},{3,6},{4,1},{5,0},{6,3},{7,2},{8,13},{9,12},{10,... | collective-permute-start | bytes 393224 | tf_op jit(solution)/shard_map/ppermute | solution.py:246
  211.7 18.0 %collective-permute-start.42 = (bf16[1,128,512]{2,1,0:T(8,128)(2,1)}, bf16[1,128,512]{2,1,0:T(8,128)(2,1)S(1)}, u32[]{:S(2)}, u32[]{:S(2)}) collective-permute-start(bf16[1,128,512]{2,1,0:T(8,128)(2,1)} %copy-done.15), channel_id=1, source_target_pairs={{0,6},{1,7},{2,4},{3,5},{4,2},{5,3},{6,0},{7,1},{8,14},{9,15},{10,... | collective-permute-start | bytes 393224 | tf_op jit(solution)/shard_map/ppermute | solution.py:246
  212.4 21.0 %collective-permute-start.43 = (bf16[1,128,512]{2,1,0:T(8,128)(2,1)}, bf16[1,128,512]{2,1,0:T(8,128)(2,1)S(1)}, u32[]{:S(2)}, u32[]{:S(2)}) collective-permute-start(bf16[1,128,512]{2,1,0:T(8,128)(2,1)} %copy-done.14), channel_id=1, source_target_pairs={{0,7},{1,6},{2,5},{3,4},{4,3},{5,2},{6,1},{7,0},{8,15},{9,14},{10,... | collective-permute-start | bytes 393224 | tf_op jit(solution)/shard_map/ppermute | solution.py:246
  (33 other events, 639.7 us)

commit v3 on v2

--- a/solution.py
+++ b/solution.py
@@ -142,7 +142,7 @@
     states, rows, width = cosine_ref.shape
     piece = slabs.shape[2] // 2
     cuts = width // piece
-    for n, out in enumerate(outs):
+    for n in range(len(outs) // states):
         for s, part in enumerate(ins):
             slabs[me ^ s] = part[n]
         pairs = []
@@ -166,7 +166,11 @@
             )
         left = jnp.concatenate([p[0] for p in pairs] + [p[1] for p in pairs], 0)
         product = jnp.dot(left, second_ref[...], preferred_element_type=jnp.float32)
-        out[...] = product.astype(jnp.bfloat16).reshape(2, states, rows, width)
+        product = product.astype(jnp.bfloat16)
+        for c in range(2):
+            for j in range(states):
+                first = (c * states + j) * rows
+                outs[n * states + j][c] = product[first : first + rows]
 
 
 def phase_call(after, me, second, cosine, sine, slabs):
@@ -181,8 +185,8 @@
         in_specs=[SMEM, pl.BlockSpec(second.shape, lambda i: (0, 0)), table, table]
         + [AFTER] * len(after)
         + [pl.BlockSpec((kinds, block, wide), lambda i: (0, i, 0))] * ranks,
-        out_specs=[pl.BlockSpec((2, states, block, width), lambda i: (0, 0, i, 0))] * kinds,
-        out_shape=[jax.ShapeDtypeStruct((2, states, rows, width), jnp.bfloat16)] * kinds,
+        out_specs=[pl.BlockSpec((2, block, width), lambda i: (0, i, 0))] * (kinds * states),
+        out_shape=[jax.ShapeDtypeStruct((2, rows, width), jnp.bfloat16)] * (kinds * states),
         scratch_shapes=[pltpu.VMEM((ranks, block, wide), jnp.bfloat16)],
         compiler_params=params(),
         cost_estimate=cost(
@@ -194,21 +198,22 @@
 
 def mix_kernel(up_ref, down_ref, weight_ref, *refs):
     kinetic, out, wide = refs[:-2], refs[-2], refs[-1]
-    _, states, rows, width = kinetic[0].shape
+    _, rows, width = kinetic[0].shape
+    blocks, states = up_ref.shape
     tiles = width // LANES
     group = tiles * states
     weight = weight_ref[...]
-    for k in range(len(kinetic) - 2):
-        below, here, above = kinetic[k : k + 3]
+    for k in range(blocks):
         for j in range(states):
+            below, here, above = (kinetic[(k + n) * states + j] for n in range(3))
             up, down = up_ref[k, j], down_ref[k, j]
             mixed = [
-                up * above[c, j].astype(jnp.float32) + down * below[c, j].astype(jnp.float32)
+                up * above[c].astype(jnp.float32) + down * below[c].astype(jnp.float32)
                 for c in range(2)
             ]
             parts = (
-                here[0, j].astype(jnp.float32) + weight * mixed[1],
-                here[1, j].astype(jnp.float32) - weight * mixed[0],
+                here[0].astype(jnp.float32) + weight * mixed[1],
+                here[1].astype(jnp.float32) - weight * mixed[0],
             )
             for c in range(2):
                 for t in range(tiles):
@@ -219,15 +224,15 @@
 
 
 def mix_call(up, down, weight, kinetic):
-    _, states, rows, width = kinetic[0].shape
-    blocks = len(kinetic) - 2
+    _, rows, width = kinetic[0].shape
+    blocks, states = up.shape
     group = width // LANES * states
     block = rows // 4
     return pl.pallas_call(
         mix_kernel,
         grid=(rows // block,),
         in_specs=[SMEM, SMEM, pl.BlockSpec((block, width), lambda i: (i, 0))]
-        + [pl.BlockSpec((2, states, block, width), lambda i: (0, 0, i, 0))] * len(kinetic),
+        + [pl.BlockSpec((2, block, width), lambda i: (0, i, 0))] * len(kinetic),
         out_specs=pl.BlockSpec((block, 2, blocks, group, LANES), lambda i: (i, 0, 0, 0, 0)),
         out_shape=jax.ShapeDtypeStruct((rows, 2, blocks, group, LANES), jnp.bfloat16),
         scratch_shapes=[pltpu.VMEM((block * 2 * group, LANES), jnp.float32)],
@@ -265,7 +270,7 @@
     view = packet.reshape(rows, 2, blocks, states, tiles, LANES).transpose(0, 1, 2, 4, 3, 5)
     view = view.reshape(rows, 2, blocks, tiles * states, LANES)
     edges = sorted({0, blocks - 1})
-    chunks = [edges] + [[k] for k in range(blocks) if k not in edges]
+    chunks = [edges, [k for k in range(blocks) if k not in edges]]
 
     last = me
     lines = []
@@ -283,16 +288,14 @@
     cosine, sine = jnp.cos(angles), jnp.sin(angles)
     kinetic = [None] * blocks
     for n, (chosen, back) in enumerate(zip(chunks, backs)):
-        after = [last, below, above] if n == 1 else [last]
-        if n == 0:
-            after += backs[1][4:]
+        after = [last]
         values = phase_call(after, me, second, cosine, sine, back)
         last = values[0]
-        for k, value in zip(chosen, values):
-            kinetic[k] = value
+        for i, k in enumerate(chosen):
+            kinetic[k] = values[i * states : (i + 1) * states]
         if n == 0:
-            below = neighbour(kinetic[-1], "hel", 1)
-            above = neighbour(kinetic[0], "hel", -1)
+            below = [neighbour(edge, "hel", 1) for edge in kinetic[-1]]
+            above = [neighbour(edge, "hel", -1) for edge in kinetic[0]]
 
     count = coupling.shape[0]
     helicities = jnp.arange(count, dtype=jnp.int32)
@@ -303,7 +306,7 @@
     start = lax.axis_index("hel") * blocks
     up = lax.dynamic_slice_in_dim(couple_up, start, blocks, 0)
     down = lax.dynamic_slice_in_dim(couple_down, start, blocks, 0)
-    out = mix_call(up, down, radial_weight, [below] + kinetic + [above])
+    out = mix_call(up, down, radial_weight, sum([list(x) for x in (below, *kinetic, above)], []))
     out = out.reshape(rows, 2, blocks, tiles, states, LANES).transpose(0, 1, 2, 4, 3, 5)
     return out.reshape(rows, 2, blocks, states, width)
 

time: 246 us -> 230 us (0.935)
  waiting for transfers between devices: 120 us -> 77 us
  starting transfers between devices: 52.8 us -> 82.7 us
  Pallas kernels: 50.6 us -> 45.4 us
    ppermute x42 -> x28, waiting for transfers between devices: 120 us -> 77 us  [exchanged(): result[s] = lax.ppermute(slabs[s], axis, [(i, i ^ s) for i in range(count)])]
    ppermute x2 -> x8, starting transfers between devices: 6.97 us -> 40.4 us  [neighbour(): return lax.ppermute(edge, axis, pairs)]
    ppermute x42 -> x28, starting transfers between devices: 45.9 us -> 42.3 us  [exchanged(): result[s] = lax.ppermute(slabs[s], axis, [(i, i ^ s) for i in range(count)])]
    pallas_call x3 -> x2, Pallas kernels: 17.9 us -> 15.5 us  [left_call(): pl.pallas_call(functools.partial(left_kernel, len(after), ranks), grid=(k...]
    unnamed x76 -> x40, local copies, waits for them, and re-layouts: 9.48 us -> 11.4 us
    pallas_call x3 -> x2, Pallas kernels: 9.88 us -> 8.09 us  [phase_call(): pl.pallas_call(functools.partial(phase_kernel, len(after), ranks), grid=(...]
    pallas_call x3 -> x2, Pallas kernels: 13.3 us -> 12.3 us  [right_call(): pl.pallas_call(functools.partial(right_kernel, len(after), ranks, states)...]
  transfers between devices with their start and end apart: 44 -> 36, of which waited for: 24 -> 11; matrix products, arithmetic and copies ran while one was open for 5% -> 5% of each run, Pallas kernels for 11% -> 13%
where the time goes in v3:
time: 230 us; the launch traced here: 228 us
  starting transfers between devices  82.7 us (36%)
  waiting for transfers between devices  77 us (33%)
  Pallas kernels  45.4 us (20%)
  local copies, waits for them, and re-layouts  22.7 us (10%)
    ppermute x28, waiting for transfers between devices, exchanged(): result[s] = lax.ppermute(slabs[s], axis, [(i, i ^ s) for i in range(count)])  77 us
    ppermute x28, starting transfers between devices, exchanged(): result[s] = lax.ppermute(slabs[s], axis, [(i, i ^ s) for i in range(count)])  42.3 us
    ppermute x8, starting transfers between devices, neighbour(): return lax.ppermute(edge, axis, pairs)  40.4 us
    pallas_call x2, Pallas kernels, left_call(): pl.pallas_call(functools.partial(left_kernel, len(after), ranks), grid=(k...  15.5 us
    pallas_call x2, Pallas kernels, right_call(): pl.pallas_call(functools.partial(right_kernel, len(after), ranks, states)...  12.3 us
    unnamed x40, local copies, waits for them, and re-layouts  11.4 us
    pallas_call x1, Pallas kernels, mix_call(): pl.pallas_call(mix_kernel, grid=(rows // block,), in_specs=[SMEM, SMEM, p...  9.64 us
    pallas_call x2, Pallas kernels, phase_call(): pl.pallas_call(functools.partial(phase_kernel, len(after), ranks), grid=(...  8.09 us
  transfers between devices with their start and end apart: 36, of which 11 were waited for; matrix products, arithmetic and copies ran while one was open for 5% of the time, Pallas kernels for 13%

profile of v3, /device:TPU:9, one launch (start us, length us, event | category | flops | bytes accessed | tf_op | source)
XLA Modules:
  0.0 228.3 jit_solution(10069940058996924556)
XLA Ops:
  0.0 1.2 copy-done
  1.2 6.5 %right.2 = (bf16[2,128,512]{2,1,0:T(8,128)(2,1)S(1)}, bf16[2,128,512]{2,1,0:T(8,128)(2,1)S(1)}, bf16[2,128,512]{2,1,0:T(8,128)(2,1)S(1)}, bf16[2,128,512]{2,1,0:...) custom-call(s32[1]{0:T(128)} %bitcast.me_ref.refs_0_, ...), custom_call_target="tpu_custom_call" | custom-call | flops 2147483648 | bytes 4194304 | tf_op jit(solution)/shard_map/right/pallas_call | solution.py:70
  7.7 1.2 collective-permute-start
  9.1 1.2 collective-permute-start.2
  10.4 2.3 %collective-permute-start.3 = (bf16[2,128,512]{2,1,0:T(8,128)(2,1)}, bf16[2,128,512]{2,1,0:T(8,128)(2,1)S(1)}, u32[]{:S(2)}, u32[]{:S(2)}) collective-permute-start(bf16[2,128,512]{2,1,0:T(8,128)(2,1)} %get-tuple-element.58), channel_id=1, source_target_pairs={{0,4},{1,5},{2,6},{3,7},{4,0},{5,1},{6,2},{7,3},{8,12},{9,13},{10,... | collective-permute-start | bytes 786440 | tf_op jit(solution)/shard_map/ppermute | solution.py:251
  12.7 1.0 collective-permute-start.4
  13.7 1.2 collective-permute-done.refs_2_
  14.9 1.3 collective-permute-start.5
  16.2 7.3 %collective-permute-done.1.refs_3_ = bf16[2,128,512]{2,1,0:T(8,128)(2,1)S(1)} collective-permute-done((bf16[2,128,512]{2,1,0:T(8,128)(2,1)S(1)}, bf16[2,128,512]{2,1,0:T(8,128)(2,1)S(1)}, u32[]{:S(2)}, u32[]{:S(2)}) %collective-permute-start.1) | collective-permute-done | bytes 262176 | tf_op jit(solution)/shard_map/ppermute | solution.py:251
  23.5 6.5 %copy.14 = bf16[2048,1024]{0,1:T(8,128)(2,1)} copy(bf16[2048,1024]{1,0:T(8,128)(2,1)} %bitcast.27) | data formatting | bytes 8388608 | tf_op jit(solution)/shard_map/reshape | solution.py:269
  30.0 5.8 %right.3 = (bf16[2,128,512]{2,1,0:T(8,128)(2,1)S(1)}, bf16[2,128,512]{2,1,0:T(8,128)(2,1)S(1)}, bf16[2,128,512]{2,1,0:T(8,128)(2,1)S(1)}, bf16[2,128,512]{2,1,0:...) custom-call(s32[1]{0:T(128)} %bitcast.me_ref.refs_0_, ...), custom_call_target="tpu_custom_call" | custom-call | flops 2147483648 | bytes 4194304 | tf_op jit(solution)/shard_map/right/pallas_call | solution.py:70
  35.8 3.6 %collective-permute-start.10 = (bf16[2,128,512]{2,1,0:T(8,128)(2,1)S(1)}, bf16[2,128,512]{2,1,0:T(8,128)(2,1)S(1)}, u32[]{:S(2)}, u32[]{:S(2)}) collective-permute-start(bf16[2,128,512]{2,1,0:T(8,128)(2,1)S(1)} %get-tuple-element.66), channel_id=1, source_target_pairs={{0,4},{1,5},{2,6},{3,7},{4,0},{5,1},{6,2},{7,3},{8,12},{9,13},{10,... | collective-permute-start | bytes 786440 | tf_op jit(solution)/shard_map/ppermute | solution.py:251
  39.4 2.0 collective-permute-start.11
  41.4 14.9 %collective-permute-done.4.refs_6_ = bf16[2,128,512]{2,1,0:T(8,128)(2,1)S(1)} collective-permute-done((bf16[2,128,512]{2,1,0:T(8,128)(2,1)}, bf16[2,128,512]{2,1,0:T(8,128)(2,1)S(1)}, u32[]{:S(2)}, u32[]{:S(2)}) %collective-permute-start.4) | collective-permute-done | bytes 262176 | tf_op jit(solution)/shard_map/ppermute | solution.py:251
  56.3 8.5 %collective-permute-done.5.refs_7_ = bf16[2,128,512]{2,1,0:T(8,128)(2,1)S(1)} collective-permute-done((bf16[2,128,512]{2,1,0:T(8,128)(2,1)S(1)}, bf16[2,128,512]{2,1,0:T(8,128)(2,1)S(1)}, u32[]{:S(2)}, u32[]{:S(2)}) %collective-permute-start.5) | collective-permute-done | bytes 262176 | tf_op jit(solution)/shard_map/ppermute | solution.py:251
  64.8 11.6 %collective-permute-start.13 = (bf16[2,128,512]{2,1,0:T(8,128)(2,1)S(1)}, bf16[2,128,512]{2,1,0:T(8,128)(2,1)S(1)}, u32[]{:S(2)}, u32[]{:S(2)}) collective-permute-start(bf16[2,128,512]{2,1,0:T(8,128)(2,1)S(1)} %get-tuple-element.69), channel_id=1, source_target_pairs={{0,7},{1,6},{2,5},{3,4},{4,3},{5,2},{6,1},{7,0},{8,15},{9,14},{10,... | collective-permute-start | bytes 786440 | tf_op jit(solution)/shard_map/ppermute | solution.py:251
  76.4 3.3 %collective-permute-done.6.refs_8_ = bf16[2,128,512]{2,1,0:T(8,128)(2,1)} collective-permute-done((bf16[2,128,512]{2,1,0:T(8,128)(2,1)S(1)}, bf16[2,128,512]{2,1,0:T(8,128)(2,1)}, u32[]{:S(2)}, u32[]{:S(2)}) %collective-permute-start.6) | collective-permute-done | bytes 262176 | tf_op jit(solution)/shard_map/ppermute | solution.py:251
  80.1 7.4 %left.2 = (bf16[2,128,512]{2,1,0:T(8,128)(2,1)S(1)}, bf16[2,128,512]{2,1,0:T(8,128)(2,1)S(1)}, bf16[2,128,512]{2,1,0:T(8,128)(2,1)S(1)}, bf16[2,128,512]{2,1,0:T...) custom-call(s32[1]{0:T(128)} %bitcast.me_ref.refs_0_, ...), custom_call_target="tpu_custom_call" | custom-call | flops 4294967296 | bytes 8388608 | tf_op jit(solution)/shard_map/left/pallas_call | solution.py:118
  87.6 2.5 %collective-permute-done.11.refs_6_ = bf16[2,128,512]{2,1,0:T(8,128)(2,1)S(1)} collective-permute-done((bf16[2,128,512]{2,1,0:T(8,128)(2,1)S(1)}, bf16[2,128,512]{2,1,0:T(8,128)(2,1)S(1)}, u32[]{:S(2)}, u32[]{:S(2)}) %collective-permute-start.11) | collective-permute-done | bytes 262176 | tf_op jit(solution)/shard_map/ppermute | solution.py:251
  90.1 2.1 collective-permute-start.9
  92.2 3.5 %collective-permute-done.12.refs_7_ = bf16[2,128,512]{2,1,0:T(8,128)(2,1)S(1)} collective-permute-done((bf16[2,128,512]{2,1,0:T(8,128)(2,1)S(1)}, bf16[2,128,512]{2,1,0:T(8,128)(2,1)S(1)}, u32[]{:S(2)}, u32[]{:S(2)}) %collective-permute-start.12) | collective-permute-done | bytes 262176 | tf_op jit(solution)/shard_map/ppermute | solution.py:251
  95.7 1.2 collective-permute-start.14
  96.9 6.8 %collective-permute-done.13.refs_8_ = bf16[2,128,512]{2,1,0:T(8,128)(2,1)S(1)} collective-permute-done((bf16[2,128,512]{2,1,0:T(8,128)(2,1)S(1)}, bf16[2,128,512]{2,1,0:T(8,128)(2,1)S(1)}, u32[]{:S(2)}, u32[]{:S(2)}) %collective-permute-start.13) | collective-permute-done | bytes 262176 | tf_op jit(solution)/shard_map/ppermute | solution.py:251
  103.7 1.7 collective-permute-start.16
  105.4 1.9 collective-permute-start.17
  107.4 1.1 collective-permute-start.18
  108.4 4.5 %collective-permute-done.14.refs_2_ = bf16[2,128,512]{2,1,0:T(8,128)(2,1)S(1)} collective-permute-done((bf16[2,128,512]{2,1,0:T(8,128)(2,1)S(1)}, bf16[2,128,512]{2,1,0:T(8,128)(2,1)S(1)}, u32[]{:S(2)}, u32[]{:S(2)}) %collective-permute-start.14) | collective-permute-done | bytes 262176 | tf_op jit(solution)/shard_map/ppermute | solution.py:251
  113.0 2.5 %collective-permute-start.19 = (bf16[2,128,512]{2,1,0:T(8,128)(2,1)S(1)}, bf16[2,128,512]{2,1,0:T(8,128)(2,1)S(1)}, u32[]{:S(2)}, u32[]{:S(2)}) collective-permute-start(bf16[2,128,512]{2,1,0:T(8,128)(2,1)S(1)} %get-tuple-element.76), channel_id=1, source_target_pairs={{0,6},{1,7},{2,4},{3,5},{4,2},{5,3},{6,0},{7,1},{8,14},{9,15},{10,... | collective-permute-start | bytes 786440 | tf_op jit(solution)/shard_map/ppermute | solution.py:251
  115.8 8.1 %left.3 = (bf16[2,128,512]{2,1,0:T(8,128)(2,1)S(1)}, bf16[2,128,512]{2,1,0:T(8,128)(2,1)S(1)}, bf16[2,128,512]{2,1,0:T(8,128)(2,1)S(1)}, bf16[2,128,512]{2,1,0:T...) custom-call(s32[1]{0:T(128)} %bitcast.me_ref.refs_0_, ...), custom_call_target="tpu_custom_call" | custom-call | flops 4294967296 | bytes 8388608 | tf_op jit(solution)/shard_map/left/pallas_call | solution.py:118
  124.8 2.8 %collective-permute-start.26 = (bf16[2,128,512]{2,1,0:T(8,128)(2,1)S(1)}, bf16[2,128,512]{2,1,0:T(8,128)(2,1)S(1)}, u32[]{:S(2)}, u32[]{:S(2)}) collective-permute-start(bf16[2,128,512]{2,1,0:T(8,128)(2,1)S(1)} %get-tuple-element.87), channel_id=1, source_target_pairs={{0,2},{1,3},{2,0},{3,1},{4,6},{5,7},{6,4},{7,5},{8,10},{9,11},{10,... | collective-permute-start | bytes 786440 | tf_op jit(solution)/shard_map/ppermute | solution.py:251
  127.6 16.7 %collective-permute-done.19.refs_7_ = bf16[2,128,512]{2,1,0:T(8,128)(2,1)S(1)} collective-permute-done((bf16[2,128,512]{2,1,0:T(8,128)(2,1)S(1)}, bf16[2,128,512]{2,1,0:T(8,128)(2,1)S(1)}, u32[]{:S(2)}, u32[]{:S(2)}) %collective-permute-start.19) | collective-permute-done | bytes 262176 | tf_op jit(solution)/shard_map/ppermute | solution.py:251
  144.3 7.8 %collective-permute-done.20.refs_8_ = bf16[2,128,512]{2,1,0:T(8,128)(2,1)S(1)} collective-permute-done((bf16[2,128,512]{2,1,0:T(8,128)(2,1)S(1)}, bf16[2,128,512]{2,1,0:T(8,128)(2,1)S(1)}, u32[]{:S(2)}, u32[]{:S(2)}) %collective-permute-start.20) | collective-permute-done | bytes 262176 | tf_op jit(solution)/shard_map/ppermute | solution.py:251
  152.0 4.6 %sine_bitcast_fusion = (f32[4,128,512]{2,1,0:T(8,128)}, f32[4,128,512]{2,1,0:T(8,128)}) fusion(f32[128,4,512]{2,1,0:T(4,128)S(1)} %copy-done.15), kind=kLoop, calls=%fused_computation | loop fusion | bytes 3145728 | tf_op jit(solution)/shard_map/sin | solution.py:288
  156.7 4.0 %phase.2 = (bf16[2,128,512]{2,1,0:T(8,128)(2,1)S(1)}, bf16[2,128,512]{2,1,0:T(8,128)(2,1)S(1)}, bf16[2,128,512]{2,1,0:T(8,128)(2,1)S(1)}, bf16[2,128,512]{2,1,0:...) custom-call(s32[1]{0:T(128)} %bitcast.me_ref.refs_0_, ...), custom_call_target="tpu_custom_call" | custom-call | flops 2147483648 | bytes 4194304 | tf_op jit(solution)/shard_map/phase/pallas_call | solution.py:182
  161.4 2.8 %collective-permute-start.30 = (bf16[2,128,512]{2,1,0:T(8,128)(2,1)}, bf16[2,128,512]{2,1,0:T(8,128)(2,1)}, u32[]{:S(2)}, u32[]{:S(2)}) collective-permute-start(bf16[2,128,512]{2,1,0:T(8,128)(2,1)} %get-tuple-element.91), channel_id=1, source_target_pairs={{0,6},{1,7},{2,4},{3,5},{4,2},{5,3},{6,0},{7,1},{8,14},{9,15},{10,... | collective-permute-start | bytes 786440 | tf_op jit(solution)/shard_map/ppermute | solution.py:251
  165.7 17.8 %collective-permute-start.21 = (bf16[2,128,512]{2,1,0:T(8,128)(2,1)S(1)}, bf16[2,128,512]{2,1,0:T(8,128)(2,1)}, u32[]{:S(2)}, u32[]{:S(2)}) collective-permute-start(bf16[2,128,512]{2,1,0:T(8,128)(2,1)S(1)} %get-tuple-element.78.refs_16_), channel_id=1, source_target_pairs={{0,8},{8,16},{16,24},{1,9},{9,17},{17,25},{2,10},{10,18},{18,26},{... | collective-permute-start | bytes 786440 | tf_op jit(solution)/shard_map/ppermute | solution.py:258
  184.2 1.9 collective-permute-start.22
  186.8 7.9 %collective-permute-start.23 = (bf16[2,128,512]{2,1,0:T(8,128)(2,1)S(1)}, bf16[2,128,512]{2,1,0:T(8,128)(2,1)}, u32[]{:S(2)}, u32[]{:S(2)}) collective-permute-start(bf16[2,128,512]{2,1,0:T(8,128)(2,1)S(1)} %get-tuple-element.80.refs_18_), channel_id=1, source_target_pairs={{0,8},{8,16},{16,24},{1,9},{9,17},{17,25},{2,10},{10,18},{18,26},{... | collective-permute-start | bytes 786440 | tf_op jit(solution)/shard_map/ppermute | solution.py:258
  195.1 5.1 %collective-permute-start.24 = (bf16[2,128,512]{2,1,0:T(8,128)(2,1)S(1)}, bf16[2,128,512]{2,1,0:T(8,128)(2,1)S(1)}, u32[]{:S(2)}, u32[]{:S(2)}) collective-permute-start(bf16[2,128,512]{2,1,0:T(8,128)(2,1)S(1)} %get-tuple-element.81.refs_19_), channel_id=1, source_target_pairs={{0,8},{8,16},{16,24},{1,9},{9,17},{17,25},{2,10},{10,18},{18,26},{... | collective-permute-start | bytes 786440 | tf_op jit(solution)/shard_map/ppermute | solution.py:258
  200.2 1.9 collective-permute-start.32
  202.1 1.9 collective-permute-start.33
  204.1 1.9 collective-permute-start.34
  206.0 1.9 collective-permute-start.35
  208.0 0.9 copy-done.4
  209.0 0.9 copy-done.6
  209.9 0.9 copy-done.8
  213.7 4.1 %phase.3 = (bf16[2,128,512]{2,1,0:T(8,128)(2,1)S(1)}, bf16[2,128,512]{2,1,0:T(8,128)(2,1)S(1)}, bf16[2,128,512]{2,1,0:T(8,128)(2,1)S(1)}, bf16[2,128,512]{2,1,0:...) custom-call(s32[1]{0:T(128)} %bitcast.me_ref.refs_0_, ...), custom_call_target="tpu_custom_call" | custom-call | flops 2147483648 | bytes 4194304 | tf_op jit(solution)/shard_map/phase/pallas_call | solution.py:182
  218.7 9.6 %mix.1 = bf16[128,2,4,16,128]{4,3,2,1,0:T(8,128)(2,1)} custom-call(f32[4,4]{1,0:T(4,128)S(1)} %get-tuple-element.104.up_ref, f32[4,4]{1,0:T(4,128)S(1)} %get-tuple-element.103.down_ref, f32[128,512]{1,0:T(8,128)S(1)} %copy-done.2, bf16[2,128,512]{2,1,0:T(8,128)(2,1)} %collective-permute-done.21.refs_0_, ...), custom_call_target="tpu_custom_call" | custom-call | flops 20971520 | bytes 10485760 | tf_op jit(solution)/shard_map/mix/pallas_call | solution.py:231
  (77 shorter events, 9.6 us)
Async XLA Ops:
  0.0 1.2 copy-start
  7.7 7.2 %collective-permute-start = (bf16[2,128,512]{2,1,0:T(8,128)(2,1)S(1)}, bf16[2,128,512]{2,1,0:T(8,128)(2,1)S(1)}, u32[]{:S(2)}, u32[]{:S(2)}) collective-permute-start(bf16[2,128,512]{2,1,0:T(8,128)(2,1)S(1)} %get-tuple-element.55), channel_id=1, source_target_pairs={{0,1},{1,0},{2,3},{3,2},{4,5},{5,4},{6,7},{7,6},{8,9},{9,8},{10,11... | collective-permute-start | bytes 786440 | tf_op jit(solution)/shard_map/ppermute | solution.py:251
  8.9 14.5 %collective-permute-start.1 = (bf16[2,128,512]{2,1,0:T(8,128)(2,1)S(1)}, bf16[2,128,512]{2,1,0:T(8,128)(2,1)S(1)}, u32[]{:S(2)}, u32[]{:S(2)}) collective-permute-start(bf16[2,128,512]{2,1,0:T(8,128)(2,1)S(1)} %get-tuple-element.56), channel_id=1, source_target_pairs={{0,2},{1,3},{2,0},{3,1},{4,6},{5,7},{6,4},{7,5},{8,10},{9,11},{10,... | collective-permute-start | bytes 786440 | tf_op jit(solution)/shard_map/ppermute | solution.py:251
  9.1 26.7 %collective-permute-start.2 = (bf16[2,128,512]{2,1,0:T(8,128)(2,1)}, bf16[2,128,512]{2,1,0:T(8,128)(2,1)S(1)}, u32[]{:S(2)}, u32[]{:S(2)}) collective-permute-start(bf16[2,128,512]{2,1,0:T(8,128)(2,1)} %get-tuple-element.57), channel_id=1, source_target_pairs={{0,3},{1,2},{2,1},{3,0},{4,7},{5,6},{6,5},{7,4},{8,11},{9,10},{10,... | collective-permute-start | bytes 786440 | tf_op jit(solution)/shard_map/ppermute | solution.py:251
  10.4 29.1 %collective-permute-start.3 = (bf16[2,128,512]{2,1,0:T(8,128)(2,1)}, bf16[2,128,512]{2,1,0:T(8,128)(2,1)S(1)}, u32[]{:S(2)}, u32[]{:S(2)}) collective-permute-start(bf16[2,128,512]{2,1,0:T(8,128)(2,1)} %get-tuple-element.58), channel_id=1, source_target_pairs={{0,4},{1,5},{2,6},{3,7},{4,0},{5,1},{6,2},{7,3},{8,12},{9,13},{10,... | collective-permute-start | bytes 786440 | tf_op jit(solution)/shard_map/ppermute | solution.py:251
  12.7 43.7 %collective-permute-start.4 = (bf16[2,128,512]{2,1,0:T(8,128)(2,1)}, bf16[2,128,512]{2,1,0:T(8,128)(2,1)S(1)}, u32[]{:S(2)}, u32[]{:S(2)}) collective-permute-start(bf16[2,128,512]{2,1,0:T(8,128)(2,1)} %get-tuple-element.59), channel_id=1, source_target_pairs={{0,5},{1,4},{2,7},{3,6},{4,1},{5,0},{6,3},{7,2},{8,13},{9,12},{10,... | collective-permute-start | bytes 786440 | tf_op jit(solution)/shard_map/ppermute | solution.py:251
  14.9 49.9 %collective-permute-start.5 = (bf16[2,128,512]{2,1,0:T(8,128)(2,1)S(1)}, bf16[2,128,512]{2,1,0:T(8,128)(2,1)S(1)}, u32[]{:S(2)}, u32[]{:S(2)}) collective-permute-start(bf16[2,128,512]{2,1,0:T(8,128)(2,1)S(1)} %get-tuple-element.60), channel_id=1, source_target_pairs={{0,6},{1,7},{2,4},{3,5},{4,2},{5,3},{6,0},{7,1},{8,14},{9,15},{10,... | collective-permute-start | bytes 786440 | tf_op jit(solution)/shard_map/ppermute | solution.py:251
  23.5 56.2 %collective-permute-start.6 = (bf16[2,128,512]{2,1,0:T(8,128)(2,1)S(1)}, bf16[2,128,512]{2,1,0:T(8,128)(2,1)}, u32[]{:S(2)}, u32[]{:S(2)}) collective-permute-start(bf16[2,128,512]{2,1,0:T(8,128)(2,1)S(1)} %get-tuple-element.61), channel_id=1, source_target_pairs={{0,7},{1,6},{2,5},{3,4},{4,3},{5,2},{6,1},{7,0},{8,15},{9,14},{10,... | collective-permute-start | bytes 786440 | tf_op jit(solution)/shard_map/ppermute | solution.py:251
  23.5 6.5 %copy-start.1 = (bf16[2,512,512]{2,1,0:T(8,128)(2,1)S(1)}, bf16[2,512,512]{2,1,0:T(8,128)(2,1)}, u32[]{:S(2)}) copy-start(bf16[2,512,512]{2,1,0:T(8,128)(2,1)} %param.8) | copy-start | bytes 3145732
  35.8 51.7 %collective-permute-start.10 = (bf16[2,128,512]{2,1,0:T(8,128)(2,1)S(1)}, bf16[2,128,512]{2,1,0:T(8,128)(2,1)S(1)}, u32[]{:S(2)}, u32[]{:S(2)}) collective-permute-start(bf16[2,128,512]{2,1,0:T(8,128)(2,1)S(1)} %get-tuple-element.66), channel_id=1, source_target_pairs={{0,4},{1,5},{2,6},{3,7},{4,0},{5,1},{6,2},{7,3},{8,12},{9,13},{10,... | collective-permute-start | bytes 786440 | tf_op jit(solution)/shard_map/ppermute | solution.py:251
  39.4 50.7 %collective-permute-start.11 = (bf16[2,128,512]{2,1,0:T(8,128)(2,1)S(1)}, bf16[2,128,512]{2,1,0:T(8,128)(2,1)S(1)}, u32[]{:S(2)}, u32[]{:S(2)}) collective-permute-start(bf16[2,128,512]{2,1,0:T(8,128)(2,1)S(1)} %get-tuple-element.67), channel_id=1, source_target_pairs={{0,5},{1,4},{2,7},{3,6},{4,1},{5,0},{6,3},{7,2},{8,13},{9,12},{10,... | collective-permute-start | bytes 786440 | tf_op jit(solution)/shard_map/ppermute | solution.py:251
  56.3 39.4 %collective-permute-start.12 = (bf16[2,128,512]{2,1,0:T(8,128)(2,1)S(1)}, bf16[2,128,512]{2,1,0:T(8,128)(2,1)S(1)}, u32[]{:S(2)}, u32[]{:S(2)}) collective-permute-start(bf16[2,128,512]{2,1,0:T(8,128)(2,1)S(1)} %get-tuple-element.68), channel_id=1, source_target_pairs={{0,6},{1,7},{2,4},{3,5},{4,2},{5,3},{6,0},{7,1},{8,14},{9,15},{10,... | collective-permute-start | bytes 786440 | tf_op jit(solution)/shard_map/ppermute | solution.py:251
  64.8 38.9 %collective-permute-start.13 = (bf16[2,128,512]{2,1,0:T(8,128)(2,1)S(1)}, bf16[2,128,512]{2,1,0:T(8,128)(2,1)S(1)}, u32[]{:S(2)}, u32[]{:S(2)}) collective-permute-start(bf16[2,128,512]{2,1,0:T(8,128)(2,1)S(1)} %get-tuple-element.69), channel_id=1, source_target_pairs={{0,7},{1,6},{2,5},{3,4},{4,3},{5,2},{6,1},{7,0},{8,15},{9,14},{10,... | collective-permute-start | bytes 786440 | tf_op jit(solution)/shard_map/ppermute | solution.py:251
  79.7 24.0 %collective-permute-start.7 = (bf16[2,128,512]{2,1,0:T(8,128)(2,1)S(1)}, bf16[2,128,512]{2,1,0:T(8,128)(2,1)S(1)}, u32[]{:S(2)}, u32[]{:S(2)}) collective-permute-start(bf16[2,128,512]{2,1,0:T(8,128)(2,1)S(1)} %get-tuple-element.63), channel_id=1, source_target_pairs={{0,1},{1,0},{2,3},{3,2},{4,5},{5,4},{6,7},{7,6},{8,9},{9,8},{10,11... | collective-permute-start | bytes 786440 | tf_op jit(solution)/shard_map/ppermute | solution.py:251
  87.5 17.9 %collective-permute-start.8 = (bf16[2,128,512]{2,1,0:T(8,128)(2,1)S(1)}, bf16[2,128,512]{2,1,0:T(8,128)(2,1)S(1)}, u32[]{:S(2)}, u32[]{:S(2)}) collective-permute-start(bf16[2,128,512]{2,1,0:T(8,128)(2,1)S(1)} %get-tuple-element.64), channel_id=1, source_target_pairs={{0,2},{1,3},{2,0},{3,1},{4,6},{5,7},{6,4},{7,5},{8,10},{9,11},{10,... | collective-permute-start | bytes 786440 | tf_op jit(solution)/shard_map/ppermute | solution.py:251
  90.1 17.3 %collective-permute-start.9 = (bf16[2,128,512]{2,1,0:T(8,128)(2,1)S(1)}, bf16[2,128,512]{2,1,0:T(8,128)(2,1)S(1)}, u32[]{:S(2)}, u32[]{:S(2)}) collective-permute-start(bf16[2,128,512]{2,1,0:T(8,128)(2,1)S(1)} %get-tuple-element.65), channel_id=1, source_target_pairs={{0,3},{1,2},{2,1},{3,0},{4,7},{5,6},{6,5},{7,4},{8,11},{9,10},{10,... | collective-permute-start | bytes 786440 | tf_op jit(solution)/shard_map/ppermute | solution.py:251
  95.7 17.3 %collective-permute-start.14 = (bf16[2,128,512]{2,1,0:T(8,128)(2,1)S(1)}, bf16[2,128,512]{2,1,0:T(8,128)(2,1)S(1)}, u32[]{:S(2)}, u32[]{:S(2)}) collective-permute-start(bf16[2,128,512]{2,1,0:T(8,128)(2,1)S(1)} %get-tuple-element.71), channel_id=1, source_target_pairs={{0,1},{1,0},{2,3},{3,2},{4,5},{5,4},{6,7},{7,6},{8,9},{9,8},{10,11... | collective-permute-start | bytes 786440 | tf_op jit(solution)/shard_map/ppermute | solution.py:251
  103.7 11.7 %collective-permute-start.15 = (bf16[2,128,512]{2,1,0:T(8,128)(2,1)S(1)}, bf16[2,128,512]{2,1,0:T(8,128)(2,1)S(1)}, u32[]{:S(2)}, u32[]{:S(2)}) collective-permute-start(bf16[2,128,512]{2,1,0:T(8,128)(2,1)S(1)} %get-tuple-element.72), channel_id=1, source_target_pairs={{0,2},{1,3},{2,0},{3,1},{4,6},{5,7},{6,4},{7,5},{8,10},{9,11},{10,... | collective-permute-start | bytes 786440 | tf_op jit(solution)/shard_map/ppermute | solution.py:251
  103.7 20.2 %collective-permute-start.16 = (bf16[2,128,512]{2,1,0:T(8,128)(2,1)S(1)}, bf16[2,128,512]{2,1,0:T(8,128)(2,1)S(1)}, u32[]{:S(2)}, u32[]{:S(2)}) collective-permute-start(bf16[2,128,512]{2,1,0:T(8,128)(2,1)S(1)} %get-tuple-element.73), channel_id=1, source_target_pairs={{0,3},{1,2},{2,1},{3,0},{4,7},{5,6},{6,5},{7,4},{8,11},{9,10},{10,... | collective-permute-start | bytes 786440 | tf_op jit(solution)/shard_map/ppermute | solution.py:251
  105.4 19.3 %collective-permute-start.17 = (bf16[2,128,512]{2,1,0:T(8,128)(2,1)S(1)}, bf16[2,128,512]{2,1,0:T(8,128)(2,1)S(1)}, u32[]{:S(2)}, u32[]{:S(2)}) collective-permute-start(bf16[2,128,512]{2,1,0:T(8,128)(2,1)S(1)} %get-tuple-element.74), channel_id=1, source_target_pairs={{0,4},{1,5},{2,6},{3,7},{4,0},{5,1},{6,2},{7,3},{8,12},{9,13},{10,... | collective-permute-start | bytes 786440 | tf_op jit(solution)/shard_map/ppermute | solution.py:251
  107.4 20.2 %collective-permute-start.18 = (bf16[2,128,512]{2,1,0:T(8,128)(2,1)S(1)}, bf16[2,128,512]{2,1,0:T(8,128)(2,1)S(1)}, u32[]{:S(2)}, u32[]{:S(2)}) collective-permute-start(bf16[2,128,512]{2,1,0:T(8,128)(2,1)S(1)} %get-tuple-element.75), channel_id=1, source_target_pairs={{0,5},{1,4},{2,7},{3,6},{4,1},{5,0},{6,3},{7,2},{8,13},{9,12},{10,... | collective-permute-start | bytes 786440 | tf_op jit(solution)/shard_map/ppermute | solution.py:251
  113.0 31.3 %collective-permute-start.19 = (bf16[2,128,512]{2,1,0:T(8,128)(2,1)S(1)}, bf16[2,128,512]{2,1,0:T(8,128)(2,1)S(1)}, u32[]{:S(2)}, u32[]{:S(2)}) collective-permute-start(bf16[2,128,512]{2,1,0:T(8,128)(2,1)S(1)} %get-tuple-element.76), channel_id=1, source_target_pairs={{0,6},{1,7},{2,4},{3,5},{4,2},{5,3},{6,0},{7,1},{8,14},{9,15},{10,... | collective-permute-start | bytes 786440 | tf_op jit(solution)/shard_map/ppermute | solution.py:251
  115.4 36.6 %collective-permute-start.20 = (bf16[2,128,512]{2,1,0:T(8,128)(2,1)S(1)}, bf16[2,128,512]{2,1,0:T(8,128)(2,1)S(1)}, u32[]{:S(2)}, u32[]{:S(2)}) collective-permute-start(bf16[2,128,512]{2,1,0:T(8,128)(2,1)S(1)} %get-tuple-element.77), channel_id=1, source_target_pairs={{0,7},{1,6},{2,5},{3,4},{4,3},{5,2},{6,1},{7,0},{8,15},{9,14},{10,... | collective-permute-start | bytes 786440 | tf_op jit(solution)/shard_map/ppermute | solution.py:251
  115.8 36.2 %copy-start.15 = (f32[128,4,512]{2,1,0:T(4,128)S(1)}, f32[128,4,512]{2,1,0:T(4,128)}, u32[]{:S(2)}) copy-start(f32[128,4,512]{2,1,0:T(4,128)} %param.9) | copy-start | bytes 3145732
  123.9 36.8 %copy-start.13 = (bf16[2,128,512]{2,1,0:T(8,128)(2,1)}, bf16[2,128,512]{2,1,0:T(8,128)(2,1)S(1)}, u32[]{:S(2)}) copy-start(bf16[2,128,512]{2,1,0:T(8,128)(2,1)S(1)} %get-tuple-element.70.refs_0_.refs_1_) | copy-start | bytes 786436
  123.9 36.8 %collective-permute-start.25 = (bf16[2,128,512]{2,1,0:T(8,128)(2,1)S(1)}, bf16[2,128,512]{2,1,0:T(8,128)(2,1)S(1)}, u32[]{:S(2)}, u32[]{:S(2)}) collective-permute-start(bf16[2,128,512]{2,1,0:T(8,128)(2,1)S(1)} %get-tuple-element.86), channel_id=1, source_target_pairs={{0,1},{1,0},{2,3},{3,2},{4,5},{5,4},{6,7},{7,6},{8,9},{9,8},{10,11... | collective-permute-start | bytes 786440 | tf_op jit(solution)/shard_map/ppermute | solution.py:251
  124.8 39.5 %collective-permute-start.26 = (bf16[2,128,512]{2,1,0:T(8,128)(2,1)S(1)}, bf16[2,128,512]{2,1,0:T(8,128)(2,1)S(1)}, u32[]{:S(2)}, u32[]{:S(2)}) collective-permute-start(bf16[2,128,512]{2,1,0:T(8,128)(2,1)S(1)} %get-tuple-element.87), channel_id=1, source_target_pairs={{0,2},{1,3},{2,0},{3,1},{4,6},{5,7},{6,4},{7,5},{8,10},{9,11},{10,... | collective-permute-start | bytes 786440 | tf_op jit(solution)/shard_map/ppermute | solution.py:251
  127.6 37.4 %collective-permute-start.27 = (bf16[2,128,512]{2,1,0:T(8,128)(2,1)S(1)}, bf16[2,128,512]{2,1,0:T(8,128)(2,1)S(1)}, u32[]{:S(2)}, u32[]{:S(2)}) collective-permute-start(bf16[2,128,512]{2,1,0:T(8,128)(2,1)S(1)} %get-tuple-element.88), channel_id=1, source_target_pairs={{0,3},{1,2},{2,1},{3,0},{4,7},{5,6},{6,5},{7,4},{8,11},{9,10},{10,... | collective-permute-start | bytes 786440 | tf_op jit(solution)/shard_map/ppermute | solution.py:251
  144.3 39.1 %collective-permute-start.28 = (bf16[2,128,512]{2,1,0:T(8,128)(2,1)S(1)}, bf16[2,128,512]{2,1,0:T(8,128)(2,1)S(1)}, u32[]{:S(2)}, u32[]{:S(2)}) collective-permute-start(bf16[2,128,512]{2,1,0:T(8,128)(2,1)S(1)} %get-tuple-element.89), channel_id=1, source_target_pairs={{0,4},{1,5},{2,6},{3,7},{4,0},{5,1},{6,2},{7,3},{8,12},{9,13},{10,... | collective-permute-start | bytes 786440 | tf_op jit(solution)/shard_map/ppermute | solution.py:251
  152.0 34.0 %collective-permute-start.29 = (bf16[2,128,512]{2,1,0:T(8,128)(2,1)S(1)}, bf16[2,128,512]{2,1,0:T(8,128)(2,1)S(1)}, u32[]{:S(2)}, u32[]{:S(2)}) collective-permute-start(bf16[2,128,512]{2,1,0:T(8,128)(2,1)S(1)} %get-tuple-element.90), channel_id=1, source_target_pairs={{0,5},{1,4},{2,7},{3,6},{4,1},{5,0},{6,3},{7,2},{8,13},{9,12},{10,... | collective-permute-start | bytes 786440 | tf_op jit(solution)/shard_map/ppermute | solution.py:251
  156.7 38.0 %copy-start.18 = (f32[16,4]{0,1:T(4,128)S(1)}, f32[16,4]{0,1:T(4,128)}, u32[]{:S(2)}) copy-start(f32[16,4]{0,1:T(4,128)} %param.10) | copy-start | bytes 772
  160.7 57.9 %copy-start.2 = (f32[128,512]{1,0:T(8,128)S(1)}, f32[128,512]{1,0:T(8,128)}, u32[]{:S(2)}) copy-start(f32[128,512]{1,0:T(8,128)} %weight_ref.1) | copy-start | bytes 786436
  161.4 33.7 %collective-permute-start.30 = (bf16[2,128,512]{2,1,0:T(8,128)(2,1)}, bf16[2,128,512]{2,1,0:T(8,128)(2,1)}, u32[]{:S(2)}, u32[]{:S(2)}) collective-permute-start(bf16[2,128,512]{2,1,0:T(8,128)(2,1)} %get-tuple-element.91), channel_id=1, source_target_pairs={{0,6},{1,7},{2,4},{3,5},{4,2},{5,3},{6,0},{7,1},{8,14},{9,15},{10,... | collective-permute-start | bytes 786440 | tf_op jit(solution)/shard_map/ppermute | solution.py:251
  164.9 35.2 %collective-permute-start.31 = (bf16[2,128,512]{2,1,0:T(8,128)(2,1)}, bf16[2,128,512]{2,1,0:T(8,128)(2,1)}, u32[]{:S(2)}, u32[]{:S(2)}) collective-permute-start(bf16[2,128,512]{2,1,0:T(8,128)(2,1)} %get-tuple-element.92), channel_id=1, source_target_pairs={{0,7},{1,6},{2,5},{3,4},{4,3},{5,2},{6,1},{7,0},{8,15},{9,14},{10,... | collective-permute-start | bytes 786440 | tf_op jit(solution)/shard_map/ppermute | solution.py:251
  165.7 36.5 %collective-permute-start.21 = (bf16[2,128,512]{2,1,0:T(8,128)(2,1)S(1)}, bf16[2,128,512]{2,1,0:T(8,128)(2,1)}, u32[]{:S(2)}, u32[]{:S(2)}) collective-permute-start(bf16[2,128,512]{2,1,0:T(8,128)(2,1)S(1)} %get-tuple-element.78.refs_16_), channel_id=1, source_target_pairs={{0,8},{8,16},{16,24},{1,9},{9,17},{17,25},{2,10},{10,18},{18,26},{... | collective-permute-start | bytes 786440 | tf_op jit(solution)/shard_map/ppermute | solution.py:258
  184.2 19.9 %collective-permute-start.22 = (bf16[2,128,512]{2,1,0:T(8,128)(2,1)S(1)}, bf16[2,128,512]{2,1,0:T(8,128)(2,1)}, u32[]{:S(2)}, u32[]{:S(2)}) collective-permute-start(bf16[2,128,512]{2,1,0:T(8,128)(2,1)S(1)} %get-tuple-element.79.refs_17_), channel_id=1, source_target_pairs={{0,8},{8,16},{16,24},{1,9},{9,17},{17,25},{2,10},{10,18},{18,26},{... | collective-permute-start | bytes 786440 | tf_op jit(solution)/shard_map/ppermute | solution.py:258
  186.8 19.2 %collective-permute-start.23 = (bf16[2,128,512]{2,1,0:T(8,128)(2,1)S(1)}, bf16[2,128,512]{2,1,0:T(8,128)(2,1)}, u32[]{:S(2)}, u32[]{:S(2)}) collective-permute-start(bf16[2,128,512]{2,1,0:T(8,128)(2,1)S(1)} %get-tuple-element.80.refs_18_), channel_id=1, source_target_pairs={{0,8},{8,16},{16,24},{1,9},{9,17},{17,25},{2,10},{10,18},{18,26},{... | collective-permute-start | bytes 786440 | tf_op jit(solution)/shard_map/ppermute | solution.py:258
  195.1 22.7 %collective-permute-start.24 = (bf16[2,128,512]{2,1,0:T(8,128)(2,1)S(1)}, bf16[2,128,512]{2,1,0:T(8,128)(2,1)S(1)}, u32[]{:S(2)}, u32[]{:S(2)}) collective-permute-start(bf16[2,128,512]{2,1,0:T(8,128)(2,1)S(1)} %get-tuple-element.81.refs_19_), channel_id=1, source_target_pairs={{0,8},{8,16},{16,24},{1,9},{9,17},{17,25},{2,10},{10,18},{18,26},{... | collective-permute-start | bytes 786440 | tf_op jit(solution)/shard_map/ppermute | solution.py:258
  200.2 17.7 %collective-permute-start.32 = (bf16[2,128,512]{2,1,0:T(8,128)(2,1)S(1)}, bf16[2,128,512]{2,1,0:T(8,128)(2,1)S(1)}, u32[]{:S(2)}, u32[]{:S(2)}) collective-permute-start(bf16[2,128,512]{2,1,0:T(8,128)(2,1)S(1)} %get-tuple-element.82.refs_0_.refs_4_), channel_id=1, source_target_pairs={{8,0},{16,8},{24,16},{9,1},{17,9},{25,17},{10,2},{18,10},{26,18},{... | collective-permute-start | bytes 786440 | tf_op jit(solution)/shard_map/ppermute | solution.py:258
  202.1 15.7 %collective-permute-start.33 = (bf16[2,128,512]{2,1,0:T(8,128)(2,1)S(1)}, bf16[2,128,512]{2,1,0:T(8,128)(2,1)S(1)}, u32[]{:S(2)}, u32[]{:S(2)}) collective-permute-start(bf16[2,128,512]{2,1,0:T(8,128)(2,1)S(1)} %get-tuple-element.83.refs_5_), channel_id=1, source_target_pairs={{8,0},{16,8},{24,16},{9,1},{17,9},{25,17},{10,2},{18,10},{26,18},{... | collective-permute-start | bytes 786440 | tf_op jit(solution)/shard_map/ppermute | solution.py:258
  204.1 13.8 %collective-permute-start.34 = (bf16[2,128,512]{2,1,0:T(8,128)(2,1)S(1)}, bf16[2,128,512]{2,1,0:T(8,128)(2,1)S(1)}, u32[]{:S(2)}, u32[]{:S(2)}) collective-permute-start(bf16[2,128,512]{2,1,0:T(8,128)(2,1)S(1)} %get-tuple-element.84.refs_6_), channel_id=1, source_target_pairs={{8,0},{16,8},{24,16},{9,1},{17,9},{25,17},{10,2},{18,10},{26,18},{... | collective-permute-start | bytes 786440 | tf_op jit(solution)/shard_map/ppermute | solution.py:258
  206.0 11.9 %collective-permute-start.35 = (bf16[2,128,512]{2,1,0:T(8,128)(2,1)S(1)}, bf16[2,128,512]{2,1,0:T(8,128)(2,1)S(1)}, u32[]{:S(2)}, u32[]{:S(2)}) collective-permute-start(bf16[2,128,512]{2,1,0:T(8,128)(2,1)S(1)} %get-tuple-element.85.refs_7_), channel_id=1, source_target_pairs={{8,0},{16,8},{24,16},{9,1},{17,9},{25,17},{10,2},{18,10},{26,18},{... | collective-permute-start | bytes 786440 | tf_op jit(solution)/shard_map/ppermute | solution.py:258
  208.0 1.0 copy-start.4
  209.0 0.9 copy-start.6
  209.9 0.9 copy-start.8
  210.9 0.9 copy-start.10
  211.8 0.9 copy-start.12
  212.8 0.9 copy-start.14
  (7 other events, 5.1 us)

commit v4 on v3

--- a/solution.py
+++ b/solution.py
@@ -8,6 +8,7 @@
 from jax.sharding import PartitionSpec as P
 
 LANES = 128
+PIECES = 2
 LIMIT = 48 * 1024 * 1024
 SMEM = pl.BlockSpec(memory_space=pltpu.SMEM)
 AFTER = pl.BlockSpec(memory_space=pl.ANY)
@@ -27,8 +28,8 @@
 
 def right_kernel(after, ranks, states, me_ref, second_ref, *refs):
     refs = refs[after:]
-    kinds = len(refs) - 2 - ranks
-    packets, outs, wide, slabs = refs[:kinds], refs[kinds:-2], refs[-2], refs[-1]
+    kinds = len(refs) - 1 - ranks
+    packets, outs, slabs = refs[:kinds], refs[kinds:-1], refs[-1]
     me = me_ref[0]
     rows = packets[0].shape[0]
     group = packets[0].shape[2]
@@ -36,16 +37,13 @@
     piece = slabs.shape[2] // 2
     cuts = tiles * LANES // piece
     for n, packet in enumerate(packets):
-        wide[...] = packet[...].reshape(rows * 2 * group, LANES).astype(jnp.float32)
+        turned = [
+            packet[:, c].astype(jnp.float32).transpose(1, 0, 2).astype(jnp.bfloat16)
+            for c in range(2)
+        ]
 
         def part(c, j):
-            return jnp.concatenate(
-                [
-                    wide[pl.ds(c * group + t * states + j, rows, stride=2 * group), :]
-                    for t in range(tiles)
-                ],
-                1,
-            ).astype(jnp.bfloat16)
+            return jnp.concatenate([turned[c][t * states + j] for t in range(tiles)], 1)
 
         pairs = [complex_rows(part(0, j), part(1, j)) for j in range(states)]
         left = jnp.concatenate([p[0] for p in pairs] + [p[1] for p in pairs], 0)
@@ -79,7 +77,6 @@
         out_specs=[pl.BlockSpec((kinds, block, 2 * piece), lambda i: (0, i, 0))] * ranks,
         out_shape=[jax.ShapeDtypeStruct((kinds, rows, 2 * piece), jnp.bfloat16)] * ranks,
         scratch_shapes=[
-            pltpu.VMEM((block * 2 * group, LANES), jnp.float32),
             pltpu.VMEM((ranks, block, 2 * piece), jnp.bfloat16),
         ],
         compiler_params=params(),
@@ -135,42 +132,46 @@
     )(me, first, *after, *slabs)
 
 
+def phased_product(me, n, second_ref, cosine_ref, sine_ref, ins, order, slabs):
+    states, _, width = cosine_ref.shape
+    piece = slabs.shape[2] // 2
+    cuts = width // piece
+    for s, part in zip(order, ins):
+        slabs[me ^ s] = part[n]
+    pairs = []
+    for j in range(states):
+        real, imag = (
+            jnp.concatenate(
+                [slabs[j * cuts + p, :, c * piece : (c + 1) * piece] for p in range(cuts)], 1
+            ).astype(jnp.float32)
+            for c in range(2)
+        )
+        cosine, sine = cosine_ref[j], sine_ref[j]
+        pairs.append(
+            complex_rows(
+                (real * cosine + imag * sine).astype(jnp.bfloat16),
+                (imag * cosine - real * sine).astype(jnp.bfloat16),
+            )
+        )
+    left = jnp.concatenate([p[0] for p in pairs] + [p[1] for p in pairs], 0)
+    product = jnp.dot(left, second_ref[...], preferred_element_type=jnp.float32)
+    return product.astype(jnp.bfloat16)
+
+
 def phase_kernel(after, ranks, me_ref, second_ref, cosine_ref, sine_ref, *refs):
     refs = refs[after:]
     ins, outs, slabs = refs[:ranks], refs[ranks:-1], refs[-1]
-    me = me_ref[0]
-    states, rows, width = cosine_ref.shape
-    piece = slabs.shape[2] // 2
-    cuts = width // piece
-    for n in range(len(outs) // states):
-        for s, part in enumerate(ins):
-            slabs[me ^ s] = part[n]
-        pairs = []
-        for j in range(states):
-            real, imag = (
-                jnp.concatenate(
-                    [
-                        slabs[j * cuts + p, :, c * piece : (c + 1) * piece]
-                        for p in range(cuts)
-                    ],
-                    1,
-                ).astype(jnp.float32)
-                for c in range(2)
-            )
-            cosine, sine = cosine_ref[j], sine_ref[j]
-            pairs.append(
-                complex_rows(
-                    (real * cosine + imag * sine).astype(jnp.bfloat16),
-                    (imag * cosine - real * sine).astype(jnp.bfloat16),
-                )
-            )
-        left = jnp.concatenate([p[0] for p in pairs] + [p[1] for p in pairs], 0)
-        product = jnp.dot(left, second_ref[...], preferred_element_type=jnp.float32)
-        product = product.astype(jnp.bfloat16)
+    states, rows, _ = cosine_ref.shape
+    share = outs[0].shape[1]
+    pieces = states // share
+    for n in range(len(outs) // pieces):
+        product = phased_product(
+            me_ref[0], n, second_ref, cosine_ref, sine_ref, ins, range(ranks), slabs
+        )
         for c in range(2):
             for j in range(states):
                 first = (c * states + j) * rows
-                outs[n * states + j][c] = product[first : first + rows]
+                outs[n * pieces + j // share][c, j % share] = product[first : first + rows]
 
 
 def phase_call(after, me, second, cosine, sine, slabs):
@@ -178,6 +179,8 @@
     kinds, rows, wide = slabs[0].shape
     states, _, width = cosine.shape
     block = rows // 2
+    share = states // PIECES
+    count = kinds * PIECES
     table = pl.BlockSpec((states, block, width), lambda i: (0, i, 0))
     return pl.pallas_call(
         functools.partial(phase_kernel, len(after), ranks),
@@ -185,8 +188,8 @@
         in_specs=[SMEM, pl.BlockSpec(second.shape, lambda i: (0, 0)), table, table]
         + [AFTER] * len(after)
         + [pl.BlockSpec((kinds, block, wide), lambda i: (0, i, 0))] * ranks,
-        out_specs=[pl.BlockSpec((2, block, width), lambda i: (0, i, 0))] * (kinds * states),
-        out_shape=[jax.ShapeDtypeStruct((2, rows, width), jnp.bfloat16)] * (kinds * states),
+        out_specs=[pl.BlockSpec((2, share, block, width), lambda i: (0, 0, i, 0))] * count,
+        out_shape=[jax.ShapeDtypeStruct((2, share, rows, width), jnp.bfloat16)] * count,
         scratch_shapes=[pltpu.VMEM((ranks, block, wide), jnp.bfloat16)],
         compiler_params=params(),
         cost_estimate=cost(
@@ -196,52 +199,77 @@
     )(me, second, cosine, sine, *after, *slabs)
 
 
-def mix_kernel(up_ref, down_ref, weight_ref, *refs):
-    kinetic, out, wide = refs[:-2], refs[-2], refs[-1]
-    _, rows, width = kinetic[0].shape
+def mix_kernel(
+    chosen, order, me_ref, up_ref, down_ref, second_ref, cosine_ref, sine_ref, weight_ref, *refs
+):
+    ranks = len(order)
+    ins, known, (out, slabs, fresh) = refs[:ranks], refs[ranks:-3], refs[-3:]
     blocks, states = up_ref.shape
-    tiles = width // LANES
-    group = tiles * states
+    rows, width = weight_ref.shape
+    share = known[0].shape[1]
+    pieces = states // share
+    group = out.shape[3]
     weight = weight_ref[...]
+    others = [k for k in range(-1, blocks + 1) if k not in chosen]
+    for n in range(len(chosen)):
+        product = phased_product(
+            me_ref[0], n, second_ref, cosine_ref, sine_ref, ins, order, slabs
+        )
+        fresh[n] = product.reshape(2, states, rows, width)
+
+    def kinetic(k, c, j):
+        if k in chosen:
+            value = fresh[chosen.index(k), c, j]
+        else:
+            value = known[others.index(k) * pieces + j // share][c, j % share]
+        return value.astype(jnp.float32)
+
     for k in range(blocks):
+        columns = [[None] * group for _ in range(2)]
         for j in range(states):
-            below, here, above = (kinetic[(k + n) * states + j] for n in range(3))
             up, down = up_ref[k, j], down_ref[k, j]
-            mixed = [
-                up * above[c].astype(jnp.float32) + down * below[c].astype(jnp.float32)
-                for c in range(2)
-            ]
+            mixed = [up * kinetic(k + 1, c, j) + down * kinetic(k - 1, c, j) for c in range(2)]
             parts = (
-                here[0].astype(jnp.float32) + weight * mixed[1],
-                here[1].astype(jnp.float32) - weight * mixed[0],
+                kinetic(k, 0, j) + weight * mixed[1],
+                kinetic(k, 1, j) - weight * mixed[0],
             )
             for c in range(2):
-                for t in range(tiles):
-                    wide[pl.ds(c * group + t * states + j, rows, stride=2 * group), :] = parts[c][
-                        :, t * LANES : (t + 1) * LANES
-                    ]
-        out[:, :, k] = wide[...].astype(jnp.bfloat16).reshape(rows, 2, group, LANES)
-
-
-def mix_call(up, down, weight, kinetic):
-    _, rows, width = kinetic[0].shape
+                for t in range(width // LANES):
+                    columns[c][t * states + j] = parts[c][:, t * LANES : (t + 1) * LANES]
+        for c in range(2):
+            out[:, c, k] = jnp.stack(columns[c], 0).transpose(1, 0, 2).astype(jnp.bfloat16)
+
+
+def mix_call(me, up, down, second, cosine, sine, weight, chosen, slabs, known):
+    ranks = len(slabs)
+    half = ranks // 2
+    order = (*range(half, ranks), *range(half))
+    kinds, rows, wide = slabs[0].shape
+    _, share, _, width = known[0].shape
     blocks, states = up.shape
     group = width // LANES * states
     block = rows // 4
+    table = pl.BlockSpec((states, block, width), lambda i: (0, i, 0))
     return pl.pallas_call(
-        mix_kernel,
+        functools.partial(mix_kernel, tuple(chosen), order),
         grid=(rows // block,),
-        in_specs=[SMEM, SMEM, pl.BlockSpec((block, width), lambda i: (i, 0))]
-        + [pl.BlockSpec((2, block, width), lambda i: (0, i, 0))] * len(kinetic),
+        in_specs=[SMEM] * 3
+        + [pl.BlockSpec(second.shape, lambda i: (0, 0)), table, table]
+        + [pl.BlockSpec((block, width), lambda i: (i, 0))]
+        + [pl.BlockSpec((kinds, block, wide), lambda i: (0, i, 0))] * ranks
+        + [pl.BlockSpec((2, share, block, width), lambda i: (0, 0, i, 0))] * len(known),
         out_specs=pl.BlockSpec((block, 2, blocks, group, LANES), lambda i: (i, 0, 0, 0, 0)),
         out_shape=jax.ShapeDtypeStruct((rows, 2, blocks, group, LANES), jnp.bfloat16),
-        scratch_shapes=[pltpu.VMEM((block * 2 * group, LANES), jnp.float32)],
+        scratch_shapes=[
+            pltpu.VMEM((ranks, block, wide), jnp.bfloat16),
+            pltpu.VMEM((kinds, 2, states, block, width), jnp.bfloat16),
+        ],
         compiler_params=params(),
         cost_estimate=cost(
-            20 * blocks * states * rows * width, 10 * blocks * states * rows * width
+            8 * kinds * states * rows * width * width, 10 * blocks * states * rows * width
         ),
         name="mix",
-    )(up, down, weight, *kinetic)
+    )(me, up, down, second, cosine, sine, weight, *[slabs[s] for s in order], *known)
 
 
 def exchanged(slabs, axis):
@@ -286,16 +314,10 @@
 
     angles = potential.transpose(1, 0, 2)
     cosine, sine = jnp.cos(angles), jnp.sin(angles)
-    kinetic = [None] * blocks
-    for n, (chosen, back) in enumerate(zip(chunks, backs)):
-        after = [last]
-        values = phase_call(after, me, second, cosine, sine, back)
-        last = values[0]
-        for i, k in enumerate(chosen):
-            kinetic[k] = values[i * states : (i + 1) * states]
-        if n == 0:
-            below = [neighbour(edge, "hel", 1) for edge in kinetic[-1]]
-            above = [neighbour(edge, "hel", -1) for edge in kinetic[0]]
+    edge = phase_call([last], me, second, cosine, sine, backs[0])
+    low, high = edge[:PIECES], edge[-PIECES:]
+    below = [neighbour(x, "hel", 1) for x in high]
+    above = [neighbour(x, "hel", -1) for x in low]
 
     count = coupling.shape[0]
     helicities = jnp.arange(count, dtype=jnp.int32)
@@ -306,7 +328,10 @@
     start = lax.axis_index("hel") * blocks
     up = lax.dynamic_slice_in_dim(couple_up, start, blocks, 0)
     down = lax.dynamic_slice_in_dim(couple_down, start, blocks, 0)
-    out = mix_call(up, down, radial_weight, sum([list(x) for x in (below, *kinetic, above)], []))
+    known = [*below, *low, *high, *above]
+    out = mix_call(
+        me, up, down, second, cosine, sine, radial_weight, chunks[1], backs[1], known
+    )
     out = out.reshape(rows, 2, blocks, tiles, states, LANES).transpose(0, 1, 2, 4, 3, 5)
     return out.reshape(rows, 2, blocks, states, width)
 

time: 230 us -> 232 us (level)
  waiting for transfers between devices: 77 us -> 105 us
  starting transfers between devices: 82.7 us -> 66 us
  Pallas kernels: 45.4 us -> 37.4 us
    ppermute x28, waiting for transfers between devices: 77 us -> 101 us  [exchanged(): result[s] = lax.ppermute(slabs[s], axis, [(i, i ^ s) for i in range(count)])]
    ppermute x8 -> x4, starting transfers between devices: 40.4 us -> 18.6 us  [neighbour(): return lax.ppermute(edge, axis, pairs)]
    ppermute x28, starting transfers between devices: 42.3 us -> 47.5 us  [exchanged(): result[s] = lax.ppermute(slabs[s], axis, [(i, i ^ s) for i in range(count)])]
    pallas_call x2 -> x1, Pallas kernels: 8.09 us -> 3.95 us  [phase_call(): pl.pallas_call(functools.partial(phase_kernel, len(after), ranks), grid=(...]
    ppermute x8 -> x4, waiting for transfers between devices: 0.02 us -> 3.62 us  [neighbour(): return lax.ppermute(edge, axis, pairs)]
    pallas_call x2, Pallas kernels: 12.3 us -> 9.06 us  [right_call(): pl.pallas_call(functools.partial(right_kernel, len(after), ranks, states)...]
    unnamed x40 -> x38, local copies, waits for them, and re-layouts: 11.4 us -> 10.6 us
  transfers between devices with their start and end apart: 36 -> 32, of which waited for: 11 -> 15; matrix products, arithmetic and copies ran while one was open for 5% -> 5% of each run, Pallas kernels for 13% -> 10%
where the time goes in v4:
time: 232 us; the launch traced here: 231 us
  waiting for transfers between devices  105 us (45%)
  starting transfers between devices  66 us (28%)
  Pallas kernels  37.4 us (16%)
  local copies, waits for them, and re-layouts  21.9 us (9%)
    ppermute x28, waiting for transfers between devices, exchanged(): result[s] = lax.ppermute(slabs[s], axis, [(i, i ^ s) for i in range(count)])  101 us
    ppermute x28, starting transfers between devices, exchanged(): result[s] = lax.ppermute(slabs[s], axis, [(i, i ^ s) for i in range(count)])  47.5 us
    ppermute x4, starting transfers between devices, neighbour(): return lax.ppermute(edge, axis, pairs)  18.6 us
    pallas_call x2, Pallas kernels, left_call(): pl.pallas_call(functools.partial(left_kernel, len(after), ranks), grid=(k...  15.4 us
    unnamed x38, local copies, waits for them, and re-layouts  10.6 us
    pallas_call x2, Pallas kernels, right_call(): pl.pallas_call(functools.partial(right_kernel, len(after), ranks, states)...  9.06 us
    pallas_call x1, Pallas kernels, mix_call(): pl.pallas_call(functools.partial(mix_kernel, tuple(chosen), order), grid=...  8.93 us
    reshape x1, local copies, waits for them, and re-layouts, per_device(): first = first_propagator.reshape(2 * whole, whole).T  6.51 us
  transfers between devices with their start and end apart: 32, of which 15 were waited for; matrix products, arithmetic and copies ran while one was open for 5% of the time, Pallas kernels for 10%

profile of v4, /device:TPU:9, one launch (start us, length us, event | category | flops | bytes accessed | tf_op | source)
XLA Modules:
  0.0 230.5 jit_solution(10473054490336068279)
XLA Ops:
  0.0 1.2 copy-done
  1.2 4.9 %right.2 = (bf16[2,128,512]{2,1,0:T(8,128)(2,1)S(1)}, bf16[2,128,512]{2,1,0:T(8,128)(2,1)S(1)}, bf16[2,128,512]{2,1,0:T(8,128)(2,1)S(1)}, bf16[2,128,512]{2,1,0:...) custom-call(s32[1]{0:T(128)} %bitcast.me_ref.refs_0_, ...), custom_call_target="tpu_custom_call" | custom-call | flops 2147483648 | bytes 4194304 | tf_op jit(solution)/shard_map/right/pallas_call | solution.py:68
  6.1 1.2 collective-permute-start
  7.5 1.2 collective-permute-start.2
  8.7 2.3 collective-permute-start.3
  11.0 1.0 collective-permute-start.4
  12.1 1.2 collective-permute-done.refs_2_
  13.3 1.3 collective-permute-start.5
  14.6 7.3 %collective-permute-done.1.refs_3_ = bf16[2,128,512]{2,1,0:T(8,128)(2,1)S(1)} collective-permute-done((bf16[2,128,512]{2,1,0:T(8,128)(2,1)S(1)}, bf16[2,128,512]{2,1,0:T(8,128)(2,1)S(1)}, u32[]{:S(2)}, u32[]{:S(2)}) %collective-permute-start.1) | collective-permute-done | bytes 262176 | tf_op jit(solution)/shard_map/ppermute | solution.py:279
  21.9 6.5 %copy.14 = bf16[2048,1024]{0,1:T(8,128)(2,1)} copy(bf16[2048,1024]{1,0:T(8,128)(2,1)} %bitcast.27) | data formatting | bytes 8388608 | tf_op jit(solution)/shard_map/reshape | solution.py:297
  28.4 4.2 %right.3 = (bf16[2,128,512]{2,1,0:T(8,128)(2,1)S(1)}, bf16[2,128,512]{2,1,0:T(8,128)(2,1)S(1)}, bf16[2,128,512]{2,1,0:T(8,128)(2,1)S(1)}, bf16[2,128,512]{2,1,0:...) custom-call(s32[1]{0:T(128)} %bitcast.me_ref.refs_0_, ...), custom_call_target="tpu_custom_call" | custom-call | flops 2147483648 | bytes 4194304 | tf_op jit(solution)/shard_map/right/pallas_call | solution.py:68
  32.6 3.6 %collective-permute-start.10 = (bf16[2,128,512]{2,1,0:T(8,128)(2,1)S(1)}, bf16[2,128,512]{2,1,0:T(8,128)(2,1)S(1)}, u32[]{:S(2)}, u32[]{:S(2)}) collective-permute-start(bf16[2,128,512]{2,1,0:T(8,128)(2,1)S(1)} %get-tuple-element.54), channel_id=1, source_target_pairs={{0,4},{1,5},{2,6},{3,7},{4,0},{5,1},{6,2},{7,3},{8,12},{9,13},{10,... | collective-permute-start | bytes 786440 | tf_op jit(solution)/shard_map/ppermute | solution.py:279
  36.3 1.9 collective-permute-start.11
  38.2 16.5 %collective-permute-done.4.refs_6_ = bf16[2,128,512]{2,1,0:T(8,128)(2,1)S(1)} collective-permute-done((bf16[2,128,512]{2,1,0:T(8,128)(2,1)}, bf16[2,128,512]{2,1,0:T(8,128)(2,1)S(1)}, u32[]{:S(2)}, u32[]{:S(2)}) %collective-permute-start.4) | collective-permute-done | bytes 262176 | tf_op jit(solution)/shard_map/ppermute | solution.py:279
  54.7 8.5 %collective-permute-done.5.refs_7_ = bf16[2,128,512]{2,1,0:T(8,128)(2,1)S(1)} collective-permute-done((bf16[2,128,512]{2,1,0:T(8,128)(2,1)S(1)}, bf16[2,128,512]{2,1,0:T(8,128)(2,1)S(1)}, u32[]{:S(2)}, u32[]{:S(2)}) %collective-permute-start.5) | collective-permute-done | bytes 262176 | tf_op jit(solution)/shard_map/ppermute | solution.py:279
  63.2 11.6 %collective-permute-start.13 = (bf16[2,128,512]{2,1,0:T(8,128)(2,1)S(1)}, bf16[2,128,512]{2,1,0:T(8,128)(2,1)S(1)}, u32[]{:S(2)}, u32[]{:S(2)}) collective-permute-start(bf16[2,128,512]{2,1,0:T(8,128)(2,1)S(1)} %get-tuple-element.57), channel_id=1, source_target_pairs={{0,7},{1,6},{2,5},{3,4},{4,3},{5,2},{6,1},{7,0},{8,15},{9,14},{10,... | collective-permute-start | bytes 786440 | tf_op jit(solution)/shard_map/ppermute | solution.py:279
  74.7 3.3 %collective-permute-done.6.refs_8_ = bf16[2,128,512]{2,1,0:T(8,128)(2,1)} collective-permute-done((bf16[2,128,512]{2,1,0:T(8,128)(2,1)S(1)}, bf16[2,128,512]{2,1,0:T(8,128)(2,1)}, u32[]{:S(2)}, u32[]{:S(2)}) %collective-permute-start.6) | collective-permute-done | bytes 262176 | tf_op jit(solution)/shard_map/ppermute | solution.py:279
  78.5 7.4 %left.2 = (bf16[2,128,512]{2,1,0:T(8,128)(2,1)S(1)}, bf16[2,128,512]{2,1,0:T(8,128)(2,1)S(1)}, bf16[2,128,512]{2,1,0:T(8,128)(2,1)S(1)}, bf16[2,128,512]{2,1,0:T...) custom-call(s32[1]{0:T(128)} %bitcast.me_ref.refs_0_, ...), custom_call_target="tpu_custom_call" | custom-call | flops 4294967296 | bytes 8388608 | tf_op jit(solution)/shard_map/left/pallas_call | solution.py:115
  86.0 2.5 %collective-permute-done.11.refs_6_ = bf16[2,128,512]{2,1,0:T(8,128)(2,1)S(1)} collective-permute-done((bf16[2,128,512]{2,1,0:T(8,128)(2,1)S(1)}, bf16[2,128,512]{2,1,0:T(8,128)(2,1)S(1)}, u32[]{:S(2)}, u32[]{:S(2)}) %collective-permute-start.11) | collective-permute-done | bytes 262176 | tf_op jit(solution)/shard_map/ppermute | solution.py:279
  88.5 2.1 collective-permute-start.9
  90.6 3.5 %collective-permute-done.12.refs_7_ = bf16[2,128,512]{2,1,0:T(8,128)(2,1)S(1)} collective-permute-done((bf16[2,128,512]{2,1,0:T(8,128)(2,1)S(1)}, bf16[2,128,512]{2,1,0:T(8,128)(2,1)S(1)}, u32[]{:S(2)}, u32[]{:S(2)}) %collective-permute-start.12) | collective-permute-done | bytes 262176 | tf_op jit(solution)/shard_map/ppermute | solution.py:279
  94.1 1.2 collective-permute-start.21
  95.3 6.8 %collective-permute-done.13.refs_8_ = bf16[2,128,512]{2,1,0:T(8,128)(2,1)S(1)} collective-permute-done((bf16[2,128,512]{2,1,0:T(8,128)(2,1)S(1)}, bf16[2,128,512]{2,1,0:T(8,128)(2,1)S(1)}, u32[]{:S(2)}, u32[]{:S(2)}) %collective-permute-start.13) | collective-permute-done | bytes 262176 | tf_op jit(solution)/shard_map/ppermute | solution.py:279
  102.1 1.7 collective-permute-start.23
  103.9 1.9 collective-permute-start.24
  105.7 1.1 collective-permute-start.25
  106.8 4.5 %collective-permute-done.21.refs_2_ = bf16[2,128,512]{2,1,0:T(8,128)(2,1)S(1)} collective-permute-done((bf16[2,128,512]{2,1,0:T(8,128)(2,1)S(1)}, bf16[2,128,512]{2,1,0:T(8,128)(2,1)S(1)}, u32[]{:S(2)}, u32[]{:S(2)}) %collective-permute-start.21) | collective-permute-done | bytes 262176 | tf_op jit(solution)/shard_map/ppermute | solution.py:279
  111.3 2.5 %collective-permute-start.26 = (bf16[2,128,512]{2,1,0:T(8,128)(2,1)S(1)}, bf16[2,128,512]{2,1,0:T(8,128)(2,1)S(1)}, u32[]{:S(2)}, u32[]{:S(2)}) collective-permute-start(bf16[2,128,512]{2,1,0:T(8,128)(2,1)S(1)} %get-tuple-element.71), channel_id=1, source_target_pairs={{0,6},{1,7},{2,4},{3,5},{4,2},{5,3},{6,0},{7,1},{8,14},{9,15},{10,... | collective-permute-start | bytes 786440 | tf_op jit(solution)/shard_map/ppermute | solution.py:279
  114.2 8.0 %left.3 = (bf16[2,128,512]{2,1,0:T(8,128)(2,1)S(1)}, bf16[2,128,512]{2,1,0:T(8,128)(2,1)S(1)}, bf16[2,128,512]{2,1,0:T(8,128)(2,1)}, bf16[2,128,512]{2,1,0:T(8,1...) custom-call(s32[1]{0:T(128)} %bitcast.me_ref.refs_0_, ...), custom_call_target="tpu_custom_call" | custom-call | flops 4294967296 | bytes 8388608 | tf_op jit(solution)/shard_map/left/pallas_call | solution.py:115
  122.3 1.3 collective-permute-start.14
  123.6 1.6 collective-permute-start.15
  125.3 1.7 collective-permute-start.16
  127.0 31.5 %collective-permute-done.26.refs_7_ = bf16[2,128,512]{2,1,0:T(8,128)(2,1)S(1)} collective-permute-done((bf16[2,128,512]{2,1,0:T(8,128)(2,1)S(1)}, bf16[2,128,512]{2,1,0:T(8,128)(2,1)S(1)}, u32[]{:S(2)}, u32[]{:S(2)}) %collective-permute-start.26) | collective-permute-done | bytes 262176 | tf_op jit(solution)/shard_map/ppermute | solution.py:279
  158.5 2.8 %collective-permute-start.17 = (bf16[2,128,512]{2,1,0:T(8,128)(2,1)S(1)}, bf16[2,128,512]{2,1,0:T(8,128)(2,1)S(1)}, u32[]{:S(2)}, u32[]{:S(2)}) collective-permute-start(bf16[2,128,512]{2,1,0:T(8,128)(2,1)S(1)} %get-tuple-element.61), channel_id=1, source_target_pairs={{0,7},{1,6},{2,5},{3,4},{4,3},{5,2},{6,1},{7,0},{8,15},{9,14},{10,... | collective-permute-start | bytes 786440 | tf_op jit(solution)/shard_map/ppermute | solution.py:279
  161.3 4.4 %collective-permute-done.27.refs_8_ = bf16[2,128,512]{2,1,0:T(8,128)(2,1)S(1)} collective-permute-done((bf16[2,128,512]{2,1,0:T(8,128)(2,1)S(1)}, bf16[2,128,512]{2,1,0:T(8,128)(2,1)S(1)}, u32[]{:S(2)}, u32[]{:S(2)}) %collective-permute-start.27) | collective-permute-done | bytes 262176 | tf_op jit(solution)/shard_map/ppermute | solution.py:279
  165.7 1.1 collective-permute-start.18
  166.8 4.6 %sine_bitcast_fusion = (f32[4,128,512]{2,1,0:T(8,128)}, f32[4,128,512]{2,1,0:T(8,128)}) fusion(f32[128,4,512]{2,1,0:T(4,128)S(1)} %copy-done.16), kind=kLoop, calls=%fused_computation | loop fusion | bytes 3145728 | tf_op jit(solution)/shard_map/sin | solution.py:316
  171.5 3.9 %collective-permute-done.14.refs_0_ = bf16[2,128,512]{2,1,0:T(8,128)(2,1)S(1)} collective-permute-done((bf16[2,128,512]{2,1,0:T(8,128)(2,1)S(1)}, bf16[2,128,512]{2,1,0:T(8,128)(2,1)S(1)}, u32[]{:S(2)}, u32[]{:S(2)}) %collective-permute-start.14) | collective-permute-done | bytes 262176 | tf_op jit(solution)/shard_map/ppermute | solution.py:279
  176.0 2.7 %collective-permute-start.19 = (bf16[2,128,512]{2,1,0:T(8,128)(2,1)}, bf16[2,128,512]{2,1,0:T(8,128)(2,1)}, u32[]{:S(2)}, u32[]{:S(2)}) collective-permute-start(bf16[2,128,512]{2,1,0:T(8,128)(2,1)} %get-tuple-element.64), channel_id=1, source_target_pairs={{0,2},{1,3},{2,0},{3,1},{4,6},{5,7},{6,4},{7,5},{8,10},{9,11},{10,... | collective-permute-start | bytes 786440 | tf_op jit(solution)/shard_map/ppermute | solution.py:279
  178.8 4.0 %phase.1 = (bf16[2,2,128,512]{3,2,1,0:T(8,128)(2,1)S(1)}, bf16[2,2,128,512]{3,2,1,0:T(8,128)(2,1)S(1)}, bf16[2,2,128,512]{3,2,1,0:T(8,128)(2,1)S(1)}, bf16[2,2,128,512]{3,2,1,0:T(8,128)(2,1)S(1)}) custom-call(s32[1]{0:T(128)} %bitcast.me_ref.refs_0_, bf16[1024,512]{1,0:T(8,128)(2,1)S(1)} %bitcast.22, f32[4,128,512]{2,1,0:T(8,128)} %get-tuple-element.78.cosine_ref, ...), custom_call_target="tpu_custom_call" | custom-call | flops 2147483648 | bytes 4194304 | tf_op jit(solution)/shard_map/phase/pallas_call | solution.py:185
  183.5 11.1 %collective-permute-start.28 = (bf16[2,2,128,512]{3,2,1,0:T(8,128)(2,1)S(1)}, bf16[2,2,128,512]{3,2,1,0:T(8,128)(2,1)S(1)}, u32[]{:S(2)}, u32[]{:S(2)}) collective-permute-start(bf16[2,2,128,512]{3,2,1,0:T(8,128)(2,1)S(1)} %get-tuple-element.73.refs_12_), channel_id=1, source_target_pairs={{0,8},{8,16},{16,24},{1,9},{9,17},{17,25},{2,10},{10,18},{18,26},{... | collective-permute-start | bytes 1572872 | tf_op jit(solution)/shard_map/ppermute | solution.py:286
  195.3 3.6 %collective-permute-start.29 = (bf16[2,2,128,512]{3,2,1,0:T(8,128)(2,1)S(1)}, bf16[2,2,128,512]{3,2,1,0:T(8,128)(2,1)S(1)}, u32[]{:S(2)}, u32[]{:S(2)}) collective-permute-start(bf16[2,2,128,512]{3,2,1,0:T(8,128)(2,1)S(1)} %get-tuple-element.74.refs_13_), channel_id=1, source_target_pairs={{0,8},{8,16},{16,24},{1,9},{9,17},{17,25},{2,10},{10,18},{18,26},{... | collective-permute-start | bytes 1572872 | tf_op jit(solution)/shard_map/ppermute | solution.py:286
  199.7 1.9 collective-permute-start.30
  202.3 1.9 collective-permute-start.31
  205.0 7.3 %collective-permute-done.20.refs_7_ = bf16[2,128,512]{2,1,0:T(8,128)(2,1)} collective-permute-done((bf16[2,128,512]{2,1,0:T(8,128)(2,1)}, bf16[2,128,512]{2,1,0:T(8,128)(2,1)}, u32[]{:S(2)}, u32[]{:S(2)}) %collective-permute-start.20) | collective-permute-done | bytes 262176 | tf_op jit(solution)/shard_map/ppermute | solution.py:279
  212.3 3.6 %collective-permute-done.31.refs_15_ = bf16[2,2,128,512]{3,2,1,0:T(8,128)(2,1)} collective-permute-done((bf16[2,2,128,512]{3,2,1,0:T(8,128)(2,1)S(1)}, bf16[2,2,128,512]{3,2,1,0:T(8,128)(2,1)}, u32[]{:S(2)}, u32[]{:S(2)}) %collective-permute-start.31) | collective-permute-done | bytes 524320 | tf_op jit(solution)/shard_map/ppermute | solution.py:286
  215.9 0.9 copy-done.4
  221.6 8.9 %mix.1 = bf16[128,2,4,16,128]{4,3,2,1,0:T(8,128)(2,1)} custom-call(s32[1]{0:T(128)} %bitcast.me_ref.refs_0_, f32[4,4]{1,0:T(4,128)S(1)} %get-tuple-element.80.up_ref, f32[4,4]{1,0:T(4,128)S(1)} %get-tuple-element.79.down_ref, bf16[1024,512]{1,0:T(8,128)(2,1)} %bitcast.19, f32[4,128,512]{2,1,0:T(8,128)} %get-tuple-element.78.cosine_ref, ...), custom_call_target="tpu_custom_call" | custom-call | flops 2147483648 | bytes 10485760 | tf_op jit(solution)/shard_map/mix/pallas_call | solution.py:253
  (66 shorter events, 10.3 us)
Async XLA Ops:
  0.0 1.2 copy-start
  6.1 7.2 %collective-permute-start = (bf16[2,128,512]{2,1,0:T(8,128)(2,1)S(1)}, bf16[2,128,512]{2,1,0:T(8,128)(2,1)S(1)}, u32[]{:S(2)}, u32[]{:S(2)}) collective-permute-start(bf16[2,128,512]{2,1,0:T(8,128)(2,1)S(1)} %get-tuple-element.43), channel_id=1, source_target_pairs={{0,1},{1,0},{2,3},{3,2},{4,5},{5,4},{6,7},{7,6},{8,9},{9,8},{10,11... | collective-permute-start | bytes 786440 | tf_op jit(solution)/shard_map/ppermute | solution.py:279
  7.3 14.6 %collective-permute-start.1 = (bf16[2,128,512]{2,1,0:T(8,128)(2,1)S(1)}, bf16[2,128,512]{2,1,0:T(8,128)(2,1)S(1)}, u32[]{:S(2)}, u32[]{:S(2)}) collective-permute-start(bf16[2,128,512]{2,1,0:T(8,128)(2,1)S(1)} %get-tuple-element.44), channel_id=1, source_target_pairs={{0,2},{1,3},{2,0},{3,1},{4,6},{5,7},{6,4},{7,5},{8,10},{9,11},{10,... | collective-permute-start | bytes 786440 | tf_op jit(solution)/shard_map/ppermute | solution.py:279
  7.5 25.1 %collective-permute-start.2 = (bf16[2,128,512]{2,1,0:T(8,128)(2,1)}, bf16[2,128,512]{2,1,0:T(8,128)(2,1)S(1)}, u32[]{:S(2)}, u32[]{:S(2)}) collective-permute-start(bf16[2,128,512]{2,1,0:T(8,128)(2,1)} %get-tuple-element.45), channel_id=1, source_target_pairs={{0,3},{1,2},{2,1},{3,0},{4,7},{5,6},{6,5},{7,4},{8,11},{9,10},{10,... | collective-permute-start | bytes 786440 | tf_op jit(solution)/shard_map/ppermute | solution.py:279
  8.7 27.5 %collective-permute-start.3 = (bf16[2,128,512]{2,1,0:T(8,128)(2,1)}, bf16[2,128,512]{2,1,0:T(8,128)(2,1)S(1)}, u32[]{:S(2)}, u32[]{:S(2)}) collective-permute-start(bf16[2,128,512]{2,1,0:T(8,128)(2,1)} %get-tuple-element.46), channel_id=1, source_target_pairs={{0,4},{1,5},{2,6},{3,7},{4,0},{5,1},{6,2},{7,3},{8,12},{9,13},{10,... | collective-permute-start | bytes 786440 | tf_op jit(solution)/shard_map/ppermute | solution.py:279
  11.0 43.7 %collective-permute-start.4 = (bf16[2,128,512]{2,1,0:T(8,128)(2,1)}, bf16[2,128,512]{2,1,0:T(8,128)(2,1)S(1)}, u32[]{:S(2)}, u32[]{:S(2)}) collective-permute-start(bf16[2,128,512]{2,1,0:T(8,128)(2,1)} %get-tuple-element.47), channel_id=1, source_target_pairs={{0,5},{1,4},{2,7},{3,6},{4,1},{5,0},{6,3},{7,2},{8,13},{9,12},{10,... | collective-permute-start | bytes 786440 | tf_op jit(solution)/shard_map/ppermute | solution.py:279
  13.3 49.9 %collective-permute-start.5 = (bf16[2,128,512]{2,1,0:T(8,128)(2,1)S(1)}, bf16[2,128,512]{2,1,0:T(8,128)(2,1)S(1)}, u32[]{:S(2)}, u32[]{:S(2)}) collective-permute-start(bf16[2,128,512]{2,1,0:T(8,128)(2,1)S(1)} %get-tuple-element.48), channel_id=1, source_target_pairs={{0,6},{1,7},{2,4},{3,5},{4,2},{5,3},{6,0},{7,1},{8,14},{9,15},{10,... | collective-permute-start | bytes 786440 | tf_op jit(solution)/shard_map/ppermute | solution.py:279
  21.9 56.2 %collective-permute-start.6 = (bf16[2,128,512]{2,1,0:T(8,128)(2,1)S(1)}, bf16[2,128,512]{2,1,0:T(8,128)(2,1)}, u32[]{:S(2)}, u32[]{:S(2)}) collective-permute-start(bf16[2,128,512]{2,1,0:T(8,128)(2,1)S(1)} %get-tuple-element.49), channel_id=1, source_target_pairs={{0,7},{1,6},{2,5},{3,4},{4,3},{5,2},{6,1},{7,0},{8,15},{9,14},{10,... | collective-permute-start | bytes 786440 | tf_op jit(solution)/shard_map/ppermute | solution.py:279
  21.9 6.5 %copy-start.1 = (bf16[2,512,512]{2,1,0:T(8,128)(2,1)S(1)}, bf16[2,512,512]{2,1,0:T(8,128)(2,1)}, u32[]{:S(2)}) copy-start(bf16[2,512,512]{2,1,0:T(8,128)(2,1)} %param.8) | copy-start | bytes 3145732
  32.6 53.3 %collective-permute-start.10 = (bf16[2,128,512]{2,1,0:T(8,128)(2,1)S(1)}, bf16[2,128,512]{2,1,0:T(8,128)(2,1)S(1)}, u32[]{:S(2)}, u32[]{:S(2)}) collective-permute-start(bf16[2,128,512]{2,1,0:T(8,128)(2,1)S(1)} %get-tuple-element.54), channel_id=1, source_target_pairs={{0,4},{1,5},{2,6},{3,7},{4,0},{5,1},{6,2},{7,3},{8,12},{9,13},{10,... | collective-permute-start | bytes 786440 | tf_op jit(solution)/shard_map/ppermute | solution.py:279
  36.3 52.2 %collective-permute-start.11 = (bf16[2,128,512]{2,1,0:T(8,128)(2,1)S(1)}, bf16[2,128,512]{2,1,0:T(8,128)(2,1)S(1)}, u32[]{:S(2)}, u32[]{:S(2)}) collective-permute-start(bf16[2,128,512]{2,1,0:T(8,128)(2,1)S(1)} %get-tuple-element.55), channel_id=1, source_target_pairs={{0,5},{1,4},{2,7},{3,6},{4,1},{5,0},{6,3},{7,2},{8,13},{9,12},{10,... | collective-permute-start | bytes 786440 | tf_op jit(solution)/shard_map/ppermute | solution.py:279
  54.7 39.4 %collective-permute-start.12 = (bf16[2,128,512]{2,1,0:T(8,128)(2,1)S(1)}, bf16[2,128,512]{2,1,0:T(8,128)(2,1)S(1)}, u32[]{:S(2)}, u32[]{:S(2)}) collective-permute-start(bf16[2,128,512]{2,1,0:T(8,128)(2,1)S(1)} %get-tuple-element.56), channel_id=1, source_target_pairs={{0,6},{1,7},{2,4},{3,5},{4,2},{5,3},{6,0},{7,1},{8,14},{9,15},{10,... | collective-permute-start | bytes 786440 | tf_op jit(solution)/shard_map/ppermute | solution.py:279
  63.2 38.9 %collective-permute-start.13 = (bf16[2,128,512]{2,1,0:T(8,128)(2,1)S(1)}, bf16[2,128,512]{2,1,0:T(8,128)(2,1)S(1)}, u32[]{:S(2)}, u32[]{:S(2)}) collective-permute-start(bf16[2,128,512]{2,1,0:T(8,128)(2,1)S(1)} %get-tuple-element.57), channel_id=1, source_target_pairs={{0,7},{1,6},{2,5},{3,4},{4,3},{5,2},{6,1},{7,0},{8,15},{9,14},{10,... | collective-permute-start | bytes 786440 | tf_op jit(solution)/shard_map/ppermute | solution.py:279
  78.1 24.0 %collective-permute-start.7 = (bf16[2,128,512]{2,1,0:T(8,128)(2,1)S(1)}, bf16[2,128,512]{2,1,0:T(8,128)(2,1)S(1)}, u32[]{:S(2)}, u32[]{:S(2)}) collective-permute-start(bf16[2,128,512]{2,1,0:T(8,128)(2,1)S(1)} %get-tuple-element.51), channel_id=1, source_target_pairs={{0,1},{1,0},{2,3},{3,2},{4,5},{5,4},{6,7},{7,6},{8,9},{9,8},{10,11... | collective-permute-start | bytes 786440 | tf_op jit(solution)/shard_map/ppermute | solution.py:279
  85.9 17.9 %collective-permute-start.8 = (bf16[2,128,512]{2,1,0:T(8,128)(2,1)S(1)}, bf16[2,128,512]{2,1,0:T(8,128)(2,1)S(1)}, u32[]{:S(2)}, u32[]{:S(2)}) collective-permute-start(bf16[2,128,512]{2,1,0:T(8,128)(2,1)S(1)} %get-tuple-element.52), channel_id=1, source_target_pairs={{0,2},{1,3},{2,0},{3,1},{4,6},{5,7},{6,4},{7,5},{8,10},{9,11},{10,... | collective-permute-start | bytes 786440 | tf_op jit(solution)/shard_map/ppermute | solution.py:279
  88.5 17.3 %collective-permute-start.9 = (bf16[2,128,512]{2,1,0:T(8,128)(2,1)S(1)}, bf16[2,128,512]{2,1,0:T(8,128)(2,1)S(1)}, u32[]{:S(2)}, u32[]{:S(2)}) collective-permute-start(bf16[2,128,512]{2,1,0:T(8,128)(2,1)S(1)} %get-tuple-element.53), channel_id=1, source_target_pairs={{0,3},{1,2},{2,1},{3,0},{4,7},{5,6},{6,5},{7,4},{8,11},{9,10},{10,... | collective-permute-start | bytes 786440 | tf_op jit(solution)/shard_map/ppermute | solution.py:279
  94.1 17.3 %collective-permute-start.21 = (bf16[2,128,512]{2,1,0:T(8,128)(2,1)S(1)}, bf16[2,128,512]{2,1,0:T(8,128)(2,1)S(1)}, u32[]{:S(2)}, u32[]{:S(2)}) collective-permute-start(bf16[2,128,512]{2,1,0:T(8,128)(2,1)S(1)} %get-tuple-element.66), channel_id=1, source_target_pairs={{0,1},{1,0},{2,3},{3,2},{4,5},{5,4},{6,7},{7,6},{8,9},{9,8},{10,11... | collective-permute-start | bytes 786440 | tf_op jit(solution)/shard_map/ppermute | solution.py:279
  102.1 11.7 %collective-permute-start.22 = (bf16[2,128,512]{2,1,0:T(8,128)(2,1)S(1)}, bf16[2,128,512]{2,1,0:T(8,128)(2,1)S(1)}, u32[]{:S(2)}, u32[]{:S(2)}) collective-permute-start(bf16[2,128,512]{2,1,0:T(8,128)(2,1)S(1)} %get-tuple-element.67), channel_id=1, source_target_pairs={{0,2},{1,3},{2,0},{3,1},{4,6},{5,7},{6,4},{7,5},{8,10},{9,11},{10,... | collective-permute-start | bytes 786440 | tf_op jit(solution)/shard_map/ppermute | solution.py:279
  102.1 20.2 %collective-permute-start.23 = (bf16[2,128,512]{2,1,0:T(8,128)(2,1)S(1)}, bf16[2,128,512]{2,1,0:T(8,128)(2,1)S(1)}, u32[]{:S(2)}, u32[]{:S(2)}) collective-permute-start(bf16[2,128,512]{2,1,0:T(8,128)(2,1)S(1)} %get-tuple-element.68), channel_id=1, source_target_pairs={{0,3},{1,2},{2,1},{3,0},{4,7},{5,6},{6,5},{7,4},{8,11},{9,10},{10,... | collective-permute-start | bytes 786440 | tf_op jit(solution)/shard_map/ppermute | solution.py:279
  103.9 19.8 %collective-permute-start.24 = (bf16[2,128,512]{2,1,0:T(8,128)(2,1)S(1)}, bf16[2,128,512]{2,1,0:T(8,128)(2,1)S(1)}, u32[]{:S(2)}, u32[]{:S(2)}) collective-permute-start(bf16[2,128,512]{2,1,0:T(8,128)(2,1)S(1)} %get-tuple-element.69), channel_id=1, source_target_pairs={{0,4},{1,5},{2,6},{3,7},{4,0},{5,1},{6,2},{7,3},{8,12},{9,13},{10,... | collective-permute-start | bytes 786440 | tf_op jit(solution)/shard_map/ppermute | solution.py:279
  105.7 19.5 %collective-permute-start.25 = (bf16[2,128,512]{2,1,0:T(8,128)(2,1)S(1)}, bf16[2,128,512]{2,1,0:T(8,128)(2,1)S(1)}, u32[]{:S(2)}, u32[]{:S(2)}) collective-permute-start(bf16[2,128,512]{2,1,0:T(8,128)(2,1)S(1)} %get-tuple-element.70), channel_id=1, source_target_pairs={{0,5},{1,4},{2,7},{3,6},{4,1},{5,0},{6,3},{7,2},{8,13},{9,12},{10,... | collective-permute-start | bytes 786440 | tf_op jit(solution)/shard_map/ppermute | solution.py:279
  111.3 47.1 %collective-permute-start.26 = (bf16[2,128,512]{2,1,0:T(8,128)(2,1)S(1)}, bf16[2,128,512]{2,1,0:T(8,128)(2,1)S(1)}, u32[]{:S(2)}, u32[]{:S(2)}) collective-permute-start(bf16[2,128,512]{2,1,0:T(8,128)(2,1)S(1)} %get-tuple-element.71), channel_id=1, source_target_pairs={{0,6},{1,7},{2,4},{3,5},{4,2},{5,3},{6,0},{7,1},{8,14},{9,15},{10,... | collective-permute-start | bytes 786440 | tf_op jit(solution)/shard_map/ppermute | solution.py:279
  113.8 51.9 %collective-permute-start.27 = (bf16[2,128,512]{2,1,0:T(8,128)(2,1)S(1)}, bf16[2,128,512]{2,1,0:T(8,128)(2,1)S(1)}, u32[]{:S(2)}, u32[]{:S(2)}) collective-permute-start(bf16[2,128,512]{2,1,0:T(8,128)(2,1)S(1)} %get-tuple-element.72), channel_id=1, source_target_pairs={{0,7},{1,6},{2,5},{3,4},{4,3},{5,2},{6,1},{7,0},{8,15},{9,14},{10,... | collective-permute-start | bytes 786440 | tf_op jit(solution)/shard_map/ppermute | solution.py:279
  114.2 52.6 %copy-start.16 = (f32[128,4,512]{2,1,0:T(4,128)S(1)}, f32[128,4,512]{2,1,0:T(4,128)}, u32[]{:S(2)}) copy-start(f32[128,4,512]{2,1,0:T(4,128)} %param.9) | copy-start | bytes 3145732
  122.3 60.4 %copy-start.3 = (bf16[2,128,512]{2,1,0:T(8,128)(2,1)}, bf16[2,128,512]{2,1,0:T(8,128)(2,1)S(1)}, u32[]{:S(2)}) copy-start(bf16[2,128,512]{2,1,0:T(8,128)(2,1)S(1)} %get-tuple-element.62.refs_0_.refs_4_) | copy-start | bytes 786436
  122.3 60.5 %copy-start.15 = (bf16[2,128,512]{2,1,0:T(8,128)(2,1)}, bf16[2,128,512]{2,1,0:T(8,128)(2,1)S(1)}, u32[]{:S(2)}) copy-start(bf16[2,128,512]{2,1,0:T(8,128)(2,1)S(1)} %get-tuple-element.65) | copy-start | bytes 786436
  122.3 53.0 %collective-permute-start.14 = (bf16[2,128,512]{2,1,0:T(8,128)(2,1)S(1)}, bf16[2,128,512]{2,1,0:T(8,128)(2,1)S(1)}, u32[]{:S(2)}, u32[]{:S(2)}) collective-permute-start(bf16[2,128,512]{2,1,0:T(8,128)(2,1)S(1)} %get-tuple-element.58), channel_id=1, source_target_pairs={{0,4},{1,5},{2,6},{3,7},{4,0},{5,1},{6,2},{7,3},{8,12},{9,13},{10,... | collective-permute-start | bytes 786440 | tf_op jit(solution)/shard_map/ppermute | solution.py:279
  123.6 59.1 %collective-permute-start.15 = (bf16[2,128,512]{2,1,0:T(8,128)(2,1)S(1)}, bf16[2,128,512]{2,1,0:T(8,128)(2,1)S(1)}, u32[]{:S(2)}, u32[]{:S(2)}) collective-permute-start(bf16[2,128,512]{2,1,0:T(8,128)(2,1)S(1)} %get-tuple-element.59), channel_id=1, source_target_pairs={{0,5},{1,4},{2,7},{3,6},{4,1},{5,0},{6,3},{7,2},{8,13},{9,12},{10,... | collective-permute-start | bytes 786440 | tf_op jit(solution)/shard_map/ppermute | solution.py:279
  125.3 69.3 %collective-permute-start.16 = (bf16[2,128,512]{2,1,0:T(8,128)(2,1)S(1)}, bf16[2,128,512]{2,1,0:T(8,128)(2,1)S(1)}, u32[]{:S(2)}, u32[]{:S(2)}) collective-permute-start(bf16[2,128,512]{2,1,0:T(8,128)(2,1)S(1)} %get-tuple-element.60), channel_id=1, source_target_pairs={{0,6},{1,7},{2,4},{3,5},{4,2},{5,3},{6,0},{7,1},{8,14},{9,15},{10,... | collective-permute-start | bytes 786440 | tf_op jit(solution)/shard_map/ppermute | solution.py:279
  158.5 40.5 %collective-permute-start.17 = (bf16[2,128,512]{2,1,0:T(8,128)(2,1)S(1)}, bf16[2,128,512]{2,1,0:T(8,128)(2,1)S(1)}, u32[]{:S(2)}, u32[]{:S(2)}) collective-permute-start(bf16[2,128,512]{2,1,0:T(8,128)(2,1)S(1)} %get-tuple-element.61), channel_id=1, source_target_pairs={{0,7},{1,6},{2,5},{3,4},{4,3},{5,2},{6,1},{7,0},{8,15},{9,14},{10,... | collective-permute-start | bytes 786440 | tf_op jit(solution)/shard_map/ppermute | solution.py:279
  165.7 35.9 %collective-permute-start.18 = (bf16[2,128,512]{2,1,0:T(8,128)(2,1)S(1)}, bf16[2,128,512]{2,1,0:T(8,128)(2,1)S(1)}, u32[]{:S(2)}, u32[]{:S(2)}) collective-permute-start(bf16[2,128,512]{2,1,0:T(8,128)(2,1)S(1)} %get-tuple-element.63), channel_id=1, source_target_pairs={{0,1},{1,0},{2,3},{3,2},{4,5},{5,4},{6,7},{7,6},{8,9},{9,8},{10,11... | collective-permute-start | bytes 786440 | tf_op jit(solution)/shard_map/ppermute | solution.py:279
  171.5 32.8 %copy-start.17 = (f32[16,4]{0,1:T(4,128)S(1)}, f32[16,4]{0,1:T(4,128)}, u32[]{:S(2)}) copy-start(f32[16,4]{0,1:T(4,128)} %param.10) | copy-start | bytes 772
  171.5 44.5 %copy-start.2 = (f32[128,512]{1,0:T(8,128)S(1)}, f32[128,512]{1,0:T(8,128)}, u32[]{:S(2)}) copy-start(f32[128,512]{1,0:T(8,128)} %weight_ref.1) | copy-start | bytes 786436
  175.3 0.7 copy-start.5
  176.0 28.3 %collective-permute-start.19 = (bf16[2,128,512]{2,1,0:T(8,128)(2,1)}, bf16[2,128,512]{2,1,0:T(8,128)(2,1)}, u32[]{:S(2)}, u32[]{:S(2)}) collective-permute-start(bf16[2,128,512]{2,1,0:T(8,128)(2,1)} %get-tuple-element.64), channel_id=1, source_target_pairs={{0,2},{1,3},{2,0},{3,1},{4,6},{5,7},{6,4},{7,5},{8,10},{9,11},{10,... | collective-permute-start | bytes 786440 | tf_op jit(solution)/shard_map/ppermute | solution.py:279
  183.5 28.8 %collective-permute-start.28 = (bf16[2,2,128,512]{3,2,1,0:T(8,128)(2,1)S(1)}, bf16[2,2,128,512]{3,2,1,0:T(8,128)(2,1)S(1)}, u32[]{:S(2)}, u32[]{:S(2)}) collective-permute-start(bf16[2,2,128,512]{3,2,1,0:T(8,128)(2,1)S(1)} %get-tuple-element.73.refs_12_), channel_id=1, source_target_pairs={{0,8},{8,16},{16,24},{1,9},{9,17},{17,25},{2,10},{10,18},{18,26},{... | collective-permute-start | bytes 1572872 | tf_op jit(solution)/shard_map/ppermute | solution.py:286
  194.6 0.7 copy-start.9
  195.3 16.9 %collective-permute-start.29 = (bf16[2,2,128,512]{3,2,1,0:T(8,128)(2,1)S(1)}, bf16[2,2,128,512]{3,2,1,0:T(8,128)(2,1)S(1)}, u32[]{:S(2)}, u32[]{:S(2)}) collective-permute-start(bf16[2,2,128,512]{3,2,1,0:T(8,128)(2,1)S(1)} %get-tuple-element.74.refs_13_), channel_id=1, source_target_pairs={{0,8},{8,16},{16,24},{1,9},{9,17},{17,25},{2,10},{10,18},{18,26},{... | collective-permute-start | bytes 1572872 | tf_op jit(solution)/shard_map/ppermute | solution.py:286
  199.0 0.7 copy-start.11
  199.7 12.6 %collective-permute-start.30 = (bf16[2,2,128,512]{3,2,1,0:T(8,128)(2,1)S(1)}, bf16[2,2,128,512]{3,2,1,0:T(8,128)(2,1)}, u32[]{:S(2)}, u32[]{:S(2)}) collective-permute-start(bf16[2,2,128,512]{3,2,1,0:T(8,128)(2,1)S(1)} %get-tuple-element.75.refs_10_), channel_id=1, source_target_pairs={{8,0},{16,8},{24,16},{9,1},{17,9},{25,17},{10,2},{18,10},{26,18},{... | collective-permute-start | bytes 1572872 | tf_op jit(solution)/shard_map/ppermute | solution.py:286
  202.3 13.6 %collective-permute-start.31 = (bf16[2,2,128,512]{3,2,1,0:T(8,128)(2,1)S(1)}, bf16[2,2,128,512]{3,2,1,0:T(8,128)(2,1)}, u32[]{:S(2)}, u32[]{:S(2)}) collective-permute-start(bf16[2,2,128,512]{3,2,1,0:T(8,128)(2,1)S(1)} %get-tuple-element.76.refs_11_), channel_id=1, source_target_pairs={{8,0},{16,8},{24,16},{9,1},{17,9},{25,17},{10,2},{18,10},{26,18},{... | collective-permute-start | bytes 1572872 | tf_op jit(solution)/shard_map/ppermute | solution.py:286
  204.3 8.0 %collective-permute-start.20 = (bf16[2,128,512]{2,1,0:T(8,128)(2,1)}, bf16[2,128,512]{2,1,0:T(8,128)(2,1)}, u32[]{:S(2)}, u32[]{:S(2)}) collective-permute-start(bf16[2,128,512]{2,1,0:T(8,128)(2,1)} %copy-done.15), channel_id=1, source_target_pairs={{0,3},{1,2},{2,1},{3,0},{4,7},{5,6},{6,5},{7,4},{8,11},{9,10},{10,... | collective-permute-start | bytes 786440 | tf_op jit(solution)/shard_map/ppermute | solution.py:279
  215.9 1.0 copy-start.4
  216.9 0.9 copy-start.6
  217.8 0.9 copy-start.8
  218.8 0.9 copy-start.10
  219.7 0.9 copy-start.12
  220.7 0.9 copy-start.14
  (2 other events, 1.4 us)

commit v5 on v4

--- a/solution.py
+++ b/solution.py
@@ -9,7 +9,7 @@
 
 LANES = 128
 PIECES = 2
-LIMIT = 48 * 1024 * 1024
+LIMIT = 20 * 1024 * 1024
 SMEM = pl.BlockSpec(memory_space=pltpu.SMEM)
 AFTER = pl.BlockSpec(memory_space=pl.ANY)
 
@@ -60,7 +60,7 @@
             out[n] = slabs[me ^ s]
 
 
-def right_call(after, me, second, view, chosen, ranks, states, piece):
+def right_call(after, me, second, view, chosen, ranks, states, piece, limit):
     rows, _, _, group, _ = view.shape
     width = second.shape[1]
     block = rows // 2
@@ -79,7 +79,7 @@
         scratch_shapes=[
             pltpu.VMEM((ranks, block, 2 * piece), jnp.bfloat16),
         ],
-        compiler_params=params(),
+        compiler_params=params(limit),
         cost_estimate=cost(
             8 * kinds * states * rows * width * width, 8 * kinds * states * rows * width
         ),
@@ -302,8 +302,9 @@
 
     last = me
     lines = []
-    for chosen in chunks:
-        half = right_call([last], me, second, view, chosen, ranks, states, piece)
+    for n, chosen in enumerate(chunks):
+        limit = LIMIT if n else 2 * LIMIT + LIMIT // 2
+        half = right_call([last], me, second, view, chosen, ranks, states, piece, limit)
         last = half[0]
         lines.append(exchanged(half, "rad"))
     backs = []

time: 232 us -> 231 us (level)
  Pallas kernels: 37.4 us -> 32.7 us
  starting transfers between devices: 66 us -> 68.9 us
    pallas_call x2, Pallas kernels: 15.4 us -> 11.7 us  [left_call(): pl.pallas_call(functools.partial(left_kernel, len(after), ranks), grid=(k...]
    ppermute x28, starting transfers between devices: 47.5 us -> 50.8 us  [exchanged(): result[s] = lax.ppermute(slabs[s], axis, [(i, i ^ s) for i in range(count)])]
    unnamed x38 -> x42, local copies, waits for them, and re-layouts: 10.6 us -> 12.8 us
  transfers between devices with their start and end apart: 32 -> 32, of which waited for: 15 -> 15; matrix products, arithmetic and copies ran while one was open for 5% -> 5% of each run, Pallas kernels for 10% -> 8%
where the time goes in v5:
time: 231 us
  waiting for transfers between devices  106 us (46%)
  starting transfers between devices  68.9 us (30%)
  Pallas kernels  32.7 us (14%)
  local copies, waits for them, and re-layouts  23.2 us (10%)
    ppermute x28, waiting for transfers between devices, exchanged(): result[s] = lax.ppermute(slabs[s], axis, [(i, i ^ s) for i in range(count)])  102 us
    ppermute x28, starting transfers between devices, exchanged(): result[s] = lax.ppermute(slabs[s], axis, [(i, i ^ s) for i in range(count)])  50.8 us
    ppermute x4, starting transfers between devices, neighbour(): return lax.ppermute(edge, axis, pairs)  18.2 us
    unnamed x42, local copies, waits for them, and re-layouts  12.8 us
    pallas_call x2, Pallas kernels, left_call(): pl.pallas_call(functools.partial(left_kernel, len(after), ranks), grid=(k...  11.7 us
    pallas_call x1, Pallas kernels, mix_call(): pl.pallas_call(functools.partial(mix_kernel, tuple(chosen), order), grid=...  8.82 us
    pallas_call x2, Pallas kernels, right_call(): pl.pallas_call(functools.partial(right_kernel, len(after), ranks, states)...  8.11 us
    reshape x1, local copies, waits for them, and re-layouts, per_device(): first = first_propagator.reshape(2 * whole, whole).T  6.51 us
  transfers between devices with their start and end apart: 32, of which 15 were waited for; matrix products, arithmetic and copies ran while one was open for 5% of the time, Pallas kernels for 8%

profile of v5, /device:TPU:9, one launch (start us, length us, event | category | flops | bytes accessed | tf_op | source)
XLA Modules:
  0.0 230.8 jit_solution(12500372389849345336)
XLA Ops:
  0.0 1.2 copy-done.1
  1.2 4.8 %right.2 = (bf16[2,128,512]{2,1,0:T(8,128)(2,1)S(1)}, bf16[2,128,512]{2,1,0:T(8,128)(2,1)S(1)}, bf16[2,128,512]{2,1,0:T(8,128)(2,1)S(1)}, bf16[2,128,512]{2,1,0:...) custom-call(s32[1]{0:T(128)} %bitcast.me_ref.refs_0_, ...), custom_call_target="tpu_custom_call" | custom-call | flops 2147483648 | bytes 4194304 | tf_op jit(solution)/shard_map/right/pallas_call | solution.py:68
  6.1 1.2 collective-permute-start
  7.5 1.2 collective-permute-start.2
  8.7 2.3 %collective-permute-start.3 = (bf16[2,128,512]{2,1,0:T(8,128)(2,1)}, bf16[2,128,512]{2,1,0:T(8,128)(2,1)S(1)}, u32[]{:S(2)}, u32[]{:S(2)}) collective-permute-start(bf16[2,128,512]{2,1,0:T(8,128)(2,1)} %get-tuple-element.46), channel_id=1, source_target_pairs={{0,4},{1,5},{2,6},{3,7},{4,0},{5,1},{6,2},{7,3},{8,12},{9,13},{10,... | collective-permute-start | bytes 786440 | tf_op jit(solution)/shard_map/ppermute | solution.py:279
  11.0 1.0 collective-permute-start.4
  12.0 1.2 collective-permute-done.refs_2_
  13.2 1.3 collective-permute-start.5
  14.6 7.3 %collective-permute-done.1.refs_3_ = bf16[2,128,512]{2,1,0:T(8,128)(2,1)S(1)} collective-permute-done((bf16[2,128,512]{2,1,0:T(8,128)(2,1)S(1)}, bf16[2,128,512]{2,1,0:T(8,128)(2,1)S(1)}, u32[]{:S(2)}, u32[]{:S(2)}) %collective-permute-start.1) | collective-permute-done | bytes 262176 | tf_op jit(solution)/shard_map/ppermute | solution.py:279
  21.9 6.5 %copy.14 = bf16[2048,1024]{0,1:T(8,128)(2,1)} copy(bf16[2048,1024]{1,0:T(8,128)(2,1)} %bitcast.29) | data formatting | bytes 8388608 | tf_op jit(solution)/shard_map/reshape | solution.py:297
  28.4 2.2 copy-done
  30.6 3.3 %right.3 = (bf16[2,128,512]{2,1,0:T(8,128)(2,1)S(1)}, bf16[2,128,512]{2,1,0:T(8,128)(2,1)S(1)}, bf16[2,128,512]{2,1,0:T(8,128)(2,1)S(1)}, bf16[2,128,512]{2,1,0:...) custom-call(s32[1]{0:T(128)} %bitcast.me_ref.refs_0_, ...), custom_call_target="tpu_custom_call" | custom-call | flops 2147483648 | bytes 4194304 | tf_op jit(solution)/shard_map/right/pallas_call | solution.py:68
  33.9 3.6 %collective-permute-start.10 = (bf16[2,128,512]{2,1,0:T(8,128)(2,1)S(1)}, bf16[2,128,512]{2,1,0:T(8,128)(2,1)S(1)}, u32[]{:S(2)}, u32[]{:S(2)}) collective-permute-start(bf16[2,128,512]{2,1,0:T(8,128)(2,1)S(1)} %get-tuple-element.54), channel_id=1, source_target_pairs={{0,4},{1,5},{2,6},{3,7},{4,0},{5,1},{6,2},{7,3},{8,12},{9,13},{10,... | collective-permute-start | bytes 786440 | tf_op jit(solution)/shard_map/ppermute | solution.py:279
  37.5 2.0 collective-permute-start.11
  39.5 15.2 %collective-permute-done.4.refs_6_ = bf16[2,128,512]{2,1,0:T(8,128)(2,1)S(1)} collective-permute-done((bf16[2,128,512]{2,1,0:T(8,128)(2,1)}, bf16[2,128,512]{2,1,0:T(8,128)(2,1)S(1)}, u32[]{:S(2)}, u32[]{:S(2)}) %collective-permute-start.4) | collective-permute-done | bytes 262176 | tf_op jit(solution)/shard_map/ppermute | solution.py:279
  54.7 8.4 %collective-permute-done.5.refs_7_ = bf16[2,128,512]{2,1,0:T(8,128)(2,1)S(1)} collective-permute-done((bf16[2,128,512]{2,1,0:T(8,128)(2,1)S(1)}, bf16[2,128,512]{2,1,0:T(8,128)(2,1)S(1)}, u32[]{:S(2)}, u32[]{:S(2)}) %collective-permute-start.5) | collective-permute-done | bytes 262176 | tf_op jit(solution)/shard_map/ppermute | solution.py:279
  63.2 11.6 %collective-permute-start.13 = (bf16[2,128,512]{2,1,0:T(8,128)(2,1)S(1)}, bf16[2,128,512]{2,1,0:T(8,128)(2,1)S(1)}, u32[]{:S(2)}, u32[]{:S(2)}) collective-permute-start(bf16[2,128,512]{2,1,0:T(8,128)(2,1)S(1)} %get-tuple-element.57), channel_id=1, source_target_pairs={{0,7},{1,6},{2,5},{3,4},{4,3},{5,2},{6,1},{7,0},{8,15},{9,14},{10,... | collective-permute-start | bytes 786440 | tf_op jit(solution)/shard_map/ppermute | solution.py:279
  74.7 3.3 %collective-permute-done.6.refs_8_ = bf16[2,128,512]{2,1,0:T(8,128)(2,1)} collective-permute-done((bf16[2,128,512]{2,1,0:T(8,128)(2,1)S(1)}, bf16[2,128,512]{2,1,0:T(8,128)(2,1)}, u32[]{:S(2)}, u32[]{:S(2)}) %collective-permute-start.6) | collective-permute-done | bytes 262176 | tf_op jit(solution)/shard_map/ppermute | solution.py:279
  78.5 6.0 %left.2 = (bf16[2,128,512]{2,1,0:T(8,128)(2,1)S(1)}, bf16[2,128,512]{2,1,0:T(8,128)(2,1)S(1)}, bf16[2,128,512]{2,1,0:T(8,128)(2,1)S(1)}, bf16[2,128,512]{2,1,0:T...) custom-call(s32[1]{0:T(128)} %bitcast.me_ref.refs_0_, ...), custom_call_target="tpu_custom_call" | custom-call | flops 4294967296 | bytes 8388608 | tf_op jit(solution)/shard_map/left/pallas_call | solution.py:115
  84.6 3.9 %collective-permute-done.11.refs_6_ = bf16[2,128,512]{2,1,0:T(8,128)(2,1)S(1)} collective-permute-done((bf16[2,128,512]{2,1,0:T(8,128)(2,1)S(1)}, bf16[2,128,512]{2,1,0:T(8,128)(2,1)S(1)}, u32[]{:S(2)}, u32[]{:S(2)}) %collective-permute-start.11) | collective-permute-done | bytes 262176 | tf_op jit(solution)/shard_map/ppermute | solution.py:279
  88.5 2.1 collective-permute-start.9
  90.6 3.5 %collective-permute-done.12.refs_7_ = bf16[2,128,512]{2,1,0:T(8,128)(2,1)S(1)} collective-permute-done((bf16[2,128,512]{2,1,0:T(8,128)(2,1)S(1)}, bf16[2,128,512]{2,1,0:T(8,128)(2,1)S(1)}, u32[]{:S(2)}, u32[]{:S(2)}) %collective-permute-start.12) | collective-permute-done | bytes 262176 | tf_op jit(solution)/shard_map/ppermute | solution.py:279
  94.1 1.2 collective-permute-start.21
  95.3 6.9 %collective-permute-done.13.refs_8_ = bf16[2,128,512]{2,1,0:T(8,128)(2,1)S(1)} collective-permute-done((bf16[2,128,512]{2,1,0:T(8,128)(2,1)S(1)}, bf16[2,128,512]{2,1,0:T(8,128)(2,1)S(1)}, u32[]{:S(2)}, u32[]{:S(2)}) %collective-permute-start.13) | collective-permute-done | bytes 262176 | tf_op jit(solution)/shard_map/ppermute | solution.py:279
  102.2 1.7 collective-permute-start.23
  103.9 2.1 collective-permute-start.24
  106.0 1.0 collective-permute-start.25
  107.0 4.6 %collective-permute-done.21.refs_2_ = bf16[2,128,512]{2,1,0:T(8,128)(2,1)S(1)} collective-permute-done((bf16[2,128,512]{2,1,0:T(8,128)(2,1)S(1)}, bf16[2,128,512]{2,1,0:T(8,128)(2,1)S(1)}, u32[]{:S(2)}, u32[]{:S(2)}) %collective-permute-start.21) | collective-permute-done | bytes 262176 | tf_op jit(solution)/shard_map/ppermute | solution.py:279
  111.6 2.9 %collective-permute-start.26 = (bf16[2,128,512]{2,1,0:T(8,128)(2,1)S(1)}, bf16[2,128,512]{2,1,0:T(8,128)(2,1)S(1)}, u32[]{:S(2)}, u32[]{:S(2)}) collective-permute-start(bf16[2,128,512]{2,1,0:T(8,128)(2,1)S(1)} %get-tuple-element.71), channel_id=1, source_target_pairs={{0,6},{1,7},{2,4},{3,5},{4,2},{5,3},{6,0},{7,1},{8,14},{9,15},{10,... | collective-permute-start | bytes 786440 | tf_op jit(solution)/shard_map/ppermute | solution.py:279
  114.9 5.7 %left.3 = (bf16[2,128,512]{2,1,0:T(8,128)(2,1)S(1)}, bf16[2,128,512]{2,1,0:T(8,128)(2,1)S(1)}, bf16[2,128,512]{2,1,0:T(8,128)(2,1)}, bf16[2,128,512]{2,1,0:T(8,1...) custom-call(s32[1]{0:T(128)} %bitcast.me_ref.refs_0_, ...), custom_call_target="tpu_custom_call" | custom-call | flops 4294967296 | bytes 8388608 | tf_op jit(solution)/shard_map/left/pallas_call | solution.py:115
  120.7 1.9 collective-permute-start.14
  122.5 2.2 collective-permute-start.15
  125.4 33.6 %collective-permute-done.26.refs_7_ = bf16[2,128,512]{2,1,0:T(8,128)(2,1)S(1)} collective-permute-done((bf16[2,128,512]{2,1,0:T(8,128)(2,1)S(1)}, bf16[2,128,512]{2,1,0:T(8,128)(2,1)S(1)}, u32[]{:S(2)}, u32[]{:S(2)}) %collective-permute-start.26) | collective-permute-done | bytes 262176 | tf_op jit(solution)/shard_map/ppermute | solution.py:279
  158.9 3.0 %collective-permute-start.17 = (bf16[2,128,512]{2,1,0:T(8,128)(2,1)S(1)}, bf16[2,128,512]{2,1,0:T(8,128)(2,1)S(1)}, u32[]{:S(2)}, u32[]{:S(2)}) collective-permute-start(bf16[2,128,512]{2,1,0:T(8,128)(2,1)S(1)} %get-tuple-element.61), channel_id=1, source_target_pairs={{0,7},{1,6},{2,5},{3,4},{4,3},{5,2},{6,1},{7,0},{8,15},{9,14},{10,... | collective-permute-start | bytes 786440 | tf_op jit(solution)/shard_map/ppermute | solution.py:279
  162.0 4.4 %collective-permute-done.27.refs_8_ = bf16[2,128,512]{2,1,0:T(8,128)(2,1)S(1)} collective-permute-done((bf16[2,128,512]{2,1,0:T(8,128)(2,1)S(1)}, bf16[2,128,512]{2,1,0:T(8,128)(2,1)S(1)}, u32[]{:S(2)}, u32[]{:S(2)}) %collective-permute-start.27) | collective-permute-done | bytes 262176 | tf_op jit(solution)/shard_map/ppermute | solution.py:279
  166.4 3.7 %collective-permute-start.18 = (bf16[2,128,512]{2,1,0:T(8,128)(2,1)S(1)}, bf16[2,128,512]{2,1,0:T(8,128)(2,1)S(1)}, u32[]{:S(2)}, u32[]{:S(2)}) collective-permute-start(bf16[2,128,512]{2,1,0:T(8,128)(2,1)S(1)} %get-tuple-element.63), channel_id=1, source_target_pairs={{0,1},{1,0},{2,3},{3,2},{4,5},{5,4},{6,7},{7,6},{8,9},{9,8},{10,11... | collective-permute-start | bytes 786440 | tf_op jit(solution)/shard_map/ppermute | solution.py:279
  170.1 3.7 %sine_bitcast_fusion = (f32[4,128,512]{2,1,0:T(8,128)S(1)}, f32[4,128,512]{2,1,0:T(8,128)S(1)}) fusion(f32[128,4,512]{2,1,0:T(4,128)S(1)} %copy-done.18), kind=kLoop, calls=%fused_computation | loop fusion | bytes 3145728 | tf_op jit(solution)/shard_map/sin | solution.py:317
  173.8 1.9 collective-permute-done.14.refs_0_
  176.5 2.8 %collective-permute-start.19 = (bf16[2,128,512]{2,1,0:T(8,128)(2,1)}, bf16[2,128,512]{2,1,0:T(8,128)(2,1)}, u32[]{:S(2)}, u32[]{:S(2)}) collective-permute-start(bf16[2,128,512]{2,1,0:T(8,128)(2,1)} %get-tuple-element.64), channel_id=1, source_target_pairs={{0,2},{1,3},{2,0},{3,1},{4,6},{5,7},{6,4},{7,5},{8,10},{9,11},{10,... | collective-permute-start | bytes 786440 | tf_op jit(solution)/shard_map/ppermute | solution.py:279
  179.3 4.0 %phase.1 = (bf16[2,2,128,512]{3,2,1,0:T(8,128)(2,1)}, bf16[2,2,128,512]{3,2,1,0:T(8,128)(2,1)}, bf16[2,2,128,512]{3,2,1,0:T(8,128)(2,1)}, bf16[2,2,128,512]{3,2,1,0:T(8,128)(2,1)}) custom-call(s32[1]{0:T(128)} %bitcast.me_ref.refs_0_, bf16[1024,512]{1,0:T(8,128)(2,1)S(1)} %bitcast.25, f32[4,128,512]{2,1,0:T(8,128)S(1)} %get-tuple-element.78.cosine_ref, ...), custom_call_target="tpu_custom_call" | custom-call | flops 2147483648 | bytes 4194304 | tf_op jit(solution)/shard_map/phase/pallas_call | solution.py:185
  184.0 10.5 %collective-permute-start.28 = (bf16[2,2,128,512]{3,2,1,0:T(8,128)(2,1)}, bf16[2,2,128,512]{3,2,1,0:T(8,128)(2,1)}, u32[]{:S(2)}, u32[]{:S(2)}) collective-permute-start(bf16[2,2,128,512]{3,2,1,0:T(8,128)(2,1)} %get-tuple-element.73.refs_12_), channel_id=1, source_target_pairs={{0,8},{8,16},{16,24},{1,9},{9,17},{17,25},{2,10},{10,18},{18,26},{... | collective-permute-start | bytes 1572872 | tf_op jit(solution)/shard_map/ppermute | solution.py:286
  195.3 3.8 %collective-permute-start.29 = (bf16[2,2,128,512]{3,2,1,0:T(8,128)(2,1)}, bf16[2,2,128,512]{3,2,1,0:T(8,128)(2,1)}, u32[]{:S(2)}, u32[]{:S(2)}) collective-permute-start(bf16[2,2,128,512]{3,2,1,0:T(8,128)(2,1)} %get-tuple-element.74.refs_13_), channel_id=1, source_target_pairs={{0,8},{8,16},{16,24},{1,9},{9,17},{17,25},{2,10},{10,18},{18,26},{... | collective-permute-start | bytes 1572872 | tf_op jit(solution)/shard_map/ppermute | solution.py:286
  199.8 1.9 collective-permute-start.30
  202.5 1.9 collective-permute-start.31
  205.7 6.8 %collective-permute-done.20.refs_7_ = bf16[2,128,512]{2,1,0:T(8,128)(2,1)} collective-permute-done((bf16[2,128,512]{2,1,0:T(8,128)(2,1)}, bf16[2,128,512]{2,1,0:T(8,128)(2,1)}, u32[]{:S(2)}, u32[]{:S(2)}) %collective-permute-start.20) | collective-permute-done | bytes 262176 | tf_op jit(solution)/shard_map/ppermute | solution.py:279
  212.5 3.8 %collective-permute-done.31.refs_15_ = bf16[2,2,128,512]{3,2,1,0:T(8,128)(2,1)} collective-permute-done((bf16[2,2,128,512]{3,2,1,0:T(8,128)(2,1)}, bf16[2,2,128,512]{3,2,1,0:T(8,128)(2,1)}, u32[]{:S(2)}, u32[]{:S(2)}) %collective-permute-start.31) | collective-permute-done | bytes 524320 | tf_op jit(solution)/shard_map/ppermute | solution.py:286
  216.3 0.9 copy-done.6
  222.0 8.8 %mix.1 = bf16[128,2,4,16,128]{4,3,2,1,0:T(8,128)(2,1)} custom-call(s32[1]{0:T(128)} %bitcast.me_ref.refs_0_, f32[4,4]{1,0:T(4,128)S(1)} %get-tuple-element.80.up_ref, f32[4,4]{1,0:T(4,128)S(1)} %get-tuple-element.79.down_ref, bf16[1024,512]{1,0:T(8,128)(2,1)S(1)} %bitcast.26, f32[4,128,512]{2,1,0:T(8,128)S(1)} %get-tuple-element.78.cosine_ref, ...), custom_call_target="tpu_custom_call" | custom-call | flops 2147483648 | bytes 10485760 | tf_op jit(solution)/shard_map/mix/pallas_call | solution.py:253
  (70 shorter events, 11.4 us)
Async XLA Ops:
  0.0 1.2 copy-start.1
  6.1 7.2 %collective-permute-start = (bf16[2,128,512]{2,1,0:T(8,128)(2,1)S(1)}, bf16[2,128,512]{2,1,0:T(8,128)(2,1)S(1)}, u32[]{:S(2)}, u32[]{:S(2)}) collective-permute-start(bf16[2,128,512]{2,1,0:T(8,128)(2,1)S(1)} %get-tuple-element.43), channel_id=1, source_target_pairs={{0,1},{1,0},{2,3},{3,2},{4,5},{5,4},{6,7},{7,6},{8,9},{9,8},{10,11... | collective-permute-start | bytes 786440 | tf_op jit(solution)/shard_map/ppermute | solution.py:279
  7.3 14.6 %collective-permute-start.1 = (bf16[2,128,512]{2,1,0:T(8,128)(2,1)S(1)}, bf16[2,128,512]{2,1,0:T(8,128)(2,1)S(1)}, u32[]{:S(2)}, u32[]{:S(2)}) collective-permute-start(bf16[2,128,512]{2,1,0:T(8,128)(2,1)S(1)} %get-tuple-element.44), channel_id=1, source_target_pairs={{0,2},{1,3},{2,0},{3,1},{4,6},{5,7},{6,4},{7,5},{8,10},{9,11},{10,... | collective-permute-start | bytes 786440 | tf_op jit(solution)/shard_map/ppermute | solution.py:279
  7.5 26.4 %collective-permute-start.2 = (bf16[2,128,512]{2,1,0:T(8,128)(2,1)}, bf16[2,128,512]{2,1,0:T(8,128)(2,1)S(1)}, u32[]{:S(2)}, u32[]{:S(2)}) collective-permute-start(bf16[2,128,512]{2,1,0:T(8,128)(2,1)} %get-tuple-element.45), channel_id=1, source_target_pairs={{0,3},{1,2},{2,1},{3,0},{4,7},{5,6},{6,5},{7,4},{8,11},{9,10},{10,... | collective-permute-start | bytes 786440 | tf_op jit(solution)/shard_map/ppermute | solution.py:279
  8.7 28.8 %collective-permute-start.3 = (bf16[2,128,512]{2,1,0:T(8,128)(2,1)}, bf16[2,128,512]{2,1,0:T(8,128)(2,1)S(1)}, u32[]{:S(2)}, u32[]{:S(2)}) collective-permute-start(bf16[2,128,512]{2,1,0:T(8,128)(2,1)} %get-tuple-element.46), channel_id=1, source_target_pairs={{0,4},{1,5},{2,6},{3,7},{4,0},{5,1},{6,2},{7,3},{8,12},{9,13},{10,... | collective-permute-start | bytes 786440 | tf_op jit(solution)/shard_map/ppermute | solution.py:279
  11.0 43.7 %collective-permute-start.4 = (bf16[2,128,512]{2,1,0:T(8,128)(2,1)}, bf16[2,128,512]{2,1,0:T(8,128)(2,1)S(1)}, u32[]{:S(2)}, u32[]{:S(2)}) collective-permute-start(bf16[2,128,512]{2,1,0:T(8,128)(2,1)} %get-tuple-element.47), channel_id=1, source_target_pairs={{0,5},{1,4},{2,7},{3,6},{4,1},{5,0},{6,3},{7,2},{8,13},{9,12},{10,... | collective-permute-start | bytes 786440 | tf_op jit(solution)/shard_map/ppermute | solution.py:279
  13.2 49.9 %collective-permute-start.5 = (bf16[2,128,512]{2,1,0:T(8,128)(2,1)S(1)}, bf16[2,128,512]{2,1,0:T(8,128)(2,1)S(1)}, u32[]{:S(2)}, u32[]{:S(2)}) collective-permute-start(bf16[2,128,512]{2,1,0:T(8,128)(2,1)S(1)} %get-tuple-element.48), channel_id=1, source_target_pairs={{0,6},{1,7},{2,4},{3,5},{4,2},{5,3},{6,0},{7,1},{8,14},{9,15},{10,... | collective-permute-start | bytes 786440 | tf_op jit(solution)/shard_map/ppermute | solution.py:279
  21.9 56.2 %collective-permute-start.6 = (bf16[2,128,512]{2,1,0:T(8,128)(2,1)S(1)}, bf16[2,128,512]{2,1,0:T(8,128)(2,1)}, u32[]{:S(2)}, u32[]{:S(2)}) collective-permute-start(bf16[2,128,512]{2,1,0:T(8,128)(2,1)S(1)} %get-tuple-element.49), channel_id=1, source_target_pairs={{0,7},{1,6},{2,5},{3,4},{4,3},{5,2},{6,1},{7,0},{8,15},{9,14},{10,... | collective-permute-start | bytes 786440 | tf_op jit(solution)/shard_map/ppermute | solution.py:279
  21.9 6.5 %copy-start.2 = (bf16[2,512,512]{2,1,0:T(8,128)(2,1)S(1)}, bf16[2,512,512]{2,1,0:T(8,128)(2,1)}, u32[]{:S(2)}) copy-start(bf16[2,512,512]{2,1,0:T(8,128)(2,1)} %param.8) | copy-start | bytes 3145732
  28.4 2.2 copy-start
  30.6 47.9 %copy-start.3 = (bf16[2048,1024]{0,1:T(8,128)(2,1)S(1)}, bf16[2048,1024]{0,1:T(8,128)(2,1)}, u32[]{:S(2)}) copy-start(bf16[2048,1024]{0,1:T(8,128)(2,1)} %copy.14) | copy-start | bytes 12582916
  33.9 50.6 %collective-permute-start.10 = (bf16[2,128,512]{2,1,0:T(8,128)(2,1)S(1)}, bf16[2,128,512]{2,1,0:T(8,128)(2,1)S(1)}, u32[]{:S(2)}, u32[]{:S(2)}) collective-permute-start(bf16[2,128,512]{2,1,0:T(8,128)(2,1)S(1)} %get-tuple-element.54), channel_id=1, source_target_pairs={{0,4},{1,5},{2,6},{3,7},{4,0},{5,1},{6,2},{7,3},{8,12},{9,13},{10,... | collective-permute-start | bytes 786440 | tf_op jit(solution)/shard_map/ppermute | solution.py:279
  37.5 51.0 %collective-permute-start.11 = (bf16[2,128,512]{2,1,0:T(8,128)(2,1)S(1)}, bf16[2,128,512]{2,1,0:T(8,128)(2,1)S(1)}, u32[]{:S(2)}, u32[]{:S(2)}) collective-permute-start(bf16[2,128,512]{2,1,0:T(8,128)(2,1)S(1)} %get-tuple-element.55), channel_id=1, source_target_pairs={{0,5},{1,4},{2,7},{3,6},{4,1},{5,0},{6,3},{7,2},{8,13},{9,12},{10,... | collective-permute-start | bytes 786440 | tf_op jit(solution)/shard_map/ppermute | solution.py:279
  54.7 39.4 %collective-permute-start.12 = (bf16[2,128,512]{2,1,0:T(8,128)(2,1)S(1)}, bf16[2,128,512]{2,1,0:T(8,128)(2,1)S(1)}, u32[]{:S(2)}, u32[]{:S(2)}) collective-permute-start(bf16[2,128,512]{2,1,0:T(8,128)(2,1)S(1)} %get-tuple-element.56), channel_id=1, source_target_pairs={{0,6},{1,7},{2,4},{3,5},{4,2},{5,3},{6,0},{7,1},{8,14},{9,15},{10,... | collective-permute-start | bytes 786440 | tf_op jit(solution)/shard_map/ppermute | solution.py:279
  63.2 39.0 %collective-permute-start.13 = (bf16[2,128,512]{2,1,0:T(8,128)(2,1)S(1)}, bf16[2,128,512]{2,1,0:T(8,128)(2,1)S(1)}, u32[]{:S(2)}, u32[]{:S(2)}) collective-permute-start(bf16[2,128,512]{2,1,0:T(8,128)(2,1)S(1)} %get-tuple-element.57), channel_id=1, source_target_pairs={{0,7},{1,6},{2,5},{3,4},{4,3},{5,2},{6,1},{7,0},{8,15},{9,14},{10,... | collective-permute-start | bytes 786440 | tf_op jit(solution)/shard_map/ppermute | solution.py:279
  78.1 24.1 %collective-permute-start.7 = (bf16[2,128,512]{2,1,0:T(8,128)(2,1)S(1)}, bf16[2,128,512]{2,1,0:T(8,128)(2,1)S(1)}, u32[]{:S(2)}, u32[]{:S(2)}) collective-permute-start(bf16[2,128,512]{2,1,0:T(8,128)(2,1)S(1)} %get-tuple-element.51), channel_id=1, source_target_pairs={{0,1},{1,0},{2,3},{3,2},{4,5},{5,4},{6,7},{7,6},{8,9},{9,8},{10,11... | collective-permute-start | bytes 786440 | tf_op jit(solution)/shard_map/ppermute | solution.py:279
  84.5 19.3 %collective-permute-start.8 = (bf16[2,128,512]{2,1,0:T(8,128)(2,1)S(1)}, bf16[2,128,512]{2,1,0:T(8,128)(2,1)S(1)}, u32[]{:S(2)}, u32[]{:S(2)}) collective-permute-start(bf16[2,128,512]{2,1,0:T(8,128)(2,1)S(1)} %get-tuple-element.52), channel_id=1, source_target_pairs={{0,2},{1,3},{2,0},{3,1},{4,6},{5,7},{6,4},{7,5},{8,10},{9,11},{10,... | collective-permute-start | bytes 786440 | tf_op jit(solution)/shard_map/ppermute | solution.py:279
  88.5 17.4 %collective-permute-start.9 = (bf16[2,128,512]{2,1,0:T(8,128)(2,1)S(1)}, bf16[2,128,512]{2,1,0:T(8,128)(2,1)S(1)}, u32[]{:S(2)}, u32[]{:S(2)}) collective-permute-start(bf16[2,128,512]{2,1,0:T(8,128)(2,1)S(1)} %get-tuple-element.53), channel_id=1, source_target_pairs={{0,3},{1,2},{2,1},{3,0},{4,7},{5,6},{6,5},{7,4},{8,11},{9,10},{10,... | collective-permute-start | bytes 786440 | tf_op jit(solution)/shard_map/ppermute | solution.py:279
  94.1 17.4 %collective-permute-start.21 = (bf16[2,128,512]{2,1,0:T(8,128)(2,1)S(1)}, bf16[2,128,512]{2,1,0:T(8,128)(2,1)S(1)}, u32[]{:S(2)}, u32[]{:S(2)}) collective-permute-start(bf16[2,128,512]{2,1,0:T(8,128)(2,1)S(1)} %get-tuple-element.66), channel_id=1, source_target_pairs={{0,1},{1,0},{2,3},{3,2},{4,5},{5,4},{6,7},{7,6},{8,9},{9,8},{10,11... | collective-permute-start | bytes 786440 | tf_op jit(solution)/shard_map/ppermute | solution.py:279
  102.2 12.2 %collective-permute-start.22 = (bf16[2,128,512]{2,1,0:T(8,128)(2,1)S(1)}, bf16[2,128,512]{2,1,0:T(8,128)(2,1)S(1)}, u32[]{:S(2)}, u32[]{:S(2)}) collective-permute-start(bf16[2,128,512]{2,1,0:T(8,128)(2,1)S(1)} %get-tuple-element.67), channel_id=1, source_target_pairs={{0,2},{1,3},{2,0},{3,1},{4,6},{5,7},{6,4},{7,5},{8,10},{9,11},{10,... | collective-permute-start | bytes 786440 | tf_op jit(solution)/shard_map/ppermute | solution.py:279
  102.2 18.4 %collective-permute-start.23 = (bf16[2,128,512]{2,1,0:T(8,128)(2,1)S(1)}, bf16[2,128,512]{2,1,0:T(8,128)(2,1)S(1)}, u32[]{:S(2)}, u32[]{:S(2)}) collective-permute-start(bf16[2,128,512]{2,1,0:T(8,128)(2,1)S(1)} %get-tuple-element.68), channel_id=1, source_target_pairs={{0,3},{1,2},{2,1},{3,0},{4,7},{5,6},{6,5},{7,4},{8,11},{9,10},{10,... | collective-permute-start | bytes 786440 | tf_op jit(solution)/shard_map/ppermute | solution.py:279
  103.9 18.6 %collective-permute-start.24 = (bf16[2,128,512]{2,1,0:T(8,128)(2,1)S(1)}, bf16[2,128,512]{2,1,0:T(8,128)(2,1)S(1)}, u32[]{:S(2)}, u32[]{:S(2)}) collective-permute-start(bf16[2,128,512]{2,1,0:T(8,128)(2,1)S(1)} %get-tuple-element.69), channel_id=1, source_target_pairs={{0,4},{1,5},{2,6},{3,7},{4,0},{5,1},{6,2},{7,3},{8,12},{9,13},{10,... | collective-permute-start | bytes 786440 | tf_op jit(solution)/shard_map/ppermute | solution.py:279
  106.0 19.4 %collective-permute-start.25 = (bf16[2,128,512]{2,1,0:T(8,128)(2,1)S(1)}, bf16[2,128,512]{2,1,0:T(8,128)(2,1)S(1)}, u32[]{:S(2)}, u32[]{:S(2)}) collective-permute-start(bf16[2,128,512]{2,1,0:T(8,128)(2,1)S(1)} %get-tuple-element.70), channel_id=1, source_target_pairs={{0,5},{1,4},{2,7},{3,6},{4,1},{5,0},{6,3},{7,2},{8,13},{9,12},{10,... | collective-permute-start | bytes 786440 | tf_op jit(solution)/shard_map/ppermute | solution.py:279
  111.6 47.4 %collective-permute-start.26 = (bf16[2,128,512]{2,1,0:T(8,128)(2,1)S(1)}, bf16[2,128,512]{2,1,0:T(8,128)(2,1)S(1)}, u32[]{:S(2)}, u32[]{:S(2)}) collective-permute-start(bf16[2,128,512]{2,1,0:T(8,128)(2,1)S(1)} %get-tuple-element.71), channel_id=1, source_target_pairs={{0,6},{1,7},{2,4},{3,5},{4,2},{5,3},{6,0},{7,1},{8,14},{9,15},{10,... | collective-permute-start | bytes 786440 | tf_op jit(solution)/shard_map/ppermute | solution.py:279
  114.5 52.0 %collective-permute-start.27 = (bf16[2,128,512]{2,1,0:T(8,128)(2,1)S(1)}, bf16[2,128,512]{2,1,0:T(8,128)(2,1)S(1)}, u32[]{:S(2)}, u32[]{:S(2)}) collective-permute-start(bf16[2,128,512]{2,1,0:T(8,128)(2,1)S(1)} %get-tuple-element.72), channel_id=1, source_target_pairs={{0,7},{1,6},{2,5},{3,4},{4,3},{5,2},{6,1},{7,0},{8,15},{9,14},{10,... | collective-permute-start | bytes 786440 | tf_op jit(solution)/shard_map/ppermute | solution.py:279
  114.9 55.2 %copy-start.18 = (f32[128,4,512]{2,1,0:T(4,128)S(1)}, f32[128,4,512]{2,1,0:T(4,128)}, u32[]{:S(2)}) copy-start(f32[128,4,512]{2,1,0:T(4,128)} %param.9) | copy-start | bytes 3145732
  120.6 62.7 %copy-start.5 = (bf16[2,128,512]{2,1,0:T(8,128)(2,1)}, bf16[2,128,512]{2,1,0:T(8,128)(2,1)S(1)}, u32[]{:S(2)}) copy-start(bf16[2,128,512]{2,1,0:T(8,128)(2,1)S(1)} %get-tuple-element.62.refs_0_.refs_4_) | copy-start | bytes 786436
  120.7 62.7 %copy-start.17 = (bf16[2,128,512]{2,1,0:T(8,128)(2,1)}, bf16[2,128,512]{2,1,0:T(8,128)(2,1)S(1)}, u32[]{:S(2)}) copy-start(bf16[2,128,512]{2,1,0:T(8,128)(2,1)S(1)} %get-tuple-element.65) | copy-start | bytes 786436
  120.7 55.1 %collective-permute-start.14 = (bf16[2,128,512]{2,1,0:T(8,128)(2,1)S(1)}, bf16[2,128,512]{2,1,0:T(8,128)(2,1)S(1)}, u32[]{:S(2)}, u32[]{:S(2)}) collective-permute-start(bf16[2,128,512]{2,1,0:T(8,128)(2,1)S(1)} %get-tuple-element.58), channel_id=1, source_target_pairs={{0,4},{1,5},{2,6},{3,7},{4,0},{5,1},{6,2},{7,3},{8,12},{9,13},{10,... | collective-permute-start | bytes 786440 | tf_op jit(solution)/shard_map/ppermute | solution.py:279
  122.5 60.8 %collective-permute-start.15 = (bf16[2,128,512]{2,1,0:T(8,128)(2,1)S(1)}, bf16[2,128,512]{2,1,0:T(8,128)(2,1)S(1)}, u32[]{:S(2)}, u32[]{:S(2)}) collective-permute-start(bf16[2,128,512]{2,1,0:T(8,128)(2,1)S(1)} %get-tuple-element.59), channel_id=1, source_target_pairs={{0,5},{1,4},{2,7},{3,6},{4,1},{5,0},{6,3},{7,2},{8,13},{9,12},{10,... | collective-permute-start | bytes 786440 | tf_op jit(solution)/shard_map/ppermute | solution.py:279
  125.4 69.2 %collective-permute-start.16 = (bf16[2,128,512]{2,1,0:T(8,128)(2,1)S(1)}, bf16[2,128,512]{2,1,0:T(8,128)(2,1)S(1)}, u32[]{:S(2)}, u32[]{:S(2)}) collective-permute-start(bf16[2,128,512]{2,1,0:T(8,128)(2,1)S(1)} %get-tuple-element.60), channel_id=1, source_target_pairs={{0,6},{1,7},{2,4},{3,5},{4,2},{5,3},{6,0},{7,1},{8,14},{9,15},{10,... | collective-permute-start | bytes 786440 | tf_op jit(solution)/shard_map/ppermute | solution.py:279
  158.9 40.2 %collective-permute-start.17 = (bf16[2,128,512]{2,1,0:T(8,128)(2,1)S(1)}, bf16[2,128,512]{2,1,0:T(8,128)(2,1)S(1)}, u32[]{:S(2)}, u32[]{:S(2)}) collective-permute-start(bf16[2,128,512]{2,1,0:T(8,128)(2,1)S(1)} %get-tuple-element.61), channel_id=1, source_target_pairs={{0,7},{1,6},{2,5},{3,4},{4,3},{5,2},{6,1},{7,0},{8,15},{9,14},{10,... | collective-permute-start | bytes 786440 | tf_op jit(solution)/shard_map/ppermute | solution.py:279
  166.4 35.4 %collective-permute-start.18 = (bf16[2,128,512]{2,1,0:T(8,128)(2,1)S(1)}, bf16[2,128,512]{2,1,0:T(8,128)(2,1)S(1)}, u32[]{:S(2)}, u32[]{:S(2)}) collective-permute-start(bf16[2,128,512]{2,1,0:T(8,128)(2,1)S(1)} %get-tuple-element.63), channel_id=1, source_target_pairs={{0,1},{1,0},{2,3},{3,2},{4,5},{5,4},{6,7},{7,6},{8,9},{9,8},{10,11... | collective-permute-start | bytes 786440 | tf_op jit(solution)/shard_map/ppermute | solution.py:279
  173.8 30.6 %copy-start.19 = (f32[16,4]{0,1:T(4,128)S(1)}, f32[16,4]{0,1:T(4,128)}, u32[]{:S(2)}) copy-start(f32[16,4]{0,1:T(4,128)} %param.10) | copy-start | bytes 772
  173.8 42.4 %copy-start.4 = (f32[128,512]{1,0:T(8,128)S(1)}, f32[128,512]{1,0:T(8,128)}, u32[]{:S(2)}) copy-start(f32[128,512]{1,0:T(8,128)} %weight_ref.1) | copy-start | bytes 786436
  175.8 0.7 copy-start.7
  176.5 28.0 %collective-permute-start.19 = (bf16[2,128,512]{2,1,0:T(8,128)(2,1)}, bf16[2,128,512]{2,1,0:T(8,128)(2,1)}, u32[]{:S(2)}, u32[]{:S(2)}) collective-permute-start(bf16[2,128,512]{2,1,0:T(8,128)(2,1)} %get-tuple-element.64), channel_id=1, source_target_pairs={{0,2},{1,3},{2,0},{3,1},{4,6},{5,7},{6,4},{7,5},{8,10},{9,11},{10,... | collective-permute-start | bytes 786440 | tf_op jit(solution)/shard_map/ppermute | solution.py:279
  184.0 28.5 %collective-permute-start.28 = (bf16[2,2,128,512]{3,2,1,0:T(8,128)(2,1)}, bf16[2,2,128,512]{3,2,1,0:T(8,128)(2,1)}, u32[]{:S(2)}, u32[]{:S(2)}) collective-permute-start(bf16[2,2,128,512]{3,2,1,0:T(8,128)(2,1)} %get-tuple-element.73.refs_12_), channel_id=1, source_target_pairs={{0,8},{8,16},{16,24},{1,9},{9,17},{17,25},{2,10},{10,18},{18,26},{... | collective-permute-start | bytes 1572872 | tf_op jit(solution)/shard_map/ppermute | solution.py:286
  195.3 17.2 %collective-permute-start.29 = (bf16[2,2,128,512]{3,2,1,0:T(8,128)(2,1)}, bf16[2,2,128,512]{3,2,1,0:T(8,128)(2,1)}, u32[]{:S(2)}, u32[]{:S(2)}) collective-permute-start(bf16[2,2,128,512]{3,2,1,0:T(8,128)(2,1)} %get-tuple-element.74.refs_13_), channel_id=1, source_target_pairs={{0,8},{8,16},{16,24},{1,9},{9,17},{17,25},{2,10},{10,18},{18,26},{... | collective-permute-start | bytes 1572872 | tf_op jit(solution)/shard_map/ppermute | solution.py:286
  199.8 12.6 %collective-permute-start.30 = (bf16[2,2,128,512]{3,2,1,0:T(8,128)(2,1)}, bf16[2,2,128,512]{3,2,1,0:T(8,128)(2,1)}, u32[]{:S(2)}, u32[]{:S(2)}) collective-permute-start(bf16[2,2,128,512]{3,2,1,0:T(8,128)(2,1)} %get-tuple-element.75.refs_10_), channel_id=1, source_target_pairs={{8,0},{16,8},{24,16},{9,1},{17,9},{25,17},{10,2},{18,10},{26,18},{... | collective-permute-start | bytes 1572872 | tf_op jit(solution)/shard_map/ppermute | solution.py:286
  202.5 13.8 %collective-permute-start.31 = (bf16[2,2,128,512]{3,2,1,0:T(8,128)(2,1)}, bf16[2,2,128,512]{3,2,1,0:T(8,128)(2,1)}, u32[]{:S(2)}, u32[]{:S(2)}) collective-permute-start(bf16[2,2,128,512]{3,2,1,0:T(8,128)(2,1)} %get-tuple-element.76.refs_11_), channel_id=1, source_target_pairs={{8,0},{16,8},{24,16},{9,1},{17,9},{25,17},{10,2},{18,10},{26,18},{... | collective-permute-start | bytes 1572872 | tf_op jit(solution)/shard_map/ppermute | solution.py:286
  204.5 8.0 %collective-permute-start.20 = (bf16[2,128,512]{2,1,0:T(8,128)(2,1)}, bf16[2,128,512]{2,1,0:T(8,128)(2,1)}, u32[]{:S(2)}, u32[]{:S(2)}) collective-permute-start(bf16[2,128,512]{2,1,0:T(8,128)(2,1)} %copy-done.17), channel_id=1, source_target_pairs={{0,3},{1,2},{2,1},{3,0},{4,7},{5,6},{6,5},{7,4},{8,11},{9,10},{10,... | collective-permute-start | bytes 786440 | tf_op jit(solution)/shard_map/ppermute | solution.py:279
  216.3 1.0 copy-start.6
  217.2 0.9 copy-start.8
  218.2 0.9 copy-start.10
  219.1 0.9 copy-start.12
  220.1 0.9 copy-start.14
  221.0 0.9 copy-start.16
  (4 other events, 2.8 us)

commit v6 on v5

--- a/solution.py
+++ b/solution.py
@@ -26,9 +26,26 @@
     return jnp.concatenate([real, -imag], 1), jnp.concatenate([imag, real], 1)
 
 
-def right_kernel(after, ranks, states, me_ref, second_ref, *refs):
+def near_slabs(me, near):
+    return pl.ds(me & -near, near)
+
+
+def slab_specs(near, ranks, kinds, block, wide):
+    return [pl.BlockSpec((near, kinds, block, wide), lambda i: (0, 0, i, 0))] + [
+        pl.BlockSpec((kinds, block, wide), lambda i: (0, i, 0))
+    ] * (ranks - near)
+
+
+def sources(me, near, parts, n):
+    for low in range(near):
+        yield (me & -near) + low, parts[0][low, n]
+    for s, part in enumerate(parts[1:], near):
+        yield me ^ s, part[n]
+
+
+def right_kernel(after, near, ranks, states, me_ref, second_ref, *refs):
     refs = refs[after:]
-    kinds = len(refs) - 1 - ranks
+    kinds = len(refs) - 2 - (ranks - near)
     packets, outs, slabs = refs[:kinds], refs[kinds:-1], refs[-1]
     me = me_ref[0]
     rows = packets[0].shape[0]
@@ -56,17 +73,18 @@
                     slabs[j * cuts + p, :, c * piece : (c + 1) * piece] = product[
                         first : first + rows, p * piece : (p + 1) * piece
                     ]
-        for s, out in enumerate(outs):
+        outs[0][:, n] = slabs[near_slabs(me, near)]
+        for s, out in enumerate(outs[1:], near):
             out[n] = slabs[me ^ s]
 
 
-def right_call(after, me, second, view, chosen, ranks, states, piece, limit):
+def right_call(after, near, me, second, view, chosen, ranks, states, piece, limit):
     rows, _, _, group, _ = view.shape
     width = second.shape[1]
     block = rows // 2
     kinds = len(chosen)
     return pl.pallas_call(
-        functools.partial(right_kernel, len(after), ranks, states),
+        functools.partial(right_kernel, len(after), near, ranks, states),
         grid=(rows // block,),
         in_specs=[SMEM, pl.BlockSpec(second.shape, lambda i: (0, 0))]
         + [AFTER] * len(after)
@@ -74,8 +92,9 @@
             pl.BlockSpec((block, 2, None, group, LANES), lambda i, k=k: (i, 0, k, 0, 0))
             for k in chosen
         ],
-        out_specs=[pl.BlockSpec((kinds, block, 2 * piece), lambda i: (0, i, 0))] * ranks,
-        out_shape=[jax.ShapeDtypeStruct((kinds, rows, 2 * piece), jnp.bfloat16)] * ranks,
+        out_specs=slab_specs(near, ranks, kinds, block, 2 * piece),
+        out_shape=[jax.ShapeDtypeStruct((near, kinds, rows, 2 * piece), jnp.bfloat16)]
+        + [jax.ShapeDtypeStruct((kinds, rows, 2 * piece), jnp.bfloat16)] * (ranks - near),
         scratch_shapes=[
             pltpu.VMEM((ranks, block, 2 * piece), jnp.bfloat16),
         ],
@@ -87,39 +106,42 @@
     )(me, second, *after, *([view] * kinds))
 
 
-def left_kernel(after, ranks, me_ref, first_ref, *refs):
+def left_kernel(after, near, ranks, me_ref, first_ref, *refs):
     refs = refs[after:]
-    ins, outs, lines, slabs = refs[:ranks], refs[ranks:-2], refs[-2], refs[-1]
+    count = 1 + ranks - near
+    ins, outs, lines, slabs = refs[:count], refs[count:-2], refs[-2], refs[-1]
     me = me_ref[0]
-    rows, wide = ins[0].shape
+    _, _, rows, wide = ins[0].shape
     piece = wide // 2
     whole = ranks * rows
-    for s, part in enumerate(ins):
-        value = part[...]
-        first = pl.multiple_of((me ^ s) * rows, rows)
+    for source, value in sources(me, near, ins, 0):
+        first = pl.multiple_of(source * rows, rows)
         lines[pl.ds(first, rows), :] = value
         lines[pl.ds(first + whole, rows), :] = jnp.concatenate(
             [-value[:, piece:], value[:, :piece]], 1
         )
     product = jnp.dot(first_ref[...], lines[...], preferred_element_type=jnp.float32)
     slabs[...] = product.astype(jnp.bfloat16).reshape(ranks, rows, wide)
-    for s, out in enumerate(outs):
-        out[...] = slabs[me ^ s]
+    outs[0][:, 0] = slabs[near_slabs(me, near)]
+    for s, out in enumerate(outs[1:], near):
+        out[0] = slabs[me ^ s]
 
 
 def left_call(after, me, first, slabs):
-    ranks = len(slabs)
-    kinds, rows, wide = slabs[0].shape
+    near, kinds, rows, wide = slabs[0].shape
+    ranks = len(slabs) - 1 + near
     whole = ranks * rows
-    spec = pl.BlockSpec((None, rows, wide), lambda i: (i, 0, 0))
+    specs = [pl.BlockSpec((near, 1, rows, wide), lambda i: (0, i, 0, 0))] + [
+        pl.BlockSpec((1, rows, wide), lambda i: (i, 0, 0))
+    ] * (ranks - near)
     return pl.pallas_call(
-        functools.partial(left_kernel, len(after), ranks),
+        functools.partial(left_kernel, len(after), near, ranks),
         grid=(kinds,),
         in_specs=[SMEM, pl.BlockSpec(first.shape, lambda i: (0, 0))]
         + [AFTER] * len(after)
-        + [spec] * ranks,
-        out_specs=[spec] * ranks,
-        out_shape=[jax.ShapeDtypeStruct(slabs[0].shape, jnp.bfloat16)] * ranks,
+        + specs,
+        out_specs=specs,
+        out_shape=[jax.ShapeDtypeStruct(x.shape, jnp.bfloat16) for x in slabs],
         scratch_shapes=[
             pltpu.VMEM((2 * whole, wide), jnp.bfloat16),
             pltpu.VMEM((ranks, rows, wide), jnp.bfloat16),
@@ -132,12 +154,12 @@
     )(me, first, *after, *slabs)
 
 
-def phased_product(me, n, second_ref, cosine_ref, sine_ref, ins, order, slabs):
+def phased_product(me, n, near, second_ref, cosine_ref, sine_ref, ins, slabs):
     states, _, width = cosine_ref.shape
     piece = slabs.shape[2] // 2
     cuts = width // piece
-    for s, part in zip(order, ins):
-        slabs[me ^ s] = part[n]
+    for source, value in sources(me, near, ins, n):
+        slabs[source] = value
     pairs = []
     for j in range(states):
         real, imag = (
@@ -158,15 +180,16 @@
     return product.astype(jnp.bfloat16)
 
 
-def phase_kernel(after, ranks, me_ref, second_ref, cosine_ref, sine_ref, *refs):
+def phase_kernel(after, near, ranks, me_ref, second_ref, cosine_ref, sine_ref, *refs):
     refs = refs[after:]
-    ins, outs, slabs = refs[:ranks], refs[ranks:-1], refs[-1]
+    count = 1 + ranks - near
+    ins, outs, slabs = refs[:count], refs[count:-1], refs[-1]
     states, rows, _ = cosine_ref.shape
     share = outs[0].shape[1]
     pieces = states // share
     for n in range(len(outs) // pieces):
         product = phased_product(
-            me_ref[0], n, second_ref, cosine_ref, sine_ref, ins, range(ranks), slabs
+            me_ref[0], n, near, second_ref, cosine_ref, sine_ref, ins, slabs
         )
         for c in range(2):
             for j in range(states):
@@ -175,19 +198,19 @@
 
 
 def phase_call(after, me, second, cosine, sine, slabs):
-    ranks = len(slabs)
-    kinds, rows, wide = slabs[0].shape
+    near, kinds, rows, wide = slabs[0].shape
+    ranks = len(slabs) - 1 + near
     states, _, width = cosine.shape
     block = rows // 2
     share = states // PIECES
     count = kinds * PIECES
     table = pl.BlockSpec((states, block, width), lambda i: (0, i, 0))
     return pl.pallas_call(
-        functools.partial(phase_kernel, len(after), ranks),
+        functools.partial(phase_kernel, len(after), near, ranks),
         grid=(rows // block,),
         in_specs=[SMEM, pl.BlockSpec(second.shape, lambda i: (0, 0)), table, table]
         + [AFTER] * len(after)
-        + [pl.BlockSpec((kinds, block, wide), lambda i: (0, i, 0))] * ranks,
+        + slab_specs(near, ranks, kinds, block, wide),
         out_specs=[pl.BlockSpec((2, share, block, width), lambda i: (0, 0, i, 0))] * count,
         out_shape=[jax.ShapeDtypeStruct((2, share, rows, width), jnp.bfloat16)] * count,
         scratch_shapes=[pltpu.VMEM((ranks, block, wide), jnp.bfloat16)],
@@ -200,10 +223,10 @@
 
 
 def mix_kernel(
-    chosen, order, me_ref, up_ref, down_ref, second_ref, cosine_ref, sine_ref, weight_ref, *refs
+    chosen, near, ranks, me_ref, up_ref, down_ref, second_ref, cosine_ref, sine_ref, weight_ref, *refs
 ):
-    ranks = len(order)
-    ins, known, (out, slabs, fresh) = refs[:ranks], refs[ranks:-3], refs[-3:]
+    count = 1 + ranks - near
+    ins, known, (out, slabs, fresh) = refs[:count], refs[count:-3], refs[-3:]
     blocks, states = up_ref.shape
     rows, width = weight_ref.shape
     share = known[0].shape[1]
@@ -213,7 +236,7 @@
     others = [k for k in range(-1, blocks + 1) if k not in chosen]
     for n in range(len(chosen)):
         product = phased_product(
-            me_ref[0], n, second_ref, cosine_ref, sine_ref, ins, order, slabs
+            me_ref[0], n, near, second_ref, cosine_ref, sine_ref, ins, slabs
         )
         fresh[n] = product.reshape(2, states, rows, width)
 
@@ -241,22 +264,20 @@
 
 
 def mix_call(me, up, down, second, cosine, sine, weight, chosen, slabs, known):
-    ranks = len(slabs)
-    half = ranks // 2
-    order = (*range(half, ranks), *range(half))
-    kinds, rows, wide = slabs[0].shape
+    near, kinds, rows, wide = slabs[0].shape
+    ranks = len(slabs) - 1 + near
     _, share, _, width = known[0].shape
     blocks, states = up.shape
     group = width // LANES * states
     block = rows // 4
     table = pl.BlockSpec((states, block, width), lambda i: (0, i, 0))
     return pl.pallas_call(
-        functools.partial(mix_kernel, tuple(chosen), order),
+        functools.partial(mix_kernel, tuple(chosen), near, ranks),
         grid=(rows // block,),
         in_specs=[SMEM] * 3
         + [pl.BlockSpec(second.shape, lambda i: (0, 0)), table, table]
         + [pl.BlockSpec((block, width), lambda i: (i, 0))]
-        + [pl.BlockSpec((kinds, block, wide), lambda i: (0, i, 0))] * ranks
+        + slab_specs(near, ranks, kinds, block, wide)
         + [pl.BlockSpec((2, share, block, width), lambda i: (0, 0, i, 0))] * len(known),
         out_specs=pl.BlockSpec((block, 2, blocks, group, LANES), lambda i: (i, 0, 0, 0, 0)),
         out_shape=jax.ShapeDtypeStruct((rows, 2, blocks, group, LANES), jnp.bfloat16),
@@ -269,14 +290,20 @@
             8 * kinds * states * rows * width * width, 10 * blocks * states * rows * width
         ),
         name="mix",
-    )(me, up, down, second, cosine, sine, weight, *[slabs[s] for s in order], *known)
+    )(me, up, down, second, cosine, sine, weight, *slabs, *known)
 
 
 def exchanged(slabs, axis):
     count = lax.axis_size(axis)
-    result = [slabs[0]] + [None] * (count - 1)
-    for s in reversed(range(1, count)):
-        result[s] = lax.ppermute(slabs[s], axis, [(i, i ^ s) for i in range(count)])
+    near = slabs[0].shape[0]
+    result = [slabs[0]]
+    if near == count:
+        result = [lax.all_to_all(slabs[0], axis, 0, 0, tiled=True)]
+    elif near > 1:
+        groups = [list(range(i, i + near)) for i in range(0, count, near)]
+        result = [lax.all_to_all(slabs[0], axis, 0, 0, axis_index_groups=groups, tiled=True)]
+    for s, slab in enumerate(slabs[1:], near):
+        result.append(lax.ppermute(slab, axis, [(i, i ^ s) for i in range(count)]))
     return result
 
 
@@ -300,11 +327,12 @@
     edges = sorted({0, blocks - 1})
     chunks = [edges, [k for k in range(blocks) if k not in edges]]
 
+    nears = (ranks, ranks)
     last = me
     lines = []
     for n, chosen in enumerate(chunks):
         limit = LIMIT if n else 2 * LIMIT + LIMIT // 2
-        half = right_call([last], me, second, view, chosen, ranks, states, piece, limit)
+        half = right_call([last], nears[n], me, second, view, chosen, ranks, states, piece, limit)
         last = half[0]
         lines.append(exchanged(half, "rad"))
     backs = []

time: 231 us -> 234 us (1.013); the launches traced: 231 us -> 230 us
  starting transfers between devices: 68.9 us -> 33.6 us
  waiting for transfers between devices: 106 us -> 128 us
  local copies, waits for them, and re-layouts: 23.2 us -> 35.7 us
    all_to_all x0 -> x4, waiting for transfers between devices: none -> 128 us  [exchanged(): result = [lax.all_to_all(slabs[0], axis, 0, 0, tiled=True)]]
    ppermute x28 -> x0, waiting for transfers between devices: 102 us -> none  [exchanged(): result[s] = lax.ppermute(slabs[s], axis, [(i, i ^ s) for i in range(count)])]
    ppermute x28 -> x0, starting transfers between devices: 50.8 us -> none  [exchanged(): result[s] = lax.ppermute(slabs[s], axis, [(i, i ^ s) for i in range(count)])]
    all_to_all x0 -> x4, starting transfers between devices: none -> 22.5 us  [exchanged(): result = [lax.all_to_all(slabs[0], axis, 0, 0, tiled=True)]]
    unnamed x42 -> x44, local copies, waits for them, and re-layouts: 12.8 us -> 24.2 us
    ppermute x4, starting transfers between devices: 18.2 us -> 11.1 us  [neighbour(): return lax.ppermute(edge, axis, pairs)]
    ppermute x4, waiting for transfers between devices: 3.78 us -> 0.01 us  [neighbour(): return lax.ppermute(edge, axis, pairs)]
  transfers between devices with their start and end apart: 32 -> 8, of which waited for: 15 -> 4; matrix products, arithmetic and copies ran while one was open for 5% -> 5% of each run, Pallas kernels for 8% -> 8%
where the time goes in v6:
time: 234 us; the launch traced here: 230 us
  waiting for transfers between devices  128 us (55%)
  local copies, waits for them, and re-layouts  35.7 us (15%)
  starting transfers between devices  33.6 us (14%)
  Pallas kernels  32.3 us (14%)
    all_to_all x4, waiting for transfers between devices, exchanged(): result = [lax.all_to_all(slabs[0], axis, 0, 0, tiled=True)]  128 us
    unnamed x44, local copies, waits for them, and re-layouts  24.2 us
    all_to_all x4, starting transfers between devices, exchanged(): result = [lax.all_to_all(slabs[0], axis, 0, 0, tiled=True)]  22.5 us
    ppermute x4, starting transfers between devices, neighbour(): return lax.ppermute(edge, axis, pairs)  11.1 us
    pallas_call x2, Pallas kernels, left_call(): pl.pallas_call(functools.partial(left_kernel, len(after), near, ranks), g...  10.8 us
    pallas_call x2, Pallas kernels, right_call(): pl.pallas_call(functools.partial(right_kernel, len(after), near, ranks, s...  9 us
    pallas_call x1, Pallas kernels, mix_call(): pl.pallas_call(functools.partial(mix_kernel, tuple(chosen), near, ranks),...  8.65 us
    reshape x1, local copies, waits for them, and re-layouts, per_device(): first = first_propagator.reshape(2 * whole, whole).T  6.42 us
  transfers between devices with their start and end apart: 8, of which 4 were waited for; matrix products, arithmetic and copies ran while one was open for 5% of the time, Pallas kernels for 8%

profile of v6, /device:TPU:9, one launch (start us, length us, event | category | flops | bytes accessed | tf_op | source)
XLA Modules:
  0.0 229.9 jit_solution(18265132497995612199)
XLA Ops:
  0.0 1.2 copy-done.1
  1.2 5.0 %right.2.refs_0_ = bf16[8,2,128,512]{3,2,1,0:T(8,128)(2,1)} custom-call(s32[1]{0:T(128)} %bitcast.me_ref.refs_0_, bf16[1024,512]{1,0:T(8,128)(2,1)S(1)} %bitcast.23, s32[1]{0:T(128)} %bitcast.me_ref.refs_0_, bf16[128,2,4,16,128]{4,3,2,1,0:T(8,128)(2,1)} %bitcast.19, bf16[128,2,4,16,128]{4,3,2,1,0:T(8,128)(2,1)} %bitcast.20), custom_call_target="tpu_custom_call" | custom-call | flops 2147483648 | bytes 4194304 | tf_op jit(solution)/shard_map/right/pallas_call | solution.py:86
  6.2 5.9 %all-to-all-start = ((bf16[8,2,128,512]{3,2,1,0:T(8,128)(2,1)}), bf16[8,2,128,512]{3,2,1,0:T(8,128)(2,1)S(1)}, u32[]{:S(2)}, u32[]{:S(2)}) async-start(bf16[8,2,128,512]{3,2,1,0:T(8,128)(2,1)} %right.2.refs_0_), calls=%async_computation | async-start | bytes 4194304 | tf_op jit(solution)/shard_map/all_to_all | solution.py:301
  12.0 2.2 copy-done
  14.2 4.0 %right.3.refs_0_ = bf16[8,2,128,512]{3,2,1,0:T(8,128)(2,1)} custom-call(s32[1]{0:T(128)} %bitcast.me_ref.refs_0_, bf16[1024,512]{1,0:T(8,128)(2,1)S(1)} %bitcast.24, bf16[8,2,128,512]{3,2,1,0:T(8,128)(2,1)} %right.2.refs_0_, bf16[128,2,4,16,128]{4,3,2,1,0:T(8,128)(2,1)S(1)} %bitcast.21, bf16[128,2,4,16,128]{4,3,2,1,0:T(8,128)(2,1)S(1)} %bitcast.22), custom_call_target="tpu_custom_call" | custom-call | flops 2147483648 | bytes 4194304 | tf_op jit(solution)/shard_map/right/pallas_call | solution.py:86
  18.3 40.3 %all-to-all-done.refs_1_ = bf16[8,2,128,512]{3,2,1,0:T(8,128)(2,1)S(1)} async-done(((bf16[8,2,128,512]{3,2,1,0:T(8,128)(2,1)}), bf16[8,2,128,512]{3,2,1,0:T(8,128)(2,1)S(1)}, u32[]{:S(2)}, u32[]{:S(2)}) %all-to-all-start) | async-done | bytes 2097184 | tf_op jit(solution)/shard_map/all_to_all | solution.py:301
  58.6 1.3 copy-done.15
  59.9 5.5 %all-to-all-start.1 = ((bf16[8,2,128,512]{3,2,1,0:T(8,128)(2,1)}), bf16[8,2,128,512]{3,2,1,0:T(8,128)(2,1)S(1)}, u32[]{:S(2)}, u32[]{:S(2)}) async-start(bf16[8,2,128,512]{3,2,1,0:T(8,128)(2,1)} %right.3.refs_0_), calls=%async_computation.1 | async-start | bytes 4194304 | tf_op jit(solution)/shard_map/all_to_all | solution.py:301
  65.4 6.4 %copy.14 = bf16[2048,1024]{0,1:T(8,128)(2,1)} copy(bf16[2048,1024]{1,0:T(8,128)(2,1)} %bitcast.29) | data formatting | bytes 8388608 | tf_op jit(solution)/shard_map/reshape | solution.py:324
  71.9 2.2 copy-done.7
  74.0 1.6 copy-done.16
  75.6 5.4 %left.2.refs_0_ = bf16[8,2,128,512]{3,2,1,0:T(8,128)(2,1)S(1)} custom-call(s32[1]{0:T(128)} %bitcast.me_ref.refs_0_, bf16[1024,2048]{1,0:T(8,128)(2,1)S(1)} %bitcast.27, bf16[8,2,128,512]{3,2,1,0:T(8,128)(2,1)} %right.3.refs_0_, bf16[8,2,128,512]{3,2,1,0:T(8,128)(2,1)S(1)} %copy-done.16), custom_call_target="tpu_custom_call" | custom-call | flops 4294967296 | bytes 8388608 | tf_op jit(solution)/shard_map/left/pallas_call | solution.py:137
  81.0 1.3 copy-done.17
  82.3 29.6 %all-to-all-done.1.refs_1_ = bf16[8,2,128,512]{3,2,1,0:T(8,128)(2,1)S(1)} async-done(((bf16[8,2,128,512]{3,2,1,0:T(8,128)(2,1)}), bf16[8,2,128,512]{3,2,1,0:T(8,128)(2,1)S(1)}, u32[]{:S(2)}, u32[]{:S(2)}) %all-to-all-start.1) | async-done | bytes 2097184 | tf_op jit(solution)/shard_map/all_to_all | solution.py:301
  112.0 1.3 copy-done.13
  113.3 5.5 %all-to-all-start.3 = ((bf16[8,2,128,512]{3,2,1,0:T(8,128)(2,1)}), bf16[8,2,128,512]{3,2,1,0:T(8,128)(2,1)S(1)}, u32[]{:S(2)}, u32[]{:S(2)}) async-start(bf16[8,2,128,512]{3,2,1,0:T(8,128)(2,1)} %copy-done.17), calls=%async_computation.3 | async-start | bytes 4194304 | tf_op jit(solution)/shard_map/all_to_all | solution.py:301
  118.8 2.2 copy-done.8
  121.0 1.6 copy-done.14
  122.6 1.6 copy-done.18
  124.2 5.4 %left.3.refs_0_ = bf16[8,2,128,512]{3,2,1,0:T(8,128)(2,1)S(1)} custom-call(s32[1]{0:T(128)} %bitcast.me_ref.refs_0_, bf16[1024,2048]{1,0:T(8,128)(2,1)S(1)} %bitcast.28, bf16[8,2,128,512]{3,2,1,0:T(8,128)(2,1)S(1)} %copy-done.18, bf16[8,2,128,512]{3,2,1,0:T(8,128)(2,1)S(1)} %copy-done.14), custom_call_target="tpu_custom_call" | custom-call | flops 4294967296 | bytes 8388608 | tf_op jit(solution)/shard_map/left/pallas_call | solution.py:137
  129.6 0.0 copy-start.9
  129.6 1.3 copy-done.9
  130.9 34.4 %all-to-all-done.3.refs_1_ = bf16[8,2,128,512]{3,2,1,0:T(8,128)(2,1)S(1)} async-done(((bf16[8,2,128,512]{3,2,1,0:T(8,128)(2,1)}), bf16[8,2,128,512]{3,2,1,0:T(8,128)(2,1)S(1)}, u32[]{:S(2)}, u32[]{:S(2)}) %all-to-all-start.3) | async-done | bytes 2097184 | tf_op jit(solution)/shard_map/all_to_all | solution.py:301
  165.4 1.3 copy-done.11
  166.7 5.5 %all-to-all-start.2 = ((bf16[8,2,128,512]{3,2,1,0:T(8,128)(2,1)}), bf16[8,2,128,512]{3,2,1,0:T(8,128)(2,1)S(1)}, u32[]{:S(2)}, u32[]{:S(2)}) async-start(bf16[8,2,128,512]{3,2,1,0:T(8,128)(2,1)} %copy-done.9), calls=%async_computation.2 | async-start | bytes 4194304 | tf_op jit(solution)/shard_map/all_to_all | solution.py:301
  172.2 4.9 %sine_bitcast_fusion = (f32[4,128,512]{2,1,0:T(8,128)S(1)}, f32[4,128,512]{2,1,0:T(8,128)S(1)}) fusion(f32[128,4,512]{2,1,0:T(4,128)} %param.9), kind=kLoop, calls=%fused_computation | loop fusion | bytes 3145728 | tf_op jit(solution)/shard_map/sin | solution.py:345
  177.2 0.0 copy-start.3
  177.2 0.0 copy-start.5
  177.2 0.0 copy-done.10
  177.2 2.3 %copy-done.12 = bf16[8,2,128,512]{3,2,1,0:T(8,128)(2,1)S(1)} copy-done((bf16[8,2,128,512]{3,2,1,0:T(8,128)(2,1)S(1)}, bf16[8,2,128,512]{3,2,1,0:T(8,128)(2,1)}, u32[]{:S(2)}) %copy-start.12) | copy-done | bytes 2097176
  179.5 3.9 %phase.1 = (bf16[2,2,128,512]{3,2,1,0:T(8,128)(2,1)}, bf16[2,2,128,512]{3,2,1,0:T(8,128)(2,1)}, bf16[2,2,128,512]{3,2,1,0:T(8,128)(2,1)}, bf16[2,2,128,512]{3,2,1,0:T(8,128)(2,1)}) custom-call(s32[1]{0:T(128)} %bitcast.me_ref.refs_0_, bf16[1024,512]{1,0:T(8,128)(2,1)S(1)} %bitcast.25, f32[4,128,512]{2,1,0:T(8,128)S(1)} %get-tuple-element.14.cosine_ref, ...), custom_call_target="tpu_custom_call" | custom-call | flops 2147483648 | bytes 4194304 | tf_op jit(solution)/shard_map/phase/pallas_call | solution.py:208
  183.4 4.1 %collective-permute-start = (bf16[2,2,128,512]{3,2,1,0:T(8,128)(2,1)}, bf16[2,2,128,512]{3,2,1,0:T(8,128)(2,1)}, u32[]{:S(2)}, u32[]{:S(2)}) collective-permute-start(bf16[2,2,128,512]{3,2,1,0:T(8,128)(2,1)} %get-tuple-element.9.refs_5_), channel_id=1, source_target_pairs={{0,8},{8,16},{16,24},{1,9},{9,17},{17,25},{2,10},{10,18},{18,26},{... | collective-permute-start | bytes 1572872 | tf_op jit(solution)/shard_map/ppermute | solution.py:313
  187.5 1.9 collective-permute-start.1
  189.4 3.2 %collective-permute-start.2 = (bf16[2,2,128,512]{3,2,1,0:T(8,128)(2,1)}, bf16[2,2,128,512]{3,2,1,0:T(8,128)(2,1)}, u32[]{:S(2)}, u32[]{:S(2)}) collective-permute-start(bf16[2,2,128,512]{3,2,1,0:T(8,128)(2,1)} %get-tuple-element.11.refs_3_), channel_id=1, source_target_pairs={{8,0},{16,8},{24,16},{9,1},{17,9},{25,17},{10,2},{18,10},{26,18},{... | collective-permute-start | bytes 1572872 | tf_op jit(solution)/shard_map/ppermute | solution.py:313
  192.7 1.9 collective-permute-start.3
  194.6 0.1 constant_dynamic-slice_fusion
  194.7 0.1 copy.15
  194.8 0.1 dynamic-slice
  194.9 0.1 copy.16
  194.9 0.1 pad_dynamic-slice_fusion
  195.0 23.7 %all-to-all-done.2.refs_0_ = bf16[8,2,128,512]{3,2,1,0:T(8,128)(2,1)S(1)} async-done(((bf16[8,2,128,512]{3,2,1,0:T(8,128)(2,1)}), bf16[8,2,128,512]{3,2,1,0:T(8,128)(2,1)S(1)}, u32[]{:S(2)}, u32[]{:S(2)}) %all-to-all-start.2) | async-done | bytes 2097184 | tf_op jit(solution)/shard_map/all_to_all | solution.py:301
  218.8 0.0 collective-permute-done.refs_1_
  218.8 0.0 collective-permute-done.1.refs_2_
  218.8 0.0 collective-permute-done.2.refs_7_
  218.8 0.0 collective-permute-done.3.refs_8_
  218.8 1.2 copy-done.4
  220.0 1.2 copy-done.6
  221.2 8.7 %mix.1 = bf16[128,2,4,16,128]{4,3,2,1,0:T(8,128)(2,1)} custom-call(s32[1]{0:T(128)} %bitcast.me_ref.refs_0_, f32[4,4]{1,0:T(4,128)S(1)} %get-tuple-element.16.up_ref, f32[4,4]{1,0:T(4,128)S(1)} %get-tuple-element.15.down_ref, bf16[1024,512]{1,0:T(8,128)(2,1)S(1)} %bitcast.26, f32[4,128,512]{2,1,0:T(8,128)S(1)} %copy-done.6, f32[4,128,512]{2,1,0:T(8,128)S(1)} %copy-done.4, ...), custom_call_target="tpu_custom_call" | custom-call | flops 2147483648 | bytes 10485760 | tf_op jit(solution)/shard_map/mix/pallas_call | solution.py:274
  (24 shorter events, 0.0 us)
Async XLA Ops:
  0.0 1.2 copy-start.1
  6.2 5.9 %copy-start.2 = (bf16[2,512,512]{2,1,0:T(8,128)(2,1)S(1)}, bf16[2,512,512]{2,1,0:T(8,128)(2,1)}, u32[]{:S(2)}) copy-start(bf16[2,512,512]{2,1,0:T(8,128)(2,1)} %param.8) | copy-start | bytes 3145732
  6.2 52.4 %all-to-all-start = ((bf16[8,2,128,512]{3,2,1,0:T(8,128)(2,1)}), bf16[8,2,128,512]{3,2,1,0:T(8,128)(2,1)S(1)}, u32[]{:S(2)}, u32[]{:S(2)}) async-start(bf16[8,2,128,512]{3,2,1,0:T(8,128)(2,1)} %right.2.refs_0_), calls=%async_computation | async-start | bytes 4194304 | tf_op jit(solution)/shard_map/all_to_all | solution.py:301
  12.0 2.2 copy-start
  58.6 1.3 copy-start.15
  59.9 52.1 %all-to-all-start.1 = ((bf16[8,2,128,512]{3,2,1,0:T(8,128)(2,1)}), bf16[8,2,128,512]{3,2,1,0:T(8,128)(2,1)S(1)}, u32[]{:S(2)}, u32[]{:S(2)}) async-start(bf16[8,2,128,512]{3,2,1,0:T(8,128)(2,1)} %right.3.refs_0_), calls=%async_computation.1 | async-start | bytes 4194304 | tf_op jit(solution)/shard_map/all_to_all | solution.py:301
  71.9 2.2 copy-start.7
  74.0 1.6 copy-start.16
  81.0 1.3 copy-start.17
  112.0 1.3 copy-start.13
  113.3 52.1 %all-to-all-start.3 = ((bf16[8,2,128,512]{3,2,1,0:T(8,128)(2,1)}), bf16[8,2,128,512]{3,2,1,0:T(8,128)(2,1)S(1)}, u32[]{:S(2)}, u32[]{:S(2)}) async-start(bf16[8,2,128,512]{3,2,1,0:T(8,128)(2,1)} %copy-done.17), calls=%async_computation.3 | async-start | bytes 4194304 | tf_op jit(solution)/shard_map/all_to_all | solution.py:301
  118.8 2.2 copy-start.8
  121.0 1.6 copy-start.14
  122.6 1.6 copy-start.18
  129.6 1.3 copy-start.9
  165.4 1.3 copy-start.11
  166.7 52.1 %all-to-all-start.2 = ((bf16[8,2,128,512]{3,2,1,0:T(8,128)(2,1)}), bf16[8,2,128,512]{3,2,1,0:T(8,128)(2,1)S(1)}, u32[]{:S(2)}, u32[]{:S(2)}) async-start(bf16[8,2,128,512]{3,2,1,0:T(8,128)(2,1)} %copy-done.9), calls=%async_computation.2 | async-start | bytes 4194304 | tf_op jit(solution)/shard_map/all_to_all | solution.py:301
  172.2 4.9 %copy-start.10 = (bf16[8,2,128,512]{3,2,1,0:T(8,128)(2,1)S(1)}, bf16[8,2,128,512]{3,2,1,0:T(8,128)(2,1)}, u32[]{:S(2)}) copy-start(bf16[8,2,128,512]{3,2,1,0:T(8,128)(2,1)} %copy-done.9) | copy-start | bytes 6291460
  177.2 6.3 %copy-start.3 = (f32[4,128,512]{2,1,0:T(8,128)}, f32[4,128,512]{2,1,0:T(8,128)S(1)}, u32[]{:S(2)}) copy-start(f32[4,128,512]{2,1,0:T(8,128)S(1)} %get-tuple-element.13.sine_ref) | copy-start | bytes 3145732
  177.2 6.3 %copy-start.5 = (f32[4,128,512]{2,1,0:T(8,128)}, f32[4,128,512]{2,1,0:T(8,128)S(1)}, u32[]{:S(2)}) copy-start(f32[4,128,512]{2,1,0:T(8,128)S(1)} %get-tuple-element.14.cosine_ref) | copy-start | bytes 3145732
  177.2 2.3 %copy-start.12 = (bf16[8,2,128,512]{3,2,1,0:T(8,128)(2,1)S(1)}, bf16[8,2,128,512]{3,2,1,0:T(8,128)(2,1)}, u32[]{:S(2)}) copy-start(bf16[8,2,128,512]{3,2,1,0:T(8,128)(2,1)} %copy-done.11) | copy-start | bytes 6291460
  179.5 15.1 %copy-start.20 = (f32[16,4]{0,1:T(4,128)S(1)}, f32[16,4]{0,1:T(4,128)}, u32[]{:S(2)}) copy-start(f32[16,4]{0,1:T(4,128)} %param.10) | copy-start | bytes 772
  179.5 39.3 %copy-start.19 = (f32[128,512]{1,0:T(8,128)S(1)}, f32[128,512]{1,0:T(8,128)}, u32[]{:S(2)}) copy-start(f32[128,512]{1,0:T(8,128)} %weight_ref.1) | copy-start | bytes 786436
  183.4 35.3 %collective-permute-start = (bf16[2,2,128,512]{3,2,1,0:T(8,128)(2,1)}, bf16[2,2,128,512]{3,2,1,0:T(8,128)(2,1)}, u32[]{:S(2)}, u32[]{:S(2)}) collective-permute-start(bf16[2,2,128,512]{3,2,1,0:T(8,128)(2,1)} %get-tuple-element.9.refs_5_), channel_id=1, source_target_pairs={{0,8},{8,16},{16,24},{1,9},{9,17},{17,25},{2,10},{10,18},{18,26},{... | collective-permute-start | bytes 1572872 | tf_op jit(solution)/shard_map/ppermute | solution.py:313
  187.5 31.3 %collective-permute-start.1 = (bf16[2,2,128,512]{3,2,1,0:T(8,128)(2,1)}, bf16[2,2,128,512]{3,2,1,0:T(8,128)(2,1)}, u32[]{:S(2)}, u32[]{:S(2)}) collective-permute-start(bf16[2,2,128,512]{3,2,1,0:T(8,128)(2,1)} %get-tuple-element.10.refs_6_), channel_id=1, source_target_pairs={{0,8},{8,16},{16,24},{1,9},{9,17},{17,25},{2,10},{10,18},{18,26},{... | collective-permute-start | bytes 1572872 | tf_op jit(solution)/shard_map/ppermute | solution.py:313
  189.4 29.3 %collective-permute-start.2 = (bf16[2,2,128,512]{3,2,1,0:T(8,128)(2,1)}, bf16[2,2,128,512]{3,2,1,0:T(8,128)(2,1)}, u32[]{:S(2)}, u32[]{:S(2)}) collective-permute-start(bf16[2,2,128,512]{3,2,1,0:T(8,128)(2,1)} %get-tuple-element.11.refs_3_), channel_id=1, source_target_pairs={{8,0},{16,8},{24,16},{9,1},{17,9},{25,17},{10,2},{18,10},{26,18},{... | collective-permute-start | bytes 1572872 | tf_op jit(solution)/shard_map/ppermute | solution.py:313
  192.7 26.1 %collective-permute-start.3 = (bf16[2,2,128,512]{3,2,1,0:T(8,128)(2,1)}, bf16[2,2,128,512]{3,2,1,0:T(8,128)(2,1)}, u32[]{:S(2)}, u32[]{:S(2)}) collective-permute-start(bf16[2,2,128,512]{3,2,1,0:T(8,128)(2,1)} %get-tuple-element.12.refs_4_), channel_id=1, source_target_pairs={{8,0},{16,8},{24,16},{9,1},{17,9},{25,17},{10,2},{18,10},{26,18},{... | collective-permute-start | bytes 1572872 | tf_op jit(solution)/shard_map/ppermute | solution.py:313
  218.8 1.2 copy-start.4
  220.0 1.2 copy-start.6

commit v7 on v6

--- a/solution.py
+++ b/solution.py
@@ -327,7 +327,7 @@
     edges = sorted({0, blocks - 1})
     chunks = [edges, [k for k in range(blocks) if k not in edges]]
 
-    nears = (ranks, ranks)
+    nears = (ranks, 1)
     last = me
     lines = []
     for n, chosen in enumerate(chunks):

time: 234 us -> 250 us (1.068); the launches traced: 230 us -> 249 us
  waiting for transfers between devices: 128 us -> 144 us
  starting transfers between devices: 33.6 us -> 43.3 us
  local copies, waits for them, and re-layouts: 35.7 us -> 27.5 us
    ppermute x0 -> x14, waiting for transfers between devices: none -> 111 us  [exchanged(): result.append(lax.ppermute(slab, axis, [(i, i ^ s) for i in range(count)]))]
    all_to_all x4 -> x2, waiting for transfers between devices: 128 us -> 29.6 us  [exchanged(): result = [lax.all_to_all(slabs[0], axis, 0, 0, tiled=True)]]
    ppermute x0 -> x14, starting transfers between devices: none -> 19.3 us  [exchanged(): result.append(lax.ppermute(slab, axis, [(i, i ^ s) for i in range(count)]))]
    all_to_all x4 -> x2, starting transfers between devices: 22.5 us -> 11.4 us  [exchanged(): result = [lax.all_to_all(slabs[0], axis, 0, 0, tiled=True)]]
    unnamed x44 -> x58, local copies, waits for them, and re-layouts: 24.2 us -> 17.2 us
    ppermute x4, waiting for transfers between devices: 0.01 us -> 3.54 us  [neighbour(): return lax.ppermute(edge, axis, pairs)]
  transfers between devices with their start and end apart: 8 -> 20, of which waited for: 4 -> 12; matrix products, arithmetic and copies ran while one was open for 5% -> 4% of each run, Pallas kernels for 8% -> 6%
where the time goes in v7:
time: 250 us; the launch traced here: 249 us
  waiting for transfers between devices  144 us (58%)
  starting transfers between devices  43.3 us (17%)
  Pallas kernels  34.3 us (14%)
  local copies, waits for them, and re-layouts  27.5 us (11%)
    ppermute x14, waiting for transfers between devices, exchanged(): result.append(lax.ppermute(slab, axis, [(i, i ^ s) for i in range(count)]))  111 us
    all_to_all x2, waiting for transfers between devices, exchanged(): result = [lax.all_to_all(slabs[0], axis, 0, 0, tiled=True)]  29.6 us
    ppermute x14, starting transfers between devices, exchanged(): result.append(lax.ppermute(slab, axis, [(i, i ^ s) for i in range(count)]))  19.3 us
    unnamed x58, local copies, waits for them, and re-layouts  17.2 us
    ppermute x4, starting transfers between devices, neighbour(): return lax.ppermute(edge, axis, pairs)  12.5 us
    pallas_call x2, Pallas kernels, left_call(): pl.pallas_call(functools.partial(left_kernel, len(after), near, ranks), g...  12.1 us
    all_to_all x2, starting transfers between devices, exchanged(): result = [lax.all_to_all(slabs[0], axis, 0, 0, tiled=True)]  11.4 us
    pallas_call x1, Pallas kernels, mix_call(): pl.pallas_call(functools.partial(mix_kernel, tuple(chosen), near, ranks),...  8.93 us
  transfers between devices with their start and end apart: 20, of which 12 were waited for; matrix products, arithmetic and copies ran while one was open for 4% of the time, Pallas kernels for 6%

profile of v7, /device:TPU:9, one launch (start us, length us, event | category | flops | bytes accessed | tf_op | source)
XLA Modules:
  0.0 249.2 jit_solution(4796618670738369796)
XLA Ops:
  0.0 1.2 copy-done.1
  1.2 5.1 %right.2.refs_0_ = bf16[8,2,128,512]{3,2,1,0:T(8,128)(2,1)} custom-call(s32[1]{0:T(128)} %bitcast.me_ref.refs_0_, bf16[1024,512]{1,0:T(8,128)(2,1)S(1)} %bitcast.23, s32[1]{0:T(128)} %bitcast.me_ref.refs_0_, bf16[128,2,4,16,128]{4,3,2,1,0:T(8,128)(2,1)} %bitcast.19, bf16[128,2,4,16,128]{4,3,2,1,0:T(8,128)(2,1)} %bitcast.20), custom_call_target="tpu_custom_call" | custom-call | flops 2147483648 | bytes 4194304 | tf_op jit(solution)/shard_map/right/pallas_call | solution.py:86
  6.3 5.7 %all-to-all-start = ((bf16[8,2,128,512]{3,2,1,0:T(8,128)(2,1)}), bf16[8,2,128,512]{3,2,1,0:T(8,128)(2,1)S(1)}, u32[]{:S(2)}, u32[]{:S(2)}) async-start(bf16[8,2,128,512]{3,2,1,0:T(8,128)(2,1)} %right.2.refs_0_), calls=%async_computation | async-start | bytes 4194304 | tf_op jit(solution)/shard_map/all_to_all | solution.py:301
  12.0 6.5 %copy.14 = bf16[2048,1024]{0,1:T(8,128)(2,1)} copy(bf16[2048,1024]{1,0:T(8,128)(2,1)} %bitcast.29) | data formatting | bytes 8388608 | tf_op jit(solution)/shard_map/reshape | solution.py:324
  18.5 2.2 copy-done
  20.7 3.3 %right.3 = (bf16[1,2,128,512]{3,2,1,0:T(8,128)(2,1)S(1)}, bf16[2,128,512]{2,1,0:T(8,128)(2,1)S(1)}, bf16[2,128,512]{2,1,0:T(8,128)(2,1)S(1)}, bf16[2,128,512]{2,...) custom-call(s32[1]{0:T(128)} %bitcast.me_ref.refs_0_, ...), custom_call_target="tpu_custom_call" | custom-call | flops 2147483648 | bytes 4194304 | tf_op jit(solution)/shard_map/right/pallas_call | solution.py:86
  24.0 0.7 copy-done.12
  24.7 0.7 copy-done.14
  25.4 0.7 copy-done.16
  26.1 0.7 copy-done.18
  28.2 0.7 copy-done.24
  28.9 29.6 %all-to-all-done.refs_1_ = bf16[8,2,128,512]{3,2,1,0:T(8,128)(2,1)S(1)} async-done(((bf16[8,2,128,512]{3,2,1,0:T(8,128)(2,1)}), bf16[8,2,128,512]{3,2,1,0:T(8,128)(2,1)S(1)}, u32[]{:S(2)}, u32[]{:S(2)}) %all-to-all-start) | async-done | bytes 2097184 | tf_op jit(solution)/shard_map/all_to_all | solution.py:301
  58.5 2.2 copy-done.3
  60.7 6.2 %left.2.refs_0_ = bf16[8,2,128,512]{3,2,1,0:T(8,128)(2,1)} custom-call(s32[1]{0:T(128)} %bitcast.me_ref.refs_0_, bf16[1024,2048]{1,0:T(8,128)(2,1)S(1)} %bitcast.27, bf16[1,2,128,512]{3,2,1,0:T(8,128)(2,1)S(1)} %get-tuple-element.25.refs_0_.refs_1_, bf16[8,2,128,512]{3,2,1,0:T(8,128)(2,1)S(1)} %all-to-all-done.refs_1_), custom_call_target="tpu_custom_call" | custom-call | flops 4294967296 | bytes 8388608 | tf_op jit(solution)/shard_map/left/pallas_call | solution.py:137
  67.0 5.7 %all-to-all-start.1 = ((bf16[8,2,128,512]{3,2,1,0:T(8,128)(2,1)}), bf16[8,2,128,512]{3,2,1,0:T(8,128)(2,1)}, u32[]{:S(2)}, u32[]{:S(2)}) async-start(bf16[8,2,128,512]{3,2,1,0:T(8,128)(2,1)} %left.2.refs_0_), calls=%async_computation.1 | async-start | bytes 4194304 | tf_op jit(solution)/shard_map/all_to_all | solution.py:301
  72.7 1.2 collective-permute-start
  74.1 1.2 collective-permute-start.2
  75.3 2.1 collective-permute-start.3
  77.4 1.2 collective-permute-start.4
  78.6 16.2 %collective-permute-done.refs_2_ = bf16[2,128,512]{2,1,0:T(8,128)(2,1)S(1)} collective-permute-done((bf16[2,128,512]{2,1,0:T(8,128)(2,1)S(1)}, bf16[2,128,512]{2,1,0:T(8,128)(2,1)S(1)}, u32[]{:S(2)}, u32[]{:S(2)}) %collective-permute-start) | collective-permute-done | bytes 262176 | tf_op jit(solution)/shard_map/ppermute | solution.py:306
  94.8 1.4 collective-permute-start.5
  96.2 16.1 %collective-permute-done.1.refs_3_ = bf16[2,128,512]{2,1,0:T(8,128)(2,1)S(1)} collective-permute-done((bf16[2,128,512]{2,1,0:T(8,128)(2,1)S(1)}, bf16[2,128,512]{2,1,0:T(8,128)(2,1)S(1)}, u32[]{:S(2)}, u32[]{:S(2)}) %collective-permute-start.1) | collective-permute-done | bytes 262176 | tf_op jit(solution)/shard_map/ppermute | solution.py:306
  112.3 2.7 %collective-permute-start.6 = (bf16[2,128,512]{2,1,0:T(8,128)(2,1)S(1)}, bf16[2,128,512]{2,1,0:T(8,128)(2,1)S(1)}, u32[]{:S(2)}, u32[]{:S(2)}) collective-permute-start(bf16[2,128,512]{2,1,0:T(8,128)(2,1)S(1)} %copy-done.13), channel_id=1, source_target_pairs={{0,7},{1,6},{2,5},{3,4},{4,3},{5,2},{6,1},{7,0},{8,15},{9,14},{10,... | collective-permute-start | bytes 786440 | tf_op jit(solution)/shard_map/ppermute | solution.py:306
  115.0 4.3 %collective-permute-done.2.refs_4_ = bf16[2,128,512]{2,1,0:T(8,128)(2,1)S(1)} collective-permute-done((bf16[2,128,512]{2,1,0:T(8,128)(2,1)S(1)}, bf16[2,128,512]{2,1,0:T(8,128)(2,1)S(1)}, u32[]{:S(2)}, u32[]{:S(2)}) %collective-permute-start.2) | collective-permute-done | bytes 262176 | tf_op jit(solution)/shard_map/ppermute | solution.py:306
  119.3 27.6 %collective-permute-done.3.refs_5_ = bf16[2,128,512]{2,1,0:T(8,128)(2,1)S(1)} collective-permute-done((bf16[2,128,512]{2,1,0:T(8,128)(2,1)S(1)}, bf16[2,128,512]{2,1,0:T(8,128)(2,1)S(1)}, u32[]{:S(2)}, u32[]{:S(2)}) %collective-permute-start.3) | collective-permute-done | bytes 262176 | tf_op jit(solution)/shard_map/ppermute | solution.py:306
  146.9 5.6 %collective-permute-done.4.refs_6_ = bf16[2,128,512]{2,1,0:T(8,128)(2,1)S(1)} collective-permute-done((bf16[2,128,512]{2,1,0:T(8,128)(2,1)S(1)}, bf16[2,128,512]{2,1,0:T(8,128)(2,1)S(1)}, u32[]{:S(2)}, u32[]{:S(2)}) %collective-permute-start.4) | collective-permute-done | bytes 262176 | tf_op jit(solution)/shard_map/ppermute | solution.py:306
  152.5 5.6 %collective-permute-done.5.refs_7_ = bf16[2,128,512]{2,1,0:T(8,128)(2,1)S(1)} collective-permute-done((bf16[2,128,512]{2,1,0:T(8,128)(2,1)S(1)}, bf16[2,128,512]{2,1,0:T(8,128)(2,1)S(1)}, u32[]{:S(2)}, u32[]{:S(2)}) %collective-permute-start.5) | collective-permute-done | bytes 262176 | tf_op jit(solution)/shard_map/ppermute | solution.py:306
  158.1 7.1 %collective-permute-done.6.refs_8_ = bf16[2,128,512]{2,1,0:T(8,128)(2,1)S(1)} collective-permute-done((bf16[2,128,512]{2,1,0:T(8,128)(2,1)S(1)}, bf16[2,128,512]{2,1,0:T(8,128)(2,1)S(1)}, u32[]{:S(2)}, u32[]{:S(2)}) %collective-permute-start.6) | collective-permute-done | bytes 262176 | tf_op jit(solution)/shard_map/ppermute | solution.py:306
  165.2 2.2 copy-done.4
  167.4 5.9 %left.3 = (bf16[1,2,128,512]{3,2,1,0:T(8,128)(2,1)S(1)}, bf16[2,128,512]{2,1,0:T(8,128)(2,1)}, bf16[2,128,512]{2,1,0:T(8,128)(2,1)}, bf16[2,128,512]{2,1,0:T(8,1...) custom-call(s32[1]{0:T(128)} %bitcast.me_ref.refs_0_, ...), custom_call_target="tpu_custom_call" | custom-call | flops 4294967296 | bytes 8388608 | tf_op jit(solution)/shard_map/left/pallas_call | solution.py:137
  174.0 1.5 collective-permute-start.11
  175.5 2.5 collective-permute-start.12
  178.0 0.7 collective-permute-start.13
  179.2 3.7 %sine_bitcast_fusion = (f32[4,128,512]{2,1,0:T(8,128)S(1)}, f32[4,128,512]{2,1,0:T(8,128)S(1)}) fusion(f32[128,4,512]{2,1,0:T(4,128)S(1)} %copy-done.26), kind=kLoop, calls=%fused_computation | loop fusion | bytes 3145728 | tf_op jit(solution)/shard_map/sin | solution.py:345
  182.9 18.0 %collective-permute-done.10.refs_4_ = bf16[2,128,512]{2,1,0:T(8,128)(2,1)S(1)} collective-permute-done((bf16[2,128,512]{2,1,0:T(8,128)(2,1)S(1)}, bf16[2,128,512]{2,1,0:T(8,128)(2,1)S(1)}, u32[]{:S(2)}, u32[]{:S(2)}) %collective-permute-start.10) | collective-permute-done | bytes 262176 | tf_op jit(solution)/shard_map/ppermute | solution.py:306
  201.6 4.1 %collective-permute-start.8 = (bf16[2,128,512]{2,1,0:T(8,128)(2,1)}, bf16[2,128,512]{2,1,0:T(8,128)(2,1)}, u32[]{:S(2)}, u32[]{:S(2)}) collective-permute-start(bf16[2,128,512]{2,1,0:T(8,128)(2,1)} %get-tuple-element.35), channel_id=1, source_target_pairs={{0,2},{1,3},{2,0},{3,1},{4,6},{5,7},{6,4},{7,5},{8,10},{9,11},{10,... | collective-permute-start | bytes 786440 | tf_op jit(solution)/shard_map/ppermute | solution.py:306
  205.7 0.9 copy-done.7
  206.6 4.9 %phase.1 = (bf16[2,2,128,512]{3,2,1,0:T(8,128)(2,1)}, bf16[2,2,128,512]{3,2,1,0:T(8,128)(2,1)}, bf16[2,2,128,512]{3,2,1,0:T(8,128)(2,1)}, bf16[2,2,128,512]{3,2,1,0:T(8,128)(2,1)}) custom-call(s32[1]{0:T(128)} %bitcast.me_ref.refs_0_, bf16[1024,512]{1,0:T(8,128)(2,1)S(1)} %bitcast.25, f32[4,128,512]{2,1,0:T(8,128)S(1)} %get-tuple-element.46.cosine_ref, ...), custom_call_target="tpu_custom_call" | custom-call | flops 2147483648 | bytes 4194304 | tf_op jit(solution)/shard_map/phase/pallas_call | solution.py:208
  211.6 4.9 %collective-permute-start.14 = (bf16[2,2,128,512]{3,2,1,0:T(8,128)(2,1)}, bf16[2,2,128,512]{3,2,1,0:T(8,128)(2,1)}, u32[]{:S(2)}, u32[]{:S(2)}) collective-permute-start(bf16[2,2,128,512]{3,2,1,0:T(8,128)(2,1)} %get-tuple-element.41.refs_12_), channel_id=1, source_target_pairs={{0,8},{8,16},{16,24},{1,9},{9,17},{17,25},{2,10},{10,18},{18,26},{... | collective-permute-start | bytes 1572872 | tf_op jit(solution)/shard_map/ppermute | solution.py:313
  216.5 3.3 %collective-permute-start.15 = (bf16[2,2,128,512]{3,2,1,0:T(8,128)(2,1)}, bf16[2,2,128,512]{3,2,1,0:T(8,128)(2,1)}, u32[]{:S(2)}, u32[]{:S(2)}) collective-permute-start(bf16[2,2,128,512]{3,2,1,0:T(8,128)(2,1)} %get-tuple-element.42.refs_13_), channel_id=1, source_target_pairs={{0,8},{8,16},{16,24},{1,9},{9,17},{17,25},{2,10},{10,18},{18,26},{... | collective-permute-start | bytes 1572872 | tf_op jit(solution)/shard_map/ppermute | solution.py:313
  219.9 1.9 collective-permute-done.13.refs_7_
  221.8 2.4 collective-permute-start.16
  224.1 1.9 collective-permute-start.17
  226.5 8.1 %collective-permute-done.9.refs_3_ = bf16[2,128,512]{2,1,0:T(8,128)(2,1)} collective-permute-done((bf16[2,128,512]{2,1,0:T(8,128)(2,1)}, bf16[2,128,512]{2,1,0:T(8,128)(2,1)}, u32[]{:S(2)}, u32[]{:S(2)}) %collective-permute-start.9) | collective-permute-done | bytes 262176 | tf_op jit(solution)/shard_map/ppermute | solution.py:306
  234.7 3.5 %collective-permute-done.17.refs_15_ = bf16[2,2,128,512]{3,2,1,0:T(8,128)(2,1)} collective-permute-done((bf16[2,2,128,512]{3,2,1,0:T(8,128)(2,1)}, bf16[2,2,128,512]{3,2,1,0:T(8,128)(2,1)}, u32[]{:S(2)}, u32[]{:S(2)}) %collective-permute-start.17) | collective-permute-done | bytes 524320 | tf_op jit(solution)/shard_map/ppermute | solution.py:313
  238.2 0.9 copy-done.8
  239.1 0.9 copy-done.10
  240.1 8.9 %mix.1 = bf16[128,2,4,16,128]{4,3,2,1,0:T(8,128)(2,1)} custom-call(s32[1]{0:T(128)} %bitcast.me_ref.refs_0_, f32[4,4]{1,0:T(4,128)S(1)} %get-tuple-element.48.up_ref, f32[4,4]{1,0:T(4,128)S(1)} %get-tuple-element.47.down_ref, bf16[1024,512]{1,0:T(8,128)(2,1)S(1)} %bitcast.26, f32[4,128,512]{2,1,0:T(8,128)S(1)} %get-tuple-element.46.cosine_ref, ...), custom_call_target="tpu_custom_call" | custom-call | flops 2147483648 | bytes 10485760 | tf_op jit(solution)/shard_map/mix/pallas_call | solution.py:274
  (62 shorter events, 4.0 us)
Async XLA Ops:
  0.0 1.2 copy-start.1
  6.3 52.2 %all-to-all-start = ((bf16[8,2,128,512]{3,2,1,0:T(8,128)(2,1)}), bf16[8,2,128,512]{3,2,1,0:T(8,128)(2,1)S(1)}, u32[]{:S(2)}, u32[]{:S(2)}) async-start(bf16[8,2,128,512]{3,2,1,0:T(8,128)(2,1)} %right.2.refs_0_), calls=%async_computation | async-start | bytes 4194304 | tf_op jit(solution)/shard_map/all_to_all | solution.py:301
  12.0 6.5 %copy-start.2 = (bf16[2,512,512]{2,1,0:T(8,128)(2,1)S(1)}, bf16[2,512,512]{2,1,0:T(8,128)(2,1)}, u32[]{:S(2)}) copy-start(bf16[2,512,512]{2,1,0:T(8,128)(2,1)} %param.8) | copy-start | bytes 3145732
  18.5 2.2 copy-start
  24.0 0.7 copy-start.12
  24.7 0.7 copy-start.14
  25.4 0.7 copy-start.16
  26.1 0.7 copy-start.18
  26.8 0.7 copy-start.20
  27.5 0.7 copy-start.22
  28.2 0.7 copy-start.24
  58.5 2.2 copy-start.3
  66.9 5.7 %copy-start.25 = (bf16[2,128,512]{2,1,0:T(8,128)(2,1)S(1)}, bf16[2,128,512]{2,1,0:T(8,128)(2,1)}, u32[]{:S(2)}) copy-start(bf16[2,128,512]{2,1,0:T(8,128)(2,1)} %copy-done.24) | copy-start | bytes 786436
  66.9 6.9 %copy-start.23 = (bf16[2,128,512]{2,1,0:T(8,128)(2,1)S(1)}, bf16[2,128,512]{2,1,0:T(8,128)(2,1)}, u32[]{:S(2)}) copy-start(bf16[2,128,512]{2,1,0:T(8,128)(2,1)} %copy-done.22) | copy-start | bytes 786436
  66.9 7.2 %copy-start.21 = (bf16[2,128,512]{2,1,0:T(8,128)(2,1)S(1)}, bf16[2,128,512]{2,1,0:T(8,128)(2,1)}, u32[]{:S(2)}) copy-start(bf16[2,128,512]{2,1,0:T(8,128)(2,1)} %copy-done.20) | copy-start | bytes 786436
  66.9 8.4 %copy-start.19 = (bf16[2,128,512]{2,1,0:T(8,128)(2,1)S(1)}, bf16[2,128,512]{2,1,0:T(8,128)(2,1)}, u32[]{:S(2)}) copy-start(bf16[2,128,512]{2,1,0:T(8,128)(2,1)} %copy-done.18) | copy-start | bytes 786436
  66.9 10.5 %copy-start.17 = (bf16[2,128,512]{2,1,0:T(8,128)(2,1)S(1)}, bf16[2,128,512]{2,1,0:T(8,128)(2,1)}, u32[]{:S(2)}) copy-start(bf16[2,128,512]{2,1,0:T(8,128)(2,1)} %copy-done.16) | copy-start | bytes 786436
  66.9 27.8 %copy-start.15 = (bf16[2,128,512]{2,1,0:T(8,128)(2,1)S(1)}, bf16[2,128,512]{2,1,0:T(8,128)(2,1)}, u32[]{:S(2)}) copy-start(bf16[2,128,512]{2,1,0:T(8,128)(2,1)} %copy-done.14) | copy-start | bytes 786436
  67.0 45.3 %copy-start.13 = (bf16[2,128,512]{2,1,0:T(8,128)(2,1)S(1)}, bf16[2,128,512]{2,1,0:T(8,128)(2,1)}, u32[]{:S(2)}) copy-start(bf16[2,128,512]{2,1,0:T(8,128)(2,1)} %copy-done.12) | copy-start | bytes 786436
  67.0 138.7 %all-to-all-start.1 = ((bf16[8,2,128,512]{3,2,1,0:T(8,128)(2,1)}), bf16[8,2,128,512]{3,2,1,0:T(8,128)(2,1)}, u32[]{:S(2)}, u32[]{:S(2)}) async-start(bf16[8,2,128,512]{3,2,1,0:T(8,128)(2,1)} %left.2.refs_0_), calls=%async_computation.1 | async-start | bytes 4194304 | tf_op jit(solution)/shard_map/all_to_all | solution.py:301
  72.7 22.1 %collective-permute-start = (bf16[2,128,512]{2,1,0:T(8,128)(2,1)S(1)}, bf16[2,128,512]{2,1,0:T(8,128)(2,1)S(1)}, u32[]{:S(2)}, u32[]{:S(2)}) collective-permute-start(bf16[2,128,512]{2,1,0:T(8,128)(2,1)S(1)} %copy-done.25), channel_id=1, source_target_pairs={{0,1},{1,0},{2,3},{3,2},{4,5},{5,4},{6,7},{7,6},{8,9},{9,8},{10,11... | collective-permute-start | bytes 786440 | tf_op jit(solution)/shard_map/ppermute | solution.py:306
  73.8 38.4 %collective-permute-start.1 = (bf16[2,128,512]{2,1,0:T(8,128)(2,1)S(1)}, bf16[2,128,512]{2,1,0:T(8,128)(2,1)S(1)}, u32[]{:S(2)}, u32[]{:S(2)}) collective-permute-start(bf16[2,128,512]{2,1,0:T(8,128)(2,1)S(1)} %copy-done.23), channel_id=1, source_target_pairs={{0,2},{1,3},{2,0},{3,1},{4,6},{5,7},{6,4},{7,5},{8,10},{9,11},{10,... | collective-permute-start | bytes 786440 | tf_op jit(solution)/shard_map/ppermute | solution.py:306
  74.1 45.1 %collective-permute-start.2 = (bf16[2,128,512]{2,1,0:T(8,128)(2,1)S(1)}, bf16[2,128,512]{2,1,0:T(8,128)(2,1)S(1)}, u32[]{:S(2)}, u32[]{:S(2)}) collective-permute-start(bf16[2,128,512]{2,1,0:T(8,128)(2,1)S(1)} %copy-done.21), channel_id=1, source_target_pairs={{0,3},{1,2},{2,1},{3,0},{4,7},{5,6},{6,5},{7,4},{8,11},{9,10},{10,... | collective-permute-start | bytes 786440 | tf_op jit(solution)/shard_map/ppermute | solution.py:306
  75.3 71.6 %collective-permute-start.3 = (bf16[2,128,512]{2,1,0:T(8,128)(2,1)S(1)}, bf16[2,128,512]{2,1,0:T(8,128)(2,1)S(1)}, u32[]{:S(2)}, u32[]{:S(2)}) collective-permute-start(bf16[2,128,512]{2,1,0:T(8,128)(2,1)S(1)} %copy-done.19), channel_id=1, source_target_pairs={{0,4},{1,5},{2,6},{3,7},{4,0},{5,1},{6,2},{7,3},{8,12},{9,13},{10,... | collective-permute-start | bytes 786440 | tf_op jit(solution)/shard_map/ppermute | solution.py:306
  77.4 75.1 %collective-permute-start.4 = (bf16[2,128,512]{2,1,0:T(8,128)(2,1)S(1)}, bf16[2,128,512]{2,1,0:T(8,128)(2,1)S(1)}, u32[]{:S(2)}, u32[]{:S(2)}) collective-permute-start(bf16[2,128,512]{2,1,0:T(8,128)(2,1)S(1)} %copy-done.17), channel_id=1, source_target_pairs={{0,5},{1,4},{2,7},{3,6},{4,1},{5,0},{6,3},{7,2},{8,13},{9,12},{10,... | collective-permute-start | bytes 786440 | tf_op jit(solution)/shard_map/ppermute | solution.py:306
  94.8 63.3 %collective-permute-start.5 = (bf16[2,128,512]{2,1,0:T(8,128)(2,1)S(1)}, bf16[2,128,512]{2,1,0:T(8,128)(2,1)S(1)}, u32[]{:S(2)}, u32[]{:S(2)}) collective-permute-start(bf16[2,128,512]{2,1,0:T(8,128)(2,1)S(1)} %copy-done.15), channel_id=1, source_target_pairs={{0,6},{1,7},{2,4},{3,5},{4,2},{5,3},{6,0},{7,1},{8,14},{9,15},{10,... | collective-permute-start | bytes 786440 | tf_op jit(solution)/shard_map/ppermute | solution.py:306
  112.3 52.9 %collective-permute-start.6 = (bf16[2,128,512]{2,1,0:T(8,128)(2,1)S(1)}, bf16[2,128,512]{2,1,0:T(8,128)(2,1)S(1)}, u32[]{:S(2)}, u32[]{:S(2)}) collective-permute-start(bf16[2,128,512]{2,1,0:T(8,128)(2,1)S(1)} %copy-done.13), channel_id=1, source_target_pairs={{0,7},{1,6},{2,5},{3,4},{4,3},{5,2},{6,1},{7,0},{8,15},{9,14},{10,... | collective-permute-start | bytes 786440 | tf_op jit(solution)/shard_map/ppermute | solution.py:306
  165.2 2.2 copy-start.4
  167.4 11.8 %copy-start.26 = (f32[128,4,512]{2,1,0:T(4,128)S(1)}, f32[128,4,512]{2,1,0:T(4,128)}, u32[]{:S(2)}) copy-start(f32[128,4,512]{2,1,0:T(4,128)} %param.9) | copy-start | bytes 3145732
  173.3 0.7 copy-start.6
  174.0 26.9 %copy-start.11 = (bf16[2,128,512]{2,1,0:T(8,128)(2,1)}, bf16[2,128,512]{2,1,0:T(8,128)(2,1)S(1)}, u32[]{:S(2)}) copy-start(bf16[2,128,512]{2,1,0:T(8,128)(2,1)S(1)} %get-tuple-element.36) | copy-start | bytes 786436
  174.0 26.9 %collective-permute-start.10 = (bf16[2,128,512]{2,1,0:T(8,128)(2,1)S(1)}, bf16[2,128,512]{2,1,0:T(8,128)(2,1)S(1)}, u32[]{:S(2)}, u32[]{:S(2)}) collective-permute-start(bf16[2,128,512]{2,1,0:T(8,128)(2,1)S(1)} %get-tuple-element.37), channel_id=1, source_target_pairs={{0,4},{1,5},{2,6},{3,7},{4,0},{5,1},{6,2},{7,3},{8,12},{9,13},{10,... | collective-permute-start | bytes 786440 | tf_op jit(solution)/shard_map/ppermute | solution.py:306
  174.0 37.6 %collective-permute-start.11 = (bf16[2,128,512]{2,1,0:T(8,128)(2,1)}, bf16[2,128,512]{2,1,0:T(8,128)(2,1)}, u32[]{:S(2)}, u32[]{:S(2)}) collective-permute-start(bf16[2,128,512]{2,1,0:T(8,128)(2,1)} %get-tuple-element.38), channel_id=1, source_target_pairs={{0,5},{1,4},{2,7},{3,6},{4,1},{5,0},{6,3},{7,2},{8,13},{9,12},{10,... | collective-permute-start | bytes 786440 | tf_op jit(solution)/shard_map/ppermute | solution.py:306
  175.5 41.0 %collective-permute-start.12 = (bf16[2,128,512]{2,1,0:T(8,128)(2,1)}, bf16[2,128,512]{2,1,0:T(8,128)(2,1)}, u32[]{:S(2)}, u32[]{:S(2)}) collective-permute-start(bf16[2,128,512]{2,1,0:T(8,128)(2,1)} %get-tuple-element.39), channel_id=1, source_target_pairs={{0,6},{1,7},{2,4},{3,5},{4,2},{5,3},{6,0},{7,1},{8,14},{9,15},{10,... | collective-permute-start | bytes 786440 | tf_op jit(solution)/shard_map/ppermute | solution.py:306
  178.0 43.8 %collective-permute-start.13 = (bf16[2,128,512]{2,1,0:T(8,128)(2,1)}, bf16[2,128,512]{2,1,0:T(8,128)(2,1)}, u32[]{:S(2)}, u32[]{:S(2)}) collective-permute-start(bf16[2,128,512]{2,1,0:T(8,128)(2,1)} %get-tuple-element.40), channel_id=1, source_target_pairs={{0,7},{1,6},{2,5},{3,4},{4,3},{5,2},{6,1},{7,0},{8,15},{9,14},{10,... | collective-permute-start | bytes 786440 | tf_op jit(solution)/shard_map/ppermute | solution.py:306
  178.7 45.4 %collective-permute-start.7 = (bf16[2,128,512]{2,1,0:T(8,128)(2,1)}, bf16[2,128,512]{2,1,0:T(8,128)(2,1)}, u32[]{:S(2)}, u32[]{:S(2)}) collective-permute-start(bf16[2,128,512]{2,1,0:T(8,128)(2,1)} %get-tuple-element.34), channel_id=1, source_target_pairs={{0,1},{1,0},{2,3},{3,2},{4,5},{5,4},{6,7},{7,6},{8,9},{9,8},{10,11... | collective-permute-start | bytes 786440 | tf_op jit(solution)/shard_map/ppermute | solution.py:306
  179.2 46.9 %copy-start.27 = (f32[16,4]{0,1:T(4,128)S(1)}, f32[16,4]{0,1:T(4,128)}, u32[]{:S(2)}) copy-start(f32[16,4]{0,1:T(4,128)} %param.10) | copy-start | bytes 772
  182.9 55.3 %copy-start.5 = (f32[128,512]{1,0:T(8,128)S(1)}, f32[128,512]{1,0:T(8,128)}, u32[]{:S(2)}) copy-start(f32[128,512]{1,0:T(8,128)} %weight_ref.1) | copy-start | bytes 786436
  200.9 0.7 copy-start.9
  201.6 24.6 %collective-permute-start.8 = (bf16[2,128,512]{2,1,0:T(8,128)(2,1)}, bf16[2,128,512]{2,1,0:T(8,128)(2,1)}, u32[]{:S(2)}, u32[]{:S(2)}) collective-permute-start(bf16[2,128,512]{2,1,0:T(8,128)(2,1)} %get-tuple-element.35), channel_id=1, source_target_pairs={{0,2},{1,3},{2,0},{3,1},{4,6},{5,7},{6,4},{7,5},{8,10},{9,11},{10,... | collective-permute-start | bytes 786440 | tf_op jit(solution)/shard_map/ppermute | solution.py:306
  205.7 1.0 copy-start.7
  211.6 23.1 %collective-permute-start.14 = (bf16[2,2,128,512]{3,2,1,0:T(8,128)(2,1)}, bf16[2,2,128,512]{3,2,1,0:T(8,128)(2,1)}, u32[]{:S(2)}, u32[]{:S(2)}) collective-permute-start(bf16[2,2,128,512]{3,2,1,0:T(8,128)(2,1)} %get-tuple-element.41.refs_12_), channel_id=1, source_target_pairs={{0,8},{8,16},{16,24},{1,9},{9,17},{17,25},{2,10},{10,18},{18,26},{... | collective-permute-start | bytes 1572872 | tf_op jit(solution)/shard_map/ppermute | solution.py:313
  216.5 18.1 %collective-permute-start.15 = (bf16[2,2,128,512]{3,2,1,0:T(8,128)(2,1)}, bf16[2,2,128,512]{3,2,1,0:T(8,128)(2,1)}, u32[]{:S(2)}, u32[]{:S(2)}) collective-permute-start(bf16[2,2,128,512]{3,2,1,0:T(8,128)(2,1)} %get-tuple-element.42.refs_13_), channel_id=1, source_target_pairs={{0,8},{8,16},{16,24},{1,9},{9,17},{17,25},{2,10},{10,18},{18,26},{... | collective-permute-start | bytes 1572872 | tf_op jit(solution)/shard_map/ppermute | solution.py:313
  221.8 12.9 %collective-permute-start.16 = (bf16[2,2,128,512]{3,2,1,0:T(8,128)(2,1)}, bf16[2,2,128,512]{3,2,1,0:T(8,128)(2,1)}, u32[]{:S(2)}, u32[]{:S(2)}) collective-permute-start(bf16[2,2,128,512]{3,2,1,0:T(8,128)(2,1)} %get-tuple-element.43.refs_10_), channel_id=1, source_target_pairs={{8,0},{16,8},{24,16},{9,1},{17,9},{25,17},{10,2},{18,10},{26,18},{... | collective-permute-start | bytes 1572872 | tf_op jit(solution)/shard_map/ppermute | solution.py:313
  224.1 14.0 %collective-permute-start.17 = (bf16[2,2,128,512]{3,2,1,0:T(8,128)(2,1)}, bf16[2,2,128,512]{3,2,1,0:T(8,128)(2,1)}, u32[]{:S(2)}, u32[]{:S(2)}) collective-permute-start(bf16[2,2,128,512]{3,2,1,0:T(8,128)(2,1)} %get-tuple-element.44.refs_11_), channel_id=1, source_target_pairs={{8,0},{16,8},{24,16},{9,1},{17,9},{25,17},{10,2},{18,10},{26,18},{... | collective-permute-start | bytes 1572872 | tf_op jit(solution)/shard_map/ppermute | solution.py:313
  226.2 8.5 %collective-permute-start.9 = (bf16[2,128,512]{2,1,0:T(8,128)(2,1)}, bf16[2,128,512]{2,1,0:T(8,128)(2,1)}, u32[]{:S(2)}, u32[]{:S(2)}) collective-permute-start(bf16[2,128,512]{2,1,0:T(8,128)(2,1)} %copy-done.11), channel_id=1, source_target_pairs={{0,3},{1,2},{2,1},{3,0},{4,7},{5,6},{6,5},{7,4},{8,11},{9,10},{10,... | collective-permute-start | bytes 786440 | tf_op jit(solution)/shard_map/ppermute | solution.py:306
  238.2 1.0 copy-start.8
  239.1 0.9 copy-start.10

commit v8 on v5

--- a/solution.py
+++ b/solution.py
@@ -8,14 +8,20 @@
 from jax.sharding import PartitionSpec as P
 
 LANES = 128
-PIECES = 2
-LIMIT = 20 * 1024 * 1024
+ROWS = 16
+PIECES = 4
+LIMIT = 18 * 1024 * 1024
+WHOLE = 3 * LIMIT
 SMEM = pl.BlockSpec(memory_space=pltpu.SMEM)
 AFTER = pl.BlockSpec(memory_space=pl.ANY)
 
 
 def params(limit=LIMIT):
     return pltpu.CompilerParams(vmem_limit_bytes=limit)
+
+
+def in_place(arrays):
+    return [pltpu.with_memory_space_constraint(x, pltpu.VMEM) for x in arrays]
 
 
 def cost(flops, moved):
@@ -209,7 +215,6 @@
     share = known[0].shape[1]
     pieces = states // share
     group = out.shape[3]
-    weight = weight_ref[...]
     others = [k for k in range(-1, blocks + 1) if k not in chosen]
     for n in range(len(chosen)):
         product = phased_product(
@@ -217,33 +222,38 @@
         )
         fresh[n] = product.reshape(2, states, rows, width)
 
-    def kinetic(k, c, j):
+    def kinetic(k, c, j, span):
         if k in chosen:
-            value = fresh[chosen.index(k), c, j]
+            value = fresh[chosen.index(k), c, j, span]
         else:
-            value = known[others.index(k) * pieces + j // share][c, j % share]
+            value = known[others.index(k) * pieces + j // share][c, j % share, span]
         return value.astype(jnp.float32)
 
-    for k in range(blocks):
-        columns = [[None] * group for _ in range(2)]
-        for j in range(states):
-            up, down = up_ref[k, j], down_ref[k, j]
-            mixed = [up * kinetic(k + 1, c, j) + down * kinetic(k - 1, c, j) for c in range(2)]
-            parts = (
-                kinetic(k, 0, j) + weight * mixed[1],
-                kinetic(k, 1, j) - weight * mixed[0],
-            )
+    for first in range(0, rows, ROWS):
+        span = slice(first, first + ROWS)
+        weight = weight_ref[span]
+        for k in range(blocks):
+            columns = [[None] * group for _ in range(2)]
+            for j in range(states):
+                up, down = up_ref[k, j], down_ref[k, j]
+                mixed = [
+                    up * kinetic(k + 1, c, j, span) + down * kinetic(k - 1, c, j, span)
+                    for c in range(2)
+                ]
+                parts = (
+                    kinetic(k, 0, j, span) + weight * mixed[1],
+                    kinetic(k, 1, j, span) - weight * mixed[0],
+                )
+                for c in range(2):
+                    for t in range(width // LANES):
+                        columns[c][t * states + j] = parts[c][:, t * LANES : (t + 1) * LANES]
             for c in range(2):
-                for t in range(width // LANES):
-                    columns[c][t * states + j] = parts[c][:, t * LANES : (t + 1) * LANES]
-        for c in range(2):
-            out[:, c, k] = jnp.stack(columns[c], 0).transpose(1, 0, 2).astype(jnp.bfloat16)
+                out[span, c, k] = jnp.stack(columns[c], 0).transpose(1, 0, 2).astype(jnp.bfloat16)
 
 
 def mix_call(me, up, down, second, cosine, sine, weight, chosen, slabs, known):
     ranks = len(slabs)
-    half = ranks // 2
-    order = (*range(half, ranks), *range(half))
+    order = tuple(range(ranks))
     kinds, rows, wide = slabs[0].shape
     _, share, _, width = known[0].shape
     blocks, states = up.shape
@@ -269,7 +279,7 @@
             8 * kinds * states * rows * width * width, 10 * blocks * states * rows * width
         ),
         name="mix",
-    )(me, up, down, second, cosine, sine, weight, *[slabs[s] for s in order], *known)
+    )(me, up, down, second, cosine, sine, weight, *in_place([slabs[s] for s in order] + known))
 
 
 def exchanged(slabs, axis):
@@ -303,7 +313,7 @@
     last = me
     lines = []
     for n, chosen in enumerate(chunks):
-        limit = LIMIT if n else 2 * LIMIT + LIMIT // 2
+        limit = LIMIT if n else WHOLE
         half = right_call([last], me, second, view, chosen, ranks, states, piece, limit)
         last = half[0]
         lines.append(exchanged(half, "rad"))

time: 231 us -> 234 us (1.013)
  waiting for transfers between devices: 106 us -> 91.2 us
  starting transfers between devices: 68.9 us -> 79.4 us
  local copies, waits for them, and re-layouts: 23.2 us -> 30.2 us
    ppermute x4 -> x8, starting transfers between devices: 18.2 us -> 37.7 us  [neighbour(): return lax.ppermute(edge, axis, pairs)]
    ppermute x28, waiting for transfers between devices: 102 us -> 83.1 us  [exchanged(): result[s] = lax.ppermute(slabs[s], axis, [(i, i ^ s) for i in range(count)])]
    ppermute x28, starting transfers between devices: 50.8 us -> 41.7 us  [exchanged(): result[s] = lax.ppermute(slabs[s], axis, [(i, i ^ s) for i in range(count)])]
    unnamed x42 -> x60, local copies, waits for them, and re-layouts: 12.8 us -> 19.8 us
    ppermute x4 -> x8, waiting for transfers between devices: 3.78 us -> 8.08 us  [neighbour(): return lax.ppermute(edge, axis, pairs)]
  transfers between devices with their start and end apart: 32 -> 36, of which waited for: 15 -> 15; matrix products, arithmetic and copies ran while one was open for 5% -> 5% of each run, Pallas kernels for 8% -> 8%
where the time goes in v8:
time: 234 us
  waiting for transfers between devices  91.2 us (39%)
  starting transfers between devices  79.4 us (34%)
  Pallas kernels  32.4 us (14%)
  local copies, waits for them, and re-layouts  30.2 us (13%)
    ppermute x28, waiting for transfers between devices, exchanged(): result[s] = lax.ppermute(slabs[s], axis, [(i, i ^ s) for i in range(count)])  83.1 us
    ppermute x28, starting transfers between devices, exchanged(): result[s] = lax.ppermute(slabs[s], axis, [(i, i ^ s) for i in range(count)])  41.7 us
    ppermute x8, starting transfers between devices, neighbour(): return lax.ppermute(edge, axis, pairs)  37.7 us
    unnamed x60, local copies, waits for them, and re-layouts  19.8 us
    pallas_call x2, Pallas kernels, left_call(): pl.pallas_call(functools.partial(left_kernel, len(after), ranks), grid=(k...  10.8 us
    pallas_call x1, Pallas kernels, mix_call(): pl.pallas_call(functools.partial(mix_kernel, tuple(chosen), order), grid=...  8.82 us
    pallas_call x2, Pallas kernels, right_call(): pl.pallas_call(functools.partial(right_kernel, len(after), ranks, states)...  8.63 us
    ppermute x8, waiting for transfers between devices, neighbour(): return lax.ppermute(edge, axis, pairs)  8.08 us
  transfers between devices with their start and end apart: 36, of which 15 were waited for; matrix products, arithmetic and copies ran while one was open for 5% of the time, Pallas kernels for 8%

profile of v8, /device:TPU:9, one launch (start us, length us, event | category | flops | bytes accessed | tf_op | source)
XLA Modules:
  0.0 233.6 jit_solution(9536568902736030029)
XLA Ops:
  0.0 5.4 %right.2 = (bf16[2,128,512]{2,1,0:T(8,128)(2,1)}, bf16[2,128,512]{2,1,0:T(8,128)(2,1)}, bf16[2,128,512]{2,1,0:T(8,128)(2,1)}, bf16[2,128,512]{2,1,0:T(8,128)(2,1...) custom-call(s32[1]{0:T(128)} %bitcast.me_ref.refs_0_, ...), custom_call_target="tpu_custom_call" | custom-call | flops 2147483648 | bytes 4194304 | tf_op jit(solution)/shard_map/right/pallas_call | solution.py:74
  5.4 1.3 collective-permute-start
  6.8 1.2 collective-permute-start.2
  8.1 2.3 collective-permute-start.3
  10.4 1.0 collective-permute-start.4
  11.4 1.4 collective-permute-done.refs_2_
  12.8 1.3 collective-permute-start.5
  14.1 7.6 %collective-permute-done.1.refs_3_ = bf16[2,128,512]{2,1,0:T(8,128)(2,1)S(1)} collective-permute-done((bf16[2,128,512]{2,1,0:T(8,128)(2,1)}, bf16[2,128,512]{2,1,0:T(8,128)(2,1)S(1)}, u32[]{:S(2)}, u32[]{:S(2)}) %collective-permute-start.1) | collective-permute-done | bytes 262176 | tf_op jit(solution)/shard_map/ppermute | solution.py:289
  21.7 6.5 %copy.14 = bf16[2048,1024]{0,1:T(8,128)(2,1)} copy(bf16[2048,1024]{1,0:T(8,128)(2,1)} %bitcast.29) | data formatting | bytes 8388608 | tf_op jit(solution)/shard_map/reshape | solution.py:307
  28.2 2.2 copy-done
  30.4 3.3 %right.3 = (bf16[2,128,512]{2,1,0:T(8,128)(2,1)S(1)}, bf16[2,128,512]{2,1,0:T(8,128)(2,1)S(1)}, bf16[2,128,512]{2,1,0:T(8,128)(2,1)S(1)}, bf16[2,128,512]{2,1,0:...) custom-call(s32[1]{0:T(128)} %bitcast.me_ref.refs_0_, ...), custom_call_target="tpu_custom_call" | custom-call | flops 2147483648 | bytes 4194304 | tf_op jit(solution)/shard_map/right/pallas_call | solution.py:74
  33.7 3.8 %collective-permute-start.10 = (bf16[2,128,512]{2,1,0:T(8,128)(2,1)S(1)}, bf16[2,128,512]{2,1,0:T(8,128)(2,1)S(1)}, u32[]{:S(2)}, u32[]{:S(2)}) collective-permute-start(bf16[2,128,512]{2,1,0:T(8,128)(2,1)S(1)} %get-tuple-element.58), channel_id=1, source_target_pairs={{0,4},{1,5},{2,6},{3,7},{4,0},{5,1},{6,2},{7,3},{8,12},{9,13},{10,... | collective-permute-start | bytes 786440 | tf_op jit(solution)/shard_map/ppermute | solution.py:289
  37.4 1.7 collective-permute-start.11
  39.2 14.9 %collective-permute-done.4.refs_6_ = bf16[2,128,512]{2,1,0:T(8,128)(2,1)S(1)} collective-permute-done((bf16[2,128,512]{2,1,0:T(8,128)(2,1)}, bf16[2,128,512]{2,1,0:T(8,128)(2,1)S(1)}, u32[]{:S(2)}, u32[]{:S(2)}) %collective-permute-start.4) | collective-permute-done | bytes 262176 | tf_op jit(solution)/shard_map/ppermute | solution.py:289
  54.0 8.5 %collective-permute-done.5.refs_7_ = bf16[2,128,512]{2,1,0:T(8,128)(2,1)S(1)} collective-permute-done((bf16[2,128,512]{2,1,0:T(8,128)(2,1)}, bf16[2,128,512]{2,1,0:T(8,128)(2,1)S(1)}, u32[]{:S(2)}, u32[]{:S(2)}) %collective-permute-start.5) | collective-permute-done | bytes 262176 | tf_op jit(solution)/shard_map/ppermute | solution.py:289
  62.5 11.6 %collective-permute-start.13 = (bf16[2,128,512]{2,1,0:T(8,128)(2,1)S(1)}, bf16[2,128,512]{2,1,0:T(8,128)(2,1)S(1)}, u32[]{:S(2)}, u32[]{:S(2)}) collective-permute-start(bf16[2,128,512]{2,1,0:T(8,128)(2,1)S(1)} %get-tuple-element.61), channel_id=1, source_target_pairs={{0,7},{1,6},{2,5},{3,4},{4,3},{5,2},{6,1},{7,0},{8,15},{9,14},{10,... | collective-permute-start | bytes 786440 | tf_op jit(solution)/shard_map/ppermute | solution.py:289
  74.1 3.2 %collective-permute-done.6.refs_8_ = bf16[2,128,512]{2,1,0:T(8,128)(2,1)S(1)} collective-permute-done((bf16[2,128,512]{2,1,0:T(8,128)(2,1)}, bf16[2,128,512]{2,1,0:T(8,128)(2,1)S(1)}, u32[]{:S(2)}, u32[]{:S(2)}) %collective-permute-start.6) | collective-permute-done | bytes 262176 | tf_op jit(solution)/shard_map/ppermute | solution.py:289
  77.9 5.1 %left.2 = (bf16[2,128,512]{2,1,0:T(8,128)(2,1)S(1)}, bf16[2,128,512]{2,1,0:T(8,128)(2,1)S(1)}, bf16[2,128,512]{2,1,0:T(8,128)(2,1)S(1)}, bf16[2,128,512]{2,1,0:T...) custom-call(s32[1]{0:T(128)} %bitcast.me_ref.refs_0_, ...), custom_call_target="tpu_custom_call" | custom-call | flops 4294967296 | bytes 8388608 | tf_op jit(solution)/shard_map/left/pallas_call | solution.py:121
  83.4 4.5 %collective-permute-done.11.refs_6_ = bf16[2,128,512]{2,1,0:T(8,128)(2,1)S(1)} collective-permute-done((bf16[2,128,512]{2,1,0:T(8,128)(2,1)S(1)}, bf16[2,128,512]{2,1,0:T(8,128)(2,1)S(1)}, u32[]{:S(2)}, u32[]{:S(2)}) %collective-permute-start.11) | collective-permute-done | bytes 262176 | tf_op jit(solution)/shard_map/ppermute | solution.py:289
  87.8 2.1 collective-permute-start.9
  89.9 3.5 %collective-permute-done.12.refs_7_ = bf16[2,128,512]{2,1,0:T(8,128)(2,1)S(1)} collective-permute-done((bf16[2,128,512]{2,1,0:T(8,128)(2,1)S(1)}, bf16[2,128,512]{2,1,0:T(8,128)(2,1)S(1)}, u32[]{:S(2)}, u32[]{:S(2)}) %collective-permute-start.12) | collective-permute-done | bytes 262176 | tf_op jit(solution)/shard_map/ppermute | solution.py:289
  93.4 1.2 collective-permute-start.21
  94.7 6.8 %collective-permute-done.13.refs_8_ = bf16[2,128,512]{2,1,0:T(8,128)(2,1)S(1)} collective-permute-done((bf16[2,128,512]{2,1,0:T(8,128)(2,1)S(1)}, bf16[2,128,512]{2,1,0:T(8,128)(2,1)S(1)}, u32[]{:S(2)}, u32[]{:S(2)}) %collective-permute-start.13) | collective-permute-done | bytes 262176 | tf_op jit(solution)/shard_map/ppermute | solution.py:289
  101.5 2.3 %collective-permute-start.23 = (bf16[2,128,512]{2,1,0:T(8,128)(2,1)S(1)}, bf16[2,128,512]{2,1,0:T(8,128)(2,1)S(1)}, u32[]{:S(2)}, u32[]{:S(2)}) collective-permute-start(bf16[2,128,512]{2,1,0:T(8,128)(2,1)S(1)} %get-tuple-element.72), channel_id=1, source_target_pairs={{0,3},{1,2},{2,1},{3,0},{4,7},{5,6},{6,5},{7,4},{8,11},{9,10},{10,... | collective-permute-start | bytes 786440 | tf_op jit(solution)/shard_map/ppermute | solution.py:289
  103.8 1.4 collective-permute-start.24
  105.2 1.0 collective-permute-start.25
  106.2 5.4 %collective-permute-done.21.refs_2_ = bf16[2,128,512]{2,1,0:T(8,128)(2,1)S(1)} collective-permute-done((bf16[2,128,512]{2,1,0:T(8,128)(2,1)S(1)}, bf16[2,128,512]{2,1,0:T(8,128)(2,1)S(1)}, u32[]{:S(2)}, u32[]{:S(2)}) %collective-permute-start.21) | collective-permute-done | bytes 262176 | tf_op jit(solution)/shard_map/ppermute | solution.py:289
  111.7 2.3 collective-permute-start.26
  114.4 5.8 %left.3 = (bf16[2,128,512]{2,1,0:T(8,128)(2,1)S(1)}, bf16[2,128,512]{2,1,0:T(8,128)(2,1)S(1)}, bf16[2,128,512]{2,1,0:T(8,128)(2,1)S(1)}, bf16[2,128,512]{2,1,0:T...) custom-call(s32[1]{0:T(128)} %bitcast.me_ref.refs_0_, ...), custom_call_target="tpu_custom_call" | custom-call | flops 4294967296 | bytes 8388608 | tf_op jit(solution)/shard_map/left/pallas_call | solution.py:121
  121.0 2.1 collective-permute-start.15
  123.1 2.0 collective-permute-done.25.refs_6_
  125.1 17.6 %collective-permute-done.26.refs_7_ = bf16[2,128,512]{2,1,0:T(8,128)(2,1)S(1)} collective-permute-done((bf16[2,128,512]{2,1,0:T(8,128)(2,1)S(1)}, bf16[2,128,512]{2,1,0:T(8,128)(2,1)S(1)}, u32[]{:S(2)}, u32[]{:S(2)}) %collective-permute-start.26) | collective-permute-done | bytes 262176 | tf_op jit(solution)/shard_map/ppermute | solution.py:289
  142.7 7.7 %collective-permute-done.27.refs_8_ = bf16[2,128,512]{2,1,0:T(8,128)(2,1)S(1)} collective-permute-done((bf16[2,128,512]{2,1,0:T(8,128)(2,1)S(1)}, bf16[2,128,512]{2,1,0:T(8,128)(2,1)S(1)}, u32[]{:S(2)}, u32[]{:S(2)}) %collective-permute-start.27) | collective-permute-done | bytes 262176 | tf_op jit(solution)/shard_map/ppermute | solution.py:289
  150.4 3.7 %sine_bitcast_fusion = (f32[4,128,512]{2,1,0:T(8,128)S(1)}, f32[4,128,512]{2,1,0:T(8,128)S(1)}) fusion(f32[128,4,512]{2,1,0:T(4,128)S(1)} %copy-done.27), kind=kLoop, calls=%fused_computation | loop fusion | bytes 3145728 | tf_op jit(solution)/shard_map/sin | solution.py:327
  154.1 4.1 %phase.1 = (bf16[2,1,128,512]{3,2,1,0:T(8,128)(2,1)S(1)}, bf16[2,1,128,512]{3,2,1,0:T(8,128)(2,1)S(1)}, bf16[2,1,128,512]{3,2,1,0:T(8,128)(2,1)S(1)}, bf16[2,1,1...) custom-call(s32[1]{0:T(128)} %bitcast.me_ref.refs_0_, ...), custom_call_target="tpu_custom_call" | custom-call | flops 2147483648 | bytes 4194304 | tf_op jit(solution)/shard_map/phase/pallas_call | solution.py:191
  162.4 2.7 %collective-permute-start.19 = (bf16[2,128,512]{2,1,0:T(8,128)(2,1)}, bf16[2,128,512]{2,1,0:T(8,128)(2,1)}, u32[]{:S(2)}, u32[]{:S(2)}) collective-permute-start(bf16[2,128,512]{2,1,0:T(8,128)(2,1)} %get-tuple-element.68), channel_id=1, source_target_pairs={{0,6},{1,7},{2,4},{3,5},{4,2},{5,3},{6,0},{7,1},{8,14},{9,15},{10,... | collective-permute-start | bytes 786440 | tf_op jit(solution)/shard_map/ppermute | solution.py:289
  166.4 17.2 %collective-permute-start.28 = (bf16[2,1,128,512]{3,2,1,0:T(8,128)(2,1)}, bf16[2,1,128,512]{3,2,1,0:T(8,128)(2,1)}, u32[]{:S(2)}, u32[]{:S(2)}) collective-permute-start(bf16[2,1,128,512]{3,2,1,0:T(8,128)(2,1)} %get-tuple-element.77.refs_16_), channel_id=1, source_target_pairs={{0,8},{8,16},{16,24},{1,9},{9,17},{17,25},{2,10},{10,18},{18,26},{... | collective-permute-start | bytes 786440 | tf_op jit(solution)/shard_map/ppermute | solution.py:296
  184.4 1.9 collective-permute-start.29
  187.0 2.4 %collective-permute-start.30 = (bf16[2,1,128,512]{3,2,1,0:T(8,128)(2,1)}, bf16[2,1,128,512]{3,2,1,0:T(8,128)(2,1)}, u32[]{:S(2)}, u32[]{:S(2)}) collective-permute-start(bf16[2,1,128,512]{3,2,1,0:T(8,128)(2,1)} %get-tuple-element.79.refs_18_), channel_id=1, source_target_pairs={{0,8},{8,16},{16,24},{1,9},{9,17},{17,25},{2,10},{10,18},{18,26},{... | collective-permute-start | bytes 786440 | tf_op jit(solution)/shard_map/ppermute | solution.py:296
  189.6 8.1 %collective-permute-start.31 = (bf16[2,1,128,512]{3,2,1,0:T(8,128)(2,1)}, bf16[2,1,128,512]{3,2,1,0:T(8,128)(2,1)}, u32[]{:S(2)}, u32[]{:S(2)}) collective-permute-start(bf16[2,1,128,512]{3,2,1,0:T(8,128)(2,1)} %copy-done.24), channel_id=1, source_target_pairs={{0,8},{8,16},{16,24},{1,9},{9,17},{17,25},{2,10},{10,18},{18,26},{... | collective-permute-start | bytes 786440 | tf_op jit(solution)/shard_map/ppermute | solution.py:296
  197.7 2.2 collective-permute-start.32
  199.9 1.9 collective-permute-start.33
  201.9 1.9 collective-permute-start.34
  203.8 1.9 collective-permute-start.35
  206.1 2.4 %collective-permute-done.33.refs_21_ = bf16[2,1,128,512]{3,2,1,0:T(8,128)(2,1)} collective-permute-done((bf16[2,1,128,512]{3,2,1,0:T(8,128)(2,1)}, bf16[2,1,128,512]{3,2,1,0:T(8,128)(2,1)}, u32[]{:S(2)}, u32[]{:S(2)}) %collective-permute-start.33) | collective-permute-done | bytes 262176 | tf_op jit(solution)/shard_map/ppermute | solution.py:296
  208.5 2.8 %collective-permute-done.34.refs_22_ = bf16[2,1,128,512]{3,2,1,0:T(8,128)(2,1)} collective-permute-done((bf16[2,1,128,512]{3,2,1,0:T(8,128)(2,1)}, bf16[2,1,128,512]{3,2,1,0:T(8,128)(2,1)}, u32[]{:S(2)}, u32[]{:S(2)}) %collective-permute-start.34) | collective-permute-done | bytes 262176 | tf_op jit(solution)/shard_map/ppermute | solution.py:296
  211.4 2.8 %collective-permute-done.35.refs_23_ = bf16[2,1,128,512]{3,2,1,0:T(8,128)(2,1)} collective-permute-done((bf16[2,1,128,512]{3,2,1,0:T(8,128)(2,1)}, bf16[2,1,128,512]{3,2,1,0:T(8,128)(2,1)}, u32[]{:S(2)}, u32[]{:S(2)}) %collective-permute-start.35) | collective-permute-done | bytes 262176 | tf_op jit(solution)/shard_map/ppermute | solution.py:296
  224.6 8.8 %mix.1 = bf16[128,2,4,16,128]{4,3,2,1,0:T(8,128)(2,1)} custom-call(s32[1]{0:T(128)} %bitcast.me_ref.refs_0_, f32[4,4]{1,0:T(4,128)S(1)} %get-tuple-element.88.up_ref, f32[4,4]{1,0:T(4,128)S(1)} %get-tuple-element.87.down_ref, bf16[1024,512]{1,0:T(8,128)(2,1)S(1)} %bitcast.26, f32[4,128,512]{2,1,0:T(8,128)S(1)} %get-tuple-element.86.cosine_ref, ...), custom_call_target="tpu_custom_call" | custom-call | flops 2147483648 | bytes 10485760 | tf_op jit(solution)/shard_map/mix/pallas_call | solution.py:263
  (96 shorter events, 20.3 us)
Async XLA Ops:
  5.4 7.4 %collective-permute-start = (bf16[2,128,512]{2,1,0:T(8,128)(2,1)}, bf16[2,128,512]{2,1,0:T(8,128)(2,1)S(1)}, u32[]{:S(2)}, u32[]{:S(2)}) collective-permute-start(bf16[2,128,512]{2,1,0:T(8,128)(2,1)} %get-tuple-element.47), channel_id=1, source_target_pairs={{0,1},{1,0},{2,3},{3,2},{4,5},{5,4},{6,7},{7,6},{8,9},{9,8},{10,11... | collective-permute-start | bytes 786440 | tf_op jit(solution)/shard_map/ppermute | solution.py:289
  6.7 15.0 %collective-permute-start.1 = (bf16[2,128,512]{2,1,0:T(8,128)(2,1)}, bf16[2,128,512]{2,1,0:T(8,128)(2,1)S(1)}, u32[]{:S(2)}, u32[]{:S(2)}) collective-permute-start(bf16[2,128,512]{2,1,0:T(8,128)(2,1)} %get-tuple-element.48), channel_id=1, source_target_pairs={{0,2},{1,3},{2,0},{3,1},{4,6},{5,7},{6,4},{7,5},{8,10},{9,11},{10,... | collective-permute-start | bytes 786440 | tf_op jit(solution)/shard_map/ppermute | solution.py:289
  6.8 26.8 %collective-permute-start.2 = (bf16[2,128,512]{2,1,0:T(8,128)(2,1)}, bf16[2,128,512]{2,1,0:T(8,128)(2,1)S(1)}, u32[]{:S(2)}, u32[]{:S(2)}) collective-permute-start(bf16[2,128,512]{2,1,0:T(8,128)(2,1)} %get-tuple-element.49), channel_id=1, source_target_pairs={{0,3},{1,2},{2,1},{3,0},{4,7},{5,6},{6,5},{7,4},{8,11},{9,10},{10,... | collective-permute-start | bytes 786440 | tf_op jit(solution)/shard_map/ppermute | solution.py:289
  8.1 29.4 %collective-permute-start.3 = (bf16[2,128,512]{2,1,0:T(8,128)(2,1)}, bf16[2,128,512]{2,1,0:T(8,128)(2,1)S(1)}, u32[]{:S(2)}, u32[]{:S(2)}) collective-permute-start(bf16[2,128,512]{2,1,0:T(8,128)(2,1)} %get-tuple-element.50), channel_id=1, source_target_pairs={{0,4},{1,5},{2,6},{3,7},{4,0},{5,1},{6,2},{7,3},{8,12},{9,13},{10,... | collective-permute-start | bytes 786440 | tf_op jit(solution)/shard_map/ppermute | solution.py:289
  10.4 43.7 %collective-permute-start.4 = (bf16[2,128,512]{2,1,0:T(8,128)(2,1)}, bf16[2,128,512]{2,1,0:T(8,128)(2,1)S(1)}, u32[]{:S(2)}, u32[]{:S(2)}) collective-permute-start(bf16[2,128,512]{2,1,0:T(8,128)(2,1)} %get-tuple-element.51), channel_id=1, source_target_pairs={{0,5},{1,4},{2,7},{3,6},{4,1},{5,0},{6,3},{7,2},{8,13},{9,12},{10,... | collective-permute-start | bytes 786440 | tf_op jit(solution)/shard_map/ppermute | solution.py:289
  12.8 49.7 %collective-permute-start.5 = (bf16[2,128,512]{2,1,0:T(8,128)(2,1)}, bf16[2,128,512]{2,1,0:T(8,128)(2,1)S(1)}, u32[]{:S(2)}, u32[]{:S(2)}) collective-permute-start(bf16[2,128,512]{2,1,0:T(8,128)(2,1)} %get-tuple-element.52), channel_id=1, source_target_pairs={{0,6},{1,7},{2,4},{3,5},{4,2},{5,3},{6,0},{7,1},{8,14},{9,15},{10,... | collective-permute-start | bytes 786440 | tf_op jit(solution)/shard_map/ppermute | solution.py:289
  21.7 55.6 %collective-permute-start.6 = (bf16[2,128,512]{2,1,0:T(8,128)(2,1)}, bf16[2,128,512]{2,1,0:T(8,128)(2,1)S(1)}, u32[]{:S(2)}, u32[]{:S(2)}) collective-permute-start(bf16[2,128,512]{2,1,0:T(8,128)(2,1)} %get-tuple-element.53), channel_id=1, source_target_pairs={{0,7},{1,6},{2,5},{3,4},{4,3},{5,2},{6,1},{7,0},{8,15},{9,14},{10,... | collective-permute-start | bytes 786440 | tf_op jit(solution)/shard_map/ppermute | solution.py:289
  21.7 6.5 %copy-start.1 = (bf16[2,512,512]{2,1,0:T(8,128)(2,1)S(1)}, bf16[2,512,512]{2,1,0:T(8,128)(2,1)}, u32[]{:S(2)}) copy-start(bf16[2,512,512]{2,1,0:T(8,128)(2,1)} %param.8) | copy-start | bytes 3145732
  21.7 6.5 %copy-start.26 = (bf16[2,128,512]{2,1,0:T(8,128)(2,1)S(1)}, bf16[2,128,512]{2,1,0:T(8,128)(2,1)}, u32[]{:S(2)}) copy-start(bf16[2,128,512]{2,1,0:T(8,128)(2,1)} %get-tuple-element.45.refs_0_.refs_1_) | copy-start | bytes 786436
  28.2 2.2 copy-start
  30.4 47.5 %copy-start.2 = (bf16[2048,1024]{0,1:T(8,128)(2,1)S(1)}, bf16[2048,1024]{0,1:T(8,128)(2,1)}, u32[]{:S(2)}) copy-start(bf16[2048,1024]{0,1:T(8,128)(2,1)} %copy.14) | copy-start | bytes 12582916
  33.7 49.3 %collective-permute-start.10 = (bf16[2,128,512]{2,1,0:T(8,128)(2,1)S(1)}, bf16[2,128,512]{2,1,0:T(8,128)(2,1)S(1)}, u32[]{:S(2)}, u32[]{:S(2)}) collective-permute-start(bf16[2,128,512]{2,1,0:T(8,128)(2,1)S(1)} %get-tuple-element.58), channel_id=1, source_target_pairs={{0,4},{1,5},{2,6},{3,7},{4,0},{5,1},{6,2},{7,3},{8,12},{9,13},{10,... | collective-permute-start | bytes 786440 | tf_op jit(solution)/shard_map/ppermute | solution.py:289
  37.4 50.4 %collective-permute-start.11 = (bf16[2,128,512]{2,1,0:T(8,128)(2,1)S(1)}, bf16[2,128,512]{2,1,0:T(8,128)(2,1)S(1)}, u32[]{:S(2)}, u32[]{:S(2)}) collective-permute-start(bf16[2,128,512]{2,1,0:T(8,128)(2,1)S(1)} %get-tuple-element.59), channel_id=1, source_target_pairs={{0,5},{1,4},{2,7},{3,6},{4,1},{5,0},{6,3},{7,2},{8,13},{9,12},{10,... | collective-permute-start | bytes 786440 | tf_op jit(solution)/shard_map/ppermute | solution.py:289
  54.0 39.4 %collective-permute-start.12 = (bf16[2,128,512]{2,1,0:T(8,128)(2,1)S(1)}, bf16[2,128,512]{2,1,0:T(8,128)(2,1)S(1)}, u32[]{:S(2)}, u32[]{:S(2)}) collective-permute-start(bf16[2,128,512]{2,1,0:T(8,128)(2,1)S(1)} %get-tuple-element.60), channel_id=1, source_target_pairs={{0,6},{1,7},{2,4},{3,5},{4,2},{5,3},{6,0},{7,1},{8,14},{9,15},{10,... | collective-permute-start | bytes 786440 | tf_op jit(solution)/shard_map/ppermute | solution.py:289
  62.5 39.0 %collective-permute-start.13 = (bf16[2,128,512]{2,1,0:T(8,128)(2,1)S(1)}, bf16[2,128,512]{2,1,0:T(8,128)(2,1)S(1)}, u32[]{:S(2)}, u32[]{:S(2)}) collective-permute-start(bf16[2,128,512]{2,1,0:T(8,128)(2,1)S(1)} %get-tuple-element.61), channel_id=1, source_target_pairs={{0,7},{1,6},{2,5},{3,4},{4,3},{5,2},{6,1},{7,0},{8,15},{9,14},{10,... | collective-permute-start | bytes 786440 | tf_op jit(solution)/shard_map/ppermute | solution.py:289
  77.3 24.2 %collective-permute-start.7 = (bf16[2,128,512]{2,1,0:T(8,128)(2,1)S(1)}, bf16[2,128,512]{2,1,0:T(8,128)(2,1)S(1)}, u32[]{:S(2)}, u32[]{:S(2)}) collective-permute-start(bf16[2,128,512]{2,1,0:T(8,128)(2,1)S(1)} %get-tuple-element.55), channel_id=1, source_target_pairs={{0,1},{1,0},{2,3},{3,2},{4,5},{5,4},{6,7},{7,6},{8,9},{9,8},{10,11... | collective-permute-start | bytes 786440 | tf_op jit(solution)/shard_map/ppermute | solution.py:289
  83.0 20.8 %collective-permute-start.8 = (bf16[2,128,512]{2,1,0:T(8,128)(2,1)S(1)}, bf16[2,128,512]{2,1,0:T(8,128)(2,1)S(1)}, u32[]{:S(2)}, u32[]{:S(2)}) collective-permute-start(bf16[2,128,512]{2,1,0:T(8,128)(2,1)S(1)} %get-tuple-element.56), channel_id=1, source_target_pairs={{0,2},{1,3},{2,0},{3,1},{4,6},{5,7},{6,4},{7,5},{8,10},{9,11},{10,... | collective-permute-start | bytes 786440 | tf_op jit(solution)/shard_map/ppermute | solution.py:289
  87.8 17.4 %collective-permute-start.9 = (bf16[2,128,512]{2,1,0:T(8,128)(2,1)S(1)}, bf16[2,128,512]{2,1,0:T(8,128)(2,1)S(1)}, u32[]{:S(2)}, u32[]{:S(2)}) collective-permute-start(bf16[2,128,512]{2,1,0:T(8,128)(2,1)S(1)} %get-tuple-element.57), channel_id=1, source_target_pairs={{0,3},{1,2},{2,1},{3,0},{4,7},{5,6},{6,5},{7,4},{8,11},{9,10},{10,... | collective-permute-start | bytes 786440 | tf_op jit(solution)/shard_map/ppermute | solution.py:289
  93.4 18.2 %collective-permute-start.21 = (bf16[2,128,512]{2,1,0:T(8,128)(2,1)S(1)}, bf16[2,128,512]{2,1,0:T(8,128)(2,1)S(1)}, u32[]{:S(2)}, u32[]{:S(2)}) collective-permute-start(bf16[2,128,512]{2,1,0:T(8,128)(2,1)S(1)} %get-tuple-element.70), channel_id=1, source_target_pairs={{0,1},{1,0},{2,3},{3,2},{4,5},{5,4},{6,7},{7,6},{8,9},{9,8},{10,11... | collective-permute-start | bytes 786440 | tf_op jit(solution)/shard_map/ppermute | solution.py:289
  101.5 12.5 %collective-permute-start.22 = (bf16[2,128,512]{2,1,0:T(8,128)(2,1)S(1)}, bf16[2,128,512]{2,1,0:T(8,128)(2,1)S(1)}, u32[]{:S(2)}, u32[]{:S(2)}) collective-permute-start(bf16[2,128,512]{2,1,0:T(8,128)(2,1)S(1)} %get-tuple-element.71), channel_id=1, source_target_pairs={{0,2},{1,3},{2,0},{3,1},{4,6},{5,7},{6,4},{7,5},{8,10},{9,11},{10,... | collective-permute-start | bytes 786440 | tf_op jit(solution)/shard_map/ppermute | solution.py:289
  101.5 18.7 %collective-permute-start.23 = (bf16[2,128,512]{2,1,0:T(8,128)(2,1)S(1)}, bf16[2,128,512]{2,1,0:T(8,128)(2,1)S(1)}, u32[]{:S(2)}, u32[]{:S(2)}) collective-permute-start(bf16[2,128,512]{2,1,0:T(8,128)(2,1)S(1)} %get-tuple-element.72), channel_id=1, source_target_pairs={{0,3},{1,2},{2,1},{3,0},{4,7},{5,6},{6,5},{7,4},{8,11},{9,10},{10,... | collective-permute-start | bytes 786440 | tf_op jit(solution)/shard_map/ppermute | solution.py:289
  103.8 17.1 %collective-permute-start.24 = (bf16[2,128,512]{2,1,0:T(8,128)(2,1)S(1)}, bf16[2,128,512]{2,1,0:T(8,128)(2,1)S(1)}, u32[]{:S(2)}, u32[]{:S(2)}) collective-permute-start(bf16[2,128,512]{2,1,0:T(8,128)(2,1)S(1)} %get-tuple-element.73), channel_id=1, source_target_pairs={{0,4},{1,5},{2,6},{3,7},{4,0},{5,1},{6,2},{7,3},{8,12},{9,13},{10,... | collective-permute-start | bytes 786440 | tf_op jit(solution)/shard_map/ppermute | solution.py:289
  105.2 19.9 %collective-permute-start.25 = (bf16[2,128,512]{2,1,0:T(8,128)(2,1)S(1)}, bf16[2,128,512]{2,1,0:T(8,128)(2,1)S(1)}, u32[]{:S(2)}, u32[]{:S(2)}) collective-permute-start(bf16[2,128,512]{2,1,0:T(8,128)(2,1)S(1)} %get-tuple-element.74), channel_id=1, source_target_pairs={{0,5},{1,4},{2,7},{3,6},{4,1},{5,0},{6,3},{7,2},{8,13},{9,12},{10,... | collective-permute-start | bytes 786440 | tf_op jit(solution)/shard_map/ppermute | solution.py:289
  111.7 31.1 %collective-permute-start.26 = (bf16[2,128,512]{2,1,0:T(8,128)(2,1)S(1)}, bf16[2,128,512]{2,1,0:T(8,128)(2,1)S(1)}, u32[]{:S(2)}, u32[]{:S(2)}) collective-permute-start(bf16[2,128,512]{2,1,0:T(8,128)(2,1)S(1)} %get-tuple-element.75), channel_id=1, source_target_pairs={{0,6},{1,7},{2,4},{3,5},{4,2},{5,3},{6,0},{7,1},{8,14},{9,15},{10,... | collective-permute-start | bytes 786440 | tf_op jit(solution)/shard_map/ppermute | solution.py:289
  114.0 36.4 %collective-permute-start.27 = (bf16[2,128,512]{2,1,0:T(8,128)(2,1)S(1)}, bf16[2,128,512]{2,1,0:T(8,128)(2,1)S(1)}, u32[]{:S(2)}, u32[]{:S(2)}) collective-permute-start(bf16[2,128,512]{2,1,0:T(8,128)(2,1)S(1)} %get-tuple-element.76), channel_id=1, source_target_pairs={{0,7},{1,6},{2,5},{3,4},{4,3},{5,2},{6,1},{7,0},{8,15},{9,14},{10,... | collective-permute-start | bytes 786440 | tf_op jit(solution)/shard_map/ppermute | solution.py:289
  114.4 36.0 %copy-start.27 = (f32[128,4,512]{2,1,0:T(4,128)S(1)}, f32[128,4,512]{2,1,0:T(4,128)}, u32[]{:S(2)}) copy-start(f32[128,4,512]{2,1,0:T(4,128)} %param.9) | copy-start | bytes 3145732
  120.1 38.1 %copy-start.4 = (bf16[2,128,512]{2,1,0:T(8,128)(2,1)}, bf16[2,128,512]{2,1,0:T(8,128)(2,1)S(1)}, u32[]{:S(2)}) copy-start(bf16[2,128,512]{2,1,0:T(8,128)(2,1)S(1)} %get-tuple-element.62.refs_0_) | copy-start | bytes 786436
  120.2 41.5 %collective-permute-start.14 = (bf16[2,128,512]{2,1,0:T(8,128)(2,1)S(1)}, bf16[2,128,512]{2,1,0:T(8,128)(2,1)S(1)}, u32[]{:S(2)}, u32[]{:S(2)}) collective-permute-start(bf16[2,128,512]{2,1,0:T(8,128)(2,1)S(1)} %get-tuple-element.63), channel_id=1, source_target_pairs={{0,1},{1,0},{2,3},{3,2},{4,5},{5,4},{6,7},{7,6},{8,9},{9,8},{10,11... | collective-permute-start | bytes 786440 | tf_op jit(solution)/shard_map/ppermute | solution.py:289
  121.0 44.1 %collective-permute-start.15 = (bf16[2,128,512]{2,1,0:T(8,128)(2,1)S(1)}, bf16[2,128,512]{2,1,0:T(8,128)(2,1)S(1)}, u32[]{:S(2)}, u32[]{:S(2)}) collective-permute-start(bf16[2,128,512]{2,1,0:T(8,128)(2,1)S(1)} %get-tuple-element.64), channel_id=1, source_target_pairs={{0,2},{1,3},{2,0},{3,1},{4,6},{5,7},{6,4},{7,5},{8,10},{9,11},{10,... | collective-permute-start | bytes 786440 | tf_op jit(solution)/shard_map/ppermute | solution.py:289
  125.1 40.6 %collective-permute-start.16 = (bf16[2,128,512]{2,1,0:T(8,128)(2,1)S(1)}, bf16[2,128,512]{2,1,0:T(8,128)(2,1)S(1)}, u32[]{:S(2)}, u32[]{:S(2)}) collective-permute-start(bf16[2,128,512]{2,1,0:T(8,128)(2,1)S(1)} %get-tuple-element.65), channel_id=1, source_target_pairs={{0,3},{1,2},{2,1},{3,0},{4,7},{5,6},{6,5},{7,4},{8,11},{9,10},{10,... | collective-permute-start | bytes 786440 | tf_op jit(solution)/shard_map/ppermute | solution.py:289
  142.7 41.0 %collective-permute-start.17 = (bf16[2,128,512]{2,1,0:T(8,128)(2,1)S(1)}, bf16[2,128,512]{2,1,0:T(8,128)(2,1)S(1)}, u32[]{:S(2)}, u32[]{:S(2)}) collective-permute-start(bf16[2,128,512]{2,1,0:T(8,128)(2,1)S(1)} %get-tuple-element.66), channel_id=1, source_target_pairs={{0,4},{1,5},{2,6},{3,7},{4,0},{5,1},{6,2},{7,3},{8,12},{9,13},{10,... | collective-permute-start | bytes 786440 | tf_op jit(solution)/shard_map/ppermute | solution.py:289
  150.4 35.9 %collective-permute-start.18 = (bf16[2,128,512]{2,1,0:T(8,128)(2,1)S(1)}, bf16[2,128,512]{2,1,0:T(8,128)(2,1)S(1)}, u32[]{:S(2)}, u32[]{:S(2)}) collective-permute-start(bf16[2,128,512]{2,1,0:T(8,128)(2,1)S(1)} %get-tuple-element.67), channel_id=1, source_target_pairs={{0,5},{1,4},{2,7},{3,6},{4,1},{5,0},{6,3},{7,2},{8,13},{9,12},{10,... | collective-permute-start | bytes 786440 | tf_op jit(solution)/shard_map/ppermute | solution.py:289
  154.1 35.4 %copy-start.28 = (f32[16,4]{0,1:T(4,128)S(1)}, f32[16,4]{0,1:T(4,128)}, u32[]{:S(2)}) copy-start(f32[16,4]{0,1:T(4,128)} %param.10) | copy-start | bytes 772
  154.1 60.1 %copy-start.3 = (f32[128,512]{1,0:T(8,128)S(1)}, f32[128,512]{1,0:T(8,128)}, u32[]{:S(2)}) copy-start(f32[128,512]{1,0:T(8,128)} %weight_ref.1) | copy-start | bytes 786436
  162.4 27.2 %collective-permute-start.19 = (bf16[2,128,512]{2,1,0:T(8,128)(2,1)}, bf16[2,128,512]{2,1,0:T(8,128)(2,1)}, u32[]{:S(2)}, u32[]{:S(2)}) collective-permute-start(bf16[2,128,512]{2,1,0:T(8,128)(2,1)} %get-tuple-element.68), channel_id=1, source_target_pairs={{0,6},{1,7},{2,4},{3,5},{4,2},{5,3},{6,0},{7,1},{8,14},{9,15},{10,... | collective-permute-start | bytes 786440 | tf_op jit(solution)/shard_map/ppermute | solution.py:289
  165.7 32.0 %collective-permute-start.20 = (bf16[2,128,512]{2,1,0:T(8,128)(2,1)}, bf16[2,128,512]{2,1,0:T(8,128)(2,1)}, u32[]{:S(2)}, u32[]{:S(2)}) collective-permute-start(bf16[2,128,512]{2,1,0:T(8,128)(2,1)} %get-tuple-element.69), channel_id=1, source_target_pairs={{0,7},{1,6},{2,5},{3,4},{4,3},{5,2},{6,1},{7,0},{8,15},{9,14},{10,... | collective-permute-start | bytes 786440 | tf_op jit(solution)/shard_map/ppermute | solution.py:289
  166.4 33.5 %collective-permute-start.28 = (bf16[2,1,128,512]{3,2,1,0:T(8,128)(2,1)}, bf16[2,1,128,512]{3,2,1,0:T(8,128)(2,1)}, u32[]{:S(2)}, u32[]{:S(2)}) collective-permute-start(bf16[2,1,128,512]{3,2,1,0:T(8,128)(2,1)} %get-tuple-element.77.refs_16_), channel_id=1, source_target_pairs={{0,8},{8,16},{16,24},{1,9},{9,17},{17,25},{2,10},{10,18},{18,26},{... | collective-permute-start | bytes 786440 | tf_op jit(solution)/shard_map/ppermute | solution.py:296
  184.4 17.5 %collective-permute-start.29 = (bf16[2,1,128,512]{3,2,1,0:T(8,128)(2,1)}, bf16[2,1,128,512]{3,2,1,0:T(8,128)(2,1)}, u32[]{:S(2)}, u32[]{:S(2)}) collective-permute-start(bf16[2,1,128,512]{3,2,1,0:T(8,128)(2,1)} %get-tuple-element.78.refs_17_), channel_id=1, source_target_pairs={{0,8},{8,16},{16,24},{1,9},{9,17},{17,25},{2,10},{10,18},{18,26},{... | collective-permute-start | bytes 786440 | tf_op jit(solution)/shard_map/ppermute | solution.py:296
  187.0 16.8 %collective-permute-start.30 = (bf16[2,1,128,512]{3,2,1,0:T(8,128)(2,1)}, bf16[2,1,128,512]{3,2,1,0:T(8,128)(2,1)}, u32[]{:S(2)}, u32[]{:S(2)}) collective-permute-start(bf16[2,1,128,512]{3,2,1,0:T(8,128)(2,1)} %get-tuple-element.79.refs_18_), channel_id=1, source_target_pairs={{0,8},{8,16},{16,24},{1,9},{9,17},{17,25},{2,10},{10,18},{18,26},{... | collective-permute-start | bytes 786440 | tf_op jit(solution)/shard_map/ppermute | solution.py:296
  189.6 16.5 %collective-permute-start.31 = (bf16[2,1,128,512]{3,2,1,0:T(8,128)(2,1)}, bf16[2,1,128,512]{3,2,1,0:T(8,128)(2,1)}, u32[]{:S(2)}, u32[]{:S(2)}) collective-permute-start(bf16[2,1,128,512]{3,2,1,0:T(8,128)(2,1)} %copy-done.24), channel_id=1, source_target_pairs={{0,8},{8,16},{16,24},{1,9},{9,17},{17,25},{2,10},{10,18},{18,26},{... | collective-permute-start | bytes 786440 | tf_op jit(solution)/shard_map/ppermute | solution.py:296
  197.7 8.4 %collective-permute-start.32 = (bf16[2,1,128,512]{3,2,1,0:T(8,128)(2,1)}, bf16[2,1,128,512]{3,2,1,0:T(8,128)(2,1)}, u32[]{:S(2)}, u32[]{:S(2)}) collective-permute-start(bf16[2,1,128,512]{3,2,1,0:T(8,128)(2,1)} %copy-done.16), channel_id=1, source_target_pairs={{8,0},{16,8},{24,16},{9,1},{17,9},{25,17},{10,2},{18,10},{26,18},{... | collective-permute-start | bytes 786440 | tf_op jit(solution)/shard_map/ppermute | solution.py:296
  199.9 8.6 %collective-permute-start.33 = (bf16[2,1,128,512]{3,2,1,0:T(8,128)(2,1)}, bf16[2,1,128,512]{3,2,1,0:T(8,128)(2,1)}, u32[]{:S(2)}, u32[]{:S(2)}) collective-permute-start(bf16[2,1,128,512]{3,2,1,0:T(8,128)(2,1)} %copy-done.18), channel_id=1, source_target_pairs={{8,0},{16,8},{24,16},{9,1},{17,9},{25,17},{10,2},{18,10},{26,18},{... | collective-permute-start | bytes 786440 | tf_op jit(solution)/shard_map/ppermute | solution.py:296
  201.9 9.5 %collective-permute-start.34 = (bf16[2,1,128,512]{3,2,1,0:T(8,128)(2,1)}, bf16[2,1,128,512]{3,2,1,0:T(8,128)(2,1)}, u32[]{:S(2)}, u32[]{:S(2)}) collective-permute-start(bf16[2,1,128,512]{3,2,1,0:T(8,128)(2,1)} %copy-done.20), channel_id=1, source_target_pairs={{8,0},{16,8},{24,16},{9,1},{17,9},{25,17},{10,2},{18,10},{26,18},{... | collective-permute-start | bytes 786440 | tf_op jit(solution)/shard_map/ppermute | solution.py:296
  203.8 10.3 %collective-permute-start.35 = (bf16[2,1,128,512]{3,2,1,0:T(8,128)(2,1)}, bf16[2,1,128,512]{3,2,1,0:T(8,128)(2,1)}, u32[]{:S(2)}, u32[]{:S(2)}) collective-permute-start(bf16[2,1,128,512]{3,2,1,0:T(8,128)(2,1)} %copy-done.22), channel_id=1, source_target_pairs={{8,0},{16,8},{24,16},{9,1},{17,9},{25,17},{10,2},{18,10},{26,18},{... | collective-permute-start | bytes 786440 | tf_op jit(solution)/shard_map/ppermute | solution.py:296
  214.2 1.0 copy-start.5
  215.1 0.9 copy-start.7
  216.1 0.9 copy-start.9
  217.0 0.9 copy-start.11
  (17 other events, 13.6 us)

commit v9 on v8

--- a/solution.py
+++ b/solution.py
@@ -21,7 +21,7 @@
 
 
 def in_place(arrays):
-    return [pltpu.with_memory_space_constraint(x, pltpu.VMEM) for x in arrays]
+    return [pltpu.with_memory_space_constraint(x, pltpu.HBM) for x in arrays]
 
 
 def cost(flops, moved):
@@ -195,7 +195,7 @@
         + [AFTER] * len(after)
         + [pl.BlockSpec((kinds, block, wide), lambda i: (0, i, 0))] * ranks,
         out_specs=[pl.BlockSpec((2, share, block, width), lambda i: (0, 0, i, 0))] * count,
-        out_shape=[jax.ShapeDtypeStruct((2, share, rows, width), jnp.bfloat16)] * count,
+        out_shape=[pltpu.HBM((2, share, rows, width), jnp.bfloat16)] * count,
         scratch_shapes=[pltpu.VMEM((ranks, block, wide), jnp.bfloat16)],
         compiler_params=params(),
         cost_estimate=cost(

time: 234 us -> 224 us (0.957)
  local copies, waits for them, and re-layouts: 30.2 us -> 13.4 us
  starting transfers between devices: 79.4 us -> 85.4 us
    unnamed x60 -> x28, local copies, waits for them, and re-layouts: 19.8 us -> 3.08 us
    ppermute x8, starting transfers between devices: 37.7 us -> 43.6 us  [neighbour(): return lax.ppermute(edge, axis, pairs)]
where the time goes in v9:
time: 224 us; the launch traced here: 223 us
  waiting for transfers between devices  91.2 us (41%)
  starting transfers between devices  85.4 us (38%)
  Pallas kernels  32.8 us (15%)
  local copies, waits for them, and re-layouts  13.4 us (6%)
    ppermute x28, waiting for transfers between devices, exchanged(): result[s] = lax.ppermute(slabs[s], axis, [(i, i ^ s) for i in range(count)])  83.1 us
    ppermute x8, starting transfers between devices, neighbour(): return lax.ppermute(edge, axis, pairs)  43.6 us
    ppermute x28, starting transfers between devices, exchanged(): result[s] = lax.ppermute(slabs[s], axis, [(i, i ^ s) for i in range(count)])  41.8 us
    pallas_call x2, Pallas kernels, left_call(): pl.pallas_call(functools.partial(left_kernel, len(after), ranks), grid=(k...  10.8 us
    pallas_call x1, Pallas kernels, mix_call(): pl.pallas_call(functools.partial(mix_kernel, tuple(chosen), order), grid=...  8.99 us
    pallas_call x2, Pallas kernels, right_call(): pl.pallas_call(functools.partial(right_kernel, len(after), ranks, states)...  8.63 us
    ppermute x8, waiting for transfers between devices, neighbour(): return lax.ppermute(edge, axis, pairs)  8.07 us
    reshape x1, local copies, waits for them, and re-layouts, per_device(): first = first_propagator.reshape(2 * whole, whole).T  6.53 us
  transfers between devices with their start and end apart: 36, of which 15 were waited for; matrix products, arithmetic and copies ran while one was open for 5% of the time, Pallas kernels for 8%

profile of v9, /device:TPU:9, one launch (start us, length us, event | category | flops | bytes accessed | tf_op | source)
XLA Modules:
  0.0 223.3 jit_solution(11013994961692298343)
XLA Ops:
  0.0 5.4 %right.2 = (bf16[2,128,512]{2,1,0:T(8,128)(2,1)}, bf16[2,128,512]{2,1,0:T(8,128)(2,1)}, bf16[2,128,512]{2,1,0:T(8,128)(2,1)}, bf16[2,128,512]{2,1,0:T(8,128)(2,1...) custom-call(s32[1]{0:T(128)} %bitcast.me_ref.refs_0_, ...), custom_call_target="tpu_custom_call" | custom-call | flops 2147483648 | bytes 4194304 | tf_op jit(solution)/shard_map/right/pallas_call | solution.py:74
  5.4 1.3 collective-permute-start
  6.8 1.2 collective-permute-start.2
  8.1 2.3 %collective-permute-start.3 = (bf16[2,128,512]{2,1,0:T(8,128)(2,1)}, bf16[2,128,512]{2,1,0:T(8,128)(2,1)S(1)}, u32[]{:S(2)}, u32[]{:S(2)}) collective-permute-start(bf16[2,128,512]{2,1,0:T(8,128)(2,1)} %get-tuple-element.50), channel_id=1, source_target_pairs={{0,4},{1,5},{2,6},{3,7},{4,0},{5,1},{6,2},{7,3},{8,12},{9,13},{10,... | collective-permute-start | bytes 786440 | tf_op jit(solution)/shard_map/ppermute | solution.py:289
  10.4 1.0 collective-permute-start.4
  11.4 1.4 collective-permute-done.refs_2_
  12.8 1.3 collective-permute-start.5
  14.1 7.6 %collective-permute-done.1.refs_3_ = bf16[2,128,512]{2,1,0:T(8,128)(2,1)S(1)} collective-permute-done((bf16[2,128,512]{2,1,0:T(8,128)(2,1)}, bf16[2,128,512]{2,1,0:T(8,128)(2,1)S(1)}, u32[]{:S(2)}, u32[]{:S(2)}) %collective-permute-start.1) | collective-permute-done | bytes 262176 | tf_op jit(solution)/shard_map/ppermute | solution.py:289
  21.7 6.5 %copy.14 = bf16[2048,1024]{0,1:T(8,128)(2,1)} copy(bf16[2048,1024]{1,0:T(8,128)(2,1)} %bitcast.29) | data formatting | bytes 8388608 | tf_op jit(solution)/shard_map/reshape | solution.py:307
  28.2 2.2 copy-done
  30.4 3.3 %right.3 = (bf16[2,128,512]{2,1,0:T(8,128)(2,1)S(1)}, bf16[2,128,512]{2,1,0:T(8,128)(2,1)S(1)}, bf16[2,128,512]{2,1,0:T(8,128)(2,1)S(1)}, bf16[2,128,512]{2,1,0:...) custom-call(s32[1]{0:T(128)} %bitcast.me_ref.refs_0_, ...), custom_call_target="tpu_custom_call" | custom-call | flops 2147483648 | bytes 4194304 | tf_op jit(solution)/shard_map/right/pallas_call | solution.py:74
  33.7 3.8 %collective-permute-start.10 = (bf16[2,128,512]{2,1,0:T(8,128)(2,1)S(1)}, bf16[2,128,512]{2,1,0:T(8,128)(2,1)S(1)}, u32[]{:S(2)}, u32[]{:S(2)}) collective-permute-start(bf16[2,128,512]{2,1,0:T(8,128)(2,1)S(1)} %get-tuple-element.58), channel_id=1, source_target_pairs={{0,4},{1,5},{2,6},{3,7},{4,0},{5,1},{6,2},{7,3},{8,12},{9,13},{10,... | collective-permute-start | bytes 786440 | tf_op jit(solution)/shard_map/ppermute | solution.py:289
  37.4 1.7 collective-permute-start.11
  39.2 14.9 %collective-permute-done.4.refs_6_ = bf16[2,128,512]{2,1,0:T(8,128)(2,1)S(1)} collective-permute-done((bf16[2,128,512]{2,1,0:T(8,128)(2,1)}, bf16[2,128,512]{2,1,0:T(8,128)(2,1)S(1)}, u32[]{:S(2)}, u32[]{:S(2)}) %collective-permute-start.4) | collective-permute-done | bytes 262176 | tf_op jit(solution)/shard_map/ppermute | solution.py:289
  54.0 8.5 %collective-permute-done.5.refs_7_ = bf16[2,128,512]{2,1,0:T(8,128)(2,1)S(1)} collective-permute-done((bf16[2,128,512]{2,1,0:T(8,128)(2,1)}, bf16[2,128,512]{2,1,0:T(8,128)(2,1)S(1)}, u32[]{:S(2)}, u32[]{:S(2)}) %collective-permute-start.5) | collective-permute-done | bytes 262176 | tf_op jit(solution)/shard_map/ppermute | solution.py:289
  62.5 11.6 %collective-permute-start.13 = (bf16[2,128,512]{2,1,0:T(8,128)(2,1)S(1)}, bf16[2,128,512]{2,1,0:T(8,128)(2,1)S(1)}, u32[]{:S(2)}, u32[]{:S(2)}) collective-permute-start(bf16[2,128,512]{2,1,0:T(8,128)(2,1)S(1)} %get-tuple-element.61), channel_id=1, source_target_pairs={{0,7},{1,6},{2,5},{3,4},{4,3},{5,2},{6,1},{7,0},{8,15},{9,14},{10,... | collective-permute-start | bytes 786440 | tf_op jit(solution)/shard_map/ppermute | solution.py:289
  74.1 3.2 %collective-permute-done.6.refs_8_ = bf16[2,128,512]{2,1,0:T(8,128)(2,1)S(1)} collective-permute-done((bf16[2,128,512]{2,1,0:T(8,128)(2,1)}, bf16[2,128,512]{2,1,0:T(8,128)(2,1)S(1)}, u32[]{:S(2)}, u32[]{:S(2)}) %collective-permute-start.6) | collective-permute-done | bytes 262176 | tf_op jit(solution)/shard_map/ppermute | solution.py:289
  77.9 5.1 %left.2 = (bf16[2,128,512]{2,1,0:T(8,128)(2,1)S(1)}, bf16[2,128,512]{2,1,0:T(8,128)(2,1)S(1)}, bf16[2,128,512]{2,1,0:T(8,128)(2,1)S(1)}, bf16[2,128,512]{2,1,0:T...) custom-call(s32[1]{0:T(128)} %bitcast.me_ref.refs_0_, ...), custom_call_target="tpu_custom_call" | custom-call | flops 4294967296 | bytes 8388608 | tf_op jit(solution)/shard_map/left/pallas_call | solution.py:121
  83.4 4.5 %collective-permute-done.11.refs_6_ = bf16[2,128,512]{2,1,0:T(8,128)(2,1)S(1)} collective-permute-done((bf16[2,128,512]{2,1,0:T(8,128)(2,1)S(1)}, bf16[2,128,512]{2,1,0:T(8,128)(2,1)S(1)}, u32[]{:S(2)}, u32[]{:S(2)}) %collective-permute-start.11) | collective-permute-done | bytes 262176 | tf_op jit(solution)/shard_map/ppermute | solution.py:289
  87.8 2.1 collective-permute-start.9
  89.9 3.5 %collective-permute-done.12.refs_7_ = bf16[2,128,512]{2,1,0:T(8,128)(2,1)S(1)} collective-permute-done((bf16[2,128,512]{2,1,0:T(8,128)(2,1)S(1)}, bf16[2,128,512]{2,1,0:T(8,128)(2,1)S(1)}, u32[]{:S(2)}, u32[]{:S(2)}) %collective-permute-start.12) | collective-permute-done | bytes 262176 | tf_op jit(solution)/shard_map/ppermute | solution.py:289
  93.4 1.2 collective-permute-start.21
  94.7 6.8 %collective-permute-done.13.refs_8_ = bf16[2,128,512]{2,1,0:T(8,128)(2,1)S(1)} collective-permute-done((bf16[2,128,512]{2,1,0:T(8,128)(2,1)S(1)}, bf16[2,128,512]{2,1,0:T(8,128)(2,1)S(1)}, u32[]{:S(2)}, u32[]{:S(2)}) %collective-permute-start.13) | collective-permute-done | bytes 262176 | tf_op jit(solution)/shard_map/ppermute | solution.py:289
  101.5 2.3 %collective-permute-start.23 = (bf16[2,128,512]{2,1,0:T(8,128)(2,1)S(1)}, bf16[2,128,512]{2,1,0:T(8,128)(2,1)S(1)}, u32[]{:S(2)}, u32[]{:S(2)}) collective-permute-start(bf16[2,128,512]{2,1,0:T(8,128)(2,1)S(1)} %get-tuple-element.72), channel_id=1, source_target_pairs={{0,3},{1,2},{2,1},{3,0},{4,7},{5,6},{6,5},{7,4},{8,11},{9,10},{10,... | collective-permute-start | bytes 786440 | tf_op jit(solution)/shard_map/ppermute | solution.py:289
  103.8 1.4 collective-permute-start.24
  105.2 1.0 collective-permute-start.25
  106.2 5.4 %collective-permute-done.21.refs_2_ = bf16[2,128,512]{2,1,0:T(8,128)(2,1)S(1)} collective-permute-done((bf16[2,128,512]{2,1,0:T(8,128)(2,1)S(1)}, bf16[2,128,512]{2,1,0:T(8,128)(2,1)S(1)}, u32[]{:S(2)}, u32[]{:S(2)}) %collective-permute-start.21) | collective-permute-done | bytes 262176 | tf_op jit(solution)/shard_map/ppermute | solution.py:289
  111.7 2.3 %collective-permute-start.26 = (bf16[2,128,512]{2,1,0:T(8,128)(2,1)S(1)}, bf16[2,128,512]{2,1,0:T(8,128)(2,1)S(1)}, u32[]{:S(2)}, u32[]{:S(2)}) collective-permute-start(bf16[2,128,512]{2,1,0:T(8,128)(2,1)S(1)} %get-tuple-element.75), channel_id=1, source_target_pairs={{0,6},{1,7},{2,4},{3,5},{4,2},{5,3},{6,0},{7,1},{8,14},{9,15},{10,... | collective-permute-start | bytes 786440 | tf_op jit(solution)/shard_map/ppermute | solution.py:289
  114.4 5.8 %left.3 = (bf16[2,128,512]{2,1,0:T(8,128)(2,1)S(1)}, bf16[2,128,512]{2,1,0:T(8,128)(2,1)S(1)}, bf16[2,128,512]{2,1,0:T(8,128)(2,1)S(1)}, bf16[2,128,512]{2,1,0:T...) custom-call(s32[1]{0:T(128)} %bitcast.me_ref.refs_0_, ...), custom_call_target="tpu_custom_call" | custom-call | flops 4294967296 | bytes 8388608 | tf_op jit(solution)/shard_map/left/pallas_call | solution.py:121
  121.0 2.1 collective-permute-start.15
  123.1 2.0 collective-permute-done.25.refs_6_
  125.1 17.6 %collective-permute-done.26.refs_7_ = bf16[2,128,512]{2,1,0:T(8,128)(2,1)S(1)} collective-permute-done((bf16[2,128,512]{2,1,0:T(8,128)(2,1)S(1)}, bf16[2,128,512]{2,1,0:T(8,128)(2,1)S(1)}, u32[]{:S(2)}, u32[]{:S(2)}) %collective-permute-start.26) | collective-permute-done | bytes 262176 | tf_op jit(solution)/shard_map/ppermute | solution.py:289
  142.7 7.7 %collective-permute-done.27.refs_8_ = bf16[2,128,512]{2,1,0:T(8,128)(2,1)S(1)} collective-permute-done((bf16[2,128,512]{2,1,0:T(8,128)(2,1)S(1)}, bf16[2,128,512]{2,1,0:T(8,128)(2,1)S(1)}, u32[]{:S(2)}, u32[]{:S(2)}) %collective-permute-start.27) | collective-permute-done | bytes 262176 | tf_op jit(solution)/shard_map/ppermute | solution.py:289
  150.4 3.7 %sine_bitcast_fusion = (f32[4,128,512]{2,1,0:T(8,128)S(1)}, f32[4,128,512]{2,1,0:T(8,128)S(1)}) fusion(f32[128,4,512]{2,1,0:T(4,128)S(1)} %copy-done.6), kind=kLoop, calls=%fused_computation | loop fusion | bytes 3145728 | tf_op jit(solution)/shard_map/sin | solution.py:327
  154.1 4.3 %phase.1 = (bf16[2,1,128,512]{3,2,1,0:T(8,128)(2,1)}, bf16[2,1,128,512]{3,2,1,0:T(8,128)(2,1)}, bf16[2,1,128,512]{3,2,1,0:T(8,128)(2,1)}, bf16[2,1,128,512]{3,2,...) custom-call(s32[1]{0:T(128)} %bitcast.me_ref.refs_0_, ...), custom_call_target="tpu_custom_call" | custom-call | flops 2147483648 | bytes 4194304 | tf_op jit(solution)/shard_map/phase/pallas_call | solution.py:191
  158.4 2.7 %collective-permute-start.19 = (bf16[2,128,512]{2,1,0:T(8,128)(2,1)}, bf16[2,128,512]{2,1,0:T(8,128)(2,1)}, u32[]{:S(2)}, u32[]{:S(2)}) collective-permute-start(bf16[2,128,512]{2,1,0:T(8,128)(2,1)} %get-tuple-element.68), channel_id=1, source_target_pairs={{0,6},{1,7},{2,4},{3,5},{4,2},{5,3},{6,0},{7,1},{8,14},{9,15},{10,... | collective-permute-start | bytes 786440 | tf_op jit(solution)/shard_map/ppermute | solution.py:289
  161.2 19.6 %collective-permute-start.28 = (bf16[2,1,128,512]{3,2,1,0:T(8,128)(2,1)}, bf16[2,1,128,512]{3,2,1,0:T(8,128)(2,1)}, u32[]{:S(2)}, u32[]{:S(2)}) collective-permute-start(bf16[2,1,128,512]{3,2,1,0:T(8,128)(2,1)} %get-tuple-element.77.refs_16_), channel_id=1, source_target_pairs={{0,8},{8,16},{16,24},{1,9},{9,17},{17,25},{2,10},{10,18},{18,26},{... | collective-permute-start | bytes 786440 | tf_op jit(solution)/shard_map/ppermute | solution.py:296
  180.9 1.9 collective-permute-start.29
  183.5 8.9 %collective-permute-start.30 = (bf16[2,1,128,512]{3,2,1,0:T(8,128)(2,1)}, bf16[2,1,128,512]{3,2,1,0:T(8,128)(2,1)}, u32[]{:S(2)}, u32[]{:S(2)}) collective-permute-start(bf16[2,1,128,512]{3,2,1,0:T(8,128)(2,1)} %get-tuple-element.79.refs_18_), channel_id=1, source_target_pairs={{0,8},{8,16},{16,24},{1,9},{9,17},{17,25},{2,10},{10,18},{18,26},{... | collective-permute-start | bytes 786440 | tf_op jit(solution)/shard_map/ppermute | solution.py:296
  192.5 5.2 %collective-permute-start.31 = (bf16[2,1,128,512]{3,2,1,0:T(8,128)(2,1)}, bf16[2,1,128,512]{3,2,1,0:T(8,128)(2,1)}, u32[]{:S(2)}, u32[]{:S(2)}) collective-permute-start(bf16[2,1,128,512]{3,2,1,0:T(8,128)(2,1)} %get-tuple-element.80.refs_19_), channel_id=1, source_target_pairs={{0,8},{8,16},{16,24},{1,9},{9,17},{17,25},{2,10},{10,18},{18,26},{... | collective-permute-start | bytes 786440 | tf_op jit(solution)/shard_map/ppermute | solution.py:296
  197.7 2.2 collective-permute-start.32
  199.9 1.9 collective-permute-start.33
  201.9 1.9 collective-permute-start.34
  203.8 1.9 collective-permute-start.35
  206.1 2.4 %collective-permute-done.33.refs_21_ = bf16[2,1,128,512]{3,2,1,0:T(8,128)(2,1)} collective-permute-done((bf16[2,1,128,512]{3,2,1,0:T(8,128)(2,1)}, bf16[2,1,128,512]{3,2,1,0:T(8,128)(2,1)}, u32[]{:S(2)}, u32[]{:S(2)}) %collective-permute-start.33) | collective-permute-done | bytes 262176 | tf_op jit(solution)/shard_map/ppermute | solution.py:296
  208.5 2.8 %collective-permute-done.34.refs_22_ = bf16[2,1,128,512]{3,2,1,0:T(8,128)(2,1)} collective-permute-done((bf16[2,1,128,512]{3,2,1,0:T(8,128)(2,1)}, bf16[2,1,128,512]{3,2,1,0:T(8,128)(2,1)}, u32[]{:S(2)}, u32[]{:S(2)}) %collective-permute-start.34) | collective-permute-done | bytes 262176 | tf_op jit(solution)/shard_map/ppermute | solution.py:296
  211.4 2.8 %collective-permute-done.35.refs_23_ = bf16[2,1,128,512]{3,2,1,0:T(8,128)(2,1)} collective-permute-done((bf16[2,1,128,512]{3,2,1,0:T(8,128)(2,1)}, bf16[2,1,128,512]{3,2,1,0:T(8,128)(2,1)}, u32[]{:S(2)}, u32[]{:S(2)}) %collective-permute-start.35) | collective-permute-done | bytes 262176 | tf_op jit(solution)/shard_map/ppermute | solution.py:296
  214.2 9.0 %mix.1 = bf16[128,2,4,16,128]{4,3,2,1,0:T(8,128)(2,1)} custom-call(s32[1]{0:T(128)} %bitcast.me_ref.refs_0_, f32[4,4]{1,0:T(4,128)S(1)} %get-tuple-element.88.up_ref, f32[4,4]{1,0:T(4,128)S(1)} %get-tuple-element.87.down_ref, bf16[1024,512]{1,0:T(8,128)(2,1)S(1)} %bitcast.26, f32[4,128,512]{2,1,0:T(8,128)S(1)} %get-tuple-element.86.cosine_ref, ...), custom_call_target="tpu_custom_call" | custom-call | flops 2147483648 | bytes 10485760 | tf_op jit(solution)/shard_map/mix/pallas_call | solution.py:263
  (64 shorter events, 3.6 us)
Async XLA Ops:
  5.4 7.4 %collective-permute-start = (bf16[2,128,512]{2,1,0:T(8,128)(2,1)}, bf16[2,128,512]{2,1,0:T(8,128)(2,1)S(1)}, u32[]{:S(2)}, u32[]{:S(2)}) collective-permute-start(bf16[2,128,512]{2,1,0:T(8,128)(2,1)} %get-tuple-element.47), channel_id=1, source_target_pairs={{0,1},{1,0},{2,3},{3,2},{4,5},{5,4},{6,7},{7,6},{8,9},{9,8},{10,11... | collective-permute-start | bytes 786440 | tf_op jit(solution)/shard_map/ppermute | solution.py:289
  6.7 15.0 %collective-permute-start.1 = (bf16[2,128,512]{2,1,0:T(8,128)(2,1)}, bf16[2,128,512]{2,1,0:T(8,128)(2,1)S(1)}, u32[]{:S(2)}, u32[]{:S(2)}) collective-permute-start(bf16[2,128,512]{2,1,0:T(8,128)(2,1)} %get-tuple-element.48), channel_id=1, source_target_pairs={{0,2},{1,3},{2,0},{3,1},{4,6},{5,7},{6,4},{7,5},{8,10},{9,11},{10,... | collective-permute-start | bytes 786440 | tf_op jit(solution)/shard_map/ppermute | solution.py:289
  6.8 26.8 %collective-permute-start.2 = (bf16[2,128,512]{2,1,0:T(8,128)(2,1)}, bf16[2,128,512]{2,1,0:T(8,128)(2,1)S(1)}, u32[]{:S(2)}, u32[]{:S(2)}) collective-permute-start(bf16[2,128,512]{2,1,0:T(8,128)(2,1)} %get-tuple-element.49), channel_id=1, source_target_pairs={{0,3},{1,2},{2,1},{3,0},{4,7},{5,6},{6,5},{7,4},{8,11},{9,10},{10,... | collective-permute-start | bytes 786440 | tf_op jit(solution)/shard_map/ppermute | solution.py:289
  8.1 29.4 %collective-permute-start.3 = (bf16[2,128,512]{2,1,0:T(8,128)(2,1)}, bf16[2,128,512]{2,1,0:T(8,128)(2,1)S(1)}, u32[]{:S(2)}, u32[]{:S(2)}) collective-permute-start(bf16[2,128,512]{2,1,0:T(8,128)(2,1)} %get-tuple-element.50), channel_id=1, source_target_pairs={{0,4},{1,5},{2,6},{3,7},{4,0},{5,1},{6,2},{7,3},{8,12},{9,13},{10,... | collective-permute-start | bytes 786440 | tf_op jit(solution)/shard_map/ppermute | solution.py:289
  10.4 43.7 %collective-permute-start.4 = (bf16[2,128,512]{2,1,0:T(8,128)(2,1)}, bf16[2,128,512]{2,1,0:T(8,128)(2,1)S(1)}, u32[]{:S(2)}, u32[]{:S(2)}) collective-permute-start(bf16[2,128,512]{2,1,0:T(8,128)(2,1)} %get-tuple-element.51), channel_id=1, source_target_pairs={{0,5},{1,4},{2,7},{3,6},{4,1},{5,0},{6,3},{7,2},{8,13},{9,12},{10,... | collective-permute-start | bytes 786440 | tf_op jit(solution)/shard_map/ppermute | solution.py:289
  12.8 49.7 %collective-permute-start.5 = (bf16[2,128,512]{2,1,0:T(8,128)(2,1)}, bf16[2,128,512]{2,1,0:T(8,128)(2,1)S(1)}, u32[]{:S(2)}, u32[]{:S(2)}) collective-permute-start(bf16[2,128,512]{2,1,0:T(8,128)(2,1)} %get-tuple-element.52), channel_id=1, source_target_pairs={{0,6},{1,7},{2,4},{3,5},{4,2},{5,3},{6,0},{7,1},{8,14},{9,15},{10,... | collective-permute-start | bytes 786440 | tf_op jit(solution)/shard_map/ppermute | solution.py:289
  21.7 55.6 %collective-permute-start.6 = (bf16[2,128,512]{2,1,0:T(8,128)(2,1)}, bf16[2,128,512]{2,1,0:T(8,128)(2,1)S(1)}, u32[]{:S(2)}, u32[]{:S(2)}) collective-permute-start(bf16[2,128,512]{2,1,0:T(8,128)(2,1)} %get-tuple-element.53), channel_id=1, source_target_pairs={{0,7},{1,6},{2,5},{3,4},{4,3},{5,2},{6,1},{7,0},{8,15},{9,14},{10,... | collective-permute-start | bytes 786440 | tf_op jit(solution)/shard_map/ppermute | solution.py:289
  21.7 6.5 %copy-start.1 = (bf16[2,512,512]{2,1,0:T(8,128)(2,1)S(1)}, bf16[2,512,512]{2,1,0:T(8,128)(2,1)}, u32[]{:S(2)}) copy-start(bf16[2,512,512]{2,1,0:T(8,128)(2,1)} %param.8) | copy-start | bytes 3145732
  21.7 6.5 %copy-start.5 = (bf16[2,128,512]{2,1,0:T(8,128)(2,1)S(1)}, bf16[2,128,512]{2,1,0:T(8,128)(2,1)}, u32[]{:S(2)}) copy-start(bf16[2,128,512]{2,1,0:T(8,128)(2,1)} %get-tuple-element.45.refs_0_.refs_1_) | copy-start | bytes 786436
  28.2 2.2 copy-start
  30.4 47.5 %copy-start.2 = (bf16[2048,1024]{0,1:T(8,128)(2,1)S(1)}, bf16[2048,1024]{0,1:T(8,128)(2,1)}, u32[]{:S(2)}) copy-start(bf16[2048,1024]{0,1:T(8,128)(2,1)} %copy.14) | copy-start | bytes 12582916
  33.7 49.3 %collective-permute-start.10 = (bf16[2,128,512]{2,1,0:T(8,128)(2,1)S(1)}, bf16[2,128,512]{2,1,0:T(8,128)(2,1)S(1)}, u32[]{:S(2)}, u32[]{:S(2)}) collective-permute-start(bf16[2,128,512]{2,1,0:T(8,128)(2,1)S(1)} %get-tuple-element.58), channel_id=1, source_target_pairs={{0,4},{1,5},{2,6},{3,7},{4,0},{5,1},{6,2},{7,3},{8,12},{9,13},{10,... | collective-permute-start | bytes 786440 | tf_op jit(solution)/shard_map/ppermute | solution.py:289
  37.4 50.4 %collective-permute-start.11 = (bf16[2,128,512]{2,1,0:T(8,128)(2,1)S(1)}, bf16[2,128,512]{2,1,0:T(8,128)(2,1)S(1)}, u32[]{:S(2)}, u32[]{:S(2)}) collective-permute-start(bf16[2,128,512]{2,1,0:T(8,128)(2,1)S(1)} %get-tuple-element.59), channel_id=1, source_target_pairs={{0,5},{1,4},{2,7},{3,6},{4,1},{5,0},{6,3},{7,2},{8,13},{9,12},{10,... | collective-permute-start | bytes 786440 | tf_op jit(solution)/shard_map/ppermute | solution.py:289
  54.0 39.4 %collective-permute-start.12 = (bf16[2,128,512]{2,1,0:T(8,128)(2,1)S(1)}, bf16[2,128,512]{2,1,0:T(8,128)(2,1)S(1)}, u32[]{:S(2)}, u32[]{:S(2)}) collective-permute-start(bf16[2,128,512]{2,1,0:T(8,128)(2,1)S(1)} %get-tuple-element.60), channel_id=1, source_target_pairs={{0,6},{1,7},{2,4},{3,5},{4,2},{5,3},{6,0},{7,1},{8,14},{9,15},{10,... | collective-permute-start | bytes 786440 | tf_op jit(solution)/shard_map/ppermute | solution.py:289
  62.5 39.0 %collective-permute-start.13 = (bf16[2,128,512]{2,1,0:T(8,128)(2,1)S(1)}, bf16[2,128,512]{2,1,0:T(8,128)(2,1)S(1)}, u32[]{:S(2)}, u32[]{:S(2)}) collective-permute-start(bf16[2,128,512]{2,1,0:T(8,128)(2,1)S(1)} %get-tuple-element.61), channel_id=1, source_target_pairs={{0,7},{1,6},{2,5},{3,4},{4,3},{5,2},{6,1},{7,0},{8,15},{9,14},{10,... | collective-permute-start | bytes 786440 | tf_op jit(solution)/shard_map/ppermute | solution.py:289
  77.3 24.2 %collective-permute-start.7 = (bf16[2,128,512]{2,1,0:T(8,128)(2,1)S(1)}, bf16[2,128,512]{2,1,0:T(8,128)(2,1)S(1)}, u32[]{:S(2)}, u32[]{:S(2)}) collective-permute-start(bf16[2,128,512]{2,1,0:T(8,128)(2,1)S(1)} %get-tuple-element.55), channel_id=1, source_target_pairs={{0,1},{1,0},{2,3},{3,2},{4,5},{5,4},{6,7},{7,6},{8,9},{9,8},{10,11... | collective-permute-start | bytes 786440 | tf_op jit(solution)/shard_map/ppermute | solution.py:289
  83.0 20.8 %collective-permute-start.8 = (bf16[2,128,512]{2,1,0:T(8,128)(2,1)S(1)}, bf16[2,128,512]{2,1,0:T(8,128)(2,1)S(1)}, u32[]{:S(2)}, u32[]{:S(2)}) collective-permute-start(bf16[2,128,512]{2,1,0:T(8,128)(2,1)S(1)} %get-tuple-element.56), channel_id=1, source_target_pairs={{0,2},{1,3},{2,0},{3,1},{4,6},{5,7},{6,4},{7,5},{8,10},{9,11},{10,... | collective-permute-start | bytes 786440 | tf_op jit(solution)/shard_map/ppermute | solution.py:289
  87.8 17.4 %collective-permute-start.9 = (bf16[2,128,512]{2,1,0:T(8,128)(2,1)S(1)}, bf16[2,128,512]{2,1,0:T(8,128)(2,1)S(1)}, u32[]{:S(2)}, u32[]{:S(2)}) collective-permute-start(bf16[2,128,512]{2,1,0:T(8,128)(2,1)S(1)} %get-tuple-element.57), channel_id=1, source_target_pairs={{0,3},{1,2},{2,1},{3,0},{4,7},{5,6},{6,5},{7,4},{8,11},{9,10},{10,... | collective-permute-start | bytes 786440 | tf_op jit(solution)/shard_map/ppermute | solution.py:289
  93.4 18.2 %collective-permute-start.21 = (bf16[2,128,512]{2,1,0:T(8,128)(2,1)S(1)}, bf16[2,128,512]{2,1,0:T(8,128)(2,1)S(1)}, u32[]{:S(2)}, u32[]{:S(2)}) collective-permute-start(bf16[2,128,512]{2,1,0:T(8,128)(2,1)S(1)} %get-tuple-element.70), channel_id=1, source_target_pairs={{0,1},{1,0},{2,3},{3,2},{4,5},{5,4},{6,7},{7,6},{8,9},{9,8},{10,11... | collective-permute-start | bytes 786440 | tf_op jit(solution)/shard_map/ppermute | solution.py:289
  101.5 12.5 %collective-permute-start.22 = (bf16[2,128,512]{2,1,0:T(8,128)(2,1)S(1)}, bf16[2,128,512]{2,1,0:T(8,128)(2,1)S(1)}, u32[]{:S(2)}, u32[]{:S(2)}) collective-permute-start(bf16[2,128,512]{2,1,0:T(8,128)(2,1)S(1)} %get-tuple-element.71), channel_id=1, source_target_pairs={{0,2},{1,3},{2,0},{3,1},{4,6},{5,7},{6,4},{7,5},{8,10},{9,11},{10,... | collective-permute-start | bytes 786440 | tf_op jit(solution)/shard_map/ppermute | solution.py:289
  101.5 18.7 %collective-permute-start.23 = (bf16[2,128,512]{2,1,0:T(8,128)(2,1)S(1)}, bf16[2,128,512]{2,1,0:T(8,128)(2,1)S(1)}, u32[]{:S(2)}, u32[]{:S(2)}) collective-permute-start(bf16[2,128,512]{2,1,0:T(8,128)(2,1)S(1)} %get-tuple-element.72), channel_id=1, source_target_pairs={{0,3},{1,2},{2,1},{3,0},{4,7},{5,6},{6,5},{7,4},{8,11},{9,10},{10,... | collective-permute-start | bytes 786440 | tf_op jit(solution)/shard_map/ppermute | solution.py:289
  103.8 17.1 %collective-permute-start.24 = (bf16[2,128,512]{2,1,0:T(8,128)(2,1)S(1)}, bf16[2,128,512]{2,1,0:T(8,128)(2,1)S(1)}, u32[]{:S(2)}, u32[]{:S(2)}) collective-permute-start(bf16[2,128,512]{2,1,0:T(8,128)(2,1)S(1)} %get-tuple-element.73), channel_id=1, source_target_pairs={{0,4},{1,5},{2,6},{3,7},{4,0},{5,1},{6,2},{7,3},{8,12},{9,13},{10,... | collective-permute-start | bytes 786440 | tf_op jit(solution)/shard_map/ppermute | solution.py:289
  105.2 19.9 %collective-permute-start.25 = (bf16[2,128,512]{2,1,0:T(8,128)(2,1)S(1)}, bf16[2,128,512]{2,1,0:T(8,128)(2,1)S(1)}, u32[]{:S(2)}, u32[]{:S(2)}) collective-permute-start(bf16[2,128,512]{2,1,0:T(8,128)(2,1)S(1)} %get-tuple-element.74), channel_id=1, source_target_pairs={{0,5},{1,4},{2,7},{3,6},{4,1},{5,0},{6,3},{7,2},{8,13},{9,12},{10,... | collective-permute-start | bytes 786440 | tf_op jit(solution)/shard_map/ppermute | solution.py:289
  111.7 31.1 %collective-permute-start.26 = (bf16[2,128,512]{2,1,0:T(8,128)(2,1)S(1)}, bf16[2,128,512]{2,1,0:T(8,128)(2,1)S(1)}, u32[]{:S(2)}, u32[]{:S(2)}) collective-permute-start(bf16[2,128,512]{2,1,0:T(8,128)(2,1)S(1)} %get-tuple-element.75), channel_id=1, source_target_pairs={{0,6},{1,7},{2,4},{3,5},{4,2},{5,3},{6,0},{7,1},{8,14},{9,15},{10,... | collective-permute-start | bytes 786440 | tf_op jit(solution)/shard_map/ppermute | solution.py:289
  114.0 36.4 %collective-permute-start.27 = (bf16[2,128,512]{2,1,0:T(8,128)(2,1)S(1)}, bf16[2,128,512]{2,1,0:T(8,128)(2,1)S(1)}, u32[]{:S(2)}, u32[]{:S(2)}) collective-permute-start(bf16[2,128,512]{2,1,0:T(8,128)(2,1)S(1)} %get-tuple-element.76), channel_id=1, source_target_pairs={{0,7},{1,6},{2,5},{3,4},{4,3},{5,2},{6,1},{7,0},{8,15},{9,14},{10,... | collective-permute-start | bytes 786440 | tf_op jit(solution)/shard_map/ppermute | solution.py:289
  114.4 36.0 %copy-start.6 = (f32[128,4,512]{2,1,0:T(4,128)S(1)}, f32[128,4,512]{2,1,0:T(4,128)}, u32[]{:S(2)}) copy-start(f32[128,4,512]{2,1,0:T(4,128)} %param.9) | copy-start | bytes 3145732
  120.1 38.3 %copy-start.4 = (bf16[2,128,512]{2,1,0:T(8,128)(2,1)}, bf16[2,128,512]{2,1,0:T(8,128)(2,1)S(1)}, u32[]{:S(2)}) copy-start(bf16[2,128,512]{2,1,0:T(8,128)(2,1)S(1)} %get-tuple-element.62.refs_0_) | copy-start | bytes 786436
  120.1 38.3 %collective-permute-start.14 = (bf16[2,128,512]{2,1,0:T(8,128)(2,1)S(1)}, bf16[2,128,512]{2,1,0:T(8,128)(2,1)S(1)}, u32[]{:S(2)}, u32[]{:S(2)}) collective-permute-start(bf16[2,128,512]{2,1,0:T(8,128)(2,1)S(1)} %get-tuple-element.63), channel_id=1, source_target_pairs={{0,1},{1,0},{2,3},{3,2},{4,5},{5,4},{6,7},{7,6},{8,9},{9,8},{10,11... | collective-permute-start | bytes 786440 | tf_op jit(solution)/shard_map/ppermute | solution.py:289
  121.0 40.2 %collective-permute-start.15 = (bf16[2,128,512]{2,1,0:T(8,128)(2,1)S(1)}, bf16[2,128,512]{2,1,0:T(8,128)(2,1)S(1)}, u32[]{:S(2)}, u32[]{:S(2)}) collective-permute-start(bf16[2,128,512]{2,1,0:T(8,128)(2,1)S(1)} %get-tuple-element.64), channel_id=1, source_target_pairs={{0,2},{1,3},{2,0},{3,1},{4,6},{5,7},{6,4},{7,5},{8,10},{9,11},{10,... | collective-permute-start | bytes 786440 | tf_op jit(solution)/shard_map/ppermute | solution.py:289
  125.1 36.1 %collective-permute-start.16 = (bf16[2,128,512]{2,1,0:T(8,128)(2,1)S(1)}, bf16[2,128,512]{2,1,0:T(8,128)(2,1)S(1)}, u32[]{:S(2)}, u32[]{:S(2)}) collective-permute-start(bf16[2,128,512]{2,1,0:T(8,128)(2,1)S(1)} %get-tuple-element.65), channel_id=1, source_target_pairs={{0,3},{1,2},{2,1},{3,0},{4,7},{5,6},{6,5},{7,4},{8,11},{9,10},{10,... | collective-permute-start | bytes 786440 | tf_op jit(solution)/shard_map/ppermute | solution.py:289
  142.7 38.1 %collective-permute-start.17 = (bf16[2,128,512]{2,1,0:T(8,128)(2,1)S(1)}, bf16[2,128,512]{2,1,0:T(8,128)(2,1)S(1)}, u32[]{:S(2)}, u32[]{:S(2)}) collective-permute-start(bf16[2,128,512]{2,1,0:T(8,128)(2,1)S(1)} %get-tuple-element.66), channel_id=1, source_target_pairs={{0,4},{1,5},{2,6},{3,7},{4,0},{5,1},{6,2},{7,3},{8,12},{9,13},{10,... | collective-permute-start | bytes 786440 | tf_op jit(solution)/shard_map/ppermute | solution.py:289
  150.4 32.4 %collective-permute-start.18 = (bf16[2,128,512]{2,1,0:T(8,128)(2,1)S(1)}, bf16[2,128,512]{2,1,0:T(8,128)(2,1)S(1)}, u32[]{:S(2)}, u32[]{:S(2)}) collective-permute-start(bf16[2,128,512]{2,1,0:T(8,128)(2,1)S(1)} %get-tuple-element.67), channel_id=1, source_target_pairs={{0,5},{1,4},{2,7},{3,6},{4,1},{5,0},{6,3},{7,2},{8,13},{9,12},{10,... | collective-permute-start | bytes 786440 | tf_op jit(solution)/shard_map/ppermute | solution.py:289
  154.1 38.3 %copy-start.12 = (f32[16,4]{0,1:T(4,128)S(1)}, f32[16,4]{0,1:T(4,128)}, u32[]{:S(2)}) copy-start(f32[16,4]{0,1:T(4,128)} %param.10) | copy-start | bytes 772
  154.1 60.1 %copy-start.3 = (f32[128,512]{1,0:T(8,128)S(1)}, f32[128,512]{1,0:T(8,128)}, u32[]{:S(2)}) copy-start(f32[128,512]{1,0:T(8,128)} %weight_ref.1) | copy-start | bytes 786436
  158.4 24.4 %copy-start.7 = (bf16[2,128,512]{2,1,0:T(8,128)(2,1)}, bf16[2,128,512]{2,1,0:T(8,128)(2,1)S(1)}, u32[]{:S(2)}) copy-start(bf16[2,128,512]{2,1,0:T(8,128)(2,1)S(1)} %collective-permute-done.14.refs_1_) | copy-start | bytes 786436
  158.4 34.1 %collective-permute-start.19 = (bf16[2,128,512]{2,1,0:T(8,128)(2,1)}, bf16[2,128,512]{2,1,0:T(8,128)(2,1)}, u32[]{:S(2)}, u32[]{:S(2)}) collective-permute-start(bf16[2,128,512]{2,1,0:T(8,128)(2,1)} %get-tuple-element.68), channel_id=1, source_target_pairs={{0,6},{1,7},{2,4},{3,5},{4,2},{5,3},{6,0},{7,1},{8,14},{9,15},{10,... | collective-permute-start | bytes 786440 | tf_op jit(solution)/shard_map/ppermute | solution.py:289
  161.2 21.7 %copy-start.8 = (bf16[2,128,512]{2,1,0:T(8,128)(2,1)}, bf16[2,128,512]{2,1,0:T(8,128)(2,1)S(1)}, u32[]{:S(2)}) copy-start(bf16[2,128,512]{2,1,0:T(8,128)(2,1)S(1)} %collective-permute-done.15.refs_2_) | copy-start | bytes 786436
  161.2 36.6 %collective-permute-start.20 = (bf16[2,128,512]{2,1,0:T(8,128)(2,1)}, bf16[2,128,512]{2,1,0:T(8,128)(2,1)}, u32[]{:S(2)}, u32[]{:S(2)}) collective-permute-start(bf16[2,128,512]{2,1,0:T(8,128)(2,1)} %get-tuple-element.69), channel_id=1, source_target_pairs={{0,7},{1,6},{2,5},{3,4},{4,3},{5,2},{6,1},{7,0},{8,15},{9,14},{10,... | collective-permute-start | bytes 786440 | tf_op jit(solution)/shard_map/ppermute | solution.py:289
  161.2 21.7 %copy-start.9 = (bf16[2,128,512]{2,1,0:T(8,128)(2,1)}, bf16[2,128,512]{2,1,0:T(8,128)(2,1)S(1)}, u32[]{:S(2)}) copy-start(bf16[2,128,512]{2,1,0:T(8,128)(2,1)S(1)} %collective-permute-done.16.refs_3_) | copy-start | bytes 786436
  161.2 38.8 %collective-permute-start.28 = (bf16[2,1,128,512]{3,2,1,0:T(8,128)(2,1)}, bf16[2,1,128,512]{3,2,1,0:T(8,128)(2,1)}, u32[]{:S(2)}, u32[]{:S(2)}) collective-permute-start(bf16[2,1,128,512]{3,2,1,0:T(8,128)(2,1)} %get-tuple-element.77.refs_16_), channel_id=1, source_target_pairs={{0,8},{8,16},{16,24},{1,9},{9,17},{17,25},{2,10},{10,18},{18,26},{... | collective-permute-start | bytes 786440 | tf_op jit(solution)/shard_map/ppermute | solution.py:296
  180.8 2.0 copy-start.10
  180.9 21.0 %collective-permute-start.29 = (bf16[2,1,128,512]{3,2,1,0:T(8,128)(2,1)}, bf16[2,1,128,512]{3,2,1,0:T(8,128)(2,1)}, u32[]{:S(2)}, u32[]{:S(2)}) collective-permute-start(bf16[2,1,128,512]{3,2,1,0:T(8,128)(2,1)} %get-tuple-element.78.refs_17_), channel_id=1, source_target_pairs={{0,8},{8,16},{16,24},{1,9},{9,17},{17,25},{2,10},{10,18},{18,26},{... | collective-permute-start | bytes 786440 | tf_op jit(solution)/shard_map/ppermute | solution.py:296
  183.5 20.3 %collective-permute-start.30 = (bf16[2,1,128,512]{3,2,1,0:T(8,128)(2,1)}, bf16[2,1,128,512]{3,2,1,0:T(8,128)(2,1)}, u32[]{:S(2)}, u32[]{:S(2)}) collective-permute-start(bf16[2,1,128,512]{3,2,1,0:T(8,128)(2,1)} %get-tuple-element.79.refs_18_), channel_id=1, source_target_pairs={{0,8},{8,16},{16,24},{1,9},{9,17},{17,25},{2,10},{10,18},{18,26},{... | collective-permute-start | bytes 786440 | tf_op jit(solution)/shard_map/ppermute | solution.py:296
  192.5 13.6 %collective-permute-start.31 = (bf16[2,1,128,512]{3,2,1,0:T(8,128)(2,1)}, bf16[2,1,128,512]{3,2,1,0:T(8,128)(2,1)}, u32[]{:S(2)}, u32[]{:S(2)}) collective-permute-start(bf16[2,1,128,512]{3,2,1,0:T(8,128)(2,1)} %get-tuple-element.80.refs_19_), channel_id=1, source_target_pairs={{0,8},{8,16},{16,24},{1,9},{9,17},{17,25},{2,10},{10,18},{18,26},{... | collective-permute-start | bytes 786440 | tf_op jit(solution)/shard_map/ppermute | solution.py:296
  197.7 8.4 %collective-permute-start.32 = (bf16[2,1,128,512]{3,2,1,0:T(8,128)(2,1)}, bf16[2,1,128,512]{3,2,1,0:T(8,128)(2,1)}, u32[]{:S(2)}, u32[]{:S(2)}) collective-permute-start(bf16[2,1,128,512]{3,2,1,0:T(8,128)(2,1)} %get-tuple-element.81.refs_12_), channel_id=1, source_target_pairs={{8,0},{16,8},{24,16},{9,1},{17,9},{25,17},{10,2},{18,10},{26,18},{... | collective-permute-start | bytes 786440 | tf_op jit(solution)/shard_map/ppermute | solution.py:296
  199.9 8.6 %collective-permute-start.33 = (bf16[2,1,128,512]{3,2,1,0:T(8,128)(2,1)}, bf16[2,1,128,512]{3,2,1,0:T(8,128)(2,1)}, u32[]{:S(2)}, u32[]{:S(2)}) collective-permute-start(bf16[2,1,128,512]{3,2,1,0:T(8,128)(2,1)} %get-tuple-element.82.refs_13_), channel_id=1, source_target_pairs={{8,0},{16,8},{24,16},{9,1},{17,9},{25,17},{10,2},{18,10},{26,18},{... | collective-permute-start | bytes 786440 | tf_op jit(solution)/shard_map/ppermute | solution.py:296
  201.9 9.5 %collective-permute-start.34 = (bf16[2,1,128,512]{3,2,1,0:T(8,128)(2,1)}, bf16[2,1,128,512]{3,2,1,0:T(8,128)(2,1)}, u32[]{:S(2)}, u32[]{:S(2)}) collective-permute-start(bf16[2,1,128,512]{3,2,1,0:T(8,128)(2,1)} %get-tuple-element.83.refs_14_), channel_id=1, source_target_pairs={{8,0},{16,8},{24,16},{9,1},{17,9},{25,17},{10,2},{18,10},{26,18},{... | collective-permute-start | bytes 786440 | tf_op jit(solution)/shard_map/ppermute | solution.py:296
  203.8 10.3 %collective-permute-start.35 = (bf16[2,1,128,512]{3,2,1,0:T(8,128)(2,1)}, bf16[2,1,128,512]{3,2,1,0:T(8,128)(2,1)}, u32[]{:S(2)}, u32[]{:S(2)}) collective-permute-start(bf16[2,1,128,512]{3,2,1,0:T(8,128)(2,1)} %get-tuple-element.84.refs_15_), channel_id=1, source_target_pairs={{8,0},{16,8},{24,16},{9,1},{17,9},{25,17},{10,2},{18,10},{26,18},{... | collective-permute-start | bytes 786440 | tf_op jit(solution)/shard_map/ppermute | solution.py:296
  (1 other events, 0.7 us)

commit v10 on v7

--- a/solution.py
+++ b/solution.py
@@ -8,14 +8,20 @@
 from jax.sharding import PartitionSpec as P
 
 LANES = 128
+ROWS = 16
 PIECES = 2
-LIMIT = 20 * 1024 * 1024
+LIMIT = 18 * 1024 * 1024
+WHOLE = 3 * LIMIT
 SMEM = pl.BlockSpec(memory_space=pltpu.SMEM)
 AFTER = pl.BlockSpec(memory_space=pl.ANY)
 
 
 def params(limit=LIMIT):
     return pltpu.CompilerParams(vmem_limit_bytes=limit)
+
+
+def in_place(arrays):
+    return [pltpu.with_memory_space_constraint(x, pltpu.HBM) for x in arrays]
 
 
 def cost(flops, moved):
@@ -212,7 +218,7 @@
         + [AFTER] * len(after)
         + slab_specs(near, ranks, kinds, block, wide),
         out_specs=[pl.BlockSpec((2, share, block, width), lambda i: (0, 0, i, 0))] * count,
-        out_shape=[jax.ShapeDtypeStruct((2, share, rows, width), jnp.bfloat16)] * count,
+        out_shape=[pltpu.HBM((2, share, rows, width), jnp.bfloat16)] * count,
         scratch_shapes=[pltpu.VMEM((ranks, block, wide), jnp.bfloat16)],
         compiler_params=params(),
         cost_estimate=cost(
@@ -232,7 +238,6 @@
     share = known[0].shape[1]
     pieces = states // share
     group = out.shape[3]
-    weight = weight_ref[...]
     others = [k for k in range(-1, blocks + 1) if k not in chosen]
     for n in range(len(chosen)):
         product = phased_product(
@@ -240,27 +245,33 @@
         )
         fresh[n] = product.reshape(2, states, rows, width)
 
-    def kinetic(k, c, j):
+    def kinetic(k, c, j, span):
         if k in chosen:
-            value = fresh[chosen.index(k), c, j]
+            value = fresh[chosen.index(k), c, j, span]
         else:
-            value = known[others.index(k) * pieces + j // share][c, j % share]
+            value = known[others.index(k) * pieces + j // share][c, j % share, span]
         return value.astype(jnp.float32)
 
-    for k in range(blocks):
-        columns = [[None] * group for _ in range(2)]
-        for j in range(states):
-            up, down = up_ref[k, j], down_ref[k, j]
-            mixed = [up * kinetic(k + 1, c, j) + down * kinetic(k - 1, c, j) for c in range(2)]
-            parts = (
-                kinetic(k, 0, j) + weight * mixed[1],
-                kinetic(k, 1, j) - weight * mixed[0],
-            )
+    for first in range(0, rows, ROWS):
+        span = slice(first, first + ROWS)
+        weight = weight_ref[span]
+        for k in range(blocks):
+            columns = [[None] * group for _ in range(2)]
+            for j in range(states):
+                up, down = up_ref[k, j], down_ref[k, j]
+                mixed = [
+                    up * kinetic(k + 1, c, j, span) + down * kinetic(k - 1, c, j, span)
+                    for c in range(2)
+                ]
+                parts = (
+                    kinetic(k, 0, j, span) + weight * mixed[1],
+                    kinetic(k, 1, j, span) - weight * mixed[0],
+                )
+                for c in range(2):
+                    for t in range(width // LANES):
+                        columns[c][t * states + j] = parts[c][:, t * LANES : (t + 1) * LANES]
             for c in range(2):
-                for t in range(width // LANES):
-                    columns[c][t * states + j] = parts[c][:, t * LANES : (t + 1) * LANES]
-        for c in range(2):
-            out[:, c, k] = jnp.stack(columns[c], 0).transpose(1, 0, 2).astype(jnp.bfloat16)
+                out[span, c, k] = jnp.stack(columns[c], 0).transpose(1, 0, 2).astype(jnp.bfloat16)
 
 
 def mix_call(me, up, down, second, cosine, sine, weight, chosen, slabs, known):
@@ -290,7 +301,7 @@
             8 * kinds * states * rows * width * width, 10 * blocks * states * rows * width
         ),
         name="mix",
-    )(me, up, down, second, cosine, sine, weight, *slabs, *known)
+    )(me, up, down, second, cosine, sine, weight, *in_place([*slabs, *known]))
 
 
 def exchanged(slabs, axis):
@@ -327,11 +338,11 @@
     edges = sorted({0, blocks - 1})
     chunks = [edges, [k for k in range(blocks) if k not in edges]]
 
-    nears = (ranks, 1)
+    nears = (1, ranks // 2)
     last = me
     lines = []
     for n, chosen in enumerate(chunks):
-        limit = LIMIT if n else 2 * LIMIT + LIMIT // 2
+        limit = LIMIT if n else WHOLE
         half = right_call([last], nears[n], me, second, view, chosen, ranks, states, piece, limit)
         last = half[0]
         lines.append(exchanged(half, "rad"))

time: 250 us -> 250 us (level)
  waiting for transfers between devices: 144 us -> 134 us
  local copies, waits for them, and re-layouts: 27.5 us -> 33.8 us
    all_to_all x2, waiting for transfers between devices: 29.6 us -> 0.01 us  [exchanged(): lax.all_to_all(slabs[0], axis, 0, 0, axis_index_groups=groups, tiled=True)]
    ppermute x14 -> x22, waiting for transfers between devices: 111 us -> 134 us  [exchanged(): result.append(lax.ppermute(slab, axis, [(i, i ^ s) for i in range(count)]))]
    ppermute x14 -> x22, starting transfers between devices: 19.3 us -> 24.8 us  [exchanged(): result.append(lax.ppermute(slab, axis, [(i, i ^ s) for i in range(count)]))]
    unnamed x58 -> x70, local copies, waits for them, and re-layouts: 17.2 us -> 22.4 us
    ppermute x4, waiting for transfers between devices: 3.54 us -> 0.01 us  [neighbour(): return lax.ppermute(edge, axis, pairs)]
    all_to_all x2, starting transfers between devices: 11.4 us -> 7.91 us  [exchanged(): lax.all_to_all(slabs[0], axis, 0, 0, axis_index_groups=groups, tiled=True)]
  transfers between devices with their start and end apart: 20 -> 28, of which waited for: 12 -> 12; matrix products, arithmetic and copies ran while one was open for 4% -> 5% of each run, Pallas kernels for 6% -> 4%
where the time goes in v10:
time: 250 us; the launch traced here: 249 us
  waiting for transfers between devices  134 us (54%)
  starting transfers between devices  45.3 us (18%)
  Pallas kernels  35.5 us (14%)
  local copies, waits for them, and re-layouts  33.8 us (14%)
    ppermute x22, waiting for transfers between devices, exchanged(): result.append(lax.ppermute(slab, axis, [(i, i ^ s) for i in range(count)]))  134 us
    ppermute x22, starting transfers between devices, exchanged(): result.append(lax.ppermute(slab, axis, [(i, i ^ s) for i in range(count)]))  24.8 us
    unnamed x70, local copies, waits for them, and re-layouts  22.4 us
    pallas_call x2, Pallas kernels, left_call(): pl.pallas_call(functools.partial(left_kernel, len(after), near, ranks), g...  13.1 us
    ppermute x4, starting transfers between devices, neighbour(): return lax.ppermute(edge, axis, pairs)  12.5 us
    pallas_call x2, Pallas kernels, right_call(): pl.pallas_call(functools.partial(right_kernel, len(after), near, ranks, s...  9.5 us
    pallas_call x1, Pallas kernels, mix_call(): pl.pallas_call(functools.partial(mix_kernel, tuple(chosen), near, ranks),...  8.86 us
    all_to_all x2, starting transfers between devices, exchanged(): lax.all_to_all(slabs[0], axis, 0, 0, axis_index_groups=groups, tiled=True)  7.91 us
  transfers between devices with their start and end apart: 28, of which 12 were waited for; matrix products, arithmetic and copies ran while one was open for 5% of the time, Pallas kernels for 4%

profile of v10, /device:TPU:9, one launch (start us, length us, event | category | flops | bytes accessed | tf_op | source)
XLA Modules:
  0.0 248.9 jit_solution(8099244280047107129)
XLA Ops:
  0.0 5.5 %right.2 = (bf16[1,2,128,512]{3,2,1,0:T(8,128)(2,1)}, bf16[2,128,512]{2,1,0:T(8,128)(2,1)}, bf16[2,128,512]{2,1,0:T(8,128)(2,1)}, bf16[2,128,512]{2,1,0:T(8,128)...) custom-call(s32[1]{0:T(128)} %bitcast.me_ref.refs_0_, ...), custom_call_target="tpu_custom_call" | custom-call | flops 2147483648 | bytes 4194304 | tf_op jit(solution)/shard_map/right/pallas_call | solution.py:92
  5.6 0.9 copy-done.5
  6.5 4.0 %right.3 = (bf16[4,2,128,512]{3,2,1,0:T(8,128)(2,1)}, bf16[2,128,512]{2,1,0:T(8,128)(2,1)S(1)}, bf16[2,128,512]{2,1,0:T(8,128)(2,1)S(1)}, bf16[2,128,512]{2,1,0:T(8,128)(2,1)S(1)}, bf16[2,128,512]{2,1,0:T(8,128)(2,1)S(1)}) custom-call(s32[1]{0:T(128)} %bitcast.me_ref.refs_0_, bf16[1024,512]{1,0:T(8,128)(2,1)S(1)} %bitcast.24, ...), custom_call_target="tpu_custom_call" | custom-call | flops 2147483648 | bytes 4194304 | tf_op jit(solution)/shard_map/right/pallas_call | solution.py:92
  10.5 3.7 %all-to-all-start = ((bf16[4,2,128,512]{3,2,1,0:T(8,128)(2,1)}), bf16[4,2,128,512]{3,2,1,0:T(8,128)(2,1)S(1)}, u32[]{:S(2)}, u32[]{:S(2)}) async-start(bf16[4,2,128,512]{3,2,1,0:T(8,128)(2,1)} %get-tuple-element.36.refs_0_), calls=%async_computation | async-start | bytes 2097152 | tf_op jit(solution)/shard_map/all_to_all | solution.py:315
  14.2 1.2 collective-permute-start
  15.6 1.2 collective-permute-start.2
  16.8 2.3 collective-permute-start.3
  19.1 0.9 collective-permute-start.4
  20.1 14.8 %collective-permute-done.refs_2_ = bf16[2,128,512]{2,1,0:T(8,128)(2,1)S(1)} collective-permute-done((bf16[2,128,512]{2,1,0:T(8,128)(2,1)}, bf16[2,128,512]{2,1,0:T(8,128)(2,1)S(1)}, u32[]{:S(2)}, u32[]{:S(2)}) %collective-permute-start) | collective-permute-done | bytes 262176 | tf_op jit(solution)/shard_map/ppermute | solution.py:317
  35.6 6.0 %collective-permute-done.1.refs_3_ = bf16[2,128,512]{2,1,0:T(8,128)(2,1)S(1)} collective-permute-done((bf16[2,128,512]{2,1,0:T(8,128)(2,1)S(1)}, bf16[2,128,512]{2,1,0:T(8,128)(2,1)S(1)}, u32[]{:S(2)}, u32[]{:S(2)}) %collective-permute-start.1) | collective-permute-done | bytes 262176 | tf_op jit(solution)/shard_map/ppermute | solution.py:317
  42.4 2.3 collective-permute-start.6
  44.6 6.5 %copy.14 = bf16[2048,1024]{0,1:T(8,128)(2,1)} copy(bf16[2048,1024]{1,0:T(8,128)(2,1)} %bitcast.29) | data formatting | bytes 8388608 | tf_op jit(solution)/shard_map/reshape | solution.py:335
  51.2 5.1 %collective-permute-start.7 = (bf16[2,128,512]{2,1,0:T(8,128)(2,1)S(1)}, bf16[2,128,512]{2,1,0:T(8,128)(2,1)S(1)}, u32[]{:S(2)}, u32[]{:S(2)}) collective-permute-start(bf16[2,128,512]{2,1,0:T(8,128)(2,1)S(1)} %get-tuple-element.45), channel_id=1, source_target_pairs={{0,4},{1,5},{2,6},{3,7},{4,0},{5,1},{6,2},{7,3},{8,12},{9,13},{10,... | collective-permute-start | bytes 786440 | tf_op jit(solution)/shard_map/ppermute | solution.py:317
  56.3 0.9 collective-permute-start.8
  57.2 31.1 %collective-permute-done.5.refs_7_ = bf16[2,128,512]{2,1,0:T(8,128)(2,1)} collective-permute-done((bf16[2,128,512]{2,1,0:T(8,128)(2,1)}, bf16[2,128,512]{2,1,0:T(8,128)(2,1)}, u32[]{:S(2)}, u32[]{:S(2)}) %collective-permute-start.5) | collective-permute-done | bytes 262176 | tf_op jit(solution)/shard_map/ppermute | solution.py:317
  88.4 4.7 %collective-permute-done.6.refs_8_ = bf16[2,128,512]{2,1,0:T(8,128)(2,1)} collective-permute-done((bf16[2,128,512]{2,1,0:T(8,128)(2,1)}, bf16[2,128,512]{2,1,0:T(8,128)(2,1)}, u32[]{:S(2)}, u32[]{:S(2)}) %collective-permute-start.6) | collective-permute-done | bytes 262176 | tf_op jit(solution)/shard_map/ppermute | solution.py:317
  93.1 2.2 copy-done.2
  95.3 0.9 copy-done.14
  96.3 0.9 copy-done.18
  97.2 7.0 %left.2 = (bf16[1,2,128,512]{3,2,1,0:T(8,128)(2,1)S(1)}, bf16[2,128,512]{2,1,0:T(8,128)(2,1)S(1)}, bf16[2,128,512]{2,1,0:T(8,128)(2,1)S(1)}, bf16[2,128,512]{2,1...) custom-call(s32[1]{0:T(128)} %bitcast.me_ref.refs_0_, ...), custom_call_target="tpu_custom_call" | custom-call | flops 4294967296 | bytes 8388608 | tf_op jit(solution)/shard_map/left/pallas_call | solution.py:143
  109.9 6.5 %collective-permute-done.9.refs_4_ = bf16[2,128,512]{2,1,0:T(8,128)(2,1)S(1)} collective-permute-done((bf16[2,128,512]{2,1,0:T(8,128)(2,1)S(1)}, bf16[2,128,512]{2,1,0:T(8,128)(2,1)S(1)}, u32[]{:S(2)}, u32[]{:S(2)}) %collective-permute-start.9) | collective-permute-done | bytes 262176 | tf_op jit(solution)/shard_map/ppermute | solution.py:317
  117.1 2.2 copy-done.3
  119.3 0.9 copy-done.20
  120.2 0.9 copy-done.24
  121.2 0.9 copy-done.26
  122.2 0.9 copy-done.28
  123.1 0.9 copy-done.30
  124.1 6.1 %left.3 = (bf16[4,2,128,512]{3,2,1,0:T(8,128)(2,1)}, bf16[2,128,512]{2,1,0:T(8,128)(2,1)}, bf16[2,128,512]{2,1,0:T(8,128)(2,1)}, bf16[2,128,512]{2,1,0:T(8,128)(2,1)S(1)}, bf16[2,128,512]{2,1,0:T(8,128)(2,1)S(1)}) custom-call(s32[1]{0:T(128)} %bitcast.me_ref.refs_0_, bf16[1024,2048]{1,0:T(8,128)(2,1)S(1)} %bitcast.28, ...), custom_call_target="tpu_custom_call" | custom-call | flops 4294967296 | bytes 8388608 | tf_op jit(solution)/shard_map/left/pallas_call | solution.py:143
  131.6 4.2 %all-to-all-start.1 = ((bf16[4,2,128,512]{3,2,1,0:T(8,128)(2,1)}), bf16[4,2,128,512]{3,2,1,0:T(8,128)(2,1)}, u32[]{:S(2)}, u32[]{:S(2)}) async-start(bf16[4,2,128,512]{3,2,1,0:T(8,128)(2,1)} %get-tuple-element.49.refs_0_), calls=%async_computation.1 | async-start | bytes 2097152 | tf_op jit(solution)/shard_map/all_to_all | solution.py:315
  136.0 2.5 %collective-permute-start.17 = (bf16[2,128,512]{2,1,0:T(8,128)(2,1)S(1)}, bf16[2,128,512]{2,1,0:T(8,128)(2,1)S(1)}, u32[]{:S(2)}, u32[]{:S(2)}) collective-permute-start(bf16[2,128,512]{2,1,0:T(8,128)(2,1)S(1)} %copy-done.12), channel_id=1, source_target_pairs={{0,3},{1,2},{2,1},{3,0},{4,7},{5,6},{6,5},{7,4},{8,11},{9,10},{10,... | collective-permute-start | bytes 786440 | tf_op jit(solution)/shard_map/ppermute | solution.py:317
  138.5 0.9 collective-permute-start.18
  139.4 1.3 collective-permute-start.19
  140.7 14.8 %collective-permute-done.15.refs_2_ = bf16[2,128,512]{2,1,0:T(8,128)(2,1)S(1)} collective-permute-done((bf16[2,128,512]{2,1,0:T(8,128)(2,1)S(1)}, bf16[2,128,512]{2,1,0:T(8,128)(2,1)S(1)}, u32[]{:S(2)}, u32[]{:S(2)}) %collective-permute-start.15) | collective-permute-done | bytes 262176 | tf_op jit(solution)/shard_map/ppermute | solution.py:317
  155.5 7.8 %collective-permute-done.16.refs_3_ = bf16[2,128,512]{2,1,0:T(8,128)(2,1)S(1)} collective-permute-done((bf16[2,128,512]{2,1,0:T(8,128)(2,1)S(1)}, bf16[2,128,512]{2,1,0:T(8,128)(2,1)S(1)}, u32[]{:S(2)}, u32[]{:S(2)}) %collective-permute-start.16) | collective-permute-done | bytes 262176 | tf_op jit(solution)/shard_map/ppermute | solution.py:317
  163.9 5.1 %collective-permute-done.17.refs_4_ = bf16[2,128,512]{2,1,0:T(8,128)(2,1)S(1)} collective-permute-done((bf16[2,128,512]{2,1,0:T(8,128)(2,1)S(1)}, bf16[2,128,512]{2,1,0:T(8,128)(2,1)S(1)}, u32[]{:S(2)}, u32[]{:S(2)}) %collective-permute-start.17) | collective-permute-done | bytes 262176 | tf_op jit(solution)/shard_map/ppermute | solution.py:317
  168.9 2.9 %collective-permute-start.11 = (bf16[2,128,512]{2,1,0:T(8,128)(2,1)}, bf16[2,128,512]{2,1,0:T(8,128)(2,1)}, u32[]{:S(2)}, u32[]{:S(2)}) collective-permute-start(bf16[2,128,512]{2,1,0:T(8,128)(2,1)} %get-tuple-element.50), channel_id=1, source_target_pairs={{0,4},{1,5},{2,6},{3,7},{4,0},{5,1},{6,2},{7,3},{8,12},{9,13},{10,... | collective-permute-start | bytes 786440 | tf_op jit(solution)/shard_map/ppermute | solution.py:317
  171.9 4.8 %sine_bitcast_fusion = (f32[4,128,512]{2,1,0:T(8,128)S(1)}, f32[4,128,512]{2,1,0:T(8,128)S(1)}) fusion(f32[128,4,512]{2,1,0:T(4,128)} %param.9), kind=kLoop, calls=%fused_computation | loop fusion | bytes 3145728 | tf_op jit(solution)/shard_map/sin | solution.py:356
  176.7 1.4 collective-permute-start.13
  178.1 24.4 %collective-permute-done.20.refs_7_ = bf16[2,128,512]{2,1,0:T(8,128)(2,1)S(1)} collective-permute-done((bf16[2,128,512]{2,1,0:T(8,128)(2,1)}, bf16[2,128,512]{2,1,0:T(8,128)(2,1)S(1)}, u32[]{:S(2)}, u32[]{:S(2)}) %collective-permute-start.20) | collective-permute-done | bytes 262176 | tf_op jit(solution)/shard_map/ppermute | solution.py:317
  202.5 4.9 %collective-permute-done.21.refs_8_ = bf16[2,128,512]{2,1,0:T(8,128)(2,1)S(1)} collective-permute-done((bf16[2,128,512]{2,1,0:T(8,128)(2,1)}, bf16[2,128,512]{2,1,0:T(8,128)(2,1)S(1)}, u32[]{:S(2)}, u32[]{:S(2)}) %collective-permute-start.21) | collective-permute-done | bytes 262176 | tf_op jit(solution)/shard_map/ppermute | solution.py:317
  207.4 0.9 copy-done.31
  208.3 4.0 %phase.1 = (bf16[2,2,128,512]{3,2,1,0:T(8,128)(2,1)}, bf16[2,2,128,512]{3,2,1,0:T(8,128)(2,1)}, bf16[2,2,128,512]{3,2,1,0:T(8,128)(2,1)}, bf16[2,2,128,512]{3,2,1,0:T(8,128)(2,1)}) custom-call(s32[1]{0:T(128)} %bitcast.me_ref.refs_0_, bf16[1024,512]{1,0:T(8,128)(2,1)S(1)} %bitcast.25, f32[4,128,512]{2,1,0:T(8,128)S(1)} %get-tuple-element.66.cosine_ref, ...), custom_call_target="tpu_custom_call" | custom-call | flops 2147483648 | bytes 4194304 | tf_op jit(solution)/shard_map/phase/pallas_call | solution.py:214
  212.3 5.5 %collective-permute-start.22 = (bf16[2,2,128,512]{3,2,1,0:T(8,128)(2,1)}, bf16[2,2,128,512]{3,2,1,0:T(8,128)(2,1)}, u32[]{:S(2)}, u32[]{:S(2)}) collective-permute-start(bf16[2,2,128,512]{3,2,1,0:T(8,128)(2,1)} %get-tuple-element.61.refs_9_), channel_id=1, source_target_pairs={{0,8},{8,16},{16,24},{1,9},{9,17},{17,25},{2,10},{10,18},{18,26},{... | collective-permute-start | bytes 1572872 | tf_op jit(solution)/shard_map/ppermute | solution.py:324
  217.8 1.9 collective-permute-start.23
  219.8 3.2 %collective-permute-start.24 = (bf16[2,2,128,512]{3,2,1,0:T(8,128)(2,1)}, bf16[2,2,128,512]{3,2,1,0:T(8,128)(2,1)}, u32[]{:S(2)}, u32[]{:S(2)}) collective-permute-start(bf16[2,2,128,512]{3,2,1,0:T(8,128)(2,1)} %get-tuple-element.63.refs_7_), channel_id=1, source_target_pairs={{8,0},{16,8},{24,16},{9,1},{17,9},{25,17},{10,2},{18,10},{26,18},{... | collective-permute-start | bytes 1572872 | tf_op jit(solution)/shard_map/ppermute | solution.py:324
  223.0 1.9 collective-permute-start.25
  226.2 13.8 %collective-permute-done.14.refs_4_ = bf16[2,128,512]{2,1,0:T(8,128)(2,1)} collective-permute-done((bf16[2,128,512]{2,1,0:T(8,128)(2,1)}, bf16[2,128,512]{2,1,0:T(8,128)(2,1)}, u32[]{:S(2)}, u32[]{:S(2)}) %collective-permute-start.14) | collective-permute-done | bytes 262176 | tf_op jit(solution)/shard_map/ppermute | solution.py:317
  240.0 8.9 %mix.1 = bf16[128,2,4,16,128]{4,3,2,1,0:T(8,128)(2,1)} custom-call(s32[1]{0:T(128)} %bitcast.me_ref.refs_0_, f32[4,4]{1,0:T(4,128)S(1)} %get-tuple-element.68.up_ref, f32[4,4]{1,0:T(4,128)S(1)} %get-tuple-element.67.down_ref, bf16[1024,512]{1,0:T(8,128)(2,1)S(1)} %bitcast.26, f32[4,128,512]{2,1,0:T(8,128)S(1)} %get-tuple-element.66.cosine_ref, ...), custom_call_target="tpu_custom_call" | custom-call | flops 2147483648 | bytes 10485760 | tf_op jit(solution)/shard_map/mix/pallas_call | solution.py:285
  (90 shorter events, 11.7 us)
Async XLA Ops:
  0.0 5.5 %copy-start = (bf16[128,2,4,4,512]{4,3,2,1,0:T(4,128)(2,1)S(1)}, bf16[128,2,4,4,512]{4,3,2,1,0:T(4,128)(2,1)}, u32[]{:S(2)}) copy-start(bf16[128,2,4,4,512]{4,3,2,1,0:T(4,128)(2,1)} %param.6) | copy-start | bytes 12582916
  0.0 5.5 %copy-start.1 = (bf16[2,512,512]{2,1,0:T(8,128)(2,1)S(1)}, bf16[2,512,512]{2,1,0:T(8,128)(2,1)}, u32[]{:S(2)}) copy-start(bf16[2,512,512]{2,1,0:T(8,128)(2,1)} %param.8) | copy-start | bytes 3145732
  5.5 1.0 copy-start.5
  6.5 8.9 %copy-start.33 = (bf16[2,128,512]{2,1,0:T(8,128)(2,1)S(1)}, bf16[2,128,512]{2,1,0:T(8,128)(2,1)}, u32[]{:S(2)}) copy-start(bf16[2,128,512]{2,1,0:T(8,128)(2,1)} %get-tuple-element.38) | copy-start | bytes 786436
  10.5 106.6 %all-to-all-start = ((bf16[4,2,128,512]{3,2,1,0:T(8,128)(2,1)}), bf16[4,2,128,512]{3,2,1,0:T(8,128)(2,1)S(1)}, u32[]{:S(2)}, u32[]{:S(2)}) async-start(bf16[4,2,128,512]{3,2,1,0:T(8,128)(2,1)} %get-tuple-element.36.refs_0_), calls=%async_computation | async-start | bytes 2097152 | tf_op jit(solution)/shard_map/all_to_all | solution.py:315
  14.2 20.7 %collective-permute-start = (bf16[2,128,512]{2,1,0:T(8,128)(2,1)}, bf16[2,128,512]{2,1,0:T(8,128)(2,1)S(1)}, u32[]{:S(2)}, u32[]{:S(2)}) collective-permute-start(bf16[2,128,512]{2,1,0:T(8,128)(2,1)} %get-tuple-element.37), channel_id=1, source_target_pairs={{0,1},{1,0},{2,3},{3,2},{4,5},{5,4},{6,7},{7,6},{8,9},{9,8},{10,11... | collective-permute-start | bytes 786440 | tf_op jit(solution)/shard_map/ppermute | solution.py:317
  15.4 26.3 %collective-permute-start.1 = (bf16[2,128,512]{2,1,0:T(8,128)(2,1)S(1)}, bf16[2,128,512]{2,1,0:T(8,128)(2,1)S(1)}, u32[]{:S(2)}, u32[]{:S(2)}) collective-permute-start(bf16[2,128,512]{2,1,0:T(8,128)(2,1)S(1)} %copy-done.33), channel_id=1, source_target_pairs={{0,2},{1,3},{2,0},{3,1},{4,6},{5,7},{6,4},{7,5},{8,10},{9,11},{10,... | collective-permute-start | bytes 786440 | tf_op jit(solution)/shard_map/ppermute | solution.py:317
  15.6 35.5 %collective-permute-start.2 = (bf16[2,128,512]{2,1,0:T(8,128)(2,1)}, bf16[2,128,512]{2,1,0:T(8,128)(2,1)}, u32[]{:S(2)}, u32[]{:S(2)}) collective-permute-start(bf16[2,128,512]{2,1,0:T(8,128)(2,1)} %get-tuple-element.39), channel_id=1, source_target_pairs={{0,3},{1,2},{2,1},{3,0},{4,7},{5,6},{6,5},{7,4},{8,11},{9,10},{10,... | collective-permute-start | bytes 786440 | tf_op jit(solution)/shard_map/ppermute | solution.py:317
  16.8 34.4 %collective-permute-start.3 = (bf16[2,128,512]{2,1,0:T(8,128)(2,1)}, bf16[2,128,512]{2,1,0:T(8,128)(2,1)}, u32[]{:S(2)}, u32[]{:S(2)}) collective-permute-start(bf16[2,128,512]{2,1,0:T(8,128)(2,1)} %get-tuple-element.40), channel_id=1, source_target_pairs={{0,4},{1,5},{2,6},{3,7},{4,0},{5,1},{6,2},{7,3},{8,12},{9,13},{10,... | collective-permute-start | bytes 786440 | tf_op jit(solution)/shard_map/ppermute | solution.py:317
  19.1 37.2 %collective-permute-start.4 = (bf16[2,128,512]{2,1,0:T(8,128)(2,1)}, bf16[2,128,512]{2,1,0:T(8,128)(2,1)}, u32[]{:S(2)}, u32[]{:S(2)}) collective-permute-start(bf16[2,128,512]{2,1,0:T(8,128)(2,1)} %get-tuple-element.41), channel_id=1, source_target_pairs={{0,5},{1,4},{2,7},{3,6},{4,1},{5,0},{6,3},{7,2},{8,13},{9,12},{10,... | collective-permute-start | bytes 786440 | tf_op jit(solution)/shard_map/ppermute | solution.py:317
  35.6 52.8 %collective-permute-start.5 = (bf16[2,128,512]{2,1,0:T(8,128)(2,1)}, bf16[2,128,512]{2,1,0:T(8,128)(2,1)}, u32[]{:S(2)}, u32[]{:S(2)}) collective-permute-start(bf16[2,128,512]{2,1,0:T(8,128)(2,1)} %get-tuple-element.42), channel_id=1, source_target_pairs={{0,6},{1,7},{2,4},{3,5},{4,2},{5,3},{6,0},{7,1},{8,14},{9,15},{10,... | collective-permute-start | bytes 786440 | tf_op jit(solution)/shard_map/ppermute | solution.py:317
  42.4 50.8 %collective-permute-start.6 = (bf16[2,128,512]{2,1,0:T(8,128)(2,1)}, bf16[2,128,512]{2,1,0:T(8,128)(2,1)}, u32[]{:S(2)}, u32[]{:S(2)}) collective-permute-start(bf16[2,128,512]{2,1,0:T(8,128)(2,1)} %get-tuple-element.43), channel_id=1, source_target_pairs={{0,7},{1,6},{2,5},{3,4},{4,3},{5,2},{6,1},{7,0},{8,15},{9,14},{10,... | collective-permute-start | bytes 786440 | tf_op jit(solution)/shard_map/ppermute | solution.py:317
  44.6 48.5 %copy-start.6 = (bf16[1,2,128,512]{3,2,1,0:T(8,128)(2,1)S(1)}, bf16[1,2,128,512]{3,2,1,0:T(8,128)(2,1)}, u32[]{:S(2)}) copy-start(bf16[1,2,128,512]{3,2,1,0:T(8,128)(2,1)} %get-tuple-element.35.refs_0_.refs_1_) | copy-start | bytes 786436
  51.1 56.7 %collective-permute-start.10 = (bf16[2,128,512]{2,1,0:T(8,128)(2,1)S(1)}, bf16[2,128,512]{2,1,0:T(8,128)(2,1)S(1)}, u32[]{:S(2)}, u32[]{:S(2)}) collective-permute-start(bf16[2,128,512]{2,1,0:T(8,128)(2,1)S(1)} %get-tuple-element.48), channel_id=1, source_target_pairs={{0,7},{1,6},{2,5},{3,4},{4,3},{5,2},{6,1},{7,0},{8,15},{9,14},{10,... | collective-permute-start | bytes 786440 | tf_op jit(solution)/shard_map/ppermute | solution.py:317
  51.2 57.3 %collective-permute-start.7 = (bf16[2,128,512]{2,1,0:T(8,128)(2,1)S(1)}, bf16[2,128,512]{2,1,0:T(8,128)(2,1)S(1)}, u32[]{:S(2)}, u32[]{:S(2)}) collective-permute-start(bf16[2,128,512]{2,1,0:T(8,128)(2,1)S(1)} %get-tuple-element.45), channel_id=1, source_target_pairs={{0,4},{1,5},{2,6},{3,7},{4,0},{5,1},{6,2},{7,3},{8,12},{9,13},{10,... | collective-permute-start | bytes 786440 | tf_op jit(solution)/shard_map/ppermute | solution.py:317
  56.3 52.9 %collective-permute-start.8 = (bf16[2,128,512]{2,1,0:T(8,128)(2,1)S(1)}, bf16[2,128,512]{2,1,0:T(8,128)(2,1)S(1)}, u32[]{:S(2)}, u32[]{:S(2)}) collective-permute-start(bf16[2,128,512]{2,1,0:T(8,128)(2,1)S(1)} %get-tuple-element.46), channel_id=1, source_target_pairs={{0,5},{1,4},{2,7},{3,6},{4,1},{5,0},{6,3},{7,2},{8,13},{9,12},{10,... | collective-permute-start | bytes 786440 | tf_op jit(solution)/shard_map/ppermute | solution.py:317
  88.4 28.0 %collective-permute-start.9 = (bf16[2,128,512]{2,1,0:T(8,128)(2,1)S(1)}, bf16[2,128,512]{2,1,0:T(8,128)(2,1)S(1)}, u32[]{:S(2)}, u32[]{:S(2)}) collective-permute-start(bf16[2,128,512]{2,1,0:T(8,128)(2,1)S(1)} %get-tuple-element.47), channel_id=1, source_target_pairs={{0,6},{1,7},{2,4},{3,5},{4,2},{5,3},{6,0},{7,1},{8,14},{9,15},{10,... | collective-permute-start | bytes 786440 | tf_op jit(solution)/shard_map/ppermute | solution.py:317
  93.1 2.2 copy-start.2
  95.3 0.9 copy-start.14
  96.3 0.9 copy-start.18
  117.1 2.2 copy-start.3
  119.3 0.9 copy-start.20
  120.2 0.9 copy-start.24
  121.2 0.9 copy-start.26
  122.1 0.9 copy-start.28
  124.0 11.8 %copy-start.22 = (bf16[2,128,512]{2,1,0:T(8,128)(2,1)S(1)}, bf16[2,128,512]{2,1,0:T(8,128)(2,1)}, u32[]{:S(2)}) copy-start(bf16[2,128,512]{2,1,0:T(8,128)(2,1)} %copy-done.21) | copy-start | bytes 786436
  124.1 11.8 %copy-start.16 = (bf16[2,128,512]{2,1,0:T(8,128)(2,1)S(1)}, bf16[2,128,512]{2,1,0:T(8,128)(2,1)}, u32[]{:S(2)}) copy-start(bf16[2,128,512]{2,1,0:T(8,128)(2,1)} %copy-done.15) | copy-start | bytes 786436
  124.1 11.9 %copy-start.12 = (bf16[2,128,512]{2,1,0:T(8,128)(2,1)S(1)}, bf16[2,128,512]{2,1,0:T(8,128)(2,1)}, u32[]{:S(2)}) copy-start(bf16[2,128,512]{2,1,0:T(8,128)(2,1)} %copy-done.11) | copy-start | bytes 786436
  124.1 14.5 %copy-start.10 = (bf16[2,128,512]{2,1,0:T(8,128)(2,1)S(1)}, bf16[2,128,512]{2,1,0:T(8,128)(2,1)}, u32[]{:S(2)}) copy-start(bf16[2,128,512]{2,1,0:T(8,128)(2,1)} %copy-done.9) | copy-start | bytes 786436
  131.6 108.4 %all-to-all-start.1 = ((bf16[4,2,128,512]{3,2,1,0:T(8,128)(2,1)}), bf16[4,2,128,512]{3,2,1,0:T(8,128)(2,1)}, u32[]{:S(2)}, u32[]{:S(2)}) async-start(bf16[4,2,128,512]{3,2,1,0:T(8,128)(2,1)} %get-tuple-element.49.refs_0_), calls=%async_computation.1 | async-start | bytes 2097152 | tf_op jit(solution)/shard_map/all_to_all | solution.py:315
  135.8 19.7 %collective-permute-start.15 = (bf16[2,128,512]{2,1,0:T(8,128)(2,1)S(1)}, bf16[2,128,512]{2,1,0:T(8,128)(2,1)S(1)}, u32[]{:S(2)}, u32[]{:S(2)}) collective-permute-start(bf16[2,128,512]{2,1,0:T(8,128)(2,1)S(1)} %copy-done.22), channel_id=1, source_target_pairs={{0,1},{1,0},{2,3},{3,2},{4,5},{5,4},{6,7},{7,6},{8,9},{9,8},{10,11... | collective-permute-start | bytes 786440 | tf_op jit(solution)/shard_map/ppermute | solution.py:317
  135.9 27.4 %collective-permute-start.16 = (bf16[2,128,512]{2,1,0:T(8,128)(2,1)S(1)}, bf16[2,128,512]{2,1,0:T(8,128)(2,1)S(1)}, u32[]{:S(2)}, u32[]{:S(2)}) collective-permute-start(bf16[2,128,512]{2,1,0:T(8,128)(2,1)S(1)} %copy-done.16), channel_id=1, source_target_pairs={{0,2},{1,3},{2,0},{3,1},{4,6},{5,7},{6,4},{7,5},{8,10},{9,11},{10,... | collective-permute-start | bytes 786440 | tf_op jit(solution)/shard_map/ppermute | solution.py:317
  136.0 32.9 %collective-permute-start.17 = (bf16[2,128,512]{2,1,0:T(8,128)(2,1)S(1)}, bf16[2,128,512]{2,1,0:T(8,128)(2,1)S(1)}, u32[]{:S(2)}, u32[]{:S(2)}) collective-permute-start(bf16[2,128,512]{2,1,0:T(8,128)(2,1)S(1)} %copy-done.12), channel_id=1, source_target_pairs={{0,3},{1,2},{2,1},{3,0},{4,7},{5,6},{6,5},{7,4},{8,11},{9,10},{10,... | collective-permute-start | bytes 786440 | tf_op jit(solution)/shard_map/ppermute | solution.py:317
  138.5 33.3 %collective-permute-start.18 = (bf16[2,128,512]{2,1,0:T(8,128)(2,1)S(1)}, bf16[2,128,512]{2,1,0:T(8,128)(2,1)S(1)}, u32[]{:S(2)}, u32[]{:S(2)}) collective-permute-start(bf16[2,128,512]{2,1,0:T(8,128)(2,1)S(1)} %copy-done.10), channel_id=1, source_target_pairs={{0,4},{1,5},{2,6},{3,7},{4,0},{5,1},{6,2},{7,3},{8,12},{9,13},{10,... | collective-permute-start | bytes 786440 | tf_op jit(solution)/shard_map/ppermute | solution.py:317
  139.4 37.3 %collective-permute-start.19 = (bf16[2,128,512]{2,1,0:T(8,128)(2,1)}, bf16[2,128,512]{2,1,0:T(8,128)(2,1)S(1)}, u32[]{:S(2)}, u32[]{:S(2)}) collective-permute-start(bf16[2,128,512]{2,1,0:T(8,128)(2,1)} %get-tuple-element.58), channel_id=1, source_target_pairs={{0,5},{1,4},{2,7},{3,6},{4,1},{5,0},{6,3},{7,2},{8,13},{9,12},{10,... | collective-permute-start | bytes 786440 | tf_op jit(solution)/shard_map/ppermute | solution.py:317
  155.5 47.0 %collective-permute-start.20 = (bf16[2,128,512]{2,1,0:T(8,128)(2,1)}, bf16[2,128,512]{2,1,0:T(8,128)(2,1)S(1)}, u32[]{:S(2)}, u32[]{:S(2)}) collective-permute-start(bf16[2,128,512]{2,1,0:T(8,128)(2,1)} %get-tuple-element.59), channel_id=1, source_target_pairs={{0,6},{1,7},{2,4},{3,5},{4,2},{5,3},{6,0},{7,1},{8,14},{9,15},{10,... | collective-permute-start | bytes 786440 | tf_op jit(solution)/shard_map/ppermute | solution.py:317
  163.3 44.1 %collective-permute-start.21 = (bf16[2,128,512]{2,1,0:T(8,128)(2,1)}, bf16[2,128,512]{2,1,0:T(8,128)(2,1)S(1)}, u32[]{:S(2)}, u32[]{:S(2)}) collective-permute-start(bf16[2,128,512]{2,1,0:T(8,128)(2,1)} %get-tuple-element.60), channel_id=1, source_target_pairs={{0,7},{1,6},{2,5},{3,4},{4,3},{5,2},{6,1},{7,0},{8,15},{9,14},{10,... | collective-permute-start | bytes 786440 | tf_op jit(solution)/shard_map/ppermute | solution.py:317
  168.9 50.8 %collective-permute-start.11 = (bf16[2,128,512]{2,1,0:T(8,128)(2,1)}, bf16[2,128,512]{2,1,0:T(8,128)(2,1)}, u32[]{:S(2)}, u32[]{:S(2)}) collective-permute-start(bf16[2,128,512]{2,1,0:T(8,128)(2,1)} %get-tuple-element.50), channel_id=1, source_target_pairs={{0,4},{1,5},{2,6},{3,7},{4,0},{5,1},{6,2},{7,3},{8,12},{9,13},{10,... | collective-permute-start | bytes 786440 | tf_op jit(solution)/shard_map/ppermute | solution.py:317
  171.8 51.1 %collective-permute-start.12 = (bf16[2,128,512]{2,1,0:T(8,128)(2,1)}, bf16[2,128,512]{2,1,0:T(8,128)(2,1)}, u32[]{:S(2)}, u32[]{:S(2)}) collective-permute-start(bf16[2,128,512]{2,1,0:T(8,128)(2,1)} %get-tuple-element.51), channel_id=1, source_target_pairs={{0,5},{1,4},{2,7},{3,6},{4,1},{5,0},{6,3},{7,2},{8,13},{9,12},{10,... | collective-permute-start | bytes 786440 | tf_op jit(solution)/shard_map/ppermute | solution.py:317
  171.9 53.0 %copy-start.32 = (f32[16,4]{0,1:T(4,128)S(1)}, f32[16,4]{0,1:T(4,128)}, u32[]{:S(2)}) copy-start(f32[16,4]{0,1:T(4,128)} %param.10) | copy-start | bytes 772
  176.7 63.3 %copy-start.4 = (f32[128,512]{1,0:T(8,128)S(1)}, f32[128,512]{1,0:T(8,128)}, u32[]{:S(2)}) copy-start(f32[128,512]{1,0:T(8,128)} %weight_ref.1) | copy-start | bytes 786436
  176.7 48.4 %collective-permute-start.13 = (bf16[2,128,512]{2,1,0:T(8,128)(2,1)}, bf16[2,128,512]{2,1,0:T(8,128)(2,1)}, u32[]{:S(2)}, u32[]{:S(2)}) collective-permute-start(bf16[2,128,512]{2,1,0:T(8,128)(2,1)} %copy-done.8), channel_id=1, source_target_pairs={{0,6},{1,7},{2,4},{3,5},{4,2},{5,3},{6,0},{7,1},{8,14},{9,15},{10,... | collective-permute-start | bytes 786440 | tf_op jit(solution)/shard_map/ppermute | solution.py:317
  207.4 1.0 copy-start.31
  212.3 27.6 %collective-permute-start.22 = (bf16[2,2,128,512]{3,2,1,0:T(8,128)(2,1)}, bf16[2,2,128,512]{3,2,1,0:T(8,128)(2,1)}, u32[]{:S(2)}, u32[]{:S(2)}) collective-permute-start(bf16[2,2,128,512]{3,2,1,0:T(8,128)(2,1)} %get-tuple-element.61.refs_9_), channel_id=1, source_target_pairs={{0,8},{8,16},{16,24},{1,9},{9,17},{17,25},{2,10},{10,18},{18,26},{... | collective-permute-start | bytes 1572872 | tf_op jit(solution)/shard_map/ppermute | solution.py:324
  217.8 22.1 %collective-permute-start.23 = (bf16[2,2,128,512]{3,2,1,0:T(8,128)(2,1)}, bf16[2,2,128,512]{3,2,1,0:T(8,128)(2,1)}, u32[]{:S(2)}, u32[]{:S(2)}) collective-permute-start(bf16[2,2,128,512]{3,2,1,0:T(8,128)(2,1)} %get-tuple-element.62.refs_10_), channel_id=1, source_target_pairs={{0,8},{8,16},{16,24},{1,9},{9,17},{17,25},{2,10},{10,18},{18,26},{... | collective-permute-start | bytes 1572872 | tf_op jit(solution)/shard_map/ppermute | solution.py:324
  219.8 20.2 %collective-permute-start.24 = (bf16[2,2,128,512]{3,2,1,0:T(8,128)(2,1)}, bf16[2,2,128,512]{3,2,1,0:T(8,128)(2,1)}, u32[]{:S(2)}, u32[]{:S(2)}) collective-permute-start(bf16[2,2,128,512]{3,2,1,0:T(8,128)(2,1)} %get-tuple-element.63.refs_7_), channel_id=1, source_target_pairs={{8,0},{16,8},{24,16},{9,1},{17,9},{25,17},{10,2},{18,10},{26,18},{... | collective-permute-start | bytes 1572872 | tf_op jit(solution)/shard_map/ppermute | solution.py:324
  223.0 17.0 %collective-permute-start.25 = (bf16[2,2,128,512]{3,2,1,0:T(8,128)(2,1)}, bf16[2,2,128,512]{3,2,1,0:T(8,128)(2,1)}, u32[]{:S(2)}, u32[]{:S(2)}) collective-permute-start(bf16[2,2,128,512]{3,2,1,0:T(8,128)(2,1)} %get-tuple-element.64.refs_8_), channel_id=1, source_target_pairs={{8,0},{16,8},{24,16},{9,1},{17,9},{25,17},{10,2},{18,10},{26,18},{... | collective-permute-start | bytes 1572872 | tf_op jit(solution)/shard_map/ppermute | solution.py:324
  225.1 14.9 %collective-permute-start.14 = (bf16[2,128,512]{2,1,0:T(8,128)(2,1)}, bf16[2,128,512]{2,1,0:T(8,128)(2,1)}, u32[]{:S(2)}, u32[]{:S(2)}) collective-permute-start(bf16[2,128,512]{2,1,0:T(8,128)(2,1)} %copy-done.7), channel_id=1, source_target_pairs={{0,7},{1,6},{2,5},{3,4},{4,3},{5,2},{6,1},{7,0},{8,15},{9,14},{10,... | collective-permute-start | bytes 786440 | tf_op jit(solution)/shard_map/ppermute | solution.py:317
  (14 other events, 10.2 us)

commit v11 on v9

--- a/solution.py
+++ b/solution.py
@@ -205,53 +205,62 @@
     )(me, second, cosine, sine, *after, *slabs)
 
 
-def mix_kernel(
-    chosen, order, me_ref, up_ref, down_ref, second_ref, cosine_ref, sine_ref, weight_ref, *refs
-):
-    ranks = len(order)
-    ins, known, (out, slabs, fresh) = refs[:ranks], refs[ranks:-3], refs[-3:]
-    blocks, states = up_ref.shape
+def coupled(kinetic, k, up_ref, down_ref, weight_ref, out):
     rows, width = weight_ref.shape
-    share = known[0].shape[1]
-    pieces = states // share
-    group = out.shape[3]
-    others = [k for k in range(-1, blocks + 1) if k not in chosen]
-    for n in range(len(chosen)):
-        product = phased_product(
-            me_ref[0], n, second_ref, cosine_ref, sine_ref, ins, order, slabs
-        )
-        fresh[n] = product.reshape(2, states, rows, width)
-
-    def kinetic(k, c, j, span):
-        if k in chosen:
-            value = fresh[chosen.index(k), c, j, span]
-        else:
-            value = known[others.index(k) * pieces + j // share][c, j % share, span]
-        return value.astype(jnp.float32)
-
+    states = up_ref.shape[1]
+    group = out.shape[2]
     for first in range(0, rows, ROWS):
         span = slice(first, first + ROWS)
         weight = weight_ref[span]
-        for k in range(blocks):
-            columns = [[None] * group for _ in range(2)]
-            for j in range(states):
-                up, down = up_ref[k, j], down_ref[k, j]
-                mixed = [
-                    up * kinetic(k + 1, c, j, span) + down * kinetic(k - 1, c, j, span)
-                    for c in range(2)
-                ]
-                parts = (
-                    kinetic(k, 0, j, span) + weight * mixed[1],
-                    kinetic(k, 1, j, span) - weight * mixed[0],
-                )
-                for c in range(2):
-                    for t in range(width // LANES):
-                        columns[c][t * states + j] = parts[c][:, t * LANES : (t + 1) * LANES]
+        columns = [[None] * group for _ in range(2)]
+        for j in range(states):
+            up, down = up_ref[k, j], down_ref[k, j]
+            here, above, below = (
+                [kinetic(n, c, j, span).astype(jnp.float32) for c in range(2)]
+                for n in (k, k + 1, k - 1)
+            )
+            mixed = [up * above[c] + down * below[c] for c in range(2)]
+            parts = here[0] + weight * mixed[1], here[1] - weight * mixed[0]
             for c in range(2):
-                out[span, c, k] = jnp.stack(columns[c], 0).transpose(1, 0, 2).astype(jnp.bfloat16)
-
-
-def mix_call(me, up, down, second, cosine, sine, weight, chosen, slabs, known):
+                for t in range(width // LANES):
+                    columns[c][t * states + j] = parts[c][:, t * LANES : (t + 1) * LANES]
+        for c in range(2):
+            out[span, c] = jnp.stack(columns[c], 0).transpose(1, 0, 2).astype(jnp.bfloat16)
+
+
+def inner_kernel(
+    order, me_ref, up_ref, down_ref, second_ref, cosine_ref, sine_ref, weight_ref, *refs
+):
+    ranks = len(order)
+    ins, known, (out, fresh, slabs) = refs[:ranks], refs[ranks:-3], refs[-3:]
+    blocks, states = up_ref.shape
+    kinds = blocks - 2
+    rows, width = weight_ref.shape
+    step = pl.program_id(1)
+
+    @pl.when(step == 0)
+    def _():
+        for n in range(kinds):
+            product = phased_product(
+                me_ref[0], n, second_ref, cosine_ref, sine_ref, ins, order, slabs
+            )
+            fresh[n] = product.reshape(2, states, rows, width)
+
+    def kinetic(k, c, j, span):
+        if 0 < k < blocks - 1:
+            return fresh[k - 1, c, j, span]
+        pieces = len(known) // 2
+        share = states // pieces
+        return known[(k > 0) * pieces + j // share][c, j % share, span]
+
+    for n in range(kinds):
+
+        @pl.when(step == n)
+        def _(n=n):
+            coupled(kinetic, n + 1, up_ref, down_ref, weight_ref, out)
+
+
+def inner_call(me, up, down, second, cosine, sine, weight, slabs, known):
     ranks = len(slabs)
     order = tuple(range(ranks))
     kinds, rows, wide = slabs[0].shape
@@ -259,27 +268,75 @@
     blocks, states = up.shape
     group = width // LANES * states
     block = rows // 4
-    table = pl.BlockSpec((states, block, width), lambda i: (0, i, 0))
+    table = pl.BlockSpec((states, block, width), lambda i, n: (0, i, 0))
     return pl.pallas_call(
-        functools.partial(mix_kernel, tuple(chosen), order),
-        grid=(rows // block,),
+        functools.partial(inner_kernel, order),
+        grid=(rows // block, kinds),
         in_specs=[SMEM] * 3
-        + [pl.BlockSpec(second.shape, lambda i: (0, 0)), table, table]
-        + [pl.BlockSpec((block, width), lambda i: (i, 0))]
-        + [pl.BlockSpec((kinds, block, wide), lambda i: (0, i, 0))] * ranks
-        + [pl.BlockSpec((2, share, block, width), lambda i: (0, 0, i, 0))] * len(known),
-        out_specs=pl.BlockSpec((block, 2, blocks, group, LANES), lambda i: (i, 0, 0, 0, 0)),
-        out_shape=jax.ShapeDtypeStruct((rows, 2, blocks, group, LANES), jnp.bfloat16),
-        scratch_shapes=[
-            pltpu.VMEM((ranks, block, wide), jnp.bfloat16),
-            pltpu.VMEM((kinds, 2, states, block, width), jnp.bfloat16),
+        + [pl.BlockSpec(second.shape, lambda i, n: (0, 0)), table, table]
+        + [pl.BlockSpec((block, width), lambda i, n: (i, 0))]
+        + [pl.BlockSpec((kinds, block, wide), lambda i, n: (0, i, 0))] * ranks
+        + [pl.BlockSpec((2, share, block, width), lambda i, n: (0, 0, i, 0))] * len(known),
+        out_specs=[
+            pl.BlockSpec((block, 2, None, group, LANES), lambda i, n: (i, 0, n + 1, 0, 0)),
+            pl.BlockSpec((kinds, 2, states, block, width), lambda i, n: (0, 0, 0, i, 0)),
         ],
+        out_shape=[
+            jax.ShapeDtypeStruct((rows, 2, blocks, group, LANES), jnp.bfloat16),
+            pltpu.HBM((kinds, 2, states, rows, width), jnp.bfloat16),
+        ],
+        scratch_shapes=[pltpu.VMEM((ranks, block, wide), jnp.bfloat16)],
         compiler_params=params(),
         cost_estimate=cost(
             8 * kinds * states * rows * width * width, 10 * blocks * states * rows * width
         ),
-        name="mix",
-    )(me, up, down, second, cosine, sine, weight, *in_place([slabs[s] for s in order] + known))
+        name="inner",
+    )(me, up, down, second, cosine, sine, weight, *in_place([*slabs, *known]))
+
+
+def edge_kernel(up_ref, down_ref, weight_ref, fresh_ref, *refs):
+    known, out = refs[:-2], refs[-1]
+    blocks, states = up_ref.shape
+    pieces = len(known) // 4
+    share = states // pieces
+    others = (-1, 0, blocks - 1, blocks)
+
+    def kinetic(k, c, j, span):
+        if 0 < k < blocks - 1:
+            return fresh_ref[0 if k == 1 else blocks - 3, c, j, span]
+        return known[others.index(k) * pieces + j // share][c, j % share, span]
+
+    for n, k in enumerate((0, blocks - 1)):
+
+        @pl.when(pl.program_id(1) == n)
+        def _(k=k):
+            coupled(kinetic, k, up_ref, down_ref, weight_ref, out)
+
+
+def edge_call(up, down, weight, fresh, known, inner):
+    kinds, _, states, rows, width = fresh.shape
+    share = known[0].shape[1]
+    _, _, blocks, group, _ = inner.shape
+    block = rows // 4
+    return pl.pallas_call(
+        edge_kernel,
+        grid=(rows // block, 2),
+        in_specs=[SMEM] * 2
+        + [pl.BlockSpec((block, width), lambda i, n: (i, 0))]
+        + [pl.BlockSpec((kinds, 2, states, block, width), lambda i, n: (0, 0, 0, i, 0))]
+        + [pl.BlockSpec((2, share, block, width), lambda i, n: (0, 0, i, 0))] * len(known)
+        + [AFTER],
+        out_specs=pl.BlockSpec(
+            (block, 2, None, group, LANES), lambda i, n: (i, 0, n * (blocks - 1), 0, 0)
+        ),
+        out_shape=jax.ShapeDtypeStruct(inner.shape, jnp.bfloat16),
+        input_output_aliases={4 + len(known): 0},
+        compiler_params=params(),
+        cost_estimate=cost(
+            20 * 2 * states * rows * width, 10 * blocks * states * rows * width
+        ),
+        name="edge",
+    )(up, down, weight, *in_place([fresh, *known]), inner)
 
 
 def exchanged(slabs, axis):
@@ -317,14 +374,14 @@
         half = right_call([last], me, second, view, chosen, ranks, states, piece, limit)
         last = half[0]
         lines.append(exchanged(half, "rad"))
+    angles = potential.transpose(1, 0, 2)
+    cosine, sine = jnp.cos(angles), jnp.sin(angles)
     backs = []
     for line in lines:
-        moved = left_call([last], me, first, line)
+        moved = left_call([last, cosine], me, first, line)
         last = moved[0]
         backs.append(exchanged(moved, "rad"))
 
-    angles = potential.transpose(1, 0, 2)
-    cosine, sine = jnp.cos(angles), jnp.sin(angles)
     edge = phase_call([last], me, second, cosine, sine, backs[0])
     low, high = edge[:PIECES], edge[-PIECES:]
     below = [neighbour(x, "hel", 1) for x in high]
@@ -339,10 +396,11 @@
     start = lax.axis_index("hel") * blocks
     up = lax.dynamic_slice_in_dim(couple_up, start, blocks, 0)
     down = lax.dynamic_slice_in_dim(couple_down, start, blocks, 0)
+    inner, fresh = inner_call(
+        me, up, down, second, cosine, sine, radial_weight, backs[1], [*low, *high]
+    )
     known = [*below, *low, *high, *above]
-    out = mix_call(
-        me, up, down, second, cosine, sine, radial_weight, chunks[1], backs[1], known
-    )
+    out = edge_call(up, down, radial_weight, fresh, known, inner)
     out = out.reshape(rows, 2, blocks, tiles, states, LANES).transpose(0, 1, 2, 4, 3, 5)
     return out.reshape(rows, 2, blocks, states, width)
 

time: 224 us -> 228 us (1.018)
  starting transfers between devices: 85.4 us -> 64.9 us
  local copies, waits for them, and re-layouts: 13.4 us -> 32.8 us
  Pallas kernels: 32.8 us -> 46.5 us
  waiting for transfers between devices: 91.2 us -> 81.8 us
    unnamed x28 -> x90, local copies, waits for them, and re-layouts: 3.08 us -> 22.4 us
    ppermute x8, starting transfers between devices: 43.6 us -> 28.9 us  [neighbour(): return lax.ppermute(edge, axis, pairs)]
    pallas_call x1 -> x2, Pallas kernels: 8.99 us -> 18.5 us  [the longest x1 10.6 us: inner_call(): pl.pallas_call(functools.partial(inner_kernel, order), grid=(rows // bloc...]
    ppermute x8, waiting for transfers between devices: 8.07 us -> 0.02 us  [neighbour(): return lax.ppermute(edge, axis, pairs)]
    ppermute x28, starting transfers between devices: 41.8 us -> 36 us  [exchanged(): result[s] = lax.ppermute(slabs[s], axis, [(i, i ^ s) for i in range(count)])]
    pallas_call x2, Pallas kernels: 10.8 us -> 13.7 us  [left_call(): pl.pallas_call(functools.partial(left_kernel, len(after), ranks), grid=(k...]
  transfers between devices with their start and end apart: 36 -> 36, of which waited for: 15 -> 11; matrix products, arithmetic and copies ran while one was open for 5% -> 5% of each run, Pallas kernels for 8% -> 15%
where the time goes in v11:
time: 228 us; the launch traced here: 226 us
  waiting for transfers between devices  81.8 us (36%)
  starting transfers between devices  64.9 us (28%)
  Pallas kernels  46.5 us (20%)
  local copies, waits for them, and re-layouts  32.8 us (14%)
    ppermute x28, waiting for transfers between devices, exchanged(): result[s] = lax.ppermute(slabs[s], axis, [(i, i ^ s) for i in range(count)])  81.8 us
    ppermute x28, starting transfers between devices, exchanged(): result[s] = lax.ppermute(slabs[s], axis, [(i, i ^ s) for i in range(count)])  36 us
    ppermute x8, starting transfers between devices, neighbour(): return lax.ppermute(edge, axis, pairs)  28.9 us
    unnamed x90, local copies, waits for them, and re-layouts  22.4 us
    pallas_call x2, Pallas kernels, left_call(): pl.pallas_call(functools.partial(left_kernel, len(after), ranks), grid=(k...  13.7 us
    pallas_call x1, Pallas kernels, inner_call(): pl.pallas_call(functools.partial(inner_kernel, order), grid=(rows // bloc...  10.6 us
    pallas_call x2, Pallas kernels, right_call(): pl.pallas_call(functools.partial(right_kernel, len(after), ranks, states)...  9.4 us
    pallas_call x1, Pallas kernels, edge_call(): pl.pallas_call(edge_kernel, grid=(rows // block, 2), in_specs=[SMEM] * 2...  7.93 us
  transfers between devices with their start and end apart: 36, of which 11 were waited for; matrix products, arithmetic and copies ran while one was open for 5% of the time, Pallas kernels for 15%

profile of v11, /device:TPU:9, one launch (start us, length us, event | category | flops | bytes accessed | tf_op | source)
XLA Modules:
  0.0 226.5 jit_solution(9287039980297200331)
XLA Ops:
  0.0 5.5 %right.2 = (bf16[2,128,512]{2,1,0:T(8,128)(2,1)}, bf16[2,128,512]{2,1,0:T(8,128)(2,1)}, bf16[2,128,512]{2,1,0:T(8,128)(2,1)}, bf16[2,128,512]{2,1,0:T(8,128)(2,1...) custom-call(s32[1]{0:T(128)} %bitcast.me_ref.refs_0_, ...), custom_call_target="tpu_custom_call" | custom-call | flops 2147483648 | bytes 4194304 | tf_op jit(solution)/shard_map/right/pallas_call | solution.py:74
  5.5 1.3 collective-permute-start
  6.9 1.2 collective-permute-start.2
  8.2 2.3 %collective-permute-start.3 = (bf16[2,128,512]{2,1,0:T(8,128)(2,1)}, bf16[2,128,512]{2,1,0:T(8,128)(2,1)}, u32[]{:S(2)}, u32[]{:S(2)}) collective-permute-start(bf16[2,128,512]{2,1,0:T(8,128)(2,1)} %get-tuple-element.52), channel_id=1, source_target_pairs={{0,4},{1,5},{2,6},{3,7},{4,0},{5,1},{6,2},{7,3},{8,12},{9,13},{10,... | collective-permute-start | bytes 786440 | tf_op jit(solution)/shard_map/ppermute | solution.py:346
  10.5 1.0 collective-permute-start.4
  11.5 6.5 %copy.15 = bf16[2048,1024]{0,1:T(8,128)(2,1)} copy(bf16[2048,1024]{1,0:T(8,128)(2,1)} %bitcast.29) | data formatting | bytes 8388608 | tf_op jit(solution)/shard_map/reshape | solution.py:364
  18.0 2.2 copy-done
  20.2 3.9 %right.3 = (bf16[2,128,512]{2,1,0:T(8,128)(2,1)S(1)}, bf16[2,128,512]{2,1,0:T(8,128)(2,1)}, bf16[2,128,512]{2,1,0:T(8,128)(2,1)}, bf16[2,128,512]{2,1,0:T(8,128)...) custom-call(s32[1]{0:T(128)} %bitcast.me_ref.refs_0_, ...), custom_call_target="tpu_custom_call" | custom-call | flops 2147483648 | bytes 4194304 | tf_op jit(solution)/shard_map/right/pallas_call | solution.py:74
  24.9 1.3 collective-permute-start.5
  27.1 3.7 %sine_bitcast_fusion = (f32[4,128,512]{2,1,0:T(8,128)S(1)}, f32[4,128,512]{2,1,0:T(8,128)S(1)}) fusion(f32[128,4,512]{2,1,0:T(4,128)S(1)} %copy-done.30), kind=kLoop, calls=%fused_computation | loop fusion | bytes 3145728 | tf_op jit(solution)/shard_map/sin | solution.py:378
  30.8 4.2 %collective-permute-start.10 = (bf16[2,128,512]{2,1,0:T(8,128)(2,1)S(1)}, bf16[2,128,512]{2,1,0:T(8,128)(2,1)S(1)}, u32[]{:S(2)}, u32[]{:S(2)}) collective-permute-start(bf16[2,128,512]{2,1,0:T(8,128)(2,1)S(1)} %get-tuple-element.60), channel_id=1, source_target_pairs={{0,4},{1,5},{2,6},{3,7},{4,0},{5,1},{6,2},{7,3},{8,12},{9,13},{10,... | collective-permute-start | bytes 786440 | tf_op jit(solution)/shard_map/ppermute | solution.py:346
  34.9 1.0 collective-permute-start.11
  36.0 18.2 %collective-permute-done.4.refs_7_ = bf16[2,128,512]{2,1,0:T(8,128)(2,1)} collective-permute-done((bf16[2,128,512]{2,1,0:T(8,128)(2,1)}, bf16[2,128,512]{2,1,0:T(8,128)(2,1)}, u32[]{:S(2)}, u32[]{:S(2)}) %collective-permute-start.4) | collective-permute-done | bytes 262176 | tf_op jit(solution)/shard_map/ppermute | solution.py:346
  54.1 18.5 %collective-permute-done.5.refs_8_ = bf16[2,128,512]{2,1,0:T(8,128)(2,1)S(1)} collective-permute-done((bf16[2,128,512]{2,1,0:T(8,128)(2,1)S(1)}, bf16[2,128,512]{2,1,0:T(8,128)(2,1)S(1)}, u32[]{:S(2)}, u32[]{:S(2)}) %collective-permute-start.5) | collective-permute-done | bytes 262176 | tf_op jit(solution)/shard_map/ppermute | solution.py:346
  72.6 1.6 collective-permute-start.13
  74.2 4.0 %collective-permute-done.6.refs_9_ = bf16[2,128,512]{2,1,0:T(8,128)(2,1)S(1)} collective-permute-done((bf16[2,128,512]{2,1,0:T(8,128)(2,1)S(1)}, bf16[2,128,512]{2,1,0:T(8,128)(2,1)S(1)}, u32[]{:S(2)}, u32[]{:S(2)}) %collective-permute-start.6) | collective-permute-done | bytes 262176 | tf_op jit(solution)/shard_map/ppermute | solution.py:346
  78.2 1.2 collective-permute-start.7
  81.3 6.8 %left.2 = (bf16[2,128,512]{2,1,0:T(8,128)(2,1)S(1)}, bf16[2,128,512]{2,1,0:T(8,128)(2,1)}, bf16[2,128,512]{2,1,0:T(8,128)(2,1)}, bf16[2,128,512]{2,1,0:T(8,128)(...) custom-call(s32[1]{0:T(128)} %bitcast.me_ref.refs_0_, ...), custom_call_target="tpu_custom_call" | custom-call | flops 4294967296 | bytes 8388608 | tf_op jit(solution)/shard_map/left/pallas_call | solution.py:121
  93.8 1.4 collective-permute-start.9
  95.9 1.2 collective-permute-start.21
  97.1 5.2 %collective-permute-done.13.refs_9_ = bf16[2,128,512]{2,1,0:T(8,128)(2,1)S(1)} collective-permute-done((bf16[2,128,512]{2,1,0:T(8,128)(2,1)S(1)}, bf16[2,128,512]{2,1,0:T(8,128)(2,1)S(1)}, u32[]{:S(2)}, u32[]{:S(2)}) %collective-permute-start.13) | collective-permute-done | bytes 262176 | tf_op jit(solution)/shard_map/ppermute | solution.py:346
  103.0 2.4 %collective-permute-start.23 = (bf16[2,128,512]{2,1,0:T(8,128)(2,1)}, bf16[2,128,512]{2,1,0:T(8,128)(2,1)S(1)}, u32[]{:S(2)}, u32[]{:S(2)}) collective-permute-start(bf16[2,128,512]{2,1,0:T(8,128)(2,1)} %copy-done.22), channel_id=1, source_target_pairs={{0,3},{1,2},{2,1},{3,0},{4,7},{5,6},{6,5},{7,4},{8,11},{9,10},{10,... | collective-permute-start | bytes 786440 | tf_op jit(solution)/shard_map/ppermute | solution.py:346
  105.8 1.9 collective-permute-start.25
  107.7 7.0 %collective-permute-done.21.refs_2_ = bf16[2,128,512]{2,1,0:T(8,128)(2,1)S(1)} collective-permute-done((bf16[2,128,512]{2,1,0:T(8,128)(2,1)}, bf16[2,128,512]{2,1,0:T(8,128)(2,1)S(1)}, u32[]{:S(2)}, u32[]{:S(2)}) %collective-permute-start.21) | collective-permute-done | bytes 262176 | tf_op jit(solution)/shard_map/ppermute | solution.py:346
  115.5 3.9 %collective-permute-start.26 = (bf16[2,128,512]{2,1,0:T(8,128)(2,1)}, bf16[2,128,512]{2,1,0:T(8,128)(2,1)S(1)}, u32[]{:S(2)}, u32[]{:S(2)}) collective-permute-start(bf16[2,128,512]{2,1,0:T(8,128)(2,1)} %copy-done.13), channel_id=1, source_target_pairs={{0,6},{1,7},{2,4},{3,5},{4,2},{5,3},{6,0},{7,1},{8,14},{9,15},{10,... | collective-permute-start | bytes 786440 | tf_op jit(solution)/shard_map/ppermute | solution.py:346
  120.1 2.2 copy-done.3
  128.0 6.9 %left.3 = (bf16[2,128,512]{2,1,0:T(8,128)(2,1)S(1)}, bf16[2,128,512]{2,1,0:T(8,128)(2,1)S(1)}, bf16[2,128,512]{2,1,0:T(8,128)(2,1)S(1)}, bf16[2,128,512]{2,1,0:T...) custom-call(s32[1]{0:T(128)} %bitcast.me_ref.refs_0_, ...), custom_call_target="tpu_custom_call" | custom-call | flops 4294967296 | bytes 8388608 | tf_op jit(solution)/shard_map/left/pallas_call | solution.py:121
  134.9 1.6 collective-permute-start.14
  136.5 3.6 %collective-permute-start.15 = (bf16[2,128,512]{2,1,0:T(8,128)(2,1)S(1)}, bf16[2,128,512]{2,1,0:T(8,128)(2,1)S(1)}, u32[]{:S(2)}, u32[]{:S(2)}) collective-permute-start(bf16[2,128,512]{2,1,0:T(8,128)(2,1)S(1)} %get-tuple-element.66), channel_id=1, source_target_pairs={{0,2},{1,3},{2,0},{3,1},{4,6},{5,7},{6,4},{7,5},{8,10},{9,11},{10,... | collective-permute-start | bytes 786440 | tf_op jit(solution)/shard_map/ppermute | solution.py:346
  140.1 6.8 %collective-permute-done.26.refs_7_ = bf16[2,128,512]{2,1,0:T(8,128)(2,1)S(1)} collective-permute-done((bf16[2,128,512]{2,1,0:T(8,128)(2,1)}, bf16[2,128,512]{2,1,0:T(8,128)(2,1)S(1)}, u32[]{:S(2)}, u32[]{:S(2)}) %collective-permute-start.26) | collective-permute-done | bytes 262176 | tf_op jit(solution)/shard_map/ppermute | solution.py:346
  147.0 10.7 %collective-permute-done.27.refs_8_ = bf16[2,128,512]{2,1,0:T(8,128)(2,1)S(1)} collective-permute-done((bf16[2,128,512]{2,1,0:T(8,128)(2,1)}, bf16[2,128,512]{2,1,0:T(8,128)(2,1)S(1)}, u32[]{:S(2)}, u32[]{:S(2)}) %collective-permute-start.27) | collective-permute-done | bytes 262176 | tf_op jit(solution)/shard_map/ppermute | solution.py:346
  157.8 4.9 %phase.1 = (bf16[2,1,128,512]{3,2,1,0:T(8,128)(2,1)}, bf16[2,1,128,512]{3,2,1,0:T(8,128)(2,1)}, bf16[2,1,128,512]{3,2,1,0:T(8,128)(2,1)}, bf16[2,1,128,512]{3,2,...) custom-call(s32[1]{0:T(128)} %bitcast.me_ref.refs_0_, ...), custom_call_target="tpu_custom_call" | custom-call | flops 2147483648 | bytes 4194304 | tf_op jit(solution)/shard_map/phase/pallas_call | solution.py:191
  162.6 2.0 collective-permute-start.19
  164.6 1.3 collective-permute-start.20
  166.0 7.9 %collective-permute-start.28 = (bf16[2,1,128,512]{3,2,1,0:T(8,128)(2,1)}, bf16[2,1,128,512]{3,2,1,0:T(8,128)(2,1)}, u32[]{:S(2)}, u32[]{:S(2)}) collective-permute-start(bf16[2,1,128,512]{3,2,1,0:T(8,128)(2,1)} %get-tuple-element.83.refs_12_.refs_8_), channel_id=1, source_target_pairs={{0,8},{8,16},{16,24},{1,9},{9,17},{17,25},{2,10},{10,18},{18,26},{... | collective-permute-start | bytes 786440 | tf_op jit(solution)/shard_map/ppermute | solution.py:353
  173.9 6.3 %collective-permute-done.17.refs_4_ = bf16[2,128,512]{2,1,0:T(8,128)(2,1)S(1)} collective-permute-done((bf16[2,128,512]{2,1,0:T(8,128)(2,1)S(1)}, bf16[2,128,512]{2,1,0:T(8,128)(2,1)S(1)}, u32[]{:S(2)}, u32[]{:S(2)}) %collective-permute-start.17) | collective-permute-done | bytes 262176 | tf_op jit(solution)/shard_map/ppermute | solution.py:346
  180.2 3.9 %collective-permute-start.29 = (bf16[2,1,128,512]{3,2,1,0:T(8,128)(2,1)}, bf16[2,1,128,512]{3,2,1,0:T(8,128)(2,1)}, u32[]{:S(2)}, u32[]{:S(2)}) collective-permute-start(bf16[2,1,128,512]{3,2,1,0:T(8,128)(2,1)} %get-tuple-element.84.refs_13_.refs_9_), channel_id=1, source_target_pairs={{0,8},{8,16},{16,24},{1,9},{9,17},{17,25},{2,10},{10,18},{18,26},{... | collective-permute-start | bytes 786440 | tf_op jit(solution)/shard_map/ppermute | solution.py:353
  184.1 1.7 collective-permute-done.18.refs_5_
  185.8 3.9 %collective-permute-start.30 = (bf16[2,1,128,512]{3,2,1,0:T(8,128)(2,1)}, bf16[2,1,128,512]{3,2,1,0:T(8,128)(2,1)}, u32[]{:S(2)}, u32[]{:S(2)}) collective-permute-start(bf16[2,1,128,512]{3,2,1,0:T(8,128)(2,1)} %get-tuple-element.85.refs_14_.refs_10_), channel_id=1, source_target_pairs={{0,8},{8,16},{16,24},{1,9},{9,17},{17,25},{2,10},{10,18},{18,26},{... | collective-permute-start | bytes 786440 | tf_op jit(solution)/shard_map/ppermute | solution.py:353
  190.1 1.9 collective-permute-done.19.refs_6_
  192.0 4.9 %collective-permute-start.31 = (bf16[2,1,128,512]{3,2,1,0:T(8,128)(2,1)}, bf16[2,1,128,512]{3,2,1,0:T(8,128)(2,1)S(1)}, u32[]{:S(2)}, u32[]{:S(2)}) collective-permute-start(bf16[2,1,128,512]{3,2,1,0:T(8,128)(2,1)} %get-tuple-element.86.refs_15_.refs_11_), channel_id=1, source_target_pairs={{0,8},{8,16},{16,24},{1,9},{9,17},{17,25},{2,10},{10,18},{18,26},{... | collective-permute-start | bytes 786440 | tf_op jit(solution)/shard_map/ppermute | solution.py:353
  196.9 1.4 collective-permute-done.20.refs_7_
  198.3 2.6 %collective-permute-start.32 = (bf16[2,1,128,512]{3,2,1,0:T(8,128)(2,1)}, bf16[2,1,128,512]{3,2,1,0:T(8,128)(2,1)S(1)}, u32[]{:S(2)}, u32[]{:S(2)}) collective-permute-start(bf16[2,1,128,512]{3,2,1,0:T(8,128)(2,1)} %get-tuple-element.79.refs_8_.refs_4_), channel_id=1, source_target_pairs={{8,0},{16,8},{24,16},{9,1},{17,9},{25,17},{10,2},{18,10},{26,18},{... | collective-permute-start | bytes 786440 | tf_op jit(solution)/shard_map/ppermute | solution.py:353
  200.9 1.9 collective-permute-start.33
  202.8 1.9 collective-permute-start.34
  204.8 1.9 collective-permute-start.35
  206.7 10.6 %inner.1 = (bf16[128,2,4,16,128]{4,3,2,1,0:T(8,128)(2,1)}, bf16[2,2,4,128,512]{4,3,2,1,0:T(8,128)(2,1)}) custom-call(s32[1]{0:T(128)} %bitcast.me_ref.refs_0_, f32[4,4]{1,0:T(4,128)S(1)} %broadcast_select_fusion.up_ref, f32[4,4]{1,0:T(4,128)S(1)} %pad_dynamic-slice_fusion.down_ref, bf16[1024,512]{1,0:T(8,128)(2,1)S(1)} %bitcast.26, ...), custom_call_target="tpu_custom_call" | custom-call | flops 2147483648 | bytes 10485760 | tf_op jit(solution)/shard_map/inner/pallas_call | solution.py:272
  218.4 7.9 %edge.1 = bf16[128,2,4,16,128]{4,3,2,1,0:T(8,128)(2,1)} custom-call(f32[4,4]{1,0:T(4,128)S(1)} %broadcast_select_fusion.up_ref, f32[4,4]{1,0:T(4,128)S(1)} %pad_dynamic-slice_fusion.down_ref, f32[128,512]{1,0:T(8,128)S(1)} %copy-done.4, bf16[2,2,4,128,512]{4,3,2,1,0:T(8,128)(2,1)} %get-tuple-element.87.fresh_ref, ...), custom_call_target="tpu_custom_call", output_to_operand_aliasing={{}: (20, {})} | custom-call | flops 10485760 | bytes 10485760 | tf_op jit(solution)/shard_map/edge/pallas_call | solution.py:321
  (128 shorter events, 19.7 us)
Async XLA Ops:
  5.5 18.7 %collective-permute-start = (bf16[2,128,512]{2,1,0:T(8,128)(2,1)}, bf16[2,128,512]{2,1,0:T(8,128)(2,1)S(1)}, u32[]{:S(2)}, u32[]{:S(2)}) collective-permute-start(bf16[2,128,512]{2,1,0:T(8,128)(2,1)} %get-tuple-element.49), channel_id=1, source_target_pairs={{0,1},{1,0},{2,3},{3,2},{4,5},{5,4},{6,7},{7,6},{8,9},{9,8},{10,11... | collective-permute-start | bytes 786440 | tf_op jit(solution)/shard_map/ppermute | solution.py:346
  6.7 19.5 %collective-permute-start.1 = (bf16[2,128,512]{2,1,0:T(8,128)(2,1)}, bf16[2,128,512]{2,1,0:T(8,128)(2,1)S(1)}, u32[]{:S(2)}, u32[]{:S(2)}) collective-permute-start(bf16[2,128,512]{2,1,0:T(8,128)(2,1)} %get-tuple-element.50), channel_id=1, source_target_pairs={{0,2},{1,3},{2,0},{3,1},{4,6},{5,7},{6,4},{7,5},{8,10},{9,11},{10,... | collective-permute-start | bytes 786440 | tf_op jit(solution)/shard_map/ppermute | solution.py:346
  6.9 23.8 %collective-permute-start.2 = (bf16[2,128,512]{2,1,0:T(8,128)(2,1)}, bf16[2,128,512]{2,1,0:T(8,128)(2,1)}, u32[]{:S(2)}, u32[]{:S(2)}) collective-permute-start(bf16[2,128,512]{2,1,0:T(8,128)(2,1)} %get-tuple-element.51), channel_id=1, source_target_pairs={{0,3},{1,2},{2,1},{3,0},{4,7},{5,6},{6,5},{7,4},{8,11},{9,10},{10,... | collective-permute-start | bytes 786440 | tf_op jit(solution)/shard_map/ppermute | solution.py:346
  8.2 26.8 %collective-permute-start.3 = (bf16[2,128,512]{2,1,0:T(8,128)(2,1)}, bf16[2,128,512]{2,1,0:T(8,128)(2,1)}, u32[]{:S(2)}, u32[]{:S(2)}) collective-permute-start(bf16[2,128,512]{2,1,0:T(8,128)(2,1)} %get-tuple-element.52), channel_id=1, source_target_pairs={{0,4},{1,5},{2,6},{3,7},{4,0},{5,1},{6,2},{7,3},{8,12},{9,13},{10,... | collective-permute-start | bytes 786440 | tf_op jit(solution)/shard_map/ppermute | solution.py:346
  10.5 43.7 %collective-permute-start.4 = (bf16[2,128,512]{2,1,0:T(8,128)(2,1)}, bf16[2,128,512]{2,1,0:T(8,128)(2,1)}, u32[]{:S(2)}, u32[]{:S(2)}) collective-permute-start(bf16[2,128,512]{2,1,0:T(8,128)(2,1)} %get-tuple-element.53), channel_id=1, source_target_pairs={{0,5},{1,4},{2,7},{3,6},{4,1},{5,0},{6,3},{7,2},{8,13},{9,12},{10,... | collective-permute-start | bytes 786440 | tf_op jit(solution)/shard_map/ppermute | solution.py:346
  20.2 6.7 %copy-start.42 = (bf16[2,128,512]{2,1,0:T(8,128)(2,1)S(1)}, bf16[2,128,512]{2,1,0:T(8,128)(2,1)}, u32[]{:S(2)}) copy-start(bf16[2,128,512]{2,1,0:T(8,128)(2,1)} %get-tuple-element.55) | copy-start | bytes 786436
  20.2 6.9 %copy-start.30 = (f32[128,4,512]{2,1,0:T(4,128)S(1)}, f32[128,4,512]{2,1,0:T(4,128)}, u32[]{:S(2)}) copy-start(f32[128,4,512]{2,1,0:T(4,128)} %param.9) | copy-start | bytes 3145732
  20.2 59.2 %copy-start.2 = (bf16[2048,1024]{0,1:T(8,128)(2,1)S(1)}, bf16[2048,1024]{0,1:T(8,128)(2,1)}, u32[]{:S(2)}) copy-start(bf16[2048,1024]{0,1:T(8,128)(2,1)} %copy.15) | copy-start | bytes 12582916
  24.2 64.0 %copy-start.6 = (bf16[2,128,512]{2,1,0:T(8,128)(2,1)}, bf16[2,128,512]{2,1,0:T(8,128)(2,1)S(1)}, u32[]{:S(2)}) copy-start(bf16[2,128,512]{2,1,0:T(8,128)(2,1)S(1)} %get-tuple-element.48.refs_0_.refs_2_) | copy-start | bytes 786436
  24.9 47.7 %collective-permute-start.5 = (bf16[2,128,512]{2,1,0:T(8,128)(2,1)S(1)}, bf16[2,128,512]{2,1,0:T(8,128)(2,1)S(1)}, u32[]{:S(2)}, u32[]{:S(2)}) collective-permute-start(bf16[2,128,512]{2,1,0:T(8,128)(2,1)S(1)} %copy-done.43), channel_id=1, source_target_pairs={{0,6},{1,7},{2,4},{3,5},{4,2},{5,3},{6,0},{7,1},{8,14},{9,15},{10,... | collective-permute-start | bytes 786440 | tf_op jit(solution)/shard_map/ppermute | solution.py:346
  26.9 51.3 %collective-permute-start.6 = (bf16[2,128,512]{2,1,0:T(8,128)(2,1)S(1)}, bf16[2,128,512]{2,1,0:T(8,128)(2,1)S(1)}, u32[]{:S(2)}, u32[]{:S(2)}) collective-permute-start(bf16[2,128,512]{2,1,0:T(8,128)(2,1)S(1)} %copy-done.42), channel_id=1, source_target_pairs={{0,7},{1,6},{2,5},{3,4},{4,3},{5,2},{6,1},{7,0},{8,15},{9,14},{10,... | collective-permute-start | bytes 786440 | tf_op jit(solution)/shard_map/ppermute | solution.py:346
  30.8 61.6 %collective-permute-start.10 = (bf16[2,128,512]{2,1,0:T(8,128)(2,1)S(1)}, bf16[2,128,512]{2,1,0:T(8,128)(2,1)S(1)}, u32[]{:S(2)}, u32[]{:S(2)}) collective-permute-start(bf16[2,128,512]{2,1,0:T(8,128)(2,1)S(1)} %get-tuple-element.60), channel_id=1, source_target_pairs={{0,4},{1,5},{2,6},{3,7},{4,0},{5,1},{6,2},{7,3},{8,12},{9,13},{10,... | collective-permute-start | bytes 786440 | tf_op jit(solution)/shard_map/ppermute | solution.py:346
  34.9 58.2 %collective-permute-start.11 = (bf16[2,128,512]{2,1,0:T(8,128)(2,1)S(1)}, bf16[2,128,512]{2,1,0:T(8,128)(2,1)S(1)}, u32[]{:S(2)}, u32[]{:S(2)}) collective-permute-start(bf16[2,128,512]{2,1,0:T(8,128)(2,1)S(1)} %get-tuple-element.61), channel_id=1, source_target_pairs={{0,5},{1,4},{2,7},{3,6},{4,1},{5,0},{6,3},{7,2},{8,13},{9,12},{10,... | collective-permute-start | bytes 786440 | tf_op jit(solution)/shard_map/ppermute | solution.py:346
  54.1 41.1 %collective-permute-start.12 = (bf16[2,128,512]{2,1,0:T(8,128)(2,1)S(1)}, bf16[2,128,512]{2,1,0:T(8,128)(2,1)S(1)}, u32[]{:S(2)}, u32[]{:S(2)}) collective-permute-start(bf16[2,128,512]{2,1,0:T(8,128)(2,1)S(1)} %get-tuple-element.62), channel_id=1, source_target_pairs={{0,6},{1,7},{2,4},{3,5},{4,2},{5,3},{6,0},{7,1},{8,14},{9,15},{10,... | collective-permute-start | bytes 786440 | tf_op jit(solution)/shard_map/ppermute | solution.py:346
  72.6 29.7 %collective-permute-start.13 = (bf16[2,128,512]{2,1,0:T(8,128)(2,1)S(1)}, bf16[2,128,512]{2,1,0:T(8,128)(2,1)S(1)}, u32[]{:S(2)}, u32[]{:S(2)}) collective-permute-start(bf16[2,128,512]{2,1,0:T(8,128)(2,1)S(1)} %get-tuple-element.63), channel_id=1, source_target_pairs={{0,7},{1,6},{2,5},{3,4},{4,3},{5,2},{6,1},{7,0},{8,15},{9,14},{10,... | collective-permute-start | bytes 786440 | tf_op jit(solution)/shard_map/ppermute | solution.py:346
  78.2 24.8 %collective-permute-start.7 = (bf16[2,128,512]{2,1,0:T(8,128)(2,1)}, bf16[2,128,512]{2,1,0:T(8,128)(2,1)}, u32[]{:S(2)}, u32[]{:S(2)}) collective-permute-start(bf16[2,128,512]{2,1,0:T(8,128)(2,1)} %get-tuple-element.57), channel_id=1, source_target_pairs={{0,1},{1,0},{2,3},{3,2},{4,5},{5,4},{6,7},{7,6},{8,9},{9,8},{10,11... | collective-permute-start | bytes 786440 | tf_op jit(solution)/shard_map/ppermute | solution.py:346
  93.1 12.3 %collective-permute-start.8 = (bf16[2,128,512]{2,1,0:T(8,128)(2,1)}, bf16[2,128,512]{2,1,0:T(8,128)(2,1)}, u32[]{:S(2)}, u32[]{:S(2)}) collective-permute-start(bf16[2,128,512]{2,1,0:T(8,128)(2,1)} %get-tuple-element.58), channel_id=1, source_target_pairs={{0,2},{1,3},{2,0},{3,1},{4,6},{5,7},{6,4},{7,5},{8,10},{9,11},{10,... | collective-permute-start | bytes 786440 | tf_op jit(solution)/shard_map/ppermute | solution.py:346
  93.8 12.0 %collective-permute-start.9 = (bf16[2,128,512]{2,1,0:T(8,128)(2,1)}, bf16[2,128,512]{2,1,0:T(8,128)(2,1)}, u32[]{:S(2)}, u32[]{:S(2)}) collective-permute-start(bf16[2,128,512]{2,1,0:T(8,128)(2,1)} %get-tuple-element.59), channel_id=1, source_target_pairs={{0,3},{1,2},{2,1},{3,0},{4,7},{5,6},{6,5},{7,4},{8,11},{9,10},{10,... | collective-permute-start | bytes 786440 | tf_op jit(solution)/shard_map/ppermute | solution.py:346
  95.9 18.9 %collective-permute-start.21 = (bf16[2,128,512]{2,1,0:T(8,128)(2,1)}, bf16[2,128,512]{2,1,0:T(8,128)(2,1)S(1)}, u32[]{:S(2)}, u32[]{:S(2)}) collective-permute-start(bf16[2,128,512]{2,1,0:T(8,128)(2,1)} %get-tuple-element.72), channel_id=1, source_target_pairs={{0,1},{1,0},{2,3},{3,2},{4,5},{5,4},{6,7},{7,6},{8,9},{9,8},{10,11... | collective-permute-start | bytes 786440 | tf_op jit(solution)/shard_map/ppermute | solution.py:346
  103.0 16.4 %collective-permute-start.22 = (bf16[2,128,512]{2,1,0:T(8,128)(2,1)}, bf16[2,128,512]{2,1,0:T(8,128)(2,1)}, u32[]{:S(2)}, u32[]{:S(2)}) collective-permute-start(bf16[2,128,512]{2,1,0:T(8,128)(2,1)} %get-tuple-element.73), channel_id=1, source_target_pairs={{0,2},{1,3},{2,0},{3,1},{4,6},{5,7},{6,4},{7,5},{8,10},{9,11},{10,... | collective-permute-start | bytes 786440 | tf_op jit(solution)/shard_map/ppermute | solution.py:346
  103.0 31.9 %collective-permute-start.23 = (bf16[2,128,512]{2,1,0:T(8,128)(2,1)}, bf16[2,128,512]{2,1,0:T(8,128)(2,1)S(1)}, u32[]{:S(2)}, u32[]{:S(2)}) collective-permute-start(bf16[2,128,512]{2,1,0:T(8,128)(2,1)} %copy-done.22), channel_id=1, source_target_pairs={{0,3},{1,2},{2,1},{3,0},{4,7},{5,6},{6,5},{7,4},{8,11},{9,10},{10,... | collective-permute-start | bytes 786440 | tf_op jit(solution)/shard_map/ppermute | solution.py:346
  105.4 31.1 %collective-permute-start.24 = (bf16[2,128,512]{2,1,0:T(8,128)(2,1)}, bf16[2,128,512]{2,1,0:T(8,128)(2,1)S(1)}, u32[]{:S(2)}, u32[]{:S(2)}) collective-permute-start(bf16[2,128,512]{2,1,0:T(8,128)(2,1)} %copy-done.21), channel_id=1, source_target_pairs={{0,4},{1,5},{2,6},{3,7},{4,0},{5,1},{6,2},{7,3},{8,12},{9,13},{10,... | collective-permute-start | bytes 786440 | tf_op jit(solution)/shard_map/ppermute | solution.py:346
  105.8 34.3 %collective-permute-start.25 = (bf16[2,128,512]{2,1,0:T(8,128)(2,1)}, bf16[2,128,512]{2,1,0:T(8,128)(2,1)S(1)}, u32[]{:S(2)}, u32[]{:S(2)}) collective-permute-start(bf16[2,128,512]{2,1,0:T(8,128)(2,1)} %copy-done.16), channel_id=1, source_target_pairs={{0,5},{1,4},{2,7},{3,6},{4,1},{5,0},{6,3},{7,2},{8,13},{9,12},{10,... | collective-permute-start | bytes 786440 | tf_op jit(solution)/shard_map/ppermute | solution.py:346
  115.5 31.5 %collective-permute-start.26 = (bf16[2,128,512]{2,1,0:T(8,128)(2,1)}, bf16[2,128,512]{2,1,0:T(8,128)(2,1)S(1)}, u32[]{:S(2)}, u32[]{:S(2)}) collective-permute-start(bf16[2,128,512]{2,1,0:T(8,128)(2,1)} %copy-done.13), channel_id=1, source_target_pairs={{0,6},{1,7},{2,4},{3,5},{4,2},{5,3},{6,0},{7,1},{8,14},{9,15},{10,... | collective-permute-start | bytes 786440 | tf_op jit(solution)/shard_map/ppermute | solution.py:346
  119.4 38.3 %collective-permute-start.27 = (bf16[2,128,512]{2,1,0:T(8,128)(2,1)}, bf16[2,128,512]{2,1,0:T(8,128)(2,1)S(1)}, u32[]{:S(2)}, u32[]{:S(2)}) collective-permute-start(bf16[2,128,512]{2,1,0:T(8,128)(2,1)} %copy-done.10), channel_id=1, source_target_pairs={{0,7},{1,6},{2,5},{3,4},{4,3},{5,2},{6,1},{7,0},{8,15},{9,14},{10,... | collective-permute-start | bytes 786440 | tf_op jit(solution)/shard_map/ppermute | solution.py:346
  128.0 29.7 %copy-start.36 = (f32[16,4]{0,1:T(4,128)S(1)}, f32[16,4]{0,1:T(4,128)}, u32[]{:S(2)}) copy-start(f32[16,4]{0,1:T(4,128)} %param.10) | copy-start | bytes 772
  128.0 29.7 %copy-start.18 = (bf16[2,128,512]{2,1,0:T(8,128)(2,1)S(1)}, bf16[2,128,512]{2,1,0:T(8,128)(2,1)}, u32[]{:S(2)}) copy-start(bf16[2,128,512]{2,1,0:T(8,128)(2,1)} %copy-done.17) | copy-start | bytes 786436
  134.9 50.9 %copy-start.27 = (bf16[2,128,512]{2,1,0:T(8,128)(2,1)}, bf16[2,128,512]{2,1,0:T(8,128)(2,1)S(1)}, u32[]{:S(2)}) copy-start(bf16[2,128,512]{2,1,0:T(8,128)(2,1)S(1)} %get-tuple-element.64.refs_0_) | copy-start | bytes 786436
  134.9 71.8 %copy-start.4 = (f32[128,512]{1,0:T(8,128)S(1)}, f32[128,512]{1,0:T(8,128)}, u32[]{:S(2)}) copy-start(f32[128,512]{1,0:T(8,128)} %weight_ref.3) | copy-start | bytes 786436
  134.9 27.7 %collective-permute-start.14 = (bf16[2,128,512]{2,1,0:T(8,128)(2,1)S(1)}, bf16[2,128,512]{2,1,0:T(8,128)(2,1)S(1)}, u32[]{:S(2)}, u32[]{:S(2)}) collective-permute-start(bf16[2,128,512]{2,1,0:T(8,128)(2,1)S(1)} %get-tuple-element.65), channel_id=1, source_target_pairs={{0,1},{1,0},{2,3},{3,2},{4,5},{5,4},{6,7},{7,6},{8,9},{9,8},{10,11... | collective-permute-start | bytes 786440 | tf_op jit(solution)/shard_map/ppermute | solution.py:346
  136.5 28.1 %collective-permute-start.15 = (bf16[2,128,512]{2,1,0:T(8,128)(2,1)S(1)}, bf16[2,128,512]{2,1,0:T(8,128)(2,1)S(1)}, u32[]{:S(2)}, u32[]{:S(2)}) collective-permute-start(bf16[2,128,512]{2,1,0:T(8,128)(2,1)S(1)} %get-tuple-element.66), channel_id=1, source_target_pairs={{0,2},{1,3},{2,0},{3,1},{4,6},{5,7},{6,4},{7,5},{8,10},{9,11},{10,... | collective-permute-start | bytes 786440 | tf_op jit(solution)/shard_map/ppermute | solution.py:346
  140.1 25.8 %collective-permute-start.16 = (bf16[2,128,512]{2,1,0:T(8,128)(2,1)S(1)}, bf16[2,128,512]{2,1,0:T(8,128)(2,1)S(1)}, u32[]{:S(2)}, u32[]{:S(2)}) collective-permute-start(bf16[2,128,512]{2,1,0:T(8,128)(2,1)S(1)} %get-tuple-element.67), channel_id=1, source_target_pairs={{0,3},{1,2},{2,1},{3,0},{4,7},{5,6},{6,5},{7,4},{8,11},{9,10},{10,... | collective-permute-start | bytes 786440 | tf_op jit(solution)/shard_map/ppermute | solution.py:346
  147.0 33.2 %collective-permute-start.17 = (bf16[2,128,512]{2,1,0:T(8,128)(2,1)S(1)}, bf16[2,128,512]{2,1,0:T(8,128)(2,1)S(1)}, u32[]{:S(2)}, u32[]{:S(2)}) collective-permute-start(bf16[2,128,512]{2,1,0:T(8,128)(2,1)S(1)} %get-tuple-element.68), channel_id=1, source_target_pairs={{0,4},{1,5},{2,6},{3,7},{4,0},{5,1},{6,2},{7,3},{8,12},{9,13},{10,... | collective-permute-start | bytes 786440 | tf_op jit(solution)/shard_map/ppermute | solution.py:346
  157.7 28.1 %collective-permute-start.18 = (bf16[2,128,512]{2,1,0:T(8,128)(2,1)S(1)}, bf16[2,128,512]{2,1,0:T(8,128)(2,1)S(1)}, u32[]{:S(2)}, u32[]{:S(2)}) collective-permute-start(bf16[2,128,512]{2,1,0:T(8,128)(2,1)S(1)} %get-tuple-element.69), channel_id=1, source_target_pairs={{0,5},{1,4},{2,7},{3,6},{4,1},{5,0},{6,3},{7,2},{8,13},{9,12},{10,... | collective-permute-start | bytes 786440 | tf_op jit(solution)/shard_map/ppermute | solution.py:346
  162.6 27.0 %copy-start.37 = (bf16[2,128,512]{2,1,0:T(8,128)(2,1)}, bf16[2,128,512]{2,1,0:T(8,128)(2,1)S(1)}, u32[]{:S(2)}) copy-start(bf16[2,128,512]{2,1,0:T(8,128)(2,1)S(1)} %collective-permute-done.14.refs_1_) | copy-start | bytes 786436
  162.6 29.4 %collective-permute-start.19 = (bf16[2,128,512]{2,1,0:T(8,128)(2,1)}, bf16[2,128,512]{2,1,0:T(8,128)(2,1)}, u32[]{:S(2)}, u32[]{:S(2)}) collective-permute-start(bf16[2,128,512]{2,1,0:T(8,128)(2,1)} %get-tuple-element.70), channel_id=1, source_target_pairs={{0,6},{1,7},{2,4},{3,5},{4,2},{5,3},{6,0},{7,1},{8,14},{9,15},{10,... | collective-permute-start | bytes 786440 | tf_op jit(solution)/shard_map/ppermute | solution.py:346
  164.6 25.1 %copy-start.38 = (bf16[2,128,512]{2,1,0:T(8,128)(2,1)}, bf16[2,128,512]{2,1,0:T(8,128)(2,1)S(1)}, u32[]{:S(2)}) copy-start(bf16[2,128,512]{2,1,0:T(8,128)(2,1)S(1)} %collective-permute-done.15.refs_2_) | copy-start | bytes 786436
  164.6 33.7 %collective-permute-start.20 = (bf16[2,128,512]{2,1,0:T(8,128)(2,1)}, bf16[2,128,512]{2,1,0:T(8,128)(2,1)}, u32[]{:S(2)}, u32[]{:S(2)}) collective-permute-start(bf16[2,128,512]{2,1,0:T(8,128)(2,1)} %get-tuple-element.71), channel_id=1, source_target_pairs={{0,7},{1,6},{2,5},{3,4},{4,3},{5,2},{6,1},{7,0},{8,15},{9,14},{10,... | collective-permute-start | bytes 786440 | tf_op jit(solution)/shard_map/ppermute | solution.py:346
  166.0 23.7 %copy-start.39 = (bf16[2,128,512]{2,1,0:T(8,128)(2,1)}, bf16[2,128,512]{2,1,0:T(8,128)(2,1)S(1)}, u32[]{:S(2)}) copy-start(bf16[2,128,512]{2,1,0:T(8,128)(2,1)S(1)} %collective-permute-done.16.refs_3_) | copy-start | bytes 786436
  166.0 34.9 %collective-permute-start.28 = (bf16[2,1,128,512]{3,2,1,0:T(8,128)(2,1)}, bf16[2,1,128,512]{3,2,1,0:T(8,128)(2,1)}, u32[]{:S(2)}, u32[]{:S(2)}) collective-permute-start(bf16[2,1,128,512]{3,2,1,0:T(8,128)(2,1)} %get-tuple-element.83.refs_12_.refs_8_), channel_id=1, source_target_pairs={{0,8},{8,16},{16,24},{1,9},{9,17},{17,25},{2,10},{10,18},{18,26},{... | collective-permute-start | bytes 786440 | tf_op jit(solution)/shard_map/ppermute | solution.py:353
  180.2 9.5 %copy-start.40 = (bf16[2,128,512]{2,1,0:T(8,128)(2,1)}, bf16[2,128,512]{2,1,0:T(8,128)(2,1)S(1)}, u32[]{:S(2)}) copy-start(bf16[2,128,512]{2,1,0:T(8,128)(2,1)S(1)} %collective-permute-done.17.refs_4_) | copy-start | bytes 786436
  180.2 22.6 %collective-permute-start.29 = (bf16[2,1,128,512]{3,2,1,0:T(8,128)(2,1)}, bf16[2,1,128,512]{3,2,1,0:T(8,128)(2,1)}, u32[]{:S(2)}, u32[]{:S(2)}) collective-permute-start(bf16[2,1,128,512]{3,2,1,0:T(8,128)(2,1)} %get-tuple-element.84.refs_13_.refs_9_), channel_id=1, source_target_pairs={{0,8},{8,16},{16,24},{1,9},{9,17},{17,25},{2,10},{10,18},{18,26},{... | collective-permute-start | bytes 786440 | tf_op jit(solution)/shard_map/ppermute | solution.py:353
  185.8 19.0 %collective-permute-start.30 = (bf16[2,1,128,512]{3,2,1,0:T(8,128)(2,1)}, bf16[2,1,128,512]{3,2,1,0:T(8,128)(2,1)}, u32[]{:S(2)}, u32[]{:S(2)}) collective-permute-start(bf16[2,1,128,512]{3,2,1,0:T(8,128)(2,1)} %get-tuple-element.85.refs_14_.refs_10_), channel_id=1, source_target_pairs={{0,8},{8,16},{16,24},{1,9},{9,17},{17,25},{2,10},{10,18},{18,26},{... | collective-permute-start | bytes 786440 | tf_op jit(solution)/shard_map/ppermute | solution.py:353
  192.0 25.3 %collective-permute-start.31 = (bf16[2,1,128,512]{3,2,1,0:T(8,128)(2,1)}, bf16[2,1,128,512]{3,2,1,0:T(8,128)(2,1)S(1)}, u32[]{:S(2)}, u32[]{:S(2)}) collective-permute-start(bf16[2,1,128,512]{3,2,1,0:T(8,128)(2,1)} %get-tuple-element.86.refs_15_.refs_11_), channel_id=1, source_target_pairs={{0,8},{8,16},{16,24},{1,9},{9,17},{17,25},{2,10},{10,18},{18,26},{... | collective-permute-start | bytes 786440 | tf_op jit(solution)/shard_map/ppermute | solution.py:353
  198.3 19.1 %collective-permute-start.32 = (bf16[2,1,128,512]{3,2,1,0:T(8,128)(2,1)}, bf16[2,1,128,512]{3,2,1,0:T(8,128)(2,1)S(1)}, u32[]{:S(2)}, u32[]{:S(2)}) collective-permute-start(bf16[2,1,128,512]{3,2,1,0:T(8,128)(2,1)} %get-tuple-element.79.refs_8_.refs_4_), channel_id=1, source_target_pairs={{8,0},{16,8},{24,16},{9,1},{17,9},{25,17},{10,2},{18,10},{26,18},{... | collective-permute-start | bytes 786440 | tf_op jit(solution)/shard_map/ppermute | solution.py:353
  200.9 16.5 %collective-permute-start.33 = (bf16[2,1,128,512]{3,2,1,0:T(8,128)(2,1)}, bf16[2,1,128,512]{3,2,1,0:T(8,128)(2,1)S(1)}, u32[]{:S(2)}, u32[]{:S(2)}) collective-permute-start(bf16[2,1,128,512]{3,2,1,0:T(8,128)(2,1)} %get-tuple-element.80.refs_9_.refs_5_), channel_id=1, source_target_pairs={{8,0},{16,8},{24,16},{9,1},{17,9},{25,17},{10,2},{18,10},{26,18},{... | collective-permute-start | bytes 786440 | tf_op jit(solution)/shard_map/ppermute | solution.py:353
  202.8 14.5 %collective-permute-start.34 = (bf16[2,1,128,512]{3,2,1,0:T(8,128)(2,1)}, bf16[2,1,128,512]{3,2,1,0:T(8,128)(2,1)S(1)}, u32[]{:S(2)}, u32[]{:S(2)}) collective-permute-start(bf16[2,1,128,512]{3,2,1,0:T(8,128)(2,1)} %get-tuple-element.81.refs_10_.refs_6_), channel_id=1, source_target_pairs={{8,0},{16,8},{24,16},{9,1},{17,9},{25,17},{10,2},{18,10},{26,18},{... | collective-permute-start | bytes 786440 | tf_op jit(solution)/shard_map/ppermute | solution.py:353
  204.8 12.6 %collective-permute-start.35 = (bf16[2,1,128,512]{3,2,1,0:T(8,128)(2,1)}, bf16[2,1,128,512]{3,2,1,0:T(8,128)(2,1)S(1)}, u32[]{:S(2)}, u32[]{:S(2)}) collective-permute-start(bf16[2,1,128,512]{3,2,1,0:T(8,128)(2,1)} %get-tuple-element.82.refs_11_.refs_7_), channel_id=1, source_target_pairs={{8,0},{16,8},{24,16},{9,1},{17,9},{25,17},{10,2},{18,10},{26,18},{... | collective-permute-start | bytes 786440 | tf_op jit(solution)/shard_map/ppermute | solution.py:353
  (32 other events, 47.2 us)

commit v12 on v9

--- a/solution.py
+++ b/solution.py
@@ -69,7 +69,7 @@
 def right_call(after, me, second, view, chosen, ranks, states, piece, limit):
     rows, _, _, group, _ = view.shape
     width = second.shape[1]
-    block = rows // 2
+    block = rows
     kinds = len(chosen)
     return pl.pallas_call(
         functools.partial(right_kernel, len(after), ranks, states),
@@ -166,8 +166,8 @@
 
 def phase_kernel(after, ranks, me_ref, second_ref, cosine_ref, sine_ref, *refs):
     refs = refs[after:]
-    ins, outs, slabs = refs[:ranks], refs[ranks:-1], refs[-1]
-    states, rows, _ = cosine_ref.shape
+    ins, outs, whole, slabs = refs[:ranks], refs[ranks:-2], refs[-2], refs[-1]
+    states, rows, width = cosine_ref.shape
     share = outs[0].shape[1]
     pieces = states // share
     for n in range(len(outs) // pieces):
@@ -178,6 +178,7 @@
             for j in range(states):
                 first = (c * states + j) * rows
                 outs[n * pieces + j // share][c, j % share] = product[first : first + rows]
+        whole[n] = product.reshape(2, states, rows, width)
 
 
 def phase_call(after, me, second, cosine, sine, slabs):
@@ -194,8 +195,10 @@
         in_specs=[SMEM, pl.BlockSpec(second.shape, lambda i: (0, 0)), table, table]
         + [AFTER] * len(after)
         + [pl.BlockSpec((kinds, block, wide), lambda i: (0, i, 0))] * ranks,
-        out_specs=[pl.BlockSpec((2, share, block, width), lambda i: (0, 0, i, 0))] * count,
-        out_shape=[pltpu.HBM((2, share, rows, width), jnp.bfloat16)] * count,
+        out_specs=[pl.BlockSpec((2, share, block, width), lambda i: (0, 0, i, 0))] * count
+        + [pl.BlockSpec((kinds, 2, states, block, width), lambda i: (0, 0, 0, i, 0))],
+        out_shape=[pltpu.HBM((2, share, rows, width), jnp.bfloat16)] * count
+        + [pltpu.HBM((kinds, 2, states, rows, width), jnp.bfloat16)],
         scratch_shapes=[pltpu.VMEM((ranks, block, wide), jnp.bfloat16)],
         compiler_params=params(),
         cost_estimate=cost(
@@ -209,13 +212,18 @@
     chosen, order, me_ref, up_ref, down_ref, second_ref, cosine_ref, sine_ref, weight_ref, *refs
 ):
     ranks = len(order)
-    ins, known, (out, slabs, fresh) = refs[:ranks], refs[ranks:-3], refs[-3:]
+    ins, edges, halo, (out, slabs, fresh) = (
+        refs[:ranks],
+        refs[ranks],
+        refs[ranks + 1 : -3],
+        refs[-3:],
+    )
     blocks, states = up_ref.shape
     rows, width = weight_ref.shape
-    share = known[0].shape[1]
+    share = halo[0].shape[1]
     pieces = states // share
     group = out.shape[3]
-    others = [k for k in range(-1, blocks + 1) if k not in chosen]
+    others = [k for k in range(blocks) if k not in chosen]
     for n in range(len(chosen)):
         product = phased_product(
             me_ref[0], n, second_ref, cosine_ref, sine_ref, ins, order, slabs
@@ -225,8 +233,10 @@
     def kinetic(k, c, j, span):
         if k in chosen:
             value = fresh[chosen.index(k), c, j, span]
+        elif k in others:
+            value = edges[others.index(k), c, j, span]
         else:
-            value = known[others.index(k) * pieces + j // share][c, j % share, span]
+            value = halo[(k > 0) * pieces + j // share][c, j % share, span]
         return value.astype(jnp.float32)
 
     for first in range(0, rows, ROWS):
@@ -251,14 +261,14 @@
                 out[span, c, k] = jnp.stack(columns[c], 0).transpose(1, 0, 2).astype(jnp.bfloat16)
 
 
-def mix_call(me, up, down, second, cosine, sine, weight, chosen, slabs, known):
+def mix_call(me, up, down, second, cosine, sine, weight, chosen, slabs, edges, halo):
     ranks = len(slabs)
     order = tuple(range(ranks))
     kinds, rows, wide = slabs[0].shape
-    _, share, _, width = known[0].shape
+    _, share, _, width = halo[0].shape
     blocks, states = up.shape
     group = width // LANES * states
-    block = rows // 4
+    block = rows // 2
     table = pl.BlockSpec((states, block, width), lambda i: (0, i, 0))
     return pl.pallas_call(
         functools.partial(mix_kernel, tuple(chosen), order),
@@ -267,19 +277,20 @@
         + [pl.BlockSpec(second.shape, lambda i: (0, 0)), table, table]
         + [pl.BlockSpec((block, width), lambda i: (i, 0))]
         + [pl.BlockSpec((kinds, block, wide), lambda i: (0, i, 0))] * ranks
-        + [pl.BlockSpec((2, share, block, width), lambda i: (0, 0, i, 0))] * len(known),
+        + [pl.BlockSpec((*edges.shape[:3], block, width), lambda i: (0, 0, 0, i, 0))]
+        + [pl.BlockSpec((2, share, block, width), lambda i: (0, 0, i, 0))] * len(halo),
         out_specs=pl.BlockSpec((block, 2, blocks, group, LANES), lambda i: (i, 0, 0, 0, 0)),
         out_shape=jax.ShapeDtypeStruct((rows, 2, blocks, group, LANES), jnp.bfloat16),
         scratch_shapes=[
             pltpu.VMEM((ranks, block, wide), jnp.bfloat16),
             pltpu.VMEM((kinds, 2, states, block, width), jnp.bfloat16),
         ],
-        compiler_params=params(),
+        compiler_params=params(LIMIT + LIMIT // 2),
         cost_estimate=cost(
             8 * kinds * states * rows * width * width, 10 * blocks * states * rows * width
         ),
         name="mix",
-    )(me, up, down, second, cosine, sine, weight, *in_place([slabs[s] for s in order] + known))
+    )(me, up, down, second, cosine, sine, weight, *in_place([slabs[s] for s in order] + [edges, *halo]))
 
 
 def exchanged(slabs, axis):
@@ -326,7 +337,7 @@
     angles = potential.transpose(1, 0, 2)
     cosine, sine = jnp.cos(angles), jnp.sin(angles)
     edge = phase_call([last], me, second, cosine, sine, backs[0])
-    low, high = edge[:PIECES], edge[-PIECES:]
+    low, high, edges_here = edge[:PIECES], edge[-PIECES - 1 : -1], edge[-1]
     below = [neighbour(x, "hel", 1) for x in high]
     above = [neighbour(x, "hel", -1) for x in low]
 
@@ -339,9 +350,9 @@
     start = lax.axis_index("hel") * blocks
     up = lax.dynamic_slice_in_dim(couple_up, start, blocks, 0)
     down = lax.dynamic_slice_in_dim(couple_down, start, blocks, 0)
-    known = [*below, *low, *high, *above]
+    halo = [*below, *above]
     out = mix_call(
-        me, up, down, second, cosine, sine, radial_weight, chunks[1], backs[1], known
+        me, up, down, second, cosine, sine, radial_weight, chunks[1], backs[1], edges_here, halo
     )
     out = out.reshape(rows, 2, blocks, tiles, states, LANES).transpose(0, 1, 2, 4, 3, 5)
     return out.reshape(rows, 2, blocks, states, width)

time: 224 us -> 224 us (level)
  no operation moved by 1% of the time
where the time goes in v12:
time: 224 us
  waiting for transfers between devices  91.6 us (41%)
  starting transfers between devices  85.1 us (38%)
  Pallas kernels  32.8 us (15%)
  local copies, waits for them, and re-layouts  13.6 us (6%)
    ppermute x28, waiting for transfers between devices, exchanged(): result[s] = lax.ppermute(slabs[s], axis, [(i, i ^ s) for i in range(count)])  83.5 us
    ppermute x8, starting transfers between devices, neighbour(): return lax.ppermute(edge, axis, pairs)  43.5 us
    ppermute x28, starting transfers between devices, exchanged(): result[s] = lax.ppermute(slabs[s], axis, [(i, i ^ s) for i in range(count)])  41.6 us
    pallas_call x2, Pallas kernels, left_call(): pl.pallas_call(functools.partial(left_kernel, len(after), ranks), grid=(k...  10.8 us
    pallas_call x1, Pallas kernels, mix_call(): pl.pallas_call(functools.partial(mix_kernel, tuple(chosen), order), grid=...  9.05 us
    pallas_call x2, Pallas kernels, right_call(): pl.pallas_call(functools.partial(right_kernel, len(after), ranks, states)...  8.5 us
    ppermute x8, waiting for transfers between devices, neighbour(): return lax.ppermute(edge, axis, pairs)  8.1 us
    reshape x1, local copies, waits for them, and re-layouts, per_device(): first = first_propagator.reshape(2 * whole, whole).T  6.7 us
  transfers between devices with their start and end apart: 36, of which 15 were waited for; matrix products, arithmetic and copies ran while one was open for 5% of the time, Pallas kernels for 8%

profile of v12, /device:TPU:9, one launch (start us, length us, event | category | flops | bytes accessed | tf_op | source)
XLA Modules:
  0.0 223.7 jit_solution(12177915573545845051)
XLA Ops:
  0.0 5.7 %right.2 = (bf16[2,128,512]{2,1,0:T(8,128)(2,1)}, bf16[2,128,512]{2,1,0:T(8,128)(2,1)}, bf16[2,128,512]{2,1,0:T(8,128)(2,1)}, bf16[2,128,512]{2,1,0:T(8,128)(2,1...) custom-call(s32[1]{0:T(128)} %bitcast.me_ref.refs_0_, ...), custom_call_target="tpu_custom_call" | custom-call | flops 2147483648 | bytes 4194304 | tf_op jit(solution)/shard_map/right/pallas_call | solution.py:74
  5.7 1.2 collective-permute-start
  7.1 1.2 collective-permute-start.2
  8.4 2.3 %collective-permute-start.3 = (bf16[2,128,512]{2,1,0:T(8,128)(2,1)}, bf16[2,128,512]{2,1,0:T(8,128)(2,1)S(1)}, u32[]{:S(2)}, u32[]{:S(2)}) collective-permute-start(bf16[2,128,512]{2,1,0:T(8,128)(2,1)} %get-tuple-element.51), channel_id=1, source_target_pairs={{0,4},{1,5},{2,6},{3,7},{4,0},{5,1},{6,2},{7,3},{8,12},{9,13},{10,... | collective-permute-start | bytes 786440 | tf_op jit(solution)/shard_map/ppermute | solution.py:300
  10.7 1.0 collective-permute-start.4
  11.7 1.4 collective-permute-done.refs_2_
  13.1 1.3 collective-permute-start.5
  14.4 7.6 %collective-permute-done.1.refs_3_ = bf16[2,128,512]{2,1,0:T(8,128)(2,1)S(1)} collective-permute-done((bf16[2,128,512]{2,1,0:T(8,128)(2,1)}, bf16[2,128,512]{2,1,0:T(8,128)(2,1)S(1)}, u32[]{:S(2)}, u32[]{:S(2)}) %collective-permute-start.1) | collective-permute-done | bytes 262176 | tf_op jit(solution)/shard_map/ppermute | solution.py:300
  22.0 6.7 %copy.14 = bf16[2048,1024]{0,1:T(8,128)(2,1)} copy(bf16[2048,1024]{1,0:T(8,128)(2,1)} %bitcast.29) | data formatting | bytes 8388608 | tf_op jit(solution)/shard_map/reshape | solution.py:318
  28.7 2.2 copy-done
  30.9 2.8 %right.3 = (bf16[2,128,512]{2,1,0:T(8,128)(2,1)S(1)}, bf16[2,128,512]{2,1,0:T(8,128)(2,1)S(1)}, bf16[2,128,512]{2,1,0:T(8,128)(2,1)S(1)}, bf16[2,128,512]{2,1,0:...) custom-call(s32[1]{0:T(128)} %bitcast.me_ref.refs_0_, ...), custom_call_target="tpu_custom_call" | custom-call | flops 2147483648 | bytes 4194304 | tf_op jit(solution)/shard_map/right/pallas_call | solution.py:74
  33.7 3.6 %collective-permute-start.10 = (bf16[2,128,512]{2,1,0:T(8,128)(2,1)S(1)}, bf16[2,128,512]{2,1,0:T(8,128)(2,1)S(1)}, u32[]{:S(2)}, u32[]{:S(2)}) collective-permute-start(bf16[2,128,512]{2,1,0:T(8,128)(2,1)S(1)} %get-tuple-element.59), channel_id=1, source_target_pairs={{0,4},{1,5},{2,6},{3,7},{4,0},{5,1},{6,2},{7,3},{8,12},{9,13},{10,... | collective-permute-start | bytes 786440 | tf_op jit(solution)/shard_map/ppermute | solution.py:300
  37.2 1.7 collective-permute-start.11
  39.0 15.4 %collective-permute-done.4.refs_6_ = bf16[2,128,512]{2,1,0:T(8,128)(2,1)S(1)} collective-permute-done((bf16[2,128,512]{2,1,0:T(8,128)(2,1)}, bf16[2,128,512]{2,1,0:T(8,128)(2,1)S(1)}, u32[]{:S(2)}, u32[]{:S(2)}) %collective-permute-start.4) | collective-permute-done | bytes 262176 | tf_op jit(solution)/shard_map/ppermute | solution.py:300
  54.4 8.5 %collective-permute-done.5.refs_7_ = bf16[2,128,512]{2,1,0:T(8,128)(2,1)S(1)} collective-permute-done((bf16[2,128,512]{2,1,0:T(8,128)(2,1)}, bf16[2,128,512]{2,1,0:T(8,128)(2,1)S(1)}, u32[]{:S(2)}, u32[]{:S(2)}) %collective-permute-start.5) | collective-permute-done | bytes 262176 | tf_op jit(solution)/shard_map/ppermute | solution.py:300
  62.8 11.6 %collective-permute-start.13 = (bf16[2,128,512]{2,1,0:T(8,128)(2,1)S(1)}, bf16[2,128,512]{2,1,0:T(8,128)(2,1)S(1)}, u32[]{:S(2)}, u32[]{:S(2)}) collective-permute-start(bf16[2,128,512]{2,1,0:T(8,128)(2,1)S(1)} %get-tuple-element.62), channel_id=1, source_target_pairs={{0,7},{1,6},{2,5},{3,4},{4,3},{5,2},{6,1},{7,0},{8,15},{9,14},{10,... | collective-permute-start | bytes 786440 | tf_op jit(solution)/shard_map/ppermute | solution.py:300
  74.4 3.2 %collective-permute-done.6.refs_8_ = bf16[2,128,512]{2,1,0:T(8,128)(2,1)S(1)} collective-permute-done((bf16[2,128,512]{2,1,0:T(8,128)(2,1)}, bf16[2,128,512]{2,1,0:T(8,128)(2,1)S(1)}, u32[]{:S(2)}, u32[]{:S(2)}) %collective-permute-start.6) | collective-permute-done | bytes 262176 | tf_op jit(solution)/shard_map/ppermute | solution.py:300
  78.2 5.1 %left.2 = (bf16[2,128,512]{2,1,0:T(8,128)(2,1)S(1)}, bf16[2,128,512]{2,1,0:T(8,128)(2,1)S(1)}, bf16[2,128,512]{2,1,0:T(8,128)(2,1)S(1)}, bf16[2,128,512]{2,1,0:T...) custom-call(s32[1]{0:T(128)} %bitcast.me_ref.refs_0_, ...), custom_call_target="tpu_custom_call" | custom-call | flops 4294967296 | bytes 8388608 | tf_op jit(solution)/shard_map/left/pallas_call | solution.py:121
  83.7 4.5 %collective-permute-done.11.refs_6_ = bf16[2,128,512]{2,1,0:T(8,128)(2,1)S(1)} collective-permute-done((bf16[2,128,512]{2,1,0:T(8,128)(2,1)S(1)}, bf16[2,128,512]{2,1,0:T(8,128)(2,1)S(1)}, u32[]{:S(2)}, u32[]{:S(2)}) %collective-permute-start.11) | collective-permute-done | bytes 262176 | tf_op jit(solution)/shard_map/ppermute | solution.py:300
  88.1 2.1 collective-permute-start.9
  90.2 3.5 %collective-permute-done.12.refs_7_ = bf16[2,128,512]{2,1,0:T(8,128)(2,1)S(1)} collective-permute-done((bf16[2,128,512]{2,1,0:T(8,128)(2,1)S(1)}, bf16[2,128,512]{2,1,0:T(8,128)(2,1)S(1)}, u32[]{:S(2)}, u32[]{:S(2)}) %collective-permute-start.12) | collective-permute-done | bytes 262176 | tf_op jit(solution)/shard_map/ppermute | solution.py:300
  93.8 1.2 collective-permute-start.21
  95.0 6.8 %collective-permute-done.13.refs_8_ = bf16[2,128,512]{2,1,0:T(8,128)(2,1)S(1)} collective-permute-done((bf16[2,128,512]{2,1,0:T(8,128)(2,1)S(1)}, bf16[2,128,512]{2,1,0:T(8,128)(2,1)S(1)}, u32[]{:S(2)}, u32[]{:S(2)}) %collective-permute-start.13) | collective-permute-done | bytes 262176 | tf_op jit(solution)/shard_map/ppermute | solution.py:300
  101.8 2.3 %collective-permute-start.23 = (bf16[2,128,512]{2,1,0:T(8,128)(2,1)S(1)}, bf16[2,128,512]{2,1,0:T(8,128)(2,1)S(1)}, u32[]{:S(2)}, u32[]{:S(2)}) collective-permute-start(bf16[2,128,512]{2,1,0:T(8,128)(2,1)S(1)} %get-tuple-element.73), channel_id=1, source_target_pairs={{0,3},{1,2},{2,1},{3,0},{4,7},{5,6},{6,5},{7,4},{8,11},{9,10},{10,... | collective-permute-start | bytes 786440 | tf_op jit(solution)/shard_map/ppermute | solution.py:300
  104.2 1.4 collective-permute-start.24
  105.5 1.1 collective-permute-start.25
  106.6 5.4 %collective-permute-done.21.refs_2_ = bf16[2,128,512]{2,1,0:T(8,128)(2,1)S(1)} collective-permute-done((bf16[2,128,512]{2,1,0:T(8,128)(2,1)S(1)}, bf16[2,128,512]{2,1,0:T(8,128)(2,1)S(1)}, u32[]{:S(2)}, u32[]{:S(2)}) %collective-permute-start.21) | collective-permute-done | bytes 262176 | tf_op jit(solution)/shard_map/ppermute | solution.py:300
  111.9 2.4 %collective-permute-start.26 = (bf16[2,128,512]{2,1,0:T(8,128)(2,1)S(1)}, bf16[2,128,512]{2,1,0:T(8,128)(2,1)S(1)}, u32[]{:S(2)}, u32[]{:S(2)}) collective-permute-start(bf16[2,128,512]{2,1,0:T(8,128)(2,1)S(1)} %get-tuple-element.76), channel_id=1, source_target_pairs={{0,6},{1,7},{2,4},{3,5},{4,2},{5,3},{6,0},{7,1},{8,14},{9,15},{10,... | collective-permute-start | bytes 786440 | tf_op jit(solution)/shard_map/ppermute | solution.py:300
  114.7 5.8 %left.3 = (bf16[2,128,512]{2,1,0:T(8,128)(2,1)S(1)}, bf16[2,128,512]{2,1,0:T(8,128)(2,1)S(1)}, bf16[2,128,512]{2,1,0:T(8,128)(2,1)S(1)}, bf16[2,128,512]{2,1,0:T...) custom-call(s32[1]{0:T(128)} %bitcast.me_ref.refs_0_, ...), custom_call_target="tpu_custom_call" | custom-call | flops 4294967296 | bytes 8388608 | tf_op jit(solution)/shard_map/left/pallas_call | solution.py:121
  121.3 2.2 collective-permute-start.15
  123.5 1.9 collective-permute-done.25.refs_6_
  125.4 17.6 %collective-permute-done.26.refs_7_ = bf16[2,128,512]{2,1,0:T(8,128)(2,1)S(1)} collective-permute-done((bf16[2,128,512]{2,1,0:T(8,128)(2,1)S(1)}, bf16[2,128,512]{2,1,0:T(8,128)(2,1)S(1)}, u32[]{:S(2)}, u32[]{:S(2)}) %collective-permute-start.26) | collective-permute-done | bytes 262176 | tf_op jit(solution)/shard_map/ppermute | solution.py:300
  143.0 7.7 %collective-permute-done.27.refs_8_ = bf16[2,128,512]{2,1,0:T(8,128)(2,1)S(1)} collective-permute-done((bf16[2,128,512]{2,1,0:T(8,128)(2,1)S(1)}, bf16[2,128,512]{2,1,0:T(8,128)(2,1)S(1)}, u32[]{:S(2)}, u32[]{:S(2)}) %collective-permute-start.27) | collective-permute-done | bytes 262176 | tf_op jit(solution)/shard_map/ppermute | solution.py:300
  150.7 3.7 %sine_bitcast_fusion = (f32[4,128,512]{2,1,0:T(8,128)S(1)}, f32[4,128,512]{2,1,0:T(8,128)S(1)}) fusion(f32[128,4,512]{2,1,0:T(4,128)S(1)} %copy-done.6), kind=kLoop, calls=%fused_computation | loop fusion | bytes 3145728 | tf_op jit(solution)/shard_map/sin | solution.py:338
  154.4 4.4 %phase.1 = (bf16[2,1,128,512]{3,2,1,0:T(8,128)(2,1)}, bf16[2,1,128,512]{3,2,1,0:T(8,128)(2,1)}, bf16[2,1,128,512]{3,2,1,0:T(8,128)(2,1)}, bf16[2,1,128,512]{3,2,...) custom-call(s32[1]{0:T(128)} %bitcast.me_ref.refs_0_, ...), custom_call_target="tpu_custom_call" | custom-call | flops 2147483648 | bytes 4194304 | tf_op jit(solution)/shard_map/phase/pallas_call | solution.py:192
  158.9 2.7 %collective-permute-start.19 = (bf16[2,128,512]{2,1,0:T(8,128)(2,1)}, bf16[2,128,512]{2,1,0:T(8,128)(2,1)}, u32[]{:S(2)}, u32[]{:S(2)}) collective-permute-start(bf16[2,128,512]{2,1,0:T(8,128)(2,1)} %get-tuple-element.69), channel_id=1, source_target_pairs={{0,6},{1,7},{2,4},{3,5},{4,2},{5,3},{6,0},{7,1},{8,14},{9,15},{10,... | collective-permute-start | bytes 786440 | tf_op jit(solution)/shard_map/ppermute | solution.py:300
  161.6 19.9 %collective-permute-start.28 = (bf16[2,1,128,512]{3,2,1,0:T(8,128)(2,1)}, bf16[2,1,128,512]{3,2,1,0:T(8,128)(2,1)}, u32[]{:S(2)}, u32[]{:S(2)}) collective-permute-start(bf16[2,1,128,512]{3,2,1,0:T(8,128)(2,1)} %get-tuple-element.79), channel_id=1, source_target_pairs={{0,8},{8,16},{16,24},{1,9},{9,17},{17,25},{2,10},{10,18},{18,26},{... | collective-permute-start | bytes 786440 | tf_op jit(solution)/shard_map/ppermute | solution.py:307
  181.6 1.9 collective-permute-start.29
  184.2 8.5 %collective-permute-start.30 = (bf16[2,1,128,512]{3,2,1,0:T(8,128)(2,1)}, bf16[2,1,128,512]{3,2,1,0:T(8,128)(2,1)}, u32[]{:S(2)}, u32[]{:S(2)}) collective-permute-start(bf16[2,1,128,512]{3,2,1,0:T(8,128)(2,1)} %get-tuple-element.81), channel_id=1, source_target_pairs={{0,8},{8,16},{16,24},{1,9},{9,17},{17,25},{2,10},{10,18},{18,26},{... | collective-permute-start | bytes 786440 | tf_op jit(solution)/shard_map/ppermute | solution.py:307
  192.8 5.2 %collective-permute-start.31 = (bf16[2,1,128,512]{3,2,1,0:T(8,128)(2,1)}, bf16[2,1,128,512]{3,2,1,0:T(8,128)(2,1)}, u32[]{:S(2)}, u32[]{:S(2)}) collective-permute-start(bf16[2,1,128,512]{3,2,1,0:T(8,128)(2,1)} %get-tuple-element.82), channel_id=1, source_target_pairs={{0,8},{8,16},{16,24},{1,9},{9,17},{17,25},{2,10},{10,18},{18,26},{... | collective-permute-start | bytes 786440 | tf_op jit(solution)/shard_map/ppermute | solution.py:307
  198.1 2.2 collective-permute-start.32
  200.3 1.9 collective-permute-start.33
  202.2 1.9 collective-permute-start.34
  204.1 1.9 collective-permute-start.35
  206.4 2.5 %collective-permute-done.33.refs_14_ = bf16[2,1,128,512]{3,2,1,0:T(8,128)(2,1)} collective-permute-done((bf16[2,1,128,512]{3,2,1,0:T(8,128)(2,1)}, bf16[2,1,128,512]{3,2,1,0:T(8,128)(2,1)}, u32[]{:S(2)}, u32[]{:S(2)}) %collective-permute-start.33) | collective-permute-done | bytes 262176 | tf_op jit(solution)/shard_map/ppermute | solution.py:307
  208.9 2.8 %collective-permute-done.34.refs_15_ = bf16[2,1,128,512]{3,2,1,0:T(8,128)(2,1)} collective-permute-done((bf16[2,1,128,512]{3,2,1,0:T(8,128)(2,1)}, bf16[2,1,128,512]{3,2,1,0:T(8,128)(2,1)}, u32[]{:S(2)}, u32[]{:S(2)}) %collective-permute-start.34) | collective-permute-done | bytes 262176 | tf_op jit(solution)/shard_map/ppermute | solution.py:307
  211.7 2.8 %collective-permute-done.35.refs_16_ = bf16[2,1,128,512]{3,2,1,0:T(8,128)(2,1)} collective-permute-done((bf16[2,1,128,512]{3,2,1,0:T(8,128)(2,1)}, bf16[2,1,128,512]{3,2,1,0:T(8,128)(2,1)}, u32[]{:S(2)}, u32[]{:S(2)}) %collective-permute-start.35) | collective-permute-done | bytes 262176 | tf_op jit(solution)/shard_map/ppermute | solution.py:307
  214.5 9.1 %mix.1 = bf16[128,2,4,16,128]{4,3,2,1,0:T(8,128)(2,1)} custom-call(s32[1]{0:T(128)} %bitcast.me_ref.refs_0_, f32[4,4]{1,0:T(4,128)S(1)} %get-tuple-element.90.up_ref, f32[4,4]{1,0:T(4,128)S(1)} %get-tuple-element.89.down_ref, bf16[1024,512]{1,0:T(8,128)(2,1)S(1)} %bitcast.26, f32[4,128,512]{2,1,0:T(8,128)S(1)} %get-tuple-element.88.cosine_ref, ...), custom_call_target="tpu_custom_call" | custom-call | flops 2147483648 | bytes 10485760 | tf_op jit(solution)/shard_map/mix/pallas_call | solution.py:273
  (64 shorter events, 3.6 us)
Async XLA Ops:
  5.7 7.4 %collective-permute-start = (bf16[2,128,512]{2,1,0:T(8,128)(2,1)}, bf16[2,128,512]{2,1,0:T(8,128)(2,1)S(1)}, u32[]{:S(2)}, u32[]{:S(2)}) collective-permute-start(bf16[2,128,512]{2,1,0:T(8,128)(2,1)} %get-tuple-element.48), channel_id=1, source_target_pairs={{0,1},{1,0},{2,3},{3,2},{4,5},{5,4},{6,7},{7,6},{8,9},{9,8},{10,11... | collective-permute-start | bytes 786440 | tf_op jit(solution)/shard_map/ppermute | solution.py:300
  7.0 15.0 %collective-permute-start.1 = (bf16[2,128,512]{2,1,0:T(8,128)(2,1)}, bf16[2,128,512]{2,1,0:T(8,128)(2,1)S(1)}, u32[]{:S(2)}, u32[]{:S(2)}) collective-permute-start(bf16[2,128,512]{2,1,0:T(8,128)(2,1)} %get-tuple-element.49), channel_id=1, source_target_pairs={{0,2},{1,3},{2,0},{3,1},{4,6},{5,7},{6,4},{7,5},{8,10},{9,11},{10,... | collective-permute-start | bytes 786440 | tf_op jit(solution)/shard_map/ppermute | solution.py:300
  7.1 26.5 %collective-permute-start.2 = (bf16[2,128,512]{2,1,0:T(8,128)(2,1)}, bf16[2,128,512]{2,1,0:T(8,128)(2,1)S(1)}, u32[]{:S(2)}, u32[]{:S(2)}) collective-permute-start(bf16[2,128,512]{2,1,0:T(8,128)(2,1)} %get-tuple-element.50), channel_id=1, source_target_pairs={{0,3},{1,2},{2,1},{3,0},{4,7},{5,6},{6,5},{7,4},{8,11},{9,10},{10,... | collective-permute-start | bytes 786440 | tf_op jit(solution)/shard_map/ppermute | solution.py:300
  8.4 28.9 %collective-permute-start.3 = (bf16[2,128,512]{2,1,0:T(8,128)(2,1)}, bf16[2,128,512]{2,1,0:T(8,128)(2,1)S(1)}, u32[]{:S(2)}, u32[]{:S(2)}) collective-permute-start(bf16[2,128,512]{2,1,0:T(8,128)(2,1)} %get-tuple-element.51), channel_id=1, source_target_pairs={{0,4},{1,5},{2,6},{3,7},{4,0},{5,1},{6,2},{7,3},{8,12},{9,13},{10,... | collective-permute-start | bytes 786440 | tf_op jit(solution)/shard_map/ppermute | solution.py:300
  10.7 43.7 %collective-permute-start.4 = (bf16[2,128,512]{2,1,0:T(8,128)(2,1)}, bf16[2,128,512]{2,1,0:T(8,128)(2,1)S(1)}, u32[]{:S(2)}, u32[]{:S(2)}) collective-permute-start(bf16[2,128,512]{2,1,0:T(8,128)(2,1)} %get-tuple-element.52), channel_id=1, source_target_pairs={{0,5},{1,4},{2,7},{3,6},{4,1},{5,0},{6,3},{7,2},{8,13},{9,12},{10,... | collective-permute-start | bytes 786440 | tf_op jit(solution)/shard_map/ppermute | solution.py:300
  13.1 49.7 %collective-permute-start.5 = (bf16[2,128,512]{2,1,0:T(8,128)(2,1)}, bf16[2,128,512]{2,1,0:T(8,128)(2,1)S(1)}, u32[]{:S(2)}, u32[]{:S(2)}) collective-permute-start(bf16[2,128,512]{2,1,0:T(8,128)(2,1)} %get-tuple-element.53), channel_id=1, source_target_pairs={{0,6},{1,7},{2,4},{3,5},{4,2},{5,3},{6,0},{7,1},{8,14},{9,15},{10,... | collective-permute-start | bytes 786440 | tf_op jit(solution)/shard_map/ppermute | solution.py:300
  22.0 55.6 %collective-permute-start.6 = (bf16[2,128,512]{2,1,0:T(8,128)(2,1)}, bf16[2,128,512]{2,1,0:T(8,128)(2,1)S(1)}, u32[]{:S(2)}, u32[]{:S(2)}) collective-permute-start(bf16[2,128,512]{2,1,0:T(8,128)(2,1)} %get-tuple-element.54), channel_id=1, source_target_pairs={{0,7},{1,6},{2,5},{3,4},{4,3},{5,2},{6,1},{7,0},{8,15},{9,14},{10,... | collective-permute-start | bytes 786440 | tf_op jit(solution)/shard_map/ppermute | solution.py:300
  22.0 6.7 %copy-start.1 = (bf16[2,512,512]{2,1,0:T(8,128)(2,1)S(1)}, bf16[2,512,512]{2,1,0:T(8,128)(2,1)}, u32[]{:S(2)}) copy-start(bf16[2,512,512]{2,1,0:T(8,128)(2,1)} %param.8) | copy-start | bytes 3145732
  22.0 6.7 %copy-start.5 = (bf16[2,128,512]{2,1,0:T(8,128)(2,1)S(1)}, bf16[2,128,512]{2,1,0:T(8,128)(2,1)}, u32[]{:S(2)}) copy-start(bf16[2,128,512]{2,1,0:T(8,128)(2,1)} %get-tuple-element.46.refs_0_.refs_1_) | copy-start | bytes 786436
  28.7 2.2 copy-start
  30.9 47.3 %copy-start.2 = (bf16[2048,1024]{0,1:T(8,128)(2,1)S(1)}, bf16[2048,1024]{0,1:T(8,128)(2,1)}, u32[]{:S(2)}) copy-start(bf16[2048,1024]{0,1:T(8,128)(2,1)} %copy.14) | copy-start | bytes 12582916
  33.7 49.6 %collective-permute-start.10 = (bf16[2,128,512]{2,1,0:T(8,128)(2,1)S(1)}, bf16[2,128,512]{2,1,0:T(8,128)(2,1)S(1)}, u32[]{:S(2)}, u32[]{:S(2)}) collective-permute-start(bf16[2,128,512]{2,1,0:T(8,128)(2,1)S(1)} %get-tuple-element.59), channel_id=1, source_target_pairs={{0,4},{1,5},{2,6},{3,7},{4,0},{5,1},{6,2},{7,3},{8,12},{9,13},{10,... | collective-permute-start | bytes 786440 | tf_op jit(solution)/shard_map/ppermute | solution.py:300
  37.2 50.9 %collective-permute-start.11 = (bf16[2,128,512]{2,1,0:T(8,128)(2,1)S(1)}, bf16[2,128,512]{2,1,0:T(8,128)(2,1)S(1)}, u32[]{:S(2)}, u32[]{:S(2)}) collective-permute-start(bf16[2,128,512]{2,1,0:T(8,128)(2,1)S(1)} %get-tuple-element.60), channel_id=1, source_target_pairs={{0,5},{1,4},{2,7},{3,6},{4,1},{5,0},{6,3},{7,2},{8,13},{9,12},{10,... | collective-permute-start | bytes 786440 | tf_op jit(solution)/shard_map/ppermute | solution.py:300
  54.4 39.4 %collective-permute-start.12 = (bf16[2,128,512]{2,1,0:T(8,128)(2,1)S(1)}, bf16[2,128,512]{2,1,0:T(8,128)(2,1)S(1)}, u32[]{:S(2)}, u32[]{:S(2)}) collective-permute-start(bf16[2,128,512]{2,1,0:T(8,128)(2,1)S(1)} %get-tuple-element.61), channel_id=1, source_target_pairs={{0,6},{1,7},{2,4},{3,5},{4,2},{5,3},{6,0},{7,1},{8,14},{9,15},{10,... | collective-permute-start | bytes 786440 | tf_op jit(solution)/shard_map/ppermute | solution.py:300
  62.8 39.0 %collective-permute-start.13 = (bf16[2,128,512]{2,1,0:T(8,128)(2,1)S(1)}, bf16[2,128,512]{2,1,0:T(8,128)(2,1)S(1)}, u32[]{:S(2)}, u32[]{:S(2)}) collective-permute-start(bf16[2,128,512]{2,1,0:T(8,128)(2,1)S(1)} %get-tuple-element.62), channel_id=1, source_target_pairs={{0,7},{1,6},{2,5},{3,4},{4,3},{5,2},{6,1},{7,0},{8,15},{9,14},{10,... | collective-permute-start | bytes 786440 | tf_op jit(solution)/shard_map/ppermute | solution.py:300
  77.6 24.2 %collective-permute-start.7 = (bf16[2,128,512]{2,1,0:T(8,128)(2,1)S(1)}, bf16[2,128,512]{2,1,0:T(8,128)(2,1)S(1)}, u32[]{:S(2)}, u32[]{:S(2)}) collective-permute-start(bf16[2,128,512]{2,1,0:T(8,128)(2,1)S(1)} %get-tuple-element.56), channel_id=1, source_target_pairs={{0,1},{1,0},{2,3},{3,2},{4,5},{5,4},{6,7},{7,6},{8,9},{9,8},{10,11... | collective-permute-start | bytes 786440 | tf_op jit(solution)/shard_map/ppermute | solution.py:300
  83.3 20.8 %collective-permute-start.8 = (bf16[2,128,512]{2,1,0:T(8,128)(2,1)S(1)}, bf16[2,128,512]{2,1,0:T(8,128)(2,1)S(1)}, u32[]{:S(2)}, u32[]{:S(2)}) collective-permute-start(bf16[2,128,512]{2,1,0:T(8,128)(2,1)S(1)} %get-tuple-element.57), channel_id=1, source_target_pairs={{0,2},{1,3},{2,0},{3,1},{4,6},{5,7},{6,4},{7,5},{8,10},{9,11},{10,... | collective-permute-start | bytes 786440 | tf_op jit(solution)/shard_map/ppermute | solution.py:300
  88.1 17.4 %collective-permute-start.9 = (bf16[2,128,512]{2,1,0:T(8,128)(2,1)S(1)}, bf16[2,128,512]{2,1,0:T(8,128)(2,1)S(1)}, u32[]{:S(2)}, u32[]{:S(2)}) collective-permute-start(bf16[2,128,512]{2,1,0:T(8,128)(2,1)S(1)} %get-tuple-element.58), channel_id=1, source_target_pairs={{0,3},{1,2},{2,1},{3,0},{4,7},{5,6},{6,5},{7,4},{8,11},{9,10},{10,... | collective-permute-start | bytes 786440 | tf_op jit(solution)/shard_map/ppermute | solution.py:300
  93.8 18.2 %collective-permute-start.21 = (bf16[2,128,512]{2,1,0:T(8,128)(2,1)S(1)}, bf16[2,128,512]{2,1,0:T(8,128)(2,1)S(1)}, u32[]{:S(2)}, u32[]{:S(2)}) collective-permute-start(bf16[2,128,512]{2,1,0:T(8,128)(2,1)S(1)} %get-tuple-element.71), channel_id=1, source_target_pairs={{0,1},{1,0},{2,3},{3,2},{4,5},{5,4},{6,7},{7,6},{8,9},{9,8},{10,11... | collective-permute-start | bytes 786440 | tf_op jit(solution)/shard_map/ppermute | solution.py:300
  101.8 12.5 %collective-permute-start.22 = (bf16[2,128,512]{2,1,0:T(8,128)(2,1)S(1)}, bf16[2,128,512]{2,1,0:T(8,128)(2,1)S(1)}, u32[]{:S(2)}, u32[]{:S(2)}) collective-permute-start(bf16[2,128,512]{2,1,0:T(8,128)(2,1)S(1)} %get-tuple-element.72), channel_id=1, source_target_pairs={{0,2},{1,3},{2,0},{3,1},{4,6},{5,7},{6,4},{7,5},{8,10},{9,11},{10,... | collective-permute-start | bytes 786440 | tf_op jit(solution)/shard_map/ppermute | solution.py:300
  101.8 18.6 %collective-permute-start.23 = (bf16[2,128,512]{2,1,0:T(8,128)(2,1)S(1)}, bf16[2,128,512]{2,1,0:T(8,128)(2,1)S(1)}, u32[]{:S(2)}, u32[]{:S(2)}) collective-permute-start(bf16[2,128,512]{2,1,0:T(8,128)(2,1)S(1)} %get-tuple-element.73), channel_id=1, source_target_pairs={{0,3},{1,2},{2,1},{3,0},{4,7},{5,6},{6,5},{7,4},{8,11},{9,10},{10,... | collective-permute-start | bytes 786440 | tf_op jit(solution)/shard_map/ppermute | solution.py:300
  104.2 17.1 %collective-permute-start.24 = (bf16[2,128,512]{2,1,0:T(8,128)(2,1)S(1)}, bf16[2,128,512]{2,1,0:T(8,128)(2,1)S(1)}, u32[]{:S(2)}, u32[]{:S(2)}) collective-permute-start(bf16[2,128,512]{2,1,0:T(8,128)(2,1)S(1)} %get-tuple-element.74), channel_id=1, source_target_pairs={{0,4},{1,5},{2,6},{3,7},{4,0},{5,1},{6,2},{7,3},{8,12},{9,13},{10,... | collective-permute-start | bytes 786440 | tf_op jit(solution)/shard_map/ppermute | solution.py:300
  105.5 19.9 %collective-permute-start.25 = (bf16[2,128,512]{2,1,0:T(8,128)(2,1)S(1)}, bf16[2,128,512]{2,1,0:T(8,128)(2,1)S(1)}, u32[]{:S(2)}, u32[]{:S(2)}) collective-permute-start(bf16[2,128,512]{2,1,0:T(8,128)(2,1)S(1)} %get-tuple-element.75), channel_id=1, source_target_pairs={{0,5},{1,4},{2,7},{3,6},{4,1},{5,0},{6,3},{7,2},{8,13},{9,12},{10,... | collective-permute-start | bytes 786440 | tf_op jit(solution)/shard_map/ppermute | solution.py:300
  111.9 31.1 %collective-permute-start.26 = (bf16[2,128,512]{2,1,0:T(8,128)(2,1)S(1)}, bf16[2,128,512]{2,1,0:T(8,128)(2,1)S(1)}, u32[]{:S(2)}, u32[]{:S(2)}) collective-permute-start(bf16[2,128,512]{2,1,0:T(8,128)(2,1)S(1)} %get-tuple-element.76), channel_id=1, source_target_pairs={{0,6},{1,7},{2,4},{3,5},{4,2},{5,3},{6,0},{7,1},{8,14},{9,15},{10,... | collective-permute-start | bytes 786440 | tf_op jit(solution)/shard_map/ppermute | solution.py:300
  114.3 36.4 %collective-permute-start.27 = (bf16[2,128,512]{2,1,0:T(8,128)(2,1)S(1)}, bf16[2,128,512]{2,1,0:T(8,128)(2,1)S(1)}, u32[]{:S(2)}, u32[]{:S(2)}) collective-permute-start(bf16[2,128,512]{2,1,0:T(8,128)(2,1)S(1)} %get-tuple-element.77), channel_id=1, source_target_pairs={{0,7},{1,6},{2,5},{3,4},{4,3},{5,2},{6,1},{7,0},{8,15},{9,14},{10,... | collective-permute-start | bytes 786440 | tf_op jit(solution)/shard_map/ppermute | solution.py:300
  114.7 36.0 %copy-start.6 = (f32[128,4,512]{2,1,0:T(4,128)S(1)}, f32[128,4,512]{2,1,0:T(4,128)}, u32[]{:S(2)}) copy-start(f32[128,4,512]{2,1,0:T(4,128)} %param.9) | copy-start | bytes 3145732
  120.5 38.4 %copy-start.4 = (bf16[2,128,512]{2,1,0:T(8,128)(2,1)}, bf16[2,128,512]{2,1,0:T(8,128)(2,1)S(1)}, u32[]{:S(2)}) copy-start(bf16[2,128,512]{2,1,0:T(8,128)(2,1)S(1)} %get-tuple-element.63.refs_0_) | copy-start | bytes 786436
  120.5 38.4 %collective-permute-start.14 = (bf16[2,128,512]{2,1,0:T(8,128)(2,1)S(1)}, bf16[2,128,512]{2,1,0:T(8,128)(2,1)S(1)}, u32[]{:S(2)}, u32[]{:S(2)}) collective-permute-start(bf16[2,128,512]{2,1,0:T(8,128)(2,1)S(1)} %get-tuple-element.64), channel_id=1, source_target_pairs={{0,1},{1,0},{2,3},{3,2},{4,5},{5,4},{6,7},{7,6},{8,9},{9,8},{10,11... | collective-permute-start | bytes 786440 | tf_op jit(solution)/shard_map/ppermute | solution.py:300
  121.3 40.3 %collective-permute-start.15 = (bf16[2,128,512]{2,1,0:T(8,128)(2,1)S(1)}, bf16[2,128,512]{2,1,0:T(8,128)(2,1)S(1)}, u32[]{:S(2)}, u32[]{:S(2)}) collective-permute-start(bf16[2,128,512]{2,1,0:T(8,128)(2,1)S(1)} %get-tuple-element.65), channel_id=1, source_target_pairs={{0,2},{1,3},{2,0},{3,1},{4,6},{5,7},{6,4},{7,5},{8,10},{9,11},{10,... | collective-permute-start | bytes 786440 | tf_op jit(solution)/shard_map/ppermute | solution.py:300
  125.4 36.2 %collective-permute-start.16 = (bf16[2,128,512]{2,1,0:T(8,128)(2,1)S(1)}, bf16[2,128,512]{2,1,0:T(8,128)(2,1)S(1)}, u32[]{:S(2)}, u32[]{:S(2)}) collective-permute-start(bf16[2,128,512]{2,1,0:T(8,128)(2,1)S(1)} %get-tuple-element.66), channel_id=1, source_target_pairs={{0,3},{1,2},{2,1},{3,0},{4,7},{5,6},{6,5},{7,4},{8,11},{9,10},{10,... | collective-permute-start | bytes 786440 | tf_op jit(solution)/shard_map/ppermute | solution.py:300
  143.0 38.5 %collective-permute-start.17 = (bf16[2,128,512]{2,1,0:T(8,128)(2,1)S(1)}, bf16[2,128,512]{2,1,0:T(8,128)(2,1)S(1)}, u32[]{:S(2)}, u32[]{:S(2)}) collective-permute-start(bf16[2,128,512]{2,1,0:T(8,128)(2,1)S(1)} %get-tuple-element.67), channel_id=1, source_target_pairs={{0,4},{1,5},{2,6},{3,7},{4,0},{5,1},{6,2},{7,3},{8,12},{9,13},{10,... | collective-permute-start | bytes 786440 | tf_op jit(solution)/shard_map/ppermute | solution.py:300
  150.7 32.8 %collective-permute-start.18 = (bf16[2,128,512]{2,1,0:T(8,128)(2,1)S(1)}, bf16[2,128,512]{2,1,0:T(8,128)(2,1)S(1)}, u32[]{:S(2)}, u32[]{:S(2)}) collective-permute-start(bf16[2,128,512]{2,1,0:T(8,128)(2,1)S(1)} %get-tuple-element.68), channel_id=1, source_target_pairs={{0,5},{1,4},{2,7},{3,6},{4,1},{5,0},{6,3},{7,2},{8,13},{9,12},{10,... | collective-permute-start | bytes 786440 | tf_op jit(solution)/shard_map/ppermute | solution.py:300
  154.4 38.3 %copy-start.12 = (f32[16,4]{0,1:T(4,128)S(1)}, f32[16,4]{0,1:T(4,128)}, u32[]{:S(2)}) copy-start(f32[16,4]{0,1:T(4,128)} %param.10) | copy-start | bytes 772
  154.4 60.1 %copy-start.3 = (f32[128,512]{1,0:T(8,128)S(1)}, f32[128,512]{1,0:T(8,128)}, u32[]{:S(2)}) copy-start(f32[128,512]{1,0:T(8,128)} %weight_ref.1) | copy-start | bytes 786436
  158.9 24.6 %copy-start.7 = (bf16[2,128,512]{2,1,0:T(8,128)(2,1)}, bf16[2,128,512]{2,1,0:T(8,128)(2,1)S(1)}, u32[]{:S(2)}) copy-start(bf16[2,128,512]{2,1,0:T(8,128)(2,1)S(1)} %collective-permute-done.14.refs_1_) | copy-start | bytes 786436
  158.9 33.9 %collective-permute-start.19 = (bf16[2,128,512]{2,1,0:T(8,128)(2,1)}, bf16[2,128,512]{2,1,0:T(8,128)(2,1)}, u32[]{:S(2)}, u32[]{:S(2)}) collective-permute-start(bf16[2,128,512]{2,1,0:T(8,128)(2,1)} %get-tuple-element.69), channel_id=1, source_target_pairs={{0,6},{1,7},{2,4},{3,5},{4,2},{5,3},{6,0},{7,1},{8,14},{9,15},{10,... | collective-permute-start | bytes 786440 | tf_op jit(solution)/shard_map/ppermute | solution.py:300
  161.6 21.9 %copy-start.8 = (bf16[2,128,512]{2,1,0:T(8,128)(2,1)}, bf16[2,128,512]{2,1,0:T(8,128)(2,1)S(1)}, u32[]{:S(2)}) copy-start(bf16[2,128,512]{2,1,0:T(8,128)(2,1)S(1)} %collective-permute-done.15.refs_2_) | copy-start | bytes 786436
  161.6 36.5 %collective-permute-start.20 = (bf16[2,128,512]{2,1,0:T(8,128)(2,1)}, bf16[2,128,512]{2,1,0:T(8,128)(2,1)}, u32[]{:S(2)}, u32[]{:S(2)}) collective-permute-start(bf16[2,128,512]{2,1,0:T(8,128)(2,1)} %get-tuple-element.70), channel_id=1, source_target_pairs={{0,7},{1,6},{2,5},{3,4},{4,3},{5,2},{6,1},{7,0},{8,15},{9,14},{10,... | collective-permute-start | bytes 786440 | tf_op jit(solution)/shard_map/ppermute | solution.py:300
  161.6 21.9 %copy-start.9 = (bf16[2,128,512]{2,1,0:T(8,128)(2,1)}, bf16[2,128,512]{2,1,0:T(8,128)(2,1)S(1)}, u32[]{:S(2)}) copy-start(bf16[2,128,512]{2,1,0:T(8,128)(2,1)S(1)} %collective-permute-done.16.refs_3_) | copy-start | bytes 786436
  161.6 38.6 %collective-permute-start.28 = (bf16[2,1,128,512]{3,2,1,0:T(8,128)(2,1)}, bf16[2,1,128,512]{3,2,1,0:T(8,128)(2,1)}, u32[]{:S(2)}, u32[]{:S(2)}) collective-permute-start(bf16[2,1,128,512]{3,2,1,0:T(8,128)(2,1)} %get-tuple-element.79), channel_id=1, source_target_pairs={{0,8},{8,16},{16,24},{1,9},{9,17},{17,25},{2,10},{10,18},{18,26},{... | collective-permute-start | bytes 786440 | tf_op jit(solution)/shard_map/ppermute | solution.py:307
  181.5 2.0 copy-start.10
  181.6 20.6 %collective-permute-start.29 = (bf16[2,1,128,512]{3,2,1,0:T(8,128)(2,1)}, bf16[2,1,128,512]{3,2,1,0:T(8,128)(2,1)}, u32[]{:S(2)}, u32[]{:S(2)}) collective-permute-start(bf16[2,1,128,512]{3,2,1,0:T(8,128)(2,1)} %get-tuple-element.80), channel_id=1, source_target_pairs={{0,8},{8,16},{16,24},{1,9},{9,17},{17,25},{2,10},{10,18},{18,26},{... | collective-permute-start | bytes 786440 | tf_op jit(solution)/shard_map/ppermute | solution.py:307
  184.2 19.9 %collective-permute-start.30 = (bf16[2,1,128,512]{3,2,1,0:T(8,128)(2,1)}, bf16[2,1,128,512]{3,2,1,0:T(8,128)(2,1)}, u32[]{:S(2)}, u32[]{:S(2)}) collective-permute-start(bf16[2,1,128,512]{3,2,1,0:T(8,128)(2,1)} %get-tuple-element.81), channel_id=1, source_target_pairs={{0,8},{8,16},{16,24},{1,9},{9,17},{17,25},{2,10},{10,18},{18,26},{... | collective-permute-start | bytes 786440 | tf_op jit(solution)/shard_map/ppermute | solution.py:307
  192.8 13.6 %collective-permute-start.31 = (bf16[2,1,128,512]{3,2,1,0:T(8,128)(2,1)}, bf16[2,1,128,512]{3,2,1,0:T(8,128)(2,1)}, u32[]{:S(2)}, u32[]{:S(2)}) collective-permute-start(bf16[2,1,128,512]{3,2,1,0:T(8,128)(2,1)} %get-tuple-element.82), channel_id=1, source_target_pairs={{0,8},{8,16},{16,24},{1,9},{9,17},{17,25},{2,10},{10,18},{18,26},{... | collective-permute-start | bytes 786440 | tf_op jit(solution)/shard_map/ppermute | solution.py:307
  198.1 8.3 %collective-permute-start.32 = (bf16[2,1,128,512]{3,2,1,0:T(8,128)(2,1)}, bf16[2,1,128,512]{3,2,1,0:T(8,128)(2,1)}, u32[]{:S(2)}, u32[]{:S(2)}) collective-permute-start(bf16[2,1,128,512]{3,2,1,0:T(8,128)(2,1)} %get-tuple-element.83), channel_id=1, source_target_pairs={{8,0},{16,8},{24,16},{9,1},{17,9},{25,17},{10,2},{18,10},{26,18},{... | collective-permute-start | bytes 786440 | tf_op jit(solution)/shard_map/ppermute | solution.py:307
  200.3 8.6 %collective-permute-start.33 = (bf16[2,1,128,512]{3,2,1,0:T(8,128)(2,1)}, bf16[2,1,128,512]{3,2,1,0:T(8,128)(2,1)}, u32[]{:S(2)}, u32[]{:S(2)}) collective-permute-start(bf16[2,1,128,512]{3,2,1,0:T(8,128)(2,1)} %get-tuple-element.84), channel_id=1, source_target_pairs={{8,0},{16,8},{24,16},{9,1},{17,9},{25,17},{10,2},{18,10},{26,18},{... | collective-permute-start | bytes 786440 | tf_op jit(solution)/shard_map/ppermute | solution.py:307
  202.2 9.5 %collective-permute-start.34 = (bf16[2,1,128,512]{3,2,1,0:T(8,128)(2,1)}, bf16[2,1,128,512]{3,2,1,0:T(8,128)(2,1)}, u32[]{:S(2)}, u32[]{:S(2)}) collective-permute-start(bf16[2,1,128,512]{3,2,1,0:T(8,128)(2,1)} %get-tuple-element.85), channel_id=1, source_target_pairs={{8,0},{16,8},{24,16},{9,1},{17,9},{25,17},{10,2},{18,10},{26,18},{... | collective-permute-start | bytes 786440 | tf_op jit(solution)/shard_map/ppermute | solution.py:307
  204.1 10.4 %collective-permute-start.35 = (bf16[2,1,128,512]{3,2,1,0:T(8,128)(2,1)}, bf16[2,1,128,512]{3,2,1,0:T(8,128)(2,1)}, u32[]{:S(2)}, u32[]{:S(2)}) collective-permute-start(bf16[2,1,128,512]{3,2,1,0:T(8,128)(2,1)} %get-tuple-element.86), channel_id=1, source_target_pairs={{8,0},{16,8},{24,16},{9,1},{17,9},{25,17},{10,2},{18,10},{26,18},{... | collective-permute-start | bytes 786440 | tf_op jit(solution)/shard_map/ppermute | solution.py:307
  (1 other events, 0.7 us)

commit v13 on v12

--- a/solution.py
+++ b/solution.py
@@ -32,19 +32,17 @@
     return jnp.concatenate([real, -imag], 1), jnp.concatenate([imag, real], 1)
 
 
-def right_kernel(after, ranks, states, me_ref, second_ref, *refs):
+def right_kernel(after, chosen, states, me_ref, second_ref, *refs):
     refs = refs[after:]
-    kinds = len(refs) - 1 - ranks
-    packets, outs, slabs = refs[:kinds], refs[kinds:-1], refs[-1]
+    packet, outs, slabs = refs[0], refs[1:-1], refs[-1]
     me = me_ref[0]
-    rows = packets[0].shape[0]
-    group = packets[0].shape[2]
+    rows, _, _, group, _ = packet.shape
     tiles = group // states
     piece = slabs.shape[2] // 2
     cuts = tiles * LANES // piece
-    for n, packet in enumerate(packets):
+    for n, k in enumerate(chosen):
         turned = [
-            packet[:, c].astype(jnp.float32).transpose(1, 0, 2).astype(jnp.bfloat16)
+            packet[:, c, k].astype(jnp.float32).transpose(1, 0, 2).astype(jnp.bfloat16)
             for c in range(2)
         ]
 
@@ -67,19 +65,16 @@
 
 
 def right_call(after, me, second, view, chosen, ranks, states, piece, limit):
-    rows, _, _, group, _ = view.shape
+    rows, _, blocks, group, _ = view.shape
     width = second.shape[1]
-    block = rows
+    block = rows // 2
     kinds = len(chosen)
     return pl.pallas_call(
-        functools.partial(right_kernel, len(after), ranks, states),
+        functools.partial(right_kernel, len(after), tuple(chosen), states),
         grid=(rows // block,),
         in_specs=[SMEM, pl.BlockSpec(second.shape, lambda i: (0, 0))]
         + [AFTER] * len(after)
-        + [
-            pl.BlockSpec((block, 2, None, group, LANES), lambda i, k=k: (i, 0, k, 0, 0))
-            for k in chosen
-        ],
+        + [pl.BlockSpec((block, 2, blocks, group, LANES), lambda i: (i, 0, 0, 0, 0))],
         out_specs=[pl.BlockSpec((kinds, block, 2 * piece), lambda i: (0, i, 0))] * ranks,
         out_shape=[jax.ShapeDtypeStruct((kinds, rows, 2 * piece), jnp.bfloat16)] * ranks,
         scratch_shapes=[
@@ -90,7 +85,7 @@
             8 * kinds * states * rows * width * width, 8 * kinds * states * rows * width
         ),
         name="right",
-    )(me, second, *after, *([view] * kinds))
+    )(me, second, *after, view)
 
 
 def left_kernel(after, ranks, me_ref, first_ref, *refs):
@@ -170,15 +165,15 @@
     states, rows, width = cosine_ref.shape
     share = outs[0].shape[1]
     pieces = states // share
-    for n in range(len(outs) // pieces):
+    for n in range(whole.shape[0]):
         product = phased_product(
             me_ref[0], n, second_ref, cosine_ref, sine_ref, ins, range(ranks), slabs
         )
-        for c in range(2):
-            for j in range(states):
-                first = (c * states + j) * rows
-                outs[n * pieces + j // share][c, j % share] = product[first : first + rows]
         whole[n] = product.reshape(2, states, rows, width)
+    for n, out in enumerate(outs):
+        end = me_ref[1] if n < pieces else 1 - me_ref[1]
+        first = n % pieces * share
+        out[...] = whole[end, :, first : first + share]
 
 
 def phase_call(after, me, second, cosine, sine, slabs):
@@ -212,17 +207,21 @@
     chosen, order, me_ref, up_ref, down_ref, second_ref, cosine_ref, sine_ref, weight_ref, *refs
 ):
     ranks = len(order)
-    ins, edges, halo, (out, slabs, fresh) = (
+    ins, edges, pairs, (out, slabs, fresh, halo) = (
         refs[:ranks],
         refs[ranks],
-        refs[ranks + 1 : -3],
-        refs[-3:],
+        refs[ranks + 1 : -4],
+        refs[-4:],
     )
     blocks, states = up_ref.shape
     rows, width = weight_ref.shape
-    share = halo[0].shape[1]
+    share = pairs[0].shape[1]
     pieces = states // share
     group = out.shape[3]
+    for n, part in enumerate(pairs):
+        end = me_ref[1] if n < pieces else 1 - me_ref[1]
+        first = n % pieces * share
+        halo[end, :, first : first + share] = part[...]
     others = [k for k in range(blocks) if k not in chosen]
     for n in range(len(chosen)):
         product = phased_product(
@@ -236,7 +235,7 @@
         elif k in others:
             value = edges[others.index(k), c, j, span]
         else:
-            value = halo[(k > 0) * pieces + j // share][c, j % share, span]
+            value = halo[int(k > 0), c, j, span]
         return value.astype(jnp.float32)
 
     for first in range(0, rows, ROWS):
@@ -284,6 +283,7 @@
         scratch_shapes=[
             pltpu.VMEM((ranks, block, wide), jnp.bfloat16),
             pltpu.VMEM((kinds, 2, states, block, width), jnp.bfloat16),
+            pltpu.VMEM((2, 2, states, block, width), jnp.bfloat16),
         ],
         compiler_params=params(LIMIT + LIMIT // 2),
         cost_estimate=cost(
@@ -301,10 +301,10 @@
     return result
 
 
-def neighbour(edge, axis, step):
+def paired(edge, axis, first):
     count = lax.axis_size(axis)
-    pairs = [(i, i + step) for i in range(count) if 0 <= i + step < count]
-    return lax.ppermute(edge, axis, pairs)
+    pairs = [(i, i + 1) for i in range(first, count - 1, 2)]
+    return lax.ppermute(edge, axis, pairs + [(j, i) for i, j in pairs])
 
 
 def per_device(packet, first_propagator, second_propagator, potential, coupling, radial_weight):
@@ -314,6 +314,7 @@
     tiles = width // LANES
     piece = states * width // ranks
     me = lax.axis_index("rad").astype(jnp.int32).reshape(1)
+    place = jnp.stack([lax.axis_index("rad"), lax.axis_index("hel") % 2]).astype(jnp.int32)
     second = second_propagator.reshape(2 * width, width)
     first = first_propagator.reshape(2 * whole, whole).T
     view = packet.reshape(rows, 2, blocks, states, tiles, LANES).transpose(0, 1, 2, 4, 3, 5)
@@ -336,10 +337,9 @@
 
     angles = potential.transpose(1, 0, 2)
     cosine, sine = jnp.cos(angles), jnp.sin(angles)
-    edge = phase_call([last], me, second, cosine, sine, backs[0])
-    low, high, edges_here = edge[:PIECES], edge[-PIECES - 1 : -1], edge[-1]
-    below = [neighbour(x, "hel", 1) for x in high]
-    above = [neighbour(x, "hel", -1) for x in low]
+    edge = phase_call([last], place, second, cosine, sine, backs[0])
+    halo = [paired(x, "hel", 1) for x in edge[:PIECES]]
+    halo += [paired(x, "hel", 0) for x in edge[PIECES:-1]]
 
     count = coupling.shape[0]
     helicities = jnp.arange(count, dtype=jnp.int32)
@@ -350,9 +350,8 @@
     start = lax.axis_index("hel") * blocks
     up = lax.dynamic_slice_in_dim(couple_up, start, blocks, 0)
     down = lax.dynamic_slice_in_dim(couple_down, start, blocks, 0)
-    halo = [*below, *above]
     out = mix_call(
-        me, up, down, second, cosine, sine, radial_weight, chunks[1], backs[1], edges_here, halo
+        place, up, down, second, cosine, sine, radial_weight, chunks[1], backs[1], edge[-1], halo
     )
     out = out.reshape(rows, 2, blocks, tiles, states, LANES).transpose(0, 1, 2, 4, 3, 5)
     return out.reshape(rows, 2, blocks, states, width)

time: 224 us -> 218 us (0.973)
  waiting for transfers between devices: 91.6 us -> 86.1 us
  starting transfers between devices: 85.1 us -> 80.7 us
    ppermute x8, starting transfers between devices: 43.5 us -> 38 us  [paired(): return lax.ppermute(edge, axis, pairs + [(j, i) for i, j in pairs])]
    ppermute x8, waiting for transfers between devices: 8.1 us -> 2.92 us  [paired(): return lax.ppermute(edge, axis, pairs + [(j, i) for i, j in pairs])]
  transfers between devices with their start and end apart: 36 -> 36, of which waited for: 15 -> 15; matrix products, arithmetic and copies ran while one was open for 5% -> 5% of each run, Pallas kernels for 8% -> 9%
where the time goes in v13:
time: 218 us; the launch traced here: 216 us
  waiting for transfers between devices  86.1 us (39%)
  starting transfers between devices  80.7 us (37%)
  Pallas kernels  34.3 us (16%)
  local copies, waits for them, and re-layouts  14.3 us (7%)
    ppermute x28, waiting for transfers between devices, exchanged(): result[s] = lax.ppermute(slabs[s], axis, [(i, i ^ s) for i in range(count)])  83.2 us
    ppermute x28, starting transfers between devices, exchanged(): result[s] = lax.ppermute(slabs[s], axis, [(i, i ^ s) for i in range(count)])  42.8 us
    ppermute x8, starting transfers between devices, paired(): return lax.ppermute(edge, axis, pairs + [(j, i) for i, j in pairs])  38 us
    pallas_call x2, Pallas kernels, left_call(): pl.pallas_call(functools.partial(left_kernel, len(after), ranks), grid=(k...  10.8 us
    pallas_call x2, Pallas kernels, right_call(): pl.pallas_call(functools.partial(right_kernel, len(after), tuple(chosen),...  9.35 us
    pallas_call x1, Pallas kernels, mix_call(): pl.pallas_call(functools.partial(mix_kernel, tuple(chosen), order), grid=...  9.07 us
    reshape x1, local copies, waits for them, and re-layouts, per_device(): first = first_propagator.reshape(2 * whole, whole).T  6.53 us
    pallas_call x1, Pallas kernels, phase_call(): pl.pallas_call(functools.partial(phase_kernel, len(after), ranks), grid=(...  5.05 us
  transfers between devices with their start and end apart: 36, of which 15 were waited for; matrix products, arithmetic and copies ran while one was open for 5% of the time, Pallas kernels for 9%

profile of v13, /device:TPU:9, one launch (start us, length us, event | category | flops | bytes accessed | tf_op | source)
XLA Modules:
  0.0 216.0 jit_solution(11765103892492063133)
XLA Ops:
  0.0 6.3 %right.2 = (bf16[2,128,512]{2,1,0:T(8,128)(2,1)}, bf16[2,128,512]{2,1,0:T(8,128)(2,1)}, bf16[2,128,512]{2,1,0:T(8,128)(2,1)}, bf16[2,128,512]{2,1,0:T(8,128)(2,1...) custom-call(s32[1]{0:T(128)} %bitcast.me_ref.refs_0_, ...), custom_call_target="tpu_custom_call" | custom-call | flops 2147483648 | bytes 4194304 | tf_op jit(solution)/shard_map/right/pallas_call | solution.py:72
  6.3 1.3 collective-permute-start
  7.8 1.2 collective-permute-start.2
  9.0 2.3 %collective-permute-start.3 = (bf16[2,128,512]{2,1,0:T(8,128)(2,1)}, bf16[2,128,512]{2,1,0:T(8,128)(2,1)S(1)}, u32[]{:S(2)}, u32[]{:S(2)}) collective-permute-start(bf16[2,128,512]{2,1,0:T(8,128)(2,1)} %get-tuple-element.51), channel_id=1, source_target_pairs={{0,4},{1,5},{2,6},{3,7},{4,0},{5,1},{6,2},{7,3},{8,12},{9,13},{10,... | collective-permute-start | bytes 786440 | tf_op jit(solution)/shard_map/ppermute | solution.py:300
  11.3 1.0 collective-permute-start.4
  12.3 1.4 collective-permute-done.refs_2_
  13.7 1.3 collective-permute-start.5
  15.0 7.6 %collective-permute-done.1.refs_3_ = bf16[2,128,512]{2,1,0:T(8,128)(2,1)S(1)} collective-permute-done((bf16[2,128,512]{2,1,0:T(8,128)(2,1)}, bf16[2,128,512]{2,1,0:T(8,128)(2,1)S(1)}, u32[]{:S(2)}, u32[]{:S(2)}) %collective-permute-start.1) | collective-permute-done | bytes 262176 | tf_op jit(solution)/shard_map/ppermute | solution.py:300
  22.6 6.5 %copy.14 = bf16[2048,1024]{0,1:T(8,128)(2,1)} copy(bf16[2048,1024]{1,0:T(8,128)(2,1)} %bitcast.28) | data formatting | bytes 8388608 | tf_op jit(solution)/shard_map/reshape | solution.py:319
  29.1 2.3 %copy-done.4 = bf16[128,2,4,4,512]{4,3,2,1,0:T(4,128)(2,1)S(1)} copy-done((bf16[128,2,4,4,512]{4,3,2,1,0:T(4,128)(2,1)S(1)}, bf16[128,2,4,4,512]{4,3,2,1,0:T(4,128)(2,1)}, u32[]{:S(2)}) %copy-start.4) | copy-done | bytes 4194328
  31.5 3.0 %right.3 = (bf16[2,128,512]{2,1,0:T(8,128)(2,1)S(1)}, bf16[2,128,512]{2,1,0:T(8,128)(2,1)S(1)}, bf16[2,128,512]{2,1,0:T(8,128)(2,1)S(1)}, bf16[2,128,512]{2,1,0:...) custom-call(s32[1]{0:T(128)} %bitcast.me_ref.refs_0_, ...), custom_call_target="tpu_custom_call" | custom-call | flops 2147483648 | bytes 4194304 | tf_op jit(solution)/shard_map/right/pallas_call | solution.py:72
  34.5 3.8 %collective-permute-start.10 = (bf16[2,128,512]{2,1,0:T(8,128)(2,1)S(1)}, bf16[2,128,512]{2,1,0:T(8,128)(2,1)S(1)}, u32[]{:S(2)}, u32[]{:S(2)}) collective-permute-start(bf16[2,128,512]{2,1,0:T(8,128)(2,1)S(1)} %get-tuple-element.59), channel_id=1, source_target_pairs={{0,4},{1,5},{2,6},{3,7},{4,0},{5,1},{6,2},{7,3},{8,12},{9,13},{10,... | collective-permute-start | bytes 786440 | tf_op jit(solution)/shard_map/ppermute | solution.py:300
  38.3 1.7 collective-permute-start.11
  40.0 15.0 %collective-permute-done.4.refs_6_ = bf16[2,128,512]{2,1,0:T(8,128)(2,1)S(1)} collective-permute-done((bf16[2,128,512]{2,1,0:T(8,128)(2,1)}, bf16[2,128,512]{2,1,0:T(8,128)(2,1)S(1)}, u32[]{:S(2)}, u32[]{:S(2)}) %collective-permute-start.4) | collective-permute-done | bytes 262176 | tf_op jit(solution)/shard_map/ppermute | solution.py:300
  55.0 8.5 %collective-permute-done.5.refs_7_ = bf16[2,128,512]{2,1,0:T(8,128)(2,1)S(1)} collective-permute-done((bf16[2,128,512]{2,1,0:T(8,128)(2,1)}, bf16[2,128,512]{2,1,0:T(8,128)(2,1)S(1)}, u32[]{:S(2)}, u32[]{:S(2)}) %collective-permute-start.5) | collective-permute-done | bytes 262176 | tf_op jit(solution)/shard_map/ppermute | solution.py:300
  63.4 11.6 %collective-permute-start.13 = (bf16[2,128,512]{2,1,0:T(8,128)(2,1)S(1)}, bf16[2,128,512]{2,1,0:T(8,128)(2,1)S(1)}, u32[]{:S(2)}, u32[]{:S(2)}) collective-permute-start(bf16[2,128,512]{2,1,0:T(8,128)(2,1)S(1)} %get-tuple-element.62), channel_id=1, source_target_pairs={{0,7},{1,6},{2,5},{3,4},{4,3},{5,2},{6,1},{7,0},{8,15},{9,14},{10,... | collective-permute-start | bytes 786440 | tf_op jit(solution)/shard_map/ppermute | solution.py:300
  75.0 3.2 %collective-permute-done.6.refs_8_ = bf16[2,128,512]{2,1,0:T(8,128)(2,1)S(1)} collective-permute-done((bf16[2,128,512]{2,1,0:T(8,128)(2,1)}, bf16[2,128,512]{2,1,0:T(8,128)(2,1)S(1)}, u32[]{:S(2)}, u32[]{:S(2)}) %collective-permute-start.6) | collective-permute-done | bytes 262176 | tf_op jit(solution)/shard_map/ppermute | solution.py:300
  78.2 0.6 collective-permute-start.7
  78.9 5.1 %left.2 = (bf16[2,128,512]{2,1,0:T(8,128)(2,1)S(1)}, bf16[2,128,512]{2,1,0:T(8,128)(2,1)S(1)}, bf16[2,128,512]{2,1,0:T(8,128)(2,1)S(1)}, bf16[2,128,512]{2,1,0:T...) custom-call(s32[1]{0:T(128)} %bitcast.me_ref.refs_0_, ...), custom_call_target="tpu_custom_call" | custom-call | flops 4294967296 | bytes 8388608 | tf_op jit(solution)/shard_map/left/pallas_call | solution.py:116
  84.3 4.5 %collective-permute-done.11.refs_6_ = bf16[2,128,512]{2,1,0:T(8,128)(2,1)S(1)} collective-permute-done((bf16[2,128,512]{2,1,0:T(8,128)(2,1)S(1)}, bf16[2,128,512]{2,1,0:T(8,128)(2,1)S(1)}, u32[]{:S(2)}, u32[]{:S(2)}) %collective-permute-start.11) | collective-permute-done | bytes 262176 | tf_op jit(solution)/shard_map/ppermute | solution.py:300
  88.8 2.1 collective-permute-start.9
  90.9 3.5 %collective-permute-done.12.refs_7_ = bf16[2,128,512]{2,1,0:T(8,128)(2,1)S(1)} collective-permute-done((bf16[2,128,512]{2,1,0:T(8,128)(2,1)S(1)}, bf16[2,128,512]{2,1,0:T(8,128)(2,1)S(1)}, u32[]{:S(2)}, u32[]{:S(2)}) %collective-permute-start.12) | collective-permute-done | bytes 262176 | tf_op jit(solution)/shard_map/ppermute | solution.py:300
  94.4 1.2 collective-permute-start.21
  95.6 6.8 %collective-permute-done.13.refs_8_ = bf16[2,128,512]{2,1,0:T(8,128)(2,1)S(1)} collective-permute-done((bf16[2,128,512]{2,1,0:T(8,128)(2,1)S(1)}, bf16[2,128,512]{2,1,0:T(8,128)(2,1)S(1)}, u32[]{:S(2)}, u32[]{:S(2)}) %collective-permute-start.13) | collective-permute-done | bytes 262176 | tf_op jit(solution)/shard_map/ppermute | solution.py:300
  102.4 3.7 %sine_bitcast_fusion = (f32[4,128,512]{2,1,0:T(8,128)S(1)}, f32[4,128,512]{2,1,0:T(8,128)S(1)}) fusion(f32[128,4,512]{2,1,0:T(4,128)S(1)} %copy-done.6), kind=kLoop, calls=%fused_computation | loop fusion | bytes 3145728 | tf_op jit(solution)/shard_map/sin | solution.py:339
  106.1 2.4 %collective-permute-start.23 = (bf16[2,128,512]{2,1,0:T(8,128)(2,1)S(1)}, bf16[2,128,512]{2,1,0:T(8,128)(2,1)S(1)}, u32[]{:S(2)}, u32[]{:S(2)}) collective-permute-start(bf16[2,128,512]{2,1,0:T(8,128)(2,1)S(1)} %get-tuple-element.73), channel_id=1, source_target_pairs={{0,3},{1,2},{2,1},{3,0},{4,7},{5,6},{6,5},{7,4},{8,11},{9,10},{10,... | collective-permute-start | bytes 786440 | tf_op jit(solution)/shard_map/ppermute | solution.py:300
  108.5 1.4 collective-permute-start.24
  110.0 0.9 collective-permute-start.25
  111.2 2.2 %collective-permute-start.26 = (bf16[2,128,512]{2,1,0:T(8,128)(2,1)S(1)}, bf16[2,128,512]{2,1,0:T(8,128)(2,1)S(1)}, u32[]{:S(2)}, u32[]{:S(2)}) collective-permute-start(bf16[2,128,512]{2,1,0:T(8,128)(2,1)S(1)} %get-tuple-element.76), channel_id=1, source_target_pairs={{0,6},{1,7},{2,4},{3,5},{4,2},{5,3},{6,0},{7,1},{8,14},{9,15},{10,... | collective-permute-start | bytes 786440 | tf_op jit(solution)/shard_map/ppermute | solution.py:300
  113.9 5.8 %left.3 = (bf16[2,128,512]{2,1,0:T(8,128)(2,1)S(1)}, bf16[2,128,512]{2,1,0:T(8,128)(2,1)S(1)}, bf16[2,128,512]{2,1,0:T(8,128)(2,1)S(1)}, bf16[2,128,512]{2,1,0:T...) custom-call(s32[1]{0:T(128)} %bitcast.me_ref.refs_0_, ...), custom_call_target="tpu_custom_call" | custom-call | flops 4294967296 | bytes 8388608 | tf_op jit(solution)/shard_map/left/pallas_call | solution.py:116
  119.8 0.6 collective-permute-start.14
  120.5 2.0 collective-permute-done.24.refs_5_
  122.4 1.2 collective-permute-start.15
  123.6 16.4 %collective-permute-done.25.refs_6_ = bf16[2,128,512]{2,1,0:T(8,128)(2,1)S(1)} collective-permute-done((bf16[2,128,512]{2,1,0:T(8,128)(2,1)S(1)}, bf16[2,128,512]{2,1,0:T(8,128)(2,1)S(1)}, u32[]{:S(2)}, u32[]{:S(2)}) %collective-permute-start.25) | collective-permute-done | bytes 262176 | tf_op jit(solution)/shard_map/ppermute | solution.py:300
  140.0 2.7 %collective-permute-start.16 = (bf16[2,128,512]{2,1,0:T(8,128)(2,1)S(1)}, bf16[2,128,512]{2,1,0:T(8,128)(2,1)S(1)}, u32[]{:S(2)}, u32[]{:S(2)}) collective-permute-start(bf16[2,128,512]{2,1,0:T(8,128)(2,1)S(1)} %get-tuple-element.66), channel_id=1, source_target_pairs={{0,3},{1,2},{2,1},{3,0},{4,7},{5,6},{6,5},{7,4},{8,11},{9,10},{10,... | collective-permute-start | bytes 786440 | tf_op jit(solution)/shard_map/ppermute | solution.py:300
  142.7 5.0 %collective-permute-done.26.refs_7_ = bf16[2,128,512]{2,1,0:T(8,128)(2,1)S(1)} collective-permute-done((bf16[2,128,512]{2,1,0:T(8,128)(2,1)S(1)}, bf16[2,128,512]{2,1,0:T(8,128)(2,1)S(1)}, u32[]{:S(2)}, u32[]{:S(2)}) %collective-permute-start.26) | collective-permute-done | bytes 262176 | tf_op jit(solution)/shard_map/ppermute | solution.py:300
  147.7 8.9 %collective-permute-done.27.refs_8_ = bf16[2,128,512]{2,1,0:T(8,128)(2,1)S(1)} collective-permute-done((bf16[2,128,512]{2,1,0:T(8,128)(2,1)S(1)}, bf16[2,128,512]{2,1,0:T(8,128)(2,1)S(1)}, u32[]{:S(2)}, u32[]{:S(2)}) %collective-permute-start.27) | collective-permute-done | bytes 262176 | tf_op jit(solution)/shard_map/ppermute | solution.py:300
  156.7 5.1 %phase.1 = (bf16[2,1,128,512]{3,2,1,0:T(8,128)(2,1)}, bf16[2,1,128,512]{3,2,1,0:T(8,128)(2,1)}, bf16[2,1,128,512]{3,2,1,0:T(8,128)(2,1)}, bf16[2,1,128,512]{3,2,...) custom-call(s32[2]{0:T(128)S(1)} %pad_add_fusion.me_ref, ...), custom_call_target="tpu_custom_call" | custom-call | flops 2147483648 | bytes 4194304 | tf_op jit(solution)/shard_map/phase/pallas_call | solution.py:187
  161.7 0.7 copy-done.3
  162.5 1.4 collective-permute-start.19
  163.9 0.7 collective-permute-start.20
  164.6 21.0 %collective-permute-start.28 = (bf16[2,1,128,512]{3,2,1,0:T(8,128)(2,1)}, bf16[2,1,128,512]{3,2,1,0:T(8,128)(2,1)}, u32[]{:S(2)}, u32[]{:S(2)}) collective-permute-start(bf16[2,1,128,512]{3,2,1,0:T(8,128)(2,1)} %get-tuple-element.79), channel_id=1, source_target_pairs={{8,16},{16,8},{9,17},{17,9},{10,18},{18,10},{11,19},{19,11},{12,20... | collective-permute-start | bytes 786440 | tf_op jit(solution)/shard_map/ppermute | solution.py:307
  185.7 1.9 collective-permute-start.29
  187.7 0.7 copy-done.11
  188.3 8.4 %collective-permute-start.30 = (bf16[2,1,128,512]{3,2,1,0:T(8,128)(2,1)}, bf16[2,1,128,512]{3,2,1,0:T(8,128)(2,1)}, u32[]{:S(2)}, u32[]{:S(2)}) collective-permute-start(bf16[2,1,128,512]{3,2,1,0:T(8,128)(2,1)} %get-tuple-element.81), channel_id=1, source_target_pairs={{8,16},{16,8},{9,17},{17,9},{10,18},{18,10},{11,19},{19,11},{12,20... | collective-permute-start | bytes 786440 | tf_op jit(solution)/shard_map/ppermute | solution.py:307
  196.8 5.6 %collective-permute-start.31 = (bf16[2,1,128,512]{3,2,1,0:T(8,128)(2,1)}, bf16[2,1,128,512]{3,2,1,0:T(8,128)(2,1)}, u32[]{:S(2)}, u32[]{:S(2)}) collective-permute-start(bf16[2,1,128,512]{3,2,1,0:T(8,128)(2,1)} %get-tuple-element.82), channel_id=1, source_target_pairs={{8,16},{16,8},{9,17},{17,9},{10,18},{18,10},{11,19},{19,11},{12,20... | collective-permute-start | bytes 786440 | tf_op jit(solution)/shard_map/ppermute | solution.py:307
  203.8 2.9 %collective-permute-done.31.refs_12_ = bf16[2,1,128,512]{3,2,1,0:T(8,128)(2,1)} collective-permute-done((bf16[2,1,128,512]{3,2,1,0:T(8,128)(2,1)}, bf16[2,1,128,512]{3,2,1,0:T(8,128)(2,1)}, u32[]{:S(2)}, u32[]{:S(2)}) %collective-permute-start.31) | collective-permute-done | bytes 262176 | tf_op jit(solution)/shard_map/ppermute | solution.py:307
  206.8 9.1 %mix.1 = bf16[128,2,4,16,128]{4,3,2,1,0:T(8,128)(2,1)} custom-call(s32[2]{0:T(128)S(1)} %pad_add_fusion.me_ref, f32[4,4]{1,0:T(4,128)S(1)} %get-tuple-element.90.up_ref, f32[4,4]{1,0:T(4,128)S(1)} %get-tuple-element.89.down_ref, bf16[1024,512]{1,0:T(8,128)(2,1)S(1)} %bitcast.25, f32[4,128,512]{2,1,0:T(8,128)S(1)} %get-tuple-element.88.cosine_ref, ...), custom_call_target="tpu_custom_call" | custom-call | flops 2147483648 | bytes 10485760 | tf_op jit(solution)/shard_map/mix/pallas_call | solution.py:272
  (65 shorter events, 3.2 us)
Async XLA Ops:
  6.3 7.4 %collective-permute-start = (bf16[2,128,512]{2,1,0:T(8,128)(2,1)}, bf16[2,128,512]{2,1,0:T(8,128)(2,1)S(1)}, u32[]{:S(2)}, u32[]{:S(2)}) collective-permute-start(bf16[2,128,512]{2,1,0:T(8,128)(2,1)} %get-tuple-element.48), channel_id=1, source_target_pairs={{0,1},{1,0},{2,3},{3,2},{4,5},{5,4},{6,7},{7,6},{8,9},{9,8},{10,11... | collective-permute-start | bytes 786440 | tf_op jit(solution)/shard_map/ppermute | solution.py:300
  7.6 15.0 %collective-permute-start.1 = (bf16[2,128,512]{2,1,0:T(8,128)(2,1)}, bf16[2,128,512]{2,1,0:T(8,128)(2,1)S(1)}, u32[]{:S(2)}, u32[]{:S(2)}) collective-permute-start(bf16[2,128,512]{2,1,0:T(8,128)(2,1)} %get-tuple-element.49), channel_id=1, source_target_pairs={{0,2},{1,3},{2,0},{3,1},{4,6},{5,7},{6,4},{7,5},{8,10},{9,11},{10,... | collective-permute-start | bytes 786440 | tf_op jit(solution)/shard_map/ppermute | solution.py:300
  7.8 26.8 %collective-permute-start.2 = (bf16[2,128,512]{2,1,0:T(8,128)(2,1)}, bf16[2,128,512]{2,1,0:T(8,128)(2,1)S(1)}, u32[]{:S(2)}, u32[]{:S(2)}) collective-permute-start(bf16[2,128,512]{2,1,0:T(8,128)(2,1)} %get-tuple-element.50), channel_id=1, source_target_pairs={{0,3},{1,2},{2,1},{3,0},{4,7},{5,6},{6,5},{7,4},{8,11},{9,10},{10,... | collective-permute-start | bytes 786440 | tf_op jit(solution)/shard_map/ppermute | solution.py:300
  9.0 29.3 %collective-permute-start.3 = (bf16[2,128,512]{2,1,0:T(8,128)(2,1)}, bf16[2,128,512]{2,1,0:T(8,128)(2,1)S(1)}, u32[]{:S(2)}, u32[]{:S(2)}) collective-permute-start(bf16[2,128,512]{2,1,0:T(8,128)(2,1)} %get-tuple-element.51), channel_id=1, source_target_pairs={{0,4},{1,5},{2,6},{3,7},{4,0},{5,1},{6,2},{7,3},{8,12},{9,13},{10,... | collective-permute-start | bytes 786440 | tf_op jit(solution)/shard_map/ppermute | solution.py:300
  11.3 43.7 %collective-permute-start.4 = (bf16[2,128,512]{2,1,0:T(8,128)(2,1)}, bf16[2,128,512]{2,1,0:T(8,128)(2,1)S(1)}, u32[]{:S(2)}, u32[]{:S(2)}) collective-permute-start(bf16[2,128,512]{2,1,0:T(8,128)(2,1)} %get-tuple-element.52), channel_id=1, source_target_pairs={{0,5},{1,4},{2,7},{3,6},{4,1},{5,0},{6,3},{7,2},{8,13},{9,12},{10,... | collective-permute-start | bytes 786440 | tf_op jit(solution)/shard_map/ppermute | solution.py:300
  13.7 49.7 %collective-permute-start.5 = (bf16[2,128,512]{2,1,0:T(8,128)(2,1)}, bf16[2,128,512]{2,1,0:T(8,128)(2,1)S(1)}, u32[]{:S(2)}, u32[]{:S(2)}) collective-permute-start(bf16[2,128,512]{2,1,0:T(8,128)(2,1)} %get-tuple-element.53), channel_id=1, source_target_pairs={{0,6},{1,7},{2,4},{3,5},{4,2},{5,3},{6,0},{7,1},{8,14},{9,15},{10,... | collective-permute-start | bytes 786440 | tf_op jit(solution)/shard_map/ppermute | solution.py:300
  22.6 55.6 %collective-permute-start.6 = (bf16[2,128,512]{2,1,0:T(8,128)(2,1)}, bf16[2,128,512]{2,1,0:T(8,128)(2,1)S(1)}, u32[]{:S(2)}, u32[]{:S(2)}) collective-permute-start(bf16[2,128,512]{2,1,0:T(8,128)(2,1)} %get-tuple-element.54), channel_id=1, source_target_pairs={{0,7},{1,6},{2,5},{3,4},{4,3},{5,2},{6,1},{7,0},{8,15},{9,14},{10,... | collective-permute-start | bytes 786440 | tf_op jit(solution)/shard_map/ppermute | solution.py:300
  22.6 6.5 %copy-start.1 = (bf16[2,512,512]{2,1,0:T(8,128)(2,1)S(1)}, bf16[2,512,512]{2,1,0:T(8,128)(2,1)}, u32[]{:S(2)}) copy-start(bf16[2,512,512]{2,1,0:T(8,128)(2,1)} %param.8) | copy-start | bytes 3145732
  22.6 6.5 %copy-start.5 = (bf16[2,128,512]{2,1,0:T(8,128)(2,1)S(1)}, bf16[2,128,512]{2,1,0:T(8,128)(2,1)}, u32[]{:S(2)}) copy-start(bf16[2,128,512]{2,1,0:T(8,128)(2,1)} %get-tuple-element.46.refs_0_.refs_1_) | copy-start | bytes 786436
  29.1 49.7 %copy-start = (bf16[2048,1024]{0,1:T(8,128)(2,1)S(1)}, bf16[2048,1024]{0,1:T(8,128)(2,1)}, u32[]{:S(2)}) copy-start(bf16[2048,1024]{0,1:T(8,128)(2,1)} %copy.14) | copy-start | bytes 12582916
  29.1 2.3 %copy-start.4 = (bf16[128,2,4,4,512]{4,3,2,1,0:T(4,128)(2,1)S(1)}, bf16[128,2,4,4,512]{4,3,2,1,0:T(4,128)(2,1)}, u32[]{:S(2)}) copy-start(bf16[128,2,4,4,512]{4,3,2,1,0:T(4,128)(2,1)} %param.6) | copy-start | bytes 12582916
  34.5 49.4 %collective-permute-start.10 = (bf16[2,128,512]{2,1,0:T(8,128)(2,1)S(1)}, bf16[2,128,512]{2,1,0:T(8,128)(2,1)S(1)}, u32[]{:S(2)}, u32[]{:S(2)}) collective-permute-start(bf16[2,128,512]{2,1,0:T(8,128)(2,1)S(1)} %get-tuple-element.59), channel_id=1, source_target_pairs={{0,4},{1,5},{2,6},{3,7},{4,0},{5,1},{6,2},{7,3},{8,12},{9,13},{10,... | collective-permute-start | bytes 786440 | tf_op jit(solution)/shard_map/ppermute | solution.py:300
  38.3 50.5 %collective-permute-start.11 = (bf16[2,128,512]{2,1,0:T(8,128)(2,1)S(1)}, bf16[2,128,512]{2,1,0:T(8,128)(2,1)S(1)}, u32[]{:S(2)}, u32[]{:S(2)}) collective-permute-start(bf16[2,128,512]{2,1,0:T(8,128)(2,1)S(1)} %get-tuple-element.60), channel_id=1, source_target_pairs={{0,5},{1,4},{2,7},{3,6},{4,1},{5,0},{6,3},{7,2},{8,13},{9,12},{10,... | collective-permute-start | bytes 786440 | tf_op jit(solution)/shard_map/ppermute | solution.py:300
  55.0 39.4 %collective-permute-start.12 = (bf16[2,128,512]{2,1,0:T(8,128)(2,1)S(1)}, bf16[2,128,512]{2,1,0:T(8,128)(2,1)S(1)}, u32[]{:S(2)}, u32[]{:S(2)}) collective-permute-start(bf16[2,128,512]{2,1,0:T(8,128)(2,1)S(1)} %get-tuple-element.61), channel_id=1, source_target_pairs={{0,6},{1,7},{2,4},{3,5},{4,2},{5,3},{6,0},{7,1},{8,14},{9,15},{10,... | collective-permute-start | bytes 786440 | tf_op jit(solution)/shard_map/ppermute | solution.py:300
  63.4 38.9 %collective-permute-start.13 = (bf16[2,128,512]{2,1,0:T(8,128)(2,1)S(1)}, bf16[2,128,512]{2,1,0:T(8,128)(2,1)S(1)}, u32[]{:S(2)}, u32[]{:S(2)}) collective-permute-start(bf16[2,128,512]{2,1,0:T(8,128)(2,1)S(1)} %get-tuple-element.62), channel_id=1, source_target_pairs={{0,7},{1,6},{2,5},{3,4},{4,3},{5,2},{6,1},{7,0},{8,15},{9,14},{10,... | collective-permute-start | bytes 786440 | tf_op jit(solution)/shard_map/ppermute | solution.py:300
  78.2 27.9 %collective-permute-start.7 = (bf16[2,128,512]{2,1,0:T(8,128)(2,1)S(1)}, bf16[2,128,512]{2,1,0:T(8,128)(2,1)S(1)}, u32[]{:S(2)}, u32[]{:S(2)}) collective-permute-start(bf16[2,128,512]{2,1,0:T(8,128)(2,1)S(1)} %get-tuple-element.56), channel_id=1, source_target_pairs={{0,1},{1,0},{2,3},{3,2},{4,5},{5,4},{6,7},{7,6},{8,9},{9,8},{10,11... | collective-permute-start | bytes 786440 | tf_op jit(solution)/shard_map/ppermute | solution.py:300
  78.8 23.6 %copy-start.6 = (f32[128,4,512]{2,1,0:T(4,128)S(1)}, f32[128,4,512]{2,1,0:T(4,128)}, u32[]{:S(2)}) copy-start(f32[128,4,512]{2,1,0:T(4,128)} %param.9) | copy-start | bytes 3145732
  84.0 24.6 %collective-permute-start.8 = (bf16[2,128,512]{2,1,0:T(8,128)(2,1)S(1)}, bf16[2,128,512]{2,1,0:T(8,128)(2,1)S(1)}, u32[]{:S(2)}, u32[]{:S(2)}) collective-permute-start(bf16[2,128,512]{2,1,0:T(8,128)(2,1)S(1)} %get-tuple-element.57), channel_id=1, source_target_pairs={{0,2},{1,3},{2,0},{3,1},{4,6},{5,7},{6,4},{7,5},{8,10},{9,11},{10,... | collective-permute-start | bytes 786440 | tf_op jit(solution)/shard_map/ppermute | solution.py:300
  88.8 21.2 %collective-permute-start.9 = (bf16[2,128,512]{2,1,0:T(8,128)(2,1)S(1)}, bf16[2,128,512]{2,1,0:T(8,128)(2,1)S(1)}, u32[]{:S(2)}, u32[]{:S(2)}) collective-permute-start(bf16[2,128,512]{2,1,0:T(8,128)(2,1)S(1)} %get-tuple-element.58), channel_id=1, source_target_pairs={{0,3},{1,2},{2,1},{3,0},{4,7},{5,6},{6,5},{7,4},{8,11},{9,10},{10,... | collective-permute-start | bytes 786440 | tf_op jit(solution)/shard_map/ppermute | solution.py:300
  94.4 16.8 %collective-permute-start.21 = (bf16[2,128,512]{2,1,0:T(8,128)(2,1)S(1)}, bf16[2,128,512]{2,1,0:T(8,128)(2,1)S(1)}, u32[]{:S(2)}, u32[]{:S(2)}) collective-permute-start(bf16[2,128,512]{2,1,0:T(8,128)(2,1)S(1)} %get-tuple-element.71), channel_id=1, source_target_pairs={{0,1},{1,0},{2,3},{3,2},{4,5},{5,4},{6,7},{7,6},{8,9},{9,8},{10,11... | collective-permute-start | bytes 786440 | tf_op jit(solution)/shard_map/ppermute | solution.py:300
  102.4 11.0 %collective-permute-start.22 = (bf16[2,128,512]{2,1,0:T(8,128)(2,1)S(1)}, bf16[2,128,512]{2,1,0:T(8,128)(2,1)S(1)}, u32[]{:S(2)}, u32[]{:S(2)}) collective-permute-start(bf16[2,128,512]{2,1,0:T(8,128)(2,1)S(1)} %get-tuple-element.72), channel_id=1, source_target_pairs={{0,2},{1,3},{2,0},{3,1},{4,6},{5,7},{6,4},{7,5},{8,10},{9,11},{10,... | collective-permute-start | bytes 786440 | tf_op jit(solution)/shard_map/ppermute | solution.py:300
  106.1 13.7 %collective-permute-start.23 = (bf16[2,128,512]{2,1,0:T(8,128)(2,1)S(1)}, bf16[2,128,512]{2,1,0:T(8,128)(2,1)S(1)}, u32[]{:S(2)}, u32[]{:S(2)}) collective-permute-start(bf16[2,128,512]{2,1,0:T(8,128)(2,1)S(1)} %get-tuple-element.73), channel_id=1, source_target_pairs={{0,3},{1,2},{2,1},{3,0},{4,7},{5,6},{6,5},{7,4},{8,11},{9,10},{10,... | collective-permute-start | bytes 786440 | tf_op jit(solution)/shard_map/ppermute | solution.py:300
  108.5 13.9 %collective-permute-start.24 = (bf16[2,128,512]{2,1,0:T(8,128)(2,1)S(1)}, bf16[2,128,512]{2,1,0:T(8,128)(2,1)S(1)}, u32[]{:S(2)}, u32[]{:S(2)}) collective-permute-start(bf16[2,128,512]{2,1,0:T(8,128)(2,1)S(1)} %get-tuple-element.74), channel_id=1, source_target_pairs={{0,4},{1,5},{2,6},{3,7},{4,0},{5,1},{6,2},{7,3},{8,12},{9,13},{10,... | collective-permute-start | bytes 786440 | tf_op jit(solution)/shard_map/ppermute | solution.py:300
  110.0 30.1 %collective-permute-start.25 = (bf16[2,128,512]{2,1,0:T(8,128)(2,1)S(1)}, bf16[2,128,512]{2,1,0:T(8,128)(2,1)S(1)}, u32[]{:S(2)}, u32[]{:S(2)}) collective-permute-start(bf16[2,128,512]{2,1,0:T(8,128)(2,1)S(1)} %get-tuple-element.75), channel_id=1, source_target_pairs={{0,5},{1,4},{2,7},{3,6},{4,1},{5,0},{6,3},{7,2},{8,13},{9,12},{10,... | collective-permute-start | bytes 786440 | tf_op jit(solution)/shard_map/ppermute | solution.py:300
  111.2 36.5 %collective-permute-start.26 = (bf16[2,128,512]{2,1,0:T(8,128)(2,1)S(1)}, bf16[2,128,512]{2,1,0:T(8,128)(2,1)S(1)}, u32[]{:S(2)}, u32[]{:S(2)}) collective-permute-start(bf16[2,128,512]{2,1,0:T(8,128)(2,1)S(1)} %get-tuple-element.76), channel_id=1, source_target_pairs={{0,6},{1,7},{2,4},{3,5},{4,2},{5,3},{6,0},{7,1},{8,14},{9,15},{10,... | collective-permute-start | bytes 786440 | tf_op jit(solution)/shard_map/ppermute | solution.py:300
  113.4 43.2 %collective-permute-start.27 = (bf16[2,128,512]{2,1,0:T(8,128)(2,1)S(1)}, bf16[2,128,512]{2,1,0:T(8,128)(2,1)S(1)}, u32[]{:S(2)}, u32[]{:S(2)}) collective-permute-start(bf16[2,128,512]{2,1,0:T(8,128)(2,1)S(1)} %get-tuple-element.77), channel_id=1, source_target_pairs={{0,7},{1,6},{2,5},{3,4},{4,3},{5,2},{6,1},{7,0},{8,15},{9,14},{10,... | collective-permute-start | bytes 786440 | tf_op jit(solution)/shard_map/ppermute | solution.py:300
  119.6 77.1 %copy-start.12 = (f32[16,4]{0,1:T(4,128)S(1)}, f32[16,4]{0,1:T(4,128)}, u32[]{:S(2)}) copy-start(f32[16,4]{0,1:T(4,128)} %param.10) | copy-start | bytes 772
  119.6 87.2 %copy-start.2 = (f32[128,512]{1,0:T(8,128)S(1)}, f32[128,512]{1,0:T(8,128)}, u32[]{:S(2)}) copy-start(f32[128,512]{1,0:T(8,128)} %weight_ref.1) | copy-start | bytes 786436
  119.8 42.6 %collective-permute-start.14 = (bf16[2,128,512]{2,1,0:T(8,128)(2,1)S(1)}, bf16[2,128,512]{2,1,0:T(8,128)(2,1)S(1)}, u32[]{:S(2)}, u32[]{:S(2)}) collective-permute-start(bf16[2,128,512]{2,1,0:T(8,128)(2,1)S(1)} %get-tuple-element.64), channel_id=1, source_target_pairs={{0,1},{1,0},{2,3},{3,2},{4,5},{5,4},{6,7},{7,6},{8,9},{9,8},{10,11... | collective-permute-start | bytes 786440 | tf_op jit(solution)/shard_map/ppermute | solution.py:300
  122.4 41.5 %collective-permute-start.15 = (bf16[2,128,512]{2,1,0:T(8,128)(2,1)S(1)}, bf16[2,128,512]{2,1,0:T(8,128)(2,1)S(1)}, u32[]{:S(2)}, u32[]{:S(2)}) collective-permute-start(bf16[2,128,512]{2,1,0:T(8,128)(2,1)S(1)} %get-tuple-element.65), channel_id=1, source_target_pairs={{0,2},{1,3},{2,0},{3,1},{4,6},{5,7},{6,4},{7,5},{8,10},{9,11},{10,... | collective-permute-start | bytes 786440 | tf_op jit(solution)/shard_map/ppermute | solution.py:300
  140.0 24.6 %collective-permute-start.16 = (bf16[2,128,512]{2,1,0:T(8,128)(2,1)S(1)}, bf16[2,128,512]{2,1,0:T(8,128)(2,1)S(1)}, u32[]{:S(2)}, u32[]{:S(2)}) collective-permute-start(bf16[2,128,512]{2,1,0:T(8,128)(2,1)S(1)} %get-tuple-element.66), channel_id=1, source_target_pairs={{0,3},{1,2},{2,1},{3,0},{4,7},{5,6},{6,5},{7,4},{8,11},{9,10},{10,... | collective-permute-start | bytes 786440 | tf_op jit(solution)/shard_map/ppermute | solution.py:300
  147.7 38.0 %collective-permute-start.17 = (bf16[2,128,512]{2,1,0:T(8,128)(2,1)S(1)}, bf16[2,128,512]{2,1,0:T(8,128)(2,1)S(1)}, u32[]{:S(2)}, u32[]{:S(2)}) collective-permute-start(bf16[2,128,512]{2,1,0:T(8,128)(2,1)S(1)} %get-tuple-element.67), channel_id=1, source_target_pairs={{0,4},{1,5},{2,6},{3,7},{4,0},{5,1},{6,2},{7,3},{8,12},{9,13},{10,... | collective-permute-start | bytes 786440 | tf_op jit(solution)/shard_map/ppermute | solution.py:300
  156.6 31.0 %collective-permute-start.18 = (bf16[2,128,512]{2,1,0:T(8,128)(2,1)S(1)}, bf16[2,128,512]{2,1,0:T(8,128)(2,1)S(1)}, u32[]{:S(2)}, u32[]{:S(2)}) collective-permute-start(bf16[2,128,512]{2,1,0:T(8,128)(2,1)S(1)} %get-tuple-element.68), channel_id=1, source_target_pairs={{0,5},{1,4},{2,7},{3,6},{4,1},{5,0},{6,3},{7,2},{8,13},{9,12},{10,... | collective-permute-start | bytes 786440 | tf_op jit(solution)/shard_map/ppermute | solution.py:300
  161.7 0.7 copy-start.3
  162.5 25.2 %copy-start.7 = (bf16[2,128,512]{2,1,0:T(8,128)(2,1)}, bf16[2,128,512]{2,1,0:T(8,128)(2,1)S(1)}, u32[]{:S(2)}) copy-start(bf16[2,128,512]{2,1,0:T(8,128)(2,1)S(1)} %collective-permute-done.14.refs_1_) | copy-start | bytes 786436
  162.5 34.3 %collective-permute-start.19 = (bf16[2,128,512]{2,1,0:T(8,128)(2,1)}, bf16[2,128,512]{2,1,0:T(8,128)(2,1)}, u32[]{:S(2)}, u32[]{:S(2)}) collective-permute-start(bf16[2,128,512]{2,1,0:T(8,128)(2,1)} %get-tuple-element.69), channel_id=1, source_target_pairs={{0,6},{1,7},{2,4},{3,5},{4,2},{5,3},{6,0},{7,1},{8,14},{9,15},{10,... | collective-permute-start | bytes 786440 | tf_op jit(solution)/shard_map/ppermute | solution.py:300
  163.9 23.8 %copy-start.8 = (bf16[2,128,512]{2,1,0:T(8,128)(2,1)}, bf16[2,128,512]{2,1,0:T(8,128)(2,1)S(1)}, u32[]{:S(2)}) copy-start(bf16[2,128,512]{2,1,0:T(8,128)(2,1)S(1)} %collective-permute-done.15.refs_2_) | copy-start | bytes 786436
  163.9 38.5 %collective-permute-start.20 = (bf16[2,128,512]{2,1,0:T(8,128)(2,1)}, bf16[2,128,512]{2,1,0:T(8,128)(2,1)}, u32[]{:S(2)}, u32[]{:S(2)}) collective-permute-start(bf16[2,128,512]{2,1,0:T(8,128)(2,1)} %get-tuple-element.70), channel_id=1, source_target_pairs={{0,7},{1,6},{2,5},{3,4},{4,3},{5,2},{6,1},{7,0},{8,15},{9,14},{10,... | collective-permute-start | bytes 786440 | tf_op jit(solution)/shard_map/ppermute | solution.py:300
  164.6 23.0 %copy-start.9 = (bf16[2,128,512]{2,1,0:T(8,128)(2,1)}, bf16[2,128,512]{2,1,0:T(8,128)(2,1)S(1)}, u32[]{:S(2)}) copy-start(bf16[2,128,512]{2,1,0:T(8,128)(2,1)S(1)} %collective-permute-done.16.refs_3_) | copy-start | bytes 786436
  164.6 38.1 %collective-permute-start.28 = (bf16[2,1,128,512]{3,2,1,0:T(8,128)(2,1)}, bf16[2,1,128,512]{3,2,1,0:T(8,128)(2,1)}, u32[]{:S(2)}, u32[]{:S(2)}) collective-permute-start(bf16[2,1,128,512]{3,2,1,0:T(8,128)(2,1)} %get-tuple-element.79), channel_id=1, source_target_pairs={{8,16},{16,8},{9,17},{17,9},{10,18},{18,10},{11,19},{19,11},{12,20... | collective-permute-start | bytes 786440 | tf_op jit(solution)/shard_map/ppermute | solution.py:307
  185.7 2.0 copy-start.10
  185.7 17.3 %collective-permute-start.29 = (bf16[2,1,128,512]{3,2,1,0:T(8,128)(2,1)}, bf16[2,1,128,512]{3,2,1,0:T(8,128)(2,1)}, u32[]{:S(2)}, u32[]{:S(2)}) collective-permute-start(bf16[2,1,128,512]{3,2,1,0:T(8,128)(2,1)} %get-tuple-element.80), channel_id=1, source_target_pairs={{8,16},{16,8},{9,17},{17,9},{10,18},{18,10},{11,19},{19,11},{12,20... | collective-permute-start | bytes 786440 | tf_op jit(solution)/shard_map/ppermute | solution.py:307
  188.3 14.9 %collective-permute-start.30 = (bf16[2,1,128,512]{3,2,1,0:T(8,128)(2,1)}, bf16[2,1,128,512]{3,2,1,0:T(8,128)(2,1)}, u32[]{:S(2)}, u32[]{:S(2)}) collective-permute-start(bf16[2,1,128,512]{3,2,1,0:T(8,128)(2,1)} %get-tuple-element.81), channel_id=1, source_target_pairs={{8,16},{16,8},{9,17},{17,9},{10,18},{18,10},{11,19},{19,11},{12,20... | collective-permute-start | bytes 786440 | tf_op jit(solution)/shard_map/ppermute | solution.py:307
  196.8 9.9 %collective-permute-start.31 = (bf16[2,1,128,512]{3,2,1,0:T(8,128)(2,1)}, bf16[2,1,128,512]{3,2,1,0:T(8,128)(2,1)}, u32[]{:S(2)}, u32[]{:S(2)}) collective-permute-start(bf16[2,1,128,512]{3,2,1,0:T(8,128)(2,1)} %get-tuple-element.82), channel_id=1, source_target_pairs={{8,16},{16,8},{9,17},{17,9},{10,18},{18,10},{11,19},{19,11},{12,20... | collective-permute-start | bytes 786440 | tf_op jit(solution)/shard_map/ppermute | solution.py:307
  202.4 4.3 %collective-permute-start.32 = (bf16[2,1,128,512]{3,2,1,0:T(8,128)(2,1)}, bf16[2,1,128,512]{3,2,1,0:T(8,128)(2,1)}, u32[]{:S(2)}, u32[]{:S(2)}) collective-permute-start(bf16[2,1,128,512]{3,2,1,0:T(8,128)(2,1)} %get-tuple-element.83), channel_id=1, source_target_pairs={{0,8},{16,24},{8,0},{24,16},{1,9},{17,25},{9,1},{25,17},{2,10},{18... | collective-permute-start | bytes 786440 | tf_op jit(solution)/shard_map/ppermute | solution.py:307
  202.7 4.0 %collective-permute-start.33 = (bf16[2,1,128,512]{3,2,1,0:T(8,128)(2,1)}, bf16[2,1,128,512]{3,2,1,0:T(8,128)(2,1)}, u32[]{:S(2)}, u32[]{:S(2)}) collective-permute-start(bf16[2,1,128,512]{3,2,1,0:T(8,128)(2,1)} %get-tuple-element.84), channel_id=1, source_target_pairs={{0,8},{16,24},{8,0},{24,16},{1,9},{17,25},{9,1},{25,17},{2,10},{18... | collective-permute-start | bytes 786440 | tf_op jit(solution)/shard_map/ppermute | solution.py:307
  203.0 3.8 %collective-permute-start.34 = (bf16[2,1,128,512]{3,2,1,0:T(8,128)(2,1)}, bf16[2,1,128,512]{3,2,1,0:T(8,128)(2,1)}, u32[]{:S(2)}, u32[]{:S(2)}) collective-permute-start(bf16[2,1,128,512]{3,2,1,0:T(8,128)(2,1)} %get-tuple-element.85), channel_id=1, source_target_pairs={{0,8},{16,24},{8,0},{24,16},{1,9},{17,25},{9,1},{25,17},{2,10},{18... | collective-permute-start | bytes 786440 | tf_op jit(solution)/shard_map/ppermute | solution.py:307
  203.2 3.5 %collective-permute-start.35 = (bf16[2,1,128,512]{3,2,1,0:T(8,128)(2,1)}, bf16[2,1,128,512]{3,2,1,0:T(8,128)(2,1)}, u32[]{:S(2)}, u32[]{:S(2)}) collective-permute-start(bf16[2,1,128,512]{3,2,1,0:T(8,128)(2,1)} %get-tuple-element.86), channel_id=1, source_target_pairs={{0,8},{16,24},{8,0},{24,16},{1,9},{17,25},{9,1},{25,17},{2,10},{18... | collective-permute-start | bytes 786440 | tf_op jit(solution)/shard_map/ppermute | solution.py:307
  (1 other events, 0.7 us)

commit v14 on v13

--- a/solution.py
+++ b/solution.py
@@ -32,17 +32,19 @@
     return jnp.concatenate([real, -imag], 1), jnp.concatenate([imag, real], 1)
 
 
-def right_kernel(after, chosen, states, me_ref, second_ref, *refs):
+def right_kernel(after, ranks, states, me_ref, second_ref, *refs):
     refs = refs[after:]
-    packet, outs, slabs = refs[0], refs[1:-1], refs[-1]
+    kinds = len(refs) - 1 - ranks
+    packets, outs, slabs = refs[:kinds], refs[kinds:-1], refs[-1]
     me = me_ref[0]
-    rows, _, _, group, _ = packet.shape
+    rows = packets[0].shape[0]
+    group = packets[0].shape[2]
     tiles = group // states
     piece = slabs.shape[2] // 2
     cuts = tiles * LANES // piece
-    for n, k in enumerate(chosen):
+    for n, packet in enumerate(packets):
         turned = [
-            packet[:, c, k].astype(jnp.float32).transpose(1, 0, 2).astype(jnp.bfloat16)
+            packet[:, c].astype(jnp.float32).transpose(1, 0, 2).astype(jnp.bfloat16)
             for c in range(2)
         ]
 
@@ -65,16 +67,19 @@
 
 
 def right_call(after, me, second, view, chosen, ranks, states, piece, limit):
-    rows, _, blocks, group, _ = view.shape
+    rows, _, _, group, _ = view.shape
     width = second.shape[1]
     block = rows // 2
     kinds = len(chosen)
     return pl.pallas_call(
-        functools.partial(right_kernel, len(after), tuple(chosen), states),
+        functools.partial(right_kernel, len(after), ranks, states),
         grid=(rows // block,),
         in_specs=[SMEM, pl.BlockSpec(second.shape, lambda i: (0, 0))]
         + [AFTER] * len(after)
-        + [pl.BlockSpec((block, 2, blocks, group, LANES), lambda i: (i, 0, 0, 0, 0))],
+        + [
+            pl.BlockSpec((block, 2, None, group, LANES), lambda i, k=k: (i, 0, k, 0, 0))
+            for k in chosen
+        ],
         out_specs=[pl.BlockSpec((kinds, block, 2 * piece), lambda i: (0, i, 0))] * ranks,
         out_shape=[jax.ShapeDtypeStruct((kinds, rows, 2 * piece), jnp.bfloat16)] * ranks,
         scratch_shapes=[
@@ -85,17 +90,18 @@
             8 * kinds * states * rows * width * width, 8 * kinds * states * rows * width
         ),
         name="right",
-    )(me, second, *after, view)
-
-
-def left_kernel(after, ranks, me_ref, first_ref, *refs):
+    )(me, second, *after, *([view] * kinds))
+
+
+def left_kernel(after, order, me_ref, first_ref, *refs):
     refs = refs[after:]
+    ranks = len(order)
     ins, outs, lines, slabs = refs[:ranks], refs[ranks:-2], refs[-2], refs[-1]
     me = me_ref[0]
     rows, wide = ins[0].shape
     piece = wide // 2
     whole = ranks * rows
-    for s, part in enumerate(ins):
+    for s, part in zip(order, ins):
         value = part[...]
         first = pl.multiple_of((me ^ s) * rows, rows)
         lines[pl.ds(first, rows), :] = value
@@ -108,13 +114,13 @@
         out[...] = slabs[me ^ s]
 
 
-def left_call(after, me, first, slabs):
+def left_call(after, me, first, slabs, order):
     ranks = len(slabs)
     kinds, rows, wide = slabs[0].shape
     whole = ranks * rows
     spec = pl.BlockSpec((None, rows, wide), lambda i: (i, 0, 0))
     return pl.pallas_call(
-        functools.partial(left_kernel, len(after), ranks),
+        functools.partial(left_kernel, len(after), order),
         grid=(kinds,),
         in_specs=[SMEM, pl.BlockSpec(first.shape, lambda i: (0, 0))]
         + [AFTER] * len(after)
@@ -130,7 +136,7 @@
             4 * kinds * whole * whole * wide, 4 * whole * whole + 4 * kinds * whole * wide
         ),
         name="left",
-    )(me, first, *after, *slabs)
+    )(me, first, *after, *[slabs[s] for s in order])
 
 
 def phased_product(me, n, second_ref, cosine_ref, sine_ref, ins, order, slabs):
@@ -330,8 +336,10 @@
         last = half[0]
         lines.append(exchanged(half, "rad"))
     backs = []
-    for line in lines:
-        moved = left_call([last], me, first, line)
+    far_first = (0, *range(ranks // 2, ranks), *range(1, ranks // 2))
+    orders = (far_first, tuple(range(ranks)))
+    for line, order in zip(lines, orders):
+        moved = left_call([last], me, first, line, order)
         last = moved[0]
         backs.append(exchanged(moved, "rad"))
 

time: 218 us -> 220 us (level)
  waiting for transfers between devices: 86.1 us -> 101 us
  starting transfers between devices: 80.7 us -> 69.7 us
    ppermute x28, waiting for transfers between devices: 83.2 us -> 99.2 us  [exchanged(): result[s] = lax.ppermute(slabs[s], axis, [(i, i ^ s) for i in range(count)])]
    ppermute x8, starting transfers between devices: 38 us -> 32.1 us  [paired(): return lax.ppermute(edge, axis, pairs + [(j, i) for i, j in pairs])]
    ppermute x28, starting transfers between devices: 42.8 us -> 37.6 us  [exchanged(): result[s] = lax.ppermute(slabs[s], axis, [(i, i ^ s) for i in range(count)])]
where the time goes in v14:
time: 220 us; the launch traced here: 219 us
  waiting for transfers between devices  101 us (46%)
  starting transfers between devices  69.7 us (32%)
  Pallas kernels  33.6 us (15%)
  local copies, waits for them, and re-layouts  14.2 us (6%)
    ppermute x28, waiting for transfers between devices, exchanged(): result[s] = lax.ppermute(slabs[s], axis, [(i, i ^ s) for i in range(count)])  99.2 us
    ppermute x28, starting transfers between devices, exchanged(): result[s] = lax.ppermute(slabs[s], axis, [(i, i ^ s) for i in range(count)])  37.6 us
    ppermute x8, starting transfers between devices, paired(): return lax.ppermute(edge, axis, pairs + [(j, i) for i, j in pairs])  32.1 us
    pallas_call x2, Pallas kernels, left_call(): pl.pallas_call(functools.partial(left_kernel, len(after), order), grid=(k...  10.8 us
    pallas_call x1, Pallas kernels, mix_call(): pl.pallas_call(functools.partial(mix_kernel, tuple(chosen), order), grid=...  9.05 us
    pallas_call x2, Pallas kernels, right_call(): pl.pallas_call(functools.partial(right_kernel, len(after), ranks, states)...  8.63 us
    reshape x1, local copies, waits for them, and re-layouts, per_device(): first = first_propagator.reshape(2 * whole, whole).T  6.53 us
    pallas_call x1, Pallas kernels, phase_call(): pl.pallas_call(functools.partial(phase_kernel, len(after), ranks), grid=(...  5.05 us
  transfers between devices with their start and end apart: 36, of which 15 were waited for; matrix products, arithmetic and copies ran while one was open for 5% of the time, Pallas kernels for 9%

profile of v14, /device:TPU:9, one launch (start us, length us, event | category | flops | bytes accessed | tf_op | source)
XLA Modules:
  0.0 218.8 jit_solution(2241428656247994313)
XLA Ops:
  0.0 5.4 %right.2 = (bf16[2,128,512]{2,1,0:T(8,128)(2,1)}, bf16[2,128,512]{2,1,0:T(8,128)(2,1)}, bf16[2,128,512]{2,1,0:T(8,128)(2,1)}, bf16[2,128,512]{2,1,0:T(8,128)(2,1...) custom-call(s32[1]{0:T(128)} %bitcast.me_ref.refs_0_, ...), custom_call_target="tpu_custom_call" | custom-call | flops 2147483648 | bytes 4194304 | tf_op jit(solution)/shard_map/right/pallas_call | solution.py:74
  5.4 2.4 %collective-permute-start = (bf16[2,128,512]{2,1,0:T(8,128)(2,1)}, bf16[2,128,512]{2,1,0:T(8,128)(2,1)S(1)}, u32[]{:S(2)}, u32[]{:S(2)}) collective-permute-start(bf16[2,128,512]{2,1,0:T(8,128)(2,1)} %get-tuple-element.48), channel_id=1, source_target_pairs={{0,4},{1,5},{2,6},{3,7},{4,0},{5,1},{6,2},{7,3},{8,12},{9,13},{10,... | collective-permute-start | bytes 786440 | tf_op jit(solution)/shard_map/ppermute | solution.py:306
  7.7 1.0 collective-permute-start.1
  8.8 1.3 collective-permute-start.2
  10.2 1.2 collective-permute-start.4
  11.4 25.0 %collective-permute-done.refs_2_ = bf16[2,128,512]{2,1,0:T(8,128)(2,1)S(1)} collective-permute-done((bf16[2,128,512]{2,1,0:T(8,128)(2,1)}, bf16[2,128,512]{2,1,0:T(8,128)(2,1)S(1)}, u32[]{:S(2)}, u32[]{:S(2)}) %collective-permute-start) | collective-permute-done | bytes 262176 | tf_op jit(solution)/shard_map/ppermute | solution.py:306
  36.6 5.5 %collective-permute-done.1.refs_3_ = bf16[2,128,512]{2,1,0:T(8,128)(2,1)S(1)} collective-permute-done((bf16[2,128,512]{2,1,0:T(8,128)(2,1)}, bf16[2,128,512]{2,1,0:T(8,128)(2,1)S(1)}, u32[]{:S(2)}, u32[]{:S(2)}) %collective-permute-start.1) | collective-permute-done | bytes 262176 | tf_op jit(solution)/shard_map/ppermute | solution.py:306
  42.1 1.1 collective-permute-start.6
  43.2 6.5 %copy.14 = bf16[2048,1024]{0,1:T(8,128)(2,1)} copy(bf16[2048,1024]{1,0:T(8,128)(2,1)} %bitcast.30) | data formatting | bytes 8388608 | tf_op jit(solution)/shard_map/reshape | solution.py:325
  49.7 2.2 copy-done
  51.9 3.3 %right.3 = (bf16[2,128,512]{2,1,0:T(8,128)(2,1)S(1)}, bf16[2,128,512]{2,1,0:T(8,128)(2,1)S(1)}, bf16[2,128,512]{2,1,0:T(8,128)(2,1)S(1)}, bf16[2,128,512]{2,1,0:...) custom-call(s32[1]{0:T(128)} %bitcast.me_ref.refs_0_, ...), custom_call_target="tpu_custom_call" | custom-call | flops 2147483648 | bytes 4194304 | tf_op jit(solution)/shard_map/right/pallas_call | solution.py:74
  55.2 3.0 %collective-permute-start.10 = (bf16[2,128,512]{2,1,0:T(8,128)(2,1)S(1)}, bf16[2,128,512]{2,1,0:T(8,128)(2,1)S(1)}, u32[]{:S(2)}, u32[]{:S(2)}) collective-permute-start(bf16[2,128,512]{2,1,0:T(8,128)(2,1)S(1)} %get-tuple-element.59), channel_id=1, source_target_pairs={{0,4},{1,5},{2,6},{3,7},{4,0},{5,1},{6,2},{7,3},{8,12},{9,13},{10,... | collective-permute-start | bytes 786440 | tf_op jit(solution)/shard_map/ppermute | solution.py:306
  58.3 3.3 %collective-permute-start.12 = (bf16[2,128,512]{2,1,0:T(8,128)(2,1)S(1)}, bf16[2,128,512]{2,1,0:T(8,128)(2,1)S(1)}, u32[]{:S(2)}, u32[]{:S(2)}) collective-permute-start(bf16[2,128,512]{2,1,0:T(8,128)(2,1)S(1)} %get-tuple-element.61), channel_id=1, source_target_pairs={{0,6},{1,7},{2,4},{3,5},{4,2},{5,3},{6,0},{7,1},{8,14},{9,15},{10,... | collective-permute-start | bytes 786440 | tf_op jit(solution)/shard_map/ppermute | solution.py:306
  61.7 1.2 collective-permute-start.7
  62.9 5.1 %left.2 = (bf16[2,128,512]{2,1,0:T(8,128)(2,1)S(1)}, bf16[2,128,512]{2,1,0:T(8,128)(2,1)S(1)}, bf16[2,128,512]{2,1,0:T(8,128)(2,1)S(1)}, bf16[2,128,512]{2,1,0:T...) custom-call(s32[1]{0:T(128)} %bitcast.me_ref.refs_0_, ...), custom_call_target="tpu_custom_call" | custom-call | flops 4294967296 | bytes 8388608 | tf_op jit(solution)/shard_map/left/pallas_call | solution.py:122
  68.0 17.7 %collective-permute-done.10.refs_5_ = bf16[2,128,512]{2,1,0:T(8,128)(2,1)S(1)} collective-permute-done((bf16[2,128,512]{2,1,0:T(8,128)(2,1)S(1)}, bf16[2,128,512]{2,1,0:T(8,128)(2,1)S(1)}, u32[]{:S(2)}, u32[]{:S(2)}) %collective-permute-start.10) | collective-permute-done | bytes 262176 | tf_op jit(solution)/shard_map/ppermute | solution.py:306
  85.7 2.9 %collective-permute-start.8 = (bf16[2,128,512]{2,1,0:T(8,128)(2,1)S(1)}, bf16[2,128,512]{2,1,0:T(8,128)(2,1)S(1)}, u32[]{:S(2)}, u32[]{:S(2)}) collective-permute-start(bf16[2,128,512]{2,1,0:T(8,128)(2,1)S(1)} %get-tuple-element.57), channel_id=1, source_target_pairs={{0,2},{1,3},{2,0},{3,1},{4,6},{5,7},{6,4},{7,5},{8,10},{9,11},{10,... | collective-permute-start | bytes 786440 | tf_op jit(solution)/shard_map/ppermute | solution.py:306
  88.5 2.8 %collective-permute-done.11.refs_6_ = bf16[2,128,512]{2,1,0:T(8,128)(2,1)S(1)} collective-permute-done((bf16[2,128,512]{2,1,0:T(8,128)(2,1)S(1)}, bf16[2,128,512]{2,1,0:T(8,128)(2,1)S(1)}, u32[]{:S(2)}, u32[]{:S(2)}) %collective-permute-start.11) | collective-permute-done | bytes 262176 | tf_op jit(solution)/shard_map/ppermute | solution.py:306
  91.3 3.8 %collective-permute-start.9 = (bf16[2,128,512]{2,1,0:T(8,128)(2,1)S(1)}, bf16[2,128,512]{2,1,0:T(8,128)(2,1)S(1)}, u32[]{:S(2)}, u32[]{:S(2)}) collective-permute-start(bf16[2,128,512]{2,1,0:T(8,128)(2,1)S(1)} %get-tuple-element.58), channel_id=1, source_target_pairs={{0,3},{1,2},{2,1},{3,0},{4,7},{5,6},{6,5},{7,4},{8,11},{9,10},{10,... | collective-permute-start | bytes 786440 | tf_op jit(solution)/shard_map/ppermute | solution.py:306
  95.1 3.5 %collective-permute-done.12.refs_7_ = bf16[2,128,512]{2,1,0:T(8,128)(2,1)S(1)} collective-permute-done((bf16[2,128,512]{2,1,0:T(8,128)(2,1)S(1)}, bf16[2,128,512]{2,1,0:T(8,128)(2,1)S(1)}, u32[]{:S(2)}, u32[]{:S(2)}) %collective-permute-start.12) | collective-permute-done | bytes 262176 | tf_op jit(solution)/shard_map/ppermute | solution.py:306
  98.6 0.5 collective-permute-start.21
  99.1 8.4 %collective-permute-done.13.refs_8_ = bf16[2,128,512]{2,1,0:T(8,128)(2,1)S(1)} collective-permute-done((bf16[2,128,512]{2,1,0:T(8,128)(2,1)S(1)}, bf16[2,128,512]{2,1,0:T(8,128)(2,1)S(1)}, u32[]{:S(2)}, u32[]{:S(2)}) %collective-permute-start.13) | collective-permute-done | bytes 262176 | tf_op jit(solution)/shard_map/ppermute | solution.py:306
  107.5 3.7 %sine_bitcast_fusion = (f32[4,128,512]{2,1,0:T(8,128)S(1)}, f32[4,128,512]{2,1,0:T(8,128)S(1)}) fusion(f32[128,4,512]{2,1,0:T(4,128)S(1)} %copy-done.6), kind=kLoop, calls=%fused_computation | loop fusion | bytes 3145728 | tf_op jit(solution)/shard_map/sin | solution.py:347
  111.2 1.7 collective-permute-start.23
  113.0 3.1 %collective-permute-start.25 = (bf16[2,128,512]{2,1,0:T(8,128)(2,1)S(1)}, bf16[2,128,512]{2,1,0:T(8,128)(2,1)S(1)}, u32[]{:S(2)}, u32[]{:S(2)}) collective-permute-start(bf16[2,128,512]{2,1,0:T(8,128)(2,1)S(1)} %get-tuple-element.75), channel_id=1, source_target_pairs={{0,5},{1,4},{2,7},{3,6},{4,1},{5,0},{6,3},{7,2},{8,13},{9,12},{10,... | collective-permute-start | bytes 786440 | tf_op jit(solution)/shard_map/ppermute | solution.py:306
  116.1 1.6 collective-permute-start.27
  117.7 5.8 %left.3 = (bf16[2,128,512]{2,1,0:T(8,128)(2,1)S(1)}, bf16[2,128,512]{2,1,0:T(8,128)(2,1)S(1)}, bf16[2,128,512]{2,1,0:T(8,128)(2,1)S(1)}, bf16[2,128,512]{2,1,0:T...) custom-call(s32[1]{0:T(128)} %bitcast.me_ref.refs_0_, ...), custom_call_target="tpu_custom_call" | custom-call | flops 4294967296 | bytes 8388608 | tf_op jit(solution)/shard_map/left/pallas_call | solution.py:122
  123.5 0.4 collective-permute-done.23.refs_4_
  123.8 0.7 collective-permute-start.14
  124.6 2.6 %collective-permute-start.15 = (bf16[2,128,512]{2,1,0:T(8,128)(2,1)S(1)}, bf16[2,128,512]{2,1,0:T(8,128)(2,1)S(1)}, u32[]{:S(2)}, u32[]{:S(2)}) collective-permute-start(bf16[2,128,512]{2,1,0:T(8,128)(2,1)S(1)} %get-tuple-element.65), channel_id=1, source_target_pairs={{0,2},{1,3},{2,0},{3,1},{4,6},{5,7},{6,4},{7,5},{8,10},{9,11},{10,... | collective-permute-start | bytes 786440 | tf_op jit(solution)/shard_map/ppermute | solution.py:306
  127.2 18.6 %collective-permute-done.25.refs_6_ = bf16[2,128,512]{2,1,0:T(8,128)(2,1)S(1)} collective-permute-done((bf16[2,128,512]{2,1,0:T(8,128)(2,1)S(1)}, bf16[2,128,512]{2,1,0:T(8,128)(2,1)S(1)}, u32[]{:S(2)}, u32[]{:S(2)}) %collective-permute-start.25) | collective-permute-done | bytes 262176 | tf_op jit(solution)/shard_map/ppermute | solution.py:306
  145.8 4.1 %collective-permute-start.16 = (bf16[2,128,512]{2,1,0:T(8,128)(2,1)S(1)}, bf16[2,128,512]{2,1,0:T(8,128)(2,1)S(1)}, u32[]{:S(2)}, u32[]{:S(2)}) collective-permute-start(bf16[2,128,512]{2,1,0:T(8,128)(2,1)S(1)} %get-tuple-element.66), channel_id=1, source_target_pairs={{0,3},{1,2},{2,1},{3,0},{4,7},{5,6},{6,5},{7,4},{8,11},{9,10},{10,... | collective-permute-start | bytes 786440 | tf_op jit(solution)/shard_map/ppermute | solution.py:306
  149.9 3.5 %collective-permute-done.26.refs_7_ = bf16[2,128,512]{2,1,0:T(8,128)(2,1)S(1)} collective-permute-done((bf16[2,128,512]{2,1,0:T(8,128)(2,1)S(1)}, bf16[2,128,512]{2,1,0:T(8,128)(2,1)S(1)}, u32[]{:S(2)}, u32[]{:S(2)}) %collective-permute-start.26) | collective-permute-done | bytes 262176 | tf_op jit(solution)/shard_map/ppermute | solution.py:306
  153.5 12.4 %collective-permute-done.27.refs_8_ = bf16[2,128,512]{2,1,0:T(8,128)(2,1)S(1)} collective-permute-done((bf16[2,128,512]{2,1,0:T(8,128)(2,1)S(1)}, bf16[2,128,512]{2,1,0:T(8,128)(2,1)S(1)}, u32[]{:S(2)}, u32[]{:S(2)}) %collective-permute-start.27) | collective-permute-done | bytes 262176 | tf_op jit(solution)/shard_map/ppermute | solution.py:306
  165.9 5.0 %phase.1 = (bf16[2,1,128,512]{3,2,1,0:T(8,128)(2,1)}, bf16[2,1,128,512]{3,2,1,0:T(8,128)(2,1)}, bf16[2,1,128,512]{3,2,1,0:T(8,128)(2,1)}, bf16[2,1,128,512]{3,2,...) custom-call(s32[2]{0:T(128)S(1)} %pad_add_fusion.me_ref, ...), custom_call_target="tpu_custom_call" | custom-call | flops 2147483648 | bytes 4194304 | tf_op jit(solution)/shard_map/phase/pallas_call | solution.py:193
  171.0 0.7 copy-done.4
  171.7 1.6 collective-permute-start.20
  173.3 6.5 %collective-permute-start.28 = (bf16[2,1,128,512]{3,2,1,0:T(8,128)(2,1)}, bf16[2,1,128,512]{3,2,1,0:T(8,128)(2,1)}, u32[]{:S(2)}, u32[]{:S(2)}) collective-permute-start(bf16[2,1,128,512]{3,2,1,0:T(8,128)(2,1)} %get-tuple-element.79), channel_id=1, source_target_pairs={{8,16},{16,8},{9,17},{17,9},{10,18},{18,10},{11,19},{19,11},{12,20... | collective-permute-start | bytes 786440 | tf_op jit(solution)/shard_map/ppermute | solution.py:313
  179.9 11.8 %collective-permute-start.29 = (bf16[2,1,128,512]{3,2,1,0:T(8,128)(2,1)}, bf16[2,1,128,512]{3,2,1,0:T(8,128)(2,1)}, u32[]{:S(2)}, u32[]{:S(2)}) collective-permute-start(bf16[2,1,128,512]{3,2,1,0:T(8,128)(2,1)} %get-tuple-element.80), channel_id=1, source_target_pairs={{8,16},{16,8},{9,17},{17,9},{10,18},{18,10},{11,19},{19,11},{12,20... | collective-permute-start | bytes 786440 | tf_op jit(solution)/shard_map/ppermute | solution.py:313
  191.7 0.7 copy-done.11
  192.4 5.6 %collective-permute-start.30 = (bf16[2,1,128,512]{3,2,1,0:T(8,128)(2,1)}, bf16[2,1,128,512]{3,2,1,0:T(8,128)(2,1)}, u32[]{:S(2)}, u32[]{:S(2)}) collective-permute-start(bf16[2,1,128,512]{3,2,1,0:T(8,128)(2,1)} %get-tuple-element.81), channel_id=1, source_target_pairs={{8,16},{16,8},{9,17},{17,9},{10,18},{18,10},{11,19},{19,11},{12,20... | collective-permute-start | bytes 786440 | tf_op jit(solution)/shard_map/ppermute | solution.py:313
  198.1 0.8 collective-permute-done.19.refs_6_
  198.9 6.0 %collective-permute-start.31 = (bf16[2,1,128,512]{3,2,1,0:T(8,128)(2,1)}, bf16[2,1,128,512]{3,2,1,0:T(8,128)(2,1)}, u32[]{:S(2)}, u32[]{:S(2)}) collective-permute-start(bf16[2,1,128,512]{3,2,1,0:T(8,128)(2,1)} %get-tuple-element.82), channel_id=1, source_target_pairs={{8,16},{16,8},{9,17},{17,9},{10,18},{18,10},{11,19},{19,11},{12,20... | collective-permute-start | bytes 786440 | tf_op jit(solution)/shard_map/ppermute | solution.py:313
  204.9 0.4 collective-permute-done.20.refs_7_
  205.3 1.7 collective-permute-start.32
  207.0 0.5 collective-permute-start.34
  207.9 1.3 collective-permute-done.31.refs_12_
  209.6 9.1 %mix.1 = bf16[128,2,4,16,128]{4,3,2,1,0:T(8,128)(2,1)} custom-call(s32[2]{0:T(128)S(1)} %pad_add_fusion.me_ref, f32[4,4]{1,0:T(4,128)S(1)} %get-tuple-element.90.up_ref, f32[4,4]{1,0:T(4,128)S(1)} %get-tuple-element.89.down_ref, bf16[1024,512]{1,0:T(8,128)(2,1)S(1)} %bitcast.27, f32[4,128,512]{2,1,0:T(8,128)S(1)} %get-tuple-element.88.cosine_ref, ...), custom_call_target="tpu_custom_call" | custom-call | flops 2147483648 | bytes 10485760 | tf_op jit(solution)/shard_map/mix/pallas_call | solution.py:278
  (65 shorter events, 1.6 us)
Async XLA Ops:
  5.4 31.1 %collective-permute-start = (bf16[2,128,512]{2,1,0:T(8,128)(2,1)}, bf16[2,128,512]{2,1,0:T(8,128)(2,1)S(1)}, u32[]{:S(2)}, u32[]{:S(2)}) collective-permute-start(bf16[2,128,512]{2,1,0:T(8,128)(2,1)} %get-tuple-element.48), channel_id=1, source_target_pairs={{0,4},{1,5},{2,6},{3,7},{4,0},{5,1},{6,2},{7,3},{8,12},{9,13},{10,... | collective-permute-start | bytes 786440 | tf_op jit(solution)/shard_map/ppermute | solution.py:306
  7.7 34.4 %collective-permute-start.1 = (bf16[2,128,512]{2,1,0:T(8,128)(2,1)}, bf16[2,128,512]{2,1,0:T(8,128)(2,1)S(1)}, u32[]{:S(2)}, u32[]{:S(2)}) collective-permute-start(bf16[2,128,512]{2,1,0:T(8,128)(2,1)} %get-tuple-element.49), channel_id=1, source_target_pairs={{0,5},{1,4},{2,7},{3,6},{4,1},{5,0},{6,3},{7,2},{8,13},{9,12},{10,... | collective-permute-start | bytes 786440 | tf_op jit(solution)/shard_map/ppermute | solution.py:306
  8.8 46.4 %collective-permute-start.2 = (bf16[2,128,512]{2,1,0:T(8,128)(2,1)}, bf16[2,128,512]{2,1,0:T(8,128)(2,1)S(1)}, u32[]{:S(2)}, u32[]{:S(2)}) collective-permute-start(bf16[2,128,512]{2,1,0:T(8,128)(2,1)} %get-tuple-element.50), channel_id=1, source_target_pairs={{0,6},{1,7},{2,4},{3,5},{4,2},{5,3},{6,0},{7,1},{8,14},{9,15},{10,... | collective-permute-start | bytes 786440 | tf_op jit(solution)/shard_map/ppermute | solution.py:306
  10.0 48.1 %collective-permute-start.3 = (bf16[2,128,512]{2,1,0:T(8,128)(2,1)}, bf16[2,128,512]{2,1,0:T(8,128)(2,1)S(1)}, u32[]{:S(2)}, u32[]{:S(2)}) collective-permute-start(bf16[2,128,512]{2,1,0:T(8,128)(2,1)} %get-tuple-element.51), channel_id=1, source_target_pairs={{0,7},{1,6},{2,5},{3,4},{4,3},{5,2},{6,1},{7,0},{8,15},{9,14},{10,... | collective-permute-start | bytes 786440 | tf_op jit(solution)/shard_map/ppermute | solution.py:306
  10.2 48.2 %collective-permute-start.4 = (bf16[2,128,512]{2,1,0:T(8,128)(2,1)}, bf16[2,128,512]{2,1,0:T(8,128)(2,1)S(1)}, u32[]{:S(2)}, u32[]{:S(2)}) collective-permute-start(bf16[2,128,512]{2,1,0:T(8,128)(2,1)} %get-tuple-element.52), channel_id=1, source_target_pairs={{0,1},{1,0},{2,3},{3,2},{4,5},{5,4},{6,7},{7,6},{8,9},{9,8},{10,11... | collective-permute-start | bytes 786440 | tf_op jit(solution)/shard_map/ppermute | solution.py:306
  36.4 25.2 %collective-permute-start.5 = (bf16[2,128,512]{2,1,0:T(8,128)(2,1)}, bf16[2,128,512]{2,1,0:T(8,128)(2,1)S(1)}, u32[]{:S(2)}, u32[]{:S(2)}) collective-permute-start(bf16[2,128,512]{2,1,0:T(8,128)(2,1)} %get-tuple-element.53), channel_id=1, source_target_pairs={{0,2},{1,3},{2,0},{3,1},{4,6},{5,7},{6,4},{7,5},{8,10},{9,11},{10,... | collective-permute-start | bytes 786440 | tf_op jit(solution)/shard_map/ppermute | solution.py:306
  42.1 19.6 %collective-permute-start.6 = (bf16[2,128,512]{2,1,0:T(8,128)(2,1)}, bf16[2,128,512]{2,1,0:T(8,128)(2,1)S(1)}, u32[]{:S(2)}, u32[]{:S(2)}) collective-permute-start(bf16[2,128,512]{2,1,0:T(8,128)(2,1)} %get-tuple-element.54), channel_id=1, source_target_pairs={{0,3},{1,2},{2,1},{3,0},{4,7},{5,6},{6,5},{7,4},{8,11},{9,10},{10,... | collective-permute-start | bytes 786440 | tf_op jit(solution)/shard_map/ppermute | solution.py:306
  43.2 6.5 %copy-start.1 = (bf16[2,512,512]{2,1,0:T(8,128)(2,1)S(1)}, bf16[2,512,512]{2,1,0:T(8,128)(2,1)}, u32[]{:S(2)}) copy-start(bf16[2,512,512]{2,1,0:T(8,128)(2,1)} %param.8) | copy-start | bytes 3145732
  43.2 6.5 %copy-start.5 = (bf16[2,128,512]{2,1,0:T(8,128)(2,1)S(1)}, bf16[2,128,512]{2,1,0:T(8,128)(2,1)}, u32[]{:S(2)}) copy-start(bf16[2,128,512]{2,1,0:T(8,128)(2,1)} %get-tuple-element.46.refs_0_.refs_1_) | copy-start | bytes 786436
  49.7 2.2 %copy-start = (bf16[128,2,4,4,512]{4,3,2,1,0:T(4,128)(2,1)S(1)}, bf16[128,2,4,4,512]{4,3,2,1,0:T(4,128)(2,1)}, u32[]{:S(2)}) copy-start(bf16[128,2,4,4,512]{4,3,2,1,0:T(4,128)(2,1)} %param.6) | copy-start | bytes 12582916
  51.9 11.0 %copy-start.2 = (bf16[2048,1024]{0,1:T(8,128)(2,1)S(1)}, bf16[2048,1024]{0,1:T(8,128)(2,1)}, u32[]{:S(2)}) copy-start(bf16[2048,1024]{0,1:T(8,128)(2,1)} %copy.14) | copy-start | bytes 12582916
  55.2 30.5 %collective-permute-start.10 = (bf16[2,128,512]{2,1,0:T(8,128)(2,1)S(1)}, bf16[2,128,512]{2,1,0:T(8,128)(2,1)S(1)}, u32[]{:S(2)}, u32[]{:S(2)}) collective-permute-start(bf16[2,128,512]{2,1,0:T(8,128)(2,1)S(1)} %get-tuple-element.59), channel_id=1, source_target_pairs={{0,4},{1,5},{2,6},{3,7},{4,0},{5,1},{6,2},{7,3},{8,12},{9,13},{10,... | collective-permute-start | bytes 786440 | tf_op jit(solution)/shard_map/ppermute | solution.py:306
  58.1 33.2 %collective-permute-start.11 = (bf16[2,128,512]{2,1,0:T(8,128)(2,1)S(1)}, bf16[2,128,512]{2,1,0:T(8,128)(2,1)S(1)}, u32[]{:S(2)}, u32[]{:S(2)}) collective-permute-start(bf16[2,128,512]{2,1,0:T(8,128)(2,1)S(1)} %get-tuple-element.60), channel_id=1, source_target_pairs={{0,5},{1,4},{2,7},{3,6},{4,1},{5,0},{6,3},{7,2},{8,13},{9,12},{10,... | collective-permute-start | bytes 786440 | tf_op jit(solution)/shard_map/ppermute | solution.py:306
  58.3 40.3 %collective-permute-start.12 = (bf16[2,128,512]{2,1,0:T(8,128)(2,1)S(1)}, bf16[2,128,512]{2,1,0:T(8,128)(2,1)S(1)}, u32[]{:S(2)}, u32[]{:S(2)}) collective-permute-start(bf16[2,128,512]{2,1,0:T(8,128)(2,1)S(1)} %get-tuple-element.61), channel_id=1, source_target_pairs={{0,6},{1,7},{2,4},{3,5},{4,2},{5,3},{6,0},{7,1},{8,14},{9,15},{10,... | collective-permute-start | bytes 786440 | tf_op jit(solution)/shard_map/ppermute | solution.py:306
  61.7 45.9 %collective-permute-start.13 = (bf16[2,128,512]{2,1,0:T(8,128)(2,1)S(1)}, bf16[2,128,512]{2,1,0:T(8,128)(2,1)S(1)}, u32[]{:S(2)}, u32[]{:S(2)}) collective-permute-start(bf16[2,128,512]{2,1,0:T(8,128)(2,1)S(1)} %get-tuple-element.62), channel_id=1, source_target_pairs={{0,7},{1,6},{2,5},{3,4},{4,3},{5,2},{6,1},{7,0},{8,15},{9,14},{10,... | collective-permute-start | bytes 786440 | tf_op jit(solution)/shard_map/ppermute | solution.py:306
  61.7 49.5 %collective-permute-start.7 = (bf16[2,128,512]{2,1,0:T(8,128)(2,1)S(1)}, bf16[2,128,512]{2,1,0:T(8,128)(2,1)S(1)}, u32[]{:S(2)}, u32[]{:S(2)}) collective-permute-start(bf16[2,128,512]{2,1,0:T(8,128)(2,1)S(1)} %get-tuple-element.56), channel_id=1, source_target_pairs={{0,1},{1,0},{2,3},{3,2},{4,5},{5,4},{6,7},{7,6},{8,9},{9,8},{10,11... | collective-permute-start | bytes 786440 | tf_op jit(solution)/shard_map/ppermute | solution.py:306
  62.9 44.6 %copy-start.6 = (f32[128,4,512]{2,1,0:T(4,128)S(1)}, f32[128,4,512]{2,1,0:T(4,128)}, u32[]{:S(2)}) copy-start(f32[128,4,512]{2,1,0:T(4,128)} %param.9) | copy-start | bytes 3145732
  85.7 27.3 %collective-permute-start.8 = (bf16[2,128,512]{2,1,0:T(8,128)(2,1)S(1)}, bf16[2,128,512]{2,1,0:T(8,128)(2,1)S(1)}, u32[]{:S(2)}, u32[]{:S(2)}) collective-permute-start(bf16[2,128,512]{2,1,0:T(8,128)(2,1)S(1)} %get-tuple-element.57), channel_id=1, source_target_pairs={{0,2},{1,3},{2,0},{3,1},{4,6},{5,7},{6,4},{7,5},{8,10},{9,11},{10,... | collective-permute-start | bytes 786440 | tf_op jit(solution)/shard_map/ppermute | solution.py:306
  91.3 21.6 %collective-permute-start.9 = (bf16[2,128,512]{2,1,0:T(8,128)(2,1)S(1)}, bf16[2,128,512]{2,1,0:T(8,128)(2,1)S(1)}, u32[]{:S(2)}, u32[]{:S(2)}) collective-permute-start(bf16[2,128,512]{2,1,0:T(8,128)(2,1)S(1)} %get-tuple-element.58), channel_id=1, source_target_pairs={{0,3},{1,2},{2,1},{3,0},{4,7},{5,6},{6,5},{7,4},{8,11},{9,10},{10,... | collective-permute-start | bytes 786440 | tf_op jit(solution)/shard_map/ppermute | solution.py:306
  98.6 17.4 %collective-permute-start.21 = (bf16[2,128,512]{2,1,0:T(8,128)(2,1)S(1)}, bf16[2,128,512]{2,1,0:T(8,128)(2,1)S(1)}, u32[]{:S(2)}, u32[]{:S(2)}) collective-permute-start(bf16[2,128,512]{2,1,0:T(8,128)(2,1)S(1)} %get-tuple-element.71), channel_id=1, source_target_pairs={{0,1},{1,0},{2,3},{3,2},{4,5},{5,4},{6,7},{7,6},{8,9},{9,8},{10,11... | collective-permute-start | bytes 786440 | tf_op jit(solution)/shard_map/ppermute | solution.py:306
  107.5 8.5 %collective-permute-start.22 = (bf16[2,128,512]{2,1,0:T(8,128)(2,1)S(1)}, bf16[2,128,512]{2,1,0:T(8,128)(2,1)S(1)}, u32[]{:S(2)}, u32[]{:S(2)}) collective-permute-start(bf16[2,128,512]{2,1,0:T(8,128)(2,1)S(1)} %get-tuple-element.72), channel_id=1, source_target_pairs={{0,2},{1,3},{2,0},{3,1},{4,6},{5,7},{6,4},{7,5},{8,10},{9,11},{10,... | collective-permute-start | bytes 786440 | tf_op jit(solution)/shard_map/ppermute | solution.py:306
  111.2 12.6 %collective-permute-start.23 = (bf16[2,128,512]{2,1,0:T(8,128)(2,1)S(1)}, bf16[2,128,512]{2,1,0:T(8,128)(2,1)S(1)}, u32[]{:S(2)}, u32[]{:S(2)}) collective-permute-start(bf16[2,128,512]{2,1,0:T(8,128)(2,1)S(1)} %get-tuple-element.73), channel_id=1, source_target_pairs={{0,3},{1,2},{2,1},{3,0},{4,7},{5,6},{6,5},{7,4},{8,11},{9,10},{10,... | collective-permute-start | bytes 786440 | tf_op jit(solution)/shard_map/ppermute | solution.py:306
  113.0 11.7 %collective-permute-start.24 = (bf16[2,128,512]{2,1,0:T(8,128)(2,1)S(1)}, bf16[2,128,512]{2,1,0:T(8,128)(2,1)S(1)}, u32[]{:S(2)}, u32[]{:S(2)}) collective-permute-start(bf16[2,128,512]{2,1,0:T(8,128)(2,1)S(1)} %get-tuple-element.74), channel_id=1, source_target_pairs={{0,4},{1,5},{2,6},{3,7},{4,0},{5,1},{6,2},{7,3},{8,12},{9,13},{10,... | collective-permute-start | bytes 786440 | tf_op jit(solution)/shard_map/ppermute | solution.py:306
  113.0 32.9 %collective-permute-start.25 = (bf16[2,128,512]{2,1,0:T(8,128)(2,1)S(1)}, bf16[2,128,512]{2,1,0:T(8,128)(2,1)S(1)}, u32[]{:S(2)}, u32[]{:S(2)}) collective-permute-start(bf16[2,128,512]{2,1,0:T(8,128)(2,1)S(1)} %get-tuple-element.75), channel_id=1, source_target_pairs={{0,5},{1,4},{2,7},{3,6},{4,1},{5,0},{6,3},{7,2},{8,13},{9,12},{10,... | collective-permute-start | bytes 786440 | tf_op jit(solution)/shard_map/ppermute | solution.py:306
  116.0 37.4 %collective-permute-start.26 = (bf16[2,128,512]{2,1,0:T(8,128)(2,1)S(1)}, bf16[2,128,512]{2,1,0:T(8,128)(2,1)S(1)}, u32[]{:S(2)}, u32[]{:S(2)}) collective-permute-start(bf16[2,128,512]{2,1,0:T(8,128)(2,1)S(1)} %get-tuple-element.76), channel_id=1, source_target_pairs={{0,6},{1,7},{2,4},{3,5},{4,2},{5,3},{6,0},{7,1},{8,14},{9,15},{10,... | collective-permute-start | bytes 786440 | tf_op jit(solution)/shard_map/ppermute | solution.py:306
  116.1 49.8 %collective-permute-start.27 = (bf16[2,128,512]{2,1,0:T(8,128)(2,1)S(1)}, bf16[2,128,512]{2,1,0:T(8,128)(2,1)S(1)}, u32[]{:S(2)}, u32[]{:S(2)}) collective-permute-start(bf16[2,128,512]{2,1,0:T(8,128)(2,1)S(1)} %get-tuple-element.77), channel_id=1, source_target_pairs={{0,7},{1,6},{2,5},{3,4},{4,3},{5,2},{6,1},{7,0},{8,15},{9,14},{10,... | collective-permute-start | bytes 786440 | tf_op jit(solution)/shard_map/ppermute | solution.py:306
  123.5 74.5 %copy-start.12 = (f32[16,4]{0,1:T(4,128)S(1)}, f32[16,4]{0,1:T(4,128)}, u32[]{:S(2)}) copy-start(f32[16,4]{0,1:T(4,128)} %param.10) | copy-start | bytes 772
  123.5 86.2 %copy-start.3 = (f32[128,512]{1,0:T(8,128)S(1)}, f32[128,512]{1,0:T(8,128)}, u32[]{:S(2)}) copy-start(f32[128,512]{1,0:T(8,128)} %weight_ref.1) | copy-start | bytes 786436
  123.8 47.9 %collective-permute-start.14 = (bf16[2,128,512]{2,1,0:T(8,128)(2,1)S(1)}, bf16[2,128,512]{2,1,0:T(8,128)(2,1)S(1)}, u32[]{:S(2)}, u32[]{:S(2)}) collective-permute-start(bf16[2,128,512]{2,1,0:T(8,128)(2,1)S(1)} %get-tuple-element.64), channel_id=1, source_target_pairs={{0,1},{1,0},{2,3},{3,2},{4,5},{5,4},{6,7},{7,6},{8,9},{9,8},{10,11... | collective-permute-start | bytes 786440 | tf_op jit(solution)/shard_map/ppermute | solution.py:306
  124.6 47.1 %collective-permute-start.15 = (bf16[2,128,512]{2,1,0:T(8,128)(2,1)S(1)}, bf16[2,128,512]{2,1,0:T(8,128)(2,1)S(1)}, u32[]{:S(2)}, u32[]{:S(2)}) collective-permute-start(bf16[2,128,512]{2,1,0:T(8,128)(2,1)S(1)} %get-tuple-element.65), channel_id=1, source_target_pairs={{0,2},{1,3},{2,0},{3,1},{4,6},{5,7},{6,4},{7,5},{8,10},{9,11},{10,... | collective-permute-start | bytes 786440 | tf_op jit(solution)/shard_map/ppermute | solution.py:306
  145.8 27.5 %collective-permute-start.16 = (bf16[2,128,512]{2,1,0:T(8,128)(2,1)S(1)}, bf16[2,128,512]{2,1,0:T(8,128)(2,1)S(1)}, u32[]{:S(2)}, u32[]{:S(2)}) collective-permute-start(bf16[2,128,512]{2,1,0:T(8,128)(2,1)S(1)} %get-tuple-element.66), channel_id=1, source_target_pairs={{0,3},{1,2},{2,1},{3,0},{4,7},{5,6},{6,5},{7,4},{8,11},{9,10},{10,... | collective-permute-start | bytes 786440 | tf_op jit(solution)/shard_map/ppermute | solution.py:306
  153.5 26.4 %collective-permute-start.17 = (bf16[2,128,512]{2,1,0:T(8,128)(2,1)S(1)}, bf16[2,128,512]{2,1,0:T(8,128)(2,1)S(1)}, u32[]{:S(2)}, u32[]{:S(2)}) collective-permute-start(bf16[2,128,512]{2,1,0:T(8,128)(2,1)S(1)} %get-tuple-element.67), channel_id=1, source_target_pairs={{0,4},{1,5},{2,6},{3,7},{4,0},{5,1},{6,2},{7,3},{8,12},{9,13},{10,... | collective-permute-start | bytes 786440 | tf_op jit(solution)/shard_map/ppermute | solution.py:306
  165.9 25.8 %collective-permute-start.18 = (bf16[2,128,512]{2,1,0:T(8,128)(2,1)S(1)}, bf16[2,128,512]{2,1,0:T(8,128)(2,1)S(1)}, u32[]{:S(2)}, u32[]{:S(2)}) collective-permute-start(bf16[2,128,512]{2,1,0:T(8,128)(2,1)S(1)} %get-tuple-element.68), channel_id=1, source_target_pairs={{0,5},{1,4},{2,7},{3,6},{4,1},{5,0},{6,3},{7,2},{8,13},{9,12},{10,... | collective-permute-start | bytes 786440 | tf_op jit(solution)/shard_map/ppermute | solution.py:306
  171.0 0.7 copy-start.4
  171.7 20.0 %copy-start.7 = (bf16[2,128,512]{2,1,0:T(8,128)(2,1)}, bf16[2,128,512]{2,1,0:T(8,128)(2,1)S(1)}, u32[]{:S(2)}) copy-start(bf16[2,128,512]{2,1,0:T(8,128)(2,1)S(1)} %collective-permute-done.14.refs_1_) | copy-start | bytes 786436
  171.7 27.2 %collective-permute-start.19 = (bf16[2,128,512]{2,1,0:T(8,128)(2,1)}, bf16[2,128,512]{2,1,0:T(8,128)(2,1)}, u32[]{:S(2)}, u32[]{:S(2)}) collective-permute-start(bf16[2,128,512]{2,1,0:T(8,128)(2,1)} %get-tuple-element.69), channel_id=1, source_target_pairs={{0,6},{1,7},{2,4},{3,5},{4,2},{5,3},{6,0},{7,1},{8,14},{9,15},{10,... | collective-permute-start | bytes 786440 | tf_op jit(solution)/shard_map/ppermute | solution.py:306
  171.7 20.0 %copy-start.8 = (bf16[2,128,512]{2,1,0:T(8,128)(2,1)}, bf16[2,128,512]{2,1,0:T(8,128)(2,1)S(1)}, u32[]{:S(2)}) copy-start(bf16[2,128,512]{2,1,0:T(8,128)(2,1)S(1)} %collective-permute-done.15.refs_2_) | copy-start | bytes 786436
  171.7 33.6 %collective-permute-start.20 = (bf16[2,128,512]{2,1,0:T(8,128)(2,1)}, bf16[2,128,512]{2,1,0:T(8,128)(2,1)}, u32[]{:S(2)}, u32[]{:S(2)}) collective-permute-start(bf16[2,128,512]{2,1,0:T(8,128)(2,1)} %get-tuple-element.70), channel_id=1, source_target_pairs={{0,7},{1,6},{2,5},{3,4},{4,3},{5,2},{6,1},{7,0},{8,15},{9,14},{10,... | collective-permute-start | bytes 786440 | tf_op jit(solution)/shard_map/ppermute | solution.py:306
  173.3 18.4 %copy-start.9 = (bf16[2,128,512]{2,1,0:T(8,128)(2,1)}, bf16[2,128,512]{2,1,0:T(8,128)(2,1)S(1)}, u32[]{:S(2)}) copy-start(bf16[2,128,512]{2,1,0:T(8,128)(2,1)S(1)} %collective-permute-done.16.refs_3_) | copy-start | bytes 786436
  173.3 33.6 %collective-permute-start.28 = (bf16[2,1,128,512]{3,2,1,0:T(8,128)(2,1)}, bf16[2,1,128,512]{3,2,1,0:T(8,128)(2,1)}, u32[]{:S(2)}, u32[]{:S(2)}) collective-permute-start(bf16[2,1,128,512]{3,2,1,0:T(8,128)(2,1)} %get-tuple-element.79), channel_id=1, source_target_pairs={{8,16},{16,8},{9,17},{17,9},{10,18},{18,10},{11,19},{19,11},{12,20... | collective-permute-start | bytes 786440 | tf_op jit(solution)/shard_map/ppermute | solution.py:313
  179.9 11.8 %copy-start.10 = (bf16[2,128,512]{2,1,0:T(8,128)(2,1)}, bf16[2,128,512]{2,1,0:T(8,128)(2,1)S(1)}, u32[]{:S(2)}) copy-start(bf16[2,128,512]{2,1,0:T(8,128)(2,1)S(1)} %collective-permute-done.17.refs_4_) | copy-start | bytes 786436
  179.9 27.1 %collective-permute-start.29 = (bf16[2,1,128,512]{3,2,1,0:T(8,128)(2,1)}, bf16[2,1,128,512]{3,2,1,0:T(8,128)(2,1)}, u32[]{:S(2)}, u32[]{:S(2)}) collective-permute-start(bf16[2,1,128,512]{3,2,1,0:T(8,128)(2,1)} %get-tuple-element.80), channel_id=1, source_target_pairs={{8,16},{16,8},{9,17},{17,9},{10,18},{18,10},{11,19},{19,11},{12,20... | collective-permute-start | bytes 786440 | tf_op jit(solution)/shard_map/ppermute | solution.py:313
  192.4 15.1 %collective-permute-start.30 = (bf16[2,1,128,512]{3,2,1,0:T(8,128)(2,1)}, bf16[2,1,128,512]{3,2,1,0:T(8,128)(2,1)}, u32[]{:S(2)}, u32[]{:S(2)}) collective-permute-start(bf16[2,1,128,512]{3,2,1,0:T(8,128)(2,1)} %get-tuple-element.81), channel_id=1, source_target_pairs={{8,16},{16,8},{9,17},{17,9},{10,18},{18,10},{11,19},{19,11},{12,20... | collective-permute-start | bytes 786440 | tf_op jit(solution)/shard_map/ppermute | solution.py:313
  198.9 10.3 %collective-permute-start.31 = (bf16[2,1,128,512]{3,2,1,0:T(8,128)(2,1)}, bf16[2,1,128,512]{3,2,1,0:T(8,128)(2,1)}, u32[]{:S(2)}, u32[]{:S(2)}) collective-permute-start(bf16[2,1,128,512]{3,2,1,0:T(8,128)(2,1)} %get-tuple-element.82), channel_id=1, source_target_pairs={{8,16},{16,8},{9,17},{17,9},{10,18},{18,10},{11,19},{19,11},{12,20... | collective-permute-start | bytes 786440 | tf_op jit(solution)/shard_map/ppermute | solution.py:313
  205.3 4.0 %collective-permute-start.32 = (bf16[2,1,128,512]{3,2,1,0:T(8,128)(2,1)}, bf16[2,1,128,512]{3,2,1,0:T(8,128)(2,1)}, u32[]{:S(2)}, u32[]{:S(2)}) collective-permute-start(bf16[2,1,128,512]{3,2,1,0:T(8,128)(2,1)} %get-tuple-element.83), channel_id=1, source_target_pairs={{0,8},{16,24},{8,0},{24,16},{1,9},{17,25},{9,1},{25,17},{2,10},{18... | collective-permute-start | bytes 786440 | tf_op jit(solution)/shard_map/ppermute | solution.py:313
  207.0 2.3 %collective-permute-start.33 = (bf16[2,1,128,512]{3,2,1,0:T(8,128)(2,1)}, bf16[2,1,128,512]{3,2,1,0:T(8,128)(2,1)}, u32[]{:S(2)}, u32[]{:S(2)}) collective-permute-start(bf16[2,1,128,512]{3,2,1,0:T(8,128)(2,1)} %get-tuple-element.84), channel_id=1, source_target_pairs={{0,8},{16,24},{8,0},{24,16},{1,9},{17,25},{9,1},{25,17},{2,10},{18... | collective-permute-start | bytes 786440 | tf_op jit(solution)/shard_map/ppermute | solution.py:313
  207.0 2.3 %collective-permute-start.34 = (bf16[2,1,128,512]{3,2,1,0:T(8,128)(2,1)}, bf16[2,1,128,512]{3,2,1,0:T(8,128)(2,1)}, u32[]{:S(2)}, u32[]{:S(2)}) collective-permute-start(bf16[2,1,128,512]{3,2,1,0:T(8,128)(2,1)} %get-tuple-element.85), channel_id=1, source_target_pairs={{0,8},{16,24},{8,0},{24,16},{1,9},{17,25},{9,1},{25,17},{2,10},{18... | collective-permute-start | bytes 786440 | tf_op jit(solution)/shard_map/ppermute | solution.py:313
  207.5 2.1 collective-permute-start.35
  (1 other events, 0.7 us)

commit v15 on v14

--- a/solution.py
+++ b/solution.py
@@ -273,7 +273,7 @@
     _, share, _, width = halo[0].shape
     blocks, states = up.shape
     group = width // LANES * states
-    block = rows // 2
+    block = rows // 4
     table = pl.BlockSpec((states, block, width), lambda i: (0, i, 0))
     return pl.pallas_call(
         functools.partial(mix_kernel, tuple(chosen), order),
@@ -336,10 +336,8 @@
         last = half[0]
         lines.append(exchanged(half, "rad"))
     backs = []
-    far_first = (0, *range(ranks // 2, ranks), *range(1, ranks // 2))
-    orders = (far_first, tuple(range(ranks)))
-    for line, order in zip(lines, orders):
-        moved = left_call([last], me, first, line, order)
+    for line in lines:
+        moved = left_call([last], me, first, line, tuple(range(ranks)))
         last = moved[0]
         backs.append(exchanged(moved, "rad"))
 

time: 220 us -> 217 us (0.986)
  waiting for transfers between devices: 101 us -> 85.9 us
  starting transfers between devices: 69.7 us -> 80.9 us
    ppermute x28, waiting for transfers between devices: 99.2 us -> 82.9 us  [exchanged(): result[s] = lax.ppermute(slabs[s], axis, [(i, i ^ s) for i in range(count)])]
    ppermute x8, starting transfers between devices: 32.1 us -> 38 us  [paired(): return lax.ppermute(edge, axis, pairs + [(j, i) for i, j in pairs])]
    ppermute x28, starting transfers between devices: 37.6 us -> 43 us  [exchanged(): result[s] = lax.ppermute(slabs[s], axis, [(i, i ^ s) for i in range(count)])]
where the time goes in v15:
time: 217 us; the launch traced here: 215 us
  waiting for transfers between devices  85.9 us (40%)
  starting transfers between devices  80.9 us (37%)
  Pallas kernels  33.5 us (15%)
  local copies, waits for them, and re-layouts  14.2 us (7%)
    ppermute x28, waiting for transfers between devices, exchanged(): result[s] = lax.ppermute(slabs[s], axis, [(i, i ^ s) for i in range(count)])  82.9 us
    ppermute x28, starting transfers between devices, exchanged(): result[s] = lax.ppermute(slabs[s], axis, [(i, i ^ s) for i in range(count)])  43 us
    ppermute x8, starting transfers between devices, paired(): return lax.ppermute(edge, axis, pairs + [(j, i) for i, j in pairs])  38 us
    pallas_call x2, Pallas kernels, left_call(): pl.pallas_call(functools.partial(left_kernel, len(after), order), grid=(k...  10.8 us
    pallas_call x1, Pallas kernels, mix_call(): pl.pallas_call(functools.partial(mix_kernel, tuple(chosen), order), grid=...  8.97 us
    pallas_call x2, Pallas kernels, right_call(): pl.pallas_call(functools.partial(right_kernel, len(after), ranks, states)...  8.63 us
    reshape x1, local copies, waits for them, and re-layouts, per_device(): first = first_propagator.reshape(2 * whole, whole).T  6.53 us
    pallas_call x1, Pallas kernels, phase_call(): pl.pallas_call(functools.partial(phase_kernel, len(after), ranks), grid=(...  5.05 us
  transfers between devices with their start and end apart: 36, of which 15 were waited for; matrix products, arithmetic and copies ran while one was open for 5% of the time, Pallas kernels for 9%

profile of v15, /device:TPU:9, one launch (start us, length us, event | category | flops | bytes accessed | tf_op | source)
XLA Modules:
  0.0 215.0 jit_solution(13818933353491060548)
XLA Ops:
  0.0 5.4 %right.2 = (bf16[2,128,512]{2,1,0:T(8,128)(2,1)}, bf16[2,128,512]{2,1,0:T(8,128)(2,1)}, bf16[2,128,512]{2,1,0:T(8,128)(2,1)}, bf16[2,128,512]{2,1,0:T(8,128)(2,1...) custom-call(s32[1]{0:T(128)} %bitcast.me_ref.refs_0_, ...), custom_call_target="tpu_custom_call" | custom-call | flops 2147483648 | bytes 4194304 | tf_op jit(solution)/shard_map/right/pallas_call | solution.py:74
  5.4 1.3 collective-permute-start
  6.8 1.2 collective-permute-start.2
  8.1 2.3 %collective-permute-start.3 = (bf16[2,128,512]{2,1,0:T(8,128)(2,1)}, bf16[2,128,512]{2,1,0:T(8,128)(2,1)S(1)}, u32[]{:S(2)}, u32[]{:S(2)}) collective-permute-start(bf16[2,128,512]{2,1,0:T(8,128)(2,1)} %get-tuple-element.51), channel_id=1, source_target_pairs={{0,4},{1,5},{2,6},{3,7},{4,0},{5,1},{6,2},{7,3},{8,12},{9,13},{10,... | collective-permute-start | bytes 786440 | tf_op jit(solution)/shard_map/ppermute | solution.py:306
  10.4 1.0 collective-permute-start.4
  11.4 1.4 collective-permute-done.refs_2_
  12.8 1.3 collective-permute-start.5
  14.1 7.6 %collective-permute-done.1.refs_3_ = bf16[2,128,512]{2,1,0:T(8,128)(2,1)S(1)} collective-permute-done((bf16[2,128,512]{2,1,0:T(8,128)(2,1)}, bf16[2,128,512]{2,1,0:T(8,128)(2,1)S(1)}, u32[]{:S(2)}, u32[]{:S(2)}) %collective-permute-start.1) | collective-permute-done | bytes 262176 | tf_op jit(solution)/shard_map/ppermute | solution.py:306
  21.7 6.5 %copy.14 = bf16[2048,1024]{0,1:T(8,128)(2,1)} copy(bf16[2048,1024]{1,0:T(8,128)(2,1)} %bitcast.30) | data formatting | bytes 8388608 | tf_op jit(solution)/shard_map/reshape | solution.py:325
  28.2 2.2 %copy-done = bf16[128,2,4,4,512]{4,3,2,1,0:T(4,128)(2,1)S(1)} copy-done((bf16[128,2,4,4,512]{4,3,2,1,0:T(4,128)(2,1)S(1)}, bf16[128,2,4,4,512]{4,3,2,1,0:T(4,128)(2,1)}, u32[]{:S(2)}) %copy-start) | copy-done | bytes 4194328
  30.4 3.3 %right.3 = (bf16[2,128,512]{2,1,0:T(8,128)(2,1)S(1)}, bf16[2,128,512]{2,1,0:T(8,128)(2,1)S(1)}, bf16[2,128,512]{2,1,0:T(8,128)(2,1)S(1)}, bf16[2,128,512]{2,1,0:...) custom-call(s32[1]{0:T(128)} %bitcast.me_ref.refs_0_, ...), custom_call_target="tpu_custom_call" | custom-call | flops 2147483648 | bytes 4194304 | tf_op jit(solution)/shard_map/right/pallas_call | solution.py:74
  33.7 3.8 %collective-permute-start.10 = (bf16[2,128,512]{2,1,0:T(8,128)(2,1)S(1)}, bf16[2,128,512]{2,1,0:T(8,128)(2,1)S(1)}, u32[]{:S(2)}, u32[]{:S(2)}) collective-permute-start(bf16[2,128,512]{2,1,0:T(8,128)(2,1)S(1)} %get-tuple-element.59), channel_id=1, source_target_pairs={{0,4},{1,5},{2,6},{3,7},{4,0},{5,1},{6,2},{7,3},{8,12},{9,13},{10,... | collective-permute-start | bytes 786440 | tf_op jit(solution)/shard_map/ppermute | solution.py:306
  37.4 1.7 collective-permute-start.11
  39.2 14.9 %collective-permute-done.4.refs_6_ = bf16[2,128,512]{2,1,0:T(8,128)(2,1)S(1)} collective-permute-done((bf16[2,128,512]{2,1,0:T(8,128)(2,1)}, bf16[2,128,512]{2,1,0:T(8,128)(2,1)S(1)}, u32[]{:S(2)}, u32[]{:S(2)}) %collective-permute-start.4) | collective-permute-done | bytes 262176 | tf_op jit(solution)/shard_map/ppermute | solution.py:306
  54.0 8.5 %collective-permute-done.5.refs_7_ = bf16[2,128,512]{2,1,0:T(8,128)(2,1)S(1)} collective-permute-done((bf16[2,128,512]{2,1,0:T(8,128)(2,1)}, bf16[2,128,512]{2,1,0:T(8,128)(2,1)S(1)}, u32[]{:S(2)}, u32[]{:S(2)}) %collective-permute-start.5) | collective-permute-done | bytes 262176 | tf_op jit(solution)/shard_map/ppermute | solution.py:306
  62.5 11.6 %collective-permute-start.13 = (bf16[2,128,512]{2,1,0:T(8,128)(2,1)S(1)}, bf16[2,128,512]{2,1,0:T(8,128)(2,1)S(1)}, u32[]{:S(2)}, u32[]{:S(2)}) collective-permute-start(bf16[2,128,512]{2,1,0:T(8,128)(2,1)S(1)} %get-tuple-element.62), channel_id=1, source_target_pairs={{0,7},{1,6},{2,5},{3,4},{4,3},{5,2},{6,1},{7,0},{8,15},{9,14},{10,... | collective-permute-start | bytes 786440 | tf_op jit(solution)/shard_map/ppermute | solution.py:306
  74.1 3.2 %collective-permute-done.6.refs_8_ = bf16[2,128,512]{2,1,0:T(8,128)(2,1)S(1)} collective-permute-done((bf16[2,128,512]{2,1,0:T(8,128)(2,1)}, bf16[2,128,512]{2,1,0:T(8,128)(2,1)S(1)}, u32[]{:S(2)}, u32[]{:S(2)}) %collective-permute-start.6) | collective-permute-done | bytes 262176 | tf_op jit(solution)/shard_map/ppermute | solution.py:306
  77.3 0.6 collective-permute-start.7
  77.9 5.1 %left.2 = (bf16[2,128,512]{2,1,0:T(8,128)(2,1)S(1)}, bf16[2,128,512]{2,1,0:T(8,128)(2,1)S(1)}, bf16[2,128,512]{2,1,0:T(8,128)(2,1)S(1)}, bf16[2,128,512]{2,1,0:T...) custom-call(s32[1]{0:T(128)} %bitcast.me_ref.refs_0_, ...), custom_call_target="tpu_custom_call" | custom-call | flops 4294967296 | bytes 8388608 | tf_op jit(solution)/shard_map/left/pallas_call | solution.py:122
  83.3 4.5 %collective-permute-done.11.refs_6_ = bf16[2,128,512]{2,1,0:T(8,128)(2,1)S(1)} collective-permute-done((bf16[2,128,512]{2,1,0:T(8,128)(2,1)S(1)}, bf16[2,128,512]{2,1,0:T(8,128)(2,1)S(1)}, u32[]{:S(2)}, u32[]{:S(2)}) %collective-permute-start.11) | collective-permute-done | bytes 262176 | tf_op jit(solution)/shard_map/ppermute | solution.py:306
  87.8 2.1 collective-permute-start.9
  89.9 3.5 %collective-permute-done.12.refs_7_ = bf16[2,128,512]{2,1,0:T(8,128)(2,1)S(1)} collective-permute-done((bf16[2,128,512]{2,1,0:T(8,128)(2,1)S(1)}, bf16[2,128,512]{2,1,0:T(8,128)(2,1)S(1)}, u32[]{:S(2)}, u32[]{:S(2)}) %collective-permute-start.12) | collective-permute-done | bytes 262176 | tf_op jit(solution)/shard_map/ppermute | solution.py:306
  93.4 1.2 collective-permute-start.21
  94.7 6.8 %collective-permute-done.13.refs_8_ = bf16[2,128,512]{2,1,0:T(8,128)(2,1)S(1)} collective-permute-done((bf16[2,128,512]{2,1,0:T(8,128)(2,1)S(1)}, bf16[2,128,512]{2,1,0:T(8,128)(2,1)S(1)}, u32[]{:S(2)}, u32[]{:S(2)}) %collective-permute-start.13) | collective-permute-done | bytes 262176 | tf_op jit(solution)/shard_map/ppermute | solution.py:306
  101.5 3.7 %sine_bitcast_fusion = (f32[4,128,512]{2,1,0:T(8,128)S(1)}, f32[4,128,512]{2,1,0:T(8,128)S(1)}) fusion(f32[128,4,512]{2,1,0:T(4,128)S(1)} %copy-done.6), kind=kLoop, calls=%fused_computation | loop fusion | bytes 3145728 | tf_op jit(solution)/shard_map/sin | solution.py:345
  105.2 2.4 %collective-permute-start.23 = (bf16[2,128,512]{2,1,0:T(8,128)(2,1)S(1)}, bf16[2,128,512]{2,1,0:T(8,128)(2,1)S(1)}, u32[]{:S(2)}, u32[]{:S(2)}) collective-permute-start(bf16[2,128,512]{2,1,0:T(8,128)(2,1)S(1)} %get-tuple-element.73), channel_id=1, source_target_pairs={{0,3},{1,2},{2,1},{3,0},{4,7},{5,6},{6,5},{7,4},{8,11},{9,10},{10,... | collective-permute-start | bytes 786440 | tf_op jit(solution)/shard_map/ppermute | solution.py:306
  107.6 1.4 collective-permute-start.24
  109.0 1.0 collective-permute-start.25
  110.3 2.2 %collective-permute-start.26 = (bf16[2,128,512]{2,1,0:T(8,128)(2,1)S(1)}, bf16[2,128,512]{2,1,0:T(8,128)(2,1)S(1)}, u32[]{:S(2)}, u32[]{:S(2)}) collective-permute-start(bf16[2,128,512]{2,1,0:T(8,128)(2,1)S(1)} %get-tuple-element.76), channel_id=1, source_target_pairs={{0,6},{1,7},{2,4},{3,5},{4,2},{5,3},{6,0},{7,1},{8,14},{9,15},{10,... | collective-permute-start | bytes 786440 | tf_op jit(solution)/shard_map/ppermute | solution.py:306
  112.9 5.8 %left.3 = (bf16[2,128,512]{2,1,0:T(8,128)(2,1)S(1)}, bf16[2,128,512]{2,1,0:T(8,128)(2,1)S(1)}, bf16[2,128,512]{2,1,0:T(8,128)(2,1)S(1)}, bf16[2,128,512]{2,1,0:T...) custom-call(s32[1]{0:T(128)} %bitcast.me_ref.refs_0_, ...), custom_call_target="tpu_custom_call" | custom-call | flops 4294967296 | bytes 8388608 | tf_op jit(solution)/shard_map/left/pallas_call | solution.py:122
  118.9 0.6 collective-permute-start.14
  119.5 1.9 collective-permute-done.24.refs_5_
  121.5 1.3 collective-permute-start.15
  122.7 16.2 %collective-permute-done.25.refs_6_ = bf16[2,128,512]{2,1,0:T(8,128)(2,1)S(1)} collective-permute-done((bf16[2,128,512]{2,1,0:T(8,128)(2,1)S(1)}, bf16[2,128,512]{2,1,0:T(8,128)(2,1)S(1)}, u32[]{:S(2)}, u32[]{:S(2)}) %collective-permute-start.25) | collective-permute-done | bytes 262176 | tf_op jit(solution)/shard_map/ppermute | solution.py:306
  138.9 2.8 %collective-permute-start.16 = (bf16[2,128,512]{2,1,0:T(8,128)(2,1)S(1)}, bf16[2,128,512]{2,1,0:T(8,128)(2,1)S(1)}, u32[]{:S(2)}, u32[]{:S(2)}) collective-permute-start(bf16[2,128,512]{2,1,0:T(8,128)(2,1)S(1)} %get-tuple-element.66), channel_id=1, source_target_pairs={{0,3},{1,2},{2,1},{3,0},{4,7},{5,6},{6,5},{7,4},{8,11},{9,10},{10,... | collective-permute-start | bytes 786440 | tf_op jit(solution)/shard_map/ppermute | solution.py:306
  141.7 5.0 %collective-permute-done.26.refs_7_ = bf16[2,128,512]{2,1,0:T(8,128)(2,1)S(1)} collective-permute-done((bf16[2,128,512]{2,1,0:T(8,128)(2,1)S(1)}, bf16[2,128,512]{2,1,0:T(8,128)(2,1)S(1)}, u32[]{:S(2)}, u32[]{:S(2)}) %collective-permute-start.26) | collective-permute-done | bytes 262176 | tf_op jit(solution)/shard_map/ppermute | solution.py:306
  146.8 8.9 %collective-permute-done.27.refs_8_ = bf16[2,128,512]{2,1,0:T(8,128)(2,1)S(1)} collective-permute-done((bf16[2,128,512]{2,1,0:T(8,128)(2,1)S(1)}, bf16[2,128,512]{2,1,0:T(8,128)(2,1)S(1)}, u32[]{:S(2)}, u32[]{:S(2)}) %collective-permute-start.27) | collective-permute-done | bytes 262176 | tf_op jit(solution)/shard_map/ppermute | solution.py:306
  155.7 5.0 %phase.1 = (bf16[2,1,128,512]{3,2,1,0:T(8,128)(2,1)}, bf16[2,1,128,512]{3,2,1,0:T(8,128)(2,1)}, bf16[2,1,128,512]{3,2,1,0:T(8,128)(2,1)}, bf16[2,1,128,512]{3,2,...) custom-call(s32[2]{0:T(128)S(1)} %pad_add_fusion.me_ref, ...), custom_call_target="tpu_custom_call" | custom-call | flops 2147483648 | bytes 4194304 | tf_op jit(solution)/shard_map/phase/pallas_call | solution.py:193
  160.8 0.7 copy-done.4
  161.5 1.4 collective-permute-start.19
  162.9 0.7 collective-permute-start.20
  163.7 21.0 %collective-permute-start.28 = (bf16[2,1,128,512]{3,2,1,0:T(8,128)(2,1)}, bf16[2,1,128,512]{3,2,1,0:T(8,128)(2,1)}, u32[]{:S(2)}, u32[]{:S(2)}) collective-permute-start(bf16[2,1,128,512]{3,2,1,0:T(8,128)(2,1)} %get-tuple-element.79), channel_id=1, source_target_pairs={{8,16},{16,8},{9,17},{17,9},{10,18},{18,10},{11,19},{19,11},{12,20... | collective-permute-start | bytes 786440 | tf_op jit(solution)/shard_map/ppermute | solution.py:313
  184.8 1.9 collective-permute-start.29
  186.8 0.7 copy-done.11
  187.4 8.4 %collective-permute-start.30 = (bf16[2,1,128,512]{3,2,1,0:T(8,128)(2,1)}, bf16[2,1,128,512]{3,2,1,0:T(8,128)(2,1)}, u32[]{:S(2)}, u32[]{:S(2)}) collective-permute-start(bf16[2,1,128,512]{3,2,1,0:T(8,128)(2,1)} %get-tuple-element.81), channel_id=1, source_target_pairs={{8,16},{16,8},{9,17},{17,9},{10,18},{18,10},{11,19},{19,11},{12,20... | collective-permute-start | bytes 786440 | tf_op jit(solution)/shard_map/ppermute | solution.py:313
  195.9 5.6 %collective-permute-start.31 = (bf16[2,1,128,512]{3,2,1,0:T(8,128)(2,1)}, bf16[2,1,128,512]{3,2,1,0:T(8,128)(2,1)}, u32[]{:S(2)}, u32[]{:S(2)}) collective-permute-start(bf16[2,1,128,512]{3,2,1,0:T(8,128)(2,1)} %get-tuple-element.82), channel_id=1, source_target_pairs={{8,16},{16,8},{9,17},{17,9},{10,18},{18,10},{11,19},{19,11},{12,20... | collective-permute-start | bytes 786440 | tf_op jit(solution)/shard_map/ppermute | solution.py:313
  202.9 2.9 %collective-permute-done.31.refs_12_ = bf16[2,1,128,512]{3,2,1,0:T(8,128)(2,1)} collective-permute-done((bf16[2,1,128,512]{3,2,1,0:T(8,128)(2,1)}, bf16[2,1,128,512]{3,2,1,0:T(8,128)(2,1)}, u32[]{:S(2)}, u32[]{:S(2)}) %collective-permute-start.31) | collective-permute-done | bytes 262176 | tf_op jit(solution)/shard_map/ppermute | solution.py:313
  205.8 9.0 %mix.1 = bf16[128,2,4,16,128]{4,3,2,1,0:T(8,128)(2,1)} custom-call(s32[2]{0:T(128)S(1)} %pad_add_fusion.me_ref, f32[4,4]{1,0:T(4,128)S(1)} %get-tuple-element.90.up_ref, f32[4,4]{1,0:T(4,128)S(1)} %get-tuple-element.89.down_ref, bf16[1024,512]{1,0:T(8,128)(2,1)S(1)} %bitcast.27, f32[4,128,512]{2,1,0:T(8,128)S(1)} %get-tuple-element.88.cosine_ref, ...), custom_call_target="tpu_custom_call" | custom-call | flops 2147483648 | bytes 10485760 | tf_op jit(solution)/shard_map/mix/pallas_call | solution.py:278
  (65 shorter events, 3.2 us)
Async XLA Ops:
  5.4 7.4 %collective-permute-start = (bf16[2,128,512]{2,1,0:T(8,128)(2,1)}, bf16[2,128,512]{2,1,0:T(8,128)(2,1)S(1)}, u32[]{:S(2)}, u32[]{:S(2)}) collective-permute-start(bf16[2,128,512]{2,1,0:T(8,128)(2,1)} %get-tuple-element.48), channel_id=1, source_target_pairs={{0,1},{1,0},{2,3},{3,2},{4,5},{5,4},{6,7},{7,6},{8,9},{9,8},{10,11... | collective-permute-start | bytes 786440 | tf_op jit(solution)/shard_map/ppermute | solution.py:306
  6.7 15.0 %collective-permute-start.1 = (bf16[2,128,512]{2,1,0:T(8,128)(2,1)}, bf16[2,128,512]{2,1,0:T(8,128)(2,1)S(1)}, u32[]{:S(2)}, u32[]{:S(2)}) collective-permute-start(bf16[2,128,512]{2,1,0:T(8,128)(2,1)} %get-tuple-element.49), channel_id=1, source_target_pairs={{0,2},{1,3},{2,0},{3,1},{4,6},{5,7},{6,4},{7,5},{8,10},{9,11},{10,... | collective-permute-start | bytes 786440 | tf_op jit(solution)/shard_map/ppermute | solution.py:306
  6.8 26.8 %collective-permute-start.2 = (bf16[2,128,512]{2,1,0:T(8,128)(2,1)}, bf16[2,128,512]{2,1,0:T(8,128)(2,1)S(1)}, u32[]{:S(2)}, u32[]{:S(2)}) collective-permute-start(bf16[2,128,512]{2,1,0:T(8,128)(2,1)} %get-tuple-element.50), channel_id=1, source_target_pairs={{0,3},{1,2},{2,1},{3,0},{4,7},{5,6},{6,5},{7,4},{8,11},{9,10},{10,... | collective-permute-start | bytes 786440 | tf_op jit(solution)/shard_map/ppermute | solution.py:306
  8.1 29.4 %collective-permute-start.3 = (bf16[2,128,512]{2,1,0:T(8,128)(2,1)}, bf16[2,128,512]{2,1,0:T(8,128)(2,1)S(1)}, u32[]{:S(2)}, u32[]{:S(2)}) collective-permute-start(bf16[2,128,512]{2,1,0:T(8,128)(2,1)} %get-tuple-element.51), channel_id=1, source_target_pairs={{0,4},{1,5},{2,6},{3,7},{4,0},{5,1},{6,2},{7,3},{8,12},{9,13},{10,... | collective-permute-start | bytes 786440 | tf_op jit(solution)/shard_map/ppermute | solution.py:306
  10.4 43.7 %collective-permute-start.4 = (bf16[2,128,512]{2,1,0:T(8,128)(2,1)}, bf16[2,128,512]{2,1,0:T(8,128)(2,1)S(1)}, u32[]{:S(2)}, u32[]{:S(2)}) collective-permute-start(bf16[2,128,512]{2,1,0:T(8,128)(2,1)} %get-tuple-element.52), channel_id=1, source_target_pairs={{0,5},{1,4},{2,7},{3,6},{4,1},{5,0},{6,3},{7,2},{8,13},{9,12},{10,... | collective-permute-start | bytes 786440 | tf_op jit(solution)/shard_map/ppermute | solution.py:306
  12.8 49.7 %collective-permute-start.5 = (bf16[2,128,512]{2,1,0:T(8,128)(2,1)}, bf16[2,128,512]{2,1,0:T(8,128)(2,1)S(1)}, u32[]{:S(2)}, u32[]{:S(2)}) collective-permute-start(bf16[2,128,512]{2,1,0:T(8,128)(2,1)} %get-tuple-element.53), channel_id=1, source_target_pairs={{0,6},{1,7},{2,4},{3,5},{4,2},{5,3},{6,0},{7,1},{8,14},{9,15},{10,... | collective-permute-start | bytes 786440 | tf_op jit(solution)/shard_map/ppermute | solution.py:306
  21.7 55.6 %collective-permute-start.6 = (bf16[2,128,512]{2,1,0:T(8,128)(2,1)}, bf16[2,128,512]{2,1,0:T(8,128)(2,1)S(1)}, u32[]{:S(2)}, u32[]{:S(2)}) collective-permute-start(bf16[2,128,512]{2,1,0:T(8,128)(2,1)} %get-tuple-element.54), channel_id=1, source_target_pairs={{0,7},{1,6},{2,5},{3,4},{4,3},{5,2},{6,1},{7,0},{8,15},{9,14},{10,... | collective-permute-start | bytes 786440 | tf_op jit(solution)/shard_map/ppermute | solution.py:306
  21.7 6.5 %copy-start.1 = (bf16[2,512,512]{2,1,0:T(8,128)(2,1)S(1)}, bf16[2,512,512]{2,1,0:T(8,128)(2,1)}, u32[]{:S(2)}) copy-start(bf16[2,512,512]{2,1,0:T(8,128)(2,1)} %param.8) | copy-start | bytes 3145732
  21.7 6.5 %copy-start.5 = (bf16[2,128,512]{2,1,0:T(8,128)(2,1)S(1)}, bf16[2,128,512]{2,1,0:T(8,128)(2,1)}, u32[]{:S(2)}) copy-start(bf16[2,128,512]{2,1,0:T(8,128)(2,1)} %get-tuple-element.46.refs_0_.refs_1_) | copy-start | bytes 786436
  28.2 2.2 %copy-start = (bf16[128,2,4,4,512]{4,3,2,1,0:T(4,128)(2,1)S(1)}, bf16[128,2,4,4,512]{4,3,2,1,0:T(4,128)(2,1)}, u32[]{:S(2)}) copy-start(bf16[128,2,4,4,512]{4,3,2,1,0:T(4,128)(2,1)} %param.6) | copy-start | bytes 12582916
  30.4 47.5 %copy-start.2 = (bf16[2048,1024]{0,1:T(8,128)(2,1)S(1)}, bf16[2048,1024]{0,1:T(8,128)(2,1)}, u32[]{:S(2)}) copy-start(bf16[2048,1024]{0,1:T(8,128)(2,1)} %copy.14) | copy-start | bytes 12582916
  33.7 49.3 %collective-permute-start.10 = (bf16[2,128,512]{2,1,0:T(8,128)(2,1)S(1)}, bf16[2,128,512]{2,1,0:T(8,128)(2,1)S(1)}, u32[]{:S(2)}, u32[]{:S(2)}) collective-permute-start(bf16[2,128,512]{2,1,0:T(8,128)(2,1)S(1)} %get-tuple-element.59), channel_id=1, source_target_pairs={{0,4},{1,5},{2,6},{3,7},{4,0},{5,1},{6,2},{7,3},{8,12},{9,13},{10,... | collective-permute-start | bytes 786440 | tf_op jit(solution)/shard_map/ppermute | solution.py:306
  37.4 50.4 %collective-permute-start.11 = (bf16[2,128,512]{2,1,0:T(8,128)(2,1)S(1)}, bf16[2,128,512]{2,1,0:T(8,128)(2,1)S(1)}, u32[]{:S(2)}, u32[]{:S(2)}) collective-permute-start(bf16[2,128,512]{2,1,0:T(8,128)(2,1)S(1)} %get-tuple-element.60), channel_id=1, source_target_pairs={{0,5},{1,4},{2,7},{3,6},{4,1},{5,0},{6,3},{7,2},{8,13},{9,12},{10,... | collective-permute-start | bytes 786440 | tf_op jit(solution)/shard_map/ppermute | solution.py:306
  54.0 39.4 %collective-permute-start.12 = (bf16[2,128,512]{2,1,0:T(8,128)(2,1)S(1)}, bf16[2,128,512]{2,1,0:T(8,128)(2,1)S(1)}, u32[]{:S(2)}, u32[]{:S(2)}) collective-permute-start(bf16[2,128,512]{2,1,0:T(8,128)(2,1)S(1)} %get-tuple-element.61), channel_id=1, source_target_pairs={{0,6},{1,7},{2,4},{3,5},{4,2},{5,3},{6,0},{7,1},{8,14},{9,15},{10,... | collective-permute-start | bytes 786440 | tf_op jit(solution)/shard_map/ppermute | solution.py:306
  62.5 39.0 %collective-permute-start.13 = (bf16[2,128,512]{2,1,0:T(8,128)(2,1)S(1)}, bf16[2,128,512]{2,1,0:T(8,128)(2,1)S(1)}, u32[]{:S(2)}, u32[]{:S(2)}) collective-permute-start(bf16[2,128,512]{2,1,0:T(8,128)(2,1)S(1)} %get-tuple-element.62), channel_id=1, source_target_pairs={{0,7},{1,6},{2,5},{3,4},{4,3},{5,2},{6,1},{7,0},{8,15},{9,14},{10,... | collective-permute-start | bytes 786440 | tf_op jit(solution)/shard_map/ppermute | solution.py:306
  77.3 27.9 %collective-permute-start.7 = (bf16[2,128,512]{2,1,0:T(8,128)(2,1)S(1)}, bf16[2,128,512]{2,1,0:T(8,128)(2,1)S(1)}, u32[]{:S(2)}, u32[]{:S(2)}) collective-permute-start(bf16[2,128,512]{2,1,0:T(8,128)(2,1)S(1)} %get-tuple-element.56), channel_id=1, source_target_pairs={{0,1},{1,0},{2,3},{3,2},{4,5},{5,4},{6,7},{7,6},{8,9},{9,8},{10,11... | collective-permute-start | bytes 786440 | tf_op jit(solution)/shard_map/ppermute | solution.py:306
  77.9 23.6 %copy-start.6 = (f32[128,4,512]{2,1,0:T(4,128)S(1)}, f32[128,4,512]{2,1,0:T(4,128)}, u32[]{:S(2)}) copy-start(f32[128,4,512]{2,1,0:T(4,128)} %param.9) | copy-start | bytes 3145732
  83.0 24.6 %collective-permute-start.8 = (bf16[2,128,512]{2,1,0:T(8,128)(2,1)S(1)}, bf16[2,128,512]{2,1,0:T(8,128)(2,1)S(1)}, u32[]{:S(2)}, u32[]{:S(2)}) collective-permute-start(bf16[2,128,512]{2,1,0:T(8,128)(2,1)S(1)} %get-tuple-element.57), channel_id=1, source_target_pairs={{0,2},{1,3},{2,0},{3,1},{4,6},{5,7},{6,4},{7,5},{8,10},{9,11},{10,... | collective-permute-start | bytes 786440 | tf_op jit(solution)/shard_map/ppermute | solution.py:306
  87.8 21.2 %collective-permute-start.9 = (bf16[2,128,512]{2,1,0:T(8,128)(2,1)S(1)}, bf16[2,128,512]{2,1,0:T(8,128)(2,1)S(1)}, u32[]{:S(2)}, u32[]{:S(2)}) collective-permute-start(bf16[2,128,512]{2,1,0:T(8,128)(2,1)S(1)} %get-tuple-element.58), channel_id=1, source_target_pairs={{0,3},{1,2},{2,1},{3,0},{4,7},{5,6},{6,5},{7,4},{8,11},{9,10},{10,... | collective-permute-start | bytes 786440 | tf_op jit(solution)/shard_map/ppermute | solution.py:306
  93.4 16.8 %collective-permute-start.21 = (bf16[2,128,512]{2,1,0:T(8,128)(2,1)S(1)}, bf16[2,128,512]{2,1,0:T(8,128)(2,1)S(1)}, u32[]{:S(2)}, u32[]{:S(2)}) collective-permute-start(bf16[2,128,512]{2,1,0:T(8,128)(2,1)S(1)} %get-tuple-element.71), channel_id=1, source_target_pairs={{0,1},{1,0},{2,3},{3,2},{4,5},{5,4},{6,7},{7,6},{8,9},{9,8},{10,11... | collective-permute-start | bytes 786440 | tf_op jit(solution)/shard_map/ppermute | solution.py:306
  101.5 11.0 %collective-permute-start.22 = (bf16[2,128,512]{2,1,0:T(8,128)(2,1)S(1)}, bf16[2,128,512]{2,1,0:T(8,128)(2,1)S(1)}, u32[]{:S(2)}, u32[]{:S(2)}) collective-permute-start(bf16[2,128,512]{2,1,0:T(8,128)(2,1)S(1)} %get-tuple-element.72), channel_id=1, source_target_pairs={{0,2},{1,3},{2,0},{3,1},{4,6},{5,7},{6,4},{7,5},{8,10},{9,11},{10,... | collective-permute-start | bytes 786440 | tf_op jit(solution)/shard_map/ppermute | solution.py:306
  105.2 13.7 %collective-permute-start.23 = (bf16[2,128,512]{2,1,0:T(8,128)(2,1)S(1)}, bf16[2,128,512]{2,1,0:T(8,128)(2,1)S(1)}, u32[]{:S(2)}, u32[]{:S(2)}) collective-permute-start(bf16[2,128,512]{2,1,0:T(8,128)(2,1)S(1)} %get-tuple-element.73), channel_id=1, source_target_pairs={{0,3},{1,2},{2,1},{3,0},{4,7},{5,6},{6,5},{7,4},{8,11},{9,10},{10,... | collective-permute-start | bytes 786440 | tf_op jit(solution)/shard_map/ppermute | solution.py:306
  107.6 13.9 %collective-permute-start.24 = (bf16[2,128,512]{2,1,0:T(8,128)(2,1)S(1)}, bf16[2,128,512]{2,1,0:T(8,128)(2,1)S(1)}, u32[]{:S(2)}, u32[]{:S(2)}) collective-permute-start(bf16[2,128,512]{2,1,0:T(8,128)(2,1)S(1)} %get-tuple-element.74), channel_id=1, source_target_pairs={{0,4},{1,5},{2,6},{3,7},{4,0},{5,1},{6,2},{7,3},{8,12},{9,13},{10,... | collective-permute-start | bytes 786440 | tf_op jit(solution)/shard_map/ppermute | solution.py:306
  109.0 29.9 %collective-permute-start.25 = (bf16[2,128,512]{2,1,0:T(8,128)(2,1)S(1)}, bf16[2,128,512]{2,1,0:T(8,128)(2,1)S(1)}, u32[]{:S(2)}, u32[]{:S(2)}) collective-permute-start(bf16[2,128,512]{2,1,0:T(8,128)(2,1)S(1)} %get-tuple-element.75), channel_id=1, source_target_pairs={{0,5},{1,4},{2,7},{3,6},{4,1},{5,0},{6,3},{7,2},{8,13},{9,12},{10,... | collective-permute-start | bytes 786440 | tf_op jit(solution)/shard_map/ppermute | solution.py:306
  110.3 36.5 %collective-permute-start.26 = (bf16[2,128,512]{2,1,0:T(8,128)(2,1)S(1)}, bf16[2,128,512]{2,1,0:T(8,128)(2,1)S(1)}, u32[]{:S(2)}, u32[]{:S(2)}) collective-permute-start(bf16[2,128,512]{2,1,0:T(8,128)(2,1)S(1)} %get-tuple-element.76), channel_id=1, source_target_pairs={{0,6},{1,7},{2,4},{3,5},{4,2},{5,3},{6,0},{7,1},{8,14},{9,15},{10,... | collective-permute-start | bytes 786440 | tf_op jit(solution)/shard_map/ppermute | solution.py:306
  112.4 43.2 %collective-permute-start.27 = (bf16[2,128,512]{2,1,0:T(8,128)(2,1)S(1)}, bf16[2,128,512]{2,1,0:T(8,128)(2,1)S(1)}, u32[]{:S(2)}, u32[]{:S(2)}) collective-permute-start(bf16[2,128,512]{2,1,0:T(8,128)(2,1)S(1)} %get-tuple-element.77), channel_id=1, source_target_pairs={{0,7},{1,6},{2,5},{3,4},{4,3},{5,2},{6,1},{7,0},{8,15},{9,14},{10,... | collective-permute-start | bytes 786440 | tf_op jit(solution)/shard_map/ppermute | solution.py:306
  118.7 77.1 %copy-start.12 = (f32[16,4]{0,1:T(4,128)S(1)}, f32[16,4]{0,1:T(4,128)}, u32[]{:S(2)}) copy-start(f32[16,4]{0,1:T(4,128)} %param.10) | copy-start | bytes 772
  118.7 87.1 %copy-start.3 = (f32[128,512]{1,0:T(8,128)S(1)}, f32[128,512]{1,0:T(8,128)}, u32[]{:S(2)}) copy-start(f32[128,512]{1,0:T(8,128)} %weight_ref.1) | copy-start | bytes 786436
  118.9 42.6 %collective-permute-start.14 = (bf16[2,128,512]{2,1,0:T(8,128)(2,1)S(1)}, bf16[2,128,512]{2,1,0:T(8,128)(2,1)S(1)}, u32[]{:S(2)}, u32[]{:S(2)}) collective-permute-start(bf16[2,128,512]{2,1,0:T(8,128)(2,1)S(1)} %get-tuple-element.64), channel_id=1, source_target_pairs={{0,1},{1,0},{2,3},{3,2},{4,5},{5,4},{6,7},{7,6},{8,9},{9,8},{10,11... | collective-permute-start | bytes 786440 | tf_op jit(solution)/shard_map/ppermute | solution.py:306
  121.5 41.5 %collective-permute-start.15 = (bf16[2,128,512]{2,1,0:T(8,128)(2,1)S(1)}, bf16[2,128,512]{2,1,0:T(8,128)(2,1)S(1)}, u32[]{:S(2)}, u32[]{:S(2)}) collective-permute-start(bf16[2,128,512]{2,1,0:T(8,128)(2,1)S(1)} %get-tuple-element.65), channel_id=1, source_target_pairs={{0,2},{1,3},{2,0},{3,1},{4,6},{5,7},{6,4},{7,5},{8,10},{9,11},{10,... | collective-permute-start | bytes 786440 | tf_op jit(solution)/shard_map/ppermute | solution.py:306
  138.9 24.7 %collective-permute-start.16 = (bf16[2,128,512]{2,1,0:T(8,128)(2,1)S(1)}, bf16[2,128,512]{2,1,0:T(8,128)(2,1)S(1)}, u32[]{:S(2)}, u32[]{:S(2)}) collective-permute-start(bf16[2,128,512]{2,1,0:T(8,128)(2,1)S(1)} %get-tuple-element.66), channel_id=1, source_target_pairs={{0,3},{1,2},{2,1},{3,0},{4,7},{5,6},{6,5},{7,4},{8,11},{9,10},{10,... | collective-permute-start | bytes 786440 | tf_op jit(solution)/shard_map/ppermute | solution.py:306
  146.8 38.0 %collective-permute-start.17 = (bf16[2,128,512]{2,1,0:T(8,128)(2,1)S(1)}, bf16[2,128,512]{2,1,0:T(8,128)(2,1)S(1)}, u32[]{:S(2)}, u32[]{:S(2)}) collective-permute-start(bf16[2,128,512]{2,1,0:T(8,128)(2,1)S(1)} %get-tuple-element.67), channel_id=1, source_target_pairs={{0,4},{1,5},{2,6},{3,7},{4,0},{5,1},{6,2},{7,3},{8,12},{9,13},{10,... | collective-permute-start | bytes 786440 | tf_op jit(solution)/shard_map/ppermute | solution.py:306
  155.7 31.0 %collective-permute-start.18 = (bf16[2,128,512]{2,1,0:T(8,128)(2,1)S(1)}, bf16[2,128,512]{2,1,0:T(8,128)(2,1)S(1)}, u32[]{:S(2)}, u32[]{:S(2)}) collective-permute-start(bf16[2,128,512]{2,1,0:T(8,128)(2,1)S(1)} %get-tuple-element.68), channel_id=1, source_target_pairs={{0,5},{1,4},{2,7},{3,6},{4,1},{5,0},{6,3},{7,2},{8,13},{9,12},{10,... | collective-permute-start | bytes 786440 | tf_op jit(solution)/shard_map/ppermute | solution.py:306
  160.8 0.7 copy-start.4
  161.5 25.2 %copy-start.7 = (bf16[2,128,512]{2,1,0:T(8,128)(2,1)}, bf16[2,128,512]{2,1,0:T(8,128)(2,1)S(1)}, u32[]{:S(2)}) copy-start(bf16[2,128,512]{2,1,0:T(8,128)(2,1)S(1)} %collective-permute-done.14.refs_1_) | copy-start | bytes 786436
  161.5 34.4 %collective-permute-start.19 = (bf16[2,128,512]{2,1,0:T(8,128)(2,1)}, bf16[2,128,512]{2,1,0:T(8,128)(2,1)}, u32[]{:S(2)}, u32[]{:S(2)}) collective-permute-start(bf16[2,128,512]{2,1,0:T(8,128)(2,1)} %get-tuple-element.69), channel_id=1, source_target_pairs={{0,6},{1,7},{2,4},{3,5},{4,2},{5,3},{6,0},{7,1},{8,14},{9,15},{10,... | collective-permute-start | bytes 786440 | tf_op jit(solution)/shard_map/ppermute | solution.py:306
  162.9 23.8 %copy-start.8 = (bf16[2,128,512]{2,1,0:T(8,128)(2,1)}, bf16[2,128,512]{2,1,0:T(8,128)(2,1)S(1)}, u32[]{:S(2)}) copy-start(bf16[2,128,512]{2,1,0:T(8,128)(2,1)S(1)} %collective-permute-done.15.refs_2_) | copy-start | bytes 786436
  162.9 38.5 %collective-permute-start.20 = (bf16[2,128,512]{2,1,0:T(8,128)(2,1)}, bf16[2,128,512]{2,1,0:T(8,128)(2,1)}, u32[]{:S(2)}, u32[]{:S(2)}) collective-permute-start(bf16[2,128,512]{2,1,0:T(8,128)(2,1)} %get-tuple-element.70), channel_id=1, source_target_pairs={{0,7},{1,6},{2,5},{3,4},{4,3},{5,2},{6,1},{7,0},{8,15},{9,14},{10,... | collective-permute-start | bytes 786440 | tf_op jit(solution)/shard_map/ppermute | solution.py:306
  163.7 23.0 %copy-start.9 = (bf16[2,128,512]{2,1,0:T(8,128)(2,1)}, bf16[2,128,512]{2,1,0:T(8,128)(2,1)S(1)}, u32[]{:S(2)}) copy-start(bf16[2,128,512]{2,1,0:T(8,128)(2,1)S(1)} %collective-permute-done.16.refs_3_) | copy-start | bytes 786436
  163.7 38.1 %collective-permute-start.28 = (bf16[2,1,128,512]{3,2,1,0:T(8,128)(2,1)}, bf16[2,1,128,512]{3,2,1,0:T(8,128)(2,1)}, u32[]{:S(2)}, u32[]{:S(2)}) collective-permute-start(bf16[2,1,128,512]{3,2,1,0:T(8,128)(2,1)} %get-tuple-element.79), channel_id=1, source_target_pairs={{8,16},{16,8},{9,17},{17,9},{10,18},{18,10},{11,19},{19,11},{12,20... | collective-permute-start | bytes 786440 | tf_op jit(solution)/shard_map/ppermute | solution.py:313
  184.8 2.0 copy-start.10
  184.8 17.3 %collective-permute-start.29 = (bf16[2,1,128,512]{3,2,1,0:T(8,128)(2,1)}, bf16[2,1,128,512]{3,2,1,0:T(8,128)(2,1)}, u32[]{:S(2)}, u32[]{:S(2)}) collective-permute-start(bf16[2,1,128,512]{3,2,1,0:T(8,128)(2,1)} %get-tuple-element.80), channel_id=1, source_target_pairs={{8,16},{16,8},{9,17},{17,9},{10,18},{18,10},{11,19},{19,11},{12,20... | collective-permute-start | bytes 786440 | tf_op jit(solution)/shard_map/ppermute | solution.py:313
  187.4 14.9 %collective-permute-start.30 = (bf16[2,1,128,512]{3,2,1,0:T(8,128)(2,1)}, bf16[2,1,128,512]{3,2,1,0:T(8,128)(2,1)}, u32[]{:S(2)}, u32[]{:S(2)}) collective-permute-start(bf16[2,1,128,512]{3,2,1,0:T(8,128)(2,1)} %get-tuple-element.81), channel_id=1, source_target_pairs={{8,16},{16,8},{9,17},{17,9},{10,18},{18,10},{11,19},{19,11},{12,20... | collective-permute-start | bytes 786440 | tf_op jit(solution)/shard_map/ppermute | solution.py:313
  195.9 9.9 %collective-permute-start.31 = (bf16[2,1,128,512]{3,2,1,0:T(8,128)(2,1)}, bf16[2,1,128,512]{3,2,1,0:T(8,128)(2,1)}, u32[]{:S(2)}, u32[]{:S(2)}) collective-permute-start(bf16[2,1,128,512]{3,2,1,0:T(8,128)(2,1)} %get-tuple-element.82), channel_id=1, source_target_pairs={{8,16},{16,8},{9,17},{17,9},{10,18},{18,10},{11,19},{19,11},{12,20... | collective-permute-start | bytes 786440 | tf_op jit(solution)/shard_map/ppermute | solution.py:313
  201.5 4.3 %collective-permute-start.32 = (bf16[2,1,128,512]{3,2,1,0:T(8,128)(2,1)}, bf16[2,1,128,512]{3,2,1,0:T(8,128)(2,1)}, u32[]{:S(2)}, u32[]{:S(2)}) collective-permute-start(bf16[2,1,128,512]{3,2,1,0:T(8,128)(2,1)} %get-tuple-element.83), channel_id=1, source_target_pairs={{0,8},{16,24},{8,0},{24,16},{1,9},{17,25},{9,1},{25,17},{2,10},{18... | collective-permute-start | bytes 786440 | tf_op jit(solution)/shard_map/ppermute | solution.py:313
  201.8 4.1 %collective-permute-start.33 = (bf16[2,1,128,512]{3,2,1,0:T(8,128)(2,1)}, bf16[2,1,128,512]{3,2,1,0:T(8,128)(2,1)}, u32[]{:S(2)}, u32[]{:S(2)}) collective-permute-start(bf16[2,1,128,512]{3,2,1,0:T(8,128)(2,1)} %get-tuple-element.84), channel_id=1, source_target_pairs={{0,8},{16,24},{8,0},{24,16},{1,9},{17,25},{9,1},{25,17},{2,10},{18... | collective-permute-start | bytes 786440 | tf_op jit(solution)/shard_map/ppermute | solution.py:313
  202.0 3.8 %collective-permute-start.34 = (bf16[2,1,128,512]{3,2,1,0:T(8,128)(2,1)}, bf16[2,1,128,512]{3,2,1,0:T(8,128)(2,1)}, u32[]{:S(2)}, u32[]{:S(2)}) collective-permute-start(bf16[2,1,128,512]{3,2,1,0:T(8,128)(2,1)} %get-tuple-element.85), channel_id=1, source_target_pairs={{0,8},{16,24},{8,0},{24,16},{1,9},{17,25},{9,1},{25,17},{2,10},{18... | collective-permute-start | bytes 786440 | tf_op jit(solution)/shard_map/ppermute | solution.py:313
  202.3 3.5 %collective-permute-start.35 = (bf16[2,1,128,512]{3,2,1,0:T(8,128)(2,1)}, bf16[2,1,128,512]{3,2,1,0:T(8,128)(2,1)}, u32[]{:S(2)}, u32[]{:S(2)}) collective-permute-start(bf16[2,1,128,512]{3,2,1,0:T(8,128)(2,1)} %get-tuple-element.86), channel_id=1, source_target_pairs={{0,8},{16,24},{8,0},{24,16},{1,9},{17,25},{9,1},{25,17},{2,10},{18... | collective-permute-start | bytes 786440 | tf_op jit(solution)/shard_map/ppermute | solution.py:313
  (1 other events, 0.7 us)

commit v16 on v15

--- a/solution.py
+++ b/solution.py
@@ -69,7 +69,7 @@
 def right_call(after, me, second, view, chosen, ranks, states, piece, limit):
     rows, _, _, group, _ = view.shape
     width = second.shape[1]
-    block = rows // 2
+    block = rows // 4
     kinds = len(chosen)
     return pl.pallas_call(
         functools.partial(right_kernel, len(after), ranks, states),

time: 217 us -> 218 us (level)
  no operation moved by 1% of the time
where the time goes in v16:
time: 218 us; the launch traced here: 215 us
  waiting for transfers between devices  85.7 us (39%)
  starting transfers between devices  81 us (37%)
  Pallas kernels  34.1 us (16%)
  local copies, waits for them, and re-layouts  14.2 us (7%)
    ppermute x28, waiting for transfers between devices, exchanged(): result[s] = lax.ppermute(slabs[s], axis, [(i, i ^ s) for i in range(count)])  82.7 us
    ppermute x28, starting transfers between devices, exchanged(): result[s] = lax.ppermute(slabs[s], axis, [(i, i ^ s) for i in range(count)])  42.9 us
    ppermute x8, starting transfers between devices, paired(): return lax.ppermute(edge, axis, pairs + [(j, i) for i, j in pairs])  38.1 us
    pallas_call x2, Pallas kernels, left_call(): pl.pallas_call(functools.partial(left_kernel, len(after), order), grid=(k...  10.8 us
    pallas_call x2, Pallas kernels, right_call(): pl.pallas_call(functools.partial(right_kernel, len(after), ranks, states)...  9.37 us
    pallas_call x1, Pallas kernels, mix_call(): pl.pallas_call(functools.partial(mix_kernel, tuple(chosen), order), grid=...  8.97 us
    reshape x1, local copies, waits for them, and re-layouts, per_device(): first = first_propagator.reshape(2 * whole, whole).T  6.53 us
    pallas_call x1, Pallas kernels, phase_call(): pl.pallas_call(functools.partial(phase_kernel, len(after), ranks), grid=(...  4.9 us
  transfers between devices with their start and end apart: 36, of which 15 were waited for; matrix products, arithmetic and copies ran while one was open for 5% of the time, Pallas kernels for 9%

profile of v16, /device:TPU:9, one launch (start us, length us, event | category | flops | bytes accessed | tf_op | source)
XLA Modules:
  0.0 215.4 jit_solution(8066503183870214517)
XLA Ops:
  0.0 5.8 %right.2 = (bf16[2,128,512]{2,1,0:T(8,128)(2,1)}, bf16[2,128,512]{2,1,0:T(8,128)(2,1)}, bf16[2,128,512]{2,1,0:T(8,128)(2,1)}, bf16[2,128,512]{2,1,0:T(8,128)(2,1...) custom-call(s32[1]{0:T(128)} %bitcast.me_ref.refs_0_, ...), custom_call_target="tpu_custom_call" | custom-call | flops 2147483648 | bytes 4194304 | tf_op jit(solution)/shard_map/right/pallas_call | solution.py:74
  5.8 1.3 collective-permute-start
  7.3 1.2 collective-permute-start.2
  8.5 2.3 %collective-permute-start.3 = (bf16[2,128,512]{2,1,0:T(8,128)(2,1)}, bf16[2,128,512]{2,1,0:T(8,128)(2,1)S(1)}, u32[]{:S(2)}, u32[]{:S(2)}) collective-permute-start(bf16[2,128,512]{2,1,0:T(8,128)(2,1)} %get-tuple-element.51), channel_id=1, source_target_pairs={{0,4},{1,5},{2,6},{3,7},{4,0},{5,1},{6,2},{7,3},{8,12},{9,13},{10,... | collective-permute-start | bytes 786440 | tf_op jit(solution)/shard_map/ppermute | solution.py:306
  10.8 1.0 collective-permute-start.4
  11.8 1.4 collective-permute-done.refs_2_
  13.2 1.3 collective-permute-start.5
  14.5 7.6 %collective-permute-done.1.refs_3_ = bf16[2,128,512]{2,1,0:T(8,128)(2,1)S(1)} collective-permute-done((bf16[2,128,512]{2,1,0:T(8,128)(2,1)}, bf16[2,128,512]{2,1,0:T(8,128)(2,1)S(1)}, u32[]{:S(2)}, u32[]{:S(2)}) %collective-permute-start.1) | collective-permute-done | bytes 262176 | tf_op jit(solution)/shard_map/ppermute | solution.py:306
  22.1 6.5 %copy.14 = bf16[2048,1024]{0,1:T(8,128)(2,1)} copy(bf16[2048,1024]{1,0:T(8,128)(2,1)} %bitcast.30) | data formatting | bytes 8388608 | tf_op jit(solution)/shard_map/reshape | solution.py:325
  28.7 2.2 %copy-done = bf16[128,2,4,4,512]{4,3,2,1,0:T(4,128)(2,1)S(1)} copy-done((bf16[128,2,4,4,512]{4,3,2,1,0:T(4,128)(2,1)S(1)}, bf16[128,2,4,4,512]{4,3,2,1,0:T(4,128)(2,1)}, u32[]{:S(2)}) %copy-start) | copy-done | bytes 4194328
  30.8 3.6 %right.3 = (bf16[2,128,512]{2,1,0:T(8,128)(2,1)S(1)}, bf16[2,128,512]{2,1,0:T(8,128)(2,1)S(1)}, bf16[2,128,512]{2,1,0:T(8,128)(2,1)S(1)}, bf16[2,128,512]{2,1,0:...) custom-call(s32[1]{0:T(128)} %bitcast.me_ref.refs_0_, ...), custom_call_target="tpu_custom_call" | custom-call | flops 2147483648 | bytes 4194304 | tf_op jit(solution)/shard_map/right/pallas_call | solution.py:74
  34.4 3.8 %collective-permute-start.10 = (bf16[2,128,512]{2,1,0:T(8,128)(2,1)S(1)}, bf16[2,128,512]{2,1,0:T(8,128)(2,1)S(1)}, u32[]{:S(2)}, u32[]{:S(2)}) collective-permute-start(bf16[2,128,512]{2,1,0:T(8,128)(2,1)S(1)} %get-tuple-element.59), channel_id=1, source_target_pairs={{0,4},{1,5},{2,6},{3,7},{4,0},{5,1},{6,2},{7,3},{8,12},{9,13},{10,... | collective-permute-start | bytes 786440 | tf_op jit(solution)/shard_map/ppermute | solution.py:306
  38.2 1.7 collective-permute-start.11
  39.9 14.6 %collective-permute-done.4.refs_6_ = bf16[2,128,512]{2,1,0:T(8,128)(2,1)S(1)} collective-permute-done((bf16[2,128,512]{2,1,0:T(8,128)(2,1)}, bf16[2,128,512]{2,1,0:T(8,128)(2,1)S(1)}, u32[]{:S(2)}, u32[]{:S(2)}) %collective-permute-start.4) | collective-permute-done | bytes 262176 | tf_op jit(solution)/shard_map/ppermute | solution.py:306
  54.5 8.5 %collective-permute-done.5.refs_7_ = bf16[2,128,512]{2,1,0:T(8,128)(2,1)S(1)} collective-permute-done((bf16[2,128,512]{2,1,0:T(8,128)(2,1)}, bf16[2,128,512]{2,1,0:T(8,128)(2,1)S(1)}, u32[]{:S(2)}, u32[]{:S(2)}) %collective-permute-start.5) | collective-permute-done | bytes 262176 | tf_op jit(solution)/shard_map/ppermute | solution.py:306
  63.0 11.6 %collective-permute-start.13 = (bf16[2,128,512]{2,1,0:T(8,128)(2,1)S(1)}, bf16[2,128,512]{2,1,0:T(8,128)(2,1)S(1)}, u32[]{:S(2)}, u32[]{:S(2)}) collective-permute-start(bf16[2,128,512]{2,1,0:T(8,128)(2,1)S(1)} %get-tuple-element.62), channel_id=1, source_target_pairs={{0,7},{1,6},{2,5},{3,4},{4,3},{5,2},{6,1},{7,0},{8,15},{9,14},{10,... | collective-permute-start | bytes 786440 | tf_op jit(solution)/shard_map/ppermute | solution.py:306
  74.6 3.2 %collective-permute-done.6.refs_8_ = bf16[2,128,512]{2,1,0:T(8,128)(2,1)S(1)} collective-permute-done((bf16[2,128,512]{2,1,0:T(8,128)(2,1)}, bf16[2,128,512]{2,1,0:T(8,128)(2,1)S(1)}, u32[]{:S(2)}, u32[]{:S(2)}) %collective-permute-start.6) | collective-permute-done | bytes 262176 | tf_op jit(solution)/shard_map/ppermute | solution.py:306
  77.7 0.6 collective-permute-start.7
  78.4 5.1 %left.2 = (bf16[2,128,512]{2,1,0:T(8,128)(2,1)S(1)}, bf16[2,128,512]{2,1,0:T(8,128)(2,1)S(1)}, bf16[2,128,512]{2,1,0:T(8,128)(2,1)S(1)}, bf16[2,128,512]{2,1,0:T...) custom-call(s32[1]{0:T(128)} %bitcast.me_ref.refs_0_, ...), custom_call_target="tpu_custom_call" | custom-call | flops 4294967296 | bytes 8388608 | tf_op jit(solution)/shard_map/left/pallas_call | solution.py:122
  83.8 4.5 %collective-permute-done.11.refs_6_ = bf16[2,128,512]{2,1,0:T(8,128)(2,1)S(1)} collective-permute-done((bf16[2,128,512]{2,1,0:T(8,128)(2,1)S(1)}, bf16[2,128,512]{2,1,0:T(8,128)(2,1)S(1)}, u32[]{:S(2)}, u32[]{:S(2)}) %collective-permute-start.11) | collective-permute-done | bytes 262176 | tf_op jit(solution)/shard_map/ppermute | solution.py:306
  88.3 2.1 collective-permute-start.9
  90.4 3.5 %collective-permute-done.12.refs_7_ = bf16[2,128,512]{2,1,0:T(8,128)(2,1)S(1)} collective-permute-done((bf16[2,128,512]{2,1,0:T(8,128)(2,1)S(1)}, bf16[2,128,512]{2,1,0:T(8,128)(2,1)S(1)}, u32[]{:S(2)}, u32[]{:S(2)}) %collective-permute-start.12) | collective-permute-done | bytes 262176 | tf_op jit(solution)/shard_map/ppermute | solution.py:306
  93.9 1.2 collective-permute-start.21
  95.2 6.8 %collective-permute-done.13.refs_8_ = bf16[2,128,512]{2,1,0:T(8,128)(2,1)S(1)} collective-permute-done((bf16[2,128,512]{2,1,0:T(8,128)(2,1)S(1)}, bf16[2,128,512]{2,1,0:T(8,128)(2,1)S(1)}, u32[]{:S(2)}, u32[]{:S(2)}) %collective-permute-start.13) | collective-permute-done | bytes 262176 | tf_op jit(solution)/shard_map/ppermute | solution.py:306
  101.9 3.7 %sine_bitcast_fusion = (f32[4,128,512]{2,1,0:T(8,128)S(1)}, f32[4,128,512]{2,1,0:T(8,128)S(1)}) fusion(f32[128,4,512]{2,1,0:T(4,128)S(1)} %copy-done.6), kind=kLoop, calls=%fused_computation | loop fusion | bytes 3145728 | tf_op jit(solution)/shard_map/sin | solution.py:345
  105.6 2.4 %collective-permute-start.23 = (bf16[2,128,512]{2,1,0:T(8,128)(2,1)S(1)}, bf16[2,128,512]{2,1,0:T(8,128)(2,1)S(1)}, u32[]{:S(2)}, u32[]{:S(2)}) collective-permute-start(bf16[2,128,512]{2,1,0:T(8,128)(2,1)S(1)} %get-tuple-element.73), channel_id=1, source_target_pairs={{0,3},{1,2},{2,1},{3,0},{4,7},{5,6},{6,5},{7,4},{8,11},{9,10},{10,... | collective-permute-start | bytes 786440 | tf_op jit(solution)/shard_map/ppermute | solution.py:306
  108.1 1.4 collective-permute-start.24
  109.5 1.0 collective-permute-start.25
  110.8 2.2 %collective-permute-start.26 = (bf16[2,128,512]{2,1,0:T(8,128)(2,1)S(1)}, bf16[2,128,512]{2,1,0:T(8,128)(2,1)S(1)}, u32[]{:S(2)}, u32[]{:S(2)}) collective-permute-start(bf16[2,128,512]{2,1,0:T(8,128)(2,1)S(1)} %get-tuple-element.76), channel_id=1, source_target_pairs={{0,6},{1,7},{2,4},{3,5},{4,2},{5,3},{6,0},{7,1},{8,14},{9,15},{10,... | collective-permute-start | bytes 786440 | tf_op jit(solution)/shard_map/ppermute | solution.py:306
  113.4 5.8 %left.3 = (bf16[2,128,512]{2,1,0:T(8,128)(2,1)S(1)}, bf16[2,128,512]{2,1,0:T(8,128)(2,1)S(1)}, bf16[2,128,512]{2,1,0:T(8,128)(2,1)S(1)}, bf16[2,128,512]{2,1,0:T...) custom-call(s32[1]{0:T(128)} %bitcast.me_ref.refs_0_, ...), custom_call_target="tpu_custom_call" | custom-call | flops 4294967296 | bytes 8388608 | tf_op jit(solution)/shard_map/left/pallas_call | solution.py:122
  119.3 0.7 collective-permute-start.14
  120.0 1.9 collective-permute-done.24.refs_5_
  122.0 1.2 collective-permute-start.15
  123.1 16.4 %collective-permute-done.25.refs_6_ = bf16[2,128,512]{2,1,0:T(8,128)(2,1)S(1)} collective-permute-done((bf16[2,128,512]{2,1,0:T(8,128)(2,1)S(1)}, bf16[2,128,512]{2,1,0:T(8,128)(2,1)S(1)}, u32[]{:S(2)}, u32[]{:S(2)}) %collective-permute-start.25) | collective-permute-done | bytes 262176 | tf_op jit(solution)/shard_map/ppermute | solution.py:306
  139.5 2.7 %collective-permute-start.16 = (bf16[2,128,512]{2,1,0:T(8,128)(2,1)S(1)}, bf16[2,128,512]{2,1,0:T(8,128)(2,1)S(1)}, u32[]{:S(2)}, u32[]{:S(2)}) collective-permute-start(bf16[2,128,512]{2,1,0:T(8,128)(2,1)S(1)} %get-tuple-element.66), channel_id=1, source_target_pairs={{0,3},{1,2},{2,1},{3,0},{4,7},{5,6},{6,5},{7,4},{8,11},{9,10},{10,... | collective-permute-start | bytes 786440 | tf_op jit(solution)/shard_map/ppermute | solution.py:306
  142.2 5.0 %collective-permute-done.26.refs_7_ = bf16[2,128,512]{2,1,0:T(8,128)(2,1)S(1)} collective-permute-done((bf16[2,128,512]{2,1,0:T(8,128)(2,1)S(1)}, bf16[2,128,512]{2,1,0:T(8,128)(2,1)S(1)}, u32[]{:S(2)}, u32[]{:S(2)}) %collective-permute-start.26) | collective-permute-done | bytes 262176 | tf_op jit(solution)/shard_map/ppermute | solution.py:306
  147.2 8.9 %collective-permute-done.27.refs_8_ = bf16[2,128,512]{2,1,0:T(8,128)(2,1)S(1)} collective-permute-done((bf16[2,128,512]{2,1,0:T(8,128)(2,1)S(1)}, bf16[2,128,512]{2,1,0:T(8,128)(2,1)S(1)}, u32[]{:S(2)}, u32[]{:S(2)}) %collective-permute-start.27) | collective-permute-done | bytes 262176 | tf_op jit(solution)/shard_map/ppermute | solution.py:306
  156.2 4.9 %phase.1 = (bf16[2,1,128,512]{3,2,1,0:T(8,128)(2,1)}, bf16[2,1,128,512]{3,2,1,0:T(8,128)(2,1)}, bf16[2,1,128,512]{3,2,1,0:T(8,128)(2,1)}, bf16[2,1,128,512]{3,2,...) custom-call(s32[2]{0:T(128)S(1)} %pad_add_fusion.me_ref, ...), custom_call_target="tpu_custom_call" | custom-call | flops 2147483648 | bytes 4194304 | tf_op jit(solution)/shard_map/phase/pallas_call | solution.py:193
  161.1 0.7 copy-done.4
  161.8 1.4 collective-permute-start.19
  163.3 0.7 collective-permute-start.20
  164.0 21.9 %collective-permute-start.28 = (bf16[2,1,128,512]{3,2,1,0:T(8,128)(2,1)}, bf16[2,1,128,512]{3,2,1,0:T(8,128)(2,1)}, u32[]{:S(2)}, u32[]{:S(2)}) collective-permute-start(bf16[2,1,128,512]{3,2,1,0:T(8,128)(2,1)} %get-tuple-element.79), channel_id=1, source_target_pairs={{8,16},{16,8},{9,17},{17,9},{10,18},{18,10},{11,19},{19,11},{12,20... | collective-permute-start | bytes 786440 | tf_op jit(solution)/shard_map/ppermute | solution.py:313
  186.0 1.9 collective-permute-start.29
  188.0 0.7 copy-done.11
  188.6 7.6 %collective-permute-start.30 = (bf16[2,1,128,512]{3,2,1,0:T(8,128)(2,1)}, bf16[2,1,128,512]{3,2,1,0:T(8,128)(2,1)}, u32[]{:S(2)}, u32[]{:S(2)}) collective-permute-start(bf16[2,1,128,512]{3,2,1,0:T(8,128)(2,1)} %get-tuple-element.81), channel_id=1, source_target_pairs={{8,16},{16,8},{9,17},{17,9},{10,18},{18,10},{11,19},{19,11},{12,20... | collective-permute-start | bytes 786440 | tf_op jit(solution)/shard_map/ppermute | solution.py:313
  196.3 5.6 %collective-permute-start.31 = (bf16[2,1,128,512]{3,2,1,0:T(8,128)(2,1)}, bf16[2,1,128,512]{3,2,1,0:T(8,128)(2,1)}, u32[]{:S(2)}, u32[]{:S(2)}) collective-permute-start(bf16[2,1,128,512]{3,2,1,0:T(8,128)(2,1)} %get-tuple-element.82), channel_id=1, source_target_pairs={{8,16},{16,8},{9,17},{17,9},{10,18},{18,10},{11,19},{19,11},{12,20... | collective-permute-start | bytes 786440 | tf_op jit(solution)/shard_map/ppermute | solution.py:313
  203.4 2.9 %collective-permute-done.31.refs_12_ = bf16[2,1,128,512]{3,2,1,0:T(8,128)(2,1)} collective-permute-done((bf16[2,1,128,512]{3,2,1,0:T(8,128)(2,1)}, bf16[2,1,128,512]{3,2,1,0:T(8,128)(2,1)}, u32[]{:S(2)}, u32[]{:S(2)}) %collective-permute-start.31) | collective-permute-done | bytes 262176 | tf_op jit(solution)/shard_map/ppermute | solution.py:313
  206.3 9.0 %mix.1 = bf16[128,2,4,16,128]{4,3,2,1,0:T(8,128)(2,1)} custom-call(s32[2]{0:T(128)S(1)} %pad_add_fusion.me_ref, f32[4,4]{1,0:T(4,128)S(1)} %get-tuple-element.90.up_ref, f32[4,4]{1,0:T(4,128)S(1)} %get-tuple-element.89.down_ref, bf16[1024,512]{1,0:T(8,128)(2,1)S(1)} %bitcast.27, f32[4,128,512]{2,1,0:T(8,128)S(1)} %get-tuple-element.88.cosine_ref, ...), custom_call_target="tpu_custom_call" | custom-call | flops 2147483648 | bytes 10485760 | tf_op jit(solution)/shard_map/mix/pallas_call | solution.py:278
  (65 shorter events, 3.2 us)
Async XLA Ops:
  5.8 7.4 %collective-permute-start = (bf16[2,128,512]{2,1,0:T(8,128)(2,1)}, bf16[2,128,512]{2,1,0:T(8,128)(2,1)S(1)}, u32[]{:S(2)}, u32[]{:S(2)}) collective-permute-start(bf16[2,128,512]{2,1,0:T(8,128)(2,1)} %get-tuple-element.48), channel_id=1, source_target_pairs={{0,1},{1,0},{2,3},{3,2},{4,5},{5,4},{6,7},{7,6},{8,9},{9,8},{10,11... | collective-permute-start | bytes 786440 | tf_op jit(solution)/shard_map/ppermute | solution.py:306
  7.1 15.0 %collective-permute-start.1 = (bf16[2,128,512]{2,1,0:T(8,128)(2,1)}, bf16[2,128,512]{2,1,0:T(8,128)(2,1)S(1)}, u32[]{:S(2)}, u32[]{:S(2)}) collective-permute-start(bf16[2,128,512]{2,1,0:T(8,128)(2,1)} %get-tuple-element.49), channel_id=1, source_target_pairs={{0,2},{1,3},{2,0},{3,1},{4,6},{5,7},{6,4},{7,5},{8,10},{9,11},{10,... | collective-permute-start | bytes 786440 | tf_op jit(solution)/shard_map/ppermute | solution.py:306
  7.3 27.2 %collective-permute-start.2 = (bf16[2,128,512]{2,1,0:T(8,128)(2,1)}, bf16[2,128,512]{2,1,0:T(8,128)(2,1)S(1)}, u32[]{:S(2)}, u32[]{:S(2)}) collective-permute-start(bf16[2,128,512]{2,1,0:T(8,128)(2,1)} %get-tuple-element.50), channel_id=1, source_target_pairs={{0,3},{1,2},{2,1},{3,0},{4,7},{5,6},{6,5},{7,4},{8,11},{9,10},{10,... | collective-permute-start | bytes 786440 | tf_op jit(solution)/shard_map/ppermute | solution.py:306
  8.5 29.7 %collective-permute-start.3 = (bf16[2,128,512]{2,1,0:T(8,128)(2,1)}, bf16[2,128,512]{2,1,0:T(8,128)(2,1)S(1)}, u32[]{:S(2)}, u32[]{:S(2)}) collective-permute-start(bf16[2,128,512]{2,1,0:T(8,128)(2,1)} %get-tuple-element.51), channel_id=1, source_target_pairs={{0,4},{1,5},{2,6},{3,7},{4,0},{5,1},{6,2},{7,3},{8,12},{9,13},{10,... | collective-permute-start | bytes 786440 | tf_op jit(solution)/shard_map/ppermute | solution.py:306
  10.8 43.7 %collective-permute-start.4 = (bf16[2,128,512]{2,1,0:T(8,128)(2,1)}, bf16[2,128,512]{2,1,0:T(8,128)(2,1)S(1)}, u32[]{:S(2)}, u32[]{:S(2)}) collective-permute-start(bf16[2,128,512]{2,1,0:T(8,128)(2,1)} %get-tuple-element.52), channel_id=1, source_target_pairs={{0,5},{1,4},{2,7},{3,6},{4,1},{5,0},{6,3},{7,2},{8,13},{9,12},{10,... | collective-permute-start | bytes 786440 | tf_op jit(solution)/shard_map/ppermute | solution.py:306
  13.2 49.7 %collective-permute-start.5 = (bf16[2,128,512]{2,1,0:T(8,128)(2,1)}, bf16[2,128,512]{2,1,0:T(8,128)(2,1)S(1)}, u32[]{:S(2)}, u32[]{:S(2)}) collective-permute-start(bf16[2,128,512]{2,1,0:T(8,128)(2,1)} %get-tuple-element.53), channel_id=1, source_target_pairs={{0,6},{1,7},{2,4},{3,5},{4,2},{5,3},{6,0},{7,1},{8,14},{9,15},{10,... | collective-permute-start | bytes 786440 | tf_op jit(solution)/shard_map/ppermute | solution.py:306
  22.1 55.6 %collective-permute-start.6 = (bf16[2,128,512]{2,1,0:T(8,128)(2,1)}, bf16[2,128,512]{2,1,0:T(8,128)(2,1)S(1)}, u32[]{:S(2)}, u32[]{:S(2)}) collective-permute-start(bf16[2,128,512]{2,1,0:T(8,128)(2,1)} %get-tuple-element.54), channel_id=1, source_target_pairs={{0,7},{1,6},{2,5},{3,4},{4,3},{5,2},{6,1},{7,0},{8,15},{9,14},{10,... | collective-permute-start | bytes 786440 | tf_op jit(solution)/shard_map/ppermute | solution.py:306
  22.1 6.5 %copy-start.1 = (bf16[2,512,512]{2,1,0:T(8,128)(2,1)S(1)}, bf16[2,512,512]{2,1,0:T(8,128)(2,1)}, u32[]{:S(2)}) copy-start(bf16[2,512,512]{2,1,0:T(8,128)(2,1)} %param.8) | copy-start | bytes 3145732
  22.1 6.5 %copy-start.5 = (bf16[2,128,512]{2,1,0:T(8,128)(2,1)S(1)}, bf16[2,128,512]{2,1,0:T(8,128)(2,1)}, u32[]{:S(2)}) copy-start(bf16[2,128,512]{2,1,0:T(8,128)(2,1)} %get-tuple-element.46.refs_0_.refs_1_) | copy-start | bytes 786436
  28.7 2.2 %copy-start = (bf16[128,2,4,4,512]{4,3,2,1,0:T(4,128)(2,1)S(1)}, bf16[128,2,4,4,512]{4,3,2,1,0:T(4,128)(2,1)}, u32[]{:S(2)}) copy-start(bf16[128,2,4,4,512]{4,3,2,1,0:T(4,128)(2,1)} %param.6) | copy-start | bytes 12582916
  30.8 47.5 %copy-start.2 = (bf16[2048,1024]{0,1:T(8,128)(2,1)S(1)}, bf16[2048,1024]{0,1:T(8,128)(2,1)}, u32[]{:S(2)}) copy-start(bf16[2048,1024]{0,1:T(8,128)(2,1)} %copy.14) | copy-start | bytes 12582916
  34.4 49.0 %collective-permute-start.10 = (bf16[2,128,512]{2,1,0:T(8,128)(2,1)S(1)}, bf16[2,128,512]{2,1,0:T(8,128)(2,1)S(1)}, u32[]{:S(2)}, u32[]{:S(2)}) collective-permute-start(bf16[2,128,512]{2,1,0:T(8,128)(2,1)S(1)} %get-tuple-element.59), channel_id=1, source_target_pairs={{0,4},{1,5},{2,6},{3,7},{4,0},{5,1},{6,2},{7,3},{8,12},{9,13},{10,... | collective-permute-start | bytes 786440 | tf_op jit(solution)/shard_map/ppermute | solution.py:306
  38.2 50.1 %collective-permute-start.11 = (bf16[2,128,512]{2,1,0:T(8,128)(2,1)S(1)}, bf16[2,128,512]{2,1,0:T(8,128)(2,1)S(1)}, u32[]{:S(2)}, u32[]{:S(2)}) collective-permute-start(bf16[2,128,512]{2,1,0:T(8,128)(2,1)S(1)} %get-tuple-element.60), channel_id=1, source_target_pairs={{0,5},{1,4},{2,7},{3,6},{4,1},{5,0},{6,3},{7,2},{8,13},{9,12},{10,... | collective-permute-start | bytes 786440 | tf_op jit(solution)/shard_map/ppermute | solution.py:306
  54.5 39.4 %collective-permute-start.12 = (bf16[2,128,512]{2,1,0:T(8,128)(2,1)S(1)}, bf16[2,128,512]{2,1,0:T(8,128)(2,1)S(1)}, u32[]{:S(2)}, u32[]{:S(2)}) collective-permute-start(bf16[2,128,512]{2,1,0:T(8,128)(2,1)S(1)} %get-tuple-element.61), channel_id=1, source_target_pairs={{0,6},{1,7},{2,4},{3,5},{4,2},{5,3},{6,0},{7,1},{8,14},{9,15},{10,... | collective-permute-start | bytes 786440 | tf_op jit(solution)/shard_map/ppermute | solution.py:306
  63.0 39.0 %collective-permute-start.13 = (bf16[2,128,512]{2,1,0:T(8,128)(2,1)S(1)}, bf16[2,128,512]{2,1,0:T(8,128)(2,1)S(1)}, u32[]{:S(2)}, u32[]{:S(2)}) collective-permute-start(bf16[2,128,512]{2,1,0:T(8,128)(2,1)S(1)} %get-tuple-element.62), channel_id=1, source_target_pairs={{0,7},{1,6},{2,5},{3,4},{4,3},{5,2},{6,1},{7,0},{8,15},{9,14},{10,... | collective-permute-start | bytes 786440 | tf_op jit(solution)/shard_map/ppermute | solution.py:306
  77.7 27.9 %collective-permute-start.7 = (bf16[2,128,512]{2,1,0:T(8,128)(2,1)S(1)}, bf16[2,128,512]{2,1,0:T(8,128)(2,1)S(1)}, u32[]{:S(2)}, u32[]{:S(2)}) collective-permute-start(bf16[2,128,512]{2,1,0:T(8,128)(2,1)S(1)} %get-tuple-element.56), channel_id=1, source_target_pairs={{0,1},{1,0},{2,3},{3,2},{4,5},{5,4},{6,7},{7,6},{8,9},{9,8},{10,11... | collective-permute-start | bytes 786440 | tf_op jit(solution)/shard_map/ppermute | solution.py:306
  78.4 23.6 %copy-start.6 = (f32[128,4,512]{2,1,0:T(4,128)S(1)}, f32[128,4,512]{2,1,0:T(4,128)}, u32[]{:S(2)}) copy-start(f32[128,4,512]{2,1,0:T(4,128)} %param.9) | copy-start | bytes 3145732
  83.5 24.6 %collective-permute-start.8 = (bf16[2,128,512]{2,1,0:T(8,128)(2,1)S(1)}, bf16[2,128,512]{2,1,0:T(8,128)(2,1)S(1)}, u32[]{:S(2)}, u32[]{:S(2)}) collective-permute-start(bf16[2,128,512]{2,1,0:T(8,128)(2,1)S(1)} %get-tuple-element.57), channel_id=1, source_target_pairs={{0,2},{1,3},{2,0},{3,1},{4,6},{5,7},{6,4},{7,5},{8,10},{9,11},{10,... | collective-permute-start | bytes 786440 | tf_op jit(solution)/shard_map/ppermute | solution.py:306
  88.3 21.2 %collective-permute-start.9 = (bf16[2,128,512]{2,1,0:T(8,128)(2,1)S(1)}, bf16[2,128,512]{2,1,0:T(8,128)(2,1)S(1)}, u32[]{:S(2)}, u32[]{:S(2)}) collective-permute-start(bf16[2,128,512]{2,1,0:T(8,128)(2,1)S(1)} %get-tuple-element.58), channel_id=1, source_target_pairs={{0,3},{1,2},{2,1},{3,0},{4,7},{5,6},{6,5},{7,4},{8,11},{9,10},{10,... | collective-permute-start | bytes 786440 | tf_op jit(solution)/shard_map/ppermute | solution.py:306
  93.9 16.8 %collective-permute-start.21 = (bf16[2,128,512]{2,1,0:T(8,128)(2,1)S(1)}, bf16[2,128,512]{2,1,0:T(8,128)(2,1)S(1)}, u32[]{:S(2)}, u32[]{:S(2)}) collective-permute-start(bf16[2,128,512]{2,1,0:T(8,128)(2,1)S(1)} %get-tuple-element.71), channel_id=1, source_target_pairs={{0,1},{1,0},{2,3},{3,2},{4,5},{5,4},{6,7},{7,6},{8,9},{9,8},{10,11... | collective-permute-start | bytes 786440 | tf_op jit(solution)/shard_map/ppermute | solution.py:306
  101.9 11.0 %collective-permute-start.22 = (bf16[2,128,512]{2,1,0:T(8,128)(2,1)S(1)}, bf16[2,128,512]{2,1,0:T(8,128)(2,1)S(1)}, u32[]{:S(2)}, u32[]{:S(2)}) collective-permute-start(bf16[2,128,512]{2,1,0:T(8,128)(2,1)S(1)} %get-tuple-element.72), channel_id=1, source_target_pairs={{0,2},{1,3},{2,0},{3,1},{4,6},{5,7},{6,4},{7,5},{8,10},{9,11},{10,... | collective-permute-start | bytes 786440 | tf_op jit(solution)/shard_map/ppermute | solution.py:306
  105.6 13.7 %collective-permute-start.23 = (bf16[2,128,512]{2,1,0:T(8,128)(2,1)S(1)}, bf16[2,128,512]{2,1,0:T(8,128)(2,1)S(1)}, u32[]{:S(2)}, u32[]{:S(2)}) collective-permute-start(bf16[2,128,512]{2,1,0:T(8,128)(2,1)S(1)} %get-tuple-element.73), channel_id=1, source_target_pairs={{0,3},{1,2},{2,1},{3,0},{4,7},{5,6},{6,5},{7,4},{8,11},{9,10},{10,... | collective-permute-start | bytes 786440 | tf_op jit(solution)/shard_map/ppermute | solution.py:306
  108.1 13.9 %collective-permute-start.24 = (bf16[2,128,512]{2,1,0:T(8,128)(2,1)S(1)}, bf16[2,128,512]{2,1,0:T(8,128)(2,1)S(1)}, u32[]{:S(2)}, u32[]{:S(2)}) collective-permute-start(bf16[2,128,512]{2,1,0:T(8,128)(2,1)S(1)} %get-tuple-element.74), channel_id=1, source_target_pairs={{0,4},{1,5},{2,6},{3,7},{4,0},{5,1},{6,2},{7,3},{8,12},{9,13},{10,... | collective-permute-start | bytes 786440 | tf_op jit(solution)/shard_map/ppermute | solution.py:306
  109.5 30.1 %collective-permute-start.25 = (bf16[2,128,512]{2,1,0:T(8,128)(2,1)S(1)}, bf16[2,128,512]{2,1,0:T(8,128)(2,1)S(1)}, u32[]{:S(2)}, u32[]{:S(2)}) collective-permute-start(bf16[2,128,512]{2,1,0:T(8,128)(2,1)S(1)} %get-tuple-element.75), channel_id=1, source_target_pairs={{0,5},{1,4},{2,7},{3,6},{4,1},{5,0},{6,3},{7,2},{8,13},{9,12},{10,... | collective-permute-start | bytes 786440 | tf_op jit(solution)/shard_map/ppermute | solution.py:306
  110.8 36.5 %collective-permute-start.26 = (bf16[2,128,512]{2,1,0:T(8,128)(2,1)S(1)}, bf16[2,128,512]{2,1,0:T(8,128)(2,1)S(1)}, u32[]{:S(2)}, u32[]{:S(2)}) collective-permute-start(bf16[2,128,512]{2,1,0:T(8,128)(2,1)S(1)} %get-tuple-element.76), channel_id=1, source_target_pairs={{0,6},{1,7},{2,4},{3,5},{4,2},{5,3},{6,0},{7,1},{8,14},{9,15},{10,... | collective-permute-start | bytes 786440 | tf_op jit(solution)/shard_map/ppermute | solution.py:306
  112.9 43.2 %collective-permute-start.27 = (bf16[2,128,512]{2,1,0:T(8,128)(2,1)S(1)}, bf16[2,128,512]{2,1,0:T(8,128)(2,1)S(1)}, u32[]{:S(2)}, u32[]{:S(2)}) collective-permute-start(bf16[2,128,512]{2,1,0:T(8,128)(2,1)S(1)} %get-tuple-element.77), channel_id=1, source_target_pairs={{0,7},{1,6},{2,5},{3,4},{4,3},{5,2},{6,1},{7,0},{8,15},{9,14},{10,... | collective-permute-start | bytes 786440 | tf_op jit(solution)/shard_map/ppermute | solution.py:306
  119.1 77.1 %copy-start.12 = (f32[16,4]{0,1:T(4,128)S(1)}, f32[16,4]{0,1:T(4,128)}, u32[]{:S(2)}) copy-start(f32[16,4]{0,1:T(4,128)} %param.10) | copy-start | bytes 772
  119.1 87.2 %copy-start.3 = (f32[128,512]{1,0:T(8,128)S(1)}, f32[128,512]{1,0:T(8,128)}, u32[]{:S(2)}) copy-start(f32[128,512]{1,0:T(8,128)} %weight_ref.1) | copy-start | bytes 786436
  119.3 42.5 %collective-permute-start.14 = (bf16[2,128,512]{2,1,0:T(8,128)(2,1)S(1)}, bf16[2,128,512]{2,1,0:T(8,128)(2,1)S(1)}, u32[]{:S(2)}, u32[]{:S(2)}) collective-permute-start(bf16[2,128,512]{2,1,0:T(8,128)(2,1)S(1)} %get-tuple-element.64), channel_id=1, source_target_pairs={{0,1},{1,0},{2,3},{3,2},{4,5},{5,4},{6,7},{7,6},{8,9},{9,8},{10,11... | collective-permute-start | bytes 786440 | tf_op jit(solution)/shard_map/ppermute | solution.py:306
  122.0 41.3 %collective-permute-start.15 = (bf16[2,128,512]{2,1,0:T(8,128)(2,1)S(1)}, bf16[2,128,512]{2,1,0:T(8,128)(2,1)S(1)}, u32[]{:S(2)}, u32[]{:S(2)}) collective-permute-start(bf16[2,128,512]{2,1,0:T(8,128)(2,1)S(1)} %get-tuple-element.65), channel_id=1, source_target_pairs={{0,2},{1,3},{2,0},{3,1},{4,6},{5,7},{6,4},{7,5},{8,10},{9,11},{10,... | collective-permute-start | bytes 786440 | tf_op jit(solution)/shard_map/ppermute | solution.py:306
  139.5 24.5 %collective-permute-start.16 = (bf16[2,128,512]{2,1,0:T(8,128)(2,1)S(1)}, bf16[2,128,512]{2,1,0:T(8,128)(2,1)S(1)}, u32[]{:S(2)}, u32[]{:S(2)}) collective-permute-start(bf16[2,128,512]{2,1,0:T(8,128)(2,1)S(1)} %get-tuple-element.66), channel_id=1, source_target_pairs={{0,3},{1,2},{2,1},{3,0},{4,7},{5,6},{6,5},{7,4},{8,11},{9,10},{10,... | collective-permute-start | bytes 786440 | tf_op jit(solution)/shard_map/ppermute | solution.py:306
  147.2 38.7 %collective-permute-start.17 = (bf16[2,128,512]{2,1,0:T(8,128)(2,1)S(1)}, bf16[2,128,512]{2,1,0:T(8,128)(2,1)S(1)}, u32[]{:S(2)}, u32[]{:S(2)}) collective-permute-start(bf16[2,128,512]{2,1,0:T(8,128)(2,1)S(1)} %get-tuple-element.67), channel_id=1, source_target_pairs={{0,4},{1,5},{2,6},{3,7},{4,0},{5,1},{6,2},{7,3},{8,12},{9,13},{10,... | collective-permute-start | bytes 786440 | tf_op jit(solution)/shard_map/ppermute | solution.py:306
  156.1 31.8 %collective-permute-start.18 = (bf16[2,128,512]{2,1,0:T(8,128)(2,1)S(1)}, bf16[2,128,512]{2,1,0:T(8,128)(2,1)S(1)}, u32[]{:S(2)}, u32[]{:S(2)}) collective-permute-start(bf16[2,128,512]{2,1,0:T(8,128)(2,1)S(1)} %get-tuple-element.68), channel_id=1, source_target_pairs={{0,5},{1,4},{2,7},{3,6},{4,1},{5,0},{6,3},{7,2},{8,13},{9,12},{10,... | collective-permute-start | bytes 786440 | tf_op jit(solution)/shard_map/ppermute | solution.py:306
  161.1 0.7 copy-start.4
  161.8 26.1 %copy-start.7 = (bf16[2,128,512]{2,1,0:T(8,128)(2,1)}, bf16[2,128,512]{2,1,0:T(8,128)(2,1)S(1)}, u32[]{:S(2)}) copy-start(bf16[2,128,512]{2,1,0:T(8,128)(2,1)S(1)} %collective-permute-done.14.refs_1_) | copy-start | bytes 786436
  161.8 34.5 %collective-permute-start.19 = (bf16[2,128,512]{2,1,0:T(8,128)(2,1)}, bf16[2,128,512]{2,1,0:T(8,128)(2,1)}, u32[]{:S(2)}, u32[]{:S(2)}) collective-permute-start(bf16[2,128,512]{2,1,0:T(8,128)(2,1)} %get-tuple-element.69), channel_id=1, source_target_pairs={{0,6},{1,7},{2,4},{3,5},{4,2},{5,3},{6,0},{7,1},{8,14},{9,15},{10,... | collective-permute-start | bytes 786440 | tf_op jit(solution)/shard_map/ppermute | solution.py:306
  163.3 24.7 %copy-start.8 = (bf16[2,128,512]{2,1,0:T(8,128)(2,1)}, bf16[2,128,512]{2,1,0:T(8,128)(2,1)S(1)}, u32[]{:S(2)}) copy-start(bf16[2,128,512]{2,1,0:T(8,128)(2,1)S(1)} %collective-permute-done.15.refs_2_) | copy-start | bytes 786436
  163.3 38.6 %collective-permute-start.20 = (bf16[2,128,512]{2,1,0:T(8,128)(2,1)}, bf16[2,128,512]{2,1,0:T(8,128)(2,1)}, u32[]{:S(2)}, u32[]{:S(2)}) collective-permute-start(bf16[2,128,512]{2,1,0:T(8,128)(2,1)} %get-tuple-element.70), channel_id=1, source_target_pairs={{0,7},{1,6},{2,5},{3,4},{4,3},{5,2},{6,1},{7,0},{8,15},{9,14},{10,... | collective-permute-start | bytes 786440 | tf_op jit(solution)/shard_map/ppermute | solution.py:306
  164.0 23.9 %copy-start.9 = (bf16[2,128,512]{2,1,0:T(8,128)(2,1)}, bf16[2,128,512]{2,1,0:T(8,128)(2,1)S(1)}, u32[]{:S(2)}) copy-start(bf16[2,128,512]{2,1,0:T(8,128)(2,1)S(1)} %collective-permute-done.16.refs_3_) | copy-start | bytes 786436
  164.0 38.2 %collective-permute-start.28 = (bf16[2,1,128,512]{3,2,1,0:T(8,128)(2,1)}, bf16[2,1,128,512]{3,2,1,0:T(8,128)(2,1)}, u32[]{:S(2)}, u32[]{:S(2)}) collective-permute-start(bf16[2,1,128,512]{3,2,1,0:T(8,128)(2,1)} %get-tuple-element.79), channel_id=1, source_target_pairs={{8,16},{16,8},{9,17},{17,9},{10,18},{18,10},{11,19},{19,11},{12,20... | collective-permute-start | bytes 786440 | tf_op jit(solution)/shard_map/ppermute | solution.py:313
  186.0 2.0 copy-start.10
  186.0 16.5 %collective-permute-start.29 = (bf16[2,1,128,512]{3,2,1,0:T(8,128)(2,1)}, bf16[2,1,128,512]{3,2,1,0:T(8,128)(2,1)}, u32[]{:S(2)}, u32[]{:S(2)}) collective-permute-start(bf16[2,1,128,512]{3,2,1,0:T(8,128)(2,1)} %get-tuple-element.80), channel_id=1, source_target_pairs={{8,16},{16,8},{9,17},{17,9},{10,18},{18,10},{11,19},{19,11},{12,20... | collective-permute-start | bytes 786440 | tf_op jit(solution)/shard_map/ppermute | solution.py:313
  188.6 14.1 %collective-permute-start.30 = (bf16[2,1,128,512]{3,2,1,0:T(8,128)(2,1)}, bf16[2,1,128,512]{3,2,1,0:T(8,128)(2,1)}, u32[]{:S(2)}, u32[]{:S(2)}) collective-permute-start(bf16[2,1,128,512]{3,2,1,0:T(8,128)(2,1)} %get-tuple-element.81), channel_id=1, source_target_pairs={{8,16},{16,8},{9,17},{17,9},{10,18},{18,10},{11,19},{19,11},{12,20... | collective-permute-start | bytes 786440 | tf_op jit(solution)/shard_map/ppermute | solution.py:313
  196.3 9.9 %collective-permute-start.31 = (bf16[2,1,128,512]{3,2,1,0:T(8,128)(2,1)}, bf16[2,1,128,512]{3,2,1,0:T(8,128)(2,1)}, u32[]{:S(2)}, u32[]{:S(2)}) collective-permute-start(bf16[2,1,128,512]{3,2,1,0:T(8,128)(2,1)} %get-tuple-element.82), channel_id=1, source_target_pairs={{8,16},{16,8},{9,17},{17,9},{10,18},{18,10},{11,19},{19,11},{12,20... | collective-permute-start | bytes 786440 | tf_op jit(solution)/shard_map/ppermute | solution.py:313
  201.9 4.3 %collective-permute-start.32 = (bf16[2,1,128,512]{3,2,1,0:T(8,128)(2,1)}, bf16[2,1,128,512]{3,2,1,0:T(8,128)(2,1)}, u32[]{:S(2)}, u32[]{:S(2)}) collective-permute-start(bf16[2,1,128,512]{3,2,1,0:T(8,128)(2,1)} %get-tuple-element.83), channel_id=1, source_target_pairs={{0,8},{16,24},{8,0},{24,16},{1,9},{17,25},{9,1},{25,17},{2,10},{18... | collective-permute-start | bytes 786440 | tf_op jit(solution)/shard_map/ppermute | solution.py:313
  202.2 4.0 %collective-permute-start.33 = (bf16[2,1,128,512]{3,2,1,0:T(8,128)(2,1)}, bf16[2,1,128,512]{3,2,1,0:T(8,128)(2,1)}, u32[]{:S(2)}, u32[]{:S(2)}) collective-permute-start(bf16[2,1,128,512]{3,2,1,0:T(8,128)(2,1)} %get-tuple-element.84), channel_id=1, source_target_pairs={{0,8},{16,24},{8,0},{24,16},{1,9},{17,25},{9,1},{25,17},{2,10},{18... | collective-permute-start | bytes 786440 | tf_op jit(solution)/shard_map/ppermute | solution.py:313
  202.5 3.8 %collective-permute-start.34 = (bf16[2,1,128,512]{3,2,1,0:T(8,128)(2,1)}, bf16[2,1,128,512]{3,2,1,0:T(8,128)(2,1)}, u32[]{:S(2)}, u32[]{:S(2)}) collective-permute-start(bf16[2,1,128,512]{3,2,1,0:T(8,128)(2,1)} %get-tuple-element.85), channel_id=1, source_target_pairs={{0,8},{16,24},{8,0},{24,16},{1,9},{17,25},{9,1},{25,17},{2,10},{18... | collective-permute-start | bytes 786440 | tf_op jit(solution)/shard_map/ppermute | solution.py:313
  202.7 3.5 %collective-permute-start.35 = (bf16[2,1,128,512]{3,2,1,0:T(8,128)(2,1)}, bf16[2,1,128,512]{3,2,1,0:T(8,128)(2,1)}, u32[]{:S(2)}, u32[]{:S(2)}) collective-permute-start(bf16[2,1,128,512]{3,2,1,0:T(8,128)(2,1)} %get-tuple-element.86), channel_id=1, source_target_pairs={{0,8},{16,24},{8,0},{24,16},{1,9},{17,25},{9,1},{25,17},{2,10},{18... | collective-permute-start | bytes 786440 | tf_op jit(solution)/shard_map/ppermute | solution.py:313
  (1 other events, 0.7 us)
